TPU v7x, 32 devices: a whole 2x2x4 slice. The times are simulated.
32 devices in a mesh: dp: 8 (over y, x, core), group: 4 (over z).
Axes of the slice: x: 2, y: 2, z: 4, core: 2. Of those that a mesh axis runs over, the one named last changes fastest.
Arguments:
- queries: bfloat16 [8, 4, 192, 2048], P('dp', 'group'), may hold values from -6 to 6
- resp_keys: bfloat16 [8, 4, 192, 512], P('dp', 'group'), may hold values from -6 to 6
- resp_values: bfloat16 [8, 4, 192, 512], P('dp', 'group'), may hold values from -6 to 6
- prompt_cache: bfloat16 [8, 4, 2, 256, 512], P('dp', 'group'), may hold values from -1.6953125 to 1.6953125
- owners: int32 [8], P('dp'), may hold values from 0 to 3
- lengths: int32 [8, 4], P('dp', 'group'), may hold values from 1 to 192, 384 in all within a row
- q_gain: float32 [128], replicated, may hold values from 0.5 to 1.5
- k_gain: float32 [128], replicated, may hold values from 0.5 to 1.5
- grad_out: bfloat16 [8, 4, 192, 2048], P('dp', 'group'), may hold values from -6 to 6
Outputs:
- attended: bfloat16 [8, 4, 192, 2048], P('dp', 'group')
- d_queries: bfloat16 [8, 4, 192, 2048], P('dp', 'group')
- d_resp_keys: bfloat16 [8, 4, 192, 512], P('dp', 'group')
- d_resp_values: bfloat16 [8, 4, 192, 512], P('dp', 'group')
- d_prompt_cache: bfloat16 [8, 4, 2, 256, 512], P('dp', 'group')
- gain_grads: float32 [2, 128], replicated
Inputs may be any that keep to these rules, and one draw needn't show every extreme that they name: In each group the lengths sum to 384 and the longest is 192.
All inputs are finite; a program needn't handle non-finite values.
Results may differ from a plain program's by a relative error of at most 0.0095.
Values may be sent and summed in bfloat16 or wider, within the bound.
No kernel may reach another device: no remote copies, remote signals or barrier semaphores. Data moves between devices by JAX's collectives and lax.ppermute only.
A program may use at most 64 MiB of HBM per device.

v0:
```python
import jax
import jax.numpy as jnp
from jax import lax
from jax.sharding import PartitionSpec as P

HD = 128


def from_root(shard, axis, root):
    mine = lax.axis_index(axis) == root
    return lax.psum(jnp.where(mine, shard, jnp.zeros_like(shard)), axis)


def normalize(raw_vals, gain_vec):
    widened = raw_vals.astype(jnp.float32)
    inverse = lax.rsqrt(jnp.mean(widened * widened, axis=-1, keepdims=True) + 1e-06)
    unit_vals = widened * inverse
    return (unit_vals * gain_vec, unit_vals, inverse)


def norm_back(unit_vals, inverse, gain_vec, upstream):
    scaled_up = upstream * gain_vec
    d_input = inverse * (
        scaled_up - unit_vals * jnp.mean(scaled_up * unit_vals, axis=-1, keepdims=True)
    )
    gain_term = jnp.sum(upstream * unit_vals, axis=tuple(range(upstream.ndim - 1)))
    return (d_input, gain_term)


def attend_local(
    queries, resp_keys, resp_values, cache, q_gain, k_gain, live_len, grad_out, head_size
):
    resp_rows = queries.shape[0]
    prompt_rows = cache.shape[1]
    kv_heads = resp_keys.shape[1] // head_size
    share = queries.shape[1] // head_size // kv_heads
    q_scaled, q_unit, q_inv = normalize(
        queries.reshape(resp_rows, kv_heads, share, head_size), q_gain
    )
    k_scaled, k_unit, k_inv = normalize(resp_keys.reshape(resp_rows, kv_heads, head_size), k_gain)
    q_hat = q_scaled.astype(jnp.bfloat16)
    k_hat = k_scaled.astype(jnp.bfloat16)
    keys_all = jnp.concatenate([cache[0].reshape(prompt_rows, kv_heads, head_size), k_hat], axis=0)
    vals_all = jnp.concatenate(
        [
            cache[1].reshape(prompt_rows, kv_heads, head_size),
            resp_values.reshape(resp_rows, kv_heads, head_size),
        ],
        axis=0,
    )
    score_scale = head_size ** (-0.5)
    scores = (
        jnp.einsum("rkgd,skd->kgrs", q_hat, keys_all, preferred_element_type=jnp.float32)
        * score_scale
    )
    row_index = jnp.arange(resp_rows, dtype=jnp.int32)[:, None]
    col_index = jnp.arange(prompt_rows + resp_rows, dtype=jnp.int32)[None, :]
    self_col = col_index - prompt_rows
    allowed = (col_index < prompt_rows) | (self_col <= row_index) & (self_col < live_len)
    expo = jnp.where(allowed, jnp.exp(scores), jnp.float32(0.0))
    probs = expo / jnp.sum(expo, axis=-1, keepdims=True)
    probs_low = probs.astype(jnp.bfloat16)
    live = (jnp.arange(resp_rows, dtype=jnp.int32) < live_len)[:, None, None, None]
    attended_full = jnp.einsum(
        "kgrs,skd->rkgd", probs_low, vals_all, preferred_element_type=jnp.float32
    )
    attended = jnp.where(live, attended_full, jnp.float32(0.0)).astype(jnp.bfloat16)
    d_out = jnp.where(
        live, grad_out.reshape(resp_rows, kv_heads, share, head_size), jnp.zeros((), jnp.bfloat16)
    )
    d_probs = jnp.einsum("rkgd,skd->kgrs", d_out, vals_all, preferred_element_type=jnp.float32)
    delta = jnp.sum(probs * d_probs, axis=-1, keepdims=True)
    d_scores = (probs * (d_probs - delta) * score_scale).astype(jnp.bfloat16)
    d_qhat = jnp.einsum("kgrs,skd->rkgd", d_scores, keys_all, preferred_element_type=jnp.float32)
    d_keys = jnp.einsum("kgrs,rkgd->skd", d_scores, q_hat, preferred_element_type=jnp.float32)
    d_vals = jnp.einsum("kgrs,rkgd->skd", probs_low, d_out, preferred_element_type=jnp.float32)
    d_query_in, q_term = norm_back(q_unit, q_inv, q_gain, d_qhat)
    d_key_in, k_term = norm_back(k_unit, k_inv, k_gain, d_keys[prompt_rows:])
    width_q = queries.shape[1]
    width_k = resp_keys.shape[1]
    prompt_part = jnp.stack(
        [
            d_keys[:prompt_rows].reshape(prompt_rows, width_k),
            d_vals[:prompt_rows].reshape(prompt_rows, width_k),
        ]
    )
    return (
        attended.reshape(resp_rows, width_q),
        d_query_in.astype(jnp.bfloat16).reshape(resp_rows, width_q),
        d_key_in.astype(jnp.bfloat16).reshape(resp_rows, width_k),
        d_vals[prompt_rows:].astype(jnp.bfloat16).reshape(resp_rows, width_k),
        prompt_part,
        jnp.stack([q_term, k_term]),
    )


def local(queries, resp_keys, resp_values, prompt_cache, owners, lengths, q_gain, k_gain, grad_out):
    owner = owners[0]
    cache = from_root(prompt_cache[0, 0], "group", owner)
    attended, d_query, d_key, d_value, prompt_part, gain_part = attend_local(
        queries[0, 0],
        resp_keys[0, 0],
        resp_values[0, 0],
        cache,
        q_gain,
        k_gain,
        lengths[0, 0],
        grad_out[0, 0],
        HD,
    )
    summed = lax.psum(prompt_part, "group")
    summed_low = summed.astype(jnp.bfloat16)
    mine = lax.axis_index("group") == owner
    placed = jnp.where(mine, summed_low, jnp.zeros((), jnp.bfloat16))
    gain_grads = lax.psum(gain_part, ("dp", "group"))
    return (
        attended[None, None],
        d_query[None, None],
        d_key[None, None],
        d_value[None, None],
        placed[None, None],
        gain_grads,
    )


def solution(mesh):
    in_specs = (
        P("dp", "group", None, None),
        P("dp", "group", None, None),
        P("dp", "group", None, None),
        P("dp", "group", None, None, None),
        P("dp"),
        P("dp", "group"),
        P(),
        P(),
        P("dp", "group", None, None),
    )
    out_specs = (
        P("dp", "group", None, None),
        P("dp", "group", None, None),
        P("dp", "group", None, None),
        P("dp", "group", None, None),
        P("dp", "group", None, None, None),
        P(),
    )
    return jax.shard_map(local, mesh=mesh, in_specs=in_specs, out_specs=out_specs, check_vma=False)
```

profile of v0, /device:TPU:0, one launch (start us, length us, event | category | flops | bytes accessed | tf_op | source)
XLA Modules:
  0.0 227.6 jit_solution(17900343633325902230)
XLA Ops:
  7.2 0.0 copy-start.5
  7.2 0.0 copy-start.2
  7.2 0.0 copy-start.11
  7.2 0.0 all-reduce.3.cloned.1.call-start
  7.2 1.3 copy.66
  9.2 0.8 select_bitcast_fusion.1
  10.1 0.0 all-reduce.3.cloned.1.call-update
  10.7 1.0 reshape_squeeze.15
  11.7 0.7 copy.68
  12.4 0.6 iota_compare_fusion.1
  13.0 2.3 %reshape.65 = f32[192,4,4,128]{3,2,1,0:T(4,128)S(1)} reshape(bf16[1,1,192,2048]{3,2,1,0:T(8,128)(2,1)} %param.9) | data formatting | bytes 2359296 | tf_op jit(solution)/shard_map/convert_element_type | solution.py:15
  15.3 1.2 multiply_reduce_fusion.1
  16.5 0.2 copy.72
  16.7 0.6 add_rsqrt_fusion
  17.4 0.0 copy-done.5
  17.4 0.1 reshape.64
  17.5 0.0 copy-start.12
  17.5 0.3 multiply_reduce_fusion.4
  17.8 0.1 copy.69
  17.9 0.0 copy-done.2
  17.9 0.6 reshape_squeeze.17
  18.5 0.5 iota_compare_fusion.2
  19.0 1.4 fusion.24
  20.4 0.0 copy-done.11
  20.4 0.8 multiply_convert_fusion.3
  21.2 30.7 %all-reduce.3.cloned.1.call-done = bf16[2,256,512]{1,2,0:T(8,128)(2,1)} async-done(((bf16[2,256,512]{1,2,0:T(8,128)(2,1)}), bf16[2,256,512]{1,2,0:T(8,128)(2,1)}) %all-reduce.3.cloned.1.call-update) | async-done | bytes 524304 | tf_op jit(solution)/shard_map/psum | solution.py:11
  52.0 1.1 fusion.43
  53.0 0.2 copy.67
  53.2 0.2 copy.71
  53.4 0.0 copy-start.6
  53.4 0.0 copy-start.7
  53.4 0.0 copy-start.9
  53.4 4.7 %fusion.26 = f32[4,448,192,4]{1,2,3,0:T(8,128)} fusion(bf16[192,4,128]{2,0,1:T(8,128)(2,1)} %copy.68, bf16[256,4,128]{2,0,1:T(8,128)(2,1)S(1)} %copy.67, bf16[192,4,4,128]{3,2,1,0:T(4,128)(2,1)S(1)} %reshape_squeeze.17, pred[192]{0:T(512)(128)(4,1)} %iota_compare_fusion.2), kind=kOutput, calls=%fused_computation.46 | convolution fusion | flops 353632256 | bytes 6750400 | tf_op jit(solution)/shard_map/rkgd,skd->kgrs/dot_general | solution.py:71
  58.1 0.0 copy-done.12
  58.1 0.0 copy-done.6
  58.1 0.0 copy-done.7
  58.1 0.0 copy-done.9
  58.1 0.0 copy-start.4
  58.1 0.0 copy-start.13
  58.1 2.6 %fusion.5 = (f32[4,4,192]{2,1,0:T(4,128)S(1)}, f32[4,448,192,4]{1,2,3,0:T(8,128)S(1)}) fusion(pred[192,448]{1,0:T(8,128)(4,1)S(1)} %copy-done.7, f32[192,4,4,128]{3,2,1,0:T(4,128)S(1)} %reshape.65, f32[128]{0:T(128)S(1)} %copy-done.12, f32[192,4,4]{0,2,1:T(4,128)S(1)} %copy-done.9, bf16[192,4,128]{2,0,1:T(8,128)(2,1)S(1)} %copy-done.6, ...), kind=kOutput, calls=%fused_computation.8 | convolution fusion | flops 358544384 | bytes 7647744 | tf_op jit(solution)/shard_map/rkgd,skd->kgrs/dot_general | solution.py:53
  60.7 2.7 %copy-done.14 = f32[4,448,192,4]{1,2,3,0:T(8,128)} copy-done((f32[4,448,192,4]{1,2,3,0:T(8,128)}, f32[4,448,192,4]{1,2,3,0:T(8,128)S(1)}, u32[]{:S(2)}) %copy-start.14) | copy-done | bytes 5505048
  63.4 0.0 copy-done.4
  63.4 2.5 %fusion.20 = bf16[192,4,4,128]{3,0,2,1:T(8,128)(2,1)} fusion(pred[192]{0:T(512)(128)(4,1)S(1)} %copy-done.13, bf16[192,4,128]{2,0,1:T(8,128)(2,1)S(1)} %copy-done.4, bf16[256,4,128]{2,0,1:T(8,128)(2,1)S(1)} %copy.67, f32[4,448,192,4]{1,2,3,0:T(8,128)S(1)} %get-tuple-element.37, f32[4,4,192]{2,1,0:T(4,128)S(1)} %get-tuple-element.36, ...), kind=kOutput, calls=%fused_computation.27 | convolution fusion | flops 359530496 | bytes 6848704 | tf_op jit(solution)/shard_map/kgrs,skd->rkgd/dot_general | solution.py:64
  65.9 28.1 %fusion.9 = (f32[128]{0:T(128)S(1)}, f32[192,4,4]{0,2,1:T(4,128)S(1)}, f32[4,128,4,192]{1,3,2,0:T(8,128)}) fusion(f32[192,4,4,128]{3,2,1,0:T(4,128)S(1)} %reshape.65, f32[192,4,4]{0,2,1:T(4,128)S(1)} %copy-done.9, f32[128]{0:T(128)S(1)} %copy-done.12, f32[4,448,192,4]{1,2,3,0:T(8,128)} %fusion.26, f32[4,4,192]{2,1,0:T(4,128)S(1)} %get-tuple-element.36, ...), kind=kOutput, calls=%fused_computation.14 | convolution fusion | flops 370737472 | bytes 14738432 | tf_op jit(solution)/shard_map/kgrs,skd->rkgd/dot_general | solution.py:74
  94.1 28.6 %fusion.19 = f32[448,4,128]{2,0,1:T(8,128)} fusion(f32[4,448,192,4]{1,2,3,0:T(8,128)} %fusion.26, f32[192,4,4,128]{3,2,1,0:T(4,128)S(1)} %reshape.65, f32[128]{0:T(128)S(1)} %copy-done.12, f32[192,4,4]{0,2,1:T(4,128)S(1)} %copy-done.9, f32[4,448,192,4]{1,2,3,0:T(8,128)} %copy-done.14, f32[4,4,192]{2,1,0:T(4,128)S(1)} %get-tuple-element.36, ...), kind=kOutput, calls=%fused_computation.26 | convolution fusion | flops 368643520 | bytes 13611520 | tf_op jit(solution)/shard_map/kgrs,rkgd->skd/dot_general | solution.py:75
  122.7 4.6 %fusion.16 = f32[448,4,128]{2,0,1:T(8,128)S(1)} fusion(bf16[192,4,4,128]{3,2,1,0:T(4,128)(2,1)S(1)} %reshape_squeeze.17, pred[192]{0:T(512)(128)(4,1)S(1)} %copy-done.13, f32[4,448,192,4]{1,2,3,0:T(8,128)} %copy-done.14, f32[4,4,192]{2,1,0:T(4,128)S(1)} %get-tuple-element.36, pred[192,448]{1,0:T(8,128)(4,1)S(1)} %copy-done.8), kind=kOutput, calls=%fused_computation.25 | convolution fusion | flops 358219776 | bytes 7307456 | tf_op jit(solution)/shard_map/kgrs,rkgd->skd/dot_general | solution.py:76
  127.3 0.4 multiply_reduce_fusion.2
  127.7 0.5 copy-done
  128.2 0.6 copy.74
  128.8 1.5 broadcast_in_dim_reshape.12
  130.3 2.4 %multiply_convert_fusion = bf16[192,4,4,128]{3,0,2,1:T(8,128)(2,1)S(1)} fusion(f32[4,128,4,192]{1,3,2,0:T(8,128)} %get-tuple-element.38, f32[192,4,4,128]{3,2,1,0:T(4,128)S(1)} %reshape.65, f32[192,4,4]{0,2,1:T(4,128)S(1)} %broadcast_multiply_fusion, f32[128]{0:T(128)S(1)} %copy-done.12, f32[192,4,4]{0,2,1:T(4,128)S(1)} %copy-done.10), kind=kLoop, calls=%fused_computation.16 | loop fusion | flops 2359296 | bytes 3957248 | tf_op jit(solution)/shard_map/convert_element_type | solution.py:89
  132.7 0.6 copy.76
  133.3 1.5 broadcast_in_dim_reshape.13
  134.8 1.3 multiply_convert_fusion.2
  136.1 0.2 copy.77
  136.2 0.8 broadcast_in_dim_reshape.14
  137.0 0.2 copy.78
  137.1 0.8 broadcast_in_dim_reshape.15
  137.9 0.2 copy.80
  138.1 0.2 copy.79
  138.3 0.1 pad_maximum_fusion
  138.4 42.2 %all-reduce.4 = bf16[2,256,512]{1,2,0:T(8,128)(2,1)S(1)} all-reduce(f32[2,256,512]{1,2,0:T(8,128)S(1)} %pad_maximum_fusion), channel_id=1, replica_groups=mesh['dp'=8,'group'=4] {'group'}, use_global_device_ids=true, to_apply=%region_7.8 | all-reduce | flops 262144 | bytes 1572864 | tf_op jit(solution)/shard_map/psum | solution.py:111
  180.7 1.0 copy.81
  181.7 39.1 %psum.23 = f32[2,128]{1,0:T(2,128)} all-reduce(f32[2,128]{1,0:T(2,128)S(1)} %pad_maximum_fusion.1), channel_id=1, replica_groups=mesh['dp'=8,'group'=4] {'dp','group'}, use_global_device_ids=true, to_apply=%region_10.11 | all-reduce | flops 256 | bytes 2048 | tf_op jit(solution)/shard_map/psum | solution.py:115
  (22 shorter events, 0.1 us)
Async XLA Ops:
  7.2 10.2 %copy-start.5 = (bf16[1,1,192,512]{3,2,1,0:T(8,128)(2,1)S(1)}, bf16[1,1,192,512]{3,2,1,0:T(8,128)(2,1)}, u32[]{:S(2)}) copy-start(bf16[1,1,192,512]{3,2,1,0:T(8,128)(2,1)} %param.10) | copy-start | bytes 589828
  7.2 10.7 %copy-start.2 = (bf16[1,1,192,2048]{3,2,1,0:T(8,128)(2,1)S(1)}, bf16[1,1,192,2048]{3,2,1,0:T(8,128)(2,1)}, u32[]{:S(2)}) copy-start(bf16[1,1,192,2048]{3,2,1,0:T(8,128)(2,1)} %param.17) | copy-start | bytes 2359300
  7.2 13.2 %copy-start.11 = (f32[128]{0:T(128)S(1)}, f32[128]{0:T(128)}, u32[]{:S(2)}) copy-start(f32[128]{0:T(128)} %param.16) | copy-start | bytes 1540
  7.2 44.8 %all-reduce.3.cloned.1.call-start = ((), (), s32[]{:S(2)}) async-start(), calls=%async_computation | async-start | bytes 1048576 | tf_op jit(solution)/shard_map/psum | solution.py:11
  17.5 40.6 %copy-start.12 = (f32[128]{0:T(128)S(1)}, f32[128]{0:T(128)}, u32[]{:S(2)}) copy-start(f32[128]{0:T(128)} %param.15) | copy-start | bytes 1540
  53.4 4.7 %copy-start.6 = (bf16[192,4,128]{2,0,1:T(8,128)(2,1)S(1)}, bf16[192,4,128]{2,0,1:T(8,128)(2,1)}, u32[]{:S(2)}) copy-start(bf16[192,4,128]{2,0,1:T(8,128)(2,1)} %multiply_convert_fusion.3) | copy-start | bytes 589828
  53.4 4.7 %copy-start.7 = (pred[192,448]{1,0:T(8,128)(4,1)S(1)}, pred[192,448]{1,0:T(8,128)(4,1)}, u32[]{:S(2)}) copy-start(pred[192,448]{1,0:T(8,128)(4,1)} %fusion.24) | copy-start | bytes 258052
  53.4 4.7 %copy-start.9 = (f32[192,4,4]{0,2,1:T(4,128)S(1)}, f32[192,4,4]{0,2,1:T(4,128)}, u32[]{:S(2)}) copy-start(f32[192,4,4]{0,2,1:T(4,128)} %add_rsqrt_fusion) | copy-start | bytes 36868
  58.1 5.3 %copy-start.4 = (bf16[192,4,128]{2,0,1:T(8,128)(2,1)S(1)}, bf16[192,4,128]{2,0,1:T(8,128)(2,1)}, u32[]{:S(2)}) copy-start(bf16[192,4,128]{2,0,1:T(8,128)(2,1)} %copy.68) | copy-start | bytes 589828
  58.1 5.3 %copy-start.13 = (pred[192]{0:T(512)(128)(4,1)S(1)}, pred[192]{0:T(512)(128)(4,1)}, u32[]{:S(2)}) copy-start(pred[192]{0:T(512)(128)(4,1)} %iota_compare_fusion.2) | copy-start | bytes 580
  60.7 2.7 %copy-start.14 = (f32[4,448,192,4]{1,2,3,0:T(8,128)}, f32[4,448,192,4]{1,2,3,0:T(8,128)S(1)}, u32[]{:S(2)}) copy-start(f32[4,448,192,4]{1,2,3,0:T(8,128)S(1)} %get-tuple-element.37) | copy-start | bytes 16515076
  65.9 28.1 %copy-start.8 = (pred[192,448]{1,0:T(8,128)(4,1)S(1)}, pred[192,448]{1,0:T(8,128)(4,1)}, u32[]{:S(2)}) copy-start(pred[192,448]{1,0:T(8,128)(4,1)} %fusion.24) | copy-start | bytes 258052
  122.7 4.7 %copy-start.1 = (f32[448,4,128]{2,0,1:T(8,128)S(1)}, f32[448,4,128]{2,0,1:T(8,128)}, u32[]{:S(2)}) copy-start(f32[448,4,128]{2,0,1:T(8,128)} %fusion.19) | copy-start | bytes 2752516
  122.7 5.5 %copy-start.3 = (bf16[192,4,4,128]{3,0,2,1:T(8,128)(2,1)S(1)}, bf16[192,4,4,128]{3,0,2,1:T(8,128)(2,1)}, u32[]{:S(2)}) copy-start(bf16[192,4,4,128]{3,0,2,1:T(8,128)(2,1)} %fusion.20) | copy-start | bytes 2359300
  127.3 0.9 copy-start
  127.3 3.0 %copy-start.10 = (f32[192,4,4]{0,2,1:T(4,128)S(1)}, f32[192,4,4]{0,2,1:T(4,128)}, u32[]{:S(2)}) copy-start(f32[192,4,4]{0,2,1:T(4,128)} %add_rsqrt_fusion) | copy-start | bytes 36868
  128.2 9.7 %slice-start = ((f32[448,4,128]{2,0,1:T(8,128)}), f32[256,4,128]{2,0,1:T(8,128)S(1)}, s32[]{:S(2)}) async-start(f32[448,4,128]{2,0,1:T(8,128)} %copy-done), calls=%async_computation.1 | async-start | bytes 1048576 | tf_op jit(solution)/shard_map/slice | solution.py:84
  130.3 7.8 %slice-start.1 = ((f32[448,4,128]{2,0,1:T(8,128)}), f32[256,4,128]{2,0,1:T(8,128)S(1)}, s32[]{:S(2)}) async-start(f32[448,4,128]{2,0,1:T(8,128)} %fusion.19), calls=%async_computation.2 | async-start | bytes 1048576 | tf_op jit(solution)/shard_map/slice | solution.py:83
Sparse Core Ops, SparseCore 0:
  11.0 40.9 all-reduce.2
where the time goes:
time: 228 us
  blocking collectives  81.3 us (36%)
  matrix products  71.1 us (31%)
  waiting for transfers between devices  30.7 us (13%)
  local copies, waits for them, and re-layouts  18.3 us (8%)
  between operations  15.6 us (7%)
  other arithmetic  10.5 us (5%)
    psum x1, blocking collectives, local(): summed = lax.psum(prompt_part, 'group')  42.2 us
    psum x1, blocking collectives, local(): gain_grads = lax.psum(gain_part, ('dp', 'group'))  39.1 us
    psum x1, waiting for transfers between devices, from_root(): return lax.psum(jnp.where(mine, shard, jnp.zeros_like(shard)), axis)  30.7 us
    dot_general x1, matrix products, attend_local(): jnp.einsum('kgrs,rkgd->skd', d_scores, q_hat, preferred_element_type=jnp....  28.6 us
    dot_general x1, matrix products, attend_local(): jnp.einsum('kgrs,skd->rkgd', d_scores, keys_all, preferred_element_type=j...  28.1 us
    unnamed x32, local copies, waits for them, and re-layouts  5.54 us
    dot_general x1, matrix products, attend_local(): jnp.einsum('rkgd,skd->kgrs', d_out, vals_all, preferred_element_type=jnp....  4.68 us
    dot_general x1, matrix products, attend_local(): jnp.einsum('kgrs,rkgd->skd', probs_low, d_out, preferred_element_type=jnp...  4.58 us
  transfers between devices with their start and end apart: 1, of which 1 were waited for; matrix products, arithmetic and copies ran while one was open for 5% of the time, Pallas kernels for 0%

commit v1 on v0

v1 whole, which is shorter than its diff:
```python
import functools

import jax
import jax.numpy as jnp
from jax import lax
from jax.experimental import pallas as pl
from jax.experimental.pallas import tpu as pltpu
from jax.sharding import PartitionSpec as P

HD = 128
EPS = 1e-06
LOG2E = 1.4426950408889634
BF = jnp.bfloat16
F32 = jnp.float32


def dot_nn(a, b):
    return lax.dot_general(a, b, (((1,), (0,)), ((), ())), preferred_element_type=F32)


def dot_nt(a, b):
    return lax.dot_general(a, b, (((1,), (1,)), ((), ())), preferred_element_type=F32)


def head_kernel(
    share, rows, width, meta, q_ref, g_ref, k_ref, v_ref, pr_ref, gain_ref, acc_ref, *rest
):
    att_ref, dq_ref, dk_ref, dv_ref, part_ref, gacc_ref = rest[-6:]
    live_len = meta[1]
    scale = HD ** (-0.5)

    def stacked(ref):
        return jnp.concatenate([ref[:, i * HD : (i + 1) * HD] for i in range(share)], axis=0)

    q_gain = gain_ref[:, 0:1]
    q_t = stacked(q_ref).T
    g_t = stacked(g_ref).T

    raw_k = k_ref[...].astype(F32)
    k_inv = lax.rsqrt(jnp.mean(raw_k * raw_k, axis=-1, keepdims=True) + EPS)
    k_unit = raw_k * k_inv
    kg_row = acc_ref[2:3, :]
    k_hat = (k_unit * kg_row).astype(BF)
    p_key = pr_ref[0]
    p_val = pr_ref[1]
    r_val = v_ref[...]
    p_key_t = p_key.T
    p_val_t = p_val.T
    k_hat_t = k_hat.T
    r_val_t = r_val.T

    total = share * rows
    d_kp = d_kr = d_vp = d_vr = q_term = None
    att_parts, dq_parts = [], []
    for start in range(0, total, width):
        cols = slice(start, start + width)
        token = (lax.broadcasted_iota(jnp.int32, (1, width), 1) + start) % rows
        live = token < live_len
        raw_q = q_t[:, cols].astype(F32)
        q_inv = lax.rsqrt(jnp.mean(raw_q * raw_q, axis=0, keepdims=True) + EPS)
        q_unit = raw_q * q_inv
        q_hat = (q_unit * q_gain).astype(BF)
        d_o = jnp.where(live, g_t[:, cols].astype(F32), 0.0)
        d_ob = d_o.astype(BF)

        e_p = jnp.exp2(dot_nn(p_key, q_hat) * (scale * LOG2E))
        causal = lax.broadcasted_iota(jnp.int32, (rows, width), 0) <= token
        e_r = jnp.where(causal, jnp.exp2(dot_nn(k_hat, q_hat) * (scale * LOG2E)), 0.0)
        inv_sum = 1.0 / (
            jnp.sum(e_p, axis=0, keepdims=True) + jnp.sum(e_r, axis=0, keepdims=True)
        )
        eb_p = e_p.astype(BF)
        eb_r = e_r.astype(BF)
        out = (dot_nn(p_val_t, eb_p) + dot_nn(r_val_t, eb_r)) * inv_sum
        att_parts.append(jnp.where(live, out, 0.0).astype(BF))
        delta = jnp.sum(d_o * out, axis=0, keepdims=True)
        ds_p = (e_p * (dot_nn(p_val, d_ob) - delta)).astype(BF)
        ds_r = (e_r * (dot_nn(r_val, d_ob) - delta)).astype(BF)
        weight = inv_sum * scale
        d_qhat = (dot_nn(p_key_t, ds_p) + dot_nn(k_hat_t, ds_r)) * weight
        q_w = (q_hat.astype(F32) * weight).astype(BF)
        d_ow = (d_o * inv_sum).astype(BF)
        terms = (
            dot_nt(ds_p, q_w),
            dot_nt(ds_r, q_w),
            dot_nt(eb_p, d_ow),
            dot_nt(eb_r, d_ow),
            d_qhat * q_unit,
        )
        if d_kp is None:
            d_kp, d_kr, d_vp, d_vr, q_term = terms
        else:
            d_kp, d_kr, d_vp, d_vr, q_term = [
                a + b for a, b in zip((d_kp, d_kr, d_vp, d_vr, q_term), terms)
            ]
        up = d_qhat * q_gain
        mean = jnp.mean(up * q_unit, axis=0, keepdims=True)
        dq_parts.append((q_inv * (up - q_unit * mean)).astype(BF))

    att = jnp.concatenate(att_parts, axis=1).T
    d_q = jnp.concatenate(dq_parts, axis=1).T
    for i in range(share):
        att_ref[:, i * HD : (i + 1) * HD] = att[i * rows : (i + 1) * rows, :]
        dq_ref[:, i * HD : (i + 1) * HD] = d_q[i * rows : (i + 1) * rows, :]
    part_ref[0] = d_kp.astype(BF)
    part_ref[1] = d_vp.astype(BF)
    dv_ref[...] = d_vr.astype(BF)
    up_k = d_kr * kg_row
    mean_k = jnp.mean(up_k * k_unit, axis=-1, keepdims=True)
    dk_ref[...] = (k_inv * (up_k - k_unit * mean_k)).astype(BF)
    folded = q_term[:, :HD]
    for start in range(HD, width, HD):
        folded = folded + q_term[:, start : start + HD]
    gacc_ref[0:1, :] = acc_ref[0:1, :] + jnp.sum(folded.T, axis=0, keepdims=True)
    gacc_ref[1:2, :] = acc_ref[1:2, :] + jnp.sum(d_kr * k_unit, axis=0, keepdims=True)
    gacc_ref[2:3, :] = kg_row


def one_head(meta, q, g, k, v, prompt, gain_cols, acc, buffers, kv_heads):
    rows, q_width = q.shape
    share = q_width // HD // kv_heads
    wide = share * HD
    by_head_q = pl.BlockSpec((rows, wide), lambda i, m: (0, m[0]))
    by_head_k = pl.BlockSpec((rows, HD), lambda i, m: (0, m[0]))
    whole = lambda a: pl.BlockSpec(a.shape, lambda i, m: (0,) * a.ndim)
    any_spec = pl.BlockSpec(memory_space=pl.ANY)
    in_specs = [by_head_q, by_head_q, by_head_k, by_head_k, whole(prompt), whole(gain_cols), whole(acc)]
    in_specs += [any_spec] * len(buffers)
    part = jax.ShapeDtypeStruct(prompt.shape, BF)
    out_shape = [
        jax.ShapeDtypeStruct((rows, q_width), BF),
        jax.ShapeDtypeStruct((rows, q_width), BF),
        jax.ShapeDtypeStruct((rows, kv_heads * HD), BF),
        jax.ShapeDtypeStruct((rows, kv_heads * HD), BF),
        part,
        jax.ShapeDtypeStruct(acc.shape, F32),
    ]
    outs = pl.pallas_call(
        functools.partial(head_kernel, share, rows, 2 * HD),
        out_shape=out_shape,
        grid_spec=pltpu.PrefetchScalarGridSpec(
            num_scalar_prefetch=1,
            grid=(1,),
            in_specs=in_specs,
            out_specs=[by_head_q, by_head_q, by_head_k, by_head_k, whole(part), whole(acc)],
        ),
        input_output_aliases={8 + i: i for i in range(len(buffers))},
        compiler_params=pltpu.CompilerParams(vmem_limit_bytes=40 * 2**20),
        cost_estimate=pl.CostEstimate(
            flops=12 * share * rows * (rows + prompt.shape[1]) * HD,
            bytes_accessed=5 * rows * wide * 2,
            transcendentals=share * rows * (rows + prompt.shape[1]),
        ),
        name="attend_head",
    )(meta, q, g, k, v, prompt, gain_cols, acc, *buffers)
    return outs[:4], outs[4], outs[5]


def place_kernel(meta, *refs):
    out_ref = refs[-1]
    mine = meta[0] > 0
    for i, ref in enumerate(refs[:-1]):
        at = pl.multiple_of(meta[1 + i] * HD, HD)
        out_ref[:, :, pl.ds(at, HD)] = jnp.where(mine, ref[...], jnp.zeros((), BF))


def place(meta, heads):
    depth, rows, _ = heads[0].shape
    return pl.pallas_call(
        place_kernel,
        out_shape=jax.ShapeDtypeStruct((depth, rows, HD * len(heads)), BF),
        in_specs=[pl.BlockSpec(memory_space=pltpu.SMEM)]
        + [pl.BlockSpec(memory_space=pltpu.VMEM)] * len(heads),
        out_specs=pl.BlockSpec(memory_space=pltpu.VMEM),
        name="place_prompt_grad",
    )(meta, *heads)


def pair_sum(value, axis, size):
    step = 1
    while step < size:
        value = value + lax.ppermute(value, axis, [(i, i ^ step) for i in range(size)])
        step *= 2
    return value


def local(
    n_dp, n_group, queries, resp_keys, resp_values, prompt_cache, owners, lengths, q_gain, k_gain, grad_out
):
    q, g = queries[0, 0], grad_out[0, 0]
    k, v = resp_keys[0, 0], resp_values[0, 0]
    cache = prompt_cache[0, 0]
    owner = owners[0]
    live_len = lengths[0, 0]
    me = lax.axis_index("group")
    kv_heads = k.shape[1] // HD
    depth, p_rows, _ = cache.shape
    direct = n_group == kv_heads

    def shift(x, s):
        return lax.ppermute(x, "group", [(i, (i + s) % n_group) for i in range(n_group)])

    def head_of(array, index):
        return lax.dynamic_slice(array, (0, 0, index * HD), (depth, p_rows, HD))

    if direct:
        got = [head_of(cache, me)]
        for s in range(1, n_group):
            got.append(shift(head_of(cache, (me + s) % n_group), s))
        mine = got[0]
        for s in range(1, n_group):
            mine = jnp.where(owner == (me - s) % n_group, got[s], mine)
        order = [(me - s) % n_group for s in range(n_group)]
        prompts = [mine] + [shift(mine, s) for s in range(1, n_group)]
    else:
        cache = lax.psum(jnp.where(me == owner, cache, jnp.zeros_like(cache)), "group")
        order = [jnp.int32(h) for h in range(kv_heads)]
        prompts = [head_of(cache, h) for h in order]

    gain_cols = jnp.stack([q_gain, k_gain], axis=1)
    acc = jnp.zeros((8, HD), F32).at[2].set(k_gain)
    buffers, parts = (), []
    for head, prompt in zip(order, prompts):
        meta = jnp.stack([head, live_len]).astype(jnp.int32)
        buffers, part, acc = one_head(meta, q, g, k, v, prompt, gain_cols, acc, buffers, kv_heads)
        parts.append(part)

    if direct:
        back = [shift(parts[s], -s).astype(F32) for s in range(1, n_group)]
        total = parts[0].astype(F32)
        for b in back:
            total = total + b
        total = total.astype(BF)
        heads = [total] + [shift(total, s) for s in range(1, n_group)]
    else:
        total = lax.psum(jnp.concatenate(parts, axis=-1).astype(F32), "group").astype(BF)
        heads = [head_of(total, h) for h in order]
    flag = (me == owner).astype(jnp.int32)
    placed = place(jnp.stack([flag] + order).astype(jnp.int32), heads)

    gains = pair_sum(pair_sum(acc[:2], "group", n_group), "dp", n_dp)
    attended, d_query, d_key, d_value = buffers
    return (
        attended[None, None],
        d_query[None, None],
        d_key[None, None],
        d_value[None, None],
        placed[None, None],
        gains,
    )


def solution(mesh):
    in_specs = (
        P("dp", "group", None, None),
        P("dp", "group", None, None),
        P("dp", "group", None, None),
        P("dp", "group", None, None, None),
        P("dp"),
        P("dp", "group"),
        P(),
        P(),
        P("dp", "group", None, None),
    )
    out_specs = (
        P("dp", "group", None, None),
        P("dp", "group", None, None),
        P("dp", "group", None, None),
        P("dp", "group", None, None),
        P("dp", "group", None, None, None),
        P(),
    )
    body = functools.partial(local, mesh.shape["dp"], mesh.shape["group"])
    return jax.shard_map(body, mesh=mesh, in_specs=in_specs, out_specs=out_specs, check_vma=False)
```

time: 228 us -> 79.7 us (0.35)
  blocking collectives: 81.3 us -> 0 us
  matrix products: 71.1 us -> 0 us
  starting transfers between devices: 0.04 us -> 29 us
  Pallas kernels: 0 us -> 15.2 us
  local copies, waits for them, and re-layouts: 18.3 us -> 4.2 us
  between operations: 15.6 us -> 2.15 us
  other arithmetic: 10.5 us -> 1.87 us
  waiting for transfers between devices: 30.7 us -> 27.1 us
    psum x2 -> x0, blocking collectives: 81.3 us -> none  [the longest x1 42.2 us: local(): summed = lax.psum(prompt_part, 'group')]
    dot_general x6 -> x0, matrix products: 71.1 us -> none  [the longest x1 28.6 us: attend_local(): jnp.einsum('kgrs,rkgd->skd', d_scores, q_hat, preferred_element_type=jnp....]
    psum x1 -> x0, waiting for transfers between devices: 30.7 us -> none  [from_root(): return lax.psum(jnp.where(mine, shard, jnp.zeros_like(shard)), axis)]
    ppermute x0 -> x17, starting transfers between devices: none -> 29 us  [the longest x12 22.4 us: shift(): lax.ppermute(x, 'group', [(i, (i + s) % n_group) for i in range(n_group)])]
    ppermute x0 -> x17, waiting for transfers between devices: none -> 27.1 us  [the longest x5 15 us: pair_sum(): lax.ppermute(value, axis, [(i, i ^ step) for i in range(size)])]
    pallas_call x0 -> x5, Pallas kernels: none -> 15.2 us  [the longest x4 13.2 us: one_head(): pl.pallas_call(functools.partial(head_kernel, share, rows, 2 * HD), out_s...]
    another operation x9 -> x2, local copies, waits for them, and re-layouts: 7.06 us -> 0.71 us  [the longest x1 0.6 us: local(): placed = place(jnp.stack([flag] + order).astype(jnp.int32), heads)]
    convert_element_type x3 -> x1, other arithmetic: 4.5 us -> 0.08 us  [local(): total = total.astype(BF)]
  transfers between devices with their start and end apart: 1 -> 17, of which waited for: 1 -> 8; matrix products, arithmetic and copies ran while one was open for 5% -> 2% of each run, Pallas kernels for 0% -> 12%
where the time goes in v1:
time: 79.7 us; the launch traced here: 79.5 us
  starting transfers between devices  29 us (36%)
  waiting for transfers between devices  27.1 us (34%)
  Pallas kernels  15.2 us (19%)
  local copies, waits for them, and re-layouts  4.2 us (5%)
  between operations  2.15 us (3%)
  other arithmetic  1.87 us (2%)
    ppermute x12, starting transfers between devices, shift(): lax.ppermute(x, 'group', [(i, (i + s) % n_group) for i in range(n_group)])  22.4 us
    ppermute x5, waiting for transfers between devices, pair_sum(): lax.ppermute(value, axis, [(i, i ^ step) for i in range(size)])  15 us
    pallas_call x4, Pallas kernels, one_head(): pl.pallas_call(functools.partial(head_kernel, share, rows, 2 * HD), out_s...  13.2 us
    ppermute x12, waiting for transfers between devices, shift(): lax.ppermute(x, 'group', [(i, (i + s) % n_group) for i in range(n_group)])  12.1 us
    ppermute x5, starting transfers between devices, pair_sum(): lax.ppermute(value, axis, [(i, i ^ step) for i in range(size)])  6.58 us
    unnamed x20, local copies, waits for them, and re-layouts  2.28 us
    pallas_call x1, Pallas kernels, place(): pl.pallas_call(place_kernel, out_shape=jax.ShapeDtypeStruct((depth, rows,...  2.01 us
  transfers between devices with their start and end apart: 17, of which 8 were waited for; matrix products, arithmetic and copies ran while one was open for 2% of the time, Pallas kernels for 12%

profile of v1, /device:TPU:0, one launch (start us, length us, event | category | flops | bytes accessed | tf_op | source)
XLA Modules:
  0.0 79.5 jit_solution(14951682794969813873)
XLA Ops:
  0.6 0.0 copy-start.9
  0.6 0.0 copy-start.2
  0.7 0.0 copy-start.8
  0.7 0.0 copy-start
  0.7 0.0 copy-start.1
  0.7 1.2 %dynamic-slice_bitcast_fusion = (bf16[2,256,128]{2,1,0:T(8,128)(2,1)S(1)}, bf16[2,256,128]{2,1,0:T(8,128)(2,1)S(1)}, bf16[2,256,128]{2,1,0:T(8,128)(2,1)S(1)}) fusion(bf16[1,1,2,256,512]{4,3,2,1,0:T(8,128)(2,1)} %param.14, s32[]{:T(128)S(6)} %select_n.80, s32[]{:T(128)S(6)} %select_n.76, s32[]{:T(128)S(6)} %select_n.72), kind=kLoop, calls=%fused_computation.4 | loop fusion | bytes 786444 | tf_op jit(solution)/shard_map/dynamic_slice | solution.py:204
  1.9 3.1 %collective-permute-start.2 = (bf16[2,256,128]{2,1,0:T(8,128)(2,1)S(1)}, bf16[2,256,128]{2,1,0:T(8,128)(2,1)S(1)}, u32[]{:S(2)}, u32[]{:S(2)}) collective-permute-start(bf16[2,256,128]{2,1,0:T(8,128)(2,1)S(1)} %get-tuple-element.66), channel_id=1, source_target_pairs={{0,1},{1,2},{2,3},{3,0},{4,5},{5,6},{6,7},{7,4},{8,9},{9,10},{10,1... | collective-permute-start | bytes 393224 | tf_op jit(solution)/shard_map/ppermute | solution.py:201
  5.0 2.6 %collective-permute-start.1 = (bf16[2,256,128]{2,1,0:T(8,128)(2,1)S(1)}, bf16[2,256,128]{2,1,0:T(8,128)(2,1)S(1)}, u32[]{:S(2)}, u32[]{:S(2)}) collective-permute-start(bf16[2,256,128]{2,1,0:T(8,128)(2,1)S(1)} %get-tuple-element.67), channel_id=1, source_target_pairs={{0,2},{1,3},{2,0},{3,1},{4,6},{5,7},{6,4},{7,5},{8,10},{9,11},{10,... | collective-permute-start | bytes 393224 | tf_op jit(solution)/shard_map/ppermute | solution.py:201
  7.6 1.3 %collective-permute-start = (bf16[2,256,128]{2,1,0:T(8,128)(2,1)S(1)}, bf16[2,256,128]{2,1,0:T(8,128)(2,1)S(1)}, u32[]{:S(2)}, u32[]{:S(2)}) collective-permute-start(bf16[2,256,128]{2,1,0:T(8,128)(2,1)S(1)} %get-tuple-element.68), channel_id=1, source_target_pairs={{0,3},{1,0},{2,1},{3,2},{4,7},{5,4},{6,5},{7,6},{8,11},{9,8},{10,9... | collective-permute-start | bytes 393224 | tf_op jit(solution)/shard_map/ppermute | solution.py:201
  9.6 0.0 copy-done.9
  9.6 0.0 copy-done.8
  9.6 0.1 pad_add_fusion.2.meta
  10.4 0.1 pad_add_fusion
  10.5 1.0 %collective-permute-done.2 = bf16[2,256,128]{2,1,0:T(8,128)(2,1)S(1)} collective-permute-done((bf16[2,256,128]{2,1,0:T(8,128)(2,1)S(1)}, bf16[2,256,128]{2,1,0:T(8,128)(2,1)S(1)}, u32[]{:S(2)}, u32[]{:S(2)}) %collective-permute-start.2) | collective-permute-done | bytes 131104 | tf_op jit(solution)/shard_map/ppermute | solution.py:201
  11.4 4.8 %collective-permute-done.1 = bf16[2,256,128]{2,1,0:T(8,128)(2,1)S(1)} collective-permute-done((bf16[2,256,128]{2,1,0:T(8,128)(2,1)S(1)}, bf16[2,256,128]{2,1,0:T(8,128)(2,1)S(1)}, u32[]{:S(2)}, u32[]{:S(2)}) %collective-permute-start.1) | collective-permute-done | bytes 131104 | tf_op jit(solution)/shard_map/ppermute | solution.py:201
  16.2 0.0 collective-permute-done
  16.2 1.0 %fusion.1.pr_ref = bf16[2,256,128]{2,1,0:T(8,128)(2,1)S(1)} fusion(bf16[2,256,128]{2,1,0:T(8,128)(2,1)S(1)} %collective-permute-done, bf16[2,256,128]{2,1,0:T(8,128)(2,1)S(1)} %collective-permute-done.1, bf16[2,256,128]{2,1,0:T(8,128)(2,1)S(1)} %collective-permute-done.2, bf16[1,1,2,256,512]{4,3,2,1,0:T(8,128)(2,1)} %param.14, s32[]{:T(128)S(6)} %select_n.81, ...), kind=kLoop, calls=%fused_computation.3 | loop fusion | flops 196608 | bytes 655367 | tf_op jit(solution)/shard_map/jit(_where)/select_n | solution.py:212
  17.2 3.3 %collective-permute-start.5 = (bf16[2,256,128]{2,1,0:T(8,128)(2,1)S(1)}, bf16[2,256,128]{2,1,0:T(8,128)(2,1)S(1)}, u32[]{:S(2)}, u32[]{:S(2)}) collective-permute-start(bf16[2,256,128]{2,1,0:T(8,128)(2,1)S(1)} %fusion.1.pr_ref), channel_id=1, source_target_pairs={{0,1},{1,2},{2,3},{3,0},{4,5},{5,6},{6,7},{7,4},{8,9},{9,10},{10,1... | collective-permute-start | bytes 393224 | tf_op jit(solution)/shard_map/ppermute | solution.py:201
  20.5 1.6 %collective-permute-start.4 = (bf16[2,256,128]{2,1,0:T(8,128)(2,1)S(1)}, bf16[2,256,128]{2,1,0:T(8,128)(2,1)S(1)}, u32[]{:S(2)}, u32[]{:S(2)}) collective-permute-start(bf16[2,256,128]{2,1,0:T(8,128)(2,1)S(1)} %fusion.1.pr_ref), channel_id=1, source_target_pairs={{0,2},{1,3},{2,0},{3,1},{4,6},{5,7},{6,4},{7,5},{8,10},{9,11},{10,... | collective-permute-start | bytes 393224 | tf_op jit(solution)/shard_map/ppermute | solution.py:201
  22.2 0.1 pad_add_fusion.3.meta
  22.3 0.1 copy.32.gain_ref
  22.4 0.9 %collective-permute-start.3 = (bf16[2,256,128]{2,1,0:T(8,128)(2,1)S(1)}, bf16[2,256,128]{2,1,0:T(8,128)(2,1)S(1)}, u32[]{:S(2)}, u32[]{:S(2)}) collective-permute-start(bf16[2,256,128]{2,1,0:T(8,128)(2,1)S(1)} %fusion.1.pr_ref), channel_id=1, source_target_pairs={{0,3},{1,0},{2,1},{3,2},{4,7},{5,4},{6,5},{7,6},{8,11},{9,8},{10,9... | collective-permute-start | bytes 393224 | tf_op jit(solution)/shard_map/ppermute | solution.py:201
  23.2 0.0 copy-done.2
  23.2 0.0 copy-done
  23.2 0.0 copy-done.1
  23.2 0.9 %copy-done.3 = bf16[1,1,192,512]{3,2,1,0:T(8,128)(2,1)S(1)} copy-done((bf16[1,1,192,512]{3,2,1,0:T(8,128)(2,1)S(1)}, bf16[1,1,192,512]{3,2,1,0:T(8,128)(2,1)}, u32[]{:S(2)}) %copy-start.3) | copy-done | bytes 196632
  24.2 3.3 %attend_head.4 = (bf16[192,2048]{1,0:T(8,128)(2,1)}, bf16[192,2048]{1,0:T(8,128)(2,1)}, bf16[192,512]{1,0:T(8,128)(2,1)}, bf16[192,512]{1,0:T(8,128)(2,1)}, bf16...) custom-call(s32[2]{0:T(128)S(1)} %pad_add_fusion.3.meta, bf16[192,2048]{1,0:T(8,128)(2,1)S(1)} %bitcast.38, ...), custom_call_target="tpu_custom_call" | custom-call | flops 528482304 | bytes 983040 | tf_op jit(solution)/shard_map/attend_head/pallas_call | solution.py:138
  27.5 0.0 collective-permute-done.5.pr_ref
  27.5 3.3 %attend_head.5 = (bf16[192,2048]{1,0:T(8,128)(2,1)}, bf16[192,2048]{1,0:T(8,128)(2,1)}, bf16[192,512]{1,0:T(8,128)(2,1)}, bf16[192,512]{1,0:T(8,128)(2,1)}, bf16...) custom-call(s32[2]{0:T(128)S(1)} %pad_add_fusion.2.meta, ...), custom_call_target="tpu_custom_call", output_to_operand_aliasing={{0}: (8, {}), {1}: (9, {}), {2}: (10, {}), {3}: (11, {})} | custom-call | flops 528482304 | bytes 983040 | tf_op jit(solution)/shard_map/attend_head/pallas_call | solution.py:138
  30.8 0.0 collective-permute-done.4.pr_ref
  30.8 3.3 %attend_head.6 = (bf16[192,2048]{1,0:T(8,128)(2,1)}, bf16[192,2048]{1,0:T(8,128)(2,1)}, bf16[192,512]{1,0:T(8,128)(2,1)}, bf16[192,512]{1,0:T(8,128)(2,1)}, bf16...) custom-call(s32[2]{0:T(128)S(1)} %get-tuple-element.70.meta, ...), custom_call_target="tpu_custom_call", output_to_operand_aliasing={{0}: (8, {}), {1}: (9, {}), {2}: (10, {}), {3}: (11, {})} | custom-call | flops 528482304 | bytes 983040 | tf_op jit(solution)/shard_map/attend_head/pallas_call | solution.py:138
  34.0 0.0 collective-permute-done.3.pr_ref
  34.0 3.3 %attend_head.7 = (bf16[192,2048]{1,0:T(8,128)(2,1)}, bf16[192,2048]{1,0:T(8,128)(2,1)}, bf16[192,512]{1,0:T(8,128)(2,1)}, bf16[192,512]{1,0:T(8,128)(2,1)}, bf16...) custom-call(s32[2]{0:T(128)S(1)} %get-tuple-element.69.meta, ...), custom_call_target="tpu_custom_call", output_to_operand_aliasing={{0}: (8, {}), {1}: (9, {}), {2}: (10, {}), {3}: (11, {})} | custom-call | flops 528482304 | bytes 983040 | tf_op jit(solution)/shard_map/attend_head/pallas_call | solution.py:138
  37.3 1.4 %collective-permute-start.8 = (bf16[2,256,128]{2,1,0:T(8,128)(2,1)S(1)}, bf16[2,256,128]{2,1,0:T(8,128)(2,1)S(1)}, u32[]{:S(2)}, u32[]{:S(2)}) collective-permute-start(bf16[2,256,128]{2,1,0:T(8,128)(2,1)S(1)} %get-tuple-element.64), channel_id=1, source_target_pairs={{0,1},{1,2},{2,3},{3,0},{4,5},{5,6},{6,7},{7,4},{8,9},{9,10},{10,1... | collective-permute-start | bytes 393224 | tf_op jit(solution)/shard_map/ppermute | solution.py:201
  38.8 3.4 %collective-permute-start.7 = (bf16[2,256,128]{2,1,0:T(8,128)(2,1)S(1)}, bf16[2,256,128]{2,1,0:T(8,128)(2,1)S(1)}, u32[]{:S(2)}, u32[]{:S(2)}) collective-permute-start(bf16[2,256,128]{2,1,0:T(8,128)(2,1)S(1)} %get-tuple-element.63), channel_id=1, source_target_pairs={{0,2},{1,3},{2,0},{3,1},{4,6},{5,7},{6,4},{7,5},{8,10},{9,11},{10,... | collective-permute-start | bytes 393224 | tf_op jit(solution)/shard_map/ppermute | solution.py:201
  42.2 0.0 collective-permute-start.6
  42.2 2.0 %collective-permute-start.12 = (f32[2,128]{1,0:T(2,128)S(1)}, f32[2,128]{1,0:T(2,128)S(1)}, u32[]{:S(2)}, u32[]{:S(2)}) collective-permute-start(f32[2,128]{1,0:T(2,128)S(1)} %slice.17), channel_id=1, source_target_pairs={{0,1},{1,0},{2,3},{3,2},{4,5},{5,4},{6,7},{7,6},{8,9},{9,8},{10,11... | collective-permute-start | bytes 3080 | tf_op jit(solution)/shard_map/ppermute | solution.py:182
  44.2 1.9 %collective-permute-done.8 = bf16[2,256,128]{2,1,0:T(8,128)(2,1)S(1)} collective-permute-done((bf16[2,256,128]{2,1,0:T(8,128)(2,1)S(1)}, bf16[2,256,128]{2,1,0:T(8,128)(2,1)S(1)}, u32[]{:S(2)}, u32[]{:S(2)}) %collective-permute-start.8) | collective-permute-done | bytes 131104 | tf_op jit(solution)/shard_map/ppermute | solution.py:201
  46.1 4.4 %collective-permute-done.7 = bf16[2,256,128]{2,1,0:T(8,128)(2,1)S(1)} collective-permute-done((bf16[2,256,128]{2,1,0:T(8,128)(2,1)S(1)}, bf16[2,256,128]{2,1,0:T(8,128)(2,1)S(1)}, u32[]{:S(2)}, u32[]{:S(2)}) %collective-permute-start.7) | collective-permute-done | bytes 131104 | tf_op jit(solution)/shard_map/ppermute | solution.py:201
  50.5 0.0 collective-permute-done.6
  50.5 0.1 add_convert_fusion.refs_0_
  50.5 0.0 copy-start.4
  50.5 2.7 %collective-permute-start.11 = (bf16[2,256,128]{2,1,0:T(8,128)(2,1)S(1)}, bf16[2,256,128]{2,1,0:T(8,128)(2,1)S(1)}, u32[]{:S(2)}, u32[]{:S(2)}) collective-permute-start(bf16[2,256,128]{2,1,0:T(8,128)(2,1)S(1)} %add_convert_fusion.refs_0_), channel_id=1, source_target_pairs={{0,3},{1,0},{2,1},{3,2},{4,7},{5,4},{6,5},{7,6},{8,11},{9,8},{10,9... | collective-permute-start | bytes 393224 | tf_op jit(solution)/shard_map/ppermute | solution.py:201
  53.2 2.1 %collective-permute-start.10 = (bf16[2,256,128]{2,1,0:T(8,128)(2,1)S(1)}, bf16[2,256,128]{2,1,0:T(8,128)(2,1)S(1)}, u32[]{:S(2)}, u32[]{:S(2)}) collective-permute-start(bf16[2,256,128]{2,1,0:T(8,128)(2,1)S(1)} %add_convert_fusion.refs_0_), channel_id=1, source_target_pairs={{0,2},{1,3},{2,0},{3,1},{4,6},{5,7},{6,4},{7,5},{8,10},{9,11},{10,... | collective-permute-start | bytes 393224 | tf_op jit(solution)/shard_map/ppermute | solution.py:201
  55.3 0.0 collective-permute-start.9
  55.3 0.0 collective-permute-done.12
  55.3 1.5 %collective-permute-start.13 = (f32[2,128]{1,0:T(2,128)S(1)}, f32[2,128]{1,0:T(2,128)S(1)}, u32[]{:S(2)}, u32[]{:S(2)}) collective-permute-start(f32[2,128]{1,0:T(2,128)S(1)} %slice_add_fusion), channel_id=1, source_target_pairs={{0,2},{1,3},{2,0},{3,1},{4,6},{5,7},{6,4},{7,5},{8,10},{9,11},{10,... | collective-permute-start | bytes 3080 | tf_op jit(solution)/shard_map/ppermute | solution.py:182
  56.9 10.3 %collective-permute-done.13 = f32[2,128]{1,0:T(2,128)S(1)} collective-permute-done((f32[2,128]{1,0:T(2,128)S(1)}, f32[2,128]{1,0:T(2,128)S(1)}, u32[]{:S(2)}, u32[]{:S(2)}) %collective-permute-start.13) | collective-permute-done | bytes 1056 | tf_op jit(solution)/shard_map/ppermute | solution.py:182
  67.2 0.0 collective-permute-start.14
  67.2 1.1 %collective-permute-done.14 = f32[2,128]{1,0:T(2,128)S(1)} collective-permute-done((f32[2,128]{1,0:T(2,128)S(1)}, f32[2,128]{1,0:T(2,128)S(1)}, u32[]{:S(2)}, u32[]{:S(2)}) %collective-permute-start.14) | collective-permute-done | bytes 1056 | tf_op jit(solution)/shard_map/ppermute | solution.py:182
  68.4 1.5 %collective-permute-start.15 = (f32[2,128]{1,0:T(2,128)S(1)}, f32[2,128]{1,0:T(2,128)S(1)}, u32[]{:S(2)}, u32[]{:S(2)}) collective-permute-start(f32[2,128]{1,0:T(2,128)S(1)} %add.96), channel_id=1, source_target_pairs={{0,8},{4,12},{8,0},{12,4},{16,24},{20,28},{24,16},{28,20},{1,9},{5... | collective-permute-start | bytes 3080 | tf_op jit(solution)/shard_map/ppermute | solution.py:182
  69.9 2.1 %collective-permute-done.15 = f32[2,128]{1,0:T(2,128)S(1)} collective-permute-done((f32[2,128]{1,0:T(2,128)S(1)}, f32[2,128]{1,0:T(2,128)S(1)}, u32[]{:S(2)}, u32[]{:S(2)}) %collective-permute-start.15) | collective-permute-done | bytes 1056 | tf_op jit(solution)/shard_map/ppermute | solution.py:182
  72.0 1.5 %collective-permute-start.16 = (f32[2,128]{1,0:T(2,128)S(1)}, f32[2,128]{1,0:T(2,128)S(1)}, u32[]{:S(2)}, u32[]{:S(2)}) collective-permute-start(f32[2,128]{1,0:T(2,128)S(1)} %add.97), channel_id=1, source_target_pairs={{0,16},{4,20},{8,24},{12,28},{16,0},{20,4},{24,8},{28,12},{1,17},{... | collective-permute-start | bytes 3080 | tf_op jit(solution)/shard_map/ppermute | solution.py:182
  73.5 0.6 stack.59.meta
  74.1 1.4 %collective-permute-done.16 = f32[2,128]{1,0:T(2,128)S(1)} collective-permute-done((f32[2,128]{1,0:T(2,128)S(1)}, f32[2,128]{1,0:T(2,128)S(1)}, u32[]{:S(2)}, u32[]{:S(2)}) %collective-permute-start.16) | collective-permute-done | bytes 1056 | tf_op jit(solution)/shard_map/ppermute | solution.py:182
  75.5 0.6 add.98
  76.1 0.0 collective-permute-done.11.refs_3_
  76.1 0.0 collective-permute-done.10.refs_2_
  76.1 0.0 copy-start.6
  76.1 0.0 collective-permute-done.9.refs_1_
  76.1 0.6 copy-done.5
  76.8 0.1 copy-done.6
  76.8 0.7 copy-done.7
  77.5 2.0 %place_prompt_grad.1 = bf16[2,256,512]{2,1,0:T(8,128)(2,1)} custom-call(s32[5]{0:T(128)} %stack.59.meta, bf16[2,256,128]{2,1,0:T(8,128)(2,1)} %copy-done.4, bf16[2,256,128]{2,1,0:T(8,128)(2,1)} %copy-done.7, bf16[2,256,128]{2,1,0:T(8,128)(2,1)} %copy-done.6, bf16[2,256,128]{2,1,0:T(8,128)(2,1)} %copy-done.5), custom_call_target="tpu_custom_call" | custom-call | tf_op jit(solution)/shard_map/place_prompt_grad/pallas_call | solution.py:169
  (11 shorter events, 0.0 us)
Async XLA Ops:
  0.6 9.0 %copy-start.9 = (f32[128]{0:T(128)S(1)}, f32[128]{0:T(128)}, u32[]{:S(2)}) copy-start(f32[128]{0:T(128)} %param.17) | copy-start | bytes 1540
  0.6 22.6 %copy-start.2 = (bf16[1,1,192,512]{3,2,1,0:T(8,128)(2,1)S(1)}, bf16[1,1,192,512]{3,2,1,0:T(8,128)(2,1)}, u32[]{:S(2)}) copy-start(bf16[1,1,192,512]{3,2,1,0:T(8,128)(2,1)} %param.12) | copy-start | bytes 589828
  0.7 8.9 %copy-start.8 = (f32[128]{0:T(128)S(1)}, f32[128]{0:T(128)}, u32[]{:S(2)}) copy-start(f32[128]{0:T(128)} %param.18) | copy-start | bytes 1540
  0.7 22.5 %copy-start = (bf16[1,1,192,2048]{3,2,1,0:T(8,128)(2,1)S(1)}, bf16[1,1,192,2048]{3,2,1,0:T(8,128)(2,1)}, u32[]{:S(2)}) copy-start(bf16[1,1,192,2048]{3,2,1,0:T(8,128)(2,1)} %param.11) | copy-start | bytes 2359300
  0.7 22.5 %copy-start.1 = (bf16[1,1,192,2048]{3,2,1,0:T(8,128)(2,1)S(1)}, bf16[1,1,192,2048]{3,2,1,0:T(8,128)(2,1)}, u32[]{:S(2)}) copy-start(bf16[1,1,192,2048]{3,2,1,0:T(8,128)(2,1)} %param.19) | copy-start | bytes 2359300
  1.9 9.5 %collective-permute-start.2 = (bf16[2,256,128]{2,1,0:T(8,128)(2,1)S(1)}, bf16[2,256,128]{2,1,0:T(8,128)(2,1)S(1)}, u32[]{:S(2)}, u32[]{:S(2)}) collective-permute-start(bf16[2,256,128]{2,1,0:T(8,128)(2,1)S(1)} %get-tuple-element.66), channel_id=1, source_target_pairs={{0,1},{1,2},{2,3},{3,0},{4,5},{5,6},{6,7},{7,4},{8,9},{9,10},{10,1... | collective-permute-start | bytes 393224 | tf_op jit(solution)/shard_map/ppermute | solution.py:201
  5.0 11.2 %collective-permute-start.1 = (bf16[2,256,128]{2,1,0:T(8,128)(2,1)S(1)}, bf16[2,256,128]{2,1,0:T(8,128)(2,1)S(1)}, u32[]{:S(2)}, u32[]{:S(2)}) collective-permute-start(bf16[2,256,128]{2,1,0:T(8,128)(2,1)S(1)} %get-tuple-element.67), channel_id=1, source_target_pairs={{0,2},{1,3},{2,0},{3,1},{4,6},{5,7},{6,4},{7,5},{8,10},{9,11},{10,... | collective-permute-start | bytes 393224 | tf_op jit(solution)/shard_map/ppermute | solution.py:201
  7.6 8.6 %collective-permute-start = (bf16[2,256,128]{2,1,0:T(8,128)(2,1)S(1)}, bf16[2,256,128]{2,1,0:T(8,128)(2,1)S(1)}, u32[]{:S(2)}, u32[]{:S(2)}) collective-permute-start(bf16[2,256,128]{2,1,0:T(8,128)(2,1)S(1)} %get-tuple-element.68), channel_id=1, source_target_pairs={{0,3},{1,0},{2,1},{3,2},{4,7},{5,4},{6,5},{7,6},{8,11},{9,8},{10,9... | collective-permute-start | bytes 393224 | tf_op jit(solution)/shard_map/ppermute | solution.py:201
  17.2 10.2 %collective-permute-start.5 = (bf16[2,256,128]{2,1,0:T(8,128)(2,1)S(1)}, bf16[2,256,128]{2,1,0:T(8,128)(2,1)S(1)}, u32[]{:S(2)}, u32[]{:S(2)}) collective-permute-start(bf16[2,256,128]{2,1,0:T(8,128)(2,1)S(1)} %fusion.1.pr_ref), channel_id=1, source_target_pairs={{0,1},{1,2},{2,3},{3,0},{4,5},{5,6},{6,7},{7,4},{8,9},{9,10},{10,1... | collective-permute-start | bytes 393224 | tf_op jit(solution)/shard_map/ppermute | solution.py:201
  20.5 10.2 %collective-permute-start.4 = (bf16[2,256,128]{2,1,0:T(8,128)(2,1)S(1)}, bf16[2,256,128]{2,1,0:T(8,128)(2,1)S(1)}, u32[]{:S(2)}, u32[]{:S(2)}) collective-permute-start(bf16[2,256,128]{2,1,0:T(8,128)(2,1)S(1)} %fusion.1.pr_ref), channel_id=1, source_target_pairs={{0,2},{1,3},{2,0},{3,1},{4,6},{5,7},{6,4},{7,5},{8,10},{9,11},{10,... | collective-permute-start | bytes 393224 | tf_op jit(solution)/shard_map/ppermute | solution.py:201
  22.4 11.7 %collective-permute-start.3 = (bf16[2,256,128]{2,1,0:T(8,128)(2,1)S(1)}, bf16[2,256,128]{2,1,0:T(8,128)(2,1)S(1)}, u32[]{:S(2)}, u32[]{:S(2)}) collective-permute-start(bf16[2,256,128]{2,1,0:T(8,128)(2,1)S(1)} %fusion.1.pr_ref), channel_id=1, source_target_pairs={{0,3},{1,0},{2,1},{3,2},{4,7},{5,4},{6,5},{7,6},{8,11},{9,8},{10,9... | collective-permute-start | bytes 393224 | tf_op jit(solution)/shard_map/ppermute | solution.py:201
  23.2 0.9 %copy-start.3 = (bf16[1,1,192,512]{3,2,1,0:T(8,128)(2,1)S(1)}, bf16[1,1,192,512]{3,2,1,0:T(8,128)(2,1)}, u32[]{:S(2)}) copy-start(bf16[1,1,192,512]{3,2,1,0:T(8,128)(2,1)} %param.13) | copy-start | bytes 589828
  37.3 8.7 %collective-permute-start.8 = (bf16[2,256,128]{2,1,0:T(8,128)(2,1)S(1)}, bf16[2,256,128]{2,1,0:T(8,128)(2,1)S(1)}, u32[]{:S(2)}, u32[]{:S(2)}) collective-permute-start(bf16[2,256,128]{2,1,0:T(8,128)(2,1)S(1)} %get-tuple-element.64), channel_id=1, source_target_pairs={{0,1},{1,2},{2,3},{3,0},{4,5},{5,6},{6,7},{7,4},{8,9},{9,10},{10,1... | collective-permute-start | bytes 393224 | tf_op jit(solution)/shard_map/ppermute | solution.py:201
  38.8 11.7 %collective-permute-start.7 = (bf16[2,256,128]{2,1,0:T(8,128)(2,1)S(1)}, bf16[2,256,128]{2,1,0:T(8,128)(2,1)S(1)}, u32[]{:S(2)}, u32[]{:S(2)}) collective-permute-start(bf16[2,256,128]{2,1,0:T(8,128)(2,1)S(1)} %get-tuple-element.63), channel_id=1, source_target_pairs={{0,2},{1,3},{2,0},{3,1},{4,6},{5,7},{6,4},{7,5},{8,10},{9,11},{10,... | collective-permute-start | bytes 393224 | tf_op jit(solution)/shard_map/ppermute | solution.py:201
  42.2 8.3 %collective-permute-start.6 = (bf16[2,256,128]{2,1,0:T(8,128)(2,1)S(1)}, bf16[2,256,128]{2,1,0:T(8,128)(2,1)S(1)}, u32[]{:S(2)}, u32[]{:S(2)}) collective-permute-start(bf16[2,256,128]{2,1,0:T(8,128)(2,1)S(1)} %get-tuple-element.62), channel_id=1, source_target_pairs={{0,3},{1,0},{2,1},{3,2},{4,7},{5,4},{6,5},{7,6},{8,11},{9,8},{10,9... | collective-permute-start | bytes 393224 | tf_op jit(solution)/shard_map/ppermute | solution.py:201
  42.2 13.2 %collective-permute-start.12 = (f32[2,128]{1,0:T(2,128)S(1)}, f32[2,128]{1,0:T(2,128)S(1)}, u32[]{:S(2)}, u32[]{:S(2)}) collective-permute-start(f32[2,128]{1,0:T(2,128)S(1)} %slice.17), channel_id=1, source_target_pairs={{0,1},{1,0},{2,3},{3,2},{4,5},{5,4},{6,7},{7,6},{8,9},{9,8},{10,11... | collective-permute-start | bytes 3080 | tf_op jit(solution)/shard_map/ppermute | solution.py:182
  50.5 25.6 %copy-start.4 = (bf16[2,256,128]{2,1,0:T(8,128)(2,1)}, bf16[2,256,128]{2,1,0:T(8,128)(2,1)S(1)}, u32[]{:S(2)}) copy-start(bf16[2,256,128]{2,1,0:T(8,128)(2,1)S(1)} %add_convert_fusion.refs_0_) | copy-start | bytes 393220
  50.5 25.5 %collective-permute-start.11 = (bf16[2,256,128]{2,1,0:T(8,128)(2,1)S(1)}, bf16[2,256,128]{2,1,0:T(8,128)(2,1)S(1)}, u32[]{:S(2)}, u32[]{:S(2)}) collective-permute-start(bf16[2,256,128]{2,1,0:T(8,128)(2,1)S(1)} %add_convert_fusion.refs_0_), channel_id=1, source_target_pairs={{0,3},{1,0},{2,1},{3,2},{4,7},{5,4},{6,5},{7,6},{8,11},{9,8},{10,9... | collective-permute-start | bytes 393224 | tf_op jit(solution)/shard_map/ppermute | solution.py:201
  53.2 22.9 %collective-permute-start.10 = (bf16[2,256,128]{2,1,0:T(8,128)(2,1)S(1)}, bf16[2,256,128]{2,1,0:T(8,128)(2,1)S(1)}, u32[]{:S(2)}, u32[]{:S(2)}) collective-permute-start(bf16[2,256,128]{2,1,0:T(8,128)(2,1)S(1)} %add_convert_fusion.refs_0_), channel_id=1, source_target_pairs={{0,2},{1,3},{2,0},{3,1},{4,6},{5,7},{6,4},{7,5},{8,10},{9,11},{10,... | collective-permute-start | bytes 393224 | tf_op jit(solution)/shard_map/ppermute | solution.py:201
  55.3 20.8 %collective-permute-start.9 = (bf16[2,256,128]{2,1,0:T(8,128)(2,1)S(1)}, bf16[2,256,128]{2,1,0:T(8,128)(2,1)S(1)}, u32[]{:S(2)}, u32[]{:S(2)}) collective-permute-start(bf16[2,256,128]{2,1,0:T(8,128)(2,1)S(1)} %add_convert_fusion.refs_0_), channel_id=1, source_target_pairs={{0,1},{1,2},{2,3},{3,0},{4,5},{5,6},{6,7},{7,4},{8,9},{9,10},{10,1... | collective-permute-start | bytes 393224 | tf_op jit(solution)/shard_map/ppermute | solution.py:201
  55.3 11.9 %collective-permute-start.13 = (f32[2,128]{1,0:T(2,128)S(1)}, f32[2,128]{1,0:T(2,128)S(1)}, u32[]{:S(2)}, u32[]{:S(2)}) collective-permute-start(f32[2,128]{1,0:T(2,128)S(1)} %slice_add_fusion), channel_id=1, source_target_pairs={{0,2},{1,3},{2,0},{3,1},{4,6},{5,7},{6,4},{7,5},{8,10},{9,11},{10,... | collective-permute-start | bytes 3080 | tf_op jit(solution)/shard_map/ppermute | solution.py:182
  67.2 1.1 %collective-permute-start.14 = (f32[2,128]{1,0:T(2,128)S(1)}, f32[2,128]{1,0:T(2,128)S(1)}, u32[]{:S(2)}, u32[]{:S(2)}) collective-permute-start(f32[2,128]{1,0:T(2,128)S(1)} %add.95), channel_id=1, source_target_pairs={{0,4},{4,0},{8,12},{12,8},{16,20},{20,16},{24,28},{28,24},{1,5},{5... | collective-permute-start | bytes 3080 | tf_op jit(solution)/shard_map/ppermute | solution.py:182
  68.4 3.6 %collective-permute-start.15 = (f32[2,128]{1,0:T(2,128)S(1)}, f32[2,128]{1,0:T(2,128)S(1)}, u32[]{:S(2)}, u32[]{:S(2)}) collective-permute-start(f32[2,128]{1,0:T(2,128)S(1)} %add.96), channel_id=1, source_target_pairs={{0,8},{4,12},{8,0},{12,4},{16,24},{20,28},{24,16},{28,20},{1,9},{5... | collective-permute-start | bytes 3080 | tf_op jit(solution)/shard_map/ppermute | solution.py:182
  72.0 3.6 %collective-permute-start.16 = (f32[2,128]{1,0:T(2,128)S(1)}, f32[2,128]{1,0:T(2,128)S(1)}, u32[]{:S(2)}, u32[]{:S(2)}) collective-permute-start(f32[2,128]{1,0:T(2,128)S(1)} %add.97), channel_id=1, source_target_pairs={{0,16},{4,20},{8,24},{12,28},{16,0},{20,4},{24,8},{28,12},{1,17},{... | collective-permute-start | bytes 3080 | tf_op jit(solution)/shard_map/ppermute | solution.py:182
  76.1 0.7 copy-start.5
  76.1 0.7 copy-start.6
  76.8 0.7 copy-start.7

commit v2 on v1

--- a/solution.py
+++ b/solution.py
@@ -156,24 +156,72 @@
     return outs[:4], outs[4], outs[5]
 
 
+TAIL = 16
+
+
+def join_kernel(own_ref, *rest):
+    backs, gains_ref, out_ref = rest[:-2], rest[-2], rest[-1]
+    depth, rows, _ = own_ref.shape
+    for d in range(depth):
+        total = own_ref[d].astype(F32)
+        for back in backs:
+            total = total + back[d].astype(F32)
+        out_ref[d * rows : (d + 1) * rows, :] = total.astype(BF)
+    gains = gains_ref[...]
+    high = gains.astype(BF)
+    gains = gains - high.astype(F32)
+    middle = gains.astype(BF)
+    low = (gains - middle.astype(F32)).astype(BF)
+    pieces = jnp.concatenate([p[0:2].astype(F32) for p in (high, middle, low)], axis=0)
+    pad = jnp.zeros((TAIL - pieces.shape[0], HD), F32)
+    out_ref[depth * rows :, :] = jnp.concatenate([pieces, pad], axis=0).astype(BF)
+
+
+def join(own, backs, gains):
+    depth, rows, _ = own.shape
+    vmem = pl.BlockSpec(memory_space=pltpu.VMEM)
+    return pl.pallas_call(
+        join_kernel,
+        out_shape=jax.ShapeDtypeStruct((depth * rows + TAIL, HD), BF),
+        in_specs=[vmem] * (2 + len(backs)),
+        out_specs=vmem,
+        compiler_params=pltpu.CompilerParams(vmem_limit_bytes=8 * 2**20),
+        name="join_parts",
+    )(own, *backs, gains)
+
+
 def place_kernel(meta, *refs):
-    out_ref = refs[-1]
+    payloads, out_ref, gain_ref, stage = refs[:-3], refs[-3], refs[-2], refs[-1]
     mine = meta[0] > 0
-    for i, ref in enumerate(refs[:-1]):
+    depth, rows, _ = out_ref.shape
+    for i, ref in enumerate(payloads):
         at = pl.multiple_of(meta[1 + i] * HD, HD)
-        out_ref[:, :, pl.ds(at, HD)] = jnp.where(mine, ref[...], jnp.zeros((), BF))
-
-
-def place(meta, heads):
-    depth, rows, _ = heads[0].shape
+        for d in range(depth):
+            block = ref[d * rows : (d + 1) * rows, :]
+            out_ref[d, :, pl.ds(at, HD)] = jnp.where(mine, block, jnp.zeros_like(block))
+        tail = ref[depth * rows :, :].astype(F32)
+        stage[meta[1 + i]] = tail[0:2] + tail[2:4] + tail[4:6]
+    total = stage[0]
+    for i in range(1, len(payloads)):
+        total = total + stage[i]
+    gain_ref[...] = total
+
+
+def place(meta, payloads, depth, rows):
+    count = len(payloads)
+    vmem = pl.BlockSpec(memory_space=pltpu.VMEM)
     return pl.pallas_call(
         place_kernel,
-        out_shape=jax.ShapeDtypeStruct((depth, rows, HD * len(heads)), BF),
-        in_specs=[pl.BlockSpec(memory_space=pltpu.SMEM)]
-        + [pl.BlockSpec(memory_space=pltpu.VMEM)] * len(heads),
-        out_specs=pl.BlockSpec(memory_space=pltpu.VMEM),
+        out_shape=[
+            jax.ShapeDtypeStruct((depth, rows, HD * count), BF),
+            jax.ShapeDtypeStruct((2, HD), F32),
+        ],
+        in_specs=[pl.BlockSpec(memory_space=pltpu.SMEM)] + [vmem] * count,
+        out_specs=[vmem, vmem],
+        scratch_shapes=[pltpu.VMEM((count, 2, HD), F32)],
+        compiler_params=pltpu.CompilerParams(vmem_limit_bytes=8 * 2**20),
         name="place_prompt_grad",
-    )(meta, *heads)
+    )(meta, *payloads)
 
 
 def pair_sum(value, axis, size):
@@ -219,26 +267,26 @@
 
     gain_cols = jnp.stack([q_gain, k_gain], axis=1)
     acc = jnp.zeros((8, HD), F32).at[2].set(k_gain)
-    buffers, parts = (), []
-    for head, prompt in zip(order, prompts):
+    buffers, parts, backs = (), [], []
+    for s, (head, prompt) in enumerate(zip(order, prompts)):
+        if direct and s == n_group - 1:
+            prompt, backs[0] = lax.optimization_barrier((prompt, backs[0]))
         meta = jnp.stack([head, live_len]).astype(jnp.int32)
         buffers, part, acc = one_head(meta, q, g, k, v, prompt, gain_cols, acc, buffers, kv_heads)
         parts.append(part)
-
+        if direct and s > 0:
+            backs.append(shift(part, -s))
+
+    mine_flag = (me == owner).astype(jnp.int32)
     if direct:
-        back = [shift(parts[s], -s).astype(F32) for s in range(1, n_group)]
-        total = parts[0].astype(F32)
-        for b in back:
-            total = total + b
-        total = total.astype(BF)
-        heads = [total] + [shift(total, s) for s in range(1, n_group)]
+        payload = join(parts[0], backs, pair_sum(acc, "dp", n_dp))
+        payloads = [payload] + [shift(payload, s) for s in range(1, n_group)]
+        meta = jnp.stack([mine_flag] + order).astype(jnp.int32)
+        placed, gains = place(meta, payloads, depth, p_rows)
     else:
         total = lax.psum(jnp.concatenate(parts, axis=-1).astype(F32), "group").astype(BF)
-        heads = [head_of(total, h) for h in order]
-    flag = (me == owner).astype(jnp.int32)
-    placed = place(jnp.stack([flag] + order).astype(jnp.int32), heads)
-
-    gains = pair_sum(pair_sum(acc[:2], "group", n_group), "dp", n_dp)
+        placed = jnp.where(mine_flag > 0, total, jnp.zeros((), BF))
+        gains = pair_sum(pair_sum(acc[:2], "dp", n_dp), "group", n_group)
     attended, d_query, d_key, d_value = buffers
     return (
         attended[None, None],

time: 79.7 us -> 66.1 us (0.83)
  waiting for transfers between devices: 27.1 us -> 20.7 us
  starting transfers between devices: 29 us -> 23.8 us
  local copies, waits for them, and re-layouts: 4.2 us -> 3.26 us
    ppermute x5 -> x3, waiting for transfers between devices: 15 us -> 5.37 us  [pair_sum(): lax.ppermute(value, axis, [(i, i ^ step) for i in range(size)])]
    ppermute x5 -> x3, starting transfers between devices: 6.58 us -> 3.01 us  [pair_sum(): lax.ppermute(value, axis, [(i, i ^ step) for i in range(size)])]
    ppermute x12, waiting for transfers between devices: 12.1 us -> 15.4 us  [shift(): lax.ppermute(x, 'group', [(i, (i + s) % n_group) for i in range(n_group)])]
    ppermute x12, starting transfers between devices: 22.4 us -> 20.8 us  [shift(): lax.ppermute(x, 'group', [(i, (i + s) % n_group) for i in range(n_group)])]
    pallas_call x1 -> x2, Pallas kernels: 2.01 us -> 1.53 us  [the longest x1 1.45 us: place(): pl.pallas_call(place_kernel, out_shape=[jax.ShapeDtypeStruct((depth, rows...]
    unnamed x20 -> x12, local copies, waits for them, and re-layouts: 2.28 us -> 1.87 us
  transfers between devices with their start and end apart: 17 -> 15, of which waited for: 8 -> 7; matrix products, arithmetic and copies ran while one was open for 2% -> 1% of each run, Pallas kernels for 12% -> 20%
where the time goes in v2:
time: 66.1 us; the launch traced here: 65.8 us
  starting transfers between devices  23.8 us (36%)
  waiting for transfers between devices  20.7 us (31%)
  Pallas kernels  14.7 us (22%)
  local copies, waits for them, and re-layouts  3.26 us (5%)
  between operations  2.15 us (3%)
  other arithmetic  1.22 us (2%)
    ppermute x12, starting transfers between devices, shift(): lax.ppermute(x, 'group', [(i, (i + s) % n_group) for i in range(n_group)])  20.8 us
    ppermute x12, waiting for transfers between devices, shift(): lax.ppermute(x, 'group', [(i, (i + s) % n_group) for i in range(n_group)])  15.4 us
    pallas_call x4, Pallas kernels, one_head(): pl.pallas_call(functools.partial(head_kernel, share, rows, 2 * HD), out_s...  13.2 us
    ppermute x3, waiting for transfers between devices, pair_sum(): lax.ppermute(value, axis, [(i, i ^ step) for i in range(size)])  5.37 us
    ppermute x3, starting transfers between devices, pair_sum(): lax.ppermute(value, axis, [(i, i ^ step) for i in range(size)])  3.01 us
    unnamed x12, local copies, waits for them, and re-layouts  1.87 us
    pallas_call x1, Pallas kernels, place(): pl.pallas_call(place_kernel, out_shape=[jax.ShapeDtypeStruct((depth, rows...  1.45 us
  transfers between devices with their start and end apart: 15, of which 7 were waited for; matrix products, arithmetic and copies ran while one was open for 1% of the time, Pallas kernels for 20%

profile of v2, /device:TPU:0, one launch (start us, length us, event | category | flops | bytes accessed | tf_op | source)
XLA Modules:
  0.0 65.8 jit_solution(5121209055514884060)
XLA Ops:
  0.7 0.0 copy-start.4
  0.7 0.0 copy-start.5
  0.7 0.0 copy-start
  0.7 0.0 copy-start.1
  0.7 1.2 %dynamic-slice_bitcast_fusion = (bf16[2,256,128]{2,1,0:T(8,128)(2,1)S(1)}, bf16[2,256,128]{2,1,0:T(8,128)(2,1)S(1)}, bf16[2,256,128]{2,1,0:T(8,128)(2,1)S(1)}) fusion(bf16[1,1,2,256,512]{4,3,2,1,0:T(8,128)(2,1)} %param.14, s32[]{:T(128)S(6)} %select_n.80, s32[]{:T(128)S(6)} %select_n.76, s32[]{:T(128)S(6)} %select_n.72), kind=kLoop, calls=%fused_computation.3 | loop fusion | bytes 786444 | tf_op jit(solution)/shard_map/dynamic_slice | solution.py:252
  1.9 3.1 %collective-permute-start.2 = (bf16[2,256,128]{2,1,0:T(8,128)(2,1)S(1)}, bf16[2,256,128]{2,1,0:T(8,128)(2,1)S(1)}, u32[]{:S(2)}, u32[]{:S(2)}) collective-permute-start(bf16[2,256,128]{2,1,0:T(8,128)(2,1)S(1)} %get-tuple-element.74), channel_id=1, source_target_pairs={{0,1},{1,2},{2,3},{3,0},{4,5},{5,6},{6,7},{7,4},{8,9},{9,10},{10,1... | collective-permute-start | bytes 393224 | tf_op jit(solution)/shard_map/ppermute | solution.py:249
  5.0 2.6 %collective-permute-start.1 = (bf16[2,256,128]{2,1,0:T(8,128)(2,1)S(1)}, bf16[2,256,128]{2,1,0:T(8,128)(2,1)S(1)}, u32[]{:S(2)}, u32[]{:S(2)}) collective-permute-start(bf16[2,256,128]{2,1,0:T(8,128)(2,1)S(1)} %get-tuple-element.75), channel_id=1, source_target_pairs={{0,2},{1,3},{2,0},{3,1},{4,6},{5,7},{6,4},{7,5},{8,10},{9,11},{10,... | collective-permute-start | bytes 393224 | tf_op jit(solution)/shard_map/ppermute | solution.py:249
  7.6 1.3 %collective-permute-start = (bf16[2,256,128]{2,1,0:T(8,128)(2,1)S(1)}, bf16[2,256,128]{2,1,0:T(8,128)(2,1)S(1)}, u32[]{:S(2)}, u32[]{:S(2)}) collective-permute-start(bf16[2,256,128]{2,1,0:T(8,128)(2,1)S(1)} %get-tuple-element.76), channel_id=1, source_target_pairs={{0,3},{1,0},{2,1},{3,2},{4,7},{5,4},{6,5},{7,6},{8,11},{9,8},{10,9... | collective-permute-start | bytes 393224 | tf_op jit(solution)/shard_map/ppermute | solution.py:249
  8.9 0.0 copy-done.4
  8.9 0.0 copy-done.5
  10.3 0.1 copy.30.gain_ref
  10.5 0.1 pad_add_fusion.1
  10.5 0.9 %collective-permute-done.2 = bf16[2,256,128]{2,1,0:T(8,128)(2,1)S(1)} collective-permute-done((bf16[2,256,128]{2,1,0:T(8,128)(2,1)S(1)}, bf16[2,256,128]{2,1,0:T(8,128)(2,1)S(1)}, u32[]{:S(2)}, u32[]{:S(2)}) %collective-permute-start.2) | collective-permute-done | bytes 131104 | tf_op jit(solution)/shard_map/ppermute | solution.py:249
  11.4 4.8 %collective-permute-done.1 = bf16[2,256,128]{2,1,0:T(8,128)(2,1)S(1)} collective-permute-done((bf16[2,256,128]{2,1,0:T(8,128)(2,1)S(1)}, bf16[2,256,128]{2,1,0:T(8,128)(2,1)S(1)}, u32[]{:S(2)}, u32[]{:S(2)}) %collective-permute-start.1) | collective-permute-done | bytes 131104 | tf_op jit(solution)/shard_map/ppermute | solution.py:249
  16.2 0.0 collective-permute-done
  16.2 1.0 %fusion.1.pr_ref = bf16[2,256,128]{2,1,0:T(8,128)(2,1)S(1)} fusion(bf16[2,256,128]{2,1,0:T(8,128)(2,1)S(1)} %collective-permute-done, bf16[2,256,128]{2,1,0:T(8,128)(2,1)S(1)} %collective-permute-done.1, bf16[2,256,128]{2,1,0:T(8,128)(2,1)S(1)} %collective-permute-done.2, bf16[1,1,2,256,512]{4,3,2,1,0:T(8,128)(2,1)} %param.14, s32[]{:T(128)S(6)} %select_n.81, ...), kind=kLoop, calls=%fused_computation.2 | loop fusion | flops 196608 | bytes 655367 | tf_op jit(solution)/shard_map/jit(_where)/select_n | solution.py:260
  17.2 3.3 %collective-permute-start.4 = (bf16[2,256,128]{2,1,0:T(8,128)(2,1)S(1)}, bf16[2,256,128]{2,1,0:T(8,128)(2,1)S(1)}, u32[]{:S(2)}, u32[]{:S(2)}) collective-permute-start(bf16[2,256,128]{2,1,0:T(8,128)(2,1)S(1)} %fusion.1.pr_ref), channel_id=1, source_target_pairs={{0,1},{1,2},{2,3},{3,0},{4,5},{5,6},{6,7},{7,4},{8,9},{9,10},{10,1... | collective-permute-start | bytes 393224 | tf_op jit(solution)/shard_map/ppermute | solution.py:249
  20.5 0.1 pad_add_fusion.2.meta
  20.6 1.6 %collective-permute-start.6 = (bf16[2,256,128]{2,1,0:T(8,128)(2,1)S(1)}, bf16[2,256,128]{2,1,0:T(8,128)(2,1)S(1)}, u32[]{:S(2)}, u32[]{:S(2)}) collective-permute-start(bf16[2,256,128]{2,1,0:T(8,128)(2,1)S(1)} %fusion.1.pr_ref), channel_id=1, source_target_pairs={{0,2},{1,3},{2,0},{3,1},{4,6},{5,7},{6,4},{7,5},{8,10},{9,11},{10,... | collective-permute-start | bytes 393224 | tf_op jit(solution)/shard_map/ppermute | solution.py:249
  22.2 0.8 %collective-permute-start.3 = (bf16[2,256,128]{2,1,0:T(8,128)(2,1)S(1)}, bf16[2,256,128]{2,1,0:T(8,128)(2,1)S(1)}, u32[]{:S(2)}, u32[]{:S(2)}) collective-permute-start(bf16[2,256,128]{2,1,0:T(8,128)(2,1)S(1)} %fusion.1.pr_ref), channel_id=1, source_target_pairs={{0,3},{1,0},{2,1},{3,2},{4,7},{5,4},{6,5},{7,6},{8,11},{9,8},{10,9... | collective-permute-start | bytes 393224 | tf_op jit(solution)/shard_map/ppermute | solution.py:249
  23.0 0.0 copy-done
  23.0 0.0 copy-done.1
  23.0 0.0 copy-start.2
  23.0 0.9 %copy-done.2 = bf16[1,1,192,512]{3,2,1,0:T(8,128)(2,1)S(1)} copy-done((bf16[1,1,192,512]{3,2,1,0:T(8,128)(2,1)S(1)}, bf16[1,1,192,512]{3,2,1,0:T(8,128)(2,1)}, u32[]{:S(2)}) %copy-start.2) | copy-done | bytes 196632
  23.9 0.0 copy-start.3
  23.9 0.9 %copy-done.3 = bf16[1,1,192,512]{3,2,1,0:T(8,128)(2,1)S(1)} copy-done((bf16[1,1,192,512]{3,2,1,0:T(8,128)(2,1)S(1)}, bf16[1,1,192,512]{3,2,1,0:T(8,128)(2,1)}, u32[]{:S(2)}) %copy-start.3) | copy-done | bytes 196632
  24.8 3.3 %attend_head.4 = (bf16[192,2048]{1,0:T(8,128)(2,1)}, bf16[192,2048]{1,0:T(8,128)(2,1)}, bf16[192,512]{1,0:T(8,128)(2,1)}, bf16[192,512]{1,0:T(8,128)(2,1)}, bf16...) custom-call(s32[2]{0:T(128)S(1)} %pad_add_fusion.2.meta, bf16[192,2048]{1,0:T(8,128)(2,1)S(1)} %bitcast.38, ...), custom_call_target="tpu_custom_call" | custom-call | flops 528482304 | bytes 983040 | tf_op jit(solution)/shard_map/attend_head/pallas_call | solution.py:138
  28.1 0.0 collective-permute-done.4.pr_ref
  28.1 3.3 %attend_head.5 = (bf16[192,2048]{1,0:T(8,128)(2,1)}, bf16[192,2048]{1,0:T(8,128)(2,1)}, bf16[192,512]{1,0:T(8,128)(2,1)}, bf16[192,512]{1,0:T(8,128)(2,1)}, bf16...) custom-call(s32[2]{0:T(128)S(1)} %get-tuple-element.77.meta, ...), custom_call_target="tpu_custom_call", output_to_operand_aliasing={{0}: (8, {}), {1}: (9, {}), {2}: (10, {}), {3}: (11, {})} | custom-call | flops 528482304 | bytes 983040 | tf_op jit(solution)/shard_map/attend_head/pallas_call | solution.py:138
  31.4 2.0 %collective-permute-start.5 = (bf16[2,256,128]{2,1,0:T(8,128)(2,1)S(1)}, bf16[2,256,128]{2,1,0:T(8,128)(2,1)S(1)}, u32[]{:S(2)}, u32[]{:S(2)}) collective-permute-start(bf16[2,256,128]{2,1,0:T(8,128)(2,1)S(1)} %get-tuple-element.51), channel_id=1, source_target_pairs={{0,3},{1,0},{2,1},{3,2},{4,7},{5,4},{6,5},{7,6},{8,11},{9,8},{10,9... | collective-permute-start | bytes 393224 | tf_op jit(solution)/shard_map/ppermute | solution.py:249
  33.5 0.1 pad_add_fusion.meta
  33.5 0.0 collective-permute-done.6.pr_ref
  33.5 3.3 %attend_head.6 = (bf16[192,2048]{1,0:T(8,128)(2,1)}, bf16[192,2048]{1,0:T(8,128)(2,1)}, bf16[192,512]{1,0:T(8,128)(2,1)}, bf16[192,512]{1,0:T(8,128)(2,1)}, bf16...) custom-call(s32[2]{0:T(128)S(1)} %get-tuple-element.78.meta, ...), custom_call_target="tpu_custom_call", output_to_operand_aliasing={{0}: (8, {}), {1}: (9, {}), {2}: (10, {}), {3}: (11, {})} | custom-call | flops 528482304 | bytes 983040 | tf_op jit(solution)/shard_map/attend_head/pallas_call | solution.py:138
  36.8 0.7 %collective-permute-start.7 = (bf16[2,256,128]{2,1,0:T(8,128)(2,1)S(1)}, bf16[2,256,128]{2,1,0:T(8,128)(2,1)S(1)}, u32[]{:S(2)}, u32[]{:S(2)}) collective-permute-start(bf16[2,256,128]{2,1,0:T(8,128)(2,1)S(1)} %get-tuple-element.69), channel_id=1, source_target_pairs={{0,2},{1,3},{2,0},{3,1},{4,6},{5,7},{6,4},{7,5},{8,10},{9,11},{10,... | collective-permute-start | bytes 393224 | tf_op jit(solution)/shard_map/ppermute | solution.py:249
  37.5 0.0 collective-permute-done.3.pr_ref
  37.5 0.0 collective-permute-done.5.rest_0_
  37.5 3.3 %attend_head.7 = (bf16[192,2048]{1,0:T(8,128)(2,1)}, bf16[192,2048]{1,0:T(8,128)(2,1)}, bf16[192,512]{1,0:T(8,128)(2,1)}, bf16[192,512]{1,0:T(8,128)(2,1)}, bf16...) custom-call(s32[2]{0:T(128)S(1)} %pad_add_fusion.meta, ...), custom_call_target="tpu_custom_call", output_to_operand_aliasing={{0}: (8, {}), {1}: (9, {}), {2}: (10, {}), {3}: (11, {})} | custom-call | flops 528482304 | bytes 983040 | tf_op jit(solution)/shard_map/attend_head/pallas_call | solution.py:138
  40.8 1.3 %collective-permute-start.8 = (bf16[2,256,128]{2,1,0:T(8,128)(2,1)S(1)}, bf16[2,256,128]{2,1,0:T(8,128)(2,1)S(1)}, u32[]{:S(2)}, u32[]{:S(2)}) collective-permute-start(bf16[2,256,128]{2,1,0:T(8,128)(2,1)S(1)} %get-tuple-element.70), channel_id=1, source_target_pairs={{0,1},{1,2},{2,3},{3,0},{4,5},{5,6},{6,7},{7,4},{8,9},{9,10},{10,1... | collective-permute-start | bytes 393224 | tf_op jit(solution)/shard_map/ppermute | solution.py:249
  42.2 0.0 collective-permute-start.9
  42.2 1.2 %collective-permute-done.9 = f32[8,128]{1,0:T(8,128)S(1)} collective-permute-done((f32[8,128]{1,0:T(8,128)S(1)}, f32[8,128]{1,0:T(8,128)S(1)}, u32[]{:S(2)}, u32[]{:S(2)}) %collective-permute-start.9) | collective-permute-done | bytes 4128 | tf_op jit(solution)/shard_map/ppermute | solution.py:230
  43.3 1.5 %collective-permute-start.10 = (f32[8,128]{1,0:T(8,128)S(1)}, f32[8,128]{1,0:T(8,128)S(1)}, u32[]{:S(2)}, u32[]{:S(2)}) collective-permute-start(f32[8,128]{1,0:T(8,128)S(1)} %add.76), channel_id=1, source_target_pairs={{0,8},{4,12},{8,0},{12,4},{16,24},{20,28},{24,16},{28,20},{1,9},{5... | collective-permute-start | bytes 12296 | tf_op jit(solution)/shard_map/ppermute | solution.py:230
  44.8 2.1 %collective-permute-done.10 = f32[8,128]{1,0:T(8,128)S(1)} collective-permute-done((f32[8,128]{1,0:T(8,128)S(1)}, f32[8,128]{1,0:T(8,128)S(1)}, u32[]{:S(2)}, u32[]{:S(2)}) %collective-permute-start.10) | collective-permute-done | bytes 4128 | tf_op jit(solution)/shard_map/ppermute | solution.py:230
  46.9 1.5 %collective-permute-start.11 = (f32[8,128]{1,0:T(8,128)S(1)}, f32[8,128]{1,0:T(8,128)S(1)}, u32[]{:S(2)}, u32[]{:S(2)}) collective-permute-start(f32[8,128]{1,0:T(8,128)S(1)} %add.77), channel_id=1, source_target_pairs={{0,16},{4,20},{8,24},{12,28},{16,0},{20,4},{24,8},{28,12},{1,17},{... | collective-permute-start | bytes 12296 | tf_op jit(solution)/shard_map/ppermute | solution.py:230
  48.5 2.1 %collective-permute-done.11 = f32[8,128]{1,0:T(8,128)S(1)} collective-permute-done((f32[8,128]{1,0:T(8,128)S(1)}, f32[8,128]{1,0:T(8,128)S(1)}, u32[]{:S(2)}, u32[]{:S(2)}) %collective-permute-start.11) | collective-permute-done | bytes 4128 | tf_op jit(solution)/shard_map/ppermute | solution.py:230
  50.5 0.0 collective-permute-done.7.rest_1_
  50.6 0.0 collective-permute-done.8.rest_2_
  50.6 0.1 join_parts.1.refs_0_
  50.6 2.6 %collective-permute-start.14 = (bf16[528,128]{1,0:T(8,128)(2,1)S(1)}, bf16[528,128]{1,0:T(8,128)(2,1)S(1)}, u32[]{:S(2)}, u32[]{:S(2)}) collective-permute-start(bf16[528,128]{1,0:T(8,128)(2,1)S(1)} %join_parts.1.refs_0_), channel_id=1, source_target_pairs={{0,3},{1,0},{2,1},{3,2},{4,7},{5,4},{6,5},{7,6},{8,11},{9,8},{10,9... | collective-permute-start | bytes 405512 | tf_op jit(solution)/shard_map/ppermute | solution.py:249
  53.2 0.4 collective-permute-start.13
  53.6 1.0 %collective-permute-start.12 = (bf16[528,128]{1,0:T(8,128)(2,1)S(1)}, bf16[528,128]{1,0:T(8,128)(2,1)S(1)}, u32[]{:S(2)}, u32[]{:S(2)}) collective-permute-start(bf16[528,128]{1,0:T(8,128)(2,1)S(1)} %join_parts.1.refs_0_), channel_id=1, source_target_pairs={{0,1},{1,2},{2,3},{3,0},{4,5},{5,6},{6,7},{7,4},{8,9},{9,10},{10,1... | collective-permute-start | bytes 405512 | tf_op jit(solution)/shard_map/ppermute | solution.py:249
  54.6 0.1 stack.59.meta
  54.7 2.5 %collective-permute-done.14.refs_3_ = bf16[528,128]{1,0:T(8,128)(2,1)S(1)} collective-permute-done((bf16[528,128]{1,0:T(8,128)(2,1)S(1)}, bf16[528,128]{1,0:T(8,128)(2,1)S(1)}, u32[]{:S(2)}, u32[]{:S(2)}) %collective-permute-start.14) | collective-permute-done | bytes 135200 | tf_op jit(solution)/shard_map/ppermute | solution.py:249
  57.2 7.1 %collective-permute-done.13.refs_2_ = bf16[528,128]{1,0:T(8,128)(2,1)S(1)} collective-permute-done((bf16[528,128]{1,0:T(8,128)(2,1)S(1)}, bf16[528,128]{1,0:T(8,128)(2,1)S(1)}, u32[]{:S(2)}, u32[]{:S(2)}) %collective-permute-start.13) | collective-permute-done | bytes 135200 | tf_op jit(solution)/shard_map/ppermute | solution.py:249
  64.4 0.0 collective-permute-done.12.refs_1_
  64.4 1.5 %place_prompt_grad.1 = (bf16[2,256,512]{2,1,0:T(8,128)(2,1)}, f32[2,128]{1,0:T(2,128)}) custom-call(s32[5]{0:T(128)S(1)} %stack.59.meta, bf16[528,128]{1,0:T(8,128)(2,1)S(1)} %join_parts.1.refs_0_, bf16[528,128]{1,0:T(8,128)(2,1)S(1)} %collective-permute-done.12.refs_1_, bf16[528,128]{1,0:T(8,128)(2,1)S(1)} %collective-permute-done.13.refs_2_, ...), custom_call_target="tpu_custom_call" | custom-call | tf_op jit(solution)/shard_map/place_prompt_grad/pallas_call | solution.py:213
  (5 shorter events, 0.0 us)
Async XLA Ops:
  0.7 8.3 %copy-start.4 = (f32[128]{0:T(128)S(1)}, f32[128]{0:T(128)}, u32[]{:S(2)}) copy-start(f32[128]{0:T(128)} %param.18) | copy-start | bytes 1540
  0.7 8.3 %copy-start.5 = (f32[128]{0:T(128)S(1)}, f32[128]{0:T(128)}, u32[]{:S(2)}) copy-start(f32[128]{0:T(128)} %param.17) | copy-start | bytes 1540
  0.7 22.3 %copy-start = (bf16[1,1,192,2048]{3,2,1,0:T(8,128)(2,1)S(1)}, bf16[1,1,192,2048]{3,2,1,0:T(8,128)(2,1)}, u32[]{:S(2)}) copy-start(bf16[1,1,192,2048]{3,2,1,0:T(8,128)(2,1)} %param.11) | copy-start | bytes 2359300
  0.7 22.3 %copy-start.1 = (bf16[1,1,192,2048]{3,2,1,0:T(8,128)(2,1)S(1)}, bf16[1,1,192,2048]{3,2,1,0:T(8,128)(2,1)}, u32[]{:S(2)}) copy-start(bf16[1,1,192,2048]{3,2,1,0:T(8,128)(2,1)} %param.19) | copy-start | bytes 2359300
  1.9 9.5 %collective-permute-start.2 = (bf16[2,256,128]{2,1,0:T(8,128)(2,1)S(1)}, bf16[2,256,128]{2,1,0:T(8,128)(2,1)S(1)}, u32[]{:S(2)}, u32[]{:S(2)}) collective-permute-start(bf16[2,256,128]{2,1,0:T(8,128)(2,1)S(1)} %get-tuple-element.74), channel_id=1, source_target_pairs={{0,1},{1,2},{2,3},{3,0},{4,5},{5,6},{6,7},{7,4},{8,9},{9,10},{10,1... | collective-permute-start | bytes 393224 | tf_op jit(solution)/shard_map/ppermute | solution.py:249
  5.0 11.2 %collective-permute-start.1 = (bf16[2,256,128]{2,1,0:T(8,128)(2,1)S(1)}, bf16[2,256,128]{2,1,0:T(8,128)(2,1)S(1)}, u32[]{:S(2)}, u32[]{:S(2)}) collective-permute-start(bf16[2,256,128]{2,1,0:T(8,128)(2,1)S(1)} %get-tuple-element.75), channel_id=1, source_target_pairs={{0,2},{1,3},{2,0},{3,1},{4,6},{5,7},{6,4},{7,5},{8,10},{9,11},{10,... | collective-permute-start | bytes 393224 | tf_op jit(solution)/shard_map/ppermute | solution.py:249
  7.6 8.6 %collective-permute-start = (bf16[2,256,128]{2,1,0:T(8,128)(2,1)S(1)}, bf16[2,256,128]{2,1,0:T(8,128)(2,1)S(1)}, u32[]{:S(2)}, u32[]{:S(2)}) collective-permute-start(bf16[2,256,128]{2,1,0:T(8,128)(2,1)S(1)} %get-tuple-element.76), channel_id=1, source_target_pairs={{0,3},{1,0},{2,1},{3,2},{4,7},{5,4},{6,5},{7,6},{8,11},{9,8},{10,9... | collective-permute-start | bytes 393224 | tf_op jit(solution)/shard_map/ppermute | solution.py:249
  17.2 10.9 %collective-permute-start.4 = (bf16[2,256,128]{2,1,0:T(8,128)(2,1)S(1)}, bf16[2,256,128]{2,1,0:T(8,128)(2,1)S(1)}, u32[]{:S(2)}, u32[]{:S(2)}) collective-permute-start(bf16[2,256,128]{2,1,0:T(8,128)(2,1)S(1)} %fusion.1.pr_ref), channel_id=1, source_target_pairs={{0,1},{1,2},{2,3},{3,0},{4,5},{5,6},{6,7},{7,4},{8,9},{9,10},{10,1... | collective-permute-start | bytes 393224 | tf_op jit(solution)/shard_map/ppermute | solution.py:249
  20.6 12.9 %collective-permute-start.6 = (bf16[2,256,128]{2,1,0:T(8,128)(2,1)S(1)}, bf16[2,256,128]{2,1,0:T(8,128)(2,1)S(1)}, u32[]{:S(2)}, u32[]{:S(2)}) collective-permute-start(bf16[2,256,128]{2,1,0:T(8,128)(2,1)S(1)} %fusion.1.pr_ref), channel_id=1, source_target_pairs={{0,2},{1,3},{2,0},{3,1},{4,6},{5,7},{6,4},{7,5},{8,10},{9,11},{10,... | collective-permute-start | bytes 393224 | tf_op jit(solution)/shard_map/ppermute | solution.py:249
  22.2 15.3 %collective-permute-start.3 = (bf16[2,256,128]{2,1,0:T(8,128)(2,1)S(1)}, bf16[2,256,128]{2,1,0:T(8,128)(2,1)S(1)}, u32[]{:S(2)}, u32[]{:S(2)}) collective-permute-start(bf16[2,256,128]{2,1,0:T(8,128)(2,1)S(1)} %fusion.1.pr_ref), channel_id=1, source_target_pairs={{0,3},{1,0},{2,1},{3,2},{4,7},{5,4},{6,5},{7,6},{8,11},{9,8},{10,9... | collective-permute-start | bytes 393224 | tf_op jit(solution)/shard_map/ppermute | solution.py:249
  23.0 0.9 %copy-start.2 = (bf16[1,1,192,512]{3,2,1,0:T(8,128)(2,1)S(1)}, bf16[1,1,192,512]{3,2,1,0:T(8,128)(2,1)}, u32[]{:S(2)}) copy-start(bf16[1,1,192,512]{3,2,1,0:T(8,128)(2,1)} %param.12) | copy-start | bytes 589828
  23.9 0.9 %copy-start.3 = (bf16[1,1,192,512]{3,2,1,0:T(8,128)(2,1)S(1)}, bf16[1,1,192,512]{3,2,1,0:T(8,128)(2,1)}, u32[]{:S(2)}) copy-start(bf16[1,1,192,512]{3,2,1,0:T(8,128)(2,1)} %param.13) | copy-start | bytes 589828
  31.4 6.1 %collective-permute-start.5 = (bf16[2,256,128]{2,1,0:T(8,128)(2,1)S(1)}, bf16[2,256,128]{2,1,0:T(8,128)(2,1)S(1)}, u32[]{:S(2)}, u32[]{:S(2)}) collective-permute-start(bf16[2,256,128]{2,1,0:T(8,128)(2,1)S(1)} %get-tuple-element.51), channel_id=1, source_target_pairs={{0,3},{1,0},{2,1},{3,2},{4,7},{5,4},{6,5},{7,6},{8,11},{9,8},{10,9... | collective-permute-start | bytes 393224 | tf_op jit(solution)/shard_map/ppermute | solution.py:249
  36.8 13.7 %collective-permute-start.7 = (bf16[2,256,128]{2,1,0:T(8,128)(2,1)S(1)}, bf16[2,256,128]{2,1,0:T(8,128)(2,1)S(1)}, u32[]{:S(2)}, u32[]{:S(2)}) collective-permute-start(bf16[2,256,128]{2,1,0:T(8,128)(2,1)S(1)} %get-tuple-element.69), channel_id=1, source_target_pairs={{0,2},{1,3},{2,0},{3,1},{4,6},{5,7},{6,4},{7,5},{8,10},{9,11},{10,... | collective-permute-start | bytes 393224 | tf_op jit(solution)/shard_map/ppermute | solution.py:249
  40.8 9.7 %collective-permute-start.8 = (bf16[2,256,128]{2,1,0:T(8,128)(2,1)S(1)}, bf16[2,256,128]{2,1,0:T(8,128)(2,1)S(1)}, u32[]{:S(2)}, u32[]{:S(2)}) collective-permute-start(bf16[2,256,128]{2,1,0:T(8,128)(2,1)S(1)} %get-tuple-element.70), channel_id=1, source_target_pairs={{0,1},{1,2},{2,3},{3,0},{4,5},{5,6},{6,7},{7,4},{8,9},{9,10},{10,1... | collective-permute-start | bytes 393224 | tf_op jit(solution)/shard_map/ppermute | solution.py:249
  42.2 1.2 %collective-permute-start.9 = (f32[8,128]{1,0:T(8,128)S(1)}, f32[8,128]{1,0:T(8,128)S(1)}, u32[]{:S(2)}, u32[]{:S(2)}) collective-permute-start(f32[8,128]{1,0:T(8,128)S(1)} %get-tuple-element.71), channel_id=1, source_target_pairs={{0,4},{4,0},{8,12},{12,8},{16,20},{20,16},{24,28},{28,24},{1,5},{5... | collective-permute-start | bytes 12296 | tf_op jit(solution)/shard_map/ppermute | solution.py:230
  43.3 3.6 %collective-permute-start.10 = (f32[8,128]{1,0:T(8,128)S(1)}, f32[8,128]{1,0:T(8,128)S(1)}, u32[]{:S(2)}, u32[]{:S(2)}) collective-permute-start(f32[8,128]{1,0:T(8,128)S(1)} %add.76), channel_id=1, source_target_pairs={{0,8},{4,12},{8,0},{12,4},{16,24},{20,28},{24,16},{28,20},{1,9},{5... | collective-permute-start | bytes 12296 | tf_op jit(solution)/shard_map/ppermute | solution.py:230
  46.9 3.6 %collective-permute-start.11 = (f32[8,128]{1,0:T(8,128)S(1)}, f32[8,128]{1,0:T(8,128)S(1)}, u32[]{:S(2)}, u32[]{:S(2)}) collective-permute-start(f32[8,128]{1,0:T(8,128)S(1)} %add.77), channel_id=1, source_target_pairs={{0,16},{4,20},{8,24},{12,28},{16,0},{20,4},{24,8},{28,12},{1,17},{... | collective-permute-start | bytes 12296 | tf_op jit(solution)/shard_map/ppermute | solution.py:230
  50.6 6.6 %collective-permute-start.14 = (bf16[528,128]{1,0:T(8,128)(2,1)S(1)}, bf16[528,128]{1,0:T(8,128)(2,1)S(1)}, u32[]{:S(2)}, u32[]{:S(2)}) collective-permute-start(bf16[528,128]{1,0:T(8,128)(2,1)S(1)} %join_parts.1.refs_0_), channel_id=1, source_target_pairs={{0,3},{1,0},{2,1},{3,2},{4,7},{5,4},{6,5},{7,6},{8,11},{9,8},{10,9... | collective-permute-start | bytes 405512 | tf_op jit(solution)/shard_map/ppermute | solution.py:249
  53.2 11.2 %collective-permute-start.13 = (bf16[528,128]{1,0:T(8,128)(2,1)S(1)}, bf16[528,128]{1,0:T(8,128)(2,1)S(1)}, u32[]{:S(2)}, u32[]{:S(2)}) collective-permute-start(bf16[528,128]{1,0:T(8,128)(2,1)S(1)} %join_parts.1.refs_0_), channel_id=1, source_target_pairs={{0,2},{1,3},{2,0},{3,1},{4,6},{5,7},{6,4},{7,5},{8,10},{9,11},{10,... | collective-permute-start | bytes 405512 | tf_op jit(solution)/shard_map/ppermute | solution.py:249
  53.6 10.7 %collective-permute-start.12 = (bf16[528,128]{1,0:T(8,128)(2,1)S(1)}, bf16[528,128]{1,0:T(8,128)(2,1)S(1)}, u32[]{:S(2)}, u32[]{:S(2)}) collective-permute-start(bf16[528,128]{1,0:T(8,128)(2,1)S(1)} %join_parts.1.refs_0_), channel_id=1, source_target_pairs={{0,1},{1,2},{2,3},{3,0},{4,5},{5,6},{6,7},{7,4},{8,9},{9,10},{10,1... | collective-permute-start | bytes 405512 | tf_op jit(solution)/shard_map/ppermute | solution.py:249

commit v3 on v1

v3 whole, which is shorter than its diff:
```python
import functools

import jax
import jax.numpy as jnp
from jax import lax
from jax.experimental import pallas as pl
from jax.experimental.pallas import tpu as pltpu
from jax.sharding import PartitionSpec as P

HD = 128
EPS = 1e-06
LOG2E = 1.4426950408889634
BF = jnp.bfloat16
F32 = jnp.float32


def dot_nn(a, b):
    return lax.dot_general(a, b, (((1,), (0,)), ((), ())), preferred_element_type=F32)


def dot_nt(a, b):
    return lax.dot_general(a, b, (((1,), (1,)), ((), ())), preferred_element_type=F32)


VMEM = pl.BlockSpec(memory_space=pltpu.VMEM)
SMEM = pl.BlockSpec(memory_space=pltpu.SMEM)
ANY = pl.BlockSpec(memory_space=pl.ANY)


def params(mib):
    return pltpu.CompilerParams(vmem_limit_bytes=mib * 2**20)


def cut_kernel(order, cache_ref, *rest):
    outs, sems = rest[:-1], rest[-1]
    copies = []
    for i, out in enumerate(outs):
        at = pl.multiple_of(order[i] * HD, HD)
        copy = pltpu.make_async_copy(cache_ref.at[:, :, pl.ds(at, HD)], out, sems.at[i])
        copy.start()
        copies.append(copy)
    for copy in copies:
        copy.wait()


def cut(order, cache, count):
    depth, rows, _ = cache.shape
    return pl.pallas_call(
        cut_kernel,
        out_shape=[jax.ShapeDtypeStruct((depth, rows, HD), BF)] * count,
        in_specs=[SMEM, ANY],
        out_specs=[VMEM] * count,
        scratch_shapes=[pltpu.SemaphoreType.DMA((count,))],
        compiler_params=params(4),
        name="cut_prompt",
    )(order, cache)


def pick_kernel(which, *refs):
    picked = refs[0][...]
    for i in range(1, len(refs) - 1):
        picked = jnp.where(which[0] == i, refs[i][...], picked)
    refs[-1][...] = picked


def pick(which, blocks):
    return pl.pallas_call(
        pick_kernel,
        out_shape=jax.ShapeDtypeStruct(blocks[0].shape, BF),
        in_specs=[SMEM] + [VMEM] * len(blocks),
        out_specs=VMEM,
        compiler_params=params(4),
        name="pick_owner",
    )(which, *blocks)


KEPT = 8


def prepare_kernel(count, share, rows, width, meta, q_ref, g_ref, k_ref, v_ref, gain_ref, kg_ref, *outs):
    live_len = meta[count]
    scale = HD ** (-0.5)
    q_gain = gain_ref[...]
    k_gain = kg_ref[...]
    for s in range(count):
        qt_ref, gt_ref, row_ref, er_ref, ot_ref, dp_ref, kh_ref, ku_ref = outs[s * KEPT : (s + 1) * KEPT]
        base = meta[s]

        def stacked(ref):
            at = [pl.multiple_of((base * share + i) * HD, HD) for i in range(share)]
            return jnp.concatenate([ref[:, pl.ds(x, HD)] for x in at], axis=0)

        q_t = stacked(q_ref).T
        g_t = stacked(g_ref).T
        qt_ref[...] = q_t
        k_at = pl.ds(pl.multiple_of(base * HD, HD), HD)
        raw_k = k_ref[:, k_at].astype(F32)
        k_unit = raw_k * lax.rsqrt(jnp.mean(raw_k * raw_k, axis=-1, keepdims=True) + EPS)
        k_hat = (k_unit * k_gain).astype(BF)
        kh_ref[...] = k_hat
        ku_ref[...] = k_unit
        r_val = v_ref[:, k_at]
        r_val_t = r_val.T
        for start in range(0, share * rows, width):
            cols = slice(start, start + width)
            token = (lax.broadcasted_iota(jnp.int32, (1, width), 1) + start) % rows
            raw_q = q_t[:, cols].astype(F32)
            q_inv = lax.rsqrt(jnp.mean(raw_q * raw_q, axis=0, keepdims=True) + EPS)
            q_hat = (raw_q * q_inv * q_gain).astype(BF)
            d_o = jnp.where(token < live_len, g_t[:, cols].astype(F32), 0.0).astype(BF)
            gt_ref[:, cols] = d_o
            causal = lax.broadcasted_iota(jnp.int32, (rows, width), 0) <= token
            e_r = jnp.where(causal, jnp.exp2(dot_nn(k_hat, q_hat) * (scale * LOG2E)), 0.0)
            eb_r = e_r.astype(BF)
            er_ref[:, cols] = eb_r
            ot_ref[:, cols] = dot_nn(r_val_t, eb_r)
            dp_ref[:, cols] = dot_nn(r_val, d_o)
            row_ref[0:1, cols] = q_inv
            row_ref[1:2, cols] = jnp.sum(e_r, axis=0, keepdims=True)


def prepare(meta, q, g, k, v, q_gain, k_gain, count):
    rows, q_width = q.shape
    share = q_width // k.shape[1]
    total = share * rows
    each = [
        jax.ShapeDtypeStruct((HD, total), BF),
        jax.ShapeDtypeStruct((HD, total), BF),
        jax.ShapeDtypeStruct((8, total), F32),
        jax.ShapeDtypeStruct((rows, total), BF),
        jax.ShapeDtypeStruct((HD, total), F32),
        jax.ShapeDtypeStruct((rows, total), F32),
        jax.ShapeDtypeStruct((rows, HD), BF),
        jax.ShapeDtypeStruct((rows, HD), F32),
    ]
    outs = pl.pallas_call(
        functools.partial(prepare_kernel, count, share, rows, 2 * HD),
        out_shape=each * count,
        in_specs=[SMEM] + [VMEM] * 6,
        out_specs=[VMEM] * (KEPT * count),
        compiler_params=params(24),
        cost_estimate=pl.CostEstimate(
            flops=6 * count * total * rows * HD,
            bytes_accessed=5 * rows * q_width * 2,
            transcendentals=count * total * rows,
        ),
        name="prepare_response",
    )(meta, q, g, k, v, q_gain, k_gain)
    return [list(outs[s * KEPT : (s + 1) * KEPT]) for s in range(count)]


def head_kernel(
    width, pr_ref, qt_ref, gt_ref, row_ref, er_ref, ot_ref, dp_ref, kh_ref, ku_ref, gain_ref, acc_ref,
    part_ref, at_ref, dq_ref, dkr_ref, dvr_ref, gacc_ref,
):
    scale = HD ** (-0.5)
    q_gain = gain_ref[...]
    p_key = pr_ref[0]
    p_val = pr_ref[1]
    k_hat_t = kh_ref[...].T
    p_key_t = p_key.T
    p_val_t = p_val.T
    sums = None
    for start in range(0, qt_ref.shape[1], width):
        cols = slice(start, start + width)
        q_unit = qt_ref[:, cols].astype(F32) * row_ref[0:1, cols]
        q_hat = (q_unit * q_gain).astype(BF)
        d_ob = gt_ref[:, cols]
        d_o = d_ob.astype(F32)
        e_p = jnp.exp2(dot_nn(p_key, q_hat) * (scale * LOG2E))
        inv_sum = 1.0 / (jnp.sum(e_p, axis=0, keepdims=True) + row_ref[1:2, cols])
        eb_p = e_p.astype(BF)
        eb_r = er_ref[:, cols]
        out = (dot_nn(p_val_t, eb_p) + ot_ref[:, cols]) * inv_sum
        at_ref[:, cols] = out.astype(BF)
        delta = jnp.sum(d_o * out, axis=0, keepdims=True)
        ds_p = (e_p * (dot_nn(p_val, d_ob) - delta)).astype(BF)
        ds_r = (eb_r.astype(F32) * (dp_ref[:, cols] - delta)).astype(BF)
        weight = inv_sum * scale
        q_w = (q_hat.astype(F32) * weight).astype(BF)
        d_ow = (d_o * inv_sum).astype(BF)
        d_qhat = (dot_nn(p_key_t, ds_p) + dot_nn(k_hat_t, ds_r)) * weight
        dq_ref[:, cols] = d_qhat
        terms = (
            dot_nt(ds_p, q_w),
            dot_nt(eb_p, d_ow),
            dot_nt(ds_r, q_w),
            dot_nt(eb_r, d_ow),
            d_qhat * q_unit,
        )
        sums = terms if sums is None else [a + b for a, b in zip(sums, terms)]
    d_kp, d_vp, d_kr, d_vr, q_term = sums
    part_ref[0] = d_kp.astype(BF)
    part_ref[1] = d_vp.astype(BF)
    dkr_ref[...] = d_kr
    dvr_ref[...] = d_vr.astype(BF)
    folded = q_term[:, :HD]
    for start in range(HD, width, HD):
        folded = folded + q_term[:, start : start + HD]
    gacc_ref[0:1, :] = acc_ref[0:1, :] + jnp.sum(folded.T, axis=0, keepdims=True)
    gacc_ref[1:2, :] = acc_ref[1:2, :] + jnp.sum(d_kr * ku_ref[...], axis=0, keepdims=True)
    gacc_ref[2:8, :] = jnp.zeros((6, HD), F32)


def one_head(prompt, kept, q_gain, acc):
    total = kept[0].shape[1]
    rows = kept[3].shape[0]
    return pl.pallas_call(
        functools.partial(head_kernel, 2 * HD),
        out_shape=[
            jax.ShapeDtypeStruct(prompt.shape, BF),
            jax.ShapeDtypeStruct((HD, total), BF),
            jax.ShapeDtypeStruct((HD, total), F32),
            jax.ShapeDtypeStruct((rows, HD), F32),
            jax.ShapeDtypeStruct((rows, HD), BF),
            jax.ShapeDtypeStruct(acc.shape, F32),
        ],
        in_specs=[VMEM] * 11,
        out_specs=[VMEM] * 6,
        compiler_params=params(16),
        cost_estimate=pl.CostEstimate(
            flops=(8 * prompt.shape[1] + 4 * rows) * total * HD,
            bytes_accessed=2**20,
            transcendentals=total * prompt.shape[1],
        ),
        name="attend_head",
    )(prompt, *kept, q_gain, acc)


def finish_kernel(count, share, rows, width, meta, k_ref, gain_ref, kg_ref, *refs):
    ins, (att_ref, dq_ref, dk_ref, dv_ref) = refs[:-4], refs[-4:]
    live_len = meta[count]
    q_gain = gain_ref[...]
    k_gain = kg_ref[...]
    for s in range(count):
        qt_ref, row_ref, ku_ref, at_in, dq_in, dkr_ref, dvr_ref = ins[s * 7 : (s + 1) * 7]
        base = meta[s]
        k_at = pl.ds(pl.multiple_of(base * HD, HD), HD)
        dv_ref[:, k_at] = dvr_ref[...]
        raw_k = k_ref[:, k_at].astype(F32)
        k_inv = lax.rsqrt(jnp.mean(raw_k * raw_k, axis=-1, keepdims=True) + EPS)
        k_unit = ku_ref[...]
        up_k = dkr_ref[...] * k_gain
        mean_k = jnp.mean(up_k * k_unit, axis=-1, keepdims=True)
        dk_ref[:, k_at] = (k_inv * (up_k - k_unit * mean_k)).astype(BF)
        parts = []
        for start in range(0, share * rows, width):
            cols = slice(start, start + width)
            q_inv = row_ref[0:1, cols]
            q_unit = qt_ref[:, cols].astype(F32) * q_inv
            up = dq_in[:, cols] * q_gain
            mean = jnp.mean(up * q_unit, axis=0, keepdims=True)
            parts.append((q_inv * (up - q_unit * mean)).astype(BF))
        d_q = jnp.concatenate(parts, axis=1).T
        att = at_in[...].T
        live = lax.broadcasted_iota(jnp.int32, (rows, HD), 0) < live_len
        for i in range(share):
            at = pl.ds(pl.multiple_of((base * share + i) * HD, HD), HD)
            block = att[i * rows : (i + 1) * rows, :].astype(F32)
            att_ref[:, at] = jnp.where(live, block, 0.0).astype(BF)
            dq_ref[:, at] = d_q[i * rows : (i + 1) * rows, :]


def finish(meta, k, q_gain, k_gain, per_head, q_width):
    rows, k_width = k.shape
    flat = [x for group in per_head for x in group]
    return pl.pallas_call(
        functools.partial(finish_kernel, len(per_head), q_width // k_width, rows, 2 * HD),
        out_shape=[
            jax.ShapeDtypeStruct((rows, q_width), BF),
            jax.ShapeDtypeStruct((rows, q_width), BF),
            jax.ShapeDtypeStruct((rows, k_width), BF),
            jax.ShapeDtypeStruct((rows, k_width), BF),
        ],
        in_specs=[SMEM] + [VMEM] * (3 + len(flat)),
        out_specs=[VMEM] * 4,
        compiler_params=params(16),
        cost_estimate=pl.CostEstimate(
            flops=40 * rows * q_width, bytes_accessed=10 * rows * q_width, transcendentals=0
        ),
        name="finish_response",
    )(meta, k, q_gain, k_gain, *flat)


def join_kernel(*refs):
    total = refs[0][...].astype(F32)
    for ref in refs[1:-1]:
        total = total + ref[...].astype(F32)
    refs[-1][...] = total.astype(BF)


def join(parts):
    return pl.pallas_call(
        join_kernel,
        out_shape=jax.ShapeDtypeStruct(parts[0].shape, BF),
        in_specs=[VMEM] * len(parts),
        out_specs=VMEM,
        compiler_params=params(4),
        name="join_parts",
    )(*parts)


def ordered_sum_kernel(count, order, *refs):
    stage = refs[-1]
    for i in range(count):
        stage[order[i]] = refs[i][...]
    total = stage[0]
    for i in range(1, count):
        total = total + stage[i]
    refs[count][...] = total


def ordered_sum(order, terms):
    count = len(terms)
    return pl.pallas_call(
        functools.partial(ordered_sum_kernel, count),
        out_shape=jax.ShapeDtypeStruct(terms[0].shape, F32),
        in_specs=[SMEM] + [VMEM] * count,
        out_specs=VMEM,
        scratch_shapes=[pltpu.VMEM((count,) + terms[0].shape, F32)],
        compiler_params=params(4),
        name="sum_gains",
    )(order, *terms)


def place_kernel(meta, *refs):
    heads, out_ref = refs[:-1], refs[-1]
    mine = meta[0] > 0
    for i, ref in enumerate(heads):
        at = pl.multiple_of(meta[1 + i] * HD, HD)
        out_ref[:, :, pl.ds(at, HD)] = jnp.where(mine, ref[...], jnp.zeros_like(ref[...]))


def place(meta, heads):
    depth, rows, _ = heads[0].shape
    return pl.pallas_call(
        place_kernel,
        out_shape=jax.ShapeDtypeStruct((depth, rows, HD * len(heads)), BF),
        in_specs=[SMEM] + [VMEM] * len(heads),
        out_specs=VMEM,
        compiler_params=params(8),
        name="place_prompt_grad",
    )(meta, *heads)


def pair_sum(value, axis, size):
    step = 1
    while step < size:
        value = value + lax.ppermute(value, axis, [(i, i ^ step) for i in range(size)])
        step *= 2
    return value


def local(
    n_dp, n_group, queries, resp_keys, resp_values, prompt_cache, owners, lengths, q_gain, k_gain, grad_out
):
    q, g = queries[0, 0], grad_out[0, 0]
    k, v = resp_keys[0, 0], resp_values[0, 0]
    cache = prompt_cache[0, 0]
    owner = owners[0]
    live_len = lengths[0, 0]
    me = lax.axis_index("group")
    kv_heads = k.shape[1] // HD
    depth, p_rows, _ = cache.shape
    direct = n_group == kv_heads

    def shift(x, s):
        return lax.ppermute(x, "group", [(i, (i + s) % n_group) for i in range(n_group)])

    gain_col = q_gain[:, None]
    gain_row = k_gain[None, :]
    if direct:
        order = jnp.stack([(me - s) % n_group for s in range(n_group)]).astype(jnp.int32)
    else:
        order = jnp.arange(kv_heads, dtype=jnp.int32)
    meta = jnp.concatenate([order, live_len[None]])
    kept = prepare(meta, q, g, k, v, gain_col, gain_row, kv_heads)
    if direct:
        blocks = cut(order, cache, kv_heads)
        got = [blocks[0]] + [shift(blocks[s], -s) for s in range(1, n_group)]
        got[1], kept[0][2] = lax.optimization_barrier((got[1], kept[0][2]))
        mine = pick(jnp.reshape((owner - me) % n_group, (1,)).astype(jnp.int32), got)
        prompts = [mine] + [shift(mine, s) for s in range(1, n_group)]
    else:
        cache = lax.psum(jnp.where(me == owner, cache, jnp.zeros_like(cache)), "group")
        prompts = cut(order, cache, kv_heads)

    acc = jnp.zeros((8, HD), F32)
    parts, backs, per_head = [], [], []
    for s, prompt in enumerate(prompts):
        if direct and s == n_group - 1:
            prompt, backs[0] = lax.optimization_barrier((prompt, backs[0]))
        part, out_t, d_q, d_kr, d_vr, acc = one_head(prompt, kept[s], gain_col, acc)
        per_head.append((kept[s][0], kept[s][2], kept[s][7], out_t, d_q, d_kr, d_vr))
        parts.append(part)
        if direct and s > 0:
            backs.append(shift(part, -s))

    mine_flag = (me == owner).astype(jnp.int32)
    if direct:
        total = join([parts[0]] + backs)
        gains = ordered_sum(order, [acc] + [shift(acc, s) for s in range(1, n_group)])
        total, gains = lax.optimization_barrier((total, gains))
        heads = [total] + [shift(total, s) for s in range(1, n_group)]
        placed = place(jnp.concatenate([mine_flag[None], order]), heads)
    else:
        total = lax.psum(jnp.concatenate(parts, axis=-1).astype(F32), "group").astype(BF)
        placed = jnp.where(mine_flag > 0, total, jnp.zeros((), BF))
        gains = pair_sum(acc, "group", n_group)
    gains = pair_sum(gains, "dp", n_dp)[:2]
    attended, d_query, d_key, d_value = finish(meta, k, gain_col, gain_row, per_head, q.shape[1])
    return (
        attended[None, None],
        d_query[None, None],
        d_key[None, None],
        d_value[None, None],
        placed[None, None],
        gains,
    )


def solution(mesh):
    in_specs = (
        P("dp", "group", None, None),
        P("dp", "group", None, None),
        P("dp", "group", None, None),
        P("dp", "group", None, None, None),
        P("dp"),
        P("dp", "group"),
        P(),
        P(),
        P("dp", "group", None, None),
    )
    out_specs = (
        P("dp", "group", None, None),
        P("dp", "group", None, None),
        P("dp", "group", None, None),
        P("dp", "group", None, None),
        P("dp", "group", None, None, None),
        P(),
    )
    body = functools.partial(local, mesh.shape["dp"], mesh.shape["group"])
    return jax.shard_map(body, mesh=mesh, in_specs=in_specs, out_specs=out_specs, check_vma=False)
```

time: 79.7 us -> 83.7 us (1.050)
  local copies, waits for them, and re-layouts: 4.2 us -> 18.4 us
  waiting for transfers between devices: 27.1 us -> 17.6 us
  starting transfers between devices: 29 us -> 27.3 us
  Pallas kernels: 15.2 us -> 16.4 us
  other arithmetic: 1.87 us -> 0.77 us
    unnamed x20 -> x70, local copies, waits for them, and re-layouts: 2.28 us -> 17.5 us
    ppermute x5 -> x3, waiting for transfers between devices: 15 us -> 3.29 us  [pair_sum(): lax.ppermute(value, axis, [(i, i ^ step) for i in range(size)])]
    ppermute x5 -> x3, starting transfers between devices: 6.58 us -> 3 us  [pair_sum(): lax.ppermute(value, axis, [(i, i ^ step) for i in range(size)])]
    ppermute x12 -> x15, waiting for transfers between devices: 12.1 us -> 14.3 us  [shift(): lax.ppermute(x, 'group', [(i, (i + s) % n_group) for i in range(n_group)])]
    ppermute x12 -> x15, starting transfers between devices: 22.4 us -> 24.3 us  [shift(): lax.ppermute(x, 'group', [(i, (i + s) % n_group) for i in range(n_group)])]
    pallas_call x4 -> x10, Pallas kernels: 13.2 us -> 14.5 us  [the longest x4 6.8 us: one_head(): pl.pallas_call(functools.partial(head_kernel, 2 * HD), out_shape=[jax.Sha...]
    dynamic_slice x1 -> x0, local copies, waits for them, and re-layouts: 1.19 us -> none  [head_of(): return lax.dynamic_slice(array, (0, 0, index * HD), (depth, p_rows, HD))]
    select_n x1 -> x0, other arithmetic: 0.98 us -> none  [local(): mine = jnp.where(owner == (me - s) % n_group, got[s], mine)]
  transfers between devices with their start and end apart: 17 -> 18, of which waited for: 8 -> 7; matrix products, arithmetic and copies ran while one was open for 2% -> 2% of each run, Pallas kernels for 12% -> 17%
where the time goes in v3:
time: 83.7 us; the launch traced here: 82.7 us
  starting transfers between devices  27.3 us (33%)
  local copies, waits for them, and re-layouts  18.4 us (22%)
  waiting for transfers between devices  17.6 us (21%)
  Pallas kernels  16.4 us (20%)
  between operations  2.31 us (3%)
    ppermute x15, starting transfers between devices, shift(): lax.ppermute(x, 'group', [(i, (i + s) % n_group) for i in range(n_group)])  24.3 us
    unnamed x70, local copies, waits for them, and re-layouts  17.5 us
    ppermute x15, waiting for transfers between devices, shift(): lax.ppermute(x, 'group', [(i, (i + s) % n_group) for i in range(n_group)])  14.3 us
    pallas_call x4, Pallas kernels, one_head(): pl.pallas_call(functools.partial(head_kernel, 2 * HD), out_shape=[jax.Sha...  6.8 us
    pallas_call x1, Pallas kernels, prepare(): pl.pallas_call(functools.partial(prepare_kernel, count, share, rows, 2 *...  3.43 us
    ppermute x3, waiting for transfers between devices, pair_sum(): lax.ppermute(value, axis, [(i, i ^ step) for i in range(size)])  3.29 us
    ppermute x3, starting transfers between devices, pair_sum(): lax.ppermute(value, axis, [(i, i ^ step) for i in range(size)])  3 us
    pallas_call x1, Pallas kernels, finish(): pl.pallas_call(functools.partial(finish_kernel, len(per_head), q_width //...  2.88 us
  transfers between devices with their start and end apart: 18, of which 7 were waited for; matrix products, arithmetic and copies ran while one was open for 2% of the time, Pallas kernels for 17%

profile of v3, /device:TPU:0, one launch (start us, length us, event | category | flops | bytes accessed | tf_op | source)
XLA Modules:
  0.0 82.7 jit_solution(10684385807421733966)
XLA Ops:
  0.7 0.1 pad_add_fusion.order
  0.8 1.0 %copy-done.3 = bf16[1,1,2,256,512]{4,3,2,1,0:T(8,128)(2,1)S(1)} copy-done((bf16[1,1,2,256,512]{4,3,2,1,0:T(8,128)(2,1)S(1)}, bf16[1,1,2,256,512]{4,3,2,1,0:T(8,128)(2,1)}, u32[]{:S(2)}) %copy-start.3) | copy-done | bytes 524312
  1.8 0.7 cut_prompt.1
  2.5 5.1 %collective-permute-start = (bf16[2,256,128]{2,1,0:T(8,128)(2,1)S(1)}, bf16[2,256,128]{2,1,0:T(8,128)(2,1)S(1)}, u32[]{:S(2)}, u32[]{:S(2)}) collective-permute-start(bf16[2,256,128]{2,1,0:T(8,128)(2,1)S(1)} %get-tuple-element.77), channel_id=1, source_target_pairs={{0,3},{1,0},{2,1},{3,2},{4,7},{5,4},{6,5},{7,6},{8,11},{9,8},{10,9... | collective-permute-start | bytes 393224 | tf_op jit(solution)/shard_map/ppermute | solution.py:368
  7.6 1.0 %collective-permute-start.2 = (bf16[2,256,128]{2,1,0:T(8,128)(2,1)S(1)}, bf16[2,256,128]{2,1,0:T(8,128)(2,1)S(1)}, u32[]{:S(2)}, u32[]{:S(2)}) collective-permute-start(bf16[2,256,128]{2,1,0:T(8,128)(2,1)S(1)} %get-tuple-element.84), channel_id=1, source_target_pairs={{0,1},{1,2},{2,3},{3,0},{4,5},{5,6},{6,7},{7,4},{8,9},{9,10},{10,1... | collective-permute-start | bytes 393224 | tf_op jit(solution)/shard_map/ppermute | solution.py:368
  10.0 0.1 concatenate.8.meta
  10.0 0.7 copy-done.34
  10.7 0.1 copy.20.gain_ref
  10.8 0.0 copy-start.33
  10.8 0.6 copy-done.33
  11.5 1.1 %copy-done.1 = bf16[1,1,192,2048]{3,2,1,0:T(8,128)(2,1)S(1)} copy-done((bf16[1,1,192,2048]{3,2,1,0:T(8,128)(2,1)S(1)}, bf16[1,1,192,2048]{3,2,1,0:T(8,128)(2,1)}, u32[]{:S(2)}) %copy-start.1) | copy-done | bytes 786456
  12.6 1.1 %copy-done.2 = bf16[1,1,192,2048]{3,2,1,0:T(8,128)(2,1)S(1)} copy-done((bf16[1,1,192,2048]{3,2,1,0:T(8,128)(2,1)S(1)}, bf16[1,1,192,2048]{3,2,1,0:T(8,128)(2,1)}, u32[]{:S(2)}) %copy-start.2) | copy-done | bytes 786456
  13.7 3.4 %prepare_response.1 = (bf16[128,768]{1,0:T(8,128)(2,1)S(1)}, bf16[128,768]{1,0:T(8,128)(2,1)S(1)}, f32[8,768]{1,0:T(8,128)S(1)}, bf16[192,768]{1,0:T(8,128)(2,1)...) custom-call(s32[5]{0:T(128)S(1)} %concatenate.8.meta, ...), custom_call_target="tpu_custom_call" | custom-call | flops 452984832 | bytes 3932160 | tf_op jit(solution)/shard_map/prepare_response/pallas_call | solution.py:136
  17.2 1.6 %collective-permute-done.1.refs_2_ = bf16[2,256,128]{2,1,0:T(8,128)(2,1)S(1)} collective-permute-done((bf16[2,256,128]{2,1,0:T(8,128)(2,1)S(1)}, bf16[2,256,128]{2,1,0:T(8,128)(2,1)S(1)}, u32[]{:S(2)}, u32[]{:S(2)}) %collective-permute-start.1) | collective-permute-done | bytes 131104 | tf_op jit(solution)/shard_map/ppermute | solution.py:368
  18.8 0.1 pick_owner.1.pr_ref
  18.9 1.0 %collective-permute-start.3 = (bf16[2,256,128]{2,1,0:T(8,128)(2,1)S(1)}, bf16[2,256,128]{2,1,0:T(8,128)(2,1)S(1)}, u32[]{:S(2)}, u32[]{:S(2)}) collective-permute-start(bf16[2,256,128]{2,1,0:T(8,128)(2,1)S(1)} %pick_owner.1.pr_ref), channel_id=1, source_target_pairs={{0,1},{1,2},{2,3},{3,0},{4,5},{5,6},{6,7},{7,4},{8,9},{9,10},{10,1... | collective-permute-start | bytes 393224 | tf_op jit(solution)/shard_map/ppermute | solution.py:368
  19.9 2.9 %collective-permute-start.5 = (bf16[2,256,128]{2,1,0:T(8,128)(2,1)S(1)}, bf16[2,256,128]{2,1,0:T(8,128)(2,1)S(1)}, u32[]{:S(2)}, u32[]{:S(2)}) collective-permute-start(bf16[2,256,128]{2,1,0:T(8,128)(2,1)S(1)} %pick_owner.1.pr_ref), channel_id=1, source_target_pairs={{0,3},{1,0},{2,1},{3,2},{4,7},{5,4},{6,5},{7,6},{8,11},{9,8},{10,9... | collective-permute-start | bytes 393224 | tf_op jit(solution)/shard_map/ppermute | solution.py:368
  22.8 0.8 %collective-permute-start.4 = (bf16[2,256,128]{2,1,0:T(8,128)(2,1)S(1)}, bf16[2,256,128]{2,1,0:T(8,128)(2,1)S(1)}, u32[]{:S(2)}, u32[]{:S(2)}) collective-permute-start(bf16[2,256,128]{2,1,0:T(8,128)(2,1)S(1)} %pick_owner.1.pr_ref), channel_id=1, source_target_pairs={{0,2},{1,3},{2,0},{3,1},{4,6},{5,7},{6,4},{7,5},{8,10},{9,11},{10,... | collective-permute-start | bytes 393224 | tf_op jit(solution)/shard_map/ppermute | solution.py:368
  23.6 1.7 %attend_head.4 = (bf16[2,256,128]{2,1,0:T(8,128)(2,1)S(1)}, bf16[128,768]{1,0:T(8,128)(2,1)S(1)}, f32[128,768]{1,0:T(8,128)S(1)}, f32[192,128]{1,0:T(8,128)S(1)}...) custom-call(bf16[2,256,128]{2,1,0:T(8,128)(2,1)S(1)} %pick_owner.1.pr_ref, ...), custom_call_target="tpu_custom_call" | custom-call | flops 276824064 | bytes 1048576 | tf_op jit(solution)/shard_map/attend_head/pallas_call | solution.py:208
  25.3 0.0 copy-start.17
  25.3 1.9 %collective-permute-done.3.pr_ref = bf16[2,256,128]{2,1,0:T(8,128)(2,1)S(1)} collective-permute-done((bf16[2,256,128]{2,1,0:T(8,128)(2,1)S(1)}, bf16[2,256,128]{2,1,0:T(8,128)(2,1)S(1)}, u32[]{:S(2)}, u32[]{:S(2)}) %collective-permute-start.3) | collective-permute-done | bytes 131104 | tf_op jit(solution)/shard_map/ppermute | solution.py:368
  27.2 1.7 %attend_head.5 = (bf16[2,256,128]{2,1,0:T(8,128)(2,1)S(1)}, bf16[128,768]{1,0:T(8,128)(2,1)S(1)}, f32[128,768]{1,0:T(8,128)S(1)}, f32[192,128]{1,0:T(8,128)S(1)}...) custom-call(bf16[2,256,128]{2,1,0:T(8,128)(2,1)S(1)} %collective-permute-done.3.pr_ref, ...), custom_call_target="tpu_custom_call" | custom-call | flops 276824064 | bytes 1048576 | tf_op jit(solution)/shard_map/attend_head/pallas_call | solution.py:208
  29.0 0.0 copy-start.19
  29.0 0.1 collective-permute-start.6
  29.1 5.6 %collective-permute-done.4.pr_ref = bf16[2,256,128]{2,1,0:T(8,128)(2,1)S(1)} collective-permute-done((bf16[2,256,128]{2,1,0:T(8,128)(2,1)S(1)}, bf16[2,256,128]{2,1,0:T(8,128)(2,1)S(1)}, u32[]{:S(2)}, u32[]{:S(2)}) %collective-permute-start.4) | collective-permute-done | bytes 131104 | tf_op jit(solution)/shard_map/ppermute | solution.py:368
  34.7 1.7 %attend_head.6 = (bf16[2,256,128]{2,1,0:T(8,128)(2,1)S(1)}, bf16[128,768]{1,0:T(8,128)(2,1)S(1)}, f32[128,768]{1,0:T(8,128)S(1)}, f32[192,128]{1,0:T(8,128)S(1)}...) custom-call(bf16[2,256,128]{2,1,0:T(8,128)(2,1)S(1)} %collective-permute-done.4.pr_ref, ...), custom_call_target="tpu_custom_call" | custom-call | flops 276824064 | bytes 1048576 | tf_op jit(solution)/shard_map/attend_head/pallas_call | solution.py:208
  36.4 0.0 copy-start.4
  36.4 0.7 copy-done.4
  37.1 0.6 copy-done.29
  37.7 3.2 %collective-permute-start.7 = (bf16[2,256,128]{2,1,0:T(8,128)(2,1)S(1)}, bf16[2,256,128]{2,1,0:T(8,128)(2,1)S(1)}, u32[]{:S(2)}, u32[]{:S(2)}) collective-permute-start(bf16[2,256,128]{2,1,0:T(8,128)(2,1)S(1)} %get-tuple-element.141), channel_id=1, source_target_pairs={{0,2},{1,3},{2,0},{3,1},{4,6},{5,7},{6,4},{7,5},{8,10},{9,11},{10,... | collective-permute-start | bytes 393224 | tf_op jit(solution)/shard_map/ppermute | solution.py:368
  40.9 1.7 %attend_head.7 = (bf16[2,256,128]{2,1,0:T(8,128)(2,1)S(1)}, bf16[128,768]{1,0:T(8,128)(2,1)S(1)}, f32[128,768]{1,0:T(8,128)S(1)}, f32[192,128]{1,0:T(8,128)S(1)}...) custom-call(bf16[2,256,128]{2,1,0:T(8,128)(2,1)S(1)} %collective-permute-done.5.pr_ref, ...), custom_call_target="tpu_custom_call" | custom-call | flops 276824064 | bytes 1048576 | tf_op jit(solution)/shard_map/attend_head/pallas_call | solution.py:208
  42.6 0.0 copy-start.6
  42.7 5.8 %collective-permute-start.8 = (bf16[2,256,128]{2,1,0:T(8,128)(2,1)S(1)}, bf16[2,256,128]{2,1,0:T(8,128)(2,1)S(1)}, u32[]{:S(2)}, u32[]{:S(2)}) collective-permute-start(bf16[2,256,128]{2,1,0:T(8,128)(2,1)S(1)} %get-tuple-element.142), channel_id=1, source_target_pairs={{0,1},{1,2},{2,3},{3,0},{4,5},{5,6},{6,7},{7,4},{8,9},{9,10},{10,1... | collective-permute-start | bytes 393224 | tf_op jit(solution)/shard_map/ppermute | solution.py:368
  48.5 1.5 %collective-permute-start.10 = (f32[8,128]{1,0:T(8,128)S(1)}, f32[8,128]{1,0:T(8,128)S(1)}, u32[]{:S(2)}, u32[]{:S(2)}) collective-permute-start(f32[8,128]{1,0:T(8,128)S(1)} %get-tuple-element.143.refs_0_), channel_id=1, source_target_pairs={{0,2},{1,3},{2,0},{3,1},{4,6},{5,7},{6,4},{7,5},{8,10},{9,11},{10,... | collective-permute-start | bytes 12296 | tf_op jit(solution)/shard_map/ppermute | solution.py:368
  50.0 0.5 collective-permute-start.9
  50.5 1.9 %collective-permute-done.11.refs_3_ = f32[8,128]{1,0:T(8,128)S(1)} collective-permute-done((f32[8,128]{1,0:T(8,128)S(1)}, f32[8,128]{1,0:T(8,128)S(1)}, u32[]{:S(2)}, u32[]{:S(2)}) %collective-permute-start.11) | collective-permute-done | bytes 4128 | tf_op jit(solution)/shard_map/ppermute | solution.py:368
  52.5 3.2 %collective-permute-done.10.refs_2_ = f32[8,128]{1,0:T(8,128)S(1)} collective-permute-done((f32[8,128]{1,0:T(8,128)S(1)}, f32[8,128]{1,0:T(8,128)S(1)}, u32[]{:S(2)}, u32[]{:S(2)}) %collective-permute-start.10) | collective-permute-done | bytes 4128 | tf_op jit(solution)/shard_map/ppermute | solution.py:368
  55.6 0.6 sum_gains.1
  56.2 0.1 join_parts.1.refs_0_
  56.3 1.2 %collective-permute-start.14 = (bf16[2,256,128]{2,1,0:T(8,128)(2,1)S(1)}, bf16[2,256,128]{2,1,0:T(8,128)(2,1)}, u32[]{:S(2)}, u32[]{:S(2)}) collective-permute-start(bf16[2,256,128]{2,1,0:T(8,128)(2,1)S(1)} %join_parts.1.refs_0_), channel_id=1, source_target_pairs={{0,3},{1,0},{2,1},{3,2},{4,7},{5,4},{6,5},{7,6},{8,11},{9,8},{10,9... | collective-permute-start | bytes 393224 | tf_op jit(solution)/shard_map/ppermute | solution.py:368
  57.5 1.2 %collective-permute-start.12 = (bf16[2,256,128]{2,1,0:T(8,128)(2,1)S(1)}, bf16[2,256,128]{2,1,0:T(8,128)(2,1)}, u32[]{:S(2)}, u32[]{:S(2)}) collective-permute-start(bf16[2,256,128]{2,1,0:T(8,128)(2,1)S(1)} %join_parts.1.refs_0_), channel_id=1, source_target_pairs={{0,1},{1,2},{2,3},{3,0},{4,5},{5,6},{6,7},{7,4},{8,9},{9,10},{10,1... | collective-permute-start | bytes 393224 | tf_op jit(solution)/shard_map/ppermute | solution.py:368
  58.7 1.2 %collective-permute-done.15 = f32[8,128]{1,0:T(8,128)S(1)} collective-permute-done((f32[8,128]{1,0:T(8,128)S(1)}, f32[8,128]{1,0:T(8,128)S(1)}, u32[]{:S(2)}, u32[]{:S(2)}) %collective-permute-start.15) | collective-permute-done | bytes 4128 | tf_op jit(solution)/shard_map/ppermute | solution.py:349
  59.9 1.5 %collective-permute-start.16 = (f32[8,128]{1,0:T(8,128)S(1)}, f32[8,128]{1,0:T(8,128)S(1)}, u32[]{:S(2)}, u32[]{:S(2)}) collective-permute-start(f32[8,128]{1,0:T(8,128)S(1)} %add.33), channel_id=1, source_target_pairs={{0,8},{4,12},{8,0},{12,4},{16,24},{20,28},{24,16},{28,20},{1,9},{5... | collective-permute-start | bytes 12296 | tf_op jit(solution)/shard_map/ppermute | solution.py:349
  61.3 2.1 %collective-permute-done.16 = f32[8,128]{1,0:T(8,128)S(1)} collective-permute-done((f32[8,128]{1,0:T(8,128)S(1)}, f32[8,128]{1,0:T(8,128)S(1)}, u32[]{:S(2)}, u32[]{:S(2)}) %collective-permute-start.16) | collective-permute-done | bytes 4128 | tf_op jit(solution)/shard_map/ppermute | solution.py:349
  63.5 1.5 %collective-permute-start.17 = (f32[8,128]{1,0:T(8,128)S(1)}, f32[8,128]{1,0:T(8,128)}, u32[]{:S(2)}, u32[]{:S(2)}) collective-permute-start(f32[8,128]{1,0:T(8,128)S(1)} %add.34), channel_id=1, source_target_pairs={{0,16},{4,20},{8,24},{12,28},{16,0},{20,4},{24,8},{28,12},{1,17},{... | collective-permute-start | bytes 12296 | tf_op jit(solution)/shard_map/ppermute | solution.py:349
  65.0 0.1 concatenate.9.meta
  65.1 0.7 copy-done.10
  65.8 0.9 %copy-done.5 = bf16[128,768]{1,0:T(8,128)(2,1)S(1)} copy-done((bf16[128,768]{1,0:T(8,128)(2,1)S(1)}, bf16[128,768]{1,0:T(8,128)(2,1)}, u32[]{:S(2)}) %copy-start.5) | copy-done | bytes 196632
  66.7 0.9 %copy-done.7 = bf16[128,768]{1,0:T(8,128)(2,1)S(1)} copy-done((bf16[128,768]{1,0:T(8,128)(2,1)S(1)}, bf16[128,768]{1,0:T(8,128)(2,1)}, u32[]{:S(2)}) %copy-start.7) | copy-done | bytes 196632
  67.7 0.7 copy-done.12
  68.4 0.7 copy-done.14
  69.1 0.7 copy-done.16
  69.9 0.9 %copy-done.18 = f32[192,128]{1,0:T(8,128)S(1)} copy-done((f32[192,128]{1,0:T(8,128)S(1)}, f32[192,128]{1,0:T(8,128)}, u32[]{:S(2)}) %copy-start.18) | copy-done | bytes 98328
  70.8 0.9 %copy-done.20 = f32[192,128]{1,0:T(8,128)S(1)} copy-done((f32[192,128]{1,0:T(8,128)S(1)}, f32[192,128]{1,0:T(8,128)}, u32[]{:S(2)}) %copy-start.20) | copy-done | bytes 98328
  71.7 0.9 %copy-done.22 = f32[192,128]{1,0:T(8,128)S(1)} copy-done((f32[192,128]{1,0:T(8,128)S(1)}, f32[192,128]{1,0:T(8,128)}, u32[]{:S(2)}) %copy-start.22) | copy-done | bytes 98328
  72.6 0.9 %copy-done.24 = f32[192,128]{1,0:T(8,128)S(1)} copy-done((f32[192,128]{1,0:T(8,128)S(1)}, f32[192,128]{1,0:T(8,128)}, u32[]{:S(2)}) %copy-start.24) | copy-done | bytes 98328
  73.4 0.8 copy-done.26
  74.2 0.8 copy-done.28
  75.0 0.8 copy-done.30
  75.8 0.8 copy-done.32
  76.6 2.9 %finish_response.1 = (bf16[192,2048]{1,0:T(8,128)(2,1)}, bf16[192,2048]{1,0:T(8,128)(2,1)}, bf16[192,512]{1,0:T(8,128)(2,1)}, bf16[192,512]{1,0:T(8,128)(2,1)}) custom-call(s32[5]{0:T(128)S(1)} %concatenate.8.meta, bf16[192,512]{1,0:T(8,128)(2,1)S(1)} %bitcast.24, f32[128,1]{1,0:T(8,128)S(1)} %copy.20.gain_ref, f32[1,128]{1,0:T(1,128)S(1)} %bitcast.30, ...), custom_call_target="tpu_custom_call" | custom-call | flops 15728640 | bytes 3932160 | tf_op jit(solution)/shard_map/finish_response/pallas_call | solution.py:267
  79.5 0.7 add.35
  80.2 0.6 slice.3
  80.8 1.9 %place_prompt_grad.1 = bf16[2,256,512]{2,1,0:T(8,128)(2,1)} custom-call(s32[5]{0:T(128)S(1)} %concatenate.9.meta, bf16[2,256,128]{2,1,0:T(8,128)(2,1)S(1)} %join_parts.1.refs_0_, bf16[2,256,128]{2,1,0:T(8,128)(2,1)} %collective-permute-done.12.refs_1_, bf16[2,256,128]{2,1,0:T(8,128)(2,1)} %collective-permute-done.13.refs_2_, ...), custom_call_target="tpu_custom_call" | custom-call | tf_op jit(solution)/shard_map/place_prompt_grad/pallas_call | solution.py:336
  (62 shorter events, 0.1 us)
Async XLA Ops:
  0.8 1.0 %copy-start.3 = (bf16[1,1,2,256,512]{4,3,2,1,0:T(8,128)(2,1)S(1)}, bf16[1,1,2,256,512]{4,3,2,1,0:T(8,128)(2,1)}, u32[]{:S(2)}) copy-start(bf16[1,1,2,256,512]{4,3,2,1,0:T(8,128)(2,1)} %param.12) | copy-start | bytes 1572868
  1.8 9.0 %copy-start = (bf16[1,1,192,512]{3,2,1,0:T(8,128)(2,1)S(1)}, bf16[1,1,192,512]{3,2,1,0:T(8,128)(2,1)}, u32[]{:S(2)}) copy-start(bf16[1,1,192,512]{3,2,1,0:T(8,128)(2,1)} %param.10) | copy-start | bytes 589828
  1.8 9.0 %copy-start.8 = (bf16[1,1,192,512]{3,2,1,0:T(8,128)(2,1)S(1)}, bf16[1,1,192,512]{3,2,1,0:T(8,128)(2,1)}, u32[]{:S(2)}) copy-start(bf16[1,1,192,512]{3,2,1,0:T(8,128)(2,1)} %param.11) | copy-start | bytes 589828
  2.5 14.7 %collective-permute-start = (bf16[2,256,128]{2,1,0:T(8,128)(2,1)S(1)}, bf16[2,256,128]{2,1,0:T(8,128)(2,1)S(1)}, u32[]{:S(2)}, u32[]{:S(2)}) collective-permute-start(bf16[2,256,128]{2,1,0:T(8,128)(2,1)S(1)} %get-tuple-element.77), channel_id=1, source_target_pairs={{0,3},{1,0},{2,1},{3,2},{4,7},{5,4},{6,5},{7,6},{8,11},{9,8},{10,9... | collective-permute-start | bytes 393224 | tf_op jit(solution)/shard_map/ppermute | solution.py:368
  7.6 11.2 %collective-permute-start.1 = (bf16[2,256,128]{2,1,0:T(8,128)(2,1)S(1)}, bf16[2,256,128]{2,1,0:T(8,128)(2,1)S(1)}, u32[]{:S(2)}, u32[]{:S(2)}) collective-permute-start(bf16[2,256,128]{2,1,0:T(8,128)(2,1)S(1)} %get-tuple-element.83), channel_id=1, source_target_pairs={{0,2},{1,3},{2,0},{3,1},{4,6},{5,7},{6,4},{7,5},{8,10},{9,11},{10,... | collective-permute-start | bytes 393224 | tf_op jit(solution)/shard_map/ppermute | solution.py:368
  7.6 11.2 %collective-permute-start.2 = (bf16[2,256,128]{2,1,0:T(8,128)(2,1)S(1)}, bf16[2,256,128]{2,1,0:T(8,128)(2,1)S(1)}, u32[]{:S(2)}, u32[]{:S(2)}) collective-permute-start(bf16[2,256,128]{2,1,0:T(8,128)(2,1)S(1)} %get-tuple-element.84), channel_id=1, source_target_pairs={{0,1},{1,2},{2,3},{3,0},{4,5},{5,6},{6,7},{7,4},{8,9},{9,10},{10,1... | collective-permute-start | bytes 393224 | tf_op jit(solution)/shard_map/ppermute | solution.py:368
  10.0 0.7 copy-start.34
  10.8 0.7 copy-start.33
  11.5 1.1 %copy-start.1 = (bf16[1,1,192,2048]{3,2,1,0:T(8,128)(2,1)S(1)}, bf16[1,1,192,2048]{3,2,1,0:T(8,128)(2,1)}, u32[]{:S(2)}) copy-start(bf16[1,1,192,2048]{3,2,1,0:T(8,128)(2,1)} %param.9) | copy-start | bytes 2359300
  12.6 1.1 %copy-start.2 = (bf16[1,1,192,2048]{3,2,1,0:T(8,128)(2,1)S(1)}, bf16[1,1,192,2048]{3,2,1,0:T(8,128)(2,1)}, u32[]{:S(2)}) copy-start(bf16[1,1,192,2048]{3,2,1,0:T(8,128)(2,1)} %param.17) | copy-start | bytes 2359300
  17.2 6.4 %copy-start.9 = (f32[8,768]{1,0:T(8,128)}, f32[8,768]{1,0:T(8,128)S(1)}, u32[]{:S(2)}) copy-start(f32[8,768]{1,0:T(8,128)S(1)} %get-tuple-element.79.row_ref.refs_1_) | copy-start | bytes 73732
  17.2 10.1 %copy-start.11 = (f32[8,768]{1,0:T(8,128)}, f32[8,768]{1,0:T(8,128)S(1)}, u32[]{:S(2)}) copy-start(f32[8,768]{1,0:T(8,128)S(1)} %get-tuple-element.95.row_ref.refs_8_) | copy-start | bytes 73732
  17.2 17.5 %copy-start.13 = (f32[8,768]{1,0:T(8,128)}, f32[8,768]{1,0:T(8,128)S(1)}, u32[]{:S(2)}) copy-start(f32[8,768]{1,0:T(8,128)S(1)} %get-tuple-element.108.row_ref.refs_15_) | copy-start | bytes 73732
  17.2 23.7 %copy-start.15 = (f32[8,768]{1,0:T(8,128)}, f32[8,768]{1,0:T(8,128)S(1)}, u32[]{:S(2)}) copy-start(f32[8,768]{1,0:T(8,128)S(1)} %get-tuple-element.121.row_ref.refs_22_) | copy-start | bytes 73732
  18.9 8.3 %collective-permute-start.3 = (bf16[2,256,128]{2,1,0:T(8,128)(2,1)S(1)}, bf16[2,256,128]{2,1,0:T(8,128)(2,1)S(1)}, u32[]{:S(2)}, u32[]{:S(2)}) collective-permute-start(bf16[2,256,128]{2,1,0:T(8,128)(2,1)S(1)} %pick_owner.1.pr_ref), channel_id=1, source_target_pairs={{0,1},{1,2},{2,3},{3,0},{4,5},{5,6},{6,7},{7,4},{8,9},{9,10},{10,1... | collective-permute-start | bytes 393224 | tf_op jit(solution)/shard_map/ppermute | solution.py:368
  19.9 21.1 %collective-permute-start.5 = (bf16[2,256,128]{2,1,0:T(8,128)(2,1)S(1)}, bf16[2,256,128]{2,1,0:T(8,128)(2,1)S(1)}, u32[]{:S(2)}, u32[]{:S(2)}) collective-permute-start(bf16[2,256,128]{2,1,0:T(8,128)(2,1)S(1)} %pick_owner.1.pr_ref), channel_id=1, source_target_pairs={{0,3},{1,0},{2,1},{3,2},{4,7},{5,4},{6,5},{7,6},{8,11},{9,8},{10,9... | collective-permute-start | bytes 393224 | tf_op jit(solution)/shard_map/ppermute | solution.py:368
  22.8 11.9 %collective-permute-start.4 = (bf16[2,256,128]{2,1,0:T(8,128)(2,1)S(1)}, bf16[2,256,128]{2,1,0:T(8,128)(2,1)S(1)}, u32[]{:S(2)}, u32[]{:S(2)}) collective-permute-start(bf16[2,256,128]{2,1,0:T(8,128)(2,1)S(1)} %pick_owner.1.pr_ref), channel_id=1, source_target_pairs={{0,2},{1,3},{2,0},{3,1},{4,6},{5,7},{6,4},{7,5},{8,10},{9,11},{10,... | collective-permute-start | bytes 393224 | tf_op jit(solution)/shard_map/ppermute | solution.py:368
  25.3 3.6 %copy-start.17 = (f32[192,128]{1,0:T(8,128)}, f32[192,128]{1,0:T(8,128)S(1)}, u32[]{:S(2)}) copy-start(f32[192,128]{1,0:T(8,128)S(1)} %get-tuple-element.92.refs_5_) | copy-start | bytes 294916
  25.3 3.6 %copy-start.25 = (bf16[192,128]{1,0:T(8,128)(2,1)}, bf16[192,128]{1,0:T(8,128)(2,1)S(1)}, u32[]{:S(2)}) copy-start(bf16[192,128]{1,0:T(8,128)(2,1)S(1)} %get-tuple-element.93.refs_6_) | copy-start | bytes 147460
  29.0 7.4 %copy-start.19 = (f32[192,128]{1,0:T(8,128)}, f32[192,128]{1,0:T(8,128)S(1)}, u32[]{:S(2)}) copy-start(f32[192,128]{1,0:T(8,128)S(1)} %get-tuple-element.105.refs_12_) | copy-start | bytes 294916
  29.0 7.4 %copy-start.27 = (bf16[192,128]{1,0:T(8,128)(2,1)}, bf16[192,128]{1,0:T(8,128)(2,1)S(1)}, u32[]{:S(2)}) copy-start(bf16[192,128]{1,0:T(8,128)(2,1)S(1)} %get-tuple-element.106.refs_13_) | copy-start | bytes 147460
  29.0 11.9 %collective-permute-start.6 = (bf16[2,256,128]{2,1,0:T(8,128)(2,1)S(1)}, bf16[2,256,128]{2,1,0:T(8,128)(2,1)S(1)}, u32[]{:S(2)}, u32[]{:S(2)}) collective-permute-start(bf16[2,256,128]{2,1,0:T(8,128)(2,1)S(1)} %get-tuple-element.123), channel_id=1, source_target_pairs={{0,3},{1,0},{2,1},{3,2},{4,7},{5,4},{6,5},{7,6},{8,11},{9,8},{10,9... | collective-permute-start | bytes 393224 | tf_op jit(solution)/shard_map/ppermute | solution.py:368
  36.4 0.7 copy-start.4
  37.1 0.6 copy-start.29
  37.7 5.0 %copy-start.21 = (f32[192,128]{1,0:T(8,128)}, f32[192,128]{1,0:T(8,128)S(1)}, u32[]{:S(2)}) copy-start(f32[192,128]{1,0:T(8,128)S(1)} %get-tuple-element.118.refs_19_) | copy-start | bytes 294916
  37.7 18.5 %collective-permute-start.7 = (bf16[2,256,128]{2,1,0:T(8,128)(2,1)S(1)}, bf16[2,256,128]{2,1,0:T(8,128)(2,1)S(1)}, u32[]{:S(2)}, u32[]{:S(2)}) collective-permute-start(bf16[2,256,128]{2,1,0:T(8,128)(2,1)S(1)} %get-tuple-element.141), channel_id=1, source_target_pairs={{0,2},{1,3},{2,0},{3,1},{4,6},{5,7},{6,4},{7,5},{8,10},{9,11},{10,... | collective-permute-start | bytes 393224 | tf_op jit(solution)/shard_map/ppermute | solution.py:368
  42.6 13.7 %copy-start.6 = (bf16[128,768]{1,0:T(8,128)(2,1)}, bf16[128,768]{1,0:T(8,128)(2,1)S(1)}, u32[]{:S(2)}) copy-start(bf16[128,768]{1,0:T(8,128)(2,1)S(1)} %get-tuple-element.131.refs_24_) | copy-start | bytes 589828
  42.7 13.7 %copy-start.23 = (f32[192,128]{1,0:T(8,128)}, f32[192,128]{1,0:T(8,128)S(1)}, u32[]{:S(2)}) copy-start(f32[192,128]{1,0:T(8,128)S(1)} %get-tuple-element.133.refs_26_) | copy-start | bytes 294916
  42.7 13.7 %copy-start.31 = (bf16[192,128]{1,0:T(8,128)(2,1)}, bf16[192,128]{1,0:T(8,128)(2,1)S(1)}, u32[]{:S(2)}) copy-start(bf16[192,128]{1,0:T(8,128)(2,1)S(1)} %get-tuple-element.134.refs_27_) | copy-start | bytes 147460
  42.7 13.5 %collective-permute-start.8 = (bf16[2,256,128]{2,1,0:T(8,128)(2,1)S(1)}, bf16[2,256,128]{2,1,0:T(8,128)(2,1)S(1)}, u32[]{:S(2)}, u32[]{:S(2)}) collective-permute-start(bf16[2,256,128]{2,1,0:T(8,128)(2,1)S(1)} %get-tuple-element.142), channel_id=1, source_target_pairs={{0,1},{1,2},{2,3},{3,0},{4,5},{5,6},{6,7},{7,4},{8,9},{9,10},{10,1... | collective-permute-start | bytes 393224 | tf_op jit(solution)/shard_map/ppermute | solution.py:368
  48.5 4.0 %collective-permute-start.11 = (f32[8,128]{1,0:T(8,128)S(1)}, f32[8,128]{1,0:T(8,128)S(1)}, u32[]{:S(2)}, u32[]{:S(2)}) collective-permute-start(f32[8,128]{1,0:T(8,128)S(1)} %get-tuple-element.143.refs_0_), channel_id=1, source_target_pairs={{0,3},{1,0},{2,1},{3,2},{4,7},{5,4},{6,5},{7,6},{8,11},{9,8},{10,9... | collective-permute-start | bytes 12296 | tf_op jit(solution)/shard_map/ppermute | solution.py:368
  48.5 7.2 %collective-permute-start.10 = (f32[8,128]{1,0:T(8,128)S(1)}, f32[8,128]{1,0:T(8,128)S(1)}, u32[]{:S(2)}, u32[]{:S(2)}) collective-permute-start(f32[8,128]{1,0:T(8,128)S(1)} %get-tuple-element.143.refs_0_), channel_id=1, source_target_pairs={{0,2},{1,3},{2,0},{3,1},{4,6},{5,7},{6,4},{7,5},{8,10},{9,11},{10,... | collective-permute-start | bytes 12296 | tf_op jit(solution)/shard_map/ppermute | solution.py:368
  50.0 5.6 %collective-permute-start.9 = (f32[8,128]{1,0:T(8,128)S(1)}, f32[8,128]{1,0:T(8,128)S(1)}, u32[]{:S(2)}, u32[]{:S(2)}) collective-permute-start(f32[8,128]{1,0:T(8,128)S(1)} %get-tuple-element.143.refs_0_), channel_id=1, source_target_pairs={{0,1},{1,2},{2,3},{3,0},{4,5},{5,6},{6,7},{7,4},{8,9},{9,10},{10,1... | collective-permute-start | bytes 12296 | tf_op jit(solution)/shard_map/ppermute | solution.py:368
  56.3 24.5 %collective-permute-start.14 = (bf16[2,256,128]{2,1,0:T(8,128)(2,1)S(1)}, bf16[2,256,128]{2,1,0:T(8,128)(2,1)}, u32[]{:S(2)}, u32[]{:S(2)}) collective-permute-start(bf16[2,256,128]{2,1,0:T(8,128)(2,1)S(1)} %join_parts.1.refs_0_), channel_id=1, source_target_pairs={{0,3},{1,0},{2,1},{3,2},{4,7},{5,4},{6,5},{7,6},{8,11},{9,8},{10,9... | collective-permute-start | bytes 393224 | tf_op jit(solution)/shard_map/ppermute | solution.py:368
  57.5 23.3 %collective-permute-start.13 = (bf16[2,256,128]{2,1,0:T(8,128)(2,1)S(1)}, bf16[2,256,128]{2,1,0:T(8,128)(2,1)}, u32[]{:S(2)}, u32[]{:S(2)}) collective-permute-start(bf16[2,256,128]{2,1,0:T(8,128)(2,1)S(1)} %join_parts.1.refs_0_), channel_id=1, source_target_pairs={{0,2},{1,3},{2,0},{3,1},{4,6},{5,7},{6,4},{7,5},{8,10},{9,11},{10,... | collective-permute-start | bytes 393224 | tf_op jit(solution)/shard_map/ppermute | solution.py:368
  57.5 23.3 %collective-permute-start.12 = (bf16[2,256,128]{2,1,0:T(8,128)(2,1)S(1)}, bf16[2,256,128]{2,1,0:T(8,128)(2,1)}, u32[]{:S(2)}, u32[]{:S(2)}) collective-permute-start(bf16[2,256,128]{2,1,0:T(8,128)(2,1)S(1)} %join_parts.1.refs_0_), channel_id=1, source_target_pairs={{0,1},{1,2},{2,3},{3,0},{4,5},{5,6},{6,7},{7,4},{8,9},{9,10},{10,1... | collective-permute-start | bytes 393224 | tf_op jit(solution)/shard_map/ppermute | solution.py:368
  58.7 1.2 %collective-permute-start.15 = (f32[8,128]{1,0:T(8,128)S(1)}, f32[8,128]{1,0:T(8,128)S(1)}, u32[]{:S(2)}, u32[]{:S(2)}) collective-permute-start(f32[8,128]{1,0:T(8,128)S(1)} %sum_gains.1), channel_id=1, source_target_pairs={{0,4},{4,0},{8,12},{12,8},{16,20},{20,16},{24,28},{28,24},{1,5},{5... | collective-permute-start | bytes 12296 | tf_op jit(solution)/shard_map/ppermute | solution.py:349
  59.9 3.6 %collective-permute-start.16 = (f32[8,128]{1,0:T(8,128)S(1)}, f32[8,128]{1,0:T(8,128)S(1)}, u32[]{:S(2)}, u32[]{:S(2)}) collective-permute-start(f32[8,128]{1,0:T(8,128)S(1)} %add.33), channel_id=1, source_target_pairs={{0,8},{4,12},{8,0},{12,4},{16,24},{20,28},{24,16},{28,20},{1,9},{5... | collective-permute-start | bytes 12296 | tf_op jit(solution)/shard_map/ppermute | solution.py:349
  63.5 16.1 %collective-permute-start.17 = (f32[8,128]{1,0:T(8,128)S(1)}, f32[8,128]{1,0:T(8,128)}, u32[]{:S(2)}, u32[]{:S(2)}) collective-permute-start(f32[8,128]{1,0:T(8,128)S(1)} %add.34), channel_id=1, source_target_pairs={{0,16},{4,20},{8,24},{12,28},{16,0},{20,4},{24,8},{28,12},{1,17},{... | collective-permute-start | bytes 12296 | tf_op jit(solution)/shard_map/ppermute | solution.py:349
  65.1 0.7 copy-start.10
  65.8 0.9 %copy-start.5 = (bf16[128,768]{1,0:T(8,128)(2,1)S(1)}, bf16[128,768]{1,0:T(8,128)(2,1)}, u32[]{:S(2)}) copy-start(bf16[128,768]{1,0:T(8,128)(2,1)} %copy-done.4) | copy-start | bytes 589828
  66.7 0.9 %copy-start.7 = (bf16[128,768]{1,0:T(8,128)(2,1)S(1)}, bf16[128,768]{1,0:T(8,128)(2,1)}, u32[]{:S(2)}) copy-start(bf16[128,768]{1,0:T(8,128)(2,1)} %copy-done.6) | copy-start | bytes 589828
  67.7 0.7 copy-start.12
  68.4 0.7 copy-start.14
  69.1 0.7 copy-start.16
  69.9 0.9 %copy-start.18 = (f32[192,128]{1,0:T(8,128)S(1)}, f32[192,128]{1,0:T(8,128)}, u32[]{:S(2)}) copy-start(f32[192,128]{1,0:T(8,128)} %copy-done.17) | copy-start | bytes 294916
  70.8 0.9 %copy-start.20 = (f32[192,128]{1,0:T(8,128)S(1)}, f32[192,128]{1,0:T(8,128)}, u32[]{:S(2)}) copy-start(f32[192,128]{1,0:T(8,128)} %copy-done.19) | copy-start | bytes 294916
  71.7 0.9 %copy-start.22 = (f32[192,128]{1,0:T(8,128)S(1)}, f32[192,128]{1,0:T(8,128)}, u32[]{:S(2)}) copy-start(f32[192,128]{1,0:T(8,128)} %copy-done.21) | copy-start | bytes 294916
  72.6 0.9 %copy-start.24 = (f32[192,128]{1,0:T(8,128)S(1)}, f32[192,128]{1,0:T(8,128)}, u32[]{:S(2)}) copy-start(f32[192,128]{1,0:T(8,128)} %copy-done.23) | copy-start | bytes 294916
  73.4 0.8 copy-start.26
  74.2 0.8 copy-start.28
  75.0 0.8 copy-start.30
  75.8 0.8 copy-start.32

commit v4 on v3

--- a/solution.py
+++ b/solution.py
@@ -24,7 +24,7 @@
 
 VMEM = pl.BlockSpec(memory_space=pltpu.VMEM)
 SMEM = pl.BlockSpec(memory_space=pltpu.SMEM)
-ANY = pl.BlockSpec(memory_space=pl.ANY)
+HBM = pl.BlockSpec(memory_space=pltpu.HBM)
 
 
 def params(mib):
@@ -48,7 +48,7 @@
     return pl.pallas_call(
         cut_kernel,
         out_shape=[jax.ShapeDtypeStruct((depth, rows, HD), BF)] * count,
-        in_specs=[SMEM, ANY],
+        in_specs=[SMEM, HBM],
         out_specs=[VMEM] * count,
         scratch_shapes=[pltpu.SemaphoreType.DMA((count,))],
         compiler_params=params(4),
@@ -77,29 +77,39 @@
 KEPT = 8
 
 
-def prepare_kernel(count, share, rows, width, meta, q_ref, g_ref, k_ref, v_ref, gain_ref, kg_ref, *outs):
+def prepare_kernel(count, share, rows, width, meta, q_in, g_in, k_in, v_in, gain_ref, kg_ref, *rest):
+    outs, (q_buf, g_buf, k_buf, v_buf, sems) = rest[:-5], rest[-5:]
     live_len = meta[count]
     scale = HD ** (-0.5)
+    wide = share * HD
+    copies = []
+    for s in range(count):
+        group = []
+        for j, (src, buf, size) in enumerate(
+            ((q_in, q_buf, wide), (k_in, k_buf, HD), (g_in, g_buf, wide), (v_in, v_buf, HD))
+        ):
+            at = pl.multiple_of(meta[s] * size, size)
+            copy = pltpu.make_async_copy(src.at[:, pl.ds(at, size)], buf.at[s], sems.at[s, j])
+            copy.start()
+            group.append(copy)
+        copies.append(group)
     q_gain = gain_ref[...]
     k_gain = kg_ref[...]
     for s in range(count):
         qt_ref, gt_ref, row_ref, er_ref, ot_ref, dp_ref, kh_ref, ku_ref = outs[s * KEPT : (s + 1) * KEPT]
-        base = meta[s]
-
-        def stacked(ref):
-            at = [pl.multiple_of((base * share + i) * HD, HD) for i in range(share)]
-            return jnp.concatenate([ref[:, pl.ds(x, HD)] for x in at], axis=0)
-
-        q_t = stacked(q_ref).T
-        g_t = stacked(g_ref).T
+        for copy in copies[s]:
+            copy.wait()
+        q_t = jnp.concatenate([q_buf[s, :, i * HD : (i + 1) * HD] for i in range(share)], axis=0).T
+        g_t = jnp.concatenate([g_buf[s, :, i * HD : (i + 1) * HD] for i in range(share)], axis=0).T
         qt_ref[...] = q_t
-        k_at = pl.ds(pl.multiple_of(base * HD, HD), HD)
-        raw_k = k_ref[:, k_at].astype(F32)
-        k_unit = raw_k * lax.rsqrt(jnp.mean(raw_k * raw_k, axis=-1, keepdims=True) + EPS)
+        raw_k = k_buf[s].astype(F32)
+        k_inv = lax.rsqrt(jnp.mean(raw_k * raw_k, axis=-1, keepdims=True) + EPS)
+        k_unit = raw_k * k_inv
         k_hat = (k_unit * k_gain).astype(BF)
         kh_ref[...] = k_hat
-        ku_ref[...] = k_unit
-        r_val = v_ref[:, k_at]
+        ku_ref[:, :HD] = k_unit
+        ku_ref[:, HD:] = jnp.broadcast_to(k_inv, (rows, HD))
+        r_val = v_buf[s]
         r_val_t = r_val.T
         for start in range(0, share * rows, width):
             cols = slice(start, start + width)
@@ -131,14 +141,21 @@
         jax.ShapeDtypeStruct((HD, total), F32),
         jax.ShapeDtypeStruct((rows, total), F32),
         jax.ShapeDtypeStruct((rows, HD), BF),
-        jax.ShapeDtypeStruct((rows, HD), F32),
+        jax.ShapeDtypeStruct((rows, 2 * HD), F32),
     ]
     outs = pl.pallas_call(
         functools.partial(prepare_kernel, count, share, rows, 2 * HD),
         out_shape=each * count,
-        in_specs=[SMEM] + [VMEM] * 6,
+        in_specs=[SMEM] + [HBM] * 4 + [VMEM] * 2,
         out_specs=[VMEM] * (KEPT * count),
-        compiler_params=params(24),
+        scratch_shapes=[
+            pltpu.VMEM((count, rows, share * HD), BF),
+            pltpu.VMEM((count, rows, share * HD), BF),
+            pltpu.VMEM((count, rows, HD), BF),
+            pltpu.VMEM((count, rows, HD), BF),
+            pltpu.SemaphoreType.DMA((count, 4)),
+        ],
+        compiler_params=params(16),
         cost_estimate=pl.CostEstimate(
             flops=6 * count * total * rows * HD,
             bytes_accessed=5 * rows * q_width * 2,
@@ -149,12 +166,9 @@
     return [list(outs[s * KEPT : (s + 1) * KEPT]) for s in range(count)]
 
 
-def head_kernel(
-    width, pr_ref, qt_ref, gt_ref, row_ref, er_ref, ot_ref, dp_ref, kh_ref, ku_ref, gain_ref, acc_ref,
-    part_ref, at_ref, dq_ref, dkr_ref, dvr_ref, gacc_ref,
-):
+def attend(width, pr_ref, kept, q_gain, acc_ref, part_ref, at_ref, dq_ref, gacc_ref):
+    qt_ref, gt_ref, row_ref, er_ref, ot_ref, dp_ref, kh_ref, ku_ref = kept
     scale = HD ** (-0.5)
-    q_gain = gain_ref[...]
     p_key = pr_ref[0]
     p_val = pr_ref[1]
     k_hat_t = kh_ref[...].T
@@ -192,94 +206,160 @@
     d_kp, d_vp, d_kr, d_vr, q_term = sums
     part_ref[0] = d_kp.astype(BF)
     part_ref[1] = d_vp.astype(BF)
-    dkr_ref[...] = d_kr
-    dvr_ref[...] = d_vr.astype(BF)
     folded = q_term[:, :HD]
     for start in range(HD, width, HD):
         folded = folded + q_term[:, start : start + HD]
     gacc_ref[0:1, :] = acc_ref[0:1, :] + jnp.sum(folded.T, axis=0, keepdims=True)
-    gacc_ref[1:2, :] = acc_ref[1:2, :] + jnp.sum(d_kr * ku_ref[...], axis=0, keepdims=True)
-    gacc_ref[2:8, :] = jnp.zeros((6, HD), F32)
-
-
-def one_head(prompt, kept, q_gain, acc):
+    gacc_ref[1:2, :] = acc_ref[1:2, :] + jnp.sum(d_kr * ku_ref[:, :HD], axis=0, keepdims=True)
+    return d_kr, d_vr
+
+
+def settle(width, head, live_len, kept, q_gain, k_gain, at_ref, dq_ref, d_kr, d_vr, outs, bufs, sems):
+    qt_ref, row_ref, ku_ref = kept[0], kept[2], kept[7]
+    a_buf, q_buf, k_buf, v_buf = bufs
+    rows, wide = a_buf.shape
+    share = wide // HD
+    copies = []
+
+    def send(j, buf):
+        size = buf.shape[1]
+        at = pl.multiple_of(head * size, size)
+        copy = pltpu.make_async_copy(buf, outs[j].at[:, pl.ds(at, size)], sems.at[j])
+        copy.start()
+        copies.append(copy)
+
+    att = at_ref[...].T
+    live = lax.broadcasted_iota(jnp.int32, (rows, HD), 0) < live_len
+    for i in range(share):
+        block = att[i * rows : (i + 1) * rows, :].astype(F32)
+        a_buf[:, i * HD : (i + 1) * HD] = jnp.where(live, block, 0.0).astype(BF)
+    send(0, a_buf)
+    v_buf[...] = d_vr.astype(BF)
+    send(3, v_buf)
+    k_unit = ku_ref[:, :HD]
+    up_k = d_kr * k_gain
+    mean_k = jnp.mean(up_k * k_unit, axis=-1, keepdims=True)
+    k_buf[...] = (ku_ref[:, HD:] * (up_k - k_unit * mean_k)).astype(BF)
+    send(2, k_buf)
+    parts = []
+    for start in range(0, share * rows, width):
+        cols = slice(start, start + width)
+        q_inv = row_ref[0:1, cols]
+        q_unit = qt_ref[:, cols].astype(F32) * q_inv
+        up = dq_ref[:, cols] * q_gain
+        mean = jnp.mean(up * q_unit, axis=0, keepdims=True)
+        parts.append((q_inv * (up - q_unit * mean)).astype(BF))
+    d_q = jnp.concatenate(parts, axis=1).T
+    for i in range(share):
+        q_buf[:, i * HD : (i + 1) * HD] = d_q[i * rows : (i + 1) * rows, :]
+    send(1, q_buf)
+    for copy in copies:
+        copy.wait()
+
+
+def whole_kernel(s, width, meta, pr_ref, *rest):
+    kept, (gain_ref, kg_ref, acc_ref) = rest[:KEPT], rest[KEPT : KEPT + 3]
+    part_ref, gacc_ref, *rest = rest[-13:]
+    outs, (at_ref, dq_ref), bufs, sems = rest[:4], rest[4:6], rest[6:10], rest[10]
+    q_gain = gain_ref[...]
+    d_kr, d_vr = attend(width, pr_ref, kept, q_gain, acc_ref, part_ref, at_ref, dq_ref, gacc_ref)
+    live_len = meta[meta.shape[0] - 1]
+    settle(width, meta[s], live_len, kept, q_gain, kg_ref[...], at_ref, dq_ref, d_kr, d_vr, outs, bufs, sems)
+
+
+def first_kernel(width, pr_ref, *rest):
+    kept, (gain_ref, acc_ref) = rest[:KEPT], rest[KEPT : KEPT + 2]
+    part_ref, gacc_ref, at_ref, dq_ref, dkr_ref, dvr_ref = rest[-6:]
+    d_kr, d_vr = attend(width, pr_ref, kept, gain_ref[...], acc_ref, part_ref, at_ref, dq_ref, gacc_ref)
+    dkr_ref[...] = d_kr
+    dvr_ref[...] = d_vr
+
+
+def second_kernel(s, width, meta, *rest):
+    kept, (gain_ref, kg_ref, at_ref, dq_ref, dkr_ref, dvr_ref) = rest[:KEPT], rest[KEPT : KEPT + 6]
+    outs, bufs, sems = rest[-9:-5], rest[-5:-1], rest[-1]
+    live_len = meta[meta.shape[0] - 1]
+    settle(
+        width, meta[s], live_len, kept, gain_ref[...], kg_ref[...], at_ref, dq_ref,
+        dkr_ref[...], dvr_ref[...], outs, bufs, sems,
+    )
+
+
+def out_shapes(rows, q_width, k_width):
+    widths = (q_width, q_width, k_width, k_width)
+    return [jax.ShapeDtypeStruct((rows, w), BF) for w in widths]
+
+
+def out_scratch(rows, share):
+    widths = (share * HD, share * HD, HD, HD)
+    return [pltpu.VMEM((rows, w), BF) for w in widths] + [pltpu.SemaphoreType.DMA((4,))]
+
+
+def cost(prompt_rows, rows, total):
+    return pl.CostEstimate(
+        flops=(8 * prompt_rows + 4 * rows) * total * HD,
+        bytes_accessed=2**20,
+        transcendentals=total * prompt_rows,
+    )
+
+
+def whole_head(s, meta, prompt, kept, q_gain, k_gain, acc, buffers, q_width, k_width):
     total = kept[0].shape[1]
     rows = kept[3].shape[0]
-    return pl.pallas_call(
-        functools.partial(head_kernel, 2 * HD),
+    outs = pl.pallas_call(
+        functools.partial(whole_kernel, s, 2 * HD),
         out_shape=[
             jax.ShapeDtypeStruct(prompt.shape, BF),
+            jax.ShapeDtypeStruct(acc.shape, F32),
+        ]
+        + out_shapes(rows, q_width, k_width),
+        in_specs=[SMEM] + [VMEM] * (4 + KEPT) + [HBM] * len(buffers),
+        out_specs=[VMEM] * 2 + [HBM] * 4,
+        scratch_shapes=[pltpu.VMEM((HD, total), BF), pltpu.VMEM((HD, total), F32)]
+        + out_scratch(rows, total // rows),
+        input_output_aliases={5 + KEPT + i: 2 + i for i in range(len(buffers))},
+        compiler_params=params(16),
+        cost_estimate=cost(prompt.shape[1], rows, total),
+        name="attend_head",
+    )(meta, prompt, *kept, q_gain, k_gain, acc, *buffers)
+    return outs[0], outs[1], outs[2:]
+
+
+def first_half(prompt, kept, q_gain, acc):
+    total = kept[0].shape[1]
+    rows = kept[3].shape[0]
+    return pl.pallas_call(
+        functools.partial(first_kernel, 2 * HD),
+        out_shape=[
+            jax.ShapeDtypeStruct(prompt.shape, BF),
+            jax.ShapeDtypeStruct(acc.shape, F32),
             jax.ShapeDtypeStruct((HD, total), BF),
             jax.ShapeDtypeStruct((HD, total), F32),
             jax.ShapeDtypeStruct((rows, HD), F32),
-            jax.ShapeDtypeStruct((rows, HD), BF),
-            jax.ShapeDtypeStruct(acc.shape, F32),
+            jax.ShapeDtypeStruct((rows, HD), F32),
         ],
-        in_specs=[VMEM] * 11,
+        in_specs=[VMEM] * (3 + KEPT),
         out_specs=[VMEM] * 6,
         compiler_params=params(16),
-        cost_estimate=pl.CostEstimate(
-            flops=(8 * prompt.shape[1] + 4 * rows) * total * HD,
-            bytes_accessed=2**20,
-            transcendentals=total * prompt.shape[1],
-        ),
-        name="attend_head",
+        cost_estimate=cost(prompt.shape[1], rows, total),
+        name="attend_last_head",
     )(prompt, *kept, q_gain, acc)
 
 
-def finish_kernel(count, share, rows, width, meta, k_ref, gain_ref, kg_ref, *refs):
-    ins, (att_ref, dq_ref, dk_ref, dv_ref) = refs[:-4], refs[-4:]
-    live_len = meta[count]
-    q_gain = gain_ref[...]
-    k_gain = kg_ref[...]
-    for s in range(count):
-        qt_ref, row_ref, ku_ref, at_in, dq_in, dkr_ref, dvr_ref = ins[s * 7 : (s + 1) * 7]
-        base = meta[s]
-        k_at = pl.ds(pl.multiple_of(base * HD, HD), HD)
-        dv_ref[:, k_at] = dvr_ref[...]
-        raw_k = k_ref[:, k_at].astype(F32)
-        k_inv = lax.rsqrt(jnp.mean(raw_k * raw_k, axis=-1, keepdims=True) + EPS)
-        k_unit = ku_ref[...]
-        up_k = dkr_ref[...] * k_gain
-        mean_k = jnp.mean(up_k * k_unit, axis=-1, keepdims=True)
-        dk_ref[:, k_at] = (k_inv * (up_k - k_unit * mean_k)).astype(BF)
-        parts = []
-        for start in range(0, share * rows, width):
-            cols = slice(start, start + width)
-            q_inv = row_ref[0:1, cols]
-            q_unit = qt_ref[:, cols].astype(F32) * q_inv
-            up = dq_in[:, cols] * q_gain
-            mean = jnp.mean(up * q_unit, axis=0, keepdims=True)
-            parts.append((q_inv * (up - q_unit * mean)).astype(BF))
-        d_q = jnp.concatenate(parts, axis=1).T
-        att = at_in[...].T
-        live = lax.broadcasted_iota(jnp.int32, (rows, HD), 0) < live_len
-        for i in range(share):
-            at = pl.ds(pl.multiple_of((base * share + i) * HD, HD), HD)
-            block = att[i * rows : (i + 1) * rows, :].astype(F32)
-            att_ref[:, at] = jnp.where(live, block, 0.0).astype(BF)
-            dq_ref[:, at] = d_q[i * rows : (i + 1) * rows, :]
-
-
-def finish(meta, k, q_gain, k_gain, per_head, q_width):
-    rows, k_width = k.shape
-    flat = [x for group in per_head for x in group]
-    return pl.pallas_call(
-        functools.partial(finish_kernel, len(per_head), q_width // k_width, rows, 2 * HD),
-        out_shape=[
-            jax.ShapeDtypeStruct((rows, q_width), BF),
-            jax.ShapeDtypeStruct((rows, q_width), BF),
-            jax.ShapeDtypeStruct((rows, k_width), BF),
-            jax.ShapeDtypeStruct((rows, k_width), BF),
-        ],
-        in_specs=[SMEM] + [VMEM] * (3 + len(flat)),
-        out_specs=[VMEM] * 4,
+def second_half(s, meta, kept, q_gain, k_gain, results, buffers):
+    total = kept[0].shape[1]
+    rows = kept[3].shape[0]
+    return pl.pallas_call(
+        functools.partial(second_kernel, s, 2 * HD),
+        out_shape=out_shapes(rows, buffers[0].shape[1], buffers[2].shape[1]),
+        in_specs=[SMEM] + [VMEM] * (KEPT + 6) + [HBM] * 4,
+        out_specs=[HBM] * 4,
+        scratch_shapes=out_scratch(rows, total // rows),
+        input_output_aliases={7 + KEPT + i: i for i in range(4)},
         compiler_params=params(16),
-        cost_estimate=pl.CostEstimate(
-            flops=40 * rows * q_width, bytes_accessed=10 * rows * q_width, transcendentals=0
-        ),
-        name="finish_response",
-    )(meta, k, q_gain, k_gain, *flat)
+        cost_estimate=pl.CostEstimate(flops=0, bytes_accessed=2**20, transcendentals=0),
+        name="settle_last_head",
+    )(meta, *kept, q_gain, k_gain, *results, *buffers)
 
 
 def join_kernel(*refs):
@@ -374,9 +454,10 @@
     else:
         order = jnp.arange(kv_heads, dtype=jnp.int32)
     meta = jnp.concatenate([order, live_len[None]])
+    q, g, k, v = [pltpu.with_memory_space_constraint(x, pltpu.HBM) for x in (q, g, k, v)]
     kept = prepare(meta, q, g, k, v, gain_col, gain_row, kv_heads)
     if direct:
-        blocks = cut(order, cache, kv_heads)
+        blocks = cut(order, pltpu.with_memory_space_constraint(cache, pltpu.HBM), kv_heads)
         got = [blocks[0]] + [shift(blocks[s], -s) for s in range(1, n_group)]
         got[1], kept[0][2] = lax.optimization_barrier((got[1], kept[0][2]))
         mine = pick(jnp.reshape((owner - me) % n_group, (1,)).astype(jnp.int32), got)
@@ -385,19 +466,26 @@
         cache = lax.psum(jnp.where(me == owner, cache, jnp.zeros_like(cache)), "group")
         prompts = cut(order, cache, kv_heads)
 
-    acc = jnp.zeros((8, HD), F32)
-    parts, backs, per_head = [], [], []
+    acc = jnp.zeros((2, HD), F32)
+    parts, backs, buffers = [], [], ()
     for s, prompt in enumerate(prompts):
-        if direct and s == n_group - 1:
+        last = s == kv_heads - 1
+        if last and direct:
             prompt, backs[0] = lax.optimization_barrier((prompt, backs[0]))
-        part, out_t, d_q, d_kr, d_vr, acc = one_head(prompt, kept[s], gain_col, acc)
-        per_head.append((kept[s][0], kept[s][2], kept[s][7], out_t, d_q, d_kr, d_vr))
+        if last:
+            part, acc, *results = first_half(prompt, kept[s], gain_col, acc)
+        else:
+            part, acc, buffers = whole_head(
+                s, meta, prompt, kept[s], gain_col, gain_row, acc, buffers, q.shape[1], k.shape[1]
+            )
         parts.append(part)
         if direct and s > 0:
             backs.append(shift(part, -s))
+    buffers = list(second_half(kv_heads - 1, meta, kept[-1], gain_col, gain_row, results, buffers))
 
     mine_flag = (me == owner).astype(jnp.int32)
     if direct:
+        backs[-1], buffers[2] = lax.optimization_barrier((backs[-1], buffers[2]))
         total = join([parts[0]] + backs)
         gains = ordered_sum(order, [acc] + [shift(acc, s) for s in range(1, n_group)])
         total, gains = lax.optimization_barrier((total, gains))
@@ -407,8 +495,8 @@
         total = lax.psum(jnp.concatenate(parts, axis=-1).astype(F32), "group").astype(BF)
         placed = jnp.where(mine_flag > 0, total, jnp.zeros((), BF))
         gains = pair_sum(acc, "group", n_group)
-    gains = pair_sum(gains, "dp", n_dp)[:2]
-    attended, d_query, d_key, d_value = finish(meta, k, gain_col, gain_row, per_head, q.shape[1])
+    gains = pair_sum(gains, "dp", n_dp)
+    attended, d_query, d_key, d_value = buffers
     return (
         attended[None, None],
         d_query[None, None],

time: 83.7 us -> 73.1 us (0.87)
  local copies, waits for them, and re-layouts: 18.4 us -> 1.59 us
  Pallas kernels: 16.4 us -> 21.6 us
  starting transfers between devices: 27.3 us -> 31.3 us
  waiting for transfers between devices: 17.6 us -> 15.6 us
    unnamed x70 -> x4, local copies, waits for them, and re-layouts: 17.5 us -> 1.31 us
    ppermute x15, starting transfers between devices: 24.3 us -> 28.3 us  [shift(): lax.ppermute(x, 'group', [(i, (i + s) % n_group) for i in range(n_group)])]
    ppermute x15, waiting for transfers between devices: 14.3 us -> 10.4 us  [shift(): lax.ppermute(x, 'group', [(i, (i + s) % n_group) for i in range(n_group)])]
    pallas_call x5, Pallas kernels: 9.68 us -> 12.6 us  [the longest x3 9.23 us: whole_head(): pl.pallas_call(functools.partial(whole_kernel, s, 2 * HD), out_shape=[jax...]
    ppermute x3, waiting for transfers between devices: 3.29 us -> 5.16 us  [pair_sum(): lax.ppermute(value, axis, [(i, i ^ step) for i in range(size)])]
    pallas_call x1, Pallas kernels: 3.43 us -> 5.15 us  [prepare(): pl.pallas_call(functools.partial(prepare_kernel, count, share, rows, 2 *...]
    pallas_call x1, Pallas kernels: 0.7 us -> 1.69 us  [cut(): pl.pallas_call(cut_kernel, out_shape=[jax.ShapeDtypeStruct((depth, rows,...]
  transfers between devices with their start and end apart: 18 -> 18, of which waited for: 7 -> 7; matrix products, arithmetic and copies ran while one was open for 2% -> 1% of each run, Pallas kernels for 17% -> 23%
where the time goes in v4:
time: 73.1 us; the launch traced here: 72.9 us
  starting transfers between devices  31.3 us (43%)
  Pallas kernels  21.6 us (30%)
  waiting for transfers between devices  15.6 us (21%)
  between operations  2.17 us (3%)
  local copies, waits for them, and re-layouts  1.59 us (2%)
    ppermute x15, starting transfers between devices, shift(): lax.ppermute(x, 'group', [(i, (i + s) % n_group) for i in range(n_group)])  28.3 us
    ppermute x15, waiting for transfers between devices, shift(): lax.ppermute(x, 'group', [(i, (i + s) % n_group) for i in range(n_group)])  10.4 us
    pallas_call x3, Pallas kernels, whole_head(): pl.pallas_call(functools.partial(whole_kernel, s, 2 * HD), out_shape=[jax...  9.23 us
    ppermute x3, waiting for transfers between devices, pair_sum(): lax.ppermute(value, axis, [(i, i ^ step) for i in range(size)])  5.16 us
    pallas_call x1, Pallas kernels, prepare(): pl.pallas_call(functools.partial(prepare_kernel, count, share, rows, 2 *...  5.15 us
    ppermute x3, starting transfers between devices, pair_sum(): lax.ppermute(value, axis, [(i, i ^ step) for i in range(size)])  3.03 us
    pallas_call x1, Pallas kernels, first_half(): pl.pallas_call(functools.partial(first_kernel, 2 * HD), out_shape=[jax.Sh...  1.7 us
    pallas_call x1, Pallas kernels, cut(): pl.pallas_call(cut_kernel, out_shape=[jax.ShapeDtypeStruct((depth, rows,...  1.69 us
  transfers between devices with their start and end apart: 18, of which 7 were waited for; matrix products, arithmetic and copies ran while one was open for 1% of the time, Pallas kernels for 23%

profile of v4, /device:TPU:0, one launch (start us, length us, event | category | flops | bytes accessed | tf_op | source)
XLA Modules:
  0.0 72.9 jit_solution(17710048912613779929)
XLA Ops:
  0.7 0.1 pad_add_fusion.order
  0.8 1.7 %cut_prompt.1 = (bf16[2,256,128]{2,1,0:T(8,128)(2,1)S(1)}, bf16[2,256,128]{2,1,0:T(8,128)(2,1)S(1)}, bf16[2,256,128]{2,1,0:T(8,128)(2,1)S(1)}, bf16[2,256,128]{2,1,0:T(8,128)(2,1)S(1)}) custom-call(s32[4]{0:T(128)S(1)} %pad_add_fusion.order, bf16[2,256,512]{2,1,0:T(8,128)(2,1)} %bitcast.34), custom_call_target="tpu_custom_call" | custom-call | tf_op jit(solution)/shard_map/cut_prompt/pallas_call | solution.py:48
  2.5 5.1 %collective-permute-start = (bf16[2,256,128]{2,1,0:T(8,128)(2,1)S(1)}, bf16[2,256,128]{2,1,0:T(8,128)(2,1)S(1)}, u32[]{:S(2)}, u32[]{:S(2)}) collective-permute-start(bf16[2,256,128]{2,1,0:T(8,128)(2,1)S(1)} %get-tuple-element.87), channel_id=1, source_target_pairs={{0,3},{1,0},{2,1},{3,2},{4,7},{5,4},{6,5},{7,6},{8,11},{9,8},{10,9... | collective-permute-start | bytes 393224 | tf_op jit(solution)/shard_map/ppermute | solution.py:448
  7.6 0.0 collective-permute-start.1
  7.6 1.0 %collective-permute-start.2 = (bf16[2,256,128]{2,1,0:T(8,128)(2,1)S(1)}, bf16[2,256,128]{2,1,0:T(8,128)(2,1)S(1)}, u32[]{:S(2)}, u32[]{:S(2)}) collective-permute-start(bf16[2,256,128]{2,1,0:T(8,128)(2,1)S(1)} %get-tuple-element.91), channel_id=1, source_target_pairs={{0,1},{1,2},{2,3},{3,0},{4,5},{5,6},{6,7},{7,4},{8,9},{9,10},{10,1... | collective-permute-start | bytes 393224 | tf_op jit(solution)/shard_map/ppermute | solution.py:448
  9.9 0.1 concatenate.8.meta
  10.0 0.0 copy-start.1
  10.0 0.7 copy-done.1
  10.6 0.1 copy.27.gain_ref.rest_8_
  10.8 0.0 copy-start
  10.8 0.6 copy-done
  11.4 5.1 %prepare_response.1 = (bf16[128,768]{1,0:T(8,128)(2,1)S(1)}, bf16[128,768]{1,0:T(8,128)(2,1)S(1)}, f32[8,768]{1,0:T(8,128)S(1)}, bf16[192,768]{1,0:T(8,128)(2,1)...) custom-call(s32[5]{0:T(128)S(1)} %concatenate.8.meta, ...), custom_call_target="tpu_custom_call" | custom-call | flops 452984832 | bytes 3932160 | tf_op jit(solution)/shard_map/prepare_response/pallas_call | solution.py:146
  16.6 0.0 collective-permute-done.refs_1_
  16.6 2.2 %collective-permute-done.1.refs_2_ = bf16[2,256,128]{2,1,0:T(8,128)(2,1)S(1)} collective-permute-done((bf16[2,256,128]{2,1,0:T(8,128)(2,1)S(1)}, bf16[2,256,128]{2,1,0:T(8,128)(2,1)S(1)}, u32[]{:S(2)}, u32[]{:S(2)}) %collective-permute-start.1) | collective-permute-done | bytes 131104 | tf_op jit(solution)/shard_map/ppermute | solution.py:448
  18.8 0.0 collective-permute-done.2.refs_3_
  18.8 0.1 pick_owner.1.pr_ref
  18.8 0.8 %collective-permute-start.4 = (bf16[2,256,128]{2,1,0:T(8,128)(2,1)S(1)}, bf16[2,256,128]{2,1,0:T(8,128)(2,1)S(1)}, u32[]{:S(2)}, u32[]{:S(2)}) collective-permute-start(bf16[2,256,128]{2,1,0:T(8,128)(2,1)S(1)} %pick_owner.1.pr_ref), channel_id=1, source_target_pairs={{0,1},{1,2},{2,3},{3,0},{4,5},{5,6},{6,7},{7,4},{8,9},{9,10},{10,1... | collective-permute-start | bytes 393224 | tf_op jit(solution)/shard_map/ppermute | solution.py:448
  19.6 2.0 %collective-permute-start.6 = (bf16[2,256,128]{2,1,0:T(8,128)(2,1)S(1)}, bf16[2,256,128]{2,1,0:T(8,128)(2,1)S(1)}, u32[]{:S(2)}, u32[]{:S(2)}) collective-permute-start(bf16[2,256,128]{2,1,0:T(8,128)(2,1)S(1)} %pick_owner.1.pr_ref), channel_id=1, source_target_pairs={{0,2},{1,3},{2,0},{3,1},{4,6},{5,7},{6,4},{7,5},{8,10},{9,11},{10,... | collective-permute-start | bytes 393224 | tf_op jit(solution)/shard_map/ppermute | solution.py:448
  21.6 2.8 %collective-permute-start.3 = (bf16[2,256,128]{2,1,0:T(8,128)(2,1)S(1)}, bf16[2,256,128]{2,1,0:T(8,128)(2,1)S(1)}, u32[]{:S(2)}, u32[]{:S(2)}) collective-permute-start(bf16[2,256,128]{2,1,0:T(8,128)(2,1)S(1)} %pick_owner.1.pr_ref), channel_id=1, source_target_pairs={{0,3},{1,0},{2,1},{3,2},{4,7},{5,4},{6,5},{7,6},{8,11},{9,8},{10,9... | collective-permute-start | bytes 393224 | tf_op jit(solution)/shard_map/ppermute | solution.py:448
  24.4 3.1 %attend_head.3 = (bf16[2,256,128]{2,1,0:T(8,128)(2,1)S(1)}, f32[2,128]{1,0:T(2,128)S(1)}, bf16[192,2048]{1,0:T(8,128)(2,1)}, bf16[192,2048]{1,0:T(8,128)(2,1)}, ...) custom-call(s32[5]{0:T(128)S(1)} %concatenate.8.meta, bf16[2,256,128]{2,1,0:T(8,128)(2,1)S(1)} %pick_owner.1.pr_ref, ...), custom_call_target="tpu_custom_call" | custom-call | flops 276824064 | bytes 1048576 | tf_op jit(solution)/shard_map/attend_head/pallas_call | solution.py:309
  27.5 0.0 collective-permute-done.4.pr_ref
  27.5 3.1 %attend_head.4 = (bf16[2,256,128]{2,1,0:T(8,128)(2,1)S(1)}, f32[2,128]{1,0:T(2,128)S(1)}, bf16[192,2048]{1,0:T(8,128)(2,1)}, bf16[192,2048]{1,0:T(8,128)(2,1)}, ...) custom-call(s32[5]{0:T(128)S(1)} %concatenate.8.meta, ...), custom_call_target="tpu_custom_call", output_to_operand_aliasing={{2}: (13, {}), {3}: (14, {}), {4}: (15, {}), {5}: (16, {})} | custom-call | flops 276824064 | bytes 1048576 | tf_op jit(solution)/shard_map/attend_head/pallas_call | solution.py:309
  30.6 0.1 collective-permute-start.5
  30.7 0.5 collective-permute-done.6.pr_ref
  31.2 3.1 %attend_head.5 = (bf16[2,256,128]{2,1,0:T(8,128)(2,1)S(1)}, f32[2,128]{1,0:T(2,128)S(1)}, bf16[192,2048]{1,0:T(8,128)(2,1)}, bf16[192,2048]{1,0:T(8,128)(2,1)}, ...) custom-call(s32[5]{0:T(128)S(1)} %concatenate.8.meta, ...), custom_call_target="tpu_custom_call", output_to_operand_aliasing={{2}: (13, {}), {3}: (14, {}), {4}: (15, {}), {5}: (16, {})} | custom-call | flops 276824064 | bytes 1048576 | tf_op jit(solution)/shard_map/attend_head/pallas_call | solution.py:309
  34.3 0.0 collective-permute-done.3.pr_ref
  34.3 4.5 %collective-permute-done.5.refs_1_ = bf16[2,256,128]{2,1,0:T(8,128)(2,1)S(1)} collective-permute-done((bf16[2,256,128]{2,1,0:T(8,128)(2,1)S(1)}, bf16[2,256,128]{2,1,0:T(8,128)(2,1)S(1)}, u32[]{:S(2)}, u32[]{:S(2)}) %collective-permute-start.5) | collective-permute-done | bytes 131104 | tf_op jit(solution)/shard_map/ppermute | solution.py:448
  38.8 1.7 %attend_last_head.1 = (bf16[2,256,128]{2,1,0:T(8,128)(2,1)S(1)}, f32[2,128]{1,0:T(2,128)S(1)}, bf16[128,768]{1,0:T(8,128)(2,1)S(1)}, f32[128,768]{1,0:T(8,128)S(...) custom-call(bf16[2,256,128]{2,1,0:T(8,128)(2,1)S(1)} %collective-permute-done.3.pr_ref, ...), custom_call_target="tpu_custom_call" | custom-call | flops 276824064 | bytes 1048576 | tf_op jit(solution)/shard_map/attend_last_head/pallas_call | solution.py:331
  40.5 2.5 %collective-permute-start.7 = (bf16[2,256,128]{2,1,0:T(8,128)(2,1)S(1)}, bf16[2,256,128]{2,1,0:T(8,128)(2,1)S(1)}, u32[]{:S(2)}, u32[]{:S(2)}) collective-permute-start(bf16[2,256,128]{2,1,0:T(8,128)(2,1)S(1)} %get-tuple-element.139), channel_id=1, source_target_pairs={{0,1},{1,2},{2,3},{3,0},{4,5},{5,6},{6,7},{7,4},{8,9},{9,10},{10,1... | collective-permute-start | bytes 393224 | tf_op jit(solution)/shard_map/ppermute | solution.py:448
  43.0 2.7 %collective-permute-start.8 = (bf16[2,256,128]{2,1,0:T(8,128)(2,1)S(1)}, bf16[2,256,128]{2,1,0:T(8,128)(2,1)S(1)}, u32[]{:S(2)}, u32[]{:S(2)}) collective-permute-start(bf16[2,256,128]{2,1,0:T(8,128)(2,1)S(1)} %get-tuple-element.145), channel_id=1, source_target_pairs={{0,2},{1,3},{2,0},{3,1},{4,6},{5,7},{6,4},{7,5},{8,10},{9,11},{10,... | collective-permute-start | bytes 393224 | tf_op jit(solution)/shard_map/ppermute | solution.py:448
  45.7 0.3 collective-permute-start.10
  45.9 2.6 %collective-permute-start.11 = (f32[2,128]{1,0:T(2,128)S(1)}, f32[2,128]{1,0:T(2,128)S(1)}, u32[]{:S(2)}, u32[]{:S(2)}) collective-permute-start(f32[2,128]{1,0:T(2,128)S(1)} %get-tuple-element.147.refs_0_), channel_id=1, source_target_pairs={{0,3},{1,0},{2,1},{3,2},{4,7},{5,4},{6,5},{7,6},{8,11},{9,8},{10,9... | collective-permute-start | bytes 3080 | tf_op jit(solution)/shard_map/ppermute | solution.py:448
  48.5 0.5 collective-permute-start.9
  49.1 1.6 %settle_last_head.1 = (bf16[192,2048]{1,0:T(8,128)(2,1)}, bf16[192,2048]{1,0:T(8,128)(2,1)}, bf16[192,512]{1,0:T(8,128)(2,1)}, bf16[192,512]{1,0:T(8,128)(2,1)}) custom-call(s32[5]{0:T(128)S(1)} %concatenate.8.meta, bf16[128,768]{1,0:T(8,128)(2,1)S(1)} %get-tuple-element.78.rest_0_, ...), custom_call_target="tpu_custom_call", output_to_operand_aliasing={{0}: (15, {}), {1}: (16, {}), {2}: (17, {}), {3}: (18, {})} | custom-call | bytes 1048576 | tf_op jit(solution)/shard_map/settle_last_head/pallas_call | solution.py:352
  50.7 0.0 collective-permute-done.10.refs_2_
  50.7 0.0 collective-permute-done.11.refs_3_
  50.7 3.2 %collective-permute-done.9.refs_1_ = f32[2,128]{1,0:T(2,128)S(1)} collective-permute-done((f32[2,128]{1,0:T(2,128)S(1)}, f32[2,128]{1,0:T(2,128)S(1)}, u32[]{:S(2)}, u32[]{:S(2)}) %collective-permute-start.9) | collective-permute-done | bytes 1056 | tf_op jit(solution)/shard_map/ppermute | solution.py:448
  54.0 0.6 sum_gains.1
  54.5 0.0 collective-permute-done.7.refs_3_
  54.5 0.0 collective-permute-done.8.refs_2_
  54.6 0.1 join_parts.1.refs_0_
  54.6 3.1 %collective-permute-start.12 = (bf16[2,256,128]{2,1,0:T(8,128)(2,1)S(1)}, bf16[2,256,128]{2,1,0:T(8,128)(2,1)S(1)}, u32[]{:S(2)}, u32[]{:S(2)}) collective-permute-start(bf16[2,256,128]{2,1,0:T(8,128)(2,1)S(1)} %join_parts.1.refs_0_), channel_id=1, source_target_pairs={{0,1},{1,2},{2,3},{3,0},{4,5},{5,6},{6,7},{7,4},{8,9},{9,10},{10,1... | collective-permute-start | bytes 393224 | tf_op jit(solution)/shard_map/ppermute | solution.py:448
  57.7 3.4 %collective-permute-start.13 = (bf16[2,256,128]{2,1,0:T(8,128)(2,1)S(1)}, bf16[2,256,128]{2,1,0:T(8,128)(2,1)S(1)}, u32[]{:S(2)}, u32[]{:S(2)}) collective-permute-start(bf16[2,256,128]{2,1,0:T(8,128)(2,1)S(1)} %join_parts.1.refs_0_), channel_id=1, source_target_pairs={{0,2},{1,3},{2,0},{3,1},{4,6},{5,7},{6,4},{7,5},{8,10},{9,11},{10,... | collective-permute-start | bytes 393224 | tf_op jit(solution)/shard_map/ppermute | solution.py:448
  61.1 1.4 %collective-permute-start.14 = (bf16[2,256,128]{2,1,0:T(8,128)(2,1)S(1)}, bf16[2,256,128]{2,1,0:T(8,128)(2,1)S(1)}, u32[]{:S(2)}, u32[]{:S(2)}) collective-permute-start(bf16[2,256,128]{2,1,0:T(8,128)(2,1)S(1)} %join_parts.1.refs_0_), channel_id=1, source_target_pairs={{0,3},{1,0},{2,1},{3,2},{4,7},{5,4},{6,5},{7,6},{8,11},{9,8},{10,9... | collective-permute-start | bytes 393224 | tf_op jit(solution)/shard_map/ppermute | solution.py:448
  62.6 0.0 collective-permute-start.15
  62.6 1.1 %collective-permute-done.15 = f32[2,128]{1,0:T(2,128)S(1)} collective-permute-done((f32[2,128]{1,0:T(2,128)S(1)}, f32[2,128]{1,0:T(2,128)S(1)}, u32[]{:S(2)}, u32[]{:S(2)}) %collective-permute-start.15) | collective-permute-done | bytes 1056 | tf_op jit(solution)/shard_map/ppermute | solution.py:429
  63.7 1.5 %collective-permute-start.16 = (f32[2,128]{1,0:T(2,128)S(1)}, f32[2,128]{1,0:T(2,128)S(1)}, u32[]{:S(2)}, u32[]{:S(2)}) collective-permute-start(f32[2,128]{1,0:T(2,128)S(1)} %add.33), channel_id=1, source_target_pairs={{0,8},{4,12},{8,0},{12,4},{16,24},{20,28},{24,16},{28,20},{1,9},{5... | collective-permute-start | bytes 3080 | tf_op jit(solution)/shard_map/ppermute | solution.py:429
  65.2 2.1 %collective-permute-done.16 = f32[2,128]{1,0:T(2,128)S(1)} collective-permute-done((f32[2,128]{1,0:T(2,128)S(1)}, f32[2,128]{1,0:T(2,128)S(1)}, u32[]{:S(2)}, u32[]{:S(2)}) %collective-permute-start.16) | collective-permute-done | bytes 1056 | tf_op jit(solution)/shard_map/ppermute | solution.py:429
  67.3 1.5 %collective-permute-start.17 = (f32[2,128]{1,0:T(2,128)S(1)}, f32[2,128]{1,0:T(2,128)S(1)}, u32[]{:S(2)}, u32[]{:S(2)}) collective-permute-start(f32[2,128]{1,0:T(2,128)S(1)} %add.34), channel_id=1, source_target_pairs={{0,16},{4,20},{8,24},{12,28},{16,0},{20,4},{24,8},{28,12},{1,17},{... | collective-permute-start | bytes 3080 | tf_op jit(solution)/shard_map/ppermute | solution.py:429
  68.8 0.1 concatenate.9.meta
  68.9 2.0 %collective-permute-done.17 = f32[2,128]{1,0:T(2,128)S(1)} collective-permute-done((f32[2,128]{1,0:T(2,128)S(1)}, f32[2,128]{1,0:T(2,128)S(1)}, u32[]{:S(2)}, u32[]{:S(2)}) %collective-permute-start.17) | collective-permute-done | bytes 1056 | tf_op jit(solution)/shard_map/ppermute | solution.py:429
  70.8 0.6 add.35
  71.4 0.0 collective-permute-done.12.refs_1_
  71.4 0.0 collective-permute-done.13.refs_2_
  71.4 0.0 collective-permute-done.14.refs_3_
  71.4 1.4 %place_prompt_grad.1 = bf16[2,256,512]{2,1,0:T(8,128)(2,1)} custom-call(s32[5]{0:T(128)S(1)} %concatenate.9.meta, bf16[2,256,128]{2,1,0:T(8,128)(2,1)S(1)} %join_parts.1.refs_0_, bf16[2,256,128]{2,1,0:T(8,128)(2,1)S(1)} %collective-permute-done.12.refs_1_, bf16[2,256,128]{2,1,0:T(8,128)(2,1)S(1)} %collective-permute-done.13.refs_2_, ...), custom_call_target="tpu_custom_call" | custom-call | tf_op jit(solution)/shard_map/place_prompt_grad/pallas_call | solution.py:416
  (3 shorter events, 0.0 us)
Async XLA Ops:
  2.5 14.1 %collective-permute-start = (bf16[2,256,128]{2,1,0:T(8,128)(2,1)S(1)}, bf16[2,256,128]{2,1,0:T(8,128)(2,1)S(1)}, u32[]{:S(2)}, u32[]{:S(2)}) collective-permute-start(bf16[2,256,128]{2,1,0:T(8,128)(2,1)S(1)} %get-tuple-element.87), channel_id=1, source_target_pairs={{0,3},{1,0},{2,1},{3,2},{4,7},{5,4},{6,5},{7,6},{8,11},{9,8},{10,9... | collective-permute-start | bytes 393224 | tf_op jit(solution)/shard_map/ppermute | solution.py:448
  7.6 11.2 %collective-permute-start.1 = (bf16[2,256,128]{2,1,0:T(8,128)(2,1)S(1)}, bf16[2,256,128]{2,1,0:T(8,128)(2,1)S(1)}, u32[]{:S(2)}, u32[]{:S(2)}) collective-permute-start(bf16[2,256,128]{2,1,0:T(8,128)(2,1)S(1)} %get-tuple-element.90), channel_id=1, source_target_pairs={{0,2},{1,3},{2,0},{3,1},{4,6},{5,7},{6,4},{7,5},{8,10},{9,11},{10,... | collective-permute-start | bytes 393224 | tf_op jit(solution)/shard_map/ppermute | solution.py:448
  7.6 11.2 %collective-permute-start.2 = (bf16[2,256,128]{2,1,0:T(8,128)(2,1)S(1)}, bf16[2,256,128]{2,1,0:T(8,128)(2,1)S(1)}, u32[]{:S(2)}, u32[]{:S(2)}) collective-permute-start(bf16[2,256,128]{2,1,0:T(8,128)(2,1)S(1)} %get-tuple-element.91), channel_id=1, source_target_pairs={{0,1},{1,2},{2,3},{3,0},{4,5},{5,6},{6,7},{7,4},{8,9},{9,10},{10,1... | collective-permute-start | bytes 393224 | tf_op jit(solution)/shard_map/ppermute | solution.py:448
  10.0 0.7 copy-start.1
  10.8 0.7 copy-start
  18.8 8.7 %collective-permute-start.4 = (bf16[2,256,128]{2,1,0:T(8,128)(2,1)S(1)}, bf16[2,256,128]{2,1,0:T(8,128)(2,1)S(1)}, u32[]{:S(2)}, u32[]{:S(2)}) collective-permute-start(bf16[2,256,128]{2,1,0:T(8,128)(2,1)S(1)} %pick_owner.1.pr_ref), channel_id=1, source_target_pairs={{0,1},{1,2},{2,3},{3,0},{4,5},{5,6},{6,7},{7,4},{8,9},{9,10},{10,1... | collective-permute-start | bytes 393224 | tf_op jit(solution)/shard_map/ppermute | solution.py:448
  19.6 11.6 %collective-permute-start.6 = (bf16[2,256,128]{2,1,0:T(8,128)(2,1)S(1)}, bf16[2,256,128]{2,1,0:T(8,128)(2,1)S(1)}, u32[]{:S(2)}, u32[]{:S(2)}) collective-permute-start(bf16[2,256,128]{2,1,0:T(8,128)(2,1)S(1)} %pick_owner.1.pr_ref), channel_id=1, source_target_pairs={{0,2},{1,3},{2,0},{3,1},{4,6},{5,7},{6,4},{7,5},{8,10},{9,11},{10,... | collective-permute-start | bytes 393224 | tf_op jit(solution)/shard_map/ppermute | solution.py:448
  21.6 12.7 %collective-permute-start.3 = (bf16[2,256,128]{2,1,0:T(8,128)(2,1)S(1)}, bf16[2,256,128]{2,1,0:T(8,128)(2,1)S(1)}, u32[]{:S(2)}, u32[]{:S(2)}) collective-permute-start(bf16[2,256,128]{2,1,0:T(8,128)(2,1)S(1)} %pick_owner.1.pr_ref), channel_id=1, source_target_pairs={{0,3},{1,0},{2,1},{3,2},{4,7},{5,4},{6,5},{7,6},{8,11},{9,8},{10,9... | collective-permute-start | bytes 393224 | tf_op jit(solution)/shard_map/ppermute | solution.py:448
  30.6 8.1 %collective-permute-start.5 = (bf16[2,256,128]{2,1,0:T(8,128)(2,1)S(1)}, bf16[2,256,128]{2,1,0:T(8,128)(2,1)S(1)}, u32[]{:S(2)}, u32[]{:S(2)}) collective-permute-start(bf16[2,256,128]{2,1,0:T(8,128)(2,1)S(1)} %get-tuple-element.113), channel_id=1, source_target_pairs={{0,3},{1,0},{2,1},{3,2},{4,7},{5,4},{6,5},{7,6},{8,11},{9,8},{10,9... | collective-permute-start | bytes 393224 | tf_op jit(solution)/shard_map/ppermute | solution.py:448
  40.5 14.0 %collective-permute-start.7 = (bf16[2,256,128]{2,1,0:T(8,128)(2,1)S(1)}, bf16[2,256,128]{2,1,0:T(8,128)(2,1)S(1)}, u32[]{:S(2)}, u32[]{:S(2)}) collective-permute-start(bf16[2,256,128]{2,1,0:T(8,128)(2,1)S(1)} %get-tuple-element.139), channel_id=1, source_target_pairs={{0,1},{1,2},{2,3},{3,0},{4,5},{5,6},{6,7},{7,4},{8,9},{9,10},{10,1... | collective-permute-start | bytes 393224 | tf_op jit(solution)/shard_map/ppermute | solution.py:448
  43.0 11.6 %collective-permute-start.8 = (bf16[2,256,128]{2,1,0:T(8,128)(2,1)S(1)}, bf16[2,256,128]{2,1,0:T(8,128)(2,1)S(1)}, u32[]{:S(2)}, u32[]{:S(2)}) collective-permute-start(bf16[2,256,128]{2,1,0:T(8,128)(2,1)S(1)} %get-tuple-element.145), channel_id=1, source_target_pairs={{0,2},{1,3},{2,0},{3,1},{4,6},{5,7},{6,4},{7,5},{8,10},{9,11},{10,... | collective-permute-start | bytes 393224 | tf_op jit(solution)/shard_map/ppermute | solution.py:448
  45.7 5.1 %collective-permute-start.10 = (f32[2,128]{1,0:T(2,128)S(1)}, f32[2,128]{1,0:T(2,128)S(1)}, u32[]{:S(2)}, u32[]{:S(2)}) collective-permute-start(f32[2,128]{1,0:T(2,128)S(1)} %get-tuple-element.147.refs_0_), channel_id=1, source_target_pairs={{0,2},{1,3},{2,0},{3,1},{4,6},{5,7},{6,4},{7,5},{8,10},{9,11},{10,... | collective-permute-start | bytes 3080 | tf_op jit(solution)/shard_map/ppermute | solution.py:448
  45.9 4.8 %collective-permute-start.11 = (f32[2,128]{1,0:T(2,128)S(1)}, f32[2,128]{1,0:T(2,128)S(1)}, u32[]{:S(2)}, u32[]{:S(2)}) collective-permute-start(f32[2,128]{1,0:T(2,128)S(1)} %get-tuple-element.147.refs_0_), channel_id=1, source_target_pairs={{0,3},{1,0},{2,1},{3,2},{4,7},{5,4},{6,5},{7,6},{8,11},{9,8},{10,9... | collective-permute-start | bytes 3080 | tf_op jit(solution)/shard_map/ppermute | solution.py:448
  48.5 5.4 %collective-permute-start.9 = (f32[2,128]{1,0:T(2,128)S(1)}, f32[2,128]{1,0:T(2,128)S(1)}, u32[]{:S(2)}, u32[]{:S(2)}) collective-permute-start(f32[2,128]{1,0:T(2,128)S(1)} %get-tuple-element.147.refs_0_), channel_id=1, source_target_pairs={{0,1},{1,2},{2,3},{3,0},{4,5},{5,6},{6,7},{7,4},{8,9},{9,10},{10,1... | collective-permute-start | bytes 3080 | tf_op jit(solution)/shard_map/ppermute | solution.py:448
  54.6 16.8 %collective-permute-start.12 = (bf16[2,256,128]{2,1,0:T(8,128)(2,1)S(1)}, bf16[2,256,128]{2,1,0:T(8,128)(2,1)S(1)}, u32[]{:S(2)}, u32[]{:S(2)}) collective-permute-start(bf16[2,256,128]{2,1,0:T(8,128)(2,1)S(1)} %join_parts.1.refs_0_), channel_id=1, source_target_pairs={{0,1},{1,2},{2,3},{3,0},{4,5},{5,6},{6,7},{7,4},{8,9},{9,10},{10,1... | collective-permute-start | bytes 393224 | tf_op jit(solution)/shard_map/ppermute | solution.py:448
  57.7 13.7 %collective-permute-start.13 = (bf16[2,256,128]{2,1,0:T(8,128)(2,1)S(1)}, bf16[2,256,128]{2,1,0:T(8,128)(2,1)S(1)}, u32[]{:S(2)}, u32[]{:S(2)}) collective-permute-start(bf16[2,256,128]{2,1,0:T(8,128)(2,1)S(1)} %join_parts.1.refs_0_), channel_id=1, source_target_pairs={{0,2},{1,3},{2,0},{3,1},{4,6},{5,7},{6,4},{7,5},{8,10},{9,11},{10,... | collective-permute-start | bytes 393224 | tf_op jit(solution)/shard_map/ppermute | solution.py:448
  61.1 10.3 %collective-permute-start.14 = (bf16[2,256,128]{2,1,0:T(8,128)(2,1)S(1)}, bf16[2,256,128]{2,1,0:T(8,128)(2,1)S(1)}, u32[]{:S(2)}, u32[]{:S(2)}) collective-permute-start(bf16[2,256,128]{2,1,0:T(8,128)(2,1)S(1)} %join_parts.1.refs_0_), channel_id=1, source_target_pairs={{0,3},{1,0},{2,1},{3,2},{4,7},{5,4},{6,5},{7,6},{8,11},{9,8},{10,9... | collective-permute-start | bytes 393224 | tf_op jit(solution)/shard_map/ppermute | solution.py:448
  62.6 1.1 %collective-permute-start.15 = (f32[2,128]{1,0:T(2,128)S(1)}, f32[2,128]{1,0:T(2,128)S(1)}, u32[]{:S(2)}, u32[]{:S(2)}) collective-permute-start(f32[2,128]{1,0:T(2,128)S(1)} %sum_gains.1), channel_id=1, source_target_pairs={{0,4},{4,0},{8,12},{12,8},{16,20},{20,16},{24,28},{28,24},{1,5},{5... | collective-permute-start | bytes 3080 | tf_op jit(solution)/shard_map/ppermute | solution.py:429
  63.7 3.6 %collective-permute-start.16 = (f32[2,128]{1,0:T(2,128)S(1)}, f32[2,128]{1,0:T(2,128)S(1)}, u32[]{:S(2)}, u32[]{:S(2)}) collective-permute-start(f32[2,128]{1,0:T(2,128)S(1)} %add.33), channel_id=1, source_target_pairs={{0,8},{4,12},{8,0},{12,4},{16,24},{20,28},{24,16},{28,20},{1,9},{5... | collective-permute-start | bytes 3080 | tf_op jit(solution)/shard_map/ppermute | solution.py:429
  67.3 3.6 %collective-permute-start.17 = (f32[2,128]{1,0:T(2,128)S(1)}, f32[2,128]{1,0:T(2,128)S(1)}, u32[]{:S(2)}, u32[]{:S(2)}) collective-permute-start(f32[2,128]{1,0:T(2,128)S(1)} %add.34), channel_id=1, source_target_pairs={{0,16},{4,20},{8,24},{12,28},{16,0},{20,4},{24,8},{28,12},{1,17},{... | collective-permute-start | bytes 3080 | tf_op jit(solution)/shard_map/ppermute | solution.py:429

commit v5 on v1

v5 whole, which is shorter than its diff:
```python
import functools

import jax
import jax.numpy as jnp
from jax import lax
from jax.experimental import pallas as pl
from jax.experimental.pallas import tpu as pltpu
from jax.sharding import PartitionSpec as P

HD = 128
EPS = 1e-06
LOG2E = 1.4426950408889634
BF = jnp.bfloat16
F32 = jnp.float32


def dot_nn(a, b):
    return lax.dot_general(a, b, (((1,), (0,)), ((), ())), preferred_element_type=F32)


def dot_nt(a, b):
    return lax.dot_general(a, b, (((1,), (1,)), ((), ())), preferred_element_type=F32)


VMEM = pl.BlockSpec(memory_space=pltpu.VMEM)
SMEM = pl.BlockSpec(memory_space=pltpu.SMEM)
HBM = pl.BlockSpec(memory_space=pltpu.HBM)


SHORT = pl.CostEstimate(flops=0, bytes_accessed=0, transcendentals=0)


def params(mib):
    return pltpu.CompilerParams(vmem_limit_bytes=mib * 2**20)


def cut_kernel(cache_ref, *rest):
    outs, sems = rest[:-1], rest[-1]
    copies = []
    for i, out in enumerate(outs):
        copy = pltpu.make_async_copy(cache_ref.at[:, :, i * HD : (i + 1) * HD], out, sems.at[i])
        copy.start()
        copies.append(copy)
    for copy in copies:
        copy.wait()


def cut(cache, count):
    depth, rows, _ = cache.shape
    return pl.pallas_call(
        cut_kernel,
        out_shape=[jax.ShapeDtypeStruct((depth, rows, HD), BF)] * count,
        in_specs=[HBM],
        out_specs=[VMEM] * count,
        scratch_shapes=[pltpu.SemaphoreType.DMA((count,))],
        compiler_params=params(4),
        cost_estimate=SHORT,
        name="cut_prompt",
    )(cache)


def prepare_kernel(heads, share, rows, width, meta, q_in, g_in, k_in, v_in, gain_ref, kg_ref, *rest):
    outs, (q_buf, g_buf, k_buf, v_buf, sems) = rest[:-5], rest[-5:]
    live_len = meta[0]
    scale = HD ** (-0.5)
    wide = share * HD
    copies = []
    for s, head in enumerate(heads):
        group = []
        for j, (src, buf, size) in enumerate(
            ((q_in, q_buf, wide), (k_in, k_buf, HD), (g_in, g_buf, wide), (v_in, v_buf, HD))
        ):
            src = src.at[:, head * size : (head + 1) * size]
            copy = pltpu.make_async_copy(src, buf.at[s], sems.at[s, j])
            copy.start()
            group.append(copy)
        copies.append(group)
    q_gain = gain_ref[...]
    k_gain = kg_ref[...]
    for s in range(len(heads)):
        low_ref, high_ref, key_ref = outs[s * 3 : (s + 1) * 3]
        for copy in copies[s]:
            copy.wait()
        q_t = jnp.concatenate([q_buf[s, :, i * HD : (i + 1) * HD] for i in range(share)], axis=0).T
        g_t = jnp.concatenate([g_buf[s, :, i * HD : (i + 1) * HD] for i in range(share)], axis=0).T
        low_ref[:HD, :] = q_t
        raw_k = k_buf[s].astype(F32)
        k_inv = lax.rsqrt(jnp.mean(raw_k * raw_k, axis=-1, keepdims=True) + EPS)
        k_unit = raw_k * k_inv
        k_hat = (k_unit * k_gain).astype(BF)
        key_ref[:, :HD] = k_unit
        key_ref[:, HD : 2 * HD] = jnp.broadcast_to(k_inv, (rows, HD))
        key_ref[:, 2 * HD :] = k_hat.astype(F32)
        r_val = v_buf[s]
        r_val_t = r_val.T
        for start in range(0, share * rows, width):
            cols = slice(start, start + width)
            token = (lax.broadcasted_iota(jnp.int32, (1, width), 1) + start) % rows
            raw_q = q_t[:, cols].astype(F32)
            q_inv = lax.rsqrt(jnp.mean(raw_q * raw_q, axis=0, keepdims=True) + EPS)
            q_hat = (raw_q * q_inv * q_gain).astype(BF)
            d_o = jnp.where(token < live_len, g_t[:, cols].astype(F32), 0.0).astype(BF)
            low_ref[HD : 2 * HD, cols] = d_o
            causal = lax.broadcasted_iota(jnp.int32, (rows, width), 0) <= token
            e_r = jnp.where(causal, jnp.exp2(dot_nn(k_hat, q_hat) * (scale * LOG2E)), 0.0)
            eb_r = e_r.astype(BF)
            low_ref[2 * HD :, cols] = eb_r
            high_ref[:HD, cols] = dot_nn(r_val_t, eb_r)
            high_ref[HD : HD + rows, cols] = dot_nn(r_val, d_o)
            high_ref[HD + rows : HD + rows + 1, cols] = q_inv
            high_ref[HD + rows + 1 : HD + rows + 2, cols] = jnp.sum(e_r, axis=0, keepdims=True)


def prepare(heads, meta, q, g, k, v, q_gain, k_gain):
    count = len(heads)
    rows, q_width = q.shape
    share = q_width // k.shape[1]
    total = share * rows
    each = [
        jax.ShapeDtypeStruct((2 * HD + rows, total), BF),
        jax.ShapeDtypeStruct((HD + rows + 8, total), F32),
        jax.ShapeDtypeStruct((rows, 3 * HD), F32),
    ]
    outs = pl.pallas_call(
        functools.partial(prepare_kernel, heads, share, rows, 2 * HD),
        out_shape=each * count,
        in_specs=[SMEM] + [HBM] * 4 + [VMEM] * 2,
        out_specs=[VMEM] * (3 * count),
        scratch_shapes=[
            pltpu.VMEM((count, rows, share * HD), BF),
            pltpu.VMEM((count, rows, share * HD), BF),
            pltpu.VMEM((count, rows, HD), BF),
            pltpu.VMEM((count, rows, HD), BF),
            pltpu.SemaphoreType.DMA((count, 4)),
        ],
        compiler_params=params(16),
        cost_estimate=SHORT,
        name="prepare_response",
    )(meta, q, g, k, v, q_gain, k_gain)
    return [list(outs[s * 3 : (s + 1) * 3]) for s in range(count)]


def head_kernel(
    width, meta, near_ref, far_ref, low_ref, high_ref, key_ref, gain_ref, acc_ref, part_ref, gacc_ref, store_ref
):
    rows = key_ref.shape[0]
    scale = HD ** (-0.5)
    flag = meta[1] > 0
    q_gain = gain_ref[...]
    p_key = jnp.where(flag, far_ref[0], near_ref[0])
    p_val = jnp.where(flag, far_ref[1], near_ref[1])
    k_hat_t = key_ref[:, 2 * HD :].astype(BF).T
    p_key_t = p_key.T
    p_val_t = p_val.T
    sums = None
    for start in range(0, low_ref.shape[1], width):
        cols = slice(start, start + width)
        q_inv = high_ref[HD + rows : HD + rows + 1, cols]
        q_unit = low_ref[:HD, cols].astype(F32) * q_inv
        q_hat = (q_unit * q_gain).astype(BF)
        d_ob = low_ref[HD : 2 * HD, cols]
        d_o = d_ob.astype(F32)
        e_p = jnp.exp2(dot_nn(p_key, q_hat) * (scale * LOG2E))
        row_sum = jnp.sum(e_p, axis=0, keepdims=True) + high_ref[HD + rows + 1 : HD + rows + 2, cols]
        inv_sum = 1.0 / row_sum
        eb_p = e_p.astype(BF)
        eb_r = low_ref[2 * HD :, cols]
        out = (dot_nn(p_val_t, eb_p) + high_ref[:HD, cols]) * inv_sum
        delta = jnp.sum(d_o * out, axis=0, keepdims=True)
        ds_p = (e_p * (dot_nn(p_val, d_ob) - delta)).astype(BF)
        ds_r = (eb_r.astype(F32) * (high_ref[HD : HD + rows, cols] - delta)).astype(BF)
        weight = inv_sum * scale
        q_w = (q_hat.astype(F32) * weight).astype(BF)
        d_ow = (d_o * inv_sum).astype(BF)
        d_qhat = (dot_nn(p_key_t, ds_p) + dot_nn(k_hat_t, ds_r)) * weight
        store_ref[:HD, cols] = d_qhat
        store_ref[HD : 2 * HD, cols] = out
        store_ref[2 * HD : 3 * HD, cols] = q_unit
        store_ref[3 * HD : 3 * HD + 1, cols] = q_inv
        terms = (
            dot_nt(ds_p, q_w),
            dot_nt(eb_p, d_ow),
            dot_nt(ds_r, q_w),
            dot_nt(eb_r, d_ow),
            d_qhat * q_unit,
        )
        sums = terms if sums is None else [a + b for a, b in zip(sums, terms)]
    d_kp, d_vp, d_kr, d_vr, q_term = sums
    part_ref[0] = d_kp.astype(BF)
    part_ref[1] = d_vp.astype(BF)
    base = 3 * HD + 8
    store_ref[base:, :HD] = d_kr
    store_ref[base:, HD : 2 * HD] = d_vr
    store_ref[base:, 2 * HD : 4 * HD] = key_ref[:, : 2 * HD]
    folded = q_term[:, :HD]
    for start in range(HD, width, HD):
        folded = folded + q_term[:, start : start + HD]
    gacc_ref[0:1, :] = acc_ref[0:1, :] + jnp.sum(folded.T, axis=0, keepdims=True)
    gacc_ref[1:2, :] = acc_ref[1:2, :] + jnp.sum(d_kr * key_ref[:, :HD], axis=0, keepdims=True)


def one_head(meta, near, far, kept, q_gain, acc):
    rows = kept[2].shape[0]
    total = kept[0].shape[1]
    return pl.pallas_call(
        functools.partial(head_kernel, 2 * HD),
        out_shape=[
            jax.ShapeDtypeStruct(near.shape, BF),
            jax.ShapeDtypeStruct(acc.shape, F32),
            jax.ShapeDtypeStruct((3 * HD + 8 + rows, total), F32),
        ],
        in_specs=[SMEM] + [VMEM] * 7,
        out_specs=[VMEM] * 3,
        compiler_params=params(16),
        cost_estimate=SHORT,
        name="attend_head",
    )(meta, near, far, *kept, q_gain, acc)


def settle_kernel(heads, rows, width, meta, gain_ref, kg_ref, *rest):
    stores = rest[: len(heads)]
    outs, bufs, sems = rest[-9:-5], rest[-5:-1], rest[-1]
    live_len = meta[0]
    q_gain = gain_ref[...]
    k_gain = kg_ref[...]
    base = 3 * HD + 8
    copies = []
    for s, (head, store_ref) in enumerate(zip(heads, stores)):
        a_buf, q_buf, k_buf, v_buf = [buf.at[s] for buf in bufs]
        total = store_ref.shape[1]
        share = total // rows

        def send(j, buf):
            size = buf.shape[1]
            out = outs[j].at[:, head * size : (head + 1) * size]
            copy = pltpu.make_async_copy(buf, out, sems.at[s, j])
            copy.start()
            copies.append(copy)

        att = store_ref[HD : 2 * HD, :].astype(BF).T
        live = lax.broadcasted_iota(jnp.int32, (rows, HD), 0) < live_len
        for i in range(share):
            block = att[i * rows : (i + 1) * rows, :].astype(F32)
            a_buf[:, i * HD : (i + 1) * HD] = jnp.where(live, block, 0.0).astype(BF)
        send(0, a_buf)
        v_buf[...] = store_ref[base:, HD : 2 * HD].astype(BF)
        send(3, v_buf)
        k_unit = store_ref[base:, 2 * HD : 3 * HD]
        k_inv = store_ref[base:, 3 * HD : 4 * HD]
        up_k = store_ref[base:, :HD] * k_gain
        mean_k = jnp.mean(up_k * k_unit, axis=-1, keepdims=True)
        k_buf[...] = (k_inv * (up_k - k_unit * mean_k)).astype(BF)
        send(2, k_buf)
        parts = []
        for start in range(0, total, width):
            cols = slice(start, start + width)
            q_unit = store_ref[2 * HD : 3 * HD, cols]
            up = store_ref[:HD, cols] * q_gain
            mean = jnp.mean(up * q_unit, axis=0, keepdims=True)
            parts.append((store_ref[3 * HD : 3 * HD + 1, cols] * (up - q_unit * mean)).astype(BF))
        d_q = jnp.concatenate(parts, axis=1).T
        for i in range(share):
            q_buf[:, i * HD : (i + 1) * HD] = d_q[i * rows : (i + 1) * rows, :]
        send(1, q_buf)
    for copy in copies:
        copy.wait()


def settle(heads, meta, q_gain, k_gain, stores, buffers, q_width, k_width):
    total = stores[0].shape[1]
    rows = stores[0].shape[0] - 3 * HD - 8
    count = len(heads)
    wide = total // rows * HD
    return pl.pallas_call(
        functools.partial(settle_kernel, heads, rows, 2 * HD),
        out_shape=[jax.ShapeDtypeStruct((rows, w), BF) for w in (q_width, q_width, k_width, k_width)],
        in_specs=[SMEM] + [VMEM] * (2 + count) + [HBM] * len(buffers),
        out_specs=[HBM] * 4,
        scratch_shapes=[pltpu.VMEM((count, rows, w), BF) for w in (wide, wide, HD, HD)]
        + [pltpu.SemaphoreType.DMA((count, 4))],
        input_output_aliases={3 + count + i: i for i in range(len(buffers))},
        compiler_params=params(16),
        cost_estimate=SHORT,
        name="settle_heads",
    )(meta, q_gain, k_gain, *stores, *buffers)


def join(a, b):
    return (a.astype(F32) + b.astype(F32)).astype(BF)


def place_kernel(meta, *refs):
    ins, out_ref = refs[:-1], refs[-1]
    for i in range(len(ins) // 2):
        near, far = ins[2 * i][...], ins[2 * i + 1][...]
        block = jnp.where(meta[1] > 0, far, near)
        out_ref[:, :, i * HD : (i + 1) * HD] = jnp.where(meta[2] > 0, block, jnp.zeros_like(block))


def place(meta, pairs):
    depth, rows, _ = pairs[0][0].shape
    return pl.pallas_call(
        place_kernel,
        out_shape=jax.ShapeDtypeStruct((depth, rows, HD * len(pairs)), BF),
        in_specs=[SMEM] + [VMEM] * (2 * len(pairs)),
        out_specs=VMEM,
        compiler_params=params(8),
        cost_estimate=SHORT,
        name="place_prompt_grad",
    )(meta, *[x for pair in pairs for x in pair])


def after(x, *others):
    return lax.optimization_barrier((x,) + others)[0]


def pair_sum(value, axis, size):
    step = 1
    while step < size:
        value = value + lax.ppermute(value, axis, [(i, i ^ step) for i in range(size)])
        step *= 2
    return value


def local(
    n_dp, n_group, queries, resp_keys, resp_values, prompt_cache, owners, lengths, q_gain, k_gain, grad_out
):
    q, g = queries[0, 0], grad_out[0, 0]
    k, v = resp_keys[0, 0], resp_values[0, 0]
    cache = prompt_cache[0, 0]
    owner = owners[0]
    live_len = lengths[0, 0]
    me = lax.axis_index("group")
    kv_heads = k.shape[1] // HD
    depth, p_rows, _ = cache.shape
    q, g, k, v = [pltpu.with_memory_space_constraint(x, pltpu.HBM) for x in (q, g, k, v)]
    gain_col = q_gain[:, None]
    gain_row = k_gain[None, :]
    line = n_group == 4
    at_end = (me == 0) | (me == n_group - 1)
    far_flag = (at_end & (me != owner) if line else jnp.zeros((), bool)).astype(jnp.int32)
    meta = jnp.stack([live_len, far_flag])
    half = max(kv_heads // 2, 1)

    def prepared(low, high, order):
        return prepare(tuple(range(low, high)), order, q, g, k, v, gain_col, gain_row)

    kept = prepared(0, half, meta)

    def inward(x):
        return lax.ppermute(x, "group", [(0, 1), (3, 2)])

    def across(x):
        return lax.ppermute(x, "group", [(1, 2), (2, 1)])

    def outward(x):
        return lax.ppermute(x, "group", [(1, 0), (2, 3)])

    acc = jnp.zeros((2, HD), F32)
    mine_flag = (me == owner).astype(jnp.int32)
    heads = range(kv_heads)

    def attend(s, near, far, acc):
        return one_head(meta, near, far, kept[s], gain_col, acc)

    def settled(low, high, stores, buffers):
        return settle(
            tuple(range(low, high)), meta, gain_col, gain_row, stores[low:high], buffers, q.shape[1], k.shape[1]
        )

    if line:
        last = kv_heads - 1
        blocks = cut(pltpu.with_memory_space_constraint(cache, pltpu.HBM), kv_heads)
        from_end = ((me == 1) & (owner == 0)) | ((me == 2) & (owner == 3))
        from_side = ((me == 1) & (owner >= 2)) | ((me == 2) & (owner <= 1))
        sent = [inward(b) for b in blocks]
        sides, nears, mark = [], [], [kept[0][1]]

        def take_side(s, *waits):
            got = after(sent[s], *mark, *waits)
            sides.append(jnp.where(from_end, got, blocks[s]))
            mark[:] = sides[-1:]

        def take_near(s):
            got = after(across(sides[s]), *mark)
            nears.append(jnp.where(from_side, got, sides[s]))
            mark[:] = nears[-1:]

        for s in heads:
            if s == half:
                kept += prepared(half, kv_heads, after(meta, *mark))
            take_side(s, *([kept[half][1]] if s == half else []))
            if s >= 2:
                take_near(s - 2)
        for s in heads[len(nears) :]:
            take_near(s)
        fars = [outward(y) for y in nears]
        fars[0] = after(fars[0], nears[last])
        for s in range(1, last):
            fars[s] = after(fars[s], fars[s + 1])
        parts, stores, firsts = [], [], []
        for s in heads:
            near = nears[s]
            if s >= 2:
                firsts.append(join(parts[s - 2], inward(parts[s - 2])))
                near = after(near, firsts[s - 2])
            part, acc, store = attend(s, near, fars[s], acc)
            parts.append(part)
            stores.append(store)
        totals, lasts = [], []

        def take_total(s, *waits):
            totals.append(join(firsts[s], after(across(firsts[s]), *totals[-1:], *waits)))
            lasts.append(outward(totals[s]))

        for s in heads[len(firsts) :]:
            take_total(s - 2)
            firsts.append(join(parts[s], after(inward(parts[s]), firsts[-1], totals[-1])))
        gains = after(acc, firsts[last - 1])
        gains = gains + lax.ppermute(gains, "group", [(i, i ^ 1) for i in range(n_group)])
        gains = after(gains, firsts[last])
        gains = gains + lax.ppermute(gains, "group", [(i, i ^ 2) for i in range(n_group)])
        half_stores = [after(x, firsts[last]) for x in stores[:half]]
        buffers = settled(0, half, half_stores, ())
        take_total(last - 1, buffers[2])
        take_total(last, gains, *lasts[: last - 1])
        rest_stores = [after(x, totals[last]) for x in stores[half:]]
        buffers = settled(half, kv_heads, stores[:half] + rest_stores, buffers)
        lasts[last] = after(lasts[last], buffers[2])
        placed = place(
            jnp.stack([live_len, at_end.astype(jnp.int32), mine_flag]), list(zip(totals, lasts))
        )
        gains = pair_sum(after(gains, totals[last]), "dp", n_dp)
    else:
        kept += prepared(half, kv_heads, meta)
        cache = lax.psum(jnp.where(me == owner, cache, jnp.zeros_like(cache)), "group")
        prompts = cut(cache, kv_heads)
        parts, stores = [], []
        for s in heads:
            part, acc, store = attend(s, prompts[s], prompts[s], acc)
            parts.append(part)
            stores.append(store)
        buffers = settled(0, kv_heads, stores, ())
        total = lax.psum(jnp.concatenate(parts, axis=-1).astype(F32), "group").astype(BF)
        placed = jnp.where(mine_flag > 0, total, jnp.zeros((), BF))
        gains = pair_sum(pair_sum(acc, "group", n_group), "dp", n_dp)
    attended, d_query, d_key, d_value = buffers
    return (
        attended[None, None],
        d_query[None, None],
        d_key[None, None],
        d_value[None, None],
        placed[None, None],
        gains,
    )


def solution(mesh):
    in_specs = (
        P("dp", "group", None, None),
        P("dp", "group", None, None),
        P("dp", "group", None, None),
        P("dp", "group", None, None, None),
        P("dp"),
        P("dp", "group"),
        P(),
        P(),
        P("dp", "group", None, None),
    )
    out_specs = (
        P("dp", "group", None, None),
        P("dp", "group", None, None),
        P("dp", "group", None, None),
        P("dp", "group", None, None),
        P("dp", "group", None, None, None),
        P(),
    )
    body = functools.partial(local, mesh.shape["dp"], mesh.shape["group"])
    return jax.shard_map(body, mesh=mesh, in_specs=in_specs, out_specs=out_specs, check_vma=False)
```

time: 79.7 us -> 101 us (1.27)
  starting transfers between devices: 29 us -> 51.6 us
  waiting for transfers between devices: 27.1 us -> 18.6 us
  Pallas kernels: 15.2 us -> 22.2 us
    ppermute x12 -> x26, starting transfers between devices: 22.4 us -> 48.5 us  [the longest x8 26.6 us: inward(): return lax.ppermute(x, 'group', [(0, 1), (3, 2)])]
    ppermute x5 -> x3, waiting for transfers between devices: 15 us -> 3.21 us  [pair_sum(): lax.ppermute(value, axis, [(i, i ^ step) for i in range(size)])]
    pallas_call x4 -> x9, Pallas kernels: 13.2 us -> 20.7 us  [the longest x4 9.02 us: one_head(): pl.pallas_call(functools.partial(head_kernel, 2 * HD), out_shape=[jax.Sha...]
    ppermute x5 -> x3, starting transfers between devices: 6.58 us -> 3.08 us  [pair_sum(): lax.ppermute(value, axis, [(i, i ^ step) for i in range(size)])]
    ppermute x12 -> x26, waiting for transfers between devices: 12.1 us -> 15.4 us  [the longest x8 12.2 us: outward(): return lax.ppermute(x, 'group', [(1, 0), (2, 3)])]
    dynamic_slice x1 -> x0, local copies, waits for them, and re-layouts: 1.19 us -> none  [head_of(): return lax.dynamic_slice(array, (0, 0, index * HD), (depth, p_rows, HD))]
    unnamed x20 -> x8, local copies, waits for them, and re-layouts: 2.28 us -> 3.37 us
  transfers between devices with their start and end apart: 17 -> 29, of which waited for: 8 -> 7; matrix products, arithmetic and copies ran while one was open for 2% -> 2% of each run, Pallas kernels for 12% -> 20%
where the time goes in v5:
time: 101 us; the launch traced here: 100 us
  starting transfers between devices  51.6 us (51%)
  Pallas kernels  22.2 us (22%)
  waiting for transfers between devices  18.6 us (18%)
  local copies, waits for them, and re-layouts  4.14 us (4%)
  between operations  2.5 us (2%)
  other arithmetic  1.18 us (1%)
    ppermute x8, starting transfers between devices, inward(): return lax.ppermute(x, 'group', [(0, 1), (3, 2)])  26.6 us
    ppermute x8, waiting for transfers between devices, outward(): return lax.ppermute(x, 'group', [(1, 0), (2, 3)])  12.2 us
    ppermute x8, starting transfers between devices, outward(): return lax.ppermute(x, 'group', [(1, 0), (2, 3)])  10.3 us
    pallas_call x4, Pallas kernels, one_head(): pl.pallas_call(functools.partial(head_kernel, 2 * HD), out_shape=[jax.Sha...  9.02 us
    pallas_call x2, Pallas kernels, prepare(): pl.pallas_call(functools.partial(prepare_kernel, heads, share, rows, 2 *...  6.64 us
    ppermute x8, starting transfers between devices, across(): return lax.ppermute(x, 'group', [(1, 2), (2, 1)])  5.34 us
    ppermute x1, starting transfers between devices, local(): lax.ppermute(gains, 'group', [(i, i ^ 1) for i in range(n_group)])  4.05 us
    pallas_call x2, Pallas kernels, settle(): pl.pallas_call(functools.partial(settle_kernel, heads, rows, 2 * HD), out...  3.89 us
  transfers between devices with their start and end apart: 29, of which 7 were waited for; matrix products, arithmetic and copies ran while one was open for 2% of the time, Pallas kernels for 20%

profile of v5, /device:TPU:0, one launch (start us, length us, event | category | flops | bytes accessed | tf_op | source)
XLA Modules:
  0.0 100.2 jit_solution(11269607994299260263)
XLA Ops:
  0.6 1.1 %cut_prompt.1 = (bf16[2,256,128]{2,1,0:T(8,128)(2,1)S(1)}, bf16[2,256,128]{2,1,0:T(8,128)(2,1)S(1)}, bf16[2,256,128]{2,1,0:T(8,128)(2,1)S(1)}, bf16[2,256,128]{2,1,0:T(8,128)(2,1)S(1)}) custom-call(bf16[2,256,512]{2,1,0:T(8,128)(2,1)} %bitcast.39), custom_call_target="tpu_custom_call" | custom-call | tf_op jit(solution)/shard_map/cut_prompt/pallas_call | solution.py:50
  1.8 4.9 %collective-permute-start.2 = (bf16[2,256,128]{2,1,0:T(8,128)(2,1)S(1)}, bf16[2,256,128]{2,1,0:T(8,128)(2,1)S(1)}, u32[]{:S(2)}, u32[]{:S(2)}) collective-permute-start(bf16[2,256,128]{2,1,0:T(8,128)(2,1)S(1)} %get-tuple-element.71), channel_id=1, source_target_pairs={{0,1},{3,2},{4,5},{7,6},{8,9},{11,10},{12,13},{15,14},{16,17},{19,... | collective-permute-start | bytes 393224 | tf_op jit(solution)/shard_map/ppermute | solution.py:351
  6.7 1.3 %collective-permute-start.1 = (bf16[2,256,128]{2,1,0:T(8,128)(2,1)S(1)}, bf16[2,256,128]{2,1,0:T(8,128)(2,1)S(1)}, u32[]{:S(2)}, u32[]{:S(2)}) collective-permute-start(bf16[2,256,128]{2,1,0:T(8,128)(2,1)S(1)} %get-tuple-element.70), channel_id=1, source_target_pairs={{0,1},{3,2},{4,5},{7,6},{8,9},{11,10},{12,13},{15,14},{16,17},{19,... | collective-permute-start | bytes 393224 | tf_op jit(solution)/shard_map/ppermute | solution.py:351
  8.0 1.3 %collective-permute-start = (bf16[2,256,128]{2,1,0:T(8,128)(2,1)S(1)}, bf16[2,256,128]{2,1,0:T(8,128)(2,1)S(1)}, u32[]{:S(2)}, u32[]{:S(2)}) collective-permute-start(bf16[2,256,128]{2,1,0:T(8,128)(2,1)S(1)} %get-tuple-element.69), channel_id=1, source_target_pairs={{0,1},{3,2},{4,5},{7,6},{8,9},{11,10},{12,13},{15,14},{16,17},{19,... | collective-permute-start | bytes 393224 | tf_op jit(solution)/shard_map/ppermute | solution.py:351
  9.3 1.3 %collective-permute-start.5 = (bf16[2,256,128]{2,1,0:T(8,128)(2,1)S(1)}, bf16[2,256,128]{2,1,0:T(8,128)(2,1)S(1)}, u32[]{:S(2)}, u32[]{:S(2)}) collective-permute-start(bf16[2,256,128]{2,1,0:T(8,128)(2,1)S(1)} %get-tuple-element.78), channel_id=1, source_target_pairs={{0,1},{3,2},{4,5},{7,6},{8,9},{11,10},{12,13},{15,14},{16,17},{19,... | collective-permute-start | bytes 393224 | tf_op jit(solution)/shard_map/ppermute | solution.py:351
  11.9 0.8 copy.26.gain_ref
  12.7 0.1 pad_add_fusion.meta
  12.8 0.7 copy-done.2
  13.5 3.3 %prepare_response.2 = (bf16[448,768]{1,0:T(8,128)(2,1)S(1)}, f32[328,768]{1,0:T(8,128)S(1)}, f32[192,384]{1,0:T(8,128)S(1)}, bf16[448,768]{1,0:T(8,128)(2,1)S(1)...) custom-call(s32[2]{0:T(128)S(1)} %pad_add_fusion.meta, bf16[192,2048]{1,0:T(8,128)(2,1)} %bitcast.29, ...), custom_call_target="tpu_custom_call" | custom-call | tf_op jit(solution)/shard_map/prepare_response/pallas_call | solution.py:124
  16.8 0.7 collective-permute-start.6
  17.5 0.0 collective-permute-done.1
  17.5 0.7 collective-permute-start.4
  18.2 3.3 %prepare_response.3 = (bf16[448,768]{1,0:T(8,128)(2,1)S(1)}, f32[328,768]{1,0:T(8,128)S(1)}, f32[192,384]{1,0:T(8,128)S(1)}, bf16[448,768]{1,0:T(8,128)(2,1)S(1)...) custom-call(s32[2]{0:T(128)S(1)} %pad_add_fusion.meta, bf16[192,2048]{1,0:T(8,128)(2,1)} %bitcast.30, ...), custom_call_target="tpu_custom_call" | custom-call | tf_op jit(solution)/shard_map/prepare_response/pallas_call | solution.py:124
  21.5 0.0 collective-permute-done
  21.6 0.7 collective-permute-start.3
  22.3 1.3 %collective-permute-start.7 = (bf16[2,256,128]{2,1,0:T(8,128)(2,1)S(1)}, bf16[2,256,128]{2,1,0:T(8,128)(2,1)S(1)}, u32[]{:S(2)}, u32[]{:S(2)}) collective-permute-start(bf16[2,256,128]{2,1,0:T(8,128)(2,1)S(1)} %broadcast_select_fusion.7.near_ref), channel_id=1, source_target_pairs={{1,0},{2,3},{5,4},{6,7},{9,8},{10,11},{13,12},{14,15},{17,16},{18,... | collective-permute-start | bytes 393224 | tf_op jit(solution)/shard_map/ppermute | solution.py:357
  23.6 0.7 collective-permute-start.8
  24.3 0.0 collective-permute-done.4
  24.3 1.3 %collective-permute-start.12 = (bf16[2,256,128]{2,1,0:T(8,128)(2,1)S(1)}, bf16[2,256,128]{2,1,0:T(8,128)(2,1)S(1)}, u32[]{:S(2)}, u32[]{:S(2)}) collective-permute-start(bf16[2,256,128]{2,1,0:T(8,128)(2,1)S(1)} %broadcast_select_fusion.6.near_ref), channel_id=1, source_target_pairs={{1,0},{2,3},{5,4},{6,7},{9,8},{10,11},{13,12},{14,15},{17,16},{18,... | collective-permute-start | bytes 393224 | tf_op jit(solution)/shard_map/ppermute | solution.py:357
  25.6 0.0 collective-permute-done.3
  25.7 1.3 %collective-permute-start.10 = (bf16[2,256,128]{2,1,0:T(8,128)(2,1)S(1)}, bf16[2,256,128]{2,1,0:T(8,128)(2,1)S(1)}, u32[]{:S(2)}, u32[]{:S(2)}) collective-permute-start(bf16[2,256,128]{2,1,0:T(8,128)(2,1)S(1)} %broadcast_select_fusion.5.near_ref), channel_id=1, source_target_pairs={{1,0},{2,3},{5,4},{6,7},{9,8},{10,11},{13,12},{14,15},{17,16},{18,... | collective-permute-start | bytes 393224 | tf_op jit(solution)/shard_map/ppermute | solution.py:357
  27.0 0.0 collective-permute-done.8
  27.0 6.2 %collective-permute-done.7.far_ref = bf16[2,256,128]{2,1,0:T(8,128)(2,1)S(1)} collective-permute-done((bf16[2,256,128]{2,1,0:T(8,128)(2,1)S(1)}, bf16[2,256,128]{2,1,0:T(8,128)(2,1)S(1)}, u32[]{:S(2)}, u32[]{:S(2)}) %collective-permute-start.7) | collective-permute-done | bytes 131104 | tf_op jit(solution)/shard_map/ppermute | solution.py:357
  33.2 2.3 %attend_head.4 = (bf16[2,256,128]{2,1,0:T(8,128)(2,1)S(1)}, f32[2,128]{1,0:T(2,128)S(1)}, f32[584,768]{1,0:T(8,128)S(1)}) custom-call(s32[2]{0:T(128)S(1)} %pad_add_fusion.meta, bf16[2,256,128]{2,1,0:T(8,128)(2,1)S(1)} %broadcast_select_fusion.7.near_ref, bf16[2,256,128]{2,1,0:T(8,128)(2,1)S(1)} %collective-permute-done.7.far_ref, ...), custom_call_target="tpu_custom_call" | custom-call | tf_op jit(solution)/shard_map/attend_head/pallas_call | solution.py:205
  35.5 5.9 %collective-permute-start.9 = (bf16[2,256,128]{2,1,0:T(8,128)(2,1)S(1)}, bf16[2,256,128]{2,1,0:T(8,128)(2,1)S(1)}, u32[]{:S(2)}, u32[]{:S(2)}) collective-permute-start(bf16[2,256,128]{2,1,0:T(8,128)(2,1)S(1)} %get-tuple-element.87), channel_id=1, source_target_pairs={{0,1},{3,2},{4,5},{7,6},{8,9},{11,10},{12,13},{15,14},{16,17},{19,... | collective-permute-start | bytes 393224 | tf_op jit(solution)/shard_map/ppermute | solution.py:351
  41.4 1.3 %collective-permute-start.11 = (bf16[2,256,128]{2,1,0:T(8,128)(2,1)S(1)}, bf16[2,256,128]{2,1,0:T(8,128)(2,1)S(1)}, u32[]{:S(2)}, u32[]{:S(2)}) collective-permute-start(bf16[2,256,128]{2,1,0:T(8,128)(2,1)S(1)} %broadcast_select_fusion.4.near_ref), channel_id=1, source_target_pairs={{1,0},{2,3},{5,4},{6,7},{9,8},{10,11},{13,12},{14,15},{17,16},{18,... | collective-permute-start | bytes 393224 | tf_op jit(solution)/shard_map/ppermute | solution.py:357
  42.7 0.0 collective-permute-done.10.far_ref
  42.7 2.3 %attend_head.5 = (bf16[2,256,128]{2,1,0:T(8,128)(2,1)S(1)}, f32[2,128]{1,0:T(2,128)S(1)}, f32[584,768]{1,0:T(8,128)S(1)}) custom-call(s32[2]{0:T(128)S(1)} %pad_add_fusion.meta, bf16[2,256,128]{2,1,0:T(8,128)(2,1)S(1)} %broadcast_select_fusion.6.near_ref, bf16[2,256,128]{2,1,0:T(8,128)(2,1)S(1)} %collective-permute-done.12.far_ref, ...), custom_call_target="tpu_custom_call" | custom-call | tf_op jit(solution)/shard_map/attend_head/pallas_call | solution.py:205
  45.0 4.6 %collective-permute-start.13 = (bf16[2,256,128]{2,1,0:T(8,128)(2,1)S(1)}, bf16[2,256,128]{2,1,0:T(8,128)(2,1)S(1)}, u32[]{:S(2)}, u32[]{:S(2)}) collective-permute-start(bf16[2,256,128]{2,1,0:T(8,128)(2,1)S(1)} %get-tuple-element.99), channel_id=1, source_target_pairs={{0,1},{3,2},{4,5},{7,6},{8,9},{11,10},{12,13},{15,14},{16,17},{19,... | collective-permute-start | bytes 393224 | tf_op jit(solution)/shard_map/ppermute | solution.py:351
  49.6 0.7 collective-permute-start.16
  50.3 1.8 %collective-permute-done.13 = bf16[2,256,128]{2,1,0:T(8,128)(2,1)S(1)} collective-permute-done((bf16[2,256,128]{2,1,0:T(8,128)(2,1)S(1)}, bf16[2,256,128]{2,1,0:T(8,128)(2,1)S(1)}, u32[]{:S(2)}, u32[]{:S(2)}) %collective-permute-start.13) | collective-permute-done | bytes 131104 | tf_op jit(solution)/shard_map/ppermute | solution.py:351
  52.1 0.7 collective-permute-start.17
  52.8 2.2 %attend_head.6 = (bf16[2,256,128]{2,1,0:T(8,128)(2,1)S(1)}, f32[2,128]{1,0:T(2,128)S(1)}, f32[584,768]{1,0:T(8,128)S(1)}) custom-call(s32[2]{0:T(128)S(1)} %pad_add_fusion.meta, bf16[2,256,128]{2,1,0:T(8,128)(2,1)S(1)} %broadcast_select_fusion.5.near_ref, bf16[2,256,128]{2,1,0:T(8,128)(2,1)S(1)} %collective-permute-done.10.far_ref, ...), custom_call_target="tpu_custom_call" | custom-call | tf_op jit(solution)/shard_map/attend_head/pallas_call | solution.py:205
  55.0 6.0 %collective-permute-start.15 = (bf16[2,256,128]{2,1,0:T(8,128)(2,1)S(1)}, bf16[2,256,128]{2,1,0:T(8,128)(2,1)S(1)}, u32[]{:S(2)}, u32[]{:S(2)}) collective-permute-start(bf16[2,256,128]{2,1,0:T(8,128)(2,1)S(1)} %get-tuple-element.106), channel_id=1, source_target_pairs={{0,1},{3,2},{4,5},{7,6},{8,9},{11,10},{12,13},{15,14},{16,17},{19,... | collective-permute-start | bytes 393224 | tf_op jit(solution)/shard_map/ppermute | solution.py:351
  61.1 2.3 %attend_head.7 = (bf16[2,256,128]{2,1,0:T(8,128)(2,1)S(1)}, f32[2,128]{1,0:T(2,128)S(1)}, f32[584,768]{1,0:T(8,128)S(1)}) custom-call(s32[2]{0:T(128)S(1)} %pad_add_fusion.meta, bf16[2,256,128]{2,1,0:T(8,128)(2,1)S(1)} %broadcast_select_fusion.4.near_ref, bf16[2,256,128]{2,1,0:T(8,128)(2,1)S(1)} %collective-permute-done.11.far_ref, ...), custom_call_target="tpu_custom_call" | custom-call | tf_op jit(solution)/shard_map/attend_head/pallas_call | solution.py:205
  63.4 1.2 %copy-done = f32[584,768]{1,0:T(8,128)} copy-done((f32[584,768]{1,0:T(8,128)}, f32[584,768]{1,0:T(8,128)S(1)}, u32[]{:S(2)}) %copy-start) | copy-done | bytes 1794072
  64.6 1.3 %collective-permute-start.14 = (bf16[2,256,128]{2,1,0:T(8,128)(2,1)S(1)}, bf16[2,256,128]{2,1,0:T(8,128)(2,1)S(1)}, u32[]{:S(2)}, u32[]{:S(2)}) collective-permute-start(bf16[2,256,128]{2,1,0:T(8,128)(2,1)S(1)} %get-tuple-element.105), channel_id=1, source_target_pairs={{0,1},{3,2},{4,5},{7,6},{8,9},{11,10},{12,13},{15,14},{16,17},{19,... | collective-permute-start | bytes 393224 | tf_op jit(solution)/shard_map/ppermute | solution.py:351
  65.9 0.0 collective-permute-done.16
  66.0 0.7 collective-permute-start.19
  66.7 4.1 %collective-permute-start.20 = (f32[2,128]{1,0:T(2,128)S(1)}, f32[2,128]{1,0:T(2,128)S(1)}, u32[]{:S(2)}, u32[]{:S(2)}) collective-permute-start(f32[2,128]{1,0:T(2,128)S(1)} %get-tuple-element.117), channel_id=1, source_target_pairs={{0,1},{1,0},{2,3},{3,2},{4,5},{5,4},{6,7},{7,6},{8,9},{9,8},{10,11... | collective-permute-start | bytes 3080 | tf_op jit(solution)/shard_map/ppermute | solution.py:420
  70.7 0.0 collective-permute-done.17
  70.8 1.4 %collective-permute-done.20 = f32[2,128]{1,0:T(2,128)S(1)} collective-permute-done((f32[2,128]{1,0:T(2,128)S(1)}, f32[2,128]{1,0:T(2,128)S(1)}, u32[]{:S(2)}, u32[]{:S(2)}) %collective-permute-start.20) | collective-permute-done | bytes 1056 | tf_op jit(solution)/shard_map/ppermute | solution.py:420
  72.3 2.1 %collective-permute-start.21 = (f32[2,128]{1,0:T(2,128)S(1)}, f32[2,128]{1,0:T(2,128)S(1)}, u32[]{:S(2)}, u32[]{:S(2)}) collective-permute-start(f32[2,128]{1,0:T(2,128)S(1)} %add.46), channel_id=1, source_target_pairs={{0,2},{1,3},{2,0},{3,1},{4,6},{5,7},{6,4},{7,5},{8,10},{9,11},{10,... | collective-permute-start | bytes 3080 | tf_op jit(solution)/shard_map/ppermute | solution.py:422
  74.4 0.7 collective-permute-start.18
  75.0 1.3 %collective-permute-start.23 = (bf16[2,256,128]{2,1,0:T(8,128)(2,1)S(1)}, bf16[2,256,128]{2,1,0:T(8,128)(2,1)S(1)}, u32[]{:S(2)}, u32[]{:S(2)}) collective-permute-start(bf16[2,256,128]{2,1,0:T(8,128)(2,1)S(1)} %add_convert_fusion.3.refs_2_), channel_id=1, source_target_pairs={{1,0},{2,3},{5,4},{6,7},{9,8},{10,11},{13,12},{14,15},{17,16},{18,... | collective-permute-start | bytes 393224 | tf_op jit(solution)/shard_map/ppermute | solution.py:357
  76.3 1.3 %collective-permute-start.22 = (bf16[2,256,128]{2,1,0:T(8,128)(2,1)S(1)}, bf16[2,256,128]{2,1,0:T(8,128)(2,1)S(1)}, u32[]{:S(2)}, u32[]{:S(2)}) collective-permute-start(bf16[2,256,128]{2,1,0:T(8,128)(2,1)S(1)} %add_convert_fusion.5.refs_0_), channel_id=1, source_target_pairs={{1,0},{2,3},{5,4},{6,7},{9,8},{10,11},{13,12},{14,15},{17,16},{18,... | collective-permute-start | bytes 393224 | tf_op jit(solution)/shard_map/ppermute | solution.py:357
  77.6 0.0 copy-start.3
  77.6 2.0 %settle_heads.2 = (bf16[192,2048]{1,0:T(8,128)(2,1)}, bf16[192,2048]{1,0:T(8,128)(2,1)}, bf16[192,512]{1,0:T(8,128)(2,1)}, bf16[192,512]{1,0:T(8,128)(2,1)}) custom-call(s32[2]{0:T(128)S(1)} %pad_add_fusion.meta, f32[128,1]{1,0:T(8,128)S(1)} %copy.26.gain_ref, f32[1,128]{1,0:T(1,128)S(1)} %bitcast.27, f32[584,768]{1,0:T(8,128)S(1)} %get-tuple-element.111.rest_0_, ...), custom_call_target="tpu_custom_call" | custom-call | tf_op jit(solution)/shard_map/settle_heads/pallas_call | solution.py:274
  79.6 0.0 collective-permute-done.21
  79.7 0.0 collective-permute-done.18
  79.7 3.5 %collective-permute-done.23.refs_3_ = bf16[2,256,128]{2,1,0:T(8,128)(2,1)S(1)} collective-permute-done((bf16[2,256,128]{2,1,0:T(8,128)(2,1)S(1)}, bf16[2,256,128]{2,1,0:T(8,128)(2,1)S(1)}, u32[]{:S(2)}, u32[]{:S(2)}) %collective-permute-start.23) | collective-permute-done | bytes 131104 | tf_op jit(solution)/shard_map/ppermute | solution.py:357
  83.2 2.5 %collective-permute-done.22.refs_1_ = bf16[2,256,128]{2,1,0:T(8,128)(2,1)S(1)} collective-permute-done((bf16[2,256,128]{2,1,0:T(8,128)(2,1)S(1)}, bf16[2,256,128]{2,1,0:T(8,128)(2,1)S(1)}, u32[]{:S(2)}, u32[]{:S(2)}) %collective-permute-start.22) | collective-permute-done | bytes 131104 | tf_op jit(solution)/shard_map/ppermute | solution.py:357
  85.7 1.3 %collective-permute-start.25 = (bf16[2,256,128]{2,1,0:T(8,128)(2,1)S(1)}, bf16[2,256,128]{2,1,0:T(8,128)(2,1)S(1)}, u32[]{:S(2)}, u32[]{:S(2)}) collective-permute-start(bf16[2,256,128]{2,1,0:T(8,128)(2,1)S(1)} %add_convert_fusion.refs_6_), channel_id=1, source_target_pairs={{1,0},{2,3},{5,4},{6,7},{9,8},{10,11},{13,12},{14,15},{17,16},{18,... | collective-permute-start | bytes 393224 | tf_op jit(solution)/shard_map/ppermute | solution.py:357
  87.0 1.3 %collective-permute-start.24 = (bf16[2,256,128]{2,1,0:T(8,128)(2,1)S(1)}, bf16[2,256,128]{2,1,0:T(8,128)(2,1)S(1)}, u32[]{:S(2)}, u32[]{:S(2)}) collective-permute-start(bf16[2,256,128]{2,1,0:T(8,128)(2,1)S(1)} %add_convert_fusion.1.refs_4_), channel_id=1, source_target_pairs={{1,0},{2,3},{5,4},{6,7},{9,8},{10,11},{13,12},{14,15},{17,16},{18,... | collective-permute-start | bytes 393224 | tf_op jit(solution)/shard_map/ppermute | solution.py:357
  88.3 0.1 collective-permute-start.26
  88.4 1.1 %collective-permute-done.26 = f32[2,128]{1,0:T(2,128)S(1)} collective-permute-done((f32[2,128]{1,0:T(2,128)S(1)}, f32[2,128]{1,0:T(2,128)S(1)}, u32[]{:S(2)}, u32[]{:S(2)}) %collective-permute-start.26) | collective-permute-done | bytes 1056 | tf_op jit(solution)/shard_map/ppermute | solution.py:320
  89.5 1.5 %collective-permute-start.27 = (f32[2,128]{1,0:T(2,128)S(1)}, f32[2,128]{1,0:T(2,128)S(1)}, u32[]{:S(2)}, u32[]{:S(2)}) collective-permute-start(f32[2,128]{1,0:T(2,128)S(1)} %add.49), channel_id=1, source_target_pairs={{0,8},{4,12},{8,0},{12,4},{16,24},{20,28},{24,16},{28,20},{1,9},{5... | collective-permute-start | bytes 3080 | tf_op jit(solution)/shard_map/ppermute | solution.py:320
  91.0 2.1 %collective-permute-done.27 = f32[2,128]{1,0:T(2,128)S(1)} collective-permute-done((f32[2,128]{1,0:T(2,128)S(1)}, f32[2,128]{1,0:T(2,128)S(1)}, u32[]{:S(2)}, u32[]{:S(2)}) %collective-permute-start.27) | collective-permute-done | bytes 1056 | tf_op jit(solution)/shard_map/ppermute | solution.py:320
  93.1 1.5 %collective-permute-start.28 = (f32[2,128]{1,0:T(2,128)S(1)}, f32[2,128]{1,0:T(2,128)S(1)}, u32[]{:S(2)}, u32[]{:S(2)}) collective-permute-start(f32[2,128]{1,0:T(2,128)S(1)} %add.50), channel_id=1, source_target_pairs={{0,16},{4,20},{8,24},{12,28},{16,0},{20,4},{24,8},{28,12},{1,17},{... | collective-permute-start | bytes 3080 | tf_op jit(solution)/shard_map/ppermute | solution.py:320
  94.6 0.1 pad_add_fusion.1.meta
  94.7 1.5 %copy-done.1 = f32[584,768]{1,0:T(8,128)S(1)} copy-done((f32[584,768]{1,0:T(8,128)S(1)}, f32[584,768]{1,0:T(8,128)}, u32[]{:S(2)}) %copy-start.1) | copy-done | bytes 1794072
  96.2 1.9 %settle_heads.3 = (bf16[192,2048]{1,0:T(8,128)(2,1)}, bf16[192,2048]{1,0:T(8,128)(2,1)}, bf16[192,512]{1,0:T(8,128)(2,1)}, bf16[192,512]{1,0:T(8,128)(2,1)}) custom-call(s32[2]{0:T(128)S(1)} %pad_add_fusion.meta, f32[128,1]{1,0:T(8,128)S(1)} %copy.26.gain_ref, ...), custom_call_target="tpu_custom_call", output_to_operand_aliasing={{0}: (5, {}), {1}: (6, {}), {2}: (7, {}), {3}: (8, {})} | custom-call | tf_op jit(solution)/shard_map/settle_heads/pallas_call | solution.py:274
  98.1 0.6 add.51
  98.7 1.5 %place_prompt_grad.1 = bf16[2,256,512]{2,1,0:T(8,128)(2,1)} custom-call(s32[3]{0:T(128)S(1)} %pad_add_fusion.1.meta, bf16[2,256,128]{2,1,0:T(8,128)(2,1)S(1)} %add_convert_fusion.5.refs_0_, bf16[2,256,128]{2,1,0:T(8,128)(2,1)S(1)} %collective-permute-done.22.refs_1_, bf16[2,256,128]{2,1,0:T(8,128)(2,1)S(1)} %add_convert_fusion.3.refs_2_, ...), custom_call_target="tpu_custom_call" | custom-call | tf_op jit(solution)/shard_map/place_prompt_grad/pallas_call | solution.py:302
  (37 shorter events, 0.5 us)
Async XLA Ops:
  1.8 15.0 %collective-permute-start.2 = (bf16[2,256,128]{2,1,0:T(8,128)(2,1)S(1)}, bf16[2,256,128]{2,1,0:T(8,128)(2,1)S(1)}, u32[]{:S(2)}, u32[]{:S(2)}) collective-permute-start(bf16[2,256,128]{2,1,0:T(8,128)(2,1)S(1)} %get-tuple-element.71), channel_id=1, source_target_pairs={{0,1},{3,2},{4,5},{7,6},{8,9},{11,10},{12,13},{15,14},{16,17},{19,... | collective-permute-start | bytes 393224 | tf_op jit(solution)/shard_map/ppermute | solution.py:351
  6.7 10.8 %collective-permute-start.1 = (bf16[2,256,128]{2,1,0:T(8,128)(2,1)S(1)}, bf16[2,256,128]{2,1,0:T(8,128)(2,1)S(1)}, u32[]{:S(2)}, u32[]{:S(2)}) collective-permute-start(bf16[2,256,128]{2,1,0:T(8,128)(2,1)S(1)} %get-tuple-element.70), channel_id=1, source_target_pairs={{0,1},{3,2},{4,5},{7,6},{8,9},{11,10},{12,13},{15,14},{16,17},{19,... | collective-permute-start | bytes 393224 | tf_op jit(solution)/shard_map/ppermute | solution.py:351
  8.0 13.5 %collective-permute-start = (bf16[2,256,128]{2,1,0:T(8,128)(2,1)S(1)}, bf16[2,256,128]{2,1,0:T(8,128)(2,1)S(1)}, u32[]{:S(2)}, u32[]{:S(2)}) collective-permute-start(bf16[2,256,128]{2,1,0:T(8,128)(2,1)S(1)} %get-tuple-element.69), channel_id=1, source_target_pairs={{0,1},{3,2},{4,5},{7,6},{8,9},{11,10},{12,13},{15,14},{16,17},{19,... | collective-permute-start | bytes 393224 | tf_op jit(solution)/shard_map/ppermute | solution.py:351
  9.3 14.3 %collective-permute-start.5 = (bf16[2,256,128]{2,1,0:T(8,128)(2,1)S(1)}, bf16[2,256,128]{2,1,0:T(8,128)(2,1)S(1)}, u32[]{:S(2)}, u32[]{:S(2)}) collective-permute-start(bf16[2,256,128]{2,1,0:T(8,128)(2,1)S(1)} %get-tuple-element.78), channel_id=1, source_target_pairs={{0,1},{3,2},{4,5},{7,6},{8,9},{11,10},{12,13},{15,14},{16,17},{19,... | collective-permute-start | bytes 393224 | tf_op jit(solution)/shard_map/ppermute | solution.py:351
  12.8 0.7 copy-start.2
  16.8 5.4 %collective-permute-start.6 = (bf16[2,256,128]{2,1,0:T(8,128)(2,1)S(1)}, bf16[2,256,128]{2,1,0:T(8,128)(2,1)S(1)}, u32[]{:S(2)}, u32[]{:S(2)}) collective-permute-start(bf16[2,256,128]{2,1,0:T(8,128)(2,1)S(1)} %broadcast_select_fusion.3), channel_id=1, source_target_pairs={{1,2},{2,1},{5,6},{6,5},{9,10},{10,9},{13,14},{14,13},{17,18},{18,... | collective-permute-start | bytes 393224 | tf_op jit(solution)/shard_map/ppermute | solution.py:354
  17.5 6.8 %collective-permute-start.4 = (bf16[2,256,128]{2,1,0:T(8,128)(2,1)S(1)}, bf16[2,256,128]{2,1,0:T(8,128)(2,1)S(1)}, u32[]{:S(2)}, u32[]{:S(2)}) collective-permute-start(bf16[2,256,128]{2,1,0:T(8,128)(2,1)S(1)} %broadcast_select_fusion.2), channel_id=1, source_target_pairs={{1,2},{2,1},{5,6},{6,5},{9,10},{10,9},{13,14},{14,13},{17,18},{18,... | collective-permute-start | bytes 393224 | tf_op jit(solution)/shard_map/ppermute | solution.py:354
  21.6 4.1 %collective-permute-start.3 = (bf16[2,256,128]{2,1,0:T(8,128)(2,1)S(1)}, bf16[2,256,128]{2,1,0:T(8,128)(2,1)S(1)}, u32[]{:S(2)}, u32[]{:S(2)}) collective-permute-start(bf16[2,256,128]{2,1,0:T(8,128)(2,1)S(1)} %broadcast_select_fusion.1), channel_id=1, source_target_pairs={{1,2},{2,1},{5,6},{6,5},{9,10},{10,9},{13,14},{14,13},{17,18},{18,... | collective-permute-start | bytes 393224 | tf_op jit(solution)/shard_map/ppermute | solution.py:354
  22.3 10.9 %collective-permute-start.7 = (bf16[2,256,128]{2,1,0:T(8,128)(2,1)S(1)}, bf16[2,256,128]{2,1,0:T(8,128)(2,1)S(1)}, u32[]{:S(2)}, u32[]{:S(2)}) collective-permute-start(bf16[2,256,128]{2,1,0:T(8,128)(2,1)S(1)} %broadcast_select_fusion.7.near_ref), channel_id=1, source_target_pairs={{1,0},{2,3},{5,4},{6,7},{9,8},{10,11},{13,12},{14,15},{17,16},{18,... | collective-permute-start | bytes 393224 | tf_op jit(solution)/shard_map/ppermute | solution.py:357
  23.6 3.4 %collective-permute-start.8 = (bf16[2,256,128]{2,1,0:T(8,128)(2,1)S(1)}, bf16[2,256,128]{2,1,0:T(8,128)(2,1)S(1)}, u32[]{:S(2)}, u32[]{:S(2)}) collective-permute-start(bf16[2,256,128]{2,1,0:T(8,128)(2,1)S(1)} %broadcast_select_fusion), channel_id=1, source_target_pairs={{1,2},{2,1},{5,6},{6,5},{9,10},{10,9},{13,14},{14,13},{17,18},{18,... | collective-permute-start | bytes 393224 | tf_op jit(solution)/shard_map/ppermute | solution.py:354
  24.3 18.4 %collective-permute-start.12 = (bf16[2,256,128]{2,1,0:T(8,128)(2,1)S(1)}, bf16[2,256,128]{2,1,0:T(8,128)(2,1)S(1)}, u32[]{:S(2)}, u32[]{:S(2)}) collective-permute-start(bf16[2,256,128]{2,1,0:T(8,128)(2,1)S(1)} %broadcast_select_fusion.6.near_ref), channel_id=1, source_target_pairs={{1,0},{2,3},{5,4},{6,7},{9,8},{10,11},{13,12},{14,15},{17,16},{18,... | collective-permute-start | bytes 393224 | tf_op jit(solution)/shard_map/ppermute | solution.py:357
  25.7 17.0 %collective-permute-start.10 = (bf16[2,256,128]{2,1,0:T(8,128)(2,1)S(1)}, bf16[2,256,128]{2,1,0:T(8,128)(2,1)S(1)}, u32[]{:S(2)}, u32[]{:S(2)}) collective-permute-start(bf16[2,256,128]{2,1,0:T(8,128)(2,1)S(1)} %broadcast_select_fusion.5.near_ref), channel_id=1, source_target_pairs={{1,0},{2,3},{5,4},{6,7},{9,8},{10,11},{13,12},{14,15},{17,16},{18,... | collective-permute-start | bytes 393224 | tf_op jit(solution)/shard_map/ppermute | solution.py:357
  35.5 14.1 %collective-permute-start.9 = (bf16[2,256,128]{2,1,0:T(8,128)(2,1)S(1)}, bf16[2,256,128]{2,1,0:T(8,128)(2,1)S(1)}, u32[]{:S(2)}, u32[]{:S(2)}) collective-permute-start(bf16[2,256,128]{2,1,0:T(8,128)(2,1)S(1)} %get-tuple-element.87), channel_id=1, source_target_pairs={{0,1},{3,2},{4,5},{7,6},{8,9},{11,10},{12,13},{15,14},{16,17},{19,... | collective-permute-start | bytes 393224 | tf_op jit(solution)/shard_map/ppermute | solution.py:351
  41.4 11.4 %collective-permute-start.11 = (bf16[2,256,128]{2,1,0:T(8,128)(2,1)S(1)}, bf16[2,256,128]{2,1,0:T(8,128)(2,1)S(1)}, u32[]{:S(2)}, u32[]{:S(2)}) collective-permute-start(bf16[2,256,128]{2,1,0:T(8,128)(2,1)S(1)} %broadcast_select_fusion.4.near_ref), channel_id=1, source_target_pairs={{1,0},{2,3},{5,4},{6,7},{9,8},{10,11},{13,12},{14,15},{17,16},{18,... | collective-permute-start | bytes 393224 | tf_op jit(solution)/shard_map/ppermute | solution.py:357
  45.0 7.1 %collective-permute-start.13 = (bf16[2,256,128]{2,1,0:T(8,128)(2,1)S(1)}, bf16[2,256,128]{2,1,0:T(8,128)(2,1)S(1)}, u32[]{:S(2)}, u32[]{:S(2)}) collective-permute-start(bf16[2,256,128]{2,1,0:T(8,128)(2,1)S(1)} %get-tuple-element.99), channel_id=1, source_target_pairs={{0,1},{3,2},{4,5},{7,6},{8,9},{11,10},{12,13},{15,14},{16,17},{19,... | collective-permute-start | bytes 393224 | tf_op jit(solution)/shard_map/ppermute | solution.py:351
  49.6 16.2 %collective-permute-start.16 = (bf16[2,256,128]{2,1,0:T(8,128)(2,1)S(1)}, bf16[2,256,128]{2,1,0:T(8,128)(2,1)S(1)}, u32[]{:S(2)}, u32[]{:S(2)}) collective-permute-start(bf16[2,256,128]{2,1,0:T(8,128)(2,1)S(1)} %add_convert_fusion.7), channel_id=1, source_target_pairs={{1,2},{2,1},{5,6},{6,5},{9,10},{10,9},{13,14},{14,13},{17,18},{18,... | collective-permute-start | bytes 393224 | tf_op jit(solution)/shard_map/ppermute | solution.py:354
  52.1 18.6 %collective-permute-start.17 = (bf16[2,256,128]{2,1,0:T(8,128)(2,1)S(1)}, bf16[2,256,128]{2,1,0:T(8,128)(2,1)S(1)}, u32[]{:S(2)}, u32[]{:S(2)}) collective-permute-start(bf16[2,256,128]{2,1,0:T(8,128)(2,1)S(1)} %add_convert_fusion.6), channel_id=1, source_target_pairs={{1,2},{2,1},{5,6},{6,5},{9,10},{10,9},{13,14},{14,13},{17,18},{18,... | collective-permute-start | bytes 393224 | tf_op jit(solution)/shard_map/ppermute | solution.py:354
  55.0 10.9 %collective-permute-start.15 = (bf16[2,256,128]{2,1,0:T(8,128)(2,1)S(1)}, bf16[2,256,128]{2,1,0:T(8,128)(2,1)S(1)}, u32[]{:S(2)}, u32[]{:S(2)}) collective-permute-start(bf16[2,256,128]{2,1,0:T(8,128)(2,1)S(1)} %get-tuple-element.106), channel_id=1, source_target_pairs={{0,1},{3,2},{4,5},{7,6},{8,9},{11,10},{12,13},{15,14},{16,17},{19,... | collective-permute-start | bytes 393224 | tf_op jit(solution)/shard_map/ppermute | solution.py:351
  63.3 1.2 %copy-start = (f32[584,768]{1,0:T(8,128)}, f32[584,768]{1,0:T(8,128)S(1)}, u32[]{:S(2)}) copy-start(f32[584,768]{1,0:T(8,128)S(1)} %get-tuple-element.122.rest_1_) | copy-start | bytes 5382148
  64.6 6.2 %collective-permute-start.14 = (bf16[2,256,128]{2,1,0:T(8,128)(2,1)S(1)}, bf16[2,256,128]{2,1,0:T(8,128)(2,1)S(1)}, u32[]{:S(2)}, u32[]{:S(2)}) collective-permute-start(bf16[2,256,128]{2,1,0:T(8,128)(2,1)S(1)} %get-tuple-element.105), channel_id=1, source_target_pairs={{0,1},{3,2},{4,5},{7,6},{8,9},{11,10},{12,13},{15,14},{16,17},{19,... | collective-permute-start | bytes 393224 | tf_op jit(solution)/shard_map/ppermute | solution.py:351
  66.0 13.6 %collective-permute-start.19 = (bf16[2,256,128]{2,1,0:T(8,128)(2,1)S(1)}, bf16[2,256,128]{2,1,0:T(8,128)(2,1)S(1)}, u32[]{:S(2)}, u32[]{:S(2)}) collective-permute-start(bf16[2,256,128]{2,1,0:T(8,128)(2,1)S(1)} %add_convert_fusion.4), channel_id=1, source_target_pairs={{1,2},{2,1},{5,6},{6,5},{9,10},{10,9},{13,14},{14,13},{17,18},{18,... | collective-permute-start | bytes 393224 | tf_op jit(solution)/shard_map/ppermute | solution.py:354
  66.7 5.6 %collective-permute-start.20 = (f32[2,128]{1,0:T(2,128)S(1)}, f32[2,128]{1,0:T(2,128)S(1)}, u32[]{:S(2)}, u32[]{:S(2)}) collective-permute-start(f32[2,128]{1,0:T(2,128)S(1)} %get-tuple-element.117), channel_id=1, source_target_pairs={{0,1},{1,0},{2,3},{3,2},{4,5},{5,4},{6,7},{7,6},{8,9},{9,8},{10,11... | collective-permute-start | bytes 3080 | tf_op jit(solution)/shard_map/ppermute | solution.py:420
  72.3 7.3 %collective-permute-start.21 = (f32[2,128]{1,0:T(2,128)S(1)}, f32[2,128]{1,0:T(2,128)S(1)}, u32[]{:S(2)}, u32[]{:S(2)}) collective-permute-start(f32[2,128]{1,0:T(2,128)S(1)} %add.46), channel_id=1, source_target_pairs={{0,2},{1,3},{2,0},{3,1},{4,6},{5,7},{6,4},{7,5},{8,10},{9,11},{10,... | collective-permute-start | bytes 3080 | tf_op jit(solution)/shard_map/ppermute | solution.py:422
  74.4 5.3 %collective-permute-start.18 = (bf16[2,256,128]{2,1,0:T(8,128)(2,1)S(1)}, bf16[2,256,128]{2,1,0:T(8,128)(2,1)S(1)}, u32[]{:S(2)}, u32[]{:S(2)}) collective-permute-start(bf16[2,256,128]{2,1,0:T(8,128)(2,1)S(1)} %add_convert_fusion.2), channel_id=1, source_target_pairs={{1,2},{2,1},{5,6},{6,5},{9,10},{10,9},{13,14},{14,13},{17,18},{18,... | collective-permute-start | bytes 393224 | tf_op jit(solution)/shard_map/ppermute | solution.py:354
  75.0 8.2 %collective-permute-start.23 = (bf16[2,256,128]{2,1,0:T(8,128)(2,1)S(1)}, bf16[2,256,128]{2,1,0:T(8,128)(2,1)S(1)}, u32[]{:S(2)}, u32[]{:S(2)}) collective-permute-start(bf16[2,256,128]{2,1,0:T(8,128)(2,1)S(1)} %add_convert_fusion.3.refs_2_), channel_id=1, source_target_pairs={{1,0},{2,3},{5,4},{6,7},{9,8},{10,11},{13,12},{14,15},{17,16},{18,... | collective-permute-start | bytes 393224 | tf_op jit(solution)/shard_map/ppermute | solution.py:357
  76.3 9.3 %collective-permute-start.22 = (bf16[2,256,128]{2,1,0:T(8,128)(2,1)S(1)}, bf16[2,256,128]{2,1,0:T(8,128)(2,1)S(1)}, u32[]{:S(2)}, u32[]{:S(2)}) collective-permute-start(bf16[2,256,128]{2,1,0:T(8,128)(2,1)S(1)} %add_convert_fusion.5.refs_0_), channel_id=1, source_target_pairs={{1,0},{2,3},{5,4},{6,7},{9,8},{10,11},{13,12},{14,15},{17,16},{18,... | collective-permute-start | bytes 393224 | tf_op jit(solution)/shard_map/ppermute | solution.py:357
  77.6 17.1 %copy-start.3 = (f32[128]{0:T(128)S(1)}, f32[128]{0:T(128)}, u32[]{:S(2)}) copy-start(f32[128]{0:T(128)} %param.16) | copy-start | bytes 1540
  85.7 13.0 %collective-permute-start.25 = (bf16[2,256,128]{2,1,0:T(8,128)(2,1)S(1)}, bf16[2,256,128]{2,1,0:T(8,128)(2,1)S(1)}, u32[]{:S(2)}, u32[]{:S(2)}) collective-permute-start(bf16[2,256,128]{2,1,0:T(8,128)(2,1)S(1)} %add_convert_fusion.refs_6_), channel_id=1, source_target_pairs={{1,0},{2,3},{5,4},{6,7},{9,8},{10,11},{13,12},{14,15},{17,16},{18,... | collective-permute-start | bytes 393224 | tf_op jit(solution)/shard_map/ppermute | solution.py:357
  87.0 11.7 %collective-permute-start.24 = (bf16[2,256,128]{2,1,0:T(8,128)(2,1)S(1)}, bf16[2,256,128]{2,1,0:T(8,128)(2,1)S(1)}, u32[]{:S(2)}, u32[]{:S(2)}) collective-permute-start(bf16[2,256,128]{2,1,0:T(8,128)(2,1)S(1)} %add_convert_fusion.1.refs_4_), channel_id=1, source_target_pairs={{1,0},{2,3},{5,4},{6,7},{9,8},{10,11},{13,12},{14,15},{17,16},{18,... | collective-permute-start | bytes 393224 | tf_op jit(solution)/shard_map/ppermute | solution.py:357
  88.3 1.2 %collective-permute-start.26 = (f32[2,128]{1,0:T(2,128)S(1)}, f32[2,128]{1,0:T(2,128)S(1)}, u32[]{:S(2)}, u32[]{:S(2)}) collective-permute-start(f32[2,128]{1,0:T(2,128)S(1)} %add.47), channel_id=1, source_target_pairs={{0,4},{4,0},{8,12},{12,8},{16,20},{20,16},{24,28},{28,24},{1,5},{5... | collective-permute-start | bytes 3080 | tf_op jit(solution)/shard_map/ppermute | solution.py:320
  89.5 3.6 %collective-permute-start.27 = (f32[2,128]{1,0:T(2,128)S(1)}, f32[2,128]{1,0:T(2,128)S(1)}, u32[]{:S(2)}, u32[]{:S(2)}) collective-permute-start(f32[2,128]{1,0:T(2,128)S(1)} %add.49), channel_id=1, source_target_pairs={{0,8},{4,12},{8,0},{12,4},{16,24},{20,28},{24,16},{28,20},{1,9},{5... | collective-permute-start | bytes 3080 | tf_op jit(solution)/shard_map/ppermute | solution.py:320
  93.1 5.0 %collective-permute-start.28 = (f32[2,128]{1,0:T(2,128)S(1)}, f32[2,128]{1,0:T(2,128)S(1)}, u32[]{:S(2)}, u32[]{:S(2)}) collective-permute-start(f32[2,128]{1,0:T(2,128)S(1)} %add.50), channel_id=1, source_target_pairs={{0,16},{4,20},{8,24},{12,28},{16,0},{20,4},{24,8},{28,12},{1,17},{... | collective-permute-start | bytes 3080 | tf_op jit(solution)/shard_map/ppermute | solution.py:320
  94.7 1.5 %copy-start.1 = (f32[584,768]{1,0:T(8,128)S(1)}, f32[584,768]{1,0:T(8,128)}, u32[]{:S(2)}) copy-start(f32[584,768]{1,0:T(8,128)} %copy-done) | copy-start | bytes 5382148

commit v6 on v4

--- a/solution.py
+++ b/solution.py
@@ -362,45 +362,8 @@
     )(meta, *kept, q_gain, k_gain, *results, *buffers)
 
 
-def join_kernel(*refs):
-    total = refs[0][...].astype(F32)
-    for ref in refs[1:-1]:
-        total = total + ref[...].astype(F32)
-    refs[-1][...] = total.astype(BF)
-
-
-def join(parts):
-    return pl.pallas_call(
-        join_kernel,
-        out_shape=jax.ShapeDtypeStruct(parts[0].shape, BF),
-        in_specs=[VMEM] * len(parts),
-        out_specs=VMEM,
-        compiler_params=params(4),
-        name="join_parts",
-    )(*parts)
-
-
-def ordered_sum_kernel(count, order, *refs):
-    stage = refs[-1]
-    for i in range(count):
-        stage[order[i]] = refs[i][...]
-    total = stage[0]
-    for i in range(1, count):
-        total = total + stage[i]
-    refs[count][...] = total
-
-
-def ordered_sum(order, terms):
-    count = len(terms)
-    return pl.pallas_call(
-        functools.partial(ordered_sum_kernel, count),
-        out_shape=jax.ShapeDtypeStruct(terms[0].shape, F32),
-        in_specs=[SMEM] + [VMEM] * count,
-        out_specs=VMEM,
-        scratch_shapes=[pltpu.VMEM((count,) + terms[0].shape, F32)],
-        compiler_params=params(4),
-        name="sum_gains",
-    )(order, *terms)
+def join(a, b):
+    return (a.astype(F32) + b.astype(F32)).astype(BF)
 
 
 def place_kernel(meta, *refs):
@@ -421,6 +384,10 @@
         compiler_params=params(8),
         name="place_prompt_grad",
     )(meta, *heads)
+
+
+def after(x, *others):
+    return lax.optimization_barrier((x,) + others)[0]
 
 
 def pair_sum(value, axis, size):
@@ -461,17 +428,19 @@
         got = [blocks[0]] + [shift(blocks[s], -s) for s in range(1, n_group)]
         got[1], kept[0][2] = lax.optimization_barrier((got[1], kept[0][2]))
         mine = pick(jnp.reshape((owner - me) % n_group, (1,)).astype(jnp.int32), got)
-        prompts = [mine] + [shift(mine, s) for s in range(1, n_group)]
+        prompts = [mine]
+        for s in range(1, n_group):
+            prompts.append(shift(prompts[-1], 1))
     else:
         cache = lax.psum(jnp.where(me == owner, cache, jnp.zeros_like(cache)), "group")
         prompts = cut(order, cache, kv_heads)
 
     acc = jnp.zeros((2, HD), F32)
-    parts, backs, buffers = [], [], ()
+    parts, buffers, ring = [], (), None
     for s, prompt in enumerate(prompts):
         last = s == kv_heads - 1
-        if last and direct:
-            prompt, backs[0] = lax.optimization_barrier((prompt, backs[0]))
+        if last and ring is not None:
+            prompt = after(prompt, ring)
         if last:
             part, acc, *results = first_half(prompt, kept[s], gain_col, acc)
         else:
@@ -480,14 +449,13 @@
             )
         parts.append(part)
         if direct and s > 0:
-            backs.append(shift(part, -s))
+            ring = part if s == 1 else join(part, shift(ring, 1))
     buffers = list(second_half(kv_heads - 1, meta, kept[-1], gain_col, gain_row, results, buffers))
 
     mine_flag = (me == owner).astype(jnp.int32)
     if direct:
-        backs[-1], buffers[2] = lax.optimization_barrier((backs[-1], buffers[2]))
-        total = join([parts[0]] + backs)
-        gains = ordered_sum(order, [acc] + [shift(acc, s) for s in range(1, n_group)])
+        total = join(parts[0], after(shift(ring, 1), buffers[2]))
+        gains = pair_sum(after(acc, ring), "group", n_group)
         total, gains = lax.optimization_barrier((total, gains))
         heads = [total] + [shift(total, s) for s in range(1, n_group)]
         placed = place(jnp.concatenate([mine_flag[None], order]), heads)

time: 73.1 us -> 69 us (0.944)
  starting transfers between devices: 31.3 us -> 21.9 us
  waiting for transfers between devices: 15.6 us -> 21.5 us
    ppermute x15 -> x12, starting transfers between devices: 28.3 us -> 14.4 us  [shift(): lax.ppermute(x, 'group', [(i, (i + s) % n_group) for i in range(n_group)])]
    ppermute x3 -> x5, starting transfers between devices: 3.03 us -> 7.5 us  [pair_sum(): lax.ppermute(value, axis, [(i, i ^ step) for i in range(size)])]
    ppermute x15 -> x12, waiting for transfers between devices: 10.4 us -> 13.5 us  [shift(): lax.ppermute(x, 'group', [(i, (i + s) % n_group) for i in range(n_group)])]
    ppermute x3 -> x5, waiting for transfers between devices: 5.16 us -> 8.02 us  [pair_sum(): lax.ppermute(value, axis, [(i, i ^ step) for i in range(size)])]
  transfers between devices with their start and end apart: 18 -> 17, of which waited for: 7 -> 10; matrix products, arithmetic and copies ran while one was open for 1% -> 1% of each run, Pallas kernels for 23% -> 26%
where the time goes in v6:
time: 69 us; the launch traced here: 68.8 us
  starting transfers between devices  21.9 us (32%)
  waiting for transfers between devices  21.5 us (31%)
  Pallas kernels  20.9 us (30%)
  between operations  2.15 us (3%)
  local copies, waits for them, and re-layouts  1.59 us (2%)
  other arithmetic  0.77 us (1%)
    ppermute x12, starting transfers between devices, shift(): lax.ppermute(x, 'group', [(i, (i + s) % n_group) for i in range(n_group)])  14.4 us
    ppermute x12, waiting for transfers between devices, shift(): lax.ppermute(x, 'group', [(i, (i + s) % n_group) for i in range(n_group)])  13.5 us
    pallas_call x3, Pallas kernels, whole_head(): pl.pallas_call(functools.partial(whole_kernel, s, 2 * HD), out_shape=[jax...  9.22 us
    ppermute x5, waiting for transfers between devices, pair_sum(): lax.ppermute(value, axis, [(i, i ^ step) for i in range(size)])  8.02 us
    ppermute x5, starting transfers between devices, pair_sum(): lax.ppermute(value, axis, [(i, i ^ step) for i in range(size)])  7.5 us
    pallas_call x1, Pallas kernels, prepare(): pl.pallas_call(functools.partial(prepare_kernel, count, share, rows, 2 *...  5.15 us
    pallas_call x1, Pallas kernels, first_half(): pl.pallas_call(functools.partial(first_kernel, 2 * HD), out_shape=[jax.Sh...  1.71 us
    pallas_call x1, Pallas kernels, cut(): pl.pallas_call(cut_kernel, out_shape=[jax.ShapeDtypeStruct((depth, rows,...  1.69 us
  transfers between devices with their start and end apart: 17, of which 10 were waited for; matrix products, arithmetic and copies ran while one was open for 1% of the time, Pallas kernels for 26%

profile of v6, /device:TPU:0, one launch (start us, length us, event | category | flops | bytes accessed | tf_op | source)
XLA Modules:
  0.0 68.8 jit_solution(18314276500603493855)
XLA Ops:
  0.7 0.1 pad_add_fusion.order
  0.8 1.7 %cut_prompt.1 = (bf16[2,256,128]{2,1,0:T(8,128)(2,1)S(1)}, bf16[2,256,128]{2,1,0:T(8,128)(2,1)S(1)}, bf16[2,256,128]{2,1,0:T(8,128)(2,1)S(1)}, bf16[2,256,128]{2,1,0:T(8,128)(2,1)S(1)}) custom-call(s32[4]{0:T(128)S(1)} %pad_add_fusion.order, bf16[2,256,512]{2,1,0:T(8,128)(2,1)} %bitcast.34), custom_call_target="tpu_custom_call" | custom-call | tf_op jit(solution)/shard_map/cut_prompt/pallas_call | solution.py:48
  2.5 5.1 %collective-permute-start = (bf16[2,256,128]{2,1,0:T(8,128)(2,1)S(1)}, bf16[2,256,128]{2,1,0:T(8,128)(2,1)S(1)}, u32[]{:S(2)}, u32[]{:S(2)}) collective-permute-start(bf16[2,256,128]{2,1,0:T(8,128)(2,1)S(1)} %get-tuple-element.86), channel_id=1, source_target_pairs={{0,3},{1,0},{2,1},{3,2},{4,7},{5,4},{6,5},{7,6},{8,11},{9,8},{10,9... | collective-permute-start | bytes 393224 | tf_op jit(solution)/shard_map/ppermute | solution.py:415
  7.6 0.0 collective-permute-start.1
  7.6 1.0 %collective-permute-start.2 = (bf16[2,256,128]{2,1,0:T(8,128)(2,1)S(1)}, bf16[2,256,128]{2,1,0:T(8,128)(2,1)S(1)}, u32[]{:S(2)}, u32[]{:S(2)}) collective-permute-start(bf16[2,256,128]{2,1,0:T(8,128)(2,1)S(1)} %get-tuple-element.90), channel_id=1, source_target_pairs={{0,1},{1,2},{2,3},{3,0},{4,5},{5,6},{6,7},{7,4},{8,9},{9,10},{10,1... | collective-permute-start | bytes 393224 | tf_op jit(solution)/shard_map/ppermute | solution.py:415
  9.9 0.1 concatenate.8.meta
  10.0 0.0 copy-start.1
  10.0 0.7 copy-done.1
  10.6 0.1 copy.27.gain_ref.rest_8_
  10.8 0.0 copy-start
  10.8 0.6 copy-done
  11.4 5.1 %prepare_response.1 = (bf16[128,768]{1,0:T(8,128)(2,1)S(1)}, bf16[128,768]{1,0:T(8,128)(2,1)S(1)}, f32[8,768]{1,0:T(8,128)S(1)}, bf16[192,768]{1,0:T(8,128)(2,1)...) custom-call(s32[5]{0:T(128)S(1)} %concatenate.8.meta, ...), custom_call_target="tpu_custom_call" | custom-call | flops 452984832 | bytes 3932160 | tf_op jit(solution)/shard_map/prepare_response/pallas_call | solution.py:146
  16.6 0.0 collective-permute-done.refs_1_
  16.6 2.2 %collective-permute-done.1.refs_2_ = bf16[2,256,128]{2,1,0:T(8,128)(2,1)S(1)} collective-permute-done((bf16[2,256,128]{2,1,0:T(8,128)(2,1)S(1)}, bf16[2,256,128]{2,1,0:T(8,128)(2,1)S(1)}, u32[]{:S(2)}, u32[]{:S(2)}) %collective-permute-start.1) | collective-permute-done | bytes 131104 | tf_op jit(solution)/shard_map/ppermute | solution.py:415
  18.8 0.0 collective-permute-done.2.refs_3_
  18.8 0.1 pick_owner.1.pr_ref
  18.8 0.8 %collective-permute-start.3 = (bf16[2,256,128]{2,1,0:T(8,128)(2,1)S(1)}, bf16[2,256,128]{2,1,0:T(8,128)(2,1)S(1)}, u32[]{:S(2)}, u32[]{:S(2)}) collective-permute-start(bf16[2,256,128]{2,1,0:T(8,128)(2,1)S(1)} %pick_owner.1.pr_ref), channel_id=1, source_target_pairs={{0,1},{1,2},{2,3},{3,0},{4,5},{5,6},{6,7},{7,4},{8,9},{9,10},{10,1... | collective-permute-start | bytes 393224 | tf_op jit(solution)/shard_map/ppermute | solution.py:415
  19.6 3.1 %attend_head.3 = (bf16[2,256,128]{2,1,0:T(8,128)(2,1)S(1)}, f32[2,128]{1,0:T(2,128)S(1)}, bf16[192,2048]{1,0:T(8,128)(2,1)}, bf16[192,2048]{1,0:T(8,128)(2,1)}, ...) custom-call(s32[5]{0:T(128)S(1)} %concatenate.8.meta, bf16[2,256,128]{2,1,0:T(8,128)(2,1)S(1)} %pick_owner.1.pr_ref, ...), custom_call_target="tpu_custom_call" | custom-call | flops 276824064 | bytes 1048576 | tf_op jit(solution)/shard_map/attend_head/pallas_call | solution.py:309
  22.7 3.0 %collective-permute-done.3.pr_ref = bf16[2,256,128]{2,1,0:T(8,128)(2,1)S(1)} collective-permute-done((bf16[2,256,128]{2,1,0:T(8,128)(2,1)S(1)}, bf16[2,256,128]{2,1,0:T(8,128)(2,1)S(1)}, u32[]{:S(2)}, u32[]{:S(2)}) %collective-permute-start.3) | collective-permute-done | bytes 131104 | tf_op jit(solution)/shard_map/ppermute | solution.py:415
  25.7 0.0 collective-permute-start.4
  25.7 3.1 %attend_head.4 = (bf16[2,256,128]{2,1,0:T(8,128)(2,1)S(1)}, f32[2,128]{1,0:T(2,128)S(1)}, bf16[192,2048]{1,0:T(8,128)(2,1)}, bf16[192,2048]{1,0:T(8,128)(2,1)}, ...) custom-call(s32[5]{0:T(128)S(1)} %concatenate.8.meta, ...), custom_call_target="tpu_custom_call", output_to_operand_aliasing={{2}: (13, {}), {3}: (14, {}), {4}: (15, {}), {5}: (16, {})} | custom-call | flops 276824064 | bytes 1048576 | tf_op jit(solution)/shard_map/attend_head/pallas_call | solution.py:309
  28.7 1.4 %collective-permute-start.6 = (bf16[2,256,128]{2,1,0:T(8,128)(2,1)S(1)}, bf16[2,256,128]{2,1,0:T(8,128)(2,1)S(1)}, u32[]{:S(2)}, u32[]{:S(2)}) collective-permute-start(bf16[2,256,128]{2,1,0:T(8,128)(2,1)S(1)} %get-tuple-element.126), channel_id=1, source_target_pairs={{0,1},{1,2},{2,3},{3,0},{4,5},{5,6},{6,7},{7,4},{8,9},{9,10},{10,1... | collective-permute-start | bytes 393224 | tf_op jit(solution)/shard_map/ppermute | solution.py:415
  30.2 3.3 %collective-permute-done.4.pr_ref = bf16[2,256,128]{2,1,0:T(8,128)(2,1)S(1)} collective-permute-done((bf16[2,256,128]{2,1,0:T(8,128)(2,1)S(1)}, bf16[2,256,128]{2,1,0:T(8,128)(2,1)S(1)}, u32[]{:S(2)}, u32[]{:S(2)}) %collective-permute-start.4) | collective-permute-done | bytes 131104 | tf_op jit(solution)/shard_map/ppermute | solution.py:415
  33.5 0.0 collective-permute-start.5
  33.5 3.1 %attend_head.5 = (bf16[2,256,128]{2,1,0:T(8,128)(2,1)S(1)}, f32[2,128]{1,0:T(2,128)S(1)}, bf16[192,2048]{1,0:T(8,128)(2,1)}, bf16[192,2048]{1,0:T(8,128)(2,1)}, ...) custom-call(s32[5]{0:T(128)S(1)} %concatenate.8.meta, ...), custom_call_target="tpu_custom_call", output_to_operand_aliasing={{2}: (13, {}), {3}: (14, {}), {4}: (15, {}), {5}: (16, {})} | custom-call | flops 276824064 | bytes 1048576 | tf_op jit(solution)/shard_map/attend_head/pallas_call | solution.py:309
  36.6 0.1 collective-permute-done.6
  36.7 0.2 collective-permute-start.7
  36.9 4.0 %collective-permute-done.5.pr_ref = bf16[2,256,128]{2,1,0:T(8,128)(2,1)S(1)} collective-permute-done((bf16[2,256,128]{2,1,0:T(8,128)(2,1)S(1)}, bf16[2,256,128]{2,1,0:T(8,128)(2,1)S(1)}, u32[]{:S(2)}, u32[]{:S(2)}) %collective-permute-start.5) | collective-permute-done | bytes 131104 | tf_op jit(solution)/shard_map/ppermute | solution.py:415
  40.9 1.7 %attend_last_head.1 = (bf16[2,256,128]{2,1,0:T(8,128)(2,1)S(1)}, f32[2,128]{1,0:T(2,128)S(1)}, bf16[128,768]{1,0:T(8,128)(2,1)S(1)}, f32[128,768]{1,0:T(8,128)S(...) custom-call(bf16[2,256,128]{2,1,0:T(8,128)(2,1)S(1)} %collective-permute-done.5.pr_ref, ...), custom_call_target="tpu_custom_call" | custom-call | flops 276824064 | bytes 1048576 | tf_op jit(solution)/shard_map/attend_last_head/pallas_call | solution.py:331
  42.7 0.9 %collective-permute-done.7 = bf16[2,256,128]{2,1,0:T(8,128)(2,1)S(1)} collective-permute-done((bf16[2,256,128]{2,1,0:T(8,128)(2,1)S(1)}, bf16[2,256,128]{2,1,0:T(8,128)(2,1)S(1)}, u32[]{:S(2)}, u32[]{:S(2)}) %collective-permute-start.7) | collective-permute-done | bytes 131104 | tf_op jit(solution)/shard_map/ppermute | solution.py:415
  43.6 0.1 collective-permute-start.8
  43.7 0.8 %collective-permute-start.9 = (f32[2,128]{1,0:T(2,128)S(1)}, f32[2,128]{1,0:T(2,128)S(1)}, u32[]{:S(2)}, u32[]{:S(2)}) collective-permute-start(f32[2,128]{1,0:T(2,128)S(1)} %get-tuple-element.145), channel_id=1, source_target_pairs={{0,1},{1,0},{2,3},{3,2},{4,5},{5,4},{6,7},{7,6},{8,9},{9,8},{10,11... | collective-permute-start | bytes 3080 | tf_op jit(solution)/shard_map/ppermute | solution.py:396
  44.5 2.8 %collective-permute-done.9 = f32[2,128]{1,0:T(2,128)S(1)} collective-permute-done((f32[2,128]{1,0:T(2,128)S(1)}, f32[2,128]{1,0:T(2,128)S(1)}, u32[]{:S(2)}, u32[]{:S(2)}) %collective-permute-start.9) | collective-permute-done | bytes 1056 | tf_op jit(solution)/shard_map/ppermute | solution.py:396
  47.3 3.7 %collective-permute-start.10 = (f32[2,128]{1,0:T(2,128)S(1)}, f32[2,128]{1,0:T(2,128)S(1)}, u32[]{:S(2)}, u32[]{:S(2)}) collective-permute-start(f32[2,128]{1,0:T(2,128)S(1)} %add.51), channel_id=1, source_target_pairs={{0,2},{1,3},{2,0},{3,1},{4,6},{5,7},{6,4},{7,5},{8,10},{9,11},{10,... | collective-permute-start | bytes 3080 | tf_op jit(solution)/shard_map/ppermute | solution.py:396
  51.0 1.6 %settle_last_head.1 = (bf16[192,2048]{1,0:T(8,128)(2,1)}, bf16[192,2048]{1,0:T(8,128)(2,1)}, bf16[192,512]{1,0:T(8,128)(2,1)}, bf16[192,512]{1,0:T(8,128)(2,1)}) custom-call(s32[5]{0:T(128)S(1)} %concatenate.8.meta, bf16[128,768]{1,0:T(8,128)(2,1)S(1)} %get-tuple-element.77.rest_0_, ...), custom_call_target="tpu_custom_call", output_to_operand_aliasing={{0}: (15, {}), {1}: (16, {}), {2}: (17, {}), {3}: (18, {})} | custom-call | bytes 1048576 | tf_op jit(solution)/shard_map/settle_last_head/pallas_call | solution.py:352
  52.6 0.0 collective-permute-done.10
  52.7 0.0 collective-permute-done.8
  52.7 0.7 collective-permute-start.11
  53.4 3.4 %collective-permute-start.12 = (bf16[2,256,128]{2,1,0:T(8,128)(2,1)S(1)}, bf16[2,256,128]{2,1,0:T(8,128)(2,1)S(1)}, u32[]{:S(2)}, u32[]{:S(2)}) collective-permute-start(bf16[2,256,128]{2,1,0:T(8,128)(2,1)S(1)} %add_convert_fusion.refs_0_), channel_id=1, source_target_pairs={{0,2},{1,3},{2,0},{3,1},{4,6},{5,7},{6,4},{7,5},{8,10},{9,11},{10,... | collective-permute-start | bytes 393224 | tf_op jit(solution)/shard_map/ppermute | solution.py:415
  56.8 1.7 %collective-permute-start.13 = (bf16[2,256,128]{2,1,0:T(8,128)(2,1)S(1)}, bf16[2,256,128]{2,1,0:T(8,128)(2,1)S(1)}, u32[]{:S(2)}, u32[]{:S(2)}) collective-permute-start(bf16[2,256,128]{2,1,0:T(8,128)(2,1)S(1)} %add_convert_fusion.refs_0_), channel_id=1, source_target_pairs={{0,3},{1,0},{2,1},{3,2},{4,7},{5,4},{6,5},{7,6},{8,11},{9,8},{10,9... | collective-permute-start | bytes 393224 | tf_op jit(solution)/shard_map/ppermute | solution.py:415
  58.5 0.0 collective-permute-start.14
  58.5 1.1 %collective-permute-done.14 = f32[2,128]{1,0:T(2,128)S(1)} collective-permute-done((f32[2,128]{1,0:T(2,128)S(1)}, f32[2,128]{1,0:T(2,128)S(1)}, u32[]{:S(2)}, u32[]{:S(2)}) %collective-permute-start.14) | collective-permute-done | bytes 1056 | tf_op jit(solution)/shard_map/ppermute | solution.py:396
  59.6 1.5 %collective-permute-start.15 = (f32[2,128]{1,0:T(2,128)S(1)}, f32[2,128]{1,0:T(2,128)S(1)}, u32[]{:S(2)}, u32[]{:S(2)}) collective-permute-start(f32[2,128]{1,0:T(2,128)S(1)} %add.53), channel_id=1, source_target_pairs={{0,8},{4,12},{8,0},{12,4},{16,24},{20,28},{24,16},{28,20},{1,9},{5... | collective-permute-start | bytes 3080 | tf_op jit(solution)/shard_map/ppermute | solution.py:396
  61.1 2.1 %collective-permute-done.15 = f32[2,128]{1,0:T(2,128)S(1)} collective-permute-done((f32[2,128]{1,0:T(2,128)S(1)}, f32[2,128]{1,0:T(2,128)S(1)}, u32[]{:S(2)}, u32[]{:S(2)}) %collective-permute-start.15) | collective-permute-done | bytes 1056 | tf_op jit(solution)/shard_map/ppermute | solution.py:396
  63.2 1.5 %collective-permute-start.16 = (f32[2,128]{1,0:T(2,128)S(1)}, f32[2,128]{1,0:T(2,128)S(1)}, u32[]{:S(2)}, u32[]{:S(2)}) collective-permute-start(f32[2,128]{1,0:T(2,128)S(1)} %add.54), channel_id=1, source_target_pairs={{0,16},{4,20},{8,24},{12,28},{16,0},{20,4},{24,8},{28,12},{1,17},{... | collective-permute-start | bytes 3080 | tf_op jit(solution)/shard_map/ppermute | solution.py:396
  64.7 0.1 concatenate.9.meta
  64.8 2.0 %collective-permute-done.16 = f32[2,128]{1,0:T(2,128)S(1)} collective-permute-done((f32[2,128]{1,0:T(2,128)S(1)}, f32[2,128]{1,0:T(2,128)S(1)}, u32[]{:S(2)}, u32[]{:S(2)}) %collective-permute-start.16) | collective-permute-done | bytes 1056 | tf_op jit(solution)/shard_map/ppermute | solution.py:396
  66.8 0.6 add.55
  67.3 0.0 collective-permute-done.11.refs_1_
  67.3 0.0 collective-permute-done.12.refs_2_
  67.3 0.0 collective-permute-done.13.refs_3_
  67.3 1.4 %place_prompt_grad.1 = bf16[2,256,512]{2,1,0:T(8,128)(2,1)} custom-call(s32[5]{0:T(128)S(1)} %concatenate.9.meta, bf16[2,256,128]{2,1,0:T(8,128)(2,1)S(1)} %add_convert_fusion.refs_0_, bf16[2,256,128]{2,1,0:T(8,128)(2,1)S(1)} %collective-permute-done.11.refs_1_, bf16[2,256,128]{2,1,0:T(8,128)(2,1)S(1)} %collective-permute-done.12.refs_2_, ...), custom_call_target="tpu_custom_call" | custom-call | tf_op jit(solution)/shard_map/place_prompt_grad/pallas_call | solution.py:379
  (8 shorter events, 0.1 us)
Async XLA Ops:
  2.5 14.1 %collective-permute-start = (bf16[2,256,128]{2,1,0:T(8,128)(2,1)S(1)}, bf16[2,256,128]{2,1,0:T(8,128)(2,1)S(1)}, u32[]{:S(2)}, u32[]{:S(2)}) collective-permute-start(bf16[2,256,128]{2,1,0:T(8,128)(2,1)S(1)} %get-tuple-element.86), channel_id=1, source_target_pairs={{0,3},{1,0},{2,1},{3,2},{4,7},{5,4},{6,5},{7,6},{8,11},{9,8},{10,9... | collective-permute-start | bytes 393224 | tf_op jit(solution)/shard_map/ppermute | solution.py:415
  7.6 11.2 %collective-permute-start.1 = (bf16[2,256,128]{2,1,0:T(8,128)(2,1)S(1)}, bf16[2,256,128]{2,1,0:T(8,128)(2,1)S(1)}, u32[]{:S(2)}, u32[]{:S(2)}) collective-permute-start(bf16[2,256,128]{2,1,0:T(8,128)(2,1)S(1)} %get-tuple-element.89), channel_id=1, source_target_pairs={{0,2},{1,3},{2,0},{3,1},{4,6},{5,7},{6,4},{7,5},{8,10},{9,11},{10,... | collective-permute-start | bytes 393224 | tf_op jit(solution)/shard_map/ppermute | solution.py:415
  7.6 11.2 %collective-permute-start.2 = (bf16[2,256,128]{2,1,0:T(8,128)(2,1)S(1)}, bf16[2,256,128]{2,1,0:T(8,128)(2,1)S(1)}, u32[]{:S(2)}, u32[]{:S(2)}) collective-permute-start(bf16[2,256,128]{2,1,0:T(8,128)(2,1)S(1)} %get-tuple-element.90), channel_id=1, source_target_pairs={{0,1},{1,2},{2,3},{3,0},{4,5},{5,6},{6,7},{7,4},{8,9},{9,10},{10,1... | collective-permute-start | bytes 393224 | tf_op jit(solution)/shard_map/ppermute | solution.py:415
  10.0 0.7 copy-start.1
  10.8 0.7 copy-start
  18.8 6.8 %collective-permute-start.3 = (bf16[2,256,128]{2,1,0:T(8,128)(2,1)S(1)}, bf16[2,256,128]{2,1,0:T(8,128)(2,1)S(1)}, u32[]{:S(2)}, u32[]{:S(2)}) collective-permute-start(bf16[2,256,128]{2,1,0:T(8,128)(2,1)S(1)} %pick_owner.1.pr_ref), channel_id=1, source_target_pairs={{0,1},{1,2},{2,3},{3,0},{4,5},{5,6},{6,7},{7,4},{8,9},{9,10},{10,1... | collective-permute-start | bytes 393224 | tf_op jit(solution)/shard_map/ppermute | solution.py:415
  25.7 7.9 %collective-permute-start.4 = (bf16[2,256,128]{2,1,0:T(8,128)(2,1)S(1)}, bf16[2,256,128]{2,1,0:T(8,128)(2,1)S(1)}, u32[]{:S(2)}, u32[]{:S(2)}) collective-permute-start(bf16[2,256,128]{2,1,0:T(8,128)(2,1)S(1)} %collective-permute-done.3.pr_ref), channel_id=1, source_target_pairs={{0,1},{1,2},{2,3},{3,0},{4,5},{5,6},{6,7},{7,4},{8,9},{9,10},{10,1... | collective-permute-start | bytes 393224 | tf_op jit(solution)/shard_map/ppermute | solution.py:415
  28.7 7.9 %collective-permute-start.6 = (bf16[2,256,128]{2,1,0:T(8,128)(2,1)S(1)}, bf16[2,256,128]{2,1,0:T(8,128)(2,1)S(1)}, u32[]{:S(2)}, u32[]{:S(2)}) collective-permute-start(bf16[2,256,128]{2,1,0:T(8,128)(2,1)S(1)} %get-tuple-element.126), channel_id=1, source_target_pairs={{0,1},{1,2},{2,3},{3,0},{4,5},{5,6},{6,7},{7,4},{8,9},{9,10},{10,1... | collective-permute-start | bytes 393224 | tf_op jit(solution)/shard_map/ppermute | solution.py:415
  33.5 7.4 %collective-permute-start.5 = (bf16[2,256,128]{2,1,0:T(8,128)(2,1)S(1)}, bf16[2,256,128]{2,1,0:T(8,128)(2,1)S(1)}, u32[]{:S(2)}, u32[]{:S(2)}) collective-permute-start(bf16[2,256,128]{2,1,0:T(8,128)(2,1)S(1)} %collective-permute-done.4.pr_ref), channel_id=1, source_target_pairs={{0,1},{1,2},{2,3},{3,0},{4,5},{5,6},{6,7},{7,4},{8,9},{9,10},{10,1... | collective-permute-start | bytes 393224 | tf_op jit(solution)/shard_map/ppermute | solution.py:415
  36.7 6.8 %collective-permute-start.7 = (bf16[2,256,128]{2,1,0:T(8,128)(2,1)S(1)}, bf16[2,256,128]{2,1,0:T(8,128)(2,1)S(1)}, u32[]{:S(2)}, u32[]{:S(2)}) collective-permute-start(bf16[2,256,128]{2,1,0:T(8,128)(2,1)S(1)} %add_convert_fusion.2), channel_id=1, source_target_pairs={{0,1},{1,2},{2,3},{3,0},{4,5},{5,6},{6,7},{7,4},{8,9},{9,10},{10,1... | collective-permute-start | bytes 393224 | tf_op jit(solution)/shard_map/ppermute | solution.py:415
  43.6 9.1 %collective-permute-start.8 = (bf16[2,256,128]{2,1,0:T(8,128)(2,1)S(1)}, bf16[2,256,128]{2,1,0:T(8,128)(2,1)S(1)}, u32[]{:S(2)}, u32[]{:S(2)}) collective-permute-start(bf16[2,256,128]{2,1,0:T(8,128)(2,1)S(1)} %add_convert_fusion.1), channel_id=1, source_target_pairs={{0,1},{1,2},{2,3},{3,0},{4,5},{5,6},{6,7},{7,4},{8,9},{9,10},{10,1... | collective-permute-start | bytes 393224 | tf_op jit(solution)/shard_map/ppermute | solution.py:415
  43.7 3.6 %collective-permute-start.9 = (f32[2,128]{1,0:T(2,128)S(1)}, f32[2,128]{1,0:T(2,128)S(1)}, u32[]{:S(2)}, u32[]{:S(2)}) collective-permute-start(f32[2,128]{1,0:T(2,128)S(1)} %get-tuple-element.145), channel_id=1, source_target_pairs={{0,1},{1,0},{2,3},{3,2},{4,5},{5,4},{6,7},{7,6},{8,9},{9,8},{10,11... | collective-permute-start | bytes 3080 | tf_op jit(solution)/shard_map/ppermute | solution.py:396
  47.3 5.3 %collective-permute-start.10 = (f32[2,128]{1,0:T(2,128)S(1)}, f32[2,128]{1,0:T(2,128)S(1)}, u32[]{:S(2)}, u32[]{:S(2)}) collective-permute-start(f32[2,128]{1,0:T(2,128)S(1)} %add.51), channel_id=1, source_target_pairs={{0,2},{1,3},{2,0},{3,1},{4,6},{5,7},{6,4},{7,5},{8,10},{9,11},{10,... | collective-permute-start | bytes 3080 | tf_op jit(solution)/shard_map/ppermute | solution.py:396
  52.7 14.6 %collective-permute-start.11 = (bf16[2,256,128]{2,1,0:T(8,128)(2,1)S(1)}, bf16[2,256,128]{2,1,0:T(8,128)(2,1)S(1)}, u32[]{:S(2)}, u32[]{:S(2)}) collective-permute-start(bf16[2,256,128]{2,1,0:T(8,128)(2,1)S(1)} %add_convert_fusion.refs_0_), channel_id=1, source_target_pairs={{0,1},{1,2},{2,3},{3,0},{4,5},{5,6},{6,7},{7,4},{8,9},{9,10},{10,1... | collective-permute-start | bytes 393224 | tf_op jit(solution)/shard_map/ppermute | solution.py:415
  53.4 13.9 %collective-permute-start.12 = (bf16[2,256,128]{2,1,0:T(8,128)(2,1)S(1)}, bf16[2,256,128]{2,1,0:T(8,128)(2,1)S(1)}, u32[]{:S(2)}, u32[]{:S(2)}) collective-permute-start(bf16[2,256,128]{2,1,0:T(8,128)(2,1)S(1)} %add_convert_fusion.refs_0_), channel_id=1, source_target_pairs={{0,2},{1,3},{2,0},{3,1},{4,6},{5,7},{6,4},{7,5},{8,10},{9,11},{10,... | collective-permute-start | bytes 393224 | tf_op jit(solution)/shard_map/ppermute | solution.py:415
  56.8 10.6 %collective-permute-start.13 = (bf16[2,256,128]{2,1,0:T(8,128)(2,1)S(1)}, bf16[2,256,128]{2,1,0:T(8,128)(2,1)S(1)}, u32[]{:S(2)}, u32[]{:S(2)}) collective-permute-start(bf16[2,256,128]{2,1,0:T(8,128)(2,1)S(1)} %add_convert_fusion.refs_0_), channel_id=1, source_target_pairs={{0,3},{1,0},{2,1},{3,2},{4,7},{5,4},{6,5},{7,6},{8,11},{9,8},{10,9... | collective-permute-start | bytes 393224 | tf_op jit(solution)/shard_map/ppermute | solution.py:415
  58.5 1.1 %collective-permute-start.14 = (f32[2,128]{1,0:T(2,128)S(1)}, f32[2,128]{1,0:T(2,128)S(1)}, u32[]{:S(2)}, u32[]{:S(2)}) collective-permute-start(f32[2,128]{1,0:T(2,128)S(1)} %add.52), channel_id=1, source_target_pairs={{0,4},{4,0},{8,12},{12,8},{16,20},{20,16},{24,28},{28,24},{1,5},{5... | collective-permute-start | bytes 3080 | tf_op jit(solution)/shard_map/ppermute | solution.py:396
  59.6 3.6 %collective-permute-start.15 = (f32[2,128]{1,0:T(2,128)S(1)}, f32[2,128]{1,0:T(2,128)S(1)}, u32[]{:S(2)}, u32[]{:S(2)}) collective-permute-start(f32[2,128]{1,0:T(2,128)S(1)} %add.53), channel_id=1, source_target_pairs={{0,8},{4,12},{8,0},{12,4},{16,24},{20,28},{24,16},{28,20},{1,9},{5... | collective-permute-start | bytes 3080 | tf_op jit(solution)/shard_map/ppermute | solution.py:396
  63.2 3.6 %collective-permute-start.16 = (f32[2,128]{1,0:T(2,128)S(1)}, f32[2,128]{1,0:T(2,128)S(1)}, u32[]{:S(2)}, u32[]{:S(2)}) collective-permute-start(f32[2,128]{1,0:T(2,128)S(1)} %add.54), channel_id=1, source_target_pairs={{0,16},{4,20},{8,24},{12,28},{16,0},{20,4},{24,8},{28,12},{1,17},{... | collective-permute-start | bytes 3080 | tf_op jit(solution)/shard_map/ppermute | solution.py:396

commit v7 on v6

--- a/solution.py
+++ b/solution.py
@@ -362,28 +362,70 @@
     )(meta, *kept, q_gain, k_gain, *results, *buffers)
 
 
-def join(a, b):
-    return (a.astype(F32) + b.astype(F32)).astype(BF)
+TAIL = 16
+
+
+def join_kernel(own_ref, *rest):
+    backs, gains_ref, out_ref = rest[:-2], rest[-2], rest[-1]
+    depth, rows, _ = own_ref.shape
+    for d in range(depth):
+        total = own_ref[d].astype(F32)
+        for back in backs:
+            total = total + back[d].astype(F32)
+        out_ref[d * rows : (d + 1) * rows, :] = total.astype(BF)
+    gains = gains_ref[...]
+    high = gains.astype(BF)
+    gains = gains - high.astype(F32)
+    middle = gains.astype(BF)
+    low = (gains - middle.astype(F32)).astype(BF)
+    pieces = jnp.concatenate([p[0:2].astype(F32) for p in (high, middle, low)], axis=0)
+    pad = jnp.zeros((TAIL - pieces.shape[0], HD), F32)
+    out_ref[depth * rows :, :] = jnp.concatenate([pieces, pad], axis=0).astype(BF)
+
+
+def join(own, backs, gains):
+    depth, rows, _ = own.shape
+    return pl.pallas_call(
+        join_kernel,
+        out_shape=jax.ShapeDtypeStruct((depth * rows + TAIL, HD), BF),
+        in_specs=[VMEM] * (2 + len(backs)),
+        out_specs=VMEM,
+        compiler_params=params(8),
+        name="join_parts",
+    )(own, *backs, gains)
 
 
 def place_kernel(meta, *refs):
-    heads, out_ref = refs[:-1], refs[-1]
+    payloads, out_ref, gain_ref, stage = refs[:-3], refs[-3], refs[-2], refs[-1]
     mine = meta[0] > 0
-    for i, ref in enumerate(heads):
+    depth, rows, _ = out_ref.shape
+    for i, ref in enumerate(payloads):
         at = pl.multiple_of(meta[1 + i] * HD, HD)
-        out_ref[:, :, pl.ds(at, HD)] = jnp.where(mine, ref[...], jnp.zeros_like(ref[...]))
-
-
-def place(meta, heads):
-    depth, rows, _ = heads[0].shape
+        for d in range(depth):
+            block = ref[d * rows : (d + 1) * rows, :]
+            out_ref[d, :, pl.ds(at, HD)] = jnp.where(mine, block, jnp.zeros_like(block))
+        tail = ref[depth * rows :, :].astype(F32)
+        stage[meta[1 + i]] = tail[0:2] + tail[2:4] + tail[4:6]
+    total = stage[0]
+    for i in range(1, len(payloads)):
+        total = total + stage[i]
+    gain_ref[...] = total
+
+
+def place(meta, payloads, depth, rows):
+    count = len(payloads)
     return pl.pallas_call(
         place_kernel,
-        out_shape=jax.ShapeDtypeStruct((depth, rows, HD * len(heads)), BF),
-        in_specs=[SMEM] + [VMEM] * len(heads),
-        out_specs=VMEM,
+        out_shape=[
+            jax.ShapeDtypeStruct((depth, rows, HD * count), BF),
+            jax.ShapeDtypeStruct((2, HD), F32),
+        ],
+        in_specs=[SMEM] + [VMEM] * count,
+        out_specs=[VMEM, VMEM],
+        scratch_shapes=[pltpu.VMEM((count, 2, HD), F32)],
         compiler_params=params(8),
         name="place_prompt_grad",
-    )(meta, *heads)
+    )(meta, *payloads)
 
 
 def after(x, *others):
@@ -428,19 +470,15 @@
         got = [blocks[0]] + [shift(blocks[s], -s) for s in range(1, n_group)]
         got[1], kept[0][2] = lax.optimization_barrier((got[1], kept[0][2]))
         mine = pick(jnp.reshape((owner - me) % n_group, (1,)).astype(jnp.int32), got)
-        prompts = [mine]
-        for s in range(1, n_group):
-            prompts.append(shift(prompts[-1], 1))
+        prompts = [mine] + [shift(mine, s) for s in range(1, n_group)]
     else:
         cache = lax.psum(jnp.where(me == owner, cache, jnp.zeros_like(cache)), "group")
         prompts = cut(order, cache, kv_heads)
 
     acc = jnp.zeros((2, HD), F32)
-    parts, buffers, ring = [], (), None
+    parts, backs, buffers = [], [], ()
     for s, prompt in enumerate(prompts):
         last = s == kv_heads - 1
-        if last and ring is not None:
-            prompt = after(prompt, ring)
         if last:
             part, acc, *results = first_half(prompt, kept[s], gain_col, acc)
         else:
@@ -449,21 +487,21 @@
             )
         parts.append(part)
         if direct and s > 0:
-            ring = part if s == 1 else join(part, shift(ring, 1))
-    buffers = list(second_half(kv_heads - 1, meta, kept[-1], gain_col, gain_row, results, buffers))
-
+            backs.append(shift(part, -s))
     mine_flag = (me == owner).astype(jnp.int32)
     if direct:
-        total = join(parts[0], after(shift(ring, 1), buffers[2]))
-        gains = pair_sum(after(acc, ring), "group", n_group)
-        total, gains = lax.optimization_barrier((total, gains))
-        heads = [total] + [shift(total, s) for s in range(1, n_group)]
-        placed = place(jnp.concatenate([mine_flag[None], order]), heads)
+        results[0] = after(results[0], *backs[:-1])
+    buffers = list(second_half(kv_heads - 1, meta, kept[-1], gain_col, gain_row, results, buffers))
+    gains = pair_sum(acc, "dp", n_dp)
+    if direct:
+        backs[-1] = after(backs[-1], buffers[2])
+        payload = join(parts[0], backs, gains)
+        payloads = [payload] + [shift(payload, s) for s in range(1, n_group)]
+        placed, gains = place(jnp.concatenate([mine_flag[None], order]), payloads, depth, p_rows)
     else:
         total = lax.psum(jnp.concatenate(parts, axis=-1).astype(F32), "group").astype(BF)
         placed = jnp.where(mine_flag > 0, total, jnp.zeros((), BF))
-        gains = pair_sum(acc, "group", n_group)
-    gains = pair_sum(gains, "dp", n_dp)
+        gains = pair_sum(gains, "group", n_group)
     attended, d_query, d_key, d_value = buffers
     return (
         attended[None, None],

time: 69 us -> 66.4 us (0.962)
  waiting for transfers between devices: 21.5 us -> 15.6 us
  starting transfers between devices: 21.9 us -> 25.8 us
    ppermute x12, starting transfers between devices: 14.4 us -> 22.8 us  [shift(): lax.ppermute(x, 'group', [(i, (i + s) % n_group) for i in range(n_group)])]
    ppermute x5 -> x3, starting transfers between devices: 7.5 us -> 3.03 us  [pair_sum(): lax.ppermute(value, axis, [(i, i ^ step) for i in range(size)])]
    ppermute x12, waiting for transfers between devices: 13.5 us -> 10.3 us  [shift(): lax.ppermute(x, 'group', [(i, (i + s) % n_group) for i in range(n_group)])]
    ppermute x5 -> x3, waiting for transfers between devices: 8.02 us -> 5.25 us  [pair_sum(): lax.ppermute(value, axis, [(i, i ^ step) for i in range(size)])]
    pallas_call x1 -> x2, Pallas kernels: 1.45 us -> 1.53 us  [the longest x1 1.45 us: place(): pl.pallas_call(place_kernel, out_shape=[jax.ShapeDtypeStruct((depth, rows...]
  transfers between devices with their start and end apart: 17 -> 15, of which waited for: 10 -> 7; matrix products, arithmetic and copies ran while one was open for 1% -> 0% of each run, Pallas kernels for 26% -> 27%
where the time goes in v7:
time: 66.4 us; the launch traced here: 66.2 us
  starting transfers between devices  25.8 us (39%)
  Pallas kernels  21 us (32%)
  waiting for transfers between devices  15.6 us (23%)
  between operations  2.12 us (3%)
  local copies, waits for them, and re-layouts  1.59 us (2%)
    ppermute x12, starting transfers between devices, shift(): lax.ppermute(x, 'group', [(i, (i + s) % n_group) for i in range(n_group)])  22.8 us
    ppermute x12, waiting for transfers between devices, shift(): lax.ppermute(x, 'group', [(i, (i + s) % n_group) for i in range(n_group)])  10.3 us
    pallas_call x3, Pallas kernels, whole_head(): pl.pallas_call(functools.partial(whole_kernel, s, 2 * HD), out_shape=[jax...  9.23 us
    ppermute x3, waiting for transfers between devices, pair_sum(): lax.ppermute(value, axis, [(i, i ^ step) for i in range(size)])  5.25 us
    pallas_call x1, Pallas kernels, prepare(): pl.pallas_call(functools.partial(prepare_kernel, count, share, rows, 2 *...  5.15 us
    ppermute x3, starting transfers between devices, pair_sum(): lax.ppermute(value, axis, [(i, i ^ step) for i in range(size)])  3.03 us
    pallas_call x1, Pallas kernels, first_half(): pl.pallas_call(functools.partial(first_kernel, 2 * HD), out_shape=[jax.Sh...  1.71 us
    pallas_call x1, Pallas kernels, cut(): pl.pallas_call(cut_kernel, out_shape=[jax.ShapeDtypeStruct((depth, rows,...  1.69 us
  transfers between devices with their start and end apart: 15, of which 7 were waited for; matrix products, arithmetic and copies ran while one was open for 0% of the time, Pallas kernels for 27%

profile of v7, /device:TPU:0, one launch (start us, length us, event | category | flops | bytes accessed | tf_op | source)
XLA Modules:
  0.0 66.2 jit_solution(11291833392614544382)
XLA Ops:
  0.7 0.1 pad_add_fusion.order
  0.8 1.7 %cut_prompt.1 = (bf16[2,256,128]{2,1,0:T(8,128)(2,1)S(1)}, bf16[2,256,128]{2,1,0:T(8,128)(2,1)S(1)}, bf16[2,256,128]{2,1,0:T(8,128)(2,1)S(1)}, bf16[2,256,128]{2,1,0:T(8,128)(2,1)S(1)}) custom-call(s32[4]{0:T(128)S(1)} %pad_add_fusion.order, bf16[2,256,512]{2,1,0:T(8,128)(2,1)} %bitcast.34), custom_call_target="tpu_custom_call" | custom-call | tf_op jit(solution)/shard_map/cut_prompt/pallas_call | solution.py:48
  2.5 5.1 %collective-permute-start = (bf16[2,256,128]{2,1,0:T(8,128)(2,1)S(1)}, bf16[2,256,128]{2,1,0:T(8,128)(2,1)S(1)}, u32[]{:S(2)}, u32[]{:S(2)}) collective-permute-start(bf16[2,256,128]{2,1,0:T(8,128)(2,1)S(1)} %get-tuple-element.85), channel_id=1, source_target_pairs={{0,3},{1,0},{2,1},{3,2},{4,7},{5,4},{6,5},{7,6},{8,11},{9,8},{10,9... | collective-permute-start | bytes 393224 | tf_op jit(solution)/shard_map/ppermute | solution.py:457
  7.6 0.0 collective-permute-start.1
  7.6 1.0 %collective-permute-start.2 = (bf16[2,256,128]{2,1,0:T(8,128)(2,1)S(1)}, bf16[2,256,128]{2,1,0:T(8,128)(2,1)S(1)}, u32[]{:S(2)}, u32[]{:S(2)}) collective-permute-start(bf16[2,256,128]{2,1,0:T(8,128)(2,1)S(1)} %get-tuple-element.89), channel_id=1, source_target_pairs={{0,1},{1,2},{2,3},{3,0},{4,5},{5,6},{6,7},{7,4},{8,9},{9,10},{10,1... | collective-permute-start | bytes 393224 | tf_op jit(solution)/shard_map/ppermute | solution.py:457
  9.9 0.1 concatenate.8.meta
  10.0 0.0 copy-start.1
  10.0 0.7 copy-done.1
  10.6 0.1 copy.27.gain_ref.rest_8_
  10.8 0.0 copy-start
  10.8 0.6 copy-done
  11.4 5.1 %prepare_response.1 = (bf16[128,768]{1,0:T(8,128)(2,1)S(1)}, bf16[128,768]{1,0:T(8,128)(2,1)S(1)}, f32[8,768]{1,0:T(8,128)S(1)}, bf16[192,768]{1,0:T(8,128)(2,1)...) custom-call(s32[5]{0:T(128)S(1)} %concatenate.8.meta, ...), custom_call_target="tpu_custom_call" | custom-call | flops 452984832 | bytes 3932160 | tf_op jit(solution)/shard_map/prepare_response/pallas_call | solution.py:146
  16.6 0.0 collective-permute-done.refs_1_
  16.6 2.2 %collective-permute-done.1.refs_2_ = bf16[2,256,128]{2,1,0:T(8,128)(2,1)S(1)} collective-permute-done((bf16[2,256,128]{2,1,0:T(8,128)(2,1)S(1)}, bf16[2,256,128]{2,1,0:T(8,128)(2,1)S(1)}, u32[]{:S(2)}, u32[]{:S(2)}) %collective-permute-start.1) | collective-permute-done | bytes 131104 | tf_op jit(solution)/shard_map/ppermute | solution.py:457
  18.8 0.0 collective-permute-done.2.refs_3_
  18.8 0.1 pick_owner.1.pr_ref
  18.8 0.8 %collective-permute-start.5 = (bf16[2,256,128]{2,1,0:T(8,128)(2,1)S(1)}, bf16[2,256,128]{2,1,0:T(8,128)(2,1)S(1)}, u32[]{:S(2)}, u32[]{:S(2)}) collective-permute-start(bf16[2,256,128]{2,1,0:T(8,128)(2,1)S(1)} %pick_owner.1.pr_ref), channel_id=1, source_target_pairs={{0,1},{1,2},{2,3},{3,0},{4,5},{5,6},{6,7},{7,4},{8,9},{9,10},{10,1... | collective-permute-start | bytes 393224 | tf_op jit(solution)/shard_map/ppermute | solution.py:457
  19.6 2.0 %collective-permute-start.4 = (bf16[2,256,128]{2,1,0:T(8,128)(2,1)S(1)}, bf16[2,256,128]{2,1,0:T(8,128)(2,1)S(1)}, u32[]{:S(2)}, u32[]{:S(2)}) collective-permute-start(bf16[2,256,128]{2,1,0:T(8,128)(2,1)S(1)} %pick_owner.1.pr_ref), channel_id=1, source_target_pairs={{0,2},{1,3},{2,0},{3,1},{4,6},{5,7},{6,4},{7,5},{8,10},{9,11},{10,... | collective-permute-start | bytes 393224 | tf_op jit(solution)/shard_map/ppermute | solution.py:457
  21.6 2.8 %collective-permute-start.3 = (bf16[2,256,128]{2,1,0:T(8,128)(2,1)S(1)}, bf16[2,256,128]{2,1,0:T(8,128)(2,1)S(1)}, u32[]{:S(2)}, u32[]{:S(2)}) collective-permute-start(bf16[2,256,128]{2,1,0:T(8,128)(2,1)S(1)} %pick_owner.1.pr_ref), channel_id=1, source_target_pairs={{0,3},{1,0},{2,1},{3,2},{4,7},{5,4},{6,5},{7,6},{8,11},{9,8},{10,9... | collective-permute-start | bytes 393224 | tf_op jit(solution)/shard_map/ppermute | solution.py:457
  24.4 3.1 %attend_head.3 = (bf16[2,256,128]{2,1,0:T(8,128)(2,1)S(1)}, f32[2,128]{1,0:T(2,128)S(1)}, bf16[192,2048]{1,0:T(8,128)(2,1)}, bf16[192,2048]{1,0:T(8,128)(2,1)}, ...) custom-call(s32[5]{0:T(128)S(1)} %concatenate.8.meta, bf16[2,256,128]{2,1,0:T(8,128)(2,1)S(1)} %pick_owner.1.pr_ref, ...), custom_call_target="tpu_custom_call" | custom-call | flops 276824064 | bytes 1048576 | tf_op jit(solution)/shard_map/attend_head/pallas_call | solution.py:309
  27.5 0.0 collective-permute-done.5.pr_ref
  27.5 3.1 %attend_head.4 = (bf16[2,256,128]{2,1,0:T(8,128)(2,1)S(1)}, f32[2,128]{1,0:T(2,128)S(1)}, bf16[192,2048]{1,0:T(8,128)(2,1)}, bf16[192,2048]{1,0:T(8,128)(2,1)}, ...) custom-call(s32[5]{0:T(128)S(1)} %concatenate.8.meta, ...), custom_call_target="tpu_custom_call", output_to_operand_aliasing={{2}: (13, {}), {3}: (14, {}), {4}: (15, {}), {5}: (16, {})} | custom-call | flops 276824064 | bytes 1048576 | tf_op jit(solution)/shard_map/attend_head/pallas_call | solution.py:309
  30.6 0.6 collective-permute-done.4.pr_ref
  31.2 3.1 %attend_head.5 = (bf16[2,256,128]{2,1,0:T(8,128)(2,1)S(1)}, f32[2,128]{1,0:T(2,128)S(1)}, bf16[192,2048]{1,0:T(8,128)(2,1)}, bf16[192,2048]{1,0:T(8,128)(2,1)}, ...) custom-call(s32[5]{0:T(128)S(1)} %concatenate.8.meta, ...), custom_call_target="tpu_custom_call", output_to_operand_aliasing={{2}: (13, {}), {3}: (14, {}), {4}: (15, {}), {5}: (16, {})} | custom-call | flops 276824064 | bytes 1048576 | tf_op jit(solution)/shard_map/attend_head/pallas_call | solution.py:309
  34.3 5.1 %collective-permute-start.7 = (bf16[2,256,128]{2,1,0:T(8,128)(2,1)S(1)}, bf16[2,256,128]{2,1,0:T(8,128)(2,1)S(1)}, u32[]{:S(2)}, u32[]{:S(2)}) collective-permute-start(bf16[2,256,128]{2,1,0:T(8,128)(2,1)S(1)} %get-tuple-element.127), channel_id=1, source_target_pairs={{0,2},{1,3},{2,0},{3,1},{4,6},{5,7},{6,4},{7,5},{8,10},{9,11},{10,... | collective-permute-start | bytes 393224 | tf_op jit(solution)/shard_map/ppermute | solution.py:457
  39.4 0.5 collective-permute-start.6
  39.9 0.0 collective-permute-done.3.pr_ref
  39.9 1.7 %attend_last_head.1 = (bf16[2,256,128]{2,1,0:T(8,128)(2,1)S(1)}, f32[2,128]{1,0:T(2,128)S(1)}, bf16[128,768]{1,0:T(8,128)(2,1)S(1)}, f32[128,768]{1,0:T(8,128)S(...) custom-call(bf16[2,256,128]{2,1,0:T(8,128)(2,1)S(1)} %collective-permute-done.3.pr_ref, ...), custom_call_target="tpu_custom_call" | custom-call | flops 276824064 | bytes 1048576 | tf_op jit(solution)/shard_map/attend_last_head/pallas_call | solution.py:331
  41.6 1.6 %collective-permute-start.8 = (bf16[2,256,128]{2,1,0:T(8,128)(2,1)S(1)}, bf16[2,256,128]{2,1,0:T(8,128)(2,1)S(1)}, u32[]{:S(2)}, u32[]{:S(2)}) collective-permute-start(bf16[2,256,128]{2,1,0:T(8,128)(2,1)S(1)} %get-tuple-element.141), channel_id=1, source_target_pairs={{0,1},{1,2},{2,3},{3,0},{4,5},{5,6},{6,7},{7,4},{8,9},{9,10},{10,1... | collective-permute-start | bytes 393224 | tf_op jit(solution)/shard_map/ppermute | solution.py:457
  43.2 0.0 collective-permute-start.9
  43.2 1.1 %collective-permute-done.9 = f32[2,128]{1,0:T(2,128)S(1)} collective-permute-done((f32[2,128]{1,0:T(2,128)S(1)}, f32[2,128]{1,0:T(2,128)S(1)}, u32[]{:S(2)}, u32[]{:S(2)}) %collective-permute-start.9) | collective-permute-done | bytes 1056 | tf_op jit(solution)/shard_map/ppermute | solution.py:438
  44.4 1.5 %collective-permute-start.10 = (f32[2,128]{1,0:T(2,128)S(1)}, f32[2,128]{1,0:T(2,128)S(1)}, u32[]{:S(2)}, u32[]{:S(2)}) collective-permute-start(f32[2,128]{1,0:T(2,128)S(1)} %add.33), channel_id=1, source_target_pairs={{0,8},{4,12},{8,0},{12,4},{16,24},{20,28},{24,16},{28,20},{1,9},{5... | collective-permute-start | bytes 3080 | tf_op jit(solution)/shard_map/ppermute | solution.py:438
  45.9 2.1 %collective-permute-done.10 = f32[2,128]{1,0:T(2,128)S(1)} collective-permute-done((f32[2,128]{1,0:T(2,128)S(1)}, f32[2,128]{1,0:T(2,128)S(1)}, u32[]{:S(2)}, u32[]{:S(2)}) %collective-permute-start.10) | collective-permute-done | bytes 1056 | tf_op jit(solution)/shard_map/ppermute | solution.py:438
  47.9 1.5 %collective-permute-start.11 = (f32[2,128]{1,0:T(2,128)S(1)}, f32[2,128]{1,0:T(2,128)S(1)}, u32[]{:S(2)}, u32[]{:S(2)}) collective-permute-start(f32[2,128]{1,0:T(2,128)S(1)} %add.34), channel_id=1, source_target_pairs={{0,16},{4,20},{8,24},{12,28},{16,0},{20,4},{24,8},{28,12},{1,17},{... | collective-permute-start | bytes 3080 | tf_op jit(solution)/shard_map/ppermute | solution.py:438
  49.5 2.0 %collective-permute-done.11 = f32[2,128]{1,0:T(2,128)S(1)} collective-permute-done((f32[2,128]{1,0:T(2,128)S(1)}, f32[2,128]{1,0:T(2,128)S(1)}, u32[]{:S(2)}, u32[]{:S(2)}) %collective-permute-start.11) | collective-permute-done | bytes 1056 | tf_op jit(solution)/shard_map/ppermute | solution.py:438
  51.5 0.0 collective-permute-done.7.rest_1_
  51.5 0.0 collective-permute-done.6.rest_0_
  51.5 1.7 %settle_last_head.1 = (bf16[192,2048]{1,0:T(8,128)(2,1)}, bf16[192,2048]{1,0:T(8,128)(2,1)}, bf16[192,512]{1,0:T(8,128)(2,1)}, bf16[192,512]{1,0:T(8,128)(2,1)}) custom-call(s32[5]{0:T(128)S(1)} %concatenate.8.meta, bf16[128,768]{1,0:T(8,128)(2,1)S(1)} %get-tuple-element.76.rest_0_, ...), custom_call_target="tpu_custom_call", output_to_operand_aliasing={{0}: (15, {}), {1}: (16, {}), {2}: (17, {}), {3}: (18, {})} | custom-call | bytes 1048576 | tf_op jit(solution)/shard_map/settle_last_head/pallas_call | solution.py:352
  53.2 0.0 collective-permute-done.8.rest_2_
  53.2 0.1 join_parts.1.refs_0_
  53.3 0.1 collective-permute-start.12
  53.4 2.7 %collective-permute-start.13 = (bf16[528,128]{1,0:T(8,128)(2,1)S(1)}, bf16[528,128]{1,0:T(8,128)(2,1)S(1)}, u32[]{:S(2)}, u32[]{:S(2)}) collective-permute-start(bf16[528,128]{1,0:T(8,128)(2,1)S(1)} %join_parts.1.refs_0_), channel_id=1, source_target_pairs={{0,2},{1,3},{2,0},{3,1},{4,6},{5,7},{6,4},{7,5},{8,10},{9,11},{10,... | collective-permute-start | bytes 405512 | tf_op jit(solution)/shard_map/ppermute | solution.py:457
  56.2 1.0 %collective-permute-start.14 = (bf16[528,128]{1,0:T(8,128)(2,1)S(1)}, bf16[528,128]{1,0:T(8,128)(2,1)S(1)}, u32[]{:S(2)}, u32[]{:S(2)}) collective-permute-start(bf16[528,128]{1,0:T(8,128)(2,1)S(1)} %join_parts.1.refs_0_), channel_id=1, source_target_pairs={{0,3},{1,0},{2,1},{3,2},{4,7},{5,4},{6,5},{7,6},{8,11},{9,8},{10,9... | collective-permute-start | bytes 405512 | tf_op jit(solution)/shard_map/ppermute | solution.py:457
  57.2 0.1 concatenate.9.meta
  57.2 4.4 %collective-permute-done.12.refs_1_ = bf16[528,128]{1,0:T(8,128)(2,1)S(1)} collective-permute-done((bf16[528,128]{1,0:T(8,128)(2,1)S(1)}, bf16[528,128]{1,0:T(8,128)(2,1)S(1)}, u32[]{:S(2)}, u32[]{:S(2)}) %collective-permute-start.12) | collective-permute-done | bytes 135200 | tf_op jit(solution)/shard_map/ppermute | solution.py:457
  61.7 3.1 %collective-permute-done.13.refs_2_ = bf16[528,128]{1,0:T(8,128)(2,1)S(1)} collective-permute-done((bf16[528,128]{1,0:T(8,128)(2,1)S(1)}, bf16[528,128]{1,0:T(8,128)(2,1)S(1)}, u32[]{:S(2)}, u32[]{:S(2)}) %collective-permute-start.13) | collective-permute-done | bytes 135200 | tf_op jit(solution)/shard_map/ppermute | solution.py:457
  64.8 0.0 collective-permute-done.14.refs_3_
  64.8 1.5 %place_prompt_grad.1 = (bf16[2,256,512]{2,1,0:T(8,128)(2,1)}, f32[2,128]{1,0:T(2,128)}) custom-call(s32[5]{0:T(128)S(1)} %concatenate.9.meta, bf16[528,128]{1,0:T(8,128)(2,1)S(1)} %join_parts.1.refs_0_, bf16[528,128]{1,0:T(8,128)(2,1)S(1)} %collective-permute-done.12.refs_1_, bf16[528,128]{1,0:T(8,128)(2,1)S(1)} %collective-permute-done.13.refs_2_, ...), custom_call_target="tpu_custom_call" | custom-call | tf_op jit(solution)/shard_map/place_prompt_grad/pallas_call | solution.py:417
  (4 shorter events, 0.0 us)
Async XLA Ops:
  2.5 14.1 %collective-permute-start = (bf16[2,256,128]{2,1,0:T(8,128)(2,1)S(1)}, bf16[2,256,128]{2,1,0:T(8,128)(2,1)S(1)}, u32[]{:S(2)}, u32[]{:S(2)}) collective-permute-start(bf16[2,256,128]{2,1,0:T(8,128)(2,1)S(1)} %get-tuple-element.85), channel_id=1, source_target_pairs={{0,3},{1,0},{2,1},{3,2},{4,7},{5,4},{6,5},{7,6},{8,11},{9,8},{10,9... | collective-permute-start | bytes 393224 | tf_op jit(solution)/shard_map/ppermute | solution.py:457
  7.6 11.2 %collective-permute-start.1 = (bf16[2,256,128]{2,1,0:T(8,128)(2,1)S(1)}, bf16[2,256,128]{2,1,0:T(8,128)(2,1)S(1)}, u32[]{:S(2)}, u32[]{:S(2)}) collective-permute-start(bf16[2,256,128]{2,1,0:T(8,128)(2,1)S(1)} %get-tuple-element.88), channel_id=1, source_target_pairs={{0,2},{1,3},{2,0},{3,1},{4,6},{5,7},{6,4},{7,5},{8,10},{9,11},{10,... | collective-permute-start | bytes 393224 | tf_op jit(solution)/shard_map/ppermute | solution.py:457
  7.6 11.2 %collective-permute-start.2 = (bf16[2,256,128]{2,1,0:T(8,128)(2,1)S(1)}, bf16[2,256,128]{2,1,0:T(8,128)(2,1)S(1)}, u32[]{:S(2)}, u32[]{:S(2)}) collective-permute-start(bf16[2,256,128]{2,1,0:T(8,128)(2,1)S(1)} %get-tuple-element.89), channel_id=1, source_target_pairs={{0,1},{1,2},{2,3},{3,0},{4,5},{5,6},{6,7},{7,4},{8,9},{9,10},{10,1... | collective-permute-start | bytes 393224 | tf_op jit(solution)/shard_map/ppermute | solution.py:457
  10.0 0.7 copy-start.1
  10.8 0.7 copy-start
  18.8 8.7 %collective-permute-start.5 = (bf16[2,256,128]{2,1,0:T(8,128)(2,1)S(1)}, bf16[2,256,128]{2,1,0:T(8,128)(2,1)S(1)}, u32[]{:S(2)}, u32[]{:S(2)}) collective-permute-start(bf16[2,256,128]{2,1,0:T(8,128)(2,1)S(1)} %pick_owner.1.pr_ref), channel_id=1, source_target_pairs={{0,1},{1,2},{2,3},{3,0},{4,5},{5,6},{6,7},{7,4},{8,9},{9,10},{10,1... | collective-permute-start | bytes 393224 | tf_op jit(solution)/shard_map/ppermute | solution.py:457
  19.6 11.6 %collective-permute-start.4 = (bf16[2,256,128]{2,1,0:T(8,128)(2,1)S(1)}, bf16[2,256,128]{2,1,0:T(8,128)(2,1)S(1)}, u32[]{:S(2)}, u32[]{:S(2)}) collective-permute-start(bf16[2,256,128]{2,1,0:T(8,128)(2,1)S(1)} %pick_owner.1.pr_ref), channel_id=1, source_target_pairs={{0,2},{1,3},{2,0},{3,1},{4,6},{5,7},{6,4},{7,5},{8,10},{9,11},{10,... | collective-permute-start | bytes 393224 | tf_op jit(solution)/shard_map/ppermute | solution.py:457
  21.6 18.3 %collective-permute-start.3 = (bf16[2,256,128]{2,1,0:T(8,128)(2,1)S(1)}, bf16[2,256,128]{2,1,0:T(8,128)(2,1)S(1)}, u32[]{:S(2)}, u32[]{:S(2)}) collective-permute-start(bf16[2,256,128]{2,1,0:T(8,128)(2,1)S(1)} %pick_owner.1.pr_ref), channel_id=1, source_target_pairs={{0,3},{1,0},{2,1},{3,2},{4,7},{5,4},{6,5},{7,6},{8,11},{9,8},{10,9... | collective-permute-start | bytes 393224 | tf_op jit(solution)/shard_map/ppermute | solution.py:457
  34.3 17.2 %collective-permute-start.7 = (bf16[2,256,128]{2,1,0:T(8,128)(2,1)S(1)}, bf16[2,256,128]{2,1,0:T(8,128)(2,1)S(1)}, u32[]{:S(2)}, u32[]{:S(2)}) collective-permute-start(bf16[2,256,128]{2,1,0:T(8,128)(2,1)S(1)} %get-tuple-element.127), channel_id=1, source_target_pairs={{0,2},{1,3},{2,0},{3,1},{4,6},{5,7},{6,4},{7,5},{8,10},{9,11},{10,... | collective-permute-start | bytes 393224 | tf_op jit(solution)/shard_map/ppermute | solution.py:457
  39.4 12.1 %collective-permute-start.6 = (bf16[2,256,128]{2,1,0:T(8,128)(2,1)S(1)}, bf16[2,256,128]{2,1,0:T(8,128)(2,1)S(1)}, u32[]{:S(2)}, u32[]{:S(2)}) collective-permute-start(bf16[2,256,128]{2,1,0:T(8,128)(2,1)S(1)} %get-tuple-element.126), channel_id=1, source_target_pairs={{0,3},{1,0},{2,1},{3,2},{4,7},{5,4},{6,5},{7,6},{8,11},{9,8},{10,9... | collective-permute-start | bytes 393224 | tf_op jit(solution)/shard_map/ppermute | solution.py:457
  41.6 11.6 %collective-permute-start.8 = (bf16[2,256,128]{2,1,0:T(8,128)(2,1)S(1)}, bf16[2,256,128]{2,1,0:T(8,128)(2,1)S(1)}, u32[]{:S(2)}, u32[]{:S(2)}) collective-permute-start(bf16[2,256,128]{2,1,0:T(8,128)(2,1)S(1)} %get-tuple-element.141), channel_id=1, source_target_pairs={{0,1},{1,2},{2,3},{3,0},{4,5},{5,6},{6,7},{7,4},{8,9},{9,10},{10,1... | collective-permute-start | bytes 393224 | tf_op jit(solution)/shard_map/ppermute | solution.py:457
  43.2 1.1 %collective-permute-start.9 = (f32[2,128]{1,0:T(2,128)S(1)}, f32[2,128]{1,0:T(2,128)S(1)}, u32[]{:S(2)}, u32[]{:S(2)}) collective-permute-start(f32[2,128]{1,0:T(2,128)S(1)} %get-tuple-element.143), channel_id=1, source_target_pairs={{0,4},{4,0},{8,12},{12,8},{16,20},{20,16},{24,28},{28,24},{1,5},{5... | collective-permute-start | bytes 3080 | tf_op jit(solution)/shard_map/ppermute | solution.py:438
  44.4 3.6 %collective-permute-start.10 = (f32[2,128]{1,0:T(2,128)S(1)}, f32[2,128]{1,0:T(2,128)S(1)}, u32[]{:S(2)}, u32[]{:S(2)}) collective-permute-start(f32[2,128]{1,0:T(2,128)S(1)} %add.33), channel_id=1, source_target_pairs={{0,8},{4,12},{8,0},{12,4},{16,24},{20,28},{24,16},{28,20},{1,9},{5... | collective-permute-start | bytes 3080 | tf_op jit(solution)/shard_map/ppermute | solution.py:438
  47.9 3.6 %collective-permute-start.11 = (f32[2,128]{1,0:T(2,128)S(1)}, f32[2,128]{1,0:T(2,128)S(1)}, u32[]{:S(2)}, u32[]{:S(2)}) collective-permute-start(f32[2,128]{1,0:T(2,128)S(1)} %add.34), channel_id=1, source_target_pairs={{0,16},{4,20},{8,24},{12,28},{16,0},{20,4},{24,8},{28,12},{1,17},{... | collective-permute-start | bytes 3080 | tf_op jit(solution)/shard_map/ppermute | solution.py:438
  53.3 8.4 %collective-permute-start.12 = (bf16[528,128]{1,0:T(8,128)(2,1)S(1)}, bf16[528,128]{1,0:T(8,128)(2,1)S(1)}, u32[]{:S(2)}, u32[]{:S(2)}) collective-permute-start(bf16[528,128]{1,0:T(8,128)(2,1)S(1)} %join_parts.1.refs_0_), channel_id=1, source_target_pairs={{0,1},{1,2},{2,3},{3,0},{4,5},{5,6},{6,7},{7,4},{8,9},{9,10},{10,1... | collective-permute-start | bytes 405512 | tf_op jit(solution)/shard_map/ppermute | solution.py:457
  53.4 11.4 %collective-permute-start.13 = (bf16[528,128]{1,0:T(8,128)(2,1)S(1)}, bf16[528,128]{1,0:T(8,128)(2,1)S(1)}, u32[]{:S(2)}, u32[]{:S(2)}) collective-permute-start(bf16[528,128]{1,0:T(8,128)(2,1)S(1)} %join_parts.1.refs_0_), channel_id=1, source_target_pairs={{0,2},{1,3},{2,0},{3,1},{4,6},{5,7},{6,4},{7,5},{8,10},{9,11},{10,... | collective-permute-start | bytes 405512 | tf_op jit(solution)/shard_map/ppermute | solution.py:457
  56.2 8.6 %collective-permute-start.14 = (bf16[528,128]{1,0:T(8,128)(2,1)S(1)}, bf16[528,128]{1,0:T(8,128)(2,1)S(1)}, u32[]{:S(2)}, u32[]{:S(2)}) collective-permute-start(bf16[528,128]{1,0:T(8,128)(2,1)S(1)} %join_parts.1.refs_0_), channel_id=1, source_target_pairs={{0,3},{1,0},{2,1},{3,2},{4,7},{5,4},{6,5},{7,6},{8,11},{9,8},{10,9... | collective-permute-start | bytes 405512 | tf_op jit(solution)/shard_map/ppermute | solution.py:457

commit v8 on v5

v8 whole, which is shorter than its diff:
```python
import functools

import jax
import jax.numpy as jnp
from jax import lax
from jax.experimental import pallas as pl
from jax.experimental.pallas import tpu as pltpu
from jax.sharding import PartitionSpec as P

HD = 128
EPS = 1e-06
LOG2E = 1.4426950408889634
BF = jnp.bfloat16
F32 = jnp.float32


def dot_nn(a, b):
    return lax.dot_general(a, b, (((1,), (0,)), ((), ())), preferred_element_type=F32)


def dot_nt(a, b):
    return lax.dot_general(a, b, (((1,), (1,)), ((), ())), preferred_element_type=F32)


VMEM = pl.BlockSpec(memory_space=pltpu.VMEM)
SMEM = pl.BlockSpec(memory_space=pltpu.SMEM)
HBM = pl.BlockSpec(memory_space=pltpu.HBM)


SHORT = pl.CostEstimate(flops=0, bytes_accessed=0, transcendentals=0)


def params(mib):
    return pltpu.CompilerParams(vmem_limit_bytes=mib * 2**20)


def cut_kernel(cache_ref, out_ref, sems):
    copies = []
    for i in range(out_ref.shape[0]):
        src = cache_ref.at[:, :, i * HD : (i + 1) * HD]
        copy = pltpu.make_async_copy(src, out_ref.at[i], sems.at[i])
        copy.start()
        copies.append(copy)
    for copy in copies:
        copy.wait()


def cut(cache, count):
    depth, rows, _ = cache.shape
    return pl.pallas_call(
        cut_kernel,
        out_shape=jax.ShapeDtypeStruct((count, depth, rows, HD), BF),
        in_specs=[HBM],
        out_specs=VMEM,
        scratch_shapes=[pltpu.SemaphoreType.DMA((count,))],
        compiler_params=params(4),
        name="cut_prompt",
    )(cache)


def prepare_kernel(count, share, rows, width, meta, q_in, g_in, k_in, v_in, gain_ref, kg_ref, *rest):
    outs, (q_buf, g_buf, k_buf, v_buf, sems) = rest[:-5], rest[-5:]
    live_len = meta[count]
    scale = HD ** (-0.5)
    wide = share * HD
    copies = []
    for s in range(count):
        group = []
        for j, (src, buf, size) in enumerate(
            ((q_in, q_buf, wide), (k_in, k_buf, HD), (g_in, g_buf, wide), (v_in, v_buf, HD))
        ):
            src = src.at[:, pl.ds(pl.multiple_of(meta[s] * size, size), size)]
            copy = pltpu.make_async_copy(src, buf.at[s], sems.at[s, j])
            copy.start()
            group.append(copy)
        copies.append(group)
    q_gain = gain_ref[...]
    k_gain = kg_ref[...]
    for s in range(count):
        low_ref, high_ref, key_ref = outs[s * 3 : (s + 1) * 3]
        for copy in copies[s]:
            copy.wait()
        q_t = jnp.concatenate([q_buf[s, :, i * HD : (i + 1) * HD] for i in range(share)], axis=0).T
        g_t = jnp.concatenate([g_buf[s, :, i * HD : (i + 1) * HD] for i in range(share)], axis=0).T
        low_ref[:HD, :] = q_t
        raw_k = k_buf[s].astype(F32)
        k_inv = lax.rsqrt(jnp.mean(raw_k * raw_k, axis=-1, keepdims=True) + EPS)
        k_unit = raw_k * k_inv
        k_hat = (k_unit * k_gain).astype(BF)
        key_ref[:, :HD] = k_unit
        key_ref[:, HD : 2 * HD] = jnp.broadcast_to(k_inv, (rows, HD))
        key_ref[:, 2 * HD :] = k_hat.astype(F32)
        r_val = v_buf[s]
        r_val_t = r_val.T
        for start in range(0, share * rows, width):
            cols = slice(start, start + width)
            token = (lax.broadcasted_iota(jnp.int32, (1, width), 1) + start) % rows
            raw_q = q_t[:, cols].astype(F32)
            q_inv = lax.rsqrt(jnp.mean(raw_q * raw_q, axis=0, keepdims=True) + EPS)
            q_hat = (raw_q * q_inv * q_gain).astype(BF)
            d_o = jnp.where(token < live_len, g_t[:, cols].astype(F32), 0.0).astype(BF)
            low_ref[HD : 2 * HD, cols] = d_o
            causal = lax.broadcasted_iota(jnp.int32, (rows, width), 0) <= token
            e_r = jnp.where(causal, jnp.exp2(dot_nn(k_hat, q_hat) * (scale * LOG2E)), 0.0)
            eb_r = e_r.astype(BF)
            low_ref[2 * HD :, cols] = eb_r
            high_ref[:HD, cols] = dot_nn(r_val_t, eb_r)
            high_ref[HD : HD + rows, cols] = dot_nn(r_val, d_o)
            high_ref[HD + rows : HD + rows + 1, cols] = q_inv
            high_ref[HD + rows + 1 : HD + rows + 2, cols] = jnp.sum(e_r, axis=0, keepdims=True)


def prepare(count, meta, q, g, k, v, q_gain, k_gain):
    rows, q_width = q.shape
    share = q_width // k.shape[1]
    total = share * rows
    each = [
        jax.ShapeDtypeStruct((2 * HD + rows, total), BF),
        jax.ShapeDtypeStruct((HD + rows + 8, total), F32),
        jax.ShapeDtypeStruct((rows, 3 * HD), F32),
    ]
    outs = pl.pallas_call(
        functools.partial(prepare_kernel, count, share, rows, 2 * HD),
        out_shape=each * count,
        in_specs=[SMEM] + [HBM] * 4 + [VMEM] * 2,
        out_specs=[VMEM] * (3 * count),
        scratch_shapes=[
            pltpu.VMEM((count, rows, share * HD), BF),
            pltpu.VMEM((count, rows, share * HD), BF),
            pltpu.VMEM((count, rows, HD), BF),
            pltpu.VMEM((count, rows, HD), BF),
            pltpu.SemaphoreType.DMA((count, 4)),
        ],
        compiler_params=params(16),
        cost_estimate=SHORT,
        name="prepare_response",
    )(meta, q, g, k, v, q_gain, k_gain)
    return [list(outs[s * 3 : (s + 1) * 3]) for s in range(count)]


def attend(width, prompt, low_ref, high_ref, key_ref, q_gain, part_ref, store_ref):
    rows = key_ref.shape[0]
    scale = HD ** (-0.5)
    p_key, p_val = prompt
    k_hat_t = key_ref[:, 2 * HD :].astype(BF).T
    p_key_t = p_key.T
    p_val_t = p_val.T
    sums = None
    for start in range(0, low_ref.shape[1], width):
        cols = slice(start, start + width)
        q_inv = high_ref[HD + rows : HD + rows + 1, cols]
        q_unit = low_ref[:HD, cols].astype(F32) * q_inv
        q_hat = (q_unit * q_gain).astype(BF)
        d_ob = low_ref[HD : 2 * HD, cols]
        d_o = d_ob.astype(F32)
        e_p = jnp.exp2(dot_nn(p_key, q_hat) * (scale * LOG2E))
        row_sum = jnp.sum(e_p, axis=0, keepdims=True) + high_ref[HD + rows + 1 : HD + rows + 2, cols]
        inv_sum = 1.0 / row_sum
        eb_p = e_p.astype(BF)
        eb_r = low_ref[2 * HD :, cols]
        out = (dot_nn(p_val_t, eb_p) + high_ref[:HD, cols]) * inv_sum
        delta = jnp.sum(d_o * out, axis=0, keepdims=True)
        ds_p = (e_p * (dot_nn(p_val, d_ob) - delta)).astype(BF)
        ds_r = (eb_r.astype(F32) * (high_ref[HD : HD + rows, cols] - delta)).astype(BF)
        weight = inv_sum * scale
        q_w = (q_hat.astype(F32) * weight).astype(BF)
        d_ow = (d_o * inv_sum).astype(BF)
        d_qhat = (dot_nn(p_key_t, ds_p) + dot_nn(k_hat_t, ds_r)) * weight
        store_ref[:HD, cols] = d_qhat
        store_ref[HD : 2 * HD, cols] = out
        store_ref[2 * HD : 3 * HD, cols] = q_unit
        store_ref[3 * HD : 3 * HD + 1, cols] = q_inv
        terms = (
            dot_nt(ds_p, q_w),
            dot_nt(eb_p, d_ow),
            dot_nt(ds_r, q_w),
            dot_nt(eb_r, d_ow),
            d_qhat * q_unit,
        )
        sums = terms if sums is None else [a + b for a, b in zip(sums, terms)]
    d_kp, d_vp, d_kr, d_vr, q_term = sums
    part_ref[0] = d_kp.astype(BF)
    part_ref[1] = d_vp.astype(BF)
    base = 3 * HD + 8
    store_ref[base:, :HD] = d_kr
    store_ref[base:, HD : 2 * HD] = d_vr
    store_ref[base:, 2 * HD : 4 * HD] = key_ref[:, : 2 * HD]
    folded = q_term[:, :HD]
    for start in range(HD, width, HD):
        folded = folded + q_term[:, start : start + HD]
    return (
        jnp.sum(folded.T, axis=0, keepdims=True),
        jnp.sum(d_kr * key_ref[:, :HD], axis=0, keepdims=True),
    )


def own_kernel(width, prompt_ref, low_ref, high_ref, key_ref, gain_ref, part_ref, gacc_ref, store_ref):
    prompt = (prompt_ref[0], prompt_ref[1])
    q_term, k_term = attend(width, prompt, low_ref, high_ref, key_ref, gain_ref[...], part_ref, store_ref)
    gacc_ref[0:1, :] = q_term
    gacc_ref[1:2, :] = k_term


def others_kernel(slots, width, meta, prompts_ref, own_ref, gain_ref, acc_ref, *rest):
    count = len(slots)
    kept, (parts_ref, gacc_ref), stores = rest[: 3 * count], rest[3 * count : 3 * count + 2], rest[3 * count + 2 :]
    if len(slots) < parts_ref.shape[0]:
        parts_ref[meta[0]] = own_ref[...]
    q_gain = gain_ref[...]
    q_sum, k_sum = acc_ref[0:1, :], acc_ref[1:2, :]
    for i, s in enumerate(slots):
        head = meta[s]
        prompt = (prompts_ref[head, 0], prompts_ref[head, 1])
        low_ref, high_ref, key_ref = kept[3 * i : 3 * i + 3]
        q_term, k_term = attend(
            width, prompt, low_ref, high_ref, key_ref, q_gain, parts_ref.at[head], stores[i]
        )
        q_sum, k_sum = q_sum + q_term, k_sum + k_term
    gacc_ref[0:1, :] = q_sum
    gacc_ref[1:2, :] = k_sum


def store_shape(kept):
    return jax.ShapeDtypeStruct((3 * HD + 8 + kept[2].shape[0], kept[0].shape[1]), F32)


def own_head(prompt, kept, q_gain):
    return pl.pallas_call(
        functools.partial(own_kernel, 2 * HD),
        out_shape=[
            jax.ShapeDtypeStruct(prompt.shape, BF),
            jax.ShapeDtypeStruct((2, HD), F32),
            store_shape(kept),
        ],
        in_specs=[VMEM] * 5,
        out_specs=[VMEM] * 3,
        compiler_params=params(16),
        name="attend_own_head",
    )(prompt, *kept, q_gain)


def other_heads(slots, meta, prompts, own, kept, q_gain, acc):
    outs = pl.pallas_call(
        functools.partial(others_kernel, slots, 2 * HD),
        out_shape=[jax.ShapeDtypeStruct(prompts.shape, BF), jax.ShapeDtypeStruct((2, HD), F32)]
        + [store_shape(kept[s]) for s in slots],
        in_specs=[SMEM] + [VMEM] * (4 + 3 * len(slots)),
        out_specs=[VMEM] * (2 + len(slots)),
        compiler_params=params(16),
        name="attend_other_heads",
    )(meta, prompts, own, q_gain, acc, *[x for s in slots for x in kept[s]])
    return outs[0], outs[1], list(outs[2:])


def settle_kernel(count, rows, width, meta, gain_ref, kg_ref, *rest):
    stores = rest[:count]
    outs, bufs, sems = rest[-9:-5], rest[-5:-1], rest[-1]
    live_len = meta[count]
    q_gain = gain_ref[...]
    k_gain = kg_ref[...]
    base = 3 * HD + 8
    copies = []
    for s, store_ref in enumerate(stores):
        head = meta[s]
        a_buf, q_buf, k_buf, v_buf = [buf.at[s] for buf in bufs]
        total = store_ref.shape[1]
        share = total // rows

        def send(j, buf):
            size = buf.shape[1]
            out = outs[j].at[:, pl.ds(pl.multiple_of(head * size, size), size)]
            copy = pltpu.make_async_copy(buf, out, sems.at[s, j])
            copy.start()
            copies.append(copy)

        att = store_ref[HD : 2 * HD, :].astype(BF).T
        live = lax.broadcasted_iota(jnp.int32, (rows, HD), 0) < live_len
        for i in range(share):
            block = att[i * rows : (i + 1) * rows, :].astype(F32)
            a_buf[:, i * HD : (i + 1) * HD] = jnp.where(live, block, 0.0).astype(BF)
        send(0, a_buf)
        v_buf[...] = store_ref[base:, HD : 2 * HD].astype(BF)
        send(3, v_buf)
        k_unit = store_ref[base:, 2 * HD : 3 * HD]
        k_inv = store_ref[base:, 3 * HD : 4 * HD]
        up_k = store_ref[base:, :HD] * k_gain
        mean_k = jnp.mean(up_k * k_unit, axis=-1, keepdims=True)
        k_buf[...] = (k_inv * (up_k - k_unit * mean_k)).astype(BF)
        send(2, k_buf)
        parts = []
        for start in range(0, total, width):
            cols = slice(start, start + width)
            q_unit = store_ref[2 * HD : 3 * HD, cols]
            up = store_ref[:HD, cols] * q_gain
            mean = jnp.mean(up * q_unit, axis=0, keepdims=True)
            parts.append((store_ref[3 * HD : 3 * HD + 1, cols] * (up - q_unit * mean)).astype(BF))
        d_q = jnp.concatenate(parts, axis=1).T
        for i in range(share):
            q_buf[:, i * HD : (i + 1) * HD] = d_q[i * rows : (i + 1) * rows, :]
        send(1, q_buf)
    for copy in copies:
        copy.wait()


def settle(meta, q_gain, k_gain, stores, q_width, k_width):
    total = stores[0].shape[1]
    rows = stores[0].shape[0] - 3 * HD - 8
    count = len(stores)
    wide = total // rows * HD
    return pl.pallas_call(
        functools.partial(settle_kernel, count, rows, 2 * HD),
        out_shape=[jax.ShapeDtypeStruct((rows, w), BF) for w in (q_width, q_width, k_width, k_width)],
        in_specs=[SMEM] + [VMEM] * (2 + count),
        out_specs=[HBM] * 4,
        scratch_shapes=[pltpu.VMEM((count, rows, w), BF) for w in (wide, wide, HD, HD)]
        + [pltpu.SemaphoreType.DMA((count, 4))],
        compiler_params=params(16),
        name="settle_heads",
    )(meta, q_gain, k_gain, *stores)


TAIL = 16


def join_kernel(got_ref, gains_ref, out_ref):
    count, depth, rows, _ = got_ref.shape
    for d in range(depth):
        total = got_ref[0, d].astype(F32)
        for j in range(1, count):
            total = total + got_ref[j, d].astype(F32)
        total = total.astype(BF)
        for j in range(count):
            out_ref[j, d * rows : (d + 1) * rows, :] = total
    gains = gains_ref[...]
    high = gains.astype(BF)
    gains = gains - high.astype(F32)
    middle = gains.astype(BF)
    low = (gains - middle.astype(F32)).astype(BF)
    pieces = jnp.concatenate([p.astype(F32) for p in (high, middle, low)], axis=0)
    pad = jnp.zeros((TAIL - pieces.shape[0], HD), F32)
    tail = jnp.concatenate([pieces, pad], axis=0).astype(BF)
    for j in range(count):
        out_ref[j, depth * rows :, :] = tail


def join(got, gains):
    count, depth, rows, _ = got.shape
    return pl.pallas_call(
        join_kernel,
        out_shape=jax.ShapeDtypeStruct((count, depth * rows + TAIL, HD), BF),
        in_specs=[VMEM] * 2,
        out_specs=VMEM,
        compiler_params=params(8),
        name="join_parts",
    )(got, gains)


def place_kernel(mine, in_ref, out_ref, gain_ref):
    depth, rows, _ = out_ref.shape
    total = jnp.zeros(gain_ref.shape, F32)
    for i in range(in_ref.shape[0]):
        for d in range(depth):
            block = in_ref[i, d * rows : (d + 1) * rows, :]
            out_ref[d, :, i * HD : (i + 1) * HD] = jnp.where(mine[0] > 0, block, jnp.zeros_like(block))
        tail = in_ref[i, depth * rows :, :].astype(F32)
        total = total + (tail[0:2] + tail[2:4] + tail[4:6])
    gain_ref[...] = total


def place(mine, payloads, depth, rows):
    count = payloads.shape[0]
    return pl.pallas_call(
        place_kernel,
        out_shape=[
            jax.ShapeDtypeStruct((depth, rows, HD * count), BF),
            jax.ShapeDtypeStruct((2, HD), F32),
        ],
        in_specs=[SMEM, VMEM],
        out_specs=[VMEM, VMEM],
        compiler_params=params(8),
        name="place_prompt_grad",
    )(mine, payloads)


def after(x, *others):
    return lax.optimization_barrier((x,) + others)[0]


def pair_sum(value, axis, size):
    step = 1
    while step < size:
        value = value + lax.ppermute(value, axis, [(i, i ^ step) for i in range(size)])
        step *= 2
    return value


def local(
    n_dp, n_group, queries, resp_keys, resp_values, prompt_cache, owners, lengths, q_gain, k_gain, grad_out
):
    q, g = queries[0, 0], grad_out[0, 0]
    k, v = resp_keys[0, 0], resp_values[0, 0]
    cache = prompt_cache[0, 0]
    owner = owners[0]
    live_len = lengths[0, 0]
    me = lax.axis_index("group")
    kv_heads = k.shape[1] // HD
    depth, p_rows, _ = cache.shape
    q, g, k, v = [pltpu.with_memory_space_constraint(x, pltpu.HBM) for x in (q, g, k, v)]
    gain_col = q_gain[:, None]
    gain_row = k_gain[None, :]
    direct = n_group == kv_heads
    mine_flag = (me == owner).astype(jnp.int32)
    slots = tuple(range(kv_heads))
    order = jnp.arange(kv_heads, dtype=jnp.int32)
    if direct:
        order = (order + me) % kv_heads
    meta = jnp.concatenate([order, live_len[None]])
    kept = prepare(kv_heads, meta, q, g, k, v, gain_col, gain_row)

    def exchange(blocks):
        return lax.all_to_all(blocks, "group", 0, 0)

    if direct:
        blocks = cut(pltpu.with_memory_space_constraint(cache, pltpu.HBM), kv_heads)
        got = exchange(blocks)
        got = after(got, kept[0][1])
        mine = lax.dynamic_index_in_dim(got, owner, 0, keepdims=False)
        prompts = exchange(jnp.broadcast_to(mine[None], got.shape))
        own, acc, store = own_head(mine, kept[0], gain_col)
        prompts = after(prompts, own)
        parts, acc, stores = other_heads(slots[1:], meta, prompts, own, kept, gain_col, acc)
        attended, d_query, d_key, d_value = settle(
            meta, gain_col, gain_row, [store] + stores, q.shape[1], k.shape[1]
        )
        gains = pair_sum(acc, "dp", n_dp)
        back = after(exchange(parts), d_key)
        payloads = exchange(join(back, gains))
        placed, gains = place(mine_flag[None], payloads, depth, p_rows)
    else:
        cache = lax.psum(jnp.where(me == owner, cache, jnp.zeros_like(cache)), "group")
        prompts = cut(cache, kv_heads)
        acc = jnp.zeros((2, HD), F32)
        parts, acc, stores = other_heads(slots, meta, prompts, prompts[0], kept, gain_col, acc)
        attended, d_query, d_key, d_value = settle(
            meta, gain_col, gain_row, stores, q.shape[1], k.shape[1]
        )
        total = jnp.transpose(parts, (1, 2, 0, 3)).reshape(depth, p_rows, kv_heads * HD)
        total = lax.psum(total.astype(F32), "group").astype(BF)
        placed = jnp.where(mine_flag > 0, total, jnp.zeros((), BF))
        gains = pair_sum(pair_sum(acc, "group", n_group), "dp", n_dp)
    return (
        attended[None, None],
        d_query[None, None],
        d_key[None, None],
        d_value[None, None],
        placed[None, None],
        gains,
    )


def solution(mesh):
    in_specs = (
        P("dp", "group", None, None),
        P("dp", "group", None, None),
        P("dp", "group", None, None),
        P("dp", "group", None, None, None),
        P("dp"),
        P("dp", "group"),
        P(),
        P(),
        P("dp", "group", None, None),
    )
    out_specs = (
        P("dp", "group", None, None),
        P("dp", "group", None, None),
        P("dp", "group", None, None),
        P("dp", "group", None, None),
        P("dp", "group", None, None, None),
        P(),
    )
    body = functools.partial(local, mesh.shape["dp"], mesh.shape["group"])
    return jax.shard_map(body, mesh=mesh, in_specs=in_specs, out_specs=out_specs, check_vma=False)
```

time: 101 us -> 103 us (1.020)
  starting transfers between devices: 51.6 us -> 22.3 us
  local copies, waits for them, and re-layouts: 4.14 us -> 32.9 us
  waiting for transfers between devices: 18.6 us -> 26.3 us
  Pallas kernels: 22.2 us -> 18 us
  other arithmetic: 1.18 us -> 0.1 us
    ppermute x26 -> x0, starting transfers between devices: 48.5 us -> none  [the longest x8 26.6 us: inward(): return lax.ppermute(x, 'group', [(0, 1), (3, 2)])]
    unnamed x8 -> x66, local copies, waits for them, and re-layouts: 3.37 us -> 30.9 us
    all_to_all x0 -> x4, waiting for transfers between devices: none -> 23.1 us  [exchange(): return lax.all_to_all(blocks, 'group', 0, 0)]
    all_to_all x0 -> x4, starting transfers between devices: none -> 19.2 us  [exchange(): return lax.all_to_all(blocks, 'group', 0, 0)]
    ppermute x26 -> x0, waiting for transfers between devices: 15.4 us -> none  [the longest x8 12.2 us: outward(): return lax.ppermute(x, 'group', [(1, 0), (2, 3)])]
    pallas_call x10 -> x7, Pallas kernels: 22.2 us -> 18 us  [the longest x1 5.14 us: prepare(): pl.pallas_call(functools.partial(prepare_kernel, count, share, rows, 2 *...]
  transfers between devices with their start and end apart: 29 -> 7, of which waited for: 7 -> 5; matrix products, arithmetic and copies ran while one was open for 2% -> 0% of each run, Pallas kernels for 20% -> 9%
where the time goes in v8:
time: 103 us; the launch traced here: 102 us
  local copies, waits for them, and re-layouts  32.9 us (32%)
  waiting for transfers between devices  26.3 us (26%)
  starting transfers between devices  22.3 us (22%)
  Pallas kernels  18 us (17%)
  between operations  2.09 us (2%)
    unnamed x66, local copies, waits for them, and re-layouts  30.9 us
    all_to_all x4, waiting for transfers between devices, exchange(): return lax.all_to_all(blocks, 'group', 0, 0)  23.1 us
    all_to_all x4, starting transfers between devices, exchange(): return lax.all_to_all(blocks, 'group', 0, 0)  19.2 us
    pallas_call x1, Pallas kernels, prepare(): pl.pallas_call(functools.partial(prepare_kernel, count, share, rows, 2 *...  5.14 us
    pallas_call x1, Pallas kernels, other_heads(): pl.pallas_call(functools.partial(others_kernel, slots, 2 * HD), out_shape...  4.95 us
    ppermute x3, waiting for transfers between devices, pair_sum(): lax.ppermute(value, axis, [(i, i ^ step) for i in range(size)])  3.21 us
    ppermute x3, starting transfers between devices, pair_sum(): lax.ppermute(value, axis, [(i, i ^ step) for i in range(size)])  3.08 us
    pallas_call x1, Pallas kernels, settle(): pl.pallas_call(functools.partial(settle_kernel, count, rows, 2 * HD), out...  2.46 us
  transfers between devices with their start and end apart: 7, of which 5 were waited for; matrix products, arithmetic and copies ran while one was open for 0% of the time, Pallas kernels for 9%

profile of v8, /device:TPU:0, one launch (start us, length us, event | category | flops | bytes accessed | tf_op | source)
XLA Modules:
  0.0 101.6 jit_solution(9424651909518584924)
XLA Ops:
  0.6 0.0 copy-start.32
  0.6 0.0 copy-start.31
  0.7 1.9 %cut_prompt.1 = bf16[4,2,256,128]{3,2,1,0:T(8,128)(2,1)} custom-call(bf16[2,256,512]{2,1,0:T(8,128)(2,1)} %bitcast.26), custom_call_target="tpu_custom_call" | custom-call | tf_op jit(solution)/shard_map/cut_prompt/pallas_call | solution.py:50
  2.6 6.3 %all-to-all-start = ((bf16[4,2,256,128]{3,2,1,0:T(8,128)(2,1)}), bf16[4,2,256,128]{3,2,1,0:T(8,128)(2,1)}, u32[]{:S(2)}, u32[]{:S(2)}) async-start(bf16[4,2,256,128]{3,2,1,0:T(8,128)(2,1)} %cut_prompt.1), calls=%async_computation | async-start | bytes 1048576 | tf_op jit(solution)/shard_map/all_to_all | solution.py:421
  10.2 0.0 copy-done.32
  10.2 0.1 copy.18.gain_ref
  10.4 0.1 pad_add_fusion.meta
  10.5 0.0 copy-done.31
  10.5 5.1 %prepare_response.1 = (bf16[448,768]{1,0:T(8,128)(2,1)S(1)}, f32[328,768]{1,0:T(8,128)S(1)}, f32[192,384]{1,0:T(8,128)S(1)}, bf16[448,768]{1,0:T(8,128)(2,1)S(1)...) custom-call(s32[5]{0:T(128)S(1)} %pad_add_fusion.meta, ...), custom_call_target="tpu_custom_call" | custom-call | tf_op jit(solution)/shard_map/prepare_response/pallas_call | solution.py:122
  15.6 0.0 copy-start.6
  15.6 1.0 copy-done.6
  16.6 0.0 copy-start.8
  16.6 1.0 copy-done.8
  17.6 1.0 copy-done.10
  18.5 0.8 copy-done.12
  19.4 0.8 copy-done.14
  20.2 0.9 copy-done.16
  21.1 0.8 copy-done.18
  22.0 0.7 copy-done.21
  22.7 0.7 copy-done.23
  23.4 0.7 copy-done.25
  24.1 0.0 all-to-all-done
  24.1 1.0 %dynamic-slice_bitcast_fusion.prompt_ref = bf16[2,256,128]{2,1,0:T(8,128)(2,1)S(1)} fusion(bf16[4,2,256,128]{3,2,1,0:T(8,128)(2,1)} %all-to-all-done, s32[]{:T(128)S(6)} %select_n.12), kind=kLoop, calls=%fused_computation | loop fusion | bytes 262148 | tf_op jit(solution)/shard_map/jit(dynamic_index_in_dim)/squeeze | solution.py:427
  25.2 0.9 broadcast_in_dim.34
  26.0 0.0 copy-done.27
  26.0 5.1 %all-to-all-start.1 = ((bf16[4,2,256,128]{3,2,1,0:T(8,128)(2,1)}), bf16[4,2,256,128]{3,2,1,0:T(8,128)(2,1)S(1)}, u32[]{:S(2)}, u32[]{:S(2)}) async-start(bf16[4,2,256,128]{3,2,1,0:T(8,128)(2,1)} %broadcast_in_dim.34), calls=%async_computation.1 | async-start | bytes 1048576 | tf_op jit(solution)/shard_map/all_to_all | solution.py:421
  31.1 1.2 %copy-done.11 = f32[328,768]{1,0:T(8,128)S(1)} copy-done((f32[328,768]{1,0:T(8,128)S(1)}, f32[328,768]{1,0:T(8,128)}, u32[]{:S(2)}) %copy-start.11) | copy-done | bytes 1007640
  32.3 1.1 %copy-done.19 = bf16[448,768]{1,0:T(8,128)(2,1)S(1)} copy-done((bf16[448,768]{1,0:T(8,128)(2,1)S(1)}, bf16[448,768]{1,0:T(8,128)(2,1)}, u32[]{:S(2)}) %copy-start.19) | copy-done | bytes 688152
  33.4 1.0 copy-done.28
  34.4 1.7 %attend_own_head.1 = (bf16[2,256,128]{2,1,0:T(8,128)(2,1)S(1)}, f32[2,128]{1,0:T(2,128)S(1)}, f32[584,768]{1,0:T(8,128)S(1)}) custom-call(bf16[2,256,128]{2,1,0:T(8,128)(2,1)S(1)} %dynamic-slice_bitcast_fusion.prompt_ref, bf16[448,768]{1,0:T(8,128)(2,1)S(1)} %copy-done.19, f32[328,768]{1,0:T(8,128)S(1)} %copy-done.11, f32[192,384]{1,0:T(8,128)S(1)} %copy-done.28, ...), custom_call_target="tpu_custom_call" | custom-call | tf_op jit(solution)/shard_map/attend_own_head/pallas_call | solution.py:228
  36.1 0.0 copy-start.29
  36.1 0.6 copy-done.29
  36.7 8.3 %all-to-all-done.1.prompts_ref = bf16[4,2,256,128]{3,2,1,0:T(8,128)(2,1)S(1)} async-done(((bf16[4,2,256,128]{3,2,1,0:T(8,128)(2,1)}), bf16[4,2,256,128]{3,2,1,0:T(8,128)(2,1)S(1)}, u32[]{:S(2)}, u32[]{:S(2)}) %all-to-all-start.1) | async-done | bytes 524320 | tf_op jit(solution)/shard_map/all_to_all | solution.py:421
  45.0 1.2 %copy-done.7 = f32[328,768]{1,0:T(8,128)S(1)} copy-done((f32[328,768]{1,0:T(8,128)S(1)}, f32[328,768]{1,0:T(8,128)}, u32[]{:S(2)}) %copy-start.7) | copy-done | bytes 1007640
  46.3 1.2 %copy-done.9 = f32[328,768]{1,0:T(8,128)S(1)} copy-done((f32[328,768]{1,0:T(8,128)S(1)}, f32[328,768]{1,0:T(8,128)}, u32[]{:S(2)}) %copy-start.9) | copy-done | bytes 1007640
  47.5 1.1 %copy-done.13 = bf16[448,768]{1,0:T(8,128)(2,1)S(1)} copy-done((bf16[448,768]{1,0:T(8,128)(2,1)S(1)}, bf16[448,768]{1,0:T(8,128)(2,1)}, u32[]{:S(2)}) %copy-start.13) | copy-done | bytes 688152
  48.6 1.1 %copy-done.15 = bf16[448,768]{1,0:T(8,128)(2,1)S(1)} copy-done((bf16[448,768]{1,0:T(8,128)(2,1)S(1)}, bf16[448,768]{1,0:T(8,128)(2,1)}, u32[]{:S(2)}) %copy-start.15) | copy-done | bytes 688152
  49.7 1.1 %copy-done.17 = bf16[448,768]{1,0:T(8,128)(2,1)S(1)} copy-done((bf16[448,768]{1,0:T(8,128)(2,1)S(1)}, bf16[448,768]{1,0:T(8,128)(2,1)}, u32[]{:S(2)}) %copy-start.17) | copy-done | bytes 688152
  50.8 1.0 copy-done.22
  51.7 1.0 copy-done.24
  52.7 1.0 copy-done.26
  53.7 0.9 copy-done.30
  54.6 5.0 %attend_other_heads.1 = (bf16[4,2,256,128]{3,2,1,0:T(8,128)(2,1)S(1)}, f32[2,128]{1,0:T(2,128)S(1)}, f32[584,768]{1,0:T(8,128)S(1)}, f32[584,768]{1,0:T(8,128)S(1)}, f32[584,768]{1,0:T(8,128)S(1)}) custom-call(s32[5]{0:T(128)S(1)} %pad_add_fusion.meta, bf16[4,2,256,128]{3,2,1,0:T(8,128)(2,1)S(1)} %all-to-all-done.1.prompts_ref, ...), custom_call_target="tpu_custom_call" | custom-call | tf_op jit(solution)/shard_map/attend_other_heads/pallas_call | solution.py:243
  59.5 0.0 copy-start
  59.5 1.3 %copy-done = f32[584,768]{1,0:T(8,128)} copy-done((f32[584,768]{1,0:T(8,128)}, f32[584,768]{1,0:T(8,128)S(1)}, u32[]{:S(2)}) %copy-start) | copy-done | bytes 1794072
  60.8 1.2 %copy-done.2 = f32[584,768]{1,0:T(8,128)} copy-done((f32[584,768]{1,0:T(8,128)}, f32[584,768]{1,0:T(8,128)S(1)}, u32[]{:S(2)}) %copy-start.2) | copy-done | bytes 1794072
  62.0 1.3 %copy-done.4 = f32[584,768]{1,0:T(8,128)} copy-done((f32[584,768]{1,0:T(8,128)}, f32[584,768]{1,0:T(8,128)S(1)}, u32[]{:S(2)}) %copy-start.4) | copy-done | bytes 1794072
  63.3 0.8 copy-done.20
  64.1 3.5 %all-to-all-start.2 = ((bf16[4,2,256,128]{3,2,1,0:T(8,128)(2,1)}), bf16[4,2,256,128]{3,2,1,0:T(8,128)(2,1)S(1)}, u32[]{:S(2)}, u32[]{:S(2)}) async-start(bf16[4,2,256,128]{3,2,1,0:T(8,128)(2,1)} %copy-done.20), calls=%async_computation.2 | async-start | bytes 1048576 | tf_op jit(solution)/shard_map/all_to_all | solution.py:421
  67.5 0.1 collective-permute-start
  67.6 1.1 %collective-permute-done = f32[2,128]{1,0:T(2,128)S(1)} collective-permute-done((f32[2,128]{1,0:T(2,128)S(1)}, f32[2,128]{1,0:T(2,128)S(1)}, u32[]{:S(2)}, u32[]{:S(2)}) %collective-permute-start) | collective-permute-done | bytes 1056 | tf_op jit(solution)/shard_map/ppermute | solution.py:392
  68.7 1.5 %collective-permute-start.1 = (f32[2,128]{1,0:T(2,128)S(1)}, f32[2,128]{1,0:T(2,128)S(1)}, u32[]{:S(2)}, u32[]{:S(2)}) collective-permute-start(f32[2,128]{1,0:T(2,128)S(1)} %add.29), channel_id=1, source_target_pairs={{0,8},{4,12},{8,0},{12,4},{16,24},{20,28},{24,16},{28,20},{1,9},{5... | collective-permute-start | bytes 3080 | tf_op jit(solution)/shard_map/ppermute | solution.py:392
  70.2 2.1 %collective-permute-done.1 = f32[2,128]{1,0:T(2,128)S(1)} collective-permute-done((f32[2,128]{1,0:T(2,128)S(1)}, f32[2,128]{1,0:T(2,128)S(1)}, u32[]{:S(2)}, u32[]{:S(2)}) %collective-permute-start.1) | collective-permute-done | bytes 1056 | tf_op jit(solution)/shard_map/ppermute | solution.py:392
  72.3 1.5 %collective-permute-start.2 = (f32[2,128]{1,0:T(2,128)S(1)}, f32[2,128]{1,0:T(2,128)S(1)}, u32[]{:S(2)}, u32[]{:S(2)}) collective-permute-start(f32[2,128]{1,0:T(2,128)S(1)} %add.30), channel_id=1, source_target_pairs={{0,16},{4,20},{8,24},{12,28},{16,0},{20,4},{24,8},{28,12},{1,17},{... | collective-permute-start | bytes 3080 | tf_op jit(solution)/shard_map/ppermute | solution.py:392
  73.8 1.5 %copy-done.1 = f32[584,768]{1,0:T(8,128)S(1)} copy-done((f32[584,768]{1,0:T(8,128)S(1)}, f32[584,768]{1,0:T(8,128)}, u32[]{:S(2)}) %copy-start.1) | copy-done | bytes 1794072
  75.3 1.5 %copy-done.3 = f32[584,768]{1,0:T(8,128)S(1)} copy-done((f32[584,768]{1,0:T(8,128)S(1)}, f32[584,768]{1,0:T(8,128)}, u32[]{:S(2)}) %copy-start.3) | copy-done | bytes 1794072
  76.8 1.5 %copy-done.5 = f32[584,768]{1,0:T(8,128)S(1)} copy-done((f32[584,768]{1,0:T(8,128)S(1)}, f32[584,768]{1,0:T(8,128)}, u32[]{:S(2)}) %copy-start.5) | copy-done | bytes 1794072
  78.3 2.5 %settle_heads.1 = (bf16[192,2048]{1,0:T(8,128)(2,1)}, bf16[192,2048]{1,0:T(8,128)(2,1)}, bf16[192,512]{1,0:T(8,128)(2,1)}, bf16[192,512]{1,0:T(8,128)(2,1)}) custom-call(s32[5]{0:T(128)S(1)} %pad_add_fusion.meta, f32[128,1]{1,0:T(8,128)S(1)} %copy.18.gain_ref, f32[1,128]{1,0:T(1,128)S(1)} %bitcast.23, f32[584,768]{1,0:T(8,128)S(1)} %get-tuple-element.39.rest_0_, ...), custom_call_target="tpu_custom_call" | custom-call | tf_op jit(solution)/shard_map/settle_heads/pallas_call | solution.py:310
  80.8 0.0 collective-permute-done.2
  80.8 0.7 all-to-all-done.2.got_ref
  81.5 0.9 join_parts.1
  82.4 4.3 %all-to-all-start.3 = ((bf16[4,528,128]{2,1,0:T(8,128)(2,1)}), bf16[4,528,128]{2,1,0:T(8,128)(2,1)S(1)}, u32[]{:S(2)}, u32[]{:S(2)}) async-start(bf16[4,528,128]{2,1,0:T(8,128)(2,1)} %join_parts.1), calls=%async_computation.3 | async-start | bytes 1081344 | tf_op jit(solution)/shard_map/all_to_all | solution.py:421
  86.7 14.1 %all-to-all-done.3.in_ref = bf16[4,528,128]{2,1,0:T(8,128)(2,1)S(1)} async-done(((bf16[4,528,128]{2,1,0:T(8,128)(2,1)}), bf16[4,528,128]{2,1,0:T(8,128)(2,1)S(1)}, u32[]{:S(2)}, u32[]{:S(2)}) %all-to-all-start.3) | async-done | bytes 540704 | tf_op jit(solution)/shard_map/all_to_all | solution.py:421
  100.7 0.9 place_prompt_grad.1
  (31 shorter events, 0.1 us)
Async XLA Ops:
  0.6 9.6 %copy-start.32 = (f32[128]{0:T(128)S(1)}, f32[128]{0:T(128)}, u32[]{:S(2)}) copy-start(f32[128]{0:T(128)} %param.15) | copy-start | bytes 1540
  0.6 9.8 %copy-start.31 = (f32[128]{0:T(128)S(1)}, f32[128]{0:T(128)}, u32[]{:S(2)}) copy-start(f32[128]{0:T(128)} %param.16) | copy-start | bytes 1540
  2.6 21.5 %all-to-all-start = ((bf16[4,2,256,128]{3,2,1,0:T(8,128)(2,1)}), bf16[4,2,256,128]{3,2,1,0:T(8,128)(2,1)}, u32[]{:S(2)}, u32[]{:S(2)}) async-start(bf16[4,2,256,128]{3,2,1,0:T(8,128)(2,1)} %cut_prompt.1), calls=%async_computation | async-start | bytes 1048576 | tf_op jit(solution)/shard_map/all_to_all | solution.py:421
  15.6 1.0 copy-start.6
  16.6 1.0 copy-start.8
  17.6 1.0 copy-start.10
  18.5 0.8 copy-start.12
  19.4 0.9 copy-start.14
  20.2 0.9 copy-start.16
  21.1 0.8 copy-start.18
  22.0 0.7 copy-start.21
  22.7 0.7 copy-start.23
  23.4 0.7 copy-start.25
  24.1 1.9 %copy-start.27 = (f32[192,384]{1,0:T(8,128)}, f32[192,384]{1,0:T(8,128)S(1)}, u32[]{:S(2)}) copy-start(f32[192,384]{1,0:T(8,128)S(1)} %get-tuple-element.38.key_ref) | copy-start | bytes 884740
  26.0 19.0 %all-to-all-start.1 = ((bf16[4,2,256,128]{3,2,1,0:T(8,128)(2,1)}), bf16[4,2,256,128]{3,2,1,0:T(8,128)(2,1)S(1)}, u32[]{:S(2)}, u32[]{:S(2)}) async-start(bf16[4,2,256,128]{3,2,1,0:T(8,128)(2,1)} %broadcast_in_dim.34), calls=%async_computation.1 | async-start | bytes 1048576 | tf_op jit(solution)/shard_map/all_to_all | solution.py:421
  31.1 1.2 %copy-start.11 = (f32[328,768]{1,0:T(8,128)S(1)}, f32[328,768]{1,0:T(8,128)}, u32[]{:S(2)}) copy-start(f32[328,768]{1,0:T(8,128)} %copy-done.10) | copy-start | bytes 3022852
  32.3 1.1 %copy-start.19 = (bf16[448,768]{1,0:T(8,128)(2,1)S(1)}, bf16[448,768]{1,0:T(8,128)(2,1)}, u32[]{:S(2)}) copy-start(bf16[448,768]{1,0:T(8,128)(2,1)} %copy-done.18) | copy-start | bytes 2064388
  33.4 1.0 copy-start.28
  36.1 0.7 copy-start.29
  45.0 1.2 %copy-start.7 = (f32[328,768]{1,0:T(8,128)S(1)}, f32[328,768]{1,0:T(8,128)}, u32[]{:S(2)}) copy-start(f32[328,768]{1,0:T(8,128)} %copy-done.6) | copy-start | bytes 3022852
  46.3 1.2 %copy-start.9 = (f32[328,768]{1,0:T(8,128)S(1)}, f32[328,768]{1,0:T(8,128)}, u32[]{:S(2)}) copy-start(f32[328,768]{1,0:T(8,128)} %copy-done.8) | copy-start | bytes 3022852
  47.5 1.1 %copy-start.13 = (bf16[448,768]{1,0:T(8,128)(2,1)S(1)}, bf16[448,768]{1,0:T(8,128)(2,1)}, u32[]{:S(2)}) copy-start(bf16[448,768]{1,0:T(8,128)(2,1)} %copy-done.12) | copy-start | bytes 2064388
  48.6 1.1 %copy-start.15 = (bf16[448,768]{1,0:T(8,128)(2,1)S(1)}, bf16[448,768]{1,0:T(8,128)(2,1)}, u32[]{:S(2)}) copy-start(bf16[448,768]{1,0:T(8,128)(2,1)} %copy-done.14) | copy-start | bytes 2064388
  49.7 1.1 %copy-start.17 = (bf16[448,768]{1,0:T(8,128)(2,1)S(1)}, bf16[448,768]{1,0:T(8,128)(2,1)}, u32[]{:S(2)}) copy-start(bf16[448,768]{1,0:T(8,128)(2,1)} %copy-done.16) | copy-start | bytes 2064388
  50.8 1.0 copy-start.22
  51.7 1.0 copy-start.24
  52.7 1.0 copy-start.26
  53.7 0.9 copy-start.30
  59.5 1.3 %copy-start = (f32[584,768]{1,0:T(8,128)}, f32[584,768]{1,0:T(8,128)S(1)}, u32[]{:S(2)}) copy-start(f32[584,768]{1,0:T(8,128)S(1)} %get-tuple-element.52.rest_1_) | copy-start | bytes 5382148
  60.8 1.2 %copy-start.2 = (f32[584,768]{1,0:T(8,128)}, f32[584,768]{1,0:T(8,128)S(1)}, u32[]{:S(2)}) copy-start(f32[584,768]{1,0:T(8,128)S(1)} %get-tuple-element.53.rest_2_) | copy-start | bytes 5382148
  62.0 1.3 %copy-start.4 = (f32[584,768]{1,0:T(8,128)}, f32[584,768]{1,0:T(8,128)S(1)}, u32[]{:S(2)}) copy-start(f32[584,768]{1,0:T(8,128)S(1)} %get-tuple-element.54.rest_3_) | copy-start | bytes 5382148
  63.3 0.8 copy-start.20
  64.1 17.4 %all-to-all-start.2 = ((bf16[4,2,256,128]{3,2,1,0:T(8,128)(2,1)}), bf16[4,2,256,128]{3,2,1,0:T(8,128)(2,1)S(1)}, u32[]{:S(2)}, u32[]{:S(2)}) async-start(bf16[4,2,256,128]{3,2,1,0:T(8,128)(2,1)} %copy-done.20), calls=%async_computation.2 | async-start | bytes 1048576 | tf_op jit(solution)/shard_map/all_to_all | solution.py:421
  67.5 1.2 %collective-permute-start = (f32[2,128]{1,0:T(2,128)S(1)}, f32[2,128]{1,0:T(2,128)S(1)}, u32[]{:S(2)}, u32[]{:S(2)}) collective-permute-start(f32[2,128]{1,0:T(2,128)S(1)} %get-tuple-element.61), channel_id=1, source_target_pairs={{0,4},{4,0},{8,12},{12,8},{16,20},{20,16},{24,28},{28,24},{1,5},{5... | collective-permute-start | bytes 3080 | tf_op jit(solution)/shard_map/ppermute | solution.py:392
  68.7 3.6 %collective-permute-start.1 = (f32[2,128]{1,0:T(2,128)S(1)}, f32[2,128]{1,0:T(2,128)S(1)}, u32[]{:S(2)}, u32[]{:S(2)}) collective-permute-start(f32[2,128]{1,0:T(2,128)S(1)} %add.29), channel_id=1, source_target_pairs={{0,8},{4,12},{8,0},{12,4},{16,24},{20,28},{24,16},{28,20},{1,9},{5... | collective-permute-start | bytes 3080 | tf_op jit(solution)/shard_map/ppermute | solution.py:392
  72.3 8.4 %collective-permute-start.2 = (f32[2,128]{1,0:T(2,128)S(1)}, f32[2,128]{1,0:T(2,128)S(1)}, u32[]{:S(2)}, u32[]{:S(2)}) collective-permute-start(f32[2,128]{1,0:T(2,128)S(1)} %add.30), channel_id=1, source_target_pairs={{0,16},{4,20},{8,24},{12,28},{16,0},{20,4},{24,8},{28,12},{1,17},{... | collective-permute-start | bytes 3080 | tf_op jit(solution)/shard_map/ppermute | solution.py:392
  73.8 1.5 %copy-start.1 = (f32[584,768]{1,0:T(8,128)S(1)}, f32[584,768]{1,0:T(8,128)}, u32[]{:S(2)}) copy-start(f32[584,768]{1,0:T(8,128)} %copy-done) | copy-start | bytes 5382148
  75.3 1.5 %copy-start.3 = (f32[584,768]{1,0:T(8,128)S(1)}, f32[584,768]{1,0:T(8,128)}, u32[]{:S(2)}) copy-start(f32[584,768]{1,0:T(8,128)} %copy-done.2) | copy-start | bytes 5382148
  76.8 1.5 %copy-start.5 = (f32[584,768]{1,0:T(8,128)S(1)}, f32[584,768]{1,0:T(8,128)}, u32[]{:S(2)}) copy-start(f32[584,768]{1,0:T(8,128)} %copy-done.4) | copy-start | bytes 5382148
  82.4 18.4 %all-to-all-start.3 = ((bf16[4,528,128]{2,1,0:T(8,128)(2,1)}), bf16[4,528,128]{2,1,0:T(8,128)(2,1)S(1)}, u32[]{:S(2)}, u32[]{:S(2)}) async-start(bf16[4,528,128]{2,1,0:T(8,128)(2,1)} %join_parts.1), calls=%async_computation.3 | async-start | bytes 1081344 | tf_op jit(solution)/shard_map/all_to_all | solution.py:421

commit v9 on v6

--- a/solution.py
+++ b/solution.py
@@ -31,47 +31,31 @@
     return pltpu.CompilerParams(vmem_limit_bytes=mib * 2**20)
 
 
-def cut_kernel(order, cache_ref, *rest):
+def cut_kernel(per, order, cache_ref, *rest):
     outs, sems = rest[:-1], rest[-1]
     copies = []
     for i, out in enumerate(outs):
-        at = pl.multiple_of(order[i] * HD, HD)
-        copy = pltpu.make_async_copy(cache_ref.at[:, :, pl.ds(at, HD)], out, sems.at[i])
-        copy.start()
-        copies.append(copy)
+        for j in range(per):
+            s = i * per + j
+            at = pl.ds(pl.multiple_of(order[s] * HD, HD), HD)
+            copy = pltpu.make_async_copy(cache_ref.at[:, :, at], out.at[j], sems.at[s])
+            copy.start()
+            copies.append(copy)
     for copy in copies:
         copy.wait()
 
 
-def cut(order, cache, count):
+def cut(order, cache, halves, per):
     depth, rows, _ = cache.shape
     return pl.pallas_call(
-        cut_kernel,
-        out_shape=[jax.ShapeDtypeStruct((depth, rows, HD), BF)] * count,
+        functools.partial(cut_kernel, per),
+        out_shape=[jax.ShapeDtypeStruct((per, depth, rows, HD), BF)] * halves,
         in_specs=[SMEM, HBM],
-        out_specs=[VMEM] * count,
-        scratch_shapes=[pltpu.SemaphoreType.DMA((count,))],
+        out_specs=[VMEM] * halves,
+        scratch_shapes=[pltpu.SemaphoreType.DMA((halves * per,))],
         compiler_params=params(4),
         name="cut_prompt",
     )(order, cache)
-
-
-def pick_kernel(which, *refs):
-    picked = refs[0][...]
-    for i in range(1, len(refs) - 1):
-        picked = jnp.where(which[0] == i, refs[i][...], picked)
-    refs[-1][...] = picked
-
-
-def pick(which, blocks):
-    return pl.pallas_call(
-        pick_kernel,
-        out_shape=jax.ShapeDtypeStruct(blocks[0].shape, BF),
-        in_specs=[SMEM] + [VMEM] * len(blocks),
-        out_specs=VMEM,
-        compiler_params=params(4),
-        name="pick_owner",
-    )(which, *blocks)
 
 
 KEPT = 8
@@ -166,7 +150,7 @@
     return [list(outs[s * KEPT : (s + 1) * KEPT]) for s in range(count)]
 
 
-def attend(width, pr_ref, kept, q_gain, acc_ref, part_ref, at_ref, dq_ref, gacc_ref):
+def attend(width, pr_ref, kept, q_gain, part_ref, at_ref, dq_ref):
     qt_ref, gt_ref, row_ref, er_ref, ot_ref, dp_ref, kh_ref, ku_ref = kept
     scale = HD ** (-0.5)
     p_key = pr_ref[0]
@@ -209,9 +193,9 @@
     folded = q_term[:, :HD]
     for start in range(HD, width, HD):
         folded = folded + q_term[:, start : start + HD]
-    gacc_ref[0:1, :] = acc_ref[0:1, :] + jnp.sum(folded.T, axis=0, keepdims=True)
-    gacc_ref[1:2, :] = acc_ref[1:2, :] + jnp.sum(d_kr * ku_ref[:, :HD], axis=0, keepdims=True)
-    return d_kr, d_vr
+    q_term = jnp.sum(folded.T, axis=0, keepdims=True)
+    k_term = jnp.sum(d_kr * ku_ref[:, :HD], axis=0, keepdims=True)
+    return d_kr, d_vr, q_term, k_term
 
 
 def settle(width, head, live_len, kept, q_gain, k_gain, at_ref, dq_ref, d_kr, d_vr, outs, bufs, sems):
@@ -253,36 +237,65 @@
     for i in range(share):
         q_buf[:, i * HD : (i + 1) * HD] = d_q[i * rows : (i + 1) * rows, :]
     send(1, q_buf)
+    return copies
+
+
+def whole_kernel(slots, width, meta, pr_ref, gain_ref, kg_ref, acc_ref, *rest):
+    count = len(slots)
+    kept, rest = rest[: KEPT * count], rest[-13:]
+    part_ref, gacc_ref, *rest = rest
+    outs, (at_ref, dq_ref), bufs, sems = rest[:4], rest[4:6], rest[6:10], rest[10]
+    q_gain = gain_ref[...]
+    k_gain = kg_ref[...]
+    q_sum, k_sum = acc_ref[0:1, :], acc_ref[1:2, :]
+    copies = []
+    for i, s in enumerate(slots):
+        mine = kept[i * KEPT : (i + 1) * KEPT]
+        d_kr, d_vr, q_term, k_term = attend(
+            width, pr_ref.at[i], mine, q_gain, part_ref.at[i], at_ref.at[i], dq_ref.at[i]
+        )
+        q_sum, k_sum = q_sum + q_term, k_sum + k_term
+        copies += settle(
+            width, meta[s], meta[meta.shape[0] - 1], mine, q_gain, k_gain, at_ref.at[i], dq_ref.at[i],
+            d_kr, d_vr, outs, [buf.at[i] for buf in bufs], sems.at[i],
+        )
+    gacc_ref[0:1, :] = q_sum
+    gacc_ref[1:2, :] = k_sum
     for copy in copies:
         copy.wait()
 
 
-def whole_kernel(s, width, meta, pr_ref, *rest):
-    kept, (gain_ref, kg_ref, acc_ref) = rest[:KEPT], rest[KEPT : KEPT + 3]
-    part_ref, gacc_ref, *rest = rest[-13:]
-    outs, (at_ref, dq_ref), bufs, sems = rest[:4], rest[4:6], rest[6:10], rest[10]
+def first_kernel(slots, width, pr_ref, gain_ref, acc_ref, *rest):
+    count = len(slots)
+    kept, (part_ref, gacc_ref, *results) = rest[: KEPT * count], rest[KEPT * count :]
     q_gain = gain_ref[...]
-    d_kr, d_vr = attend(width, pr_ref, kept, q_gain, acc_ref, part_ref, at_ref, dq_ref, gacc_ref)
-    live_len = meta[meta.shape[0] - 1]
-    settle(width, meta[s], live_len, kept, q_gain, kg_ref[...], at_ref, dq_ref, d_kr, d_vr, outs, bufs, sems)
-
-
-def first_kernel(width, pr_ref, *rest):
-    kept, (gain_ref, acc_ref) = rest[:KEPT], rest[KEPT : KEPT + 2]
-    part_ref, gacc_ref, at_ref, dq_ref, dkr_ref, dvr_ref = rest[-6:]
-    d_kr, d_vr = attend(width, pr_ref, kept, gain_ref[...], acc_ref, part_ref, at_ref, dq_ref, gacc_ref)
-    dkr_ref[...] = d_kr
-    dvr_ref[...] = d_vr
-
-
-def second_kernel(s, width, meta, *rest):
-    kept, (gain_ref, kg_ref, at_ref, dq_ref, dkr_ref, dvr_ref) = rest[:KEPT], rest[KEPT : KEPT + 6]
+    q_sum, k_sum = acc_ref[0:1, :], acc_ref[1:2, :]
+    for i in range(count):
+        at_ref, dq_ref, dkr_ref, dvr_ref = results[4 * i : 4 * i + 4]
+        d_kr, d_vr, q_term, k_term = attend(
+            width, pr_ref.at[i], kept[i * KEPT : (i + 1) * KEPT], q_gain, part_ref.at[i], at_ref, dq_ref
+        )
+        q_sum, k_sum = q_sum + q_term, k_sum + k_term
+        dkr_ref[...] = d_kr
+        dvr_ref[...] = d_vr
+    gacc_ref[0:1, :] = q_sum
+    gacc_ref[1:2, :] = k_sum
+
+
+def second_kernel(slots, width, meta, gain_ref, kg_ref, *rest):
+    count = len(slots)
+    kept, results = rest[: KEPT * count], rest[KEPT * count : (KEPT + 4) * count]
     outs, bufs, sems = rest[-9:-5], rest[-5:-1], rest[-1]
-    live_len = meta[meta.shape[0] - 1]
-    settle(
-        width, meta[s], live_len, kept, gain_ref[...], kg_ref[...], at_ref, dq_ref,
-        dkr_ref[...], dvr_ref[...], outs, bufs, sems,
-    )
+    copies = []
+    for i, s in enumerate(slots):
+        at_ref, dq_ref, dkr_ref, dvr_ref = results[4 * i : 4 * i + 4]
+        copies += settle(
+            width, meta[s], meta[meta.shape[0] - 1], kept[i * KEPT : (i + 1) * KEPT], gain_ref[...],
+            kg_ref[...], at_ref, dq_ref, dkr_ref[...], dvr_ref[...], outs,
+            [buf.at[i] for buf in bufs], sems.at[i],
+        )
+    for copy in copies:
+        copy.wait()
 
 
 def out_shapes(rows, q_width, k_width):
@@ -290,100 +303,97 @@
     return [jax.ShapeDtypeStruct((rows, w), BF) for w in widths]
 
 
-def out_scratch(rows, share):
+def out_scratch(count, rows, share):
     widths = (share * HD, share * HD, HD, HD)
-    return [pltpu.VMEM((rows, w), BF) for w in widths] + [pltpu.SemaphoreType.DMA((4,))]
-
-
-def cost(prompt_rows, rows, total):
-    return pl.CostEstimate(
-        flops=(8 * prompt_rows + 4 * rows) * total * HD,
-        bytes_accessed=2**20,
-        transcendentals=total * prompt_rows,
-    )
-
-
-def whole_head(s, meta, prompt, kept, q_gain, k_gain, acc, buffers, q_width, k_width):
-    total = kept[0].shape[1]
-    rows = kept[3].shape[0]
+    return [pltpu.VMEM((count, rows, w), BF) for w in widths] + [pltpu.SemaphoreType.DMA((count, 4))]
+
+
+def whole_heads(slots, meta, prompt, kept, q_gain, k_gain, acc, buffers, q_width, k_width):
+    count = len(slots)
+    total = kept[0][0].shape[1]
+    rows = kept[0][3].shape[0]
+    flat = [x for s in slots for x in kept[s]]
     outs = pl.pallas_call(
-        functools.partial(whole_kernel, s, 2 * HD),
+        functools.partial(whole_kernel, slots, 2 * HD),
         out_shape=[
             jax.ShapeDtypeStruct(prompt.shape, BF),
             jax.ShapeDtypeStruct(acc.shape, F32),
         ]
         + out_shapes(rows, q_width, k_width),
-        in_specs=[SMEM] + [VMEM] * (4 + KEPT) + [HBM] * len(buffers),
+        in_specs=[SMEM] + [VMEM] * (4 + len(flat)) + [HBM] * len(buffers),
         out_specs=[VMEM] * 2 + [HBM] * 4,
-        scratch_shapes=[pltpu.VMEM((HD, total), BF), pltpu.VMEM((HD, total), F32)]
-        + out_scratch(rows, total // rows),
-        input_output_aliases={5 + KEPT + i: 2 + i for i in range(len(buffers))},
+        scratch_shapes=[pltpu.VMEM((count, HD, total), BF), pltpu.VMEM((count, HD, total), F32)]
+        + out_scratch(count, rows, total // rows),
+        input_output_aliases={5 + len(flat) + i: 2 + i for i in range(len(buffers))},
         compiler_params=params(16),
-        cost_estimate=cost(prompt.shape[1], rows, total),
-        name="attend_head",
-    )(meta, prompt, *kept, q_gain, k_gain, acc, *buffers)
-    return outs[0], outs[1], outs[2:]
-
-
-def first_half(prompt, kept, q_gain, acc):
-    total = kept[0].shape[1]
-    rows = kept[3].shape[0]
-    return pl.pallas_call(
-        functools.partial(first_kernel, 2 * HD),
+        name="attend_own_half",
+    )(meta, prompt, q_gain, k_gain, acc, *flat, *buffers)
+    return outs[0], outs[1], list(outs[2:])
+
+
+def first_part(slots, prompt, kept, q_gain, acc):
+    total = kept[0][0].shape[1]
+    rows = kept[0][3].shape[0]
+    flat = [x for s in slots for x in kept[s]]
+    each = [
+        jax.ShapeDtypeStruct((HD, total), BF),
+        jax.ShapeDtypeStruct((HD, total), F32),
+        jax.ShapeDtypeStruct((rows, HD), F32),
+        jax.ShapeDtypeStruct((rows, HD), F32),
+    ]
+    outs = pl.pallas_call(
+        functools.partial(first_kernel, slots, 2 * HD),
         out_shape=[
             jax.ShapeDtypeStruct(prompt.shape, BF),
             jax.ShapeDtypeStruct(acc.shape, F32),
-            jax.ShapeDtypeStruct((HD, total), BF),
-            jax.ShapeDtypeStruct((HD, total), F32),
-            jax.ShapeDtypeStruct((rows, HD), F32),
-            jax.ShapeDtypeStruct((rows, HD), F32),
-        ],
-        in_specs=[VMEM] * (3 + KEPT),
-        out_specs=[VMEM] * 6,
+        ]
+        + each * len(slots),
+        in_specs=[VMEM] * (3 + len(flat)),
+        out_specs=[VMEM] * (2 + 4 * len(slots)),
         compiler_params=params(16),
-        cost_estimate=cost(prompt.shape[1], rows, total),
-        name="attend_last_head",
-    )(prompt, *kept, q_gain, acc)
-
-
-def second_half(s, meta, kept, q_gain, k_gain, results, buffers):
-    total = kept[0].shape[1]
-    rows = kept[3].shape[0]
+        name="attend_other_half",
+    )(prompt, q_gain, acc, *flat)
+    return outs[0], outs[1], list(outs[2:])
+
+
+def second_part(slots, meta, kept, q_gain, k_gain, results, buffers):
+    count = len(slots)
+    total = kept[0][0].shape[1]
+    rows = kept[0][3].shape[0]
+    flat = [x for s in slots for x in kept[s]]
     return pl.pallas_call(
-        functools.partial(second_kernel, s, 2 * HD),
+        functools.partial(second_kernel, slots, 2 * HD),
         out_shape=out_shapes(rows, buffers[0].shape[1], buffers[2].shape[1]),
-        in_specs=[SMEM] + [VMEM] * (KEPT + 6) + [HBM] * 4,
+        in_specs=[SMEM] + [VMEM] * (2 + len(flat) + len(results)) + [HBM] * 4,
         out_specs=[HBM] * 4,
-        scratch_shapes=out_scratch(rows, total // rows),
-        input_output_aliases={7 + KEPT + i: i for i in range(4)},
+        scratch_shapes=out_scratch(count, rows, total // rows),
+        input_output_aliases={3 + len(flat) + len(results) + i: i for i in range(4)},
         compiler_params=params(16),
-        cost_estimate=pl.CostEstimate(flops=0, bytes_accessed=2**20, transcendentals=0),
-        name="settle_last_head",
-    )(meta, *kept, q_gain, k_gain, *results, *buffers)
-
-
-def join(a, b):
-    return (a.astype(F32) + b.astype(F32)).astype(BF)
+        name="settle_other_half",
+    )(meta, q_gain, k_gain, *flat, *results, *buffers)
 
 
 def place_kernel(meta, *refs):
-    heads, out_ref = refs[:-1], refs[-1]
+    halves, out_ref = refs[:-1], refs[-1]
     mine = meta[0] > 0
-    for i, ref in enumerate(heads):
-        at = pl.multiple_of(meta[1 + i] * HD, HD)
-        out_ref[:, :, pl.ds(at, HD)] = jnp.where(mine, ref[...], jnp.zeros_like(ref[...]))
-
-
-def place(meta, heads):
-    depth, rows, _ = heads[0].shape
+    s = 1
+    for ref in halves:
+        for j in range(ref.shape[0]):
+            at = pl.ds(pl.multiple_of(meta[s] * HD, HD), HD)
+            out_ref[:, :, at] = jnp.where(mine, ref[j], jnp.zeros_like(ref[j]))
+            s += 1
+
+
+def place(meta, halves):
+    per, depth, rows, _ = halves[0].shape
     return pl.pallas_call(
         place_kernel,
-        out_shape=jax.ShapeDtypeStruct((depth, rows, HD * len(heads)), BF),
-        in_specs=[SMEM] + [VMEM] * len(heads),
+        out_shape=jax.ShapeDtypeStruct((depth, rows, HD * per * len(halves)), BF),
+        in_specs=[SMEM] + [VMEM] * len(halves),
         out_specs=VMEM,
         compiler_params=params(8),
         name="place_prompt_grad",
-    )(meta, *heads)
+    )(meta, *halves)
 
 
 def after(x, *others):
@@ -409,61 +419,55 @@
     me = lax.axis_index("group")
     kv_heads = k.shape[1] // HD
     depth, p_rows, _ = cache.shape
-    direct = n_group == kv_heads
-
-    def shift(x, s):
-        return lax.ppermute(x, "group", [(i, (i + s) % n_group) for i in range(n_group)])
-
+    pairs = n_group == 4 and kv_heads % 2 == 0
+    per = kv_heads // 2 if pairs else kv_heads
+    mine_flag = (me == owner).astype(jnp.int32)
     gain_col = q_gain[:, None]
     gain_row = k_gain[None, :]
-    if direct:
-        order = jnp.stack([(me - s) % n_group for s in range(n_group)]).astype(jnp.int32)
-    else:
-        order = jnp.arange(kv_heads, dtype=jnp.int32)
+    order = jnp.arange(kv_heads, dtype=jnp.int32)
+    if pairs:
+        order = (order + (me % 2) * per) % kv_heads
     meta = jnp.concatenate([order, live_len[None]])
     q, g, k, v = [pltpu.with_memory_space_constraint(x, pltpu.HBM) for x in (q, g, k, v)]
     kept = prepare(meta, q, g, k, v, gain_col, gain_row, kv_heads)
-    if direct:
-        blocks = cut(order, pltpu.with_memory_space_constraint(cache, pltpu.HBM), kv_heads)
-        got = [blocks[0]] + [shift(blocks[s], -s) for s in range(1, n_group)]
-        got[1], kept[0][2] = lax.optimization_barrier((got[1], kept[0][2]))
-        mine = pick(jnp.reshape((owner - me) % n_group, (1,)).astype(jnp.int32), got)
-        prompts = [mine]
-        for s in range(1, n_group):
-            prompts.append(shift(prompts[-1], 1))
+    acc = jnp.zeros((2, HD), F32)
+
+    def swap(x, step, axis="group", size=n_group):
+        return lax.ppermute(x, axis, [(i, i ^ step) for i in range(size)])
+
+    def join(a, b):
+        return (a.astype(F32) + b.astype(F32)).astype(BF)
+
+    if pairs:
+        own, other = tuple(range(per)), tuple(range(per, kv_heads))
+        mine, theirs = cut(order, pltpu.with_memory_space_constraint(cache, pltpu.HBM), 2, per)
+        got = after(swap(theirs, 1), kept[0][2])
+        mine = jnp.where(owner == me ^ 1, got, mine)
+        got = swap(mine, 2)
+        mine = jnp.where(owner // 2 == me // 2, mine, got)
+        theirs = swap(mine, 1)
+        part, acc, buffers = whole_heads(
+            own, meta, mine, kept, gain_col, gain_row, acc, (), q.shape[1], k.shape[1]
+        )
+        sent, acc, results = first_part(other, after(theirs, part), kept, gain_col, acc)
+        buffers = list(second_part(other, meta, kept, gain_col, gain_row, results, buffers))
+        gains = acc + swap(acc, 1)
+        part = join(part, after(swap(sent, 1), gains, buffers[2]))
+        gains = after(gains, part)
+        gains = gains + swap(gains, 2)
+        gains = pair_sum(gains, "dp", n_dp)
+        part = join(part, after(swap(part, 2), gains))
+        placed = place(jnp.concatenate([mine_flag[None], order]), [part, swap(part, 1)])
     else:
         cache = lax.psum(jnp.where(me == owner, cache, jnp.zeros_like(cache)), "group")
-        prompts = cut(order, cache, kv_heads)
-
-    acc = jnp.zeros((2, HD), F32)
-    parts, buffers, ring = [], (), None
-    for s, prompt in enumerate(prompts):
-        last = s == kv_heads - 1
-        if last and ring is not None:
-            prompt = after(prompt, ring)
-        if last:
-            part, acc, *results = first_half(prompt, kept[s], gain_col, acc)
-        else:
-            part, acc, buffers = whole_head(
-                s, meta, prompt, kept[s], gain_col, gain_row, acc, buffers, q.shape[1], k.shape[1]
-            )
-        parts.append(part)
-        if direct and s > 0:
-            ring = part if s == 1 else join(part, shift(ring, 1))
-    buffers = list(second_half(kv_heads - 1, meta, kept[-1], gain_col, gain_row, results, buffers))
-
-    mine_flag = (me == owner).astype(jnp.int32)
-    if direct:
-        total = join(parts[0], after(shift(ring, 1), buffers[2]))
-        gains = pair_sum(after(acc, ring), "group", n_group)
-        total, gains = lax.optimization_barrier((total, gains))
-        heads = [total] + [shift(total, s) for s in range(1, n_group)]
-        placed = place(jnp.concatenate([mine_flag[None], order]), heads)
-    else:
-        total = lax.psum(jnp.concatenate(parts, axis=-1).astype(F32), "group").astype(BF)
+        (prompt,) = cut(order, cache, 1, kv_heads)
+        part, acc, buffers = whole_heads(
+            tuple(range(kv_heads)), meta, prompt, kept, gain_col, gain_row, acc, (), q.shape[1], k.shape[1]
+        )
+        total = jnp.transpose(part, (1, 2, 0, 3)).reshape(depth, p_rows, kv_heads * HD)
+        total = lax.psum(total.astype(F32), "group").astype(BF)
         placed = jnp.where(mine_flag > 0, total, jnp.zeros((), BF))
-        gains = pair_sum(acc, "group", n_group)
-    gains = pair_sum(gains, "dp", n_dp)
+        gains = pair_sum(pair_sum(acc, "group", n_group), "dp", n_dp)
     attended, d_query, d_key, d_value = buffers
     return (
         attended[None, None],

time: 69 us -> 103 us (1.49)
  local copies, waits for them, and re-layouts: 1.59 us -> 25.1 us
  waiting for transfers between devices: 21.5 us -> 37.1 us
  starting transfers between devices: 21.9 us -> 15.1 us
  other arithmetic: 0.77 us -> 4.26 us
  Pallas kernels: 20.9 us -> 18.5 us
    unnamed x4 -> x88, local copies, waits for them, and re-layouts: 1.31 us -> 24.9 us
    ppermute x12 -> x8, waiting for transfers between devices: 13.5 us -> 31.9 us  [swap(): return lax.ppermute(x, axis, [(i, i ^ step) for i in range(size)])]
    ppermute x12 -> x8, starting transfers between devices: 14.4 us -> 9.92 us  [swap(): return lax.ppermute(x, axis, [(i, i ^ step) for i in range(size)])]
    select_n x0 -> x3, other arithmetic: none -> 2.88 us  [the longest x1 1.89 us: local(): mine = jnp.where(owner == me ^ 1, got, mine)]
    ppermute x5 -> x3, waiting for transfers between devices: 8.02 us -> 5.22 us  [pair_sum(): lax.ppermute(value, axis, [(i, i ^ step) for i in range(size)])]
    pallas_call x7 -> x4, Pallas kernels: 14.3 us -> 11.9 us  [the longest x1 4.5 us: whole_heads(): pl.pallas_call(functools.partial(whole_kernel, slots, 2 * HD), out_shape=...]
    ppermute x5 -> x3, starting transfers between devices: 7.5 us -> 5.16 us  [pair_sum(): lax.ppermute(value, axis, [(i, i ^ step) for i in range(size)])]
  transfers between devices with their start and end apart: 17 -> 11, of which waited for: 10 -> 7; matrix products, arithmetic and copies ran while one was open for 1% -> 1% of each run, Pallas kernels for 26% -> 11%
where the time goes in v9:
time: 103 us; the launch traced here: 102 us
  waiting for transfers between devices  37.1 us (36%)
  local copies, waits for them, and re-layouts  25.1 us (24%)
  Pallas kernels  18.5 us (18%)
  starting transfers between devices  15.1 us (15%)
  other arithmetic  4.26 us (4%)
  between operations  2.18 us (2%)
    ppermute x8, waiting for transfers between devices, swap(): return lax.ppermute(x, axis, [(i, i ^ step) for i in range(size)])  31.9 us
    unnamed x88, local copies, waits for them, and re-layouts  24.9 us
    ppermute x8, starting transfers between devices, swap(): return lax.ppermute(x, axis, [(i, i ^ step) for i in range(size)])  9.92 us
    ppermute x3, waiting for transfers between devices, pair_sum(): lax.ppermute(value, axis, [(i, i ^ step) for i in range(size)])  5.22 us
    ppermute x3, starting transfers between devices, pair_sum(): lax.ppermute(value, axis, [(i, i ^ step) for i in range(size)])  5.16 us
    pallas_call x1, Pallas kernels, prepare(): pl.pallas_call(functools.partial(prepare_kernel, count, share, rows, 2 *...  5.13 us
    pallas_call x1, Pallas kernels, whole_heads(): pl.pallas_call(functools.partial(whole_kernel, slots, 2 * HD), out_shape=...  4.5 us
    pallas_call x1, Pallas kernels, first_part(): pl.pallas_call(functools.partial(first_kernel, slots, 2 * HD), out_shape=...  3.05 us
  transfers between devices with their start and end apart: 11, of which 7 were waited for; matrix products, arithmetic and copies ran while one was open for 1% of the time, Pallas kernels for 11%

profile of v9, /device:TPU:0, one launch (start us, length us, event | category | flops | bytes accessed | tf_op | source)
XLA Modules:
  0.0 102.2 jit_solution(2027893659572078564)
XLA Ops:
  0.7 2.4 %cut_prompt.1 = (bf16[2,2,256,128]{3,2,1,0:T(8,128)(2,1)S(1)}, bf16[2,2,256,128]{3,2,1,0:T(8,128)(2,1)}) custom-call(s32[4]{0:T(128)S(1)} %and_select_fusion.order, bf16[2,256,512]{2,1,0:T(8,128)(2,1)} %bitcast.29), custom_call_target="tpu_custom_call" | custom-call | tf_op jit(solution)/shard_map/cut_prompt/pallas_call | solution.py:50
  3.1 0.7 copy-done.16
  3.8 3.0 %collective-permute-start = (bf16[2,2,256,128]{3,2,1,0:T(8,128)(2,1)}, bf16[2,2,256,128]{3,2,1,0:T(8,128)(2,1)}, u32[]{:S(2)}, u32[]{:S(2)}) collective-permute-start(bf16[2,2,256,128]{3,2,1,0:T(8,128)(2,1)} %get-tuple-element.81), channel_id=1, source_target_pairs={{0,1},{1,0},{2,3},{3,2},{4,5},{5,4},{6,7},{7,6},{8,9},{9,8},{10,11... | collective-permute-start | bytes 786440 | tf_op jit(solution)/shard_map/ppermute | solution.py:436
  8.1 0.6 copy-done.43
  8.7 0.1 copy.22.gain_ref
  8.9 0.7 pad_add_fusion.1
  9.5 0.6 copy-done.38
  10.1 0.1 copy-done.40
  10.2 5.1 %prepare_response.1 = (bf16[128,768]{1,0:T(8,128)(2,1)S(1)}, bf16[128,768]{1,0:T(8,128)(2,1)S(1)}, f32[8,768]{1,0:T(8,128)S(1)}, bf16[192,768]{1,0:T(8,128)(2,1)...) custom-call(s32[5]{0:T(128)S(1)} %get-tuple-element.125.meta, ...), custom_call_target="tpu_custom_call" | custom-call | flops 452984832 | bytes 3932160 | tf_op jit(solution)/shard_map/prepare_response/pallas_call | solution.py:130
  15.3 0.8 copy-done.4
  16.1 0.8 copy-done.6
  16.9 0.7 copy-done.10
  17.7 0.7 copy-done.12
  18.4 0.7 copy-done.14
  19.1 0.7 copy-done.18
  19.8 0.7 copy-done.20
  20.5 0.7 copy-done.22
  21.1 0.7 copy-done.24
  21.8 0.7 copy-done.26
  22.5 0.7 copy-done.28
  23.2 0.6 copy-done.30
  23.8 0.6 copy-done.32
  24.5 0.6 copy-done.34
  25.1 0.6 copy-done.36
  25.7 1.9 %broadcast_select_fusion = bf16[2,2,256,128]{3,2,1,0:T(8,128)(2,1)} fusion(bf16[2,2,256,128]{3,2,1,0:T(8,128)(2,1)} %collective-permute-done, bf16[2,2,256,128]{3,2,1,0:T(8,128)(2,1)S(1)} %copy-done.17, pred[]{:T(512)S(6)} %eq.14), kind=kLoop, calls=%fused_computation.2 | loop fusion | flops 131072 | bytes 786433 | tf_op jit(solution)/shard_map/jit(_where)/select_n | solution.py:445
  27.6 1.6 %collective-permute-start.1 = (bf16[2,2,256,128]{3,2,1,0:T(8,128)(2,1)}, bf16[2,2,256,128]{3,2,1,0:T(8,128)(2,1)}, u32[]{:S(2)}, u32[]{:S(2)}) collective-permute-start(bf16[2,2,256,128]{3,2,1,0:T(8,128)(2,1)} %broadcast_select_fusion), channel_id=1, source_target_pairs={{0,2},{1,3},{2,0},{3,1},{4,6},{5,7},{6,4},{7,5},{8,10},{9,11},{10,... | collective-permute-start | bytes 786440 | tf_op jit(solution)/shard_map/ppermute | solution.py:436
  29.2 12.0 %collective-permute-done.1 = bf16[2,2,256,128]{3,2,1,0:T(8,128)(2,1)} collective-permute-done((bf16[2,2,256,128]{3,2,1,0:T(8,128)(2,1)}, bf16[2,2,256,128]{3,2,1,0:T(8,128)(2,1)}, u32[]{:S(2)}, u32[]{:S(2)}) %collective-permute-start.1) | collective-permute-done | bytes 262176 | tf_op jit(solution)/shard_map/ppermute | solution.py:436
  41.2 1.0 broadcast_select_fusion.1.pr_ref
  42.2 0.1 collective-permute-start.2
  42.4 0.6 copy-done.35
  43.0 0.0 copy-done.41
  43.0 1.1 %copy-done.7 = f32[192,768]{1,0:T(8,128)S(1)} copy-done((f32[192,768]{1,0:T(8,128)S(1)}, f32[192,768]{1,0:T(8,128)}, u32[]{:S(2)}) %copy-start.7) | copy-done | bytes 589848
  44.0 1.0 copy-done.9
  45.0 1.0 copy-done.11
  46.0 1.0 copy-done.13
  47.0 1.0 copy-done.15
  48.0 0.9 copy-done.21
  48.9 0.9 copy-done.23
  49.8 0.9 copy-done.25
  50.7 0.9 copy-done.27
  51.7 0.9 copy-done.29
  52.6 0.8 copy-done.31
  53.4 0.8 copy-done.33
  54.2 0.7 copy-done.37
  54.9 4.5 %attend_own_half.1 = (bf16[2,2,256,128]{3,2,1,0:T(8,128)(2,1)S(1)}, f32[2,128]{1,0:T(2,128)S(1)}, bf16[192,2048]{1,0:T(8,128)(2,1)}, bf16[192,2048]{1,0:T(8,128)...) custom-call(s32[5]{0:T(128)S(1)} %copy-done.39, bf16[2,2,256,128]{3,2,1,0:T(8,128)(2,1)S(1)} %broadcast_select_fusion.1.pr_ref, ...), custom_call_target="tpu_custom_call" | custom-call | tf_op jit(solution)/shard_map/attend_own_half/pallas_call | solution.py:316
  59.5 3.0 %attend_other_half.1 = (bf16[2,2,256,128]{3,2,1,0:T(8,128)(2,1)S(1)}, f32[2,128]{1,0:T(2,128)S(1)}, bf16[128,768]{1,0:T(8,128)(2,1)S(1)}, f32[128,768]{1,0:T(8,1...) custom-call(bf16[2,2,256,128]{3,2,1,0:T(8,128)(2,1)S(1)} %collective, ...), custom_call_target="tpu_custom_call" | custom-call | tf_op jit(solution)/shard_map/attend_other_half/pallas_call | solution.py:344
  62.5 2.1 %collective-permute-start.3 = (bf16[2,2,256,128]{3,2,1,0:T(8,128)(2,1)S(1)}, bf16[2,2,256,128]{3,2,1,0:T(8,128)(2,1)S(1)}, u32[]{:S(2)}, u32[]{:S(2)}) collective-permute-start(bf16[2,2,256,128]{3,2,1,0:T(8,128)(2,1)S(1)} %get-tuple-element.119), channel_id=1, source_target_pairs={{0,1},{1,0},{2,3},{3,2},{4,5},{5,4},{6,7},{7,6},{8,9},{9,8},{10,11... | collective-permute-start | bytes 786440 | tf_op jit(solution)/shard_map/ppermute | solution.py:436
  64.6 0.1 collective-permute-start.4
  64.7 2.0 %settle_other_half.1 = (bf16[192,2048]{1,0:T(8,128)(2,1)}, bf16[192,2048]{1,0:T(8,128)(2,1)}, bf16[192,512]{1,0:T(8,128)(2,1)}, bf16[192,512]{1,0:T(8,128)(2,1)}) custom-call(s32[5]{0:T(128)S(1)} %copy-done.39, f32[128,1]{1,0:T(8,128)S(1)} %copy.22.gain_ref, ...), custom_call_target="tpu_custom_call", output_to_operand_aliasing={{0}: (27, {}), {1}: (28, {}), {2}: (29, {}), {3}: (30, {})} | custom-call | tf_op jit(solution)/shard_map/settle_other_half/pallas_call | solution.py:364
  66.6 3.4 %collective-permute-done.4 = f32[2,128]{1,0:T(2,128)S(1)} collective-permute-done((f32[2,128]{1,0:T(2,128)S(1)}, f32[2,128]{1,0:T(2,128)S(1)}, u32[]{:S(2)}, u32[]{:S(2)}) %collective-permute-start.4) | collective-permute-done | bytes 1056 | tf_op jit(solution)/shard_map/ppermute | solution.py:436
  70.1 0.1 add_convert_fusion.1
  70.1 2.5 %collective-permute-start.5 = (bf16[2,2,256,128]{3,2,1,0:T(8,128)(2,1)S(1)}, bf16[2,2,256,128]{3,2,1,0:T(8,128)(2,1)S(1)}, u32[]{:S(2)}, u32[]{:S(2)}) collective-permute-start(bf16[2,2,256,128]{3,2,1,0:T(8,128)(2,1)S(1)} %add_convert_fusion.1), channel_id=1, source_target_pairs={{0,2},{1,3},{2,0},{3,1},{4,6},{5,7},{6,4},{7,5},{8,10},{9,11},{10,... | collective-permute-start | bytes 786440 | tf_op jit(solution)/shard_map/ppermute | solution.py:436
  72.7 0.4 collective-permute-start.6
  73.1 10.1 %collective-permute-done.6 = f32[2,128]{1,0:T(2,128)S(1)} collective-permute-done((f32[2,128]{1,0:T(2,128)S(1)}, f32[2,128]{1,0:T(2,128)S(1)}, u32[]{:S(2)}, u32[]{:S(2)}) %collective-permute-start.6) | collective-permute-done | bytes 1056 | tf_op jit(solution)/shard_map/ppermute | solution.py:436
  83.2 1.1 %collective-permute-done.7 = f32[2,128]{1,0:T(2,128)S(1)} collective-permute-done((f32[2,128]{1,0:T(2,128)S(1)}, f32[2,128]{1,0:T(2,128)S(1)}, u32[]{:S(2)}, u32[]{:S(2)}) %collective-permute-start.7) | collective-permute-done | bytes 1056 | tf_op jit(solution)/shard_map/ppermute | solution.py:406
  84.4 4.1 %collective-permute-start.8 = (f32[2,128]{1,0:T(2,128)S(1)}, f32[2,128]{1,0:T(2,128)S(1)}, u32[]{:S(2)}, u32[]{:S(2)}) collective-permute-start(f32[2,128]{1,0:T(2,128)S(1)} %add.46), channel_id=1, source_target_pairs={{0,8},{4,12},{8,0},{12,4},{16,24},{20,28},{24,16},{28,20},{1,9},{5... | collective-permute-start | bytes 3080 | tf_op jit(solution)/shard_map/ppermute | solution.py:406
  88.5 1.5 %collective-permute-done.8 = f32[2,128]{1,0:T(2,128)S(1)} collective-permute-done((f32[2,128]{1,0:T(2,128)S(1)}, f32[2,128]{1,0:T(2,128)S(1)}, u32[]{:S(2)}, u32[]{:S(2)}) %collective-permute-start.8) | collective-permute-done | bytes 1056 | tf_op jit(solution)/shard_map/ppermute | solution.py:406
  90.1 1.0 %collective-permute-start.9 = (f32[2,128]{1,0:T(2,128)S(1)}, f32[2,128]{1,0:T(2,128)S(1)}, u32[]{:S(2)}, u32[]{:S(2)}) collective-permute-start(f32[2,128]{1,0:T(2,128)S(1)} %add.47), channel_id=1, source_target_pairs={{0,16},{4,20},{8,24},{12,28},{16,0},{20,4},{24,8},{28,12},{1,17},{... | collective-permute-start | bytes 3080 | tf_op jit(solution)/shard_map/ppermute | solution.py:406
  91.1 2.5 %collective-permute-done.9 = f32[2,128]{1,0:T(2,128)S(1)} collective-permute-done((f32[2,128]{1,0:T(2,128)S(1)}, f32[2,128]{1,0:T(2,128)S(1)}, u32[]{:S(2)}, u32[]{:S(2)}) %collective-permute-start.9) | collective-permute-done | bytes 1056 | tf_op jit(solution)/shard_map/ppermute | solution.py:406
  93.6 0.6 add.48
  94.2 0.1 add_convert_fusion.refs_0_
  94.3 0.1 collective-permute-start.10
  94.4 6.4 %collective-permute-done.10.refs_1_ = bf16[2,2,256,128]{3,2,1,0:T(8,128)(2,1)S(1)} collective-permute-done((bf16[2,2,256,128]{3,2,1,0:T(8,128)(2,1)S(1)}, bf16[2,2,256,128]{3,2,1,0:T(8,128)(2,1)S(1)}, u32[]{:S(2)}, u32[]{:S(2)}) %collective-permute-start.10) | collective-permute-done | bytes 262176 | tf_op jit(solution)/shard_map/ppermute | solution.py:436
  100.7 1.4 %place_prompt_grad.1 = bf16[2,256,512]{2,1,0:T(8,128)(2,1)} custom-call(s32[5]{0:T(128)S(1)} %copy-done.42, bf16[2,2,256,128]{3,2,1,0:T(8,128)(2,1)S(1)} %add_convert_fusion.refs_0_, bf16[2,2,256,128]{3,2,1,0:T(8,128)(2,1)S(1)} %collective-permute-done.10.refs_1_), custom_call_target="tpu_custom_call" | custom-call | tf_op jit(solution)/shard_map/place_prompt_grad/pallas_call | solution.py:389
  (65 shorter events, 0.1 us)
Async XLA Ops:
  3.1 0.7 copy-start.16
  3.8 21.9 %collective-permute-start = (bf16[2,2,256,128]{3,2,1,0:T(8,128)(2,1)}, bf16[2,2,256,128]{3,2,1,0:T(8,128)(2,1)}, u32[]{:S(2)}, u32[]{:S(2)}) collective-permute-start(bf16[2,2,256,128]{3,2,1,0:T(8,128)(2,1)} %get-tuple-element.81), channel_id=1, source_target_pairs={{0,1},{1,0},{2,3},{3,2},{4,5},{5,4},{6,7},{7,6},{8,9},{9,8},{10,11... | collective-permute-start | bytes 786440 | tf_op jit(solution)/shard_map/ppermute | solution.py:436
  8.1 0.7 copy-start.43
  9.5 0.6 copy-start.38
  9.5 0.7 copy-start.40
  10.2 15.5 %copy-start.17 = (bf16[2,2,256,128]{3,2,1,0:T(8,128)(2,1)S(1)}, bf16[2,2,256,128]{3,2,1,0:T(8,128)(2,1)}, u32[]{:S(2)}) copy-start(bf16[2,2,256,128]{3,2,1,0:T(8,128)(2,1)} %copy-done.16) | copy-start | bytes 786436
  15.3 0.8 copy-start.4
  16.1 0.8 copy-start.6
  16.9 0.7 copy-start.10
  17.7 0.7 copy-start.12
  18.4 0.7 copy-start.14
  19.1 0.7 copy-start.18
  19.8 0.7 copy-start.20
  20.5 0.7 copy-start.22
  21.1 0.7 copy-start.24
  21.8 0.7 copy-start.26
  22.5 0.7 copy-start.28
  23.2 0.6 copy-start.30
  23.8 0.6 copy-start.32
  24.5 0.6 copy-start.34
  25.1 0.6 copy-start.36
  25.7 1.9 %copy-start = (bf16[128,768]{1,0:T(8,128)(2,1)}, bf16[128,768]{1,0:T(8,128)(2,1)S(1)}, u32[]{:S(2)}) copy-start(bf16[128,768]{1,0:T(8,128)(2,1)S(1)} %get-tuple-element.74.rest_9_) | copy-start | bytes 589828
  25.7 1.9 %copy-start.2 = (f32[192,256]{1,0:T(8,128)}, f32[192,256]{1,0:T(8,128)S(1)}, u32[]{:S(2)}) copy-start(f32[192,256]{1,0:T(8,128)S(1)} %get-tuple-element.80.rest_15_) | copy-start | bytes 589828
  25.7 1.9 %copy-start.8 = (f32[128,768]{1,0:T(8,128)}, f32[128,768]{1,0:T(8,128)S(1)}, u32[]{:S(2)}) copy-start(f32[128,768]{1,0:T(8,128)S(1)} %get-tuple-element.88.rest_4_) | copy-start | bytes 1179652
  27.6 13.6 %collective-permute-start.1 = (bf16[2,2,256,128]{3,2,1,0:T(8,128)(2,1)}, bf16[2,2,256,128]{3,2,1,0:T(8,128)(2,1)}, u32[]{:S(2)}, u32[]{:S(2)}) collective-permute-start(bf16[2,2,256,128]{3,2,1,0:T(8,128)(2,1)} %broadcast_select_fusion), channel_id=1, source_target_pairs={{0,2},{1,3},{2,0},{3,1},{4,6},{5,7},{6,4},{7,5},{8,10},{9,11},{10,... | collective-permute-start | bytes 786440 | tf_op jit(solution)/shard_map/ppermute | solution.py:436
  29.2 13.1 %copy-start.5 = (f32[192,768]{1,0:T(8,128)S(1)}, f32[192,768]{1,0:T(8,128)}, u32[]{:S(2)}) copy-start(f32[192,768]{1,0:T(8,128)} %copy-done.4) | copy-start | bytes 1769476
  29.2 13.1 %copy-start.19 = (bf16[128,768]{1,0:T(8,128)(2,1)S(1)}, bf16[128,768]{1,0:T(8,128)(2,1)}, u32[]{:S(2)}) copy-start(bf16[128,768]{1,0:T(8,128)(2,1)} %copy-done.18) | copy-start | bytes 589828
  42.2 0.7 copy-start.35
  42.2 17.2 %collective-permute-start.2 = (bf16[2,2,256,128]{3,2,1,0:T(8,128)(2,1)S(1)}, bf16[2,2,256,128]{3,2,1,0:T(8,128)(2,1)S(1)}, u32[]{:S(2)}, u32[]{:S(2)}) collective-permute-start(bf16[2,2,256,128]{3,2,1,0:T(8,128)(2,1)S(1)} %broadcast_select_fusion.1.pr_ref), channel_id=1, source_target_pairs={{0,1},{1,0},{2,3},{3,2},{4,5},{5,4},{6,7},{7,6},{8,9},{9,8},{10,11... | collective-permute-start | bytes 786440 | tf_op jit(solution)/shard_map/ppermute | solution.py:436
  42.3 0.7 copy-start.39
  42.3 0.7 copy-start.41
  43.0 1.1 %copy-start.7 = (f32[192,768]{1,0:T(8,128)S(1)}, f32[192,768]{1,0:T(8,128)}, u32[]{:S(2)}) copy-start(f32[192,768]{1,0:T(8,128)} %copy-done.6) | copy-start | bytes 1769476
  44.0 1.0 copy-start.9
  45.0 1.0 copy-start.11
  46.0 1.0 copy-start.13
  47.0 1.0 copy-start.15
  48.0 0.9 copy-start.21
  48.9 0.9 copy-start.23
  49.8 0.9 copy-start.25
  50.7 0.9 copy-start.27
  51.7 0.9 copy-start.29
  52.6 0.8 copy-start.31
  53.4 0.8 copy-start.33
  54.2 0.7 copy-start.37
  54.9 4.5 %copy-start.1 = (bf16[128,768]{1,0:T(8,128)(2,1)S(1)}, bf16[128,768]{1,0:T(8,128)(2,1)}, u32[]{:S(2)}) copy-start(bf16[128,768]{1,0:T(8,128)(2,1)} %copy-done) | copy-start | bytes 589828
  54.9 4.5 %copy-start.3 = (f32[192,256]{1,0:T(8,128)S(1)}, f32[192,256]{1,0:T(8,128)}, u32[]{:S(2)}) copy-start(f32[192,256]{1,0:T(8,128)} %copy-done.2) | copy-start | bytes 589828
  62.5 7.5 %collective-permute-start.3 = (bf16[2,2,256,128]{3,2,1,0:T(8,128)(2,1)S(1)}, bf16[2,2,256,128]{3,2,1,0:T(8,128)(2,1)S(1)}, u32[]{:S(2)}, u32[]{:S(2)}) collective-permute-start(bf16[2,2,256,128]{3,2,1,0:T(8,128)(2,1)S(1)} %get-tuple-element.119), channel_id=1, source_target_pairs={{0,1},{1,0},{2,3},{3,2},{4,5},{5,4},{6,7},{7,6},{8,9},{9,8},{10,11... | collective-permute-start | bytes 786440 | tf_op jit(solution)/shard_map/ppermute | solution.py:436
  64.6 5.5 %collective-permute-start.4 = (f32[2,128]{1,0:T(2,128)S(1)}, f32[2,128]{1,0:T(2,128)S(1)}, u32[]{:S(2)}, u32[]{:S(2)}) collective-permute-start(f32[2,128]{1,0:T(2,128)S(1)} %get-tuple-element.120), channel_id=1, source_target_pairs={{0,1},{1,0},{2,3},{3,2},{4,5},{5,4},{6,7},{7,6},{8,9},{9,8},{10,11... | collective-permute-start | bytes 3080 | tf_op jit(solution)/shard_map/ppermute | solution.py:436
  70.1 24.1 %collective-permute-start.5 = (bf16[2,2,256,128]{3,2,1,0:T(8,128)(2,1)S(1)}, bf16[2,2,256,128]{3,2,1,0:T(8,128)(2,1)S(1)}, u32[]{:S(2)}, u32[]{:S(2)}) collective-permute-start(bf16[2,2,256,128]{3,2,1,0:T(8,128)(2,1)S(1)} %add_convert_fusion.1), channel_id=1, source_target_pairs={{0,2},{1,3},{2,0},{3,1},{4,6},{5,7},{6,4},{7,5},{8,10},{9,11},{10,... | collective-permute-start | bytes 786440 | tf_op jit(solution)/shard_map/ppermute | solution.py:436
  72.7 10.6 %collective-permute-start.6 = (f32[2,128]{1,0:T(2,128)S(1)}, f32[2,128]{1,0:T(2,128)S(1)}, u32[]{:S(2)}, u32[]{:S(2)}) collective-permute-start(f32[2,128]{1,0:T(2,128)S(1)} %add.43), channel_id=1, source_target_pairs={{0,2},{1,3},{2,0},{3,1},{4,6},{5,7},{6,4},{7,5},{8,10},{9,11},{10,... | collective-permute-start | bytes 3080 | tf_op jit(solution)/shard_map/ppermute | solution.py:436
  83.2 1.1 %collective-permute-start.7 = (f32[2,128]{1,0:T(2,128)S(1)}, f32[2,128]{1,0:T(2,128)S(1)}, u32[]{:S(2)}, u32[]{:S(2)}) collective-permute-start(f32[2,128]{1,0:T(2,128)S(1)} %add.45), channel_id=1, source_target_pairs={{0,4},{4,0},{8,12},{12,8},{16,20},{20,16},{24,28},{28,24},{1,5},{5... | collective-permute-start | bytes 3080 | tf_op jit(solution)/shard_map/ppermute | solution.py:406
  84.4 5.7 %collective-permute-start.8 = (f32[2,128]{1,0:T(2,128)S(1)}, f32[2,128]{1,0:T(2,128)S(1)}, u32[]{:S(2)}, u32[]{:S(2)}) collective-permute-start(f32[2,128]{1,0:T(2,128)S(1)} %add.46), channel_id=1, source_target_pairs={{0,8},{4,12},{8,0},{12,4},{16,24},{20,28},{24,16},{28,20},{1,9},{5... | collective-permute-start | bytes 3080 | tf_op jit(solution)/shard_map/ppermute | solution.py:406
  90.1 3.6 %collective-permute-start.9 = (f32[2,128]{1,0:T(2,128)S(1)}, f32[2,128]{1,0:T(2,128)S(1)}, u32[]{:S(2)}, u32[]{:S(2)}) collective-permute-start(f32[2,128]{1,0:T(2,128)S(1)} %add.47), channel_id=1, source_target_pairs={{0,16},{4,20},{8,24},{12,28},{16,0},{20,4},{24,8},{28,12},{1,17},{... | collective-permute-start | bytes 3080 | tf_op jit(solution)/shard_map/ppermute | solution.py:406
  94.3 6.5 %copy-start.42 = (s32[5]{0:T(128)S(1)}, s32[5]{0:T(128)}, u32[]{:S(2)}) copy-start(s32[5]{0:T(128)} %get-tuple-element.124.meta) | copy-start | bytes 64
  94.3 6.4 %collective-permute-start.10 = (bf16[2,2,256,128]{3,2,1,0:T(8,128)(2,1)S(1)}, bf16[2,2,256,128]{3,2,1,0:T(8,128)(2,1)S(1)}, u32[]{:S(2)}, u32[]{:S(2)}) collective-permute-start(bf16[2,2,256,128]{3,2,1,0:T(8,128)(2,1)S(1)} %add_convert_fusion.refs_0_), channel_id=1, source_target_pairs={{0,1},{1,0},{2,3},{3,2},{4,5},{5,4},{6,7},{7,6},{8,9},{9,8},{10,11... | collective-permute-start | bytes 786440 | tf_op jit(solution)/shard_map/ppermute | solution.py:436

commit v10 on v9

--- a/solution.py
+++ b/solution.py
@@ -58,96 +58,132 @@
     )(order, cache)
 
 
-KEPT = 8
-
-
-def prepare_kernel(count, share, rows, width, meta, q_in, g_in, k_in, v_in, gain_ref, kg_ref, *rest):
-    outs, (q_buf, g_buf, k_buf, v_buf, sems) = rest[:-5], rest[-5:]
-    live_len = meta[count]
-    scale = HD ** (-0.5)
-    wide = share * HD
-    copies = []
-    for s in range(count):
-        group = []
-        for j, (src, buf, size) in enumerate(
-            ((q_in, q_buf, wide), (k_in, k_buf, HD), (g_in, g_buf, wide), (v_in, v_buf, HD))
-        ):
-            at = pl.multiple_of(meta[s] * size, size)
-            copy = pltpu.make_async_copy(src.at[:, pl.ds(at, size)], buf.at[s], sems.at[s, j])
-            copy.start()
-            group.append(copy)
-        copies.append(group)
-    q_gain = gain_ref[...]
-    k_gain = kg_ref[...]
-    for s in range(count):
-        qt_ref, gt_ref, row_ref, er_ref, ot_ref, dp_ref, kh_ref, ku_ref = outs[s * KEPT : (s + 1) * KEPT]
-        for copy in copies[s]:
+def views(low, high, key):
+    rows = key.shape[0]
+    return (
+        low.at[0:HD, :],
+        low.at[HD : 2 * HD, :],
+        high.at[HD + rows : HD + rows + 8, :],
+        low.at[2 * HD : 2 * HD + rows, :],
+        high.at[0:HD, :],
+        high.at[HD : HD + rows, :],
+        key.at[:, 2 * HD : 3 * HD],
+        key.at[:, 0 : 2 * HD],
+    )
+
+
+def kept_shapes(count, rows, total):
+    return [
+        ((count, 2 * HD + rows, total), BF),
+        ((count, HD + rows + 8, total), F32),
+        ((count, rows, 3 * HD), F32),
+    ]
+
+
+def prepare_kernel(count, share, rows, width, turn, meta, q_in, g_in, k_in, v_in, gain_ref, kg_ref, *rest):
+    kept, (low, high, key, q_buf, g_buf, k_buf, v_buf, sems, out_sems) = rest[-12:-9], rest[-9:]
+
+    @pl.when(meta[count + 1] == turn)
+    def _():
+        live_len = meta[count]
+        scale = HD ** (-0.5)
+        wide = share * HD
+        copies = []
+        for s in range(count):
+            group = []
+            for j, (src, buf, size) in enumerate(
+                ((q_in, q_buf, wide), (k_in, k_buf, HD), (g_in, g_buf, wide), (v_in, v_buf, HD))
+            ):
+                at = pl.multiple_of(meta[s] * size, size)
+                copy = pltpu.make_async_copy(src.at[:, pl.ds(at, size)], buf.at[s], sems.at[s, j])
+                copy.start()
+                group.append(copy)
+            copies.append(group)
+        q_gain = gain_ref[...]
+        k_gain = kg_ref[...]
+        sent = []
+        for s in range(count):
+            qt_ref, gt_ref, row_ref, er_ref, ot_ref, dp_ref, kh_ref, ku_ref = views(
+                low.at[s], high.at[s], key.at[s]
+            )
+            for copy in copies[s]:
+                copy.wait()
+            q_t = jnp.concatenate([q_buf[s, :, i * HD : (i + 1) * HD] for i in range(share)], axis=0).T
+            g_t = jnp.concatenate([g_buf[s, :, i * HD : (i + 1) * HD] for i in range(share)], axis=0).T
+            qt_ref[...] = q_t
+            raw_k = k_buf[s].astype(F32)
+            k_inv = lax.rsqrt(jnp.mean(raw_k * raw_k, axis=-1, keepdims=True) + EPS)
+            k_unit = raw_k * k_inv
+            k_hat = (k_unit * k_gain).astype(BF)
+            kh_ref[...] = k_hat.astype(F32)
+            ku_ref[:, :HD] = k_unit
+            ku_ref[:, HD:] = jnp.broadcast_to(k_inv, (rows, HD))
+            r_val = v_buf[s]
+            r_val_t = r_val.T
+            for start in range(0, share * rows, width):
+                cols = slice(start, start + width)
+                token = (lax.broadcasted_iota(jnp.int32, (1, width), 1) + start) % rows
+                raw_q = q_t[:, cols].astype(F32)
+                q_inv = lax.rsqrt(jnp.mean(raw_q * raw_q, axis=0, keepdims=True) + EPS)
+                q_hat = (raw_q * q_inv * q_gain).astype(BF)
+                d_o = jnp.where(token < live_len, g_t[:, cols].astype(F32), 0.0).astype(BF)
+                gt_ref[:, cols] = d_o
+                causal = lax.broadcasted_iota(jnp.int32, (rows, width), 0) <= token
+                e_r = jnp.where(causal, jnp.exp2(dot_nn(k_hat, q_hat) * (scale * LOG2E)), 0.0)
+                eb_r = e_r.astype(BF)
+                er_ref[:, cols] = eb_r
+                ot_ref[:, cols] = dot_nn(r_val_t, eb_r)
+                dp_ref[:, cols] = dot_nn(r_val, d_o)
+                row_ref[0:1, cols] = q_inv
+                row_ref[1:2, cols] = jnp.sum(e_r, axis=0, keepdims=True)
+            for j, buf in enumerate((low, high, key)):
+                copy = pltpu.make_async_copy(buf.at[s], kept[j].at[s], out_sems.at[s, j])
+                copy.start()
+                sent.append(copy)
+        for copy in sent:
             copy.wait()
-        q_t = jnp.concatenate([q_buf[s, :, i * HD : (i + 1) * HD] for i in range(share)], axis=0).T
-        g_t = jnp.concatenate([g_buf[s, :, i * HD : (i + 1) * HD] for i in range(share)], axis=0).T
-        qt_ref[...] = q_t
-        raw_k = k_buf[s].astype(F32)
-        k_inv = lax.rsqrt(jnp.mean(raw_k * raw_k, axis=-1, keepdims=True) + EPS)
-        k_unit = raw_k * k_inv
-        k_hat = (k_unit * k_gain).astype(BF)
-        kh_ref[...] = k_hat
-        ku_ref[:, :HD] = k_unit
-        ku_ref[:, HD:] = jnp.broadcast_to(k_inv, (rows, HD))
-        r_val = v_buf[s]
-        r_val_t = r_val.T
-        for start in range(0, share * rows, width):
-            cols = slice(start, start + width)
-            token = (lax.broadcasted_iota(jnp.int32, (1, width), 1) + start) % rows
-            raw_q = q_t[:, cols].astype(F32)
-            q_inv = lax.rsqrt(jnp.mean(raw_q * raw_q, axis=0, keepdims=True) + EPS)
-            q_hat = (raw_q * q_inv * q_gain).astype(BF)
-            d_o = jnp.where(token < live_len, g_t[:, cols].astype(F32), 0.0).astype(BF)
-            gt_ref[:, cols] = d_o
-            causal = lax.broadcasted_iota(jnp.int32, (rows, width), 0) <= token
-            e_r = jnp.where(causal, jnp.exp2(dot_nn(k_hat, q_hat) * (scale * LOG2E)), 0.0)
-            eb_r = e_r.astype(BF)
-            er_ref[:, cols] = eb_r
-            ot_ref[:, cols] = dot_nn(r_val_t, eb_r)
-            dp_ref[:, cols] = dot_nn(r_val, d_o)
-            row_ref[0:1, cols] = q_inv
-            row_ref[1:2, cols] = jnp.sum(e_r, axis=0, keepdims=True)
-
-
-def prepare(meta, q, g, k, v, q_gain, k_gain, count):
+
+
+def prepare(turn, meta, q, g, k, v, q_gain, k_gain, count, kept):
     rows, q_width = q.shape
     share = q_width // k.shape[1]
-    total = share * rows
-    each = [
-        jax.ShapeDtypeStruct((HD, total), BF),
-        jax.ShapeDtypeStruct((HD, total), BF),
-        jax.ShapeDtypeStruct((8, total), F32),
-        jax.ShapeDtypeStruct((rows, total), BF),
-        jax.ShapeDtypeStruct((HD, total), F32),
-        jax.ShapeDtypeStruct((rows, total), F32),
-        jax.ShapeDtypeStruct((rows, HD), BF),
-        jax.ShapeDtypeStruct((rows, 2 * HD), F32),
-    ]
-    outs = pl.pallas_call(
-        functools.partial(prepare_kernel, count, share, rows, 2 * HD),
-        out_shape=each * count,
-        in_specs=[SMEM] + [HBM] * 4 + [VMEM] * 2,
-        out_specs=[VMEM] * (KEPT * count),
-        scratch_shapes=[
+    shapes = kept_shapes(count, rows, share * rows)
+    return pl.pallas_call(
+        functools.partial(prepare_kernel, count, share, rows, 2 * HD, turn),
+        out_shape=[jax.ShapeDtypeStruct(*x) for x in shapes],
+        in_specs=[SMEM] + [HBM] * 4 + [VMEM] * 2 + [HBM] * len(kept),
+        out_specs=[HBM] * 3,
+        scratch_shapes=[pltpu.VMEM(*x) for x in shapes]
+        + [
             pltpu.VMEM((count, rows, share * HD), BF),
             pltpu.VMEM((count, rows, share * HD), BF),
             pltpu.VMEM((count, rows, HD), BF),
             pltpu.VMEM((count, rows, HD), BF),
             pltpu.SemaphoreType.DMA((count, 4)),
+            pltpu.SemaphoreType.DMA((count, 3)),
         ],
-        compiler_params=params(16),
-        cost_estimate=pl.CostEstimate(
-            flops=6 * count * total * rows * HD,
-            bytes_accessed=5 * rows * q_width * 2,
-            transcendentals=count * total * rows,
-        ),
+        input_output_aliases={7 + i: i for i in range(len(kept))},
+        compiler_params=params(24),
         name="prepare_response",
-    )(meta, q, g, k, v, q_gain, k_gain)
-    return [list(outs[s * KEPT : (s + 1) * KEPT]) for s in range(count)]
+    )(meta, q, g, k, v, q_gain, k_gain, *kept)
+
+
+def fetch(slots, kept, bufs, sems):
+    copies = []
+    for i, s in enumerate(slots):
+        group = [
+            pltpu.make_async_copy(src.at[s], buf.at[i], sems.at[i, j])
+            for j, (src, buf) in enumerate(zip(kept, bufs))
+        ]
+        for copy in group:
+            copy.start()
+        copies.append(group)
+    return copies
+
+
+def fetch_scratch(count, kept):
+    shapes = [pltpu.VMEM((count,) + x.shape[1:], x.dtype) for x in kept]
+    return shapes + [pltpu.SemaphoreType.DMA((count, 3))]
 
 
 def attend(width, pr_ref, kept, q_gain, part_ref, at_ref, dq_ref):
@@ -155,7 +191,7 @@
     scale = HD ** (-0.5)
     p_key = pr_ref[0]
     p_val = pr_ref[1]
-    k_hat_t = kh_ref[...].T
+    k_hat_t = kh_ref[...].astype(BF).T
     p_key_t = p_key.T
     p_val_t = p_val.T
     sums = None
@@ -240,23 +276,25 @@
     return copies
 
 
-def whole_kernel(slots, width, meta, pr_ref, gain_ref, kg_ref, acc_ref, *rest):
+def whole_kernel(slots, width, meta, pr_ref, gain_ref, kg_ref, acc_ref, low, high, key, *rest):
     count = len(slots)
-    kept, rest = rest[: KEPT * count], rest[-13:]
     part_ref, gacc_ref, *rest = rest
-    outs, (at_ref, dq_ref), bufs, sems = rest[:4], rest[4:6], rest[6:10], rest[10]
+    outs, (at_ref, dq_ref), bufs, sems, store, got_sems = rest[:4], rest[4:6], rest[6:10], rest[10], rest[11:14], rest[14]
+    fetched = fetch(slots, (low, high, key), store, got_sems)
     q_gain = gain_ref[...]
     k_gain = kg_ref[...]
     q_sum, k_sum = acc_ref[0:1, :], acc_ref[1:2, :]
     copies = []
     for i, s in enumerate(slots):
-        mine = kept[i * KEPT : (i + 1) * KEPT]
+        for copy in fetched[i]:
+            copy.wait()
+        mine = views(*[x.at[i] for x in store])
         d_kr, d_vr, q_term, k_term = attend(
             width, pr_ref.at[i], mine, q_gain, part_ref.at[i], at_ref.at[i], dq_ref.at[i]
         )
         q_sum, k_sum = q_sum + q_term, k_sum + k_term
         copies += settle(
-            width, meta[s], meta[meta.shape[0] - 1], mine, q_gain, k_gain, at_ref.at[i], dq_ref.at[i],
+            width, meta[s], meta[meta.shape[0] - 2], mine, q_gain, k_gain, at_ref.at[i], dq_ref.at[i],
             d_kr, d_vr, outs, [buf.at[i] for buf in bufs], sems.at[i],
         )
     gacc_ref[0:1, :] = q_sum
@@ -265,15 +303,19 @@
         copy.wait()
 
 
-def first_kernel(slots, width, pr_ref, gain_ref, acc_ref, *rest):
+def first_kernel(slots, width, pr_ref, gain_ref, acc_ref, low, high, key, part_ref, gacc_ref, *rest):
     count = len(slots)
-    kept, (part_ref, gacc_ref, *results) = rest[: KEPT * count], rest[KEPT * count :]
+    results, store, got_sems = rest[: 4 * count], rest[4 * count : 4 * count + 3], rest[-1]
+    fetched = fetch(slots, (low, high, key), store, got_sems)
     q_gain = gain_ref[...]
     q_sum, k_sum = acc_ref[0:1, :], acc_ref[1:2, :]
     for i in range(count):
+        for copy in fetched[i]:
+            copy.wait()
         at_ref, dq_ref, dkr_ref, dvr_ref = results[4 * i : 4 * i + 4]
+        mine = views(*[x.at[i] for x in store])
         d_kr, d_vr, q_term, k_term = attend(
-            width, pr_ref.at[i], kept[i * KEPT : (i + 1) * KEPT], q_gain, part_ref.at[i], at_ref, dq_ref
+            width, pr_ref.at[i], mine, q_gain, part_ref.at[i], at_ref, dq_ref
         )
         q_sum, k_sum = q_sum + q_term, k_sum + k_term
         dkr_ref[...] = d_kr
@@ -282,15 +324,18 @@
     gacc_ref[1:2, :] = k_sum
 
 
-def second_kernel(slots, width, meta, gain_ref, kg_ref, *rest):
+def second_kernel(slots, width, meta, gain_ref, kg_ref, low, high, key, *rest):
     count = len(slots)
-    kept, results = rest[: KEPT * count], rest[KEPT * count : (KEPT + 4) * count]
-    outs, bufs, sems = rest[-9:-5], rest[-5:-1], rest[-1]
+    results, rest = rest[: 4 * count], rest[-13:]
+    outs, bufs, sems, store, got_sems = rest[:4], rest[4:8], rest[8], rest[9:12], rest[12]
+    fetched = fetch(slots, (low, high, key), store, got_sems)
     copies = []
     for i, s in enumerate(slots):
+        for copy in fetched[i]:
+            copy.wait()
         at_ref, dq_ref, dkr_ref, dvr_ref = results[4 * i : 4 * i + 4]
         copies += settle(
-            width, meta[s], meta[meta.shape[0] - 1], kept[i * KEPT : (i + 1) * KEPT], gain_ref[...],
+            width, meta[s], meta[meta.shape[0] - 2], views(*[x.at[i] for x in store]), gain_ref[...],
             kg_ref[...], at_ref, dq_ref, dkr_ref[...], dvr_ref[...], outs,
             [buf.at[i] for buf in bufs], sems.at[i],
         )
@@ -308,11 +353,10 @@
     return [pltpu.VMEM((count, rows, w), BF) for w in widths] + [pltpu.SemaphoreType.DMA((count, 4))]
 
 
-def whole_heads(slots, meta, prompt, kept, q_gain, k_gain, acc, buffers, q_width, k_width):
+def whole_heads(slots, meta, prompt, kept, q_gain, k_gain, acc, q_width, k_width):
     count = len(slots)
-    total = kept[0][0].shape[1]
-    rows = kept[0][3].shape[0]
-    flat = [x for s in slots for x in kept[s]]
+    total = kept[0].shape[2]
+    rows = kept[2].shape[1]
     outs = pl.pallas_call(
         functools.partial(whole_kernel, slots, 2 * HD),
         out_shape=[
@@ -320,21 +364,20 @@
             jax.ShapeDtypeStruct(acc.shape, F32),
         ]
         + out_shapes(rows, q_width, k_width),
-        in_specs=[SMEM] + [VMEM] * (4 + len(flat)) + [HBM] * len(buffers),
+        in_specs=[SMEM] + [VMEM] * 4 + [HBM] * 3,
         out_specs=[VMEM] * 2 + [HBM] * 4,
         scratch_shapes=[pltpu.VMEM((count, HD, total), BF), pltpu.VMEM((count, HD, total), F32)]
-        + out_scratch(count, rows, total // rows),
-        input_output_aliases={5 + len(flat) + i: 2 + i for i in range(len(buffers))},
-        compiler_params=params(16),
+        + out_scratch(count, rows, total // rows)
+        + fetch_scratch(count, kept),
+        compiler_params=params(24),
         name="attend_own_half",
-    )(meta, prompt, q_gain, k_gain, acc, *flat, *buffers)
+    )(meta, prompt, q_gain, k_gain, acc, *kept)
     return outs[0], outs[1], list(outs[2:])
 
 
 def first_part(slots, prompt, kept, q_gain, acc):
-    total = kept[0][0].shape[1]
-    rows = kept[0][3].shape[0]
-    flat = [x for s in slots for x in kept[s]]
+    total = kept[0].shape[2]
+    rows = kept[2].shape[1]
     each = [
         jax.ShapeDtypeStruct((HD, total), BF),
         jax.ShapeDtypeStruct((HD, total), F32),
@@ -348,29 +391,29 @@
             jax.ShapeDtypeStruct(acc.shape, F32),
         ]
         + each * len(slots),
-        in_specs=[VMEM] * (3 + len(flat)),
+        in_specs=[VMEM] * 3 + [HBM] * 3,
         out_specs=[VMEM] * (2 + 4 * len(slots)),
-        compiler_params=params(16),
+        scratch_shapes=fetch_scratch(len(slots), kept),
+        compiler_params=params(24),
         name="attend_other_half",
-    )(prompt, q_gain, acc, *flat)
+    )(prompt, q_gain, acc, *kept)
     return outs[0], outs[1], list(outs[2:])
 
 
 def second_part(slots, meta, kept, q_gain, k_gain, results, buffers):
     count = len(slots)
-    total = kept[0][0].shape[1]
-    rows = kept[0][3].shape[0]
-    flat = [x for s in slots for x in kept[s]]
+    total = kept[0].shape[2]
+    rows = kept[2].shape[1]
     return pl.pallas_call(
         functools.partial(second_kernel, slots, 2 * HD),
         out_shape=out_shapes(rows, buffers[0].shape[1], buffers[2].shape[1]),
-        in_specs=[SMEM] + [VMEM] * (2 + len(flat) + len(results)) + [HBM] * 4,
+        in_specs=[SMEM] + [VMEM] * 2 + [HBM] * 3 + [VMEM] * len(results) + [HBM] * 4,
         out_specs=[HBM] * 4,
-        scratch_shapes=out_scratch(count, rows, total // rows),
-        input_output_aliases={3 + len(flat) + len(results) + i: i for i in range(4)},
-        compiler_params=params(16),
+        scratch_shapes=out_scratch(count, rows, total // rows) + fetch_scratch(count, kept),
+        input_output_aliases={6 + len(results) + i: i for i in range(4)},
+        compiler_params=params(24),
         name="settle_other_half",
-    )(meta, q_gain, k_gain, *flat, *results, *buffers)
+    )(meta, q_gain, k_gain, *kept, *results, *buffers)
 
 
 def place_kernel(meta, *refs):
@@ -427,9 +470,10 @@
     order = jnp.arange(kv_heads, dtype=jnp.int32)
     if pairs:
         order = (order + (me % 2) * per) % kv_heads
-    meta = jnp.concatenate([order, live_len[None]])
+    turn = lax.axis_index("dp") % 2 if pairs else jnp.int32(0)
+    meta = jnp.concatenate([order, jnp.stack([live_len, turn.astype(jnp.int32)])])
     q, g, k, v = [pltpu.with_memory_space_constraint(x, pltpu.HBM) for x in (q, g, k, v)]
-    kept = prepare(meta, q, g, k, v, gain_col, gain_row, kv_heads)
+    kept = prepare(0, meta, q, g, k, v, gain_col, gain_row, kv_heads, ())
     acc = jnp.zeros((2, HD), F32)
 
     def swap(x, step, axis="group", size=n_group):
@@ -441,28 +485,37 @@
     if pairs:
         own, other = tuple(range(per)), tuple(range(per, kv_heads))
         mine, theirs = cut(order, pltpu.with_memory_space_constraint(cache, pltpu.HBM), 2, per)
-        got = after(swap(theirs, 1), kept[0][2])
+        got = swap(after(theirs, kept[2]), 1)
+        kept = prepare(1, meta, q, g, k, v, gain_col, gain_row, kv_heads, kept)
+        got = after(got, kept[2])
         mine = jnp.where(owner == me ^ 1, got, mine)
         got = swap(mine, 2)
         mine = jnp.where(owner // 2 == me // 2, mine, got)
         theirs = swap(mine, 1)
         part, acc, buffers = whole_heads(
-            own, meta, mine, kept, gain_col, gain_row, acc, (), q.shape[1], k.shape[1]
+            own, meta, mine, kept, gain_col, gain_row, acc, q.shape[1], k.shape[1]
         )
         sent, acc, results = first_part(other, after(theirs, part), kept, gain_col, acc)
+        gains = acc + swap(acc, 1)
+        gains = gains + swap(gains, 2)
+        part = join(part, after(swap(sent, 1), gains))
+        results[0] = after(results[0], part)
         buffers = list(second_part(other, meta, kept, gain_col, gain_row, results, buffers))
-        gains = acc + swap(acc, 1)
-        part = join(part, after(swap(sent, 1), gains, buffers[2]))
         gains = after(gains, part)
-        gains = gains + swap(gains, 2)
-        gains = pair_sum(gains, "dp", n_dp)
-        part = join(part, after(swap(part, 2), gains))
-        placed = place(jnp.concatenate([mine_flag[None], order]), [part, swap(part, 1)])
+        step = 1
+        while 2 * step < n_dp:
+            gains = gains + swap(gains, step, "dp", n_dp)
+            step *= 2
+        part = join(part, after(swap(part, 2), gains, buffers[2]))
+        back = swap(part, 1)
+        gains = after(gains, part)
+        gains = gains + swap(gains, step, "dp", n_dp)
+        placed = place(jnp.concatenate([mine_flag[None], order]), [part, back])
     else:
         cache = lax.psum(jnp.where(me == owner, cache, jnp.zeros_like(cache)), "group")
         (prompt,) = cut(order, cache, 1, kv_heads)
         part, acc, buffers = whole_heads(
-            tuple(range(kv_heads)), meta, prompt, kept, gain_col, gain_row, acc, (), q.shape[1], k.shape[1]
+            tuple(range(kv_heads)), meta, prompt, kept, gain_col, gain_row, acc, q.shape[1], k.shape[1]
         )
         total = jnp.transpose(part, (1, 2, 0, 3)).reshape(depth, p_rows, kv_heads * HD)
         total = lax.psum(total.astype(F32), "group").astype(BF)

time: 103 us -> 90.7 us (0.88); the launches traced: 102 us -> 91.8 us
  local copies, waits for them, and re-layouts: 25.1 us -> 14.8 us
  Pallas kernels: 18.5 us -> 26.4 us
  waiting for transfers between devices: 37.1 us -> 32.5 us
  other arithmetic: 4.26 us -> 0.96 us
    unnamed x88 -> x26, local copies, waits for them, and re-layouts: 24.9 us -> 14 us
    ppermute x3 -> x0, waiting for transfers between devices: 5.22 us -> none  [pair_sum(): lax.ppermute(value, axis, [(i, i ^ step) for i in range(size)])]
    ppermute x3 -> x0, starting transfers between devices: 5.16 us -> none  [pair_sum(): lax.ppermute(value, axis, [(i, i ^ step) for i in range(size)])]
    ppermute x8 -> x11, starting transfers between devices: 9.92 us -> 15 us  [swap(): return lax.ppermute(x, axis, [(i, i ^ step) for i in range(size)])]
    pallas_call x1 -> x2, Pallas kernels: 5.13 us -> 8.79 us  [prepare(): pl.pallas_call(functools.partial(prepare_kernel, count, share, rows, 2 *...]
    select_n x1, other arithmetic: 1.89 us -> 0.03 us  [local(): mine = jnp.where(owner == me ^ 1, got, mine)]
    pallas_call x1, Pallas kernels: 1.97 us -> 3.66 us  [second_part(): pl.pallas_call(functools.partial(second_kernel, slots, 2 * HD), out_shape...]
    pallas_call x1, Pallas kernels: 4.5 us -> 6.15 us  [whole_heads(): pl.pallas_call(functools.partial(whole_kernel, slots, 2 * HD), out_shape=...]
  transfers between devices with their start and end apart: 11 -> 11, of which waited for: 7 -> 7; matrix products, arithmetic and copies ran while one was open for 1% -> 1% of each run, Pallas kernels for 11% -> 12%
where the time goes in v10:
time: 90.7 us; the launch traced here: 91.8 us
  waiting for transfers between devices  32.5 us (36%)
  Pallas kernels  26.4 us (29%)
  starting transfers between devices  15 us (17%)
  local copies, waits for them, and re-layouts  14.8 us (16%)
  between operations  2.13 us (2%)
  other arithmetic  0.96 us (1%)
    ppermute x11, waiting for transfers between devices, swap(): return lax.ppermute(x, axis, [(i, i ^ step) for i in range(size)])  32.5 us
    ppermute x11, starting transfers between devices, swap(): return lax.ppermute(x, axis, [(i, i ^ step) for i in range(size)])  15 us
    unnamed x26, local copies, waits for them, and re-layouts  14 us
    pallas_call x2, Pallas kernels, prepare(): pl.pallas_call(functools.partial(prepare_kernel, count, share, rows, 2 *...  8.79 us
    pallas_call x1, Pallas kernels, whole_heads(): pl.pallas_call(functools.partial(whole_kernel, slots, 2 * HD), out_shape=...  6.15 us
    pallas_call x1, Pallas kernels, first_part(): pl.pallas_call(functools.partial(first_kernel, slots, 2 * HD), out_shape=...  4.69 us
    pallas_call x1, Pallas kernels, second_part(): pl.pallas_call(functools.partial(second_kernel, slots, 2 * HD), out_shape...  3.66 us
  transfers between devices with their start and end apart: 11, of which 7 were waited for; matrix products, arithmetic and copies ran while one was open for 1% of the time, Pallas kernels for 12%

profile of v10, /device:TPU:0, one launch (start us, length us, event | category | flops | bytes accessed | tf_op | source)
XLA Modules:
  0.0 91.8 jit_solution(6858203855349950549)
XLA Ops:
  1.3 0.8 copy.26.gain_ref
  2.1 1.7 %cut_prompt.1 = (bf16[2,2,256,128]{3,2,1,0:T(8,128)(2,1)S(1)}, bf16[2,2,256,128]{3,2,1,0:T(8,128)(2,1)S(1)}) custom-call(s32[4]{0:T(128)S(1)} %and_select_fusion.order, bf16[2,256,512]{2,1,0:T(8,128)(2,1)} %bitcast.37), custom_call_target="tpu_custom_call" | custom-call | tf_op jit(solution)/shard_map/cut_prompt/pallas_call | solution.py:50
  3.8 0.1 pad_add_fusion.meta
  3.8 0.0 copy-start.10
  3.9 0.7 copy-done.10
  4.5 7.8 %prepare_response.2 = (bf16[4,448,768]{2,1,0:T(8,128)(2,1)S(1)}, f32[4,328,768]{2,1,0:T(8,128)S(1)}, f32[4,192,384]{2,1,0:T(8,128)S(1)}) custom-call(s32[6]{0:T(128)S(1)} %pad_add_fusion.meta, bf16[192,2048]{1,0:T(8,128)(2,1)} %bitcast.27, bf16[192,2048]{1,0:T(8,128)(2,1)} %bitcast.29, bf16[192,512]{1,0:T(8,128)(2,1)} %bitcast.33, ...), custom_call_target="tpu_custom_call" | custom-call | tf_op jit(solution)/shard_map/prepare_response/pallas_call | solution.py:151
  12.3 0.0 copy-start
  12.3 1.9 %copy-done = f32[4,328,768]{2,1,0:T(8,128)} copy-done((f32[4,328,768]{2,1,0:T(8,128)}, f32[4,328,768]{2,1,0:T(8,128)S(1)}, u32[]{:S(2)}) %copy-start) | copy-done | bytes 4030488
  14.2 0.0 copy-start.5
  14.2 1.0 %copy-done.5 = f32[4,192,384]{2,1,0:T(8,128)} copy-done((f32[4,192,384]{2,1,0:T(8,128)}, f32[4,192,384]{2,1,0:T(8,128)S(1)}, u32[]{:S(2)}) %copy-start.5) | copy-done | bytes 1179672
  15.3 3.0 %collective-permute-start = (bf16[2,2,256,128]{3,2,1,0:T(8,128)(2,1)S(1)}, bf16[2,2,256,128]{3,2,1,0:T(8,128)(2,1)}, u32[]{:S(2)}, u32[]{:S(2)}) collective-permute-start(bf16[2,2,256,128]{3,2,1,0:T(8,128)(2,1)S(1)} %get-tuple-element.49), channel_id=1, source_target_pairs={{0,1},{1,0},{2,3},{3,2},{4,5},{5,4},{6,7},{7,6},{8,9},{9,8},{10,11... | collective-permute-start | bytes 786440 | tf_op jit(solution)/shard_map/ppermute | solution.py:480
  19.0 0.0 copy-start.1
  19.0 2.1 %copy-done.1 = f32[4,328,768]{2,1,0:T(8,128)S(1)} copy-done((f32[4,328,768]{2,1,0:T(8,128)S(1)}, f32[4,328,768]{2,1,0:T(8,128)}, u32[]{:S(2)}) %copy-start.1) | copy-done | bytes 4030488
  21.1 0.0 copy-start.6
  21.1 1.3 %copy-done.6 = f32[4,192,384]{2,1,0:T(8,128)S(1)} copy-done((f32[4,192,384]{2,1,0:T(8,128)S(1)}, f32[4,192,384]{2,1,0:T(8,128)}, u32[]{:S(2)}) %copy-start.6) | copy-done | bytes 1179672
  22.4 0.0 copy-start.11
  22.4 0.7 copy-done.11
  23.0 0.0 copy-start.12
  23.0 1.0 %prepare_response.3 = (bf16[4,448,768]{2,1,0:T(8,128)(2,1)S(1)}, f32[4,328,768]{2,1,0:T(8,128)S(1)}, f32[4,192,384]{2,1,0:T(8,128)S(1)}) custom-call(s32[6]{0:T(128)S(1)} %pad_add_fusion.meta, bf16[192,2048]{1,0:T(8,128)(2,1)} %bitcast.28, bf16[192,2048]{1,0:T(8,128)(2,1)} %bitcast.30, ...), custom_call_target="tpu_custom_call", output_to_operand_aliasing={{0}: (7, {}), {1}: (8, {}), {2}: (9, {})} | custom-call | tf_op jit(solution)/shard_map/prepare_response/pallas_call | solution.py:151
  24.0 0.0 copy-start.2
  24.0 1.9 %copy-done.2 = f32[4,328,768]{2,1,0:T(8,128)} copy-done((f32[4,328,768]{2,1,0:T(8,128)}, f32[4,328,768]{2,1,0:T(8,128)S(1)}, u32[]{:S(2)}) %copy-start.2) | copy-done | bytes 4030488
  25.9 0.0 copy-start.7
  25.9 1.0 %copy-done.7 = f32[4,192,384]{2,1,0:T(8,128)} copy-done((f32[4,192,384]{2,1,0:T(8,128)}, f32[4,192,384]{2,1,0:T(8,128)S(1)}, u32[]{:S(2)}) %copy-start.7) | copy-done | bytes 1179672
  27.0 0.0 collective-permute-done
  27.0 2.7 %collective-permute-start.1 = (bf16[2,2,256,128]{3,2,1,0:T(8,128)(2,1)S(1)}, bf16[2,2,256,128]{3,2,1,0:T(8,128)(2,1)S(1)}, u32[]{:S(2)}, u32[]{:S(2)}) collective-permute-start(bf16[2,2,256,128]{3,2,1,0:T(8,128)(2,1)S(1)} %broadcast_select_fusion), channel_id=1, source_target_pairs={{0,2},{1,3},{2,0},{3,1},{4,6},{5,7},{6,4},{7,5},{8,10},{9,11},{10,... | collective-permute-start | bytes 786440 | tf_op jit(solution)/shard_map/ppermute | solution.py:480
  29.7 11.7 %collective-permute-done.1 = bf16[2,2,256,128]{3,2,1,0:T(8,128)(2,1)S(1)} collective-permute-done((bf16[2,2,256,128]{3,2,1,0:T(8,128)(2,1)S(1)}, bf16[2,2,256,128]{3,2,1,0:T(8,128)(2,1)S(1)}, u32[]{:S(2)}, u32[]{:S(2)}) %collective-permute-start.1) | collective-permute-done | bytes 262176 | tf_op jit(solution)/shard_map/ppermute | solution.py:480
  41.4 0.7 collective-permute-start.2
  42.0 0.0 copy-done.12
  42.1 0.0 copy-start.3
  42.1 2.1 %copy-done.3 = f32[4,328,768]{2,1,0:T(8,128)S(1)} copy-done((f32[4,328,768]{2,1,0:T(8,128)S(1)}, f32[4,328,768]{2,1,0:T(8,128)}, u32[]{:S(2)}) %copy-start.3) | copy-done | bytes 4030488
  44.2 0.0 copy-start.8
  44.2 1.3 %copy-done.8 = f32[4,192,384]{2,1,0:T(8,128)S(1)} copy-done((f32[4,192,384]{2,1,0:T(8,128)S(1)}, f32[4,192,384]{2,1,0:T(8,128)}, u32[]{:S(2)}) %copy-start.8) | copy-done | bytes 1179672
  45.5 0.0 copy-start.4
  45.5 0.0 copy-start.9
  45.5 6.2 %attend_own_half.1 = (bf16[2,2,256,128]{3,2,1,0:T(8,128)(2,1)S(1)}, f32[2,128]{1,0:T(2,128)S(1)}, bf16[192,2048]{1,0:T(8,128)(2,1)}, bf16[192,2048]{1,0:T(8,128)...) custom-call(s32[6]{0:T(128)S(1)} %pad_add_fusion.meta, ...), custom_call_target="tpu_custom_call" | custom-call | tf_op jit(solution)/shard_map/attend_own_half/pallas_call | solution.py:360
  51.6 0.0 collective-permute-done.2.pr_ref
  51.6 0.0 copy-done.4
  51.6 0.0 copy-done.9
  51.7 4.7 %attend_other_half.1 = (bf16[2,2,256,128]{3,2,1,0:T(8,128)(2,1)S(1)}, f32[2,128]{1,0:T(2,128)S(1)}, bf16[128,768]{1,0:T(8,128)(2,1)S(1)}, f32[128,768]{1,0:T(8,1...) custom-call(bf16[2,2,256,128]{3,2,1,0:T(8,128)(2,1)S(1)} %collective, ...), custom_call_target="tpu_custom_call" | custom-call | tf_op jit(solution)/shard_map/attend_other_half/pallas_call | solution.py:387
  56.4 1.5 %collective-permute-start.3 = (bf16[2,2,256,128]{3,2,1,0:T(8,128)(2,1)S(1)}, bf16[2,2,256,128]{3,2,1,0:T(8,128)(2,1)S(1)}, u32[]{:S(2)}, u32[]{:S(2)}) collective-permute-start(bf16[2,2,256,128]{3,2,1,0:T(8,128)(2,1)S(1)} %get-tuple-element.56), channel_id=1, source_target_pairs={{0,1},{1,0},{2,3},{3,2},{4,5},{5,4},{6,7},{7,6},{8,9},{9,8},{10,11... | collective-permute-start | bytes 786440 | tf_op jit(solution)/shard_map/ppermute | solution.py:480
  57.8 0.6 collective-permute-start.4
  58.4 5.9 %collective-permute-done.4 = f32[2,128]{1,0:T(2,128)S(1)} collective-permute-done((f32[2,128]{1,0:T(2,128)S(1)}, f32[2,128]{1,0:T(2,128)S(1)}, u32[]{:S(2)}, u32[]{:S(2)}) %collective-permute-start.4) | collective-permute-done | bytes 1056 | tf_op jit(solution)/shard_map/ppermute | solution.py:480
  64.4 3.4 %collective-permute-start.5 = (f32[2,128]{1,0:T(2,128)S(1)}, f32[2,128]{1,0:T(2,128)S(1)}, u32[]{:S(2)}, u32[]{:S(2)}) collective-permute-start(f32[2,128]{1,0:T(2,128)S(1)} %add.47), channel_id=1, source_target_pairs={{0,2},{1,3},{2,0},{3,1},{4,6},{5,7},{6,4},{7,5},{8,10},{9,11},{10,... | collective-permute-start | bytes 3080 | tf_op jit(solution)/shard_map/ppermute | solution.py:480
  67.7 1.5 %collective-permute-done.5 = f32[2,128]{1,0:T(2,128)S(1)} collective-permute-done((f32[2,128]{1,0:T(2,128)S(1)}, f32[2,128]{1,0:T(2,128)S(1)}, u32[]{:S(2)}, u32[]{:S(2)}) %collective-permute-start.5) | collective-permute-done | bytes 1056 | tf_op jit(solution)/shard_map/ppermute | solution.py:480
  69.3 0.0 collective-permute-done.3
  69.3 0.1 add_convert_fusion.1
  69.4 3.0 %collective-permute-start.6 = (bf16[2,2,256,128]{3,2,1,0:T(8,128)(2,1)S(1)}, bf16[2,2,256,128]{3,2,1,0:T(8,128)(2,1)S(1)}, u32[]{:S(2)}, u32[]{:S(2)}) collective-permute-start(bf16[2,2,256,128]{3,2,1,0:T(8,128)(2,1)S(1)} %add_convert_fusion.1), channel_id=1, source_target_pairs={{0,2},{1,3},{2,0},{3,1},{4,6},{5,7},{6,4},{7,5},{8,10},{9,11},{10,... | collective-permute-start | bytes 786440 | tf_op jit(solution)/shard_map/ppermute | solution.py:480
  72.4 0.0 collective-permute-start.7
  72.4 1.1 %collective-permute-done.7 = f32[2,128]{1,0:T(2,128)S(1)} collective-permute-done((f32[2,128]{1,0:T(2,128)S(1)}, f32[2,128]{1,0:T(2,128)S(1)}, u32[]{:S(2)}, u32[]{:S(2)}) %collective-permute-start.7) | collective-permute-done | bytes 1056 | tf_op jit(solution)/shard_map/ppermute | solution.py:480
  73.5 0.0 collective-permute-start.8
  73.5 3.7 %settle_other_half.1 = (bf16[192,2048]{1,0:T(8,128)(2,1)}, bf16[192,2048]{1,0:T(8,128)(2,1)}, bf16[192,512]{1,0:T(8,128)(2,1)}, bf16[192,512]{1,0:T(8,128)(2,1)}) custom-call(s32[6]{0:T(128)S(1)} %pad_add_fusion.meta, f32[128,1]{1,0:T(8,128)S(1)} %copy.26.gain_ref, ...), custom_call_target="tpu_custom_call", output_to_operand_aliasing={{0}: (14, {}), {1}: (15, {}), {2}: (16, {}), {3}: (17, {})} | custom-call | tf_op jit(solution)/shard_map/settle_other_half/pallas_call | solution.py:407
  77.2 0.0 collective-permute-done.8
  77.2 4.8 %collective-permute-done.6 = bf16[2,2,256,128]{3,2,1,0:T(8,128)(2,1)S(1)} collective-permute-done((bf16[2,2,256,128]{3,2,1,0:T(8,128)(2,1)S(1)}, bf16[2,2,256,128]{3,2,1,0:T(8,128)(2,1)S(1)}, u32[]{:S(2)}, u32[]{:S(2)}) %collective-permute-start.6) | collective-permute-done | bytes 262176 | tf_op jit(solution)/shard_map/ppermute | solution.py:480
  82.0 0.1 add_convert_fusion.refs_0_
  82.1 0.1 collective-permute-start.9
  82.2 0.1 collective-permute-start.10
  82.3 0.1 pad_add_fusion.1.meta
  82.3 3.5 %collective-permute-done.10 = f32[2,128]{1,0:T(2,128)S(1)} collective-permute-done((f32[2,128]{1,0:T(2,128)S(1)}, f32[2,128]{1,0:T(2,128)S(1)}, u32[]{:S(2)}, u32[]{:S(2)}) %collective-permute-start.10) | collective-permute-done | bytes 1056 | tf_op jit(solution)/shard_map/ppermute | solution.py:480
  85.8 0.6 add.53
  86.4 3.9 %collective-permute-done.9.refs_1_ = bf16[2,2,256,128]{3,2,1,0:T(8,128)(2,1)S(1)} collective-permute-done((bf16[2,2,256,128]{3,2,1,0:T(8,128)(2,1)S(1)}, bf16[2,2,256,128]{3,2,1,0:T(8,128)(2,1)S(1)}, u32[]{:S(2)}, u32[]{:S(2)}) %collective-permute-start.9) | collective-permute-done | bytes 262176 | tf_op jit(solution)/shard_map/ppermute | solution.py:480
  90.3 1.4 %place_prompt_grad.1 = bf16[2,256,512]{2,1,0:T(8,128)(2,1)} custom-call(s32[5]{0:T(128)S(1)} %pad_add_fusion.1.meta, bf16[2,2,256,128]{3,2,1,0:T(8,128)(2,1)S(1)} %add_convert_fusion.refs_0_, bf16[2,2,256,128]{3,2,1,0:T(8,128)(2,1)S(1)} %collective-permute-done.9.refs_1_), custom_call_target="tpu_custom_call" | custom-call | tf_op jit(solution)/shard_map/place_prompt_grad/pallas_call | solution.py:432
  (8 shorter events, 0.1 us)
Async XLA Ops:
  3.8 0.7 copy-start.10
  12.3 1.9 %copy-start = (f32[4,328,768]{2,1,0:T(8,128)}, f32[4,328,768]{2,1,0:T(8,128)S(1)}, u32[]{:S(2)}) copy-start(f32[4,328,768]{2,1,0:T(8,128)S(1)} %get-tuple-element.43.rest_1_) | copy-start | bytes 12091396
  14.2 1.0 %copy-start.5 = (f32[4,192,384]{2,1,0:T(8,128)}, f32[4,192,384]{2,1,0:T(8,128)S(1)}, u32[]{:S(2)}) copy-start(f32[4,192,384]{2,1,0:T(8,128)S(1)} %get-tuple-element.44.rest_2_) | copy-start | bytes 3538948
  15.3 11.7 %collective-permute-start = (bf16[2,2,256,128]{3,2,1,0:T(8,128)(2,1)S(1)}, bf16[2,2,256,128]{3,2,1,0:T(8,128)(2,1)}, u32[]{:S(2)}, u32[]{:S(2)}) collective-permute-start(bf16[2,2,256,128]{3,2,1,0:T(8,128)(2,1)S(1)} %get-tuple-element.49), channel_id=1, source_target_pairs={{0,1},{1,0},{2,3},{3,2},{4,5},{5,4},{6,7},{7,6},{8,9},{9,8},{10,11... | collective-permute-start | bytes 786440 | tf_op jit(solution)/shard_map/ppermute | solution.py:480
  19.0 2.1 %copy-start.1 = (f32[4,328,768]{2,1,0:T(8,128)S(1)}, f32[4,328,768]{2,1,0:T(8,128)}, u32[]{:S(2)}) copy-start(f32[4,328,768]{2,1,0:T(8,128)} %copy-done) | copy-start | bytes 12091396
  21.1 1.3 %copy-start.6 = (f32[4,192,384]{2,1,0:T(8,128)S(1)}, f32[4,192,384]{2,1,0:T(8,128)}, u32[]{:S(2)}) copy-start(f32[4,192,384]{2,1,0:T(8,128)} %copy-done.5) | copy-start | bytes 3538948
  22.4 0.7 copy-start.11
  23.0 19.0 %copy-start.12 = (f32[128]{0:T(128)S(1)}, f32[128]{0:T(128)}, u32[]{:S(2)}) copy-start(f32[128]{0:T(128)} %param.16) | copy-start | bytes 1540
  24.0 1.9 %copy-start.2 = (f32[4,328,768]{2,1,0:T(8,128)}, f32[4,328,768]{2,1,0:T(8,128)S(1)}, u32[]{:S(2)}) copy-start(f32[4,328,768]{2,1,0:T(8,128)S(1)} %get-tuple-element.46.high) | copy-start | bytes 12091396
  25.9 1.0 %copy-start.7 = (f32[4,192,384]{2,1,0:T(8,128)}, f32[4,192,384]{2,1,0:T(8,128)S(1)}, u32[]{:S(2)}) copy-start(f32[4,192,384]{2,1,0:T(8,128)S(1)} %get-tuple-element.47.key) | copy-start | bytes 3538948
  27.0 14.3 %collective-permute-start.1 = (bf16[2,2,256,128]{3,2,1,0:T(8,128)(2,1)S(1)}, bf16[2,2,256,128]{3,2,1,0:T(8,128)(2,1)S(1)}, u32[]{:S(2)}, u32[]{:S(2)}) collective-permute-start(bf16[2,2,256,128]{3,2,1,0:T(8,128)(2,1)S(1)} %broadcast_select_fusion), channel_id=1, source_target_pairs={{0,2},{1,3},{2,0},{3,1},{4,6},{5,7},{6,4},{7,5},{8,10},{9,11},{10,... | collective-permute-start | bytes 786440 | tf_op jit(solution)/shard_map/ppermute | solution.py:480
  41.4 10.3 %collective-permute-start.2 = (bf16[2,2,256,128]{3,2,1,0:T(8,128)(2,1)S(1)}, bf16[2,2,256,128]{3,2,1,0:T(8,128)(2,1)S(1)}, u32[]{:S(2)}, u32[]{:S(2)}) collective-permute-start(bf16[2,2,256,128]{3,2,1,0:T(8,128)(2,1)S(1)} %broadcast_select_fusion.1.pr_ref), channel_id=1, source_target_pairs={{0,1},{1,0},{2,3},{3,2},{4,5},{5,4},{6,7},{7,6},{8,9},{9,8},{10,11... | collective-permute-start | bytes 786440 | tf_op jit(solution)/shard_map/ppermute | solution.py:480
  42.1 2.1 %copy-start.3 = (f32[4,328,768]{2,1,0:T(8,128)S(1)}, f32[4,328,768]{2,1,0:T(8,128)}, u32[]{:S(2)}) copy-start(f32[4,328,768]{2,1,0:T(8,128)} %copy-done.2) | copy-start | bytes 12091396
  44.2 1.3 %copy-start.8 = (f32[4,192,384]{2,1,0:T(8,128)S(1)}, f32[4,192,384]{2,1,0:T(8,128)}, u32[]{:S(2)}) copy-start(f32[4,192,384]{2,1,0:T(8,128)} %copy-done.7) | copy-start | bytes 3538948
  45.5 6.2 %copy-start.4 = (f32[4,328,768]{2,1,0:T(8,128)S(1)}, f32[4,328,768]{2,1,0:T(8,128)}, u32[]{:S(2)}) copy-start(f32[4,328,768]{2,1,0:T(8,128)} %copy-done.2) | copy-start | bytes 12091396
  45.5 6.2 %copy-start.9 = (f32[4,192,384]{2,1,0:T(8,128)S(1)}, f32[4,192,384]{2,1,0:T(8,128)}, u32[]{:S(2)}) copy-start(f32[4,192,384]{2,1,0:T(8,128)} %copy-done.7) | copy-start | bytes 3538948
  56.4 12.9 %collective-permute-start.3 = (bf16[2,2,256,128]{3,2,1,0:T(8,128)(2,1)S(1)}, bf16[2,2,256,128]{3,2,1,0:T(8,128)(2,1)S(1)}, u32[]{:S(2)}, u32[]{:S(2)}) collective-permute-start(bf16[2,2,256,128]{3,2,1,0:T(8,128)(2,1)S(1)} %get-tuple-element.56), channel_id=1, source_target_pairs={{0,1},{1,0},{2,3},{3,2},{4,5},{5,4},{6,7},{7,6},{8,9},{9,8},{10,11... | collective-permute-start | bytes 786440 | tf_op jit(solution)/shard_map/ppermute | solution.py:480
  57.8 6.5 %collective-permute-start.4 = (f32[2,128]{1,0:T(2,128)S(1)}, f32[2,128]{1,0:T(2,128)S(1)}, u32[]{:S(2)}, u32[]{:S(2)}) collective-permute-start(f32[2,128]{1,0:T(2,128)S(1)} %get-tuple-element.57), channel_id=1, source_target_pairs={{0,1},{1,0},{2,3},{3,2},{4,5},{5,4},{6,7},{7,6},{8,9},{9,8},{10,11... | collective-permute-start | bytes 3080 | tf_op jit(solution)/shard_map/ppermute | solution.py:480
  64.4 4.9 %collective-permute-start.5 = (f32[2,128]{1,0:T(2,128)S(1)}, f32[2,128]{1,0:T(2,128)S(1)}, u32[]{:S(2)}, u32[]{:S(2)}) collective-permute-start(f32[2,128]{1,0:T(2,128)S(1)} %add.47), channel_id=1, source_target_pairs={{0,2},{1,3},{2,0},{3,1},{4,6},{5,7},{6,4},{7,5},{8,10},{9,11},{10,... | collective-permute-start | bytes 3080 | tf_op jit(solution)/shard_map/ppermute | solution.py:480
  69.4 12.6 %collective-permute-start.6 = (bf16[2,2,256,128]{3,2,1,0:T(8,128)(2,1)S(1)}, bf16[2,2,256,128]{3,2,1,0:T(8,128)(2,1)S(1)}, u32[]{:S(2)}, u32[]{:S(2)}) collective-permute-start(bf16[2,2,256,128]{3,2,1,0:T(8,128)(2,1)S(1)} %add_convert_fusion.1), channel_id=1, source_target_pairs={{0,2},{1,3},{2,0},{3,1},{4,6},{5,7},{6,4},{7,5},{8,10},{9,11},{10,... | collective-permute-start | bytes 786440 | tf_op jit(solution)/shard_map/ppermute | solution.py:480
  72.4 1.1 %collective-permute-start.7 = (f32[2,128]{1,0:T(2,128)S(1)}, f32[2,128]{1,0:T(2,128)S(1)}, u32[]{:S(2)}, u32[]{:S(2)}) collective-permute-start(f32[2,128]{1,0:T(2,128)S(1)} %add.48), channel_id=1, source_target_pairs={{0,4},{4,0},{8,12},{12,8},{16,20},{20,16},{24,28},{28,24},{1,5},{5... | collective-permute-start | bytes 3080 | tf_op jit(solution)/shard_map/ppermute | solution.py:480
  73.5 3.7 %collective-permute-start.8 = (f32[2,128]{1,0:T(2,128)S(1)}, f32[2,128]{1,0:T(2,128)S(1)}, u32[]{:S(2)}, u32[]{:S(2)}) collective-permute-start(f32[2,128]{1,0:T(2,128)S(1)} %add.50), channel_id=1, source_target_pairs={{0,8},{4,12},{8,0},{12,4},{16,24},{20,28},{24,16},{28,20},{1,9},{5... | collective-permute-start | bytes 3080 | tf_op jit(solution)/shard_map/ppermute | solution.py:480
  82.1 8.2 %collective-permute-start.9 = (bf16[2,2,256,128]{3,2,1,0:T(8,128)(2,1)S(1)}, bf16[2,2,256,128]{3,2,1,0:T(8,128)(2,1)S(1)}, u32[]{:S(2)}, u32[]{:S(2)}) collective-permute-start(bf16[2,2,256,128]{3,2,1,0:T(8,128)(2,1)S(1)} %add_convert_fusion.refs_0_), channel_id=1, source_target_pairs={{0,1},{1,0},{2,3},{3,2},{4,5},{5,4},{6,7},{7,6},{8,9},{9,8},{10,11... | collective-permute-start | bytes 786440 | tf_op jit(solution)/shard_map/ppermute | solution.py:480
  82.2 3.6 %collective-permute-start.10 = (f32[2,128]{1,0:T(2,128)S(1)}, f32[2,128]{1,0:T(2,128)S(1)}, u32[]{:S(2)}, u32[]{:S(2)}) collective-permute-start(f32[2,128]{1,0:T(2,128)S(1)} %add.51), channel_id=1, source_target_pairs={{0,16},{4,20},{8,24},{12,28},{16,0},{20,4},{24,8},{28,12},{1,17},{... | collective-permute-start | bytes 3080 | tf_op jit(solution)/shard_map/ppermute | solution.py:480

commit v11 on v7

--- a/solution.py
+++ b/solution.py
@@ -77,8 +77,25 @@
 KEPT = 8
 
 
-def prepare_kernel(count, share, rows, width, meta, q_in, g_in, k_in, v_in, gain_ref, kg_ref, *rest):
-    outs, (q_buf, g_buf, k_buf, v_buf, sems) = rest[:-5], rest[-5:]
+def prepare_kernel(turn, count, share, rows, width, meta, q_in, g_in, k_in, v_in, gain_ref, kg_ref, *rest):
+    tail = count * KEPT + 6
+
+    @pl.when(meta[count + 1] == turn)
+    def _():
+        prepare_body(
+            count, share, rows, width, meta, q_in, g_in, k_in, v_in, gain_ref, kg_ref, *rest[-tail:]
+        )
+
+    if len(rest) > tail:
+
+        @pl.when(meta[count + 1] != turn)
+        def _():
+            for old, new in zip(rest[:-tail], rest[-tail:-6]):
+                new[...] = old[...]
+
+
+def prepare_body(count, share, rows, width, meta, q_in, g_in, k_in, v_in, gain_ref, kg_ref, *rest):
+    outs, (q_buf, g_buf, k_buf, v_buf, gain_buf, sems) = rest[:-6], rest[-6:]
     live_len = meta[count]
     scale = HD ** (-0.5)
     wide = share * HD
@@ -93,8 +110,15 @@
             copy.start()
             group.append(copy)
         copies.append(group)
-    q_gain = gain_ref[...]
-    k_gain = kg_ref[...]
+    gains = []
+    for j, src in enumerate((gain_ref, kg_ref)):
+        copy = pltpu.make_async_copy(src, gain_buf.at[j], sems.at[count, j])
+        copy.start()
+        gains.append(copy)
+    for copy in gains:
+        copy.wait()
+    q_gain = jnp.broadcast_to(gain_buf[0].reshape(1, HD), (8, HD)).T[:, 0:1]
+    k_gain = gain_buf[1].reshape(1, HD)
     for s in range(count):
         qt_ref, gt_ref, row_ref, er_ref, ot_ref, dp_ref, kh_ref, ku_ref = outs[s * KEPT : (s + 1) * KEPT]
         for copy in copies[s]:
@@ -129,7 +153,7 @@
             row_ref[1:2, cols] = jnp.sum(e_r, axis=0, keepdims=True)
 
 
-def prepare(meta, q, g, k, v, q_gain, k_gain, count):
+def prepare(turn, meta, q, g, k, v, q_gain, k_gain, count, before):
     rows, q_width = q.shape
     share = q_width // k.shape[1]
     total = share * rows
@@ -144,16 +168,17 @@
         jax.ShapeDtypeStruct((rows, 2 * HD), F32),
     ]
     outs = pl.pallas_call(
-        functools.partial(prepare_kernel, count, share, rows, 2 * HD),
+        functools.partial(prepare_kernel, turn, count, share, rows, 2 * HD),
         out_shape=each * count,
-        in_specs=[SMEM] + [HBM] * 4 + [VMEM] * 2,
+        in_specs=[SMEM] + [HBM] * 6 + [VMEM] * (KEPT * len(before)),
         out_specs=[VMEM] * (KEPT * count),
         scratch_shapes=[
             pltpu.VMEM((count, rows, share * HD), BF),
             pltpu.VMEM((count, rows, share * HD), BF),
             pltpu.VMEM((count, rows, HD), BF),
             pltpu.VMEM((count, rows, HD), BF),
-            pltpu.SemaphoreType.DMA((count, 4)),
+            pltpu.VMEM((2, HD), F32),
+            pltpu.SemaphoreType.DMA((count + 1, 4)),
         ],
         compiler_params=params(16),
         cost_estimate=pl.CostEstimate(
@@ -162,7 +187,7 @@
             transcendentals=count * total * rows,
         ),
         name="prepare_response",
-    )(meta, q, g, k, v, q_gain, k_gain)
+    )(meta, q, g, k, v, q_gain, k_gain, *[x for group in before for x in group])
     return [list(outs[s * KEPT : (s + 1) * KEPT]) for s in range(count)]
 
 
@@ -263,7 +288,7 @@
     outs, (at_ref, dq_ref), bufs, sems = rest[:4], rest[4:6], rest[6:10], rest[10]
     q_gain = gain_ref[...]
     d_kr, d_vr = attend(width, pr_ref, kept, q_gain, acc_ref, part_ref, at_ref, dq_ref, gacc_ref)
-    live_len = meta[meta.shape[0] - 1]
+    live_len = meta[meta.shape[0] - 2]
     settle(width, meta[s], live_len, kept, q_gain, kg_ref[...], at_ref, dq_ref, d_kr, d_vr, outs, bufs, sems)
 
 
@@ -278,7 +303,7 @@
 def second_kernel(s, width, meta, *rest):
     kept, (gain_ref, kg_ref, at_ref, dq_ref, dkr_ref, dvr_ref) = rest[:KEPT], rest[KEPT : KEPT + 6]
     outs, bufs, sems = rest[-9:-5], rest[-5:-1], rest[-1]
-    live_len = meta[meta.shape[0] - 1]
+    live_len = meta[meta.shape[0] - 2]
     settle(
         width, meta[s], live_len, kept, gain_ref[...], kg_ref[...], at_ref, dq_ref,
         dkr_ref[...], dvr_ref[...], outs, bufs, sems,
@@ -453,24 +478,30 @@
     depth, p_rows, _ = cache.shape
     direct = n_group == kv_heads
 
-    def shift(x, s):
-        return lax.ppermute(x, "group", [(i, (i + s) % n_group) for i in range(n_group)])
-
     gain_col = q_gain[:, None]
     gain_row = k_gain[None, :]
+    order = jnp.arange(kv_heads, dtype=jnp.int32)
     if direct:
-        order = jnp.stack([(me - s) % n_group for s in range(n_group)]).astype(jnp.int32)
-    else:
-        order = jnp.arange(kv_heads, dtype=jnp.int32)
-    meta = jnp.concatenate([order, live_len[None]])
-    q, g, k, v = [pltpu.with_memory_space_constraint(x, pltpu.HBM) for x in (q, g, k, v)]
-    kept = prepare(meta, q, g, k, v, gain_col, gain_row, kv_heads)
+        order = order ^ me
+    turn = lax.axis_index("dp") % 2 if direct else jnp.int32(0)
+    meta = jnp.concatenate([order, jnp.stack([live_len, turn.astype(jnp.int32)])])
+    q, g, k, v, *gains_in = [
+        pltpu.with_memory_space_constraint(x, pltpu.HBM) for x in (q, g, k, v, q_gain, k_gain)
+    ]
+    kept = prepare(0, meta, q, g, k, v, *gains_in, kv_heads, ())
+
+    def swap(x, step):
+        return lax.ppermute(x, "group", [(i, i ^ step) for i in range(n_group)])
+
     if direct:
-        blocks = cut(order, pltpu.with_memory_space_constraint(cache, pltpu.HBM), kv_heads)
-        got = [blocks[0]] + [shift(blocks[s], -s) for s in range(1, n_group)]
-        got[1], kept[0][2] = lax.optimization_barrier((got[1], kept[0][2]))
-        mine = pick(jnp.reshape((owner - me) % n_group, (1,)).astype(jnp.int32), got)
-        prompts = [mine] + [shift(mine, s) for s in range(1, n_group)]
+        blocks = list(cut(order, pltpu.with_memory_space_constraint(cache, pltpu.HBM), kv_heads))
+        blocks[1:] = [after(x, kept[0][2]) for x in blocks[1:]]
+        got = [blocks[0]] + [swap(blocks[s], s) for s in range(1, n_group)]
+        kept = prepare(1, meta, q, g, k, v, *gains_in, kv_heads, kept)
+        for s in range(1, n_group):
+            got[s] = after(got[s], kept[0][2])
+        mine = pick(jnp.reshape(owner ^ me, (1,)).astype(jnp.int32), got)
+        prompts = [mine] + [swap(mine, s) for s in range(1, n_group)]
     else:
         cache = lax.psum(jnp.where(me == owner, cache, jnp.zeros_like(cache)), "group")
         prompts = cut(order, cache, kv_heads)
@@ -487,21 +518,28 @@
             )
         parts.append(part)
         if direct and s > 0:
-            backs.append(shift(part, -s))
+            backs.append(swap(part, s))
     mine_flag = (me == owner).astype(jnp.int32)
+    def settled(results, buffers):
+        return list(second_half(kv_heads - 1, meta, kept[-1], gain_col, gain_row, results, buffers))
+
     if direct:
-        results[0] = after(results[0], *backs[:-1])
-    buffers = list(second_half(kv_heads - 1, meta, kept[-1], gain_col, gain_row, results, buffers))
-    gains = pair_sum(acc, "dp", n_dp)
-    if direct:
-        backs[-1] = after(backs[-1], buffers[2])
+        gains = acc + lax.ppermute(acc, "dp", [(i, i ^ 1) for i in range(n_dp)])
+        results[0] = after(results[0], gains, *backs[:-1])
+        buffers = settled(results, buffers)
+        step = 2
+        while step < n_dp:
+            hop = lax.ppermute(gains, "dp", [(i, i ^ step) for i in range(n_dp)])
+            gains = gains + (after(hop, buffers[2]) if step == 2 else hop)
+            step *= 2
         payload = join(parts[0], backs, gains)
-        payloads = [payload] + [shift(payload, s) for s in range(1, n_group)]
+        payloads = [payload] + [swap(payload, s) for s in range(1, n_group)]
         placed, gains = place(jnp.concatenate([mine_flag[None], order]), payloads, depth, p_rows)
     else:
         total = lax.psum(jnp.concatenate(parts, axis=-1).astype(F32), "group").astype(BF)
         placed = jnp.where(mine_flag > 0, total, jnp.zeros((), BF))
-        gains = pair_sum(gains, "group", n_group)
+        gains = pair_sum(pair_sum(acc, "dp", n_dp), "group", n_group)
+        buffers = settled(results, buffers)
     attended, d_query, d_key, d_value = buffers
     return (
         attended[None, None],

time: 66.4 us -> 137 us (2.06); the launches traced: 66.2 us -> 135 us
  local copies, waits for them, and re-layouts: 1.59 us -> 71.4 us
  Pallas kernels: 21 us -> 26.7 us
  waiting for transfers between devices: 15.6 us -> 11.1 us
  starting transfers between devices: 25.8 us -> 22.9 us
    unnamed x4 -> x228, local copies, waits for them, and re-layouts: 1.31 us -> 71.3 us
    ppermute x15, waiting for transfers between devices: 15.6 us -> 11.1 us  [the longest x12 7.83 us: swap(): return lax.ppermute(x, 'group', [(i, i ^ step) for i in range(n_group)])]
    ppermute x15, starting transfers between devices: 25.8 us -> 22.9 us  [the longest x12 19.6 us: swap(): return lax.ppermute(x, 'group', [(i, i ^ step) for i in range(n_group)])]
    pallas_call x1 -> x2, Pallas kernels: 5.15 us -> 7.08 us  [prepare(): pl.pallas_call(functools.partial(prepare_kernel, turn, count, share, rows...]
  transfers between devices with their start and end apart: 15 -> 15, of which waited for: 7 -> 5; matrix products, arithmetic and copies ran while one was open for 0% -> 0% of each run, Pallas kernels for 27% -> 12%
where the time goes in v11:
time: 137 us; the launch traced here: 135 us
  local copies, waits for them, and re-layouts  71.4 us (52%)
  Pallas kernels  26.7 us (19%)
  starting transfers between devices  22.9 us (17%)
  waiting for transfers between devices  11.1 us (8%)
  between operations  2.44 us (2%)
    unnamed x228, local copies, waits for them, and re-layouts  71.3 us
    ppermute x12, starting transfers between devices, swap(): return lax.ppermute(x, 'group', [(i, i ^ step) for i in range(n_group)])  19.6 us
    pallas_call x3, Pallas kernels, whole_head(): pl.pallas_call(functools.partial(whole_kernel, s, 2 * HD), out_shape=[jax...  10.1 us
    ppermute x12, waiting for transfers between devices, swap(): return lax.ppermute(x, 'group', [(i, i ^ step) for i in range(n_group)])  7.83 us
    pallas_call x2, Pallas kernels, prepare(): pl.pallas_call(functools.partial(prepare_kernel, turn, count, share, rows...  7.08 us
    ppermute x2, starting transfers between devices, local(): hop = lax.ppermute(gains, 'dp', [(i, i ^ step) for i in range(n_dp)])  3.29 us
  transfers between devices with their start and end apart: 15, of which 5 were waited for; matrix products, arithmetic and copies ran while one was open for 0% of the time, Pallas kernels for 12%

profile of v11, /device:TPU:0, one launch (start us, length us, event | category | flops | bytes accessed | tf_op | source)
XLA Modules:
  0.0 134.7 jit_solution(6573822182060784366)
XLA Ops:
  1.3 2.4 %cut_prompt.1 = (bf16[2,256,128]{2,1,0:T(8,128)(2,1)S(1)}, bf16[2,256,128]{2,1,0:T(8,128)(2,1)}, bf16[2,256,128]{2,1,0:T(8,128)(2,1)}, bf16[2,256,128]{2,1,0:T(8,128)(2,1)}) custom-call(s32[4]{0:T(128)S(1)} %iota_xor_fusion.order, bf16[2,256,512]{2,1,0:T(8,128)(2,1)} %bitcast.36), custom_call_target="tpu_custom_call" | custom-call | tf_op jit(solution)/shard_map/cut_prompt/pallas_call | solution.py:48
  4.5 5.7 %prepare_response.2 = (bf16[128,768]{1,0:T(8,128)(2,1)S(1)}, bf16[128,768]{1,0:T(8,128)(2,1)S(1)}, f32[8,768]{1,0:T(8,128)S(1)}, bf16[192,768]{1,0:T(8,128)(2,1)...) custom-call(s32[6]{0:T(128)S(1)} %pad_add_fusion.meta, ...), custom_call_target="tpu_custom_call" | custom-call | flops 452984832 | bytes 3932160 | tf_op jit(solution)/shard_map/prepare_response/pallas_call | solution.py:170
  10.2 0.8 copy-done
  11.0 0.8 copy-done.2
  11.8 0.8 copy-done.4
  12.6 0.8 copy-done.6
  13.4 0.7 copy-done.10
  14.2 0.8 copy-done.12
  14.9 0.8 copy-done.14
  30.3 5.1 %collective-permute-start.2 = (bf16[2,256,128]{2,1,0:T(8,128)(2,1)}, bf16[2,256,128]{2,1,0:T(8,128)(2,1)}, u32[]{:S(2)}, u32[]{:S(2)}) collective-permute-start(bf16[2,256,128]{2,1,0:T(8,128)(2,1)} %get-tuple-element.161), channel_id=1, source_target_pairs={{0,3},{1,2},{2,1},{3,0},{4,7},{5,6},{6,5},{7,4},{8,11},{9,10},{10,... | collective-permute-start | bytes 393224 | tf_op jit(solution)/shard_map/ppermute | solution.py:494
  36.6 0.8 copy-done.89
  37.4 1.1 copy-done.1
  38.5 1.1 copy-done.3
  39.6 1.1 copy-done.5
  40.6 1.1 copy-done.7
  41.7 1.0 copy-done.11
  42.7 1.0 copy-done.13
  43.7 1.0 copy-done.15
  44.7 1.0 copy-done.29
  45.6 1.0 copy-done.31
  46.6 1.0 copy-done.33
  47.6 1.0 copy-done.35
  48.5 0.9 copy-done.55
  49.4 0.9 copy-done.57
  50.4 0.9 copy-done.59
  51.3 0.9 copy-done.61
  52.2 0.9 copy-done.63
  53.2 0.9 copy-done.65
  54.1 0.9 copy-done.67
  55.0 0.9 copy-done.69
  55.9 0.9 copy-done.71
  56.9 0.9 copy-done.73
  57.8 0.9 copy-done.75
  58.7 0.9 copy-done.77
  59.6 0.8 copy-done.91
  60.4 0.7 copy-done.103
  63.4 1.4 %prepare_response.3 = (bf16[128,768]{1,0:T(8,128)(2,1)S(1)}, bf16[128,768]{1,0:T(8,128)(2,1)S(1)}, f32[8,768]{1,0:T(8,128)S(1)}, bf16[192,768]{1,0:T(8,128)(2,1)...) custom-call(s32[6]{0:T(128)S(1)} %pad_add_fusion.meta, ...), custom_call_target="tpu_custom_call" | custom-call | flops 452984832 | bytes 3932160 | tf_op jit(solution)/shard_map/prepare_response/pallas_call | solution.py:170
  64.9 0.7 copy-done.16
  65.6 0.7 copy-done.18
  66.3 0.7 copy-done.20
  79.6 1.3 pick_owner.1.pr_ref
  80.9 1.5 %collective-permute-start.5 = (bf16[2,256,128]{2,1,0:T(8,128)(2,1)S(1)}, bf16[2,256,128]{2,1,0:T(8,128)(2,1)}, u32[]{:S(2)}, u32[]{:S(2)}) collective-permute-start(bf16[2,256,128]{2,1,0:T(8,128)(2,1)S(1)} %pick_owner.1.pr_ref), channel_id=1, source_target_pairs={{0,1},{1,0},{2,3},{3,2},{4,5},{5,4},{6,7},{7,6},{8,9},{9,8},{10,11... | collective-permute-start | bytes 393224 | tf_op jit(solution)/shard_map/ppermute | solution.py:494
  82.4 2.9 %collective-permute-start.4 = (bf16[2,256,128]{2,1,0:T(8,128)(2,1)S(1)}, bf16[2,256,128]{2,1,0:T(8,128)(2,1)}, u32[]{:S(2)}, u32[]{:S(2)}) collective-permute-start(bf16[2,256,128]{2,1,0:T(8,128)(2,1)S(1)} %pick_owner.1.pr_ref), channel_id=1, source_target_pairs={{0,2},{1,3},{2,0},{3,1},{4,6},{5,7},{6,4},{7,5},{8,10},{9,11},{10,... | collective-permute-start | bytes 393224 | tf_op jit(solution)/shard_map/ppermute | solution.py:494
  86.2 1.1 copy-done.9
  87.2 1.0 copy-done.21
  88.2 0.9 copy-done.49
  89.1 0.9 copy-done.51
  90.1 0.9 copy-done.53
  91.0 0.8 copy-done.93
  92.6 3.1 %attend_head.3 = (bf16[2,256,128]{2,1,0:T(8,128)(2,1)S(1)}, f32[2,128]{1,0:T(2,128)S(1)}, bf16[192,2048]{1,0:T(8,128)(2,1)}, bf16[192,2048]{1,0:T(8,128)(2,1)}, ...) custom-call(s32[6]{0:T(128)S(1)} %copy-done.95, bf16[2,256,128]{2,1,0:T(8,128)(2,1)S(1)} %pick_owner.1.pr_ref, ...), custom_call_target="tpu_custom_call" | custom-call | flops 276824064 | bytes 1048576 | tf_op jit(solution)/shard_map/attend_head/pallas_call | solution.py:334
  96.4 3.6 %attend_head.4 = (bf16[2,256,128]{2,1,0:T(8,128)(2,1)S(1)}, f32[2,128]{1,0:T(2,128)S(1)}, bf16[192,2048]{1,0:T(8,128)(2,1)}, bf16[192,2048]{1,0:T(8,128)(2,1)}, ...) custom-call(s32[6]{0:T(128)S(1)} %copy-done.95, ...), custom_call_target="tpu_custom_call", output_to_operand_aliasing={{2}: (13, {}), {3}: (14, {}), {4}: (15, {}), {5}: (16, {})} | custom-call | flops 276824064 | bytes 1048576 | tf_op jit(solution)/shard_map/attend_head/pallas_call | solution.py:334
  100.7 3.4 %attend_head.5 = (bf16[2,256,128]{2,1,0:T(8,128)(2,1)S(1)}, f32[2,128]{1,0:T(2,128)S(1)}, bf16[192,2048]{1,0:T(8,128)(2,1)}, bf16[192,2048]{1,0:T(8,128)(2,1)}, ...) custom-call(s32[6]{0:T(128)S(1)} %copy-done.95, ...), custom_call_target="tpu_custom_call", output_to_operand_aliasing={{2}: (13, {}), {3}: (14, {}), {4}: (15, {}), {5}: (16, {})} | custom-call | flops 276824064 | bytes 1048576 | tf_op jit(solution)/shard_map/attend_head/pallas_call | solution.py:334
  104.2 1.6 %collective-permute-start.8 = (bf16[2,256,128]{2,1,0:T(8,128)(2,1)S(1)}, bf16[2,256,128]{2,1,0:T(8,128)(2,1)S(1)}, u32[]{:S(2)}, u32[]{:S(2)}) collective-permute-start(bf16[2,256,128]{2,1,0:T(8,128)(2,1)S(1)} %get-tuple-element.200), channel_id=1, source_target_pairs={{0,2},{1,3},{2,0},{3,1},{4,6},{5,7},{6,4},{7,5},{8,10},{9,11},{10,... | collective-permute-start | bytes 393224 | tf_op jit(solution)/shard_map/ppermute | solution.py:494
  105.8 2.8 %collective-permute-start.7 = (bf16[2,256,128]{2,1,0:T(8,128)(2,1)S(1)}, bf16[2,256,128]{2,1,0:T(8,128)(2,1)S(1)}, u32[]{:S(2)}, u32[]{:S(2)}) collective-permute-start(bf16[2,256,128]{2,1,0:T(8,128)(2,1)S(1)} %get-tuple-element.199), channel_id=1, source_target_pairs={{0,1},{1,0},{2,3},{3,2},{4,5},{5,4},{6,7},{7,6},{8,9},{9,8},{10,11... | collective-permute-start | bytes 393224 | tf_op jit(solution)/shard_map/ppermute | solution.py:494
  108.6 2.6 %attend_last_head.1 = (bf16[2,256,128]{2,1,0:T(8,128)(2,1)S(1)}, f32[2,128]{1,0:T(2,128)S(1)}, bf16[128,768]{1,0:T(8,128)(2,1)S(1)}, f32[128,768]{1,0:T(8,128)S(...) custom-call(bf16[2,256,128]{2,1,0:T(8,128)(2,1)} %collective-permute-done.3.pr_ref, ...), custom_call_target="tpu_custom_call" | custom-call | flops 276824064 | bytes 1048576 | tf_op jit(solution)/shard_map/attend_last_head/pallas_call | solution.py:356
  111.4 1.1 collective-permute-done.6
  112.5 1.6 %collective-permute-start.10 = (f32[2,128]{1,0:T(2,128)S(1)}, f32[2,128]{1,0:T(2,128)S(1)}, u32[]{:S(2)}, u32[]{:S(2)}) collective-permute-start(f32[2,128]{1,0:T(2,128)S(1)} %add.14), channel_id=1, source_target_pairs={{0,8},{4,12},{8,0},{12,4},{16,24},{20,28},{24,16},{28,20},{1,9},{5... | collective-permute-start | bytes 3080 | tf_op jit(solution)/shard_map/ppermute | solution.py:532
  114.1 1.6 %settle_last_head.1 = (bf16[192,2048]{1,0:T(8,128)(2,1)}, bf16[192,2048]{1,0:T(8,128)(2,1)}, bf16[192,512]{1,0:T(8,128)(2,1)}, bf16[192,512]{1,0:T(8,128)(2,1)}) custom-call(s32[6]{0:T(128)S(1)} %copy-done.95, bf16[128,768]{1,0:T(8,128)(2,1)S(1)} %get-tuple-element.144.rest_0_, ...), custom_call_target="tpu_custom_call", output_to_operand_aliasing={{0}: (15, {}), {1}: (16, {}), {2}: (17, {}), {3}: (18, {})} | custom-call | bytes 1048576 | tf_op jit(solution)/shard_map/settle_last_head/pallas_call | solution.py:377
  116.1 1.7 %collective-permute-start.11 = (f32[2,128]{1,0:T(2,128)S(1)}, f32[2,128]{1,0:T(2,128)S(1)}, u32[]{:S(2)}, u32[]{:S(2)}) collective-permute-start(f32[2,128]{1,0:T(2,128)S(1)} %add.15), channel_id=1, source_target_pairs={{0,16},{4,20},{8,24},{12,28},{16,0},{20,4},{24,8},{28,12},{1,17},{... | collective-permute-start | bytes 3080 | tf_op jit(solution)/shard_map/ppermute | solution.py:532
  117.7 1.9 %collective-permute-done.11 = f32[2,128]{1,0:T(2,128)S(1)} collective-permute-done((f32[2,128]{1,0:T(2,128)S(1)}, f32[2,128]{1,0:T(2,128)S(1)}, u32[]{:S(2)}, u32[]{:S(2)}) %collective-permute-start.11) | collective-permute-done | bytes 1056 | tf_op jit(solution)/shard_map/ppermute | solution.py:532
  119.7 1.6 %collective-permute-start.12 = (bf16[528,128]{1,0:T(8,128)(2,1)S(1)}, bf16[528,128]{1,0:T(8,128)(2,1)S(1)}, u32[]{:S(2)}, u32[]{:S(2)}) collective-permute-start(bf16[528,128]{1,0:T(8,128)(2,1)S(1)} %join_parts.1.refs_0_), channel_id=1, source_target_pairs={{0,1},{1,0},{2,3},{3,2},{4,5},{5,4},{6,7},{7,6},{8,9},{9,8},{10,11... | collective-permute-start | bytes 405512 | tf_op jit(solution)/shard_map/ppermute | solution.py:494
  121.3 3.3 %collective-permute-start.13 = (bf16[528,128]{1,0:T(8,128)(2,1)S(1)}, bf16[528,128]{1,0:T(8,128)(2,1)S(1)}, u32[]{:S(2)}, u32[]{:S(2)}) collective-permute-start(bf16[528,128]{1,0:T(8,128)(2,1)S(1)} %join_parts.1.refs_0_), channel_id=1, source_target_pairs={{0,2},{1,3},{2,0},{3,1},{4,6},{5,7},{6,4},{7,5},{8,10},{9,11},{10,... | collective-permute-start | bytes 405512 | tf_op jit(solution)/shard_map/ppermute | solution.py:494
  125.8 7.4 %collective-permute-done.13.refs_2_ = bf16[528,128]{1,0:T(8,128)(2,1)S(1)} collective-permute-done((bf16[528,128]{1,0:T(8,128)(2,1)S(1)}, bf16[528,128]{1,0:T(8,128)(2,1)S(1)}, u32[]{:S(2)}, u32[]{:S(2)}) %collective-permute-start.13) | collective-permute-done | bytes 135200 | tf_op jit(solution)/shard_map/ppermute | solution.py:494
  133.3 1.5 %place_prompt_grad.1 = (bf16[2,256,512]{2,1,0:T(8,128)(2,1)}, f32[2,128]{1,0:T(2,128)}) custom-call(s32[5]{0:T(128)S(1)} %pad_add_fusion.1.meta, bf16[528,128]{1,0:T(8,128)(2,1)S(1)} %join_parts.1.refs_0_, bf16[528,128]{1,0:T(8,128)(2,1)S(1)} %collective-permute-done.12.refs_1_, bf16[528,128]{1,0:T(8,128)(2,1)S(1)} %collective-permute-done.13.refs_2_, ...), custom_call_target="tpu_custom_call" | custom-call | tf_op jit(solution)/shard_map/place_prompt_grad/pallas_call | solution.py:442
  (213 shorter events, 35.2 us)
Async XLA Ops:
  0.7 3.8 %copy-start.111 = (s32[4]{0:T(128)}, s32[4]{0:T(128)S(1)}, u32[]{:S(2)}) copy-start(s32[4]{0:T(128)S(1)} %iota_xor_fusion.order) | copy-start | bytes 52
  4.5 32.2 %copy-start.94 = (s32[6]{0:T(128)}, s32[6]{0:T(128)S(1)}, u32[]{:S(2)}) copy-start(s32[6]{0:T(128)S(1)} %pad_add_fusion.meta) | copy-start | bytes 76
  30.3 49.2 %collective-permute-start.2 = (bf16[2,256,128]{2,1,0:T(8,128)(2,1)}, bf16[2,256,128]{2,1,0:T(8,128)(2,1)}, u32[]{:S(2)}, u32[]{:S(2)}) collective-permute-start(bf16[2,256,128]{2,1,0:T(8,128)(2,1)} %get-tuple-element.161), channel_id=1, source_target_pairs={{0,3},{1,2},{2,1},{3,0},{4,7},{5,6},{6,5},{7,4},{8,11},{9,10},{10,... | collective-permute-start | bytes 393224 | tf_op jit(solution)/shard_map/ppermute | solution.py:494
  35.4 44.1 %collective-permute-start.1 = (bf16[2,256,128]{2,1,0:T(8,128)(2,1)}, bf16[2,256,128]{2,1,0:T(8,128)(2,1)}, u32[]{:S(2)}, u32[]{:S(2)}) collective-permute-start(bf16[2,256,128]{2,1,0:T(8,128)(2,1)} %get-tuple-element.158), channel_id=1, source_target_pairs={{0,2},{1,3},{2,0},{3,1},{4,6},{5,7},{6,4},{7,5},{8,10},{9,11},{10,... | collective-permute-start | bytes 393224 | tf_op jit(solution)/shard_map/ppermute | solution.py:494
  35.4 44.1 %collective-permute-start = (bf16[2,256,128]{2,1,0:T(8,128)(2,1)}, bf16[2,256,128]{2,1,0:T(8,128)(2,1)}, u32[]{:S(2)}, u32[]{:S(2)}) collective-permute-start(bf16[2,256,128]{2,1,0:T(8,128)(2,1)} %get-tuple-element.154), channel_id=1, source_target_pairs={{0,1},{1,0},{2,3},{3,2},{4,5},{5,4},{6,7},{7,6},{8,9},{9,8},{10,11... | collective-permute-start | bytes 393224 | tf_op jit(solution)/shard_map/ppermute | solution.py:494
  37.4 1.1 copy-start.1
  38.5 1.1 copy-start.3
  39.6 1.1 copy-start.5
  40.6 1.1 copy-start.7
  41.7 1.0 copy-start.11
  42.7 1.0 copy-start.13
  43.7 1.0 copy-start.15
  44.7 1.0 copy-start.29
  45.6 1.0 copy-start.31
  46.6 1.0 copy-start.33
  47.6 1.0 copy-start.35
  48.5 0.9 copy-start.55
  49.4 0.9 copy-start.57
  50.4 0.9 copy-start.59
  51.3 0.9 copy-start.61
  52.2 0.9 copy-start.63
  53.2 0.9 copy-start.65
  54.1 0.9 copy-start.67
  55.0 0.9 copy-start.69
  55.9 0.9 copy-start.71
  56.9 0.9 copy-start.73
  57.8 0.9 copy-start.75
  58.7 0.9 copy-start.77
  63.4 16.1 %copy-start.81 = (bf16[2,256,128]{2,1,0:T(8,128)(2,1)S(1)}, bf16[2,256,128]{2,1,0:T(8,128)(2,1)}, u32[]{:S(2)}) copy-start(bf16[2,256,128]{2,1,0:T(8,128)(2,1)} %copy-done.80) | copy-start | bytes 393220
  79.5 1.4 %copy-start.78 = (bf16[192,128]{1,0:T(8,128)(2,1)}, bf16[192,128]{1,0:T(8,128)(2,1)S(1)}, u32[]{:S(2)}) copy-start(bf16[192,128]{1,0:T(8,128)(2,1)S(1)} %get-tuple-element.150.rest_6_) | copy-start | bytes 147460
  79.5 5.8 %copy-start.8 = (f32[192,768]{1,0:T(8,128)}, f32[192,768]{1,0:T(8,128)S(1)}, u32[]{:S(2)}) copy-start(f32[192,768]{1,0:T(8,128)S(1)} %get-tuple-element.183.rest_5_) | copy-start | bytes 1769476
  79.5 6.0 %copy-start.27 = (bf16[192,768]{1,0:T(8,128)(2,1)S(1)}, bf16[192,768]{1,0:T(8,128)(2,1)}, u32[]{:S(2)}) copy-start(bf16[192,768]{1,0:T(8,128)(2,1)} %copy-done.26) | copy-start | bytes 884740
  80.9 4.5 %copy-start.113 = (f32[128]{0:T(128)S(1)}, f32[128]{0:T(128)}, u32[]{:S(2)}) copy-start(f32[128]{0:T(128)} %gain_ref.3) | copy-start | bytes 1540
  80.9 14.8 %collective-permute-start.5 = (bf16[2,256,128]{2,1,0:T(8,128)(2,1)S(1)}, bf16[2,256,128]{2,1,0:T(8,128)(2,1)}, u32[]{:S(2)}, u32[]{:S(2)}) collective-permute-start(bf16[2,256,128]{2,1,0:T(8,128)(2,1)S(1)} %pick_owner.1.pr_ref), channel_id=1, source_target_pairs={{0,1},{1,0},{2,3},{3,2},{4,5},{5,4},{6,7},{7,6},{8,9},{9,8},{10,11... | collective-permute-start | bytes 393224 | tf_op jit(solution)/shard_map/ppermute | solution.py:494
  82.4 17.6 %collective-permute-start.4 = (bf16[2,256,128]{2,1,0:T(8,128)(2,1)S(1)}, bf16[2,256,128]{2,1,0:T(8,128)(2,1)}, u32[]{:S(2)}, u32[]{:S(2)}) collective-permute-start(bf16[2,256,128]{2,1,0:T(8,128)(2,1)S(1)} %pick_owner.1.pr_ref), channel_id=1, source_target_pairs={{0,2},{1,3},{2,0},{3,1},{4,6},{5,7},{6,4},{7,5},{8,10},{9,11},{10,... | collective-permute-start | bytes 393224 | tf_op jit(solution)/shard_map/ppermute | solution.py:494
  85.4 23.3 %collective-permute-start.3 = (bf16[2,256,128]{2,1,0:T(8,128)(2,1)S(1)}, bf16[2,256,128]{2,1,0:T(8,128)(2,1)}, u32[]{:S(2)}, u32[]{:S(2)}) collective-permute-start(bf16[2,256,128]{2,1,0:T(8,128)(2,1)S(1)} %pick_owner.1.pr_ref), channel_id=1, source_target_pairs={{0,3},{1,2},{2,1},{3,0},{4,7},{5,6},{6,5},{7,4},{8,11},{9,10},{10,... | collective-permute-start | bytes 393224 | tf_op jit(solution)/shard_map/ppermute | solution.py:494
  86.2 1.1 copy-start.9
  87.2 1.0 copy-start.21
  88.2 0.9 copy-start.49
  89.1 0.9 copy-start.51
  90.1 0.9 copy-start.53
  92.5 3.1 %copy-start.19 = (f32[128,768]{1,0:T(8,128)S(1)}, f32[128,768]{1,0:T(8,128)}, u32[]{:S(2)}) copy-start(f32[128,768]{1,0:T(8,128)} %copy-done.18) | copy-start | bytes 1179652
  92.5 3.1 %copy-start.25 = (bf16[192,768]{1,0:T(8,128)(2,1)S(1)}, bf16[192,768]{1,0:T(8,128)(2,1)}, u32[]{:S(2)}) copy-start(bf16[192,768]{1,0:T(8,128)(2,1)} %copy-done.24) | copy-start | bytes 884740
  92.5 3.2 %copy-start.43 = (bf16[128,768]{1,0:T(8,128)(2,1)S(1)}, bf16[128,768]{1,0:T(8,128)(2,1)}, u32[]{:S(2)}) copy-start(bf16[128,768]{1,0:T(8,128)(2,1)} %copy-done.42) | copy-start | bytes 589828
  92.5 3.2 %copy-start.45 = (bf16[128,768]{1,0:T(8,128)(2,1)S(1)}, bf16[128,768]{1,0:T(8,128)(2,1)}, u32[]{:S(2)}) copy-start(bf16[128,768]{1,0:T(8,128)(2,1)} %copy-done.44) | copy-start | bytes 589828
  92.5 3.2 %copy-start.47 = (f32[192,256]{1,0:T(8,128)S(1)}, f32[192,256]{1,0:T(8,128)}, u32[]{:S(2)}) copy-start(f32[192,256]{1,0:T(8,128)} %copy-done.46) | copy-start | bytes 589828
  92.6 3.2 %copy-start.87 = (bf16[192,128]{1,0:T(8,128)(2,1)S(1)}, bf16[192,128]{1,0:T(8,128)(2,1)}, u32[]{:S(2)}) copy-start(bf16[192,128]{1,0:T(8,128)(2,1)} %copy-done.86) | copy-start | bytes 147460
  96.4 3.6 %copy-start.17 = (f32[128,768]{1,0:T(8,128)S(1)}, f32[128,768]{1,0:T(8,128)}, u32[]{:S(2)}) copy-start(f32[128,768]{1,0:T(8,128)} %copy-done.16) | copy-start | bytes 1179652
  96.4 3.6 %copy-start.23 = (bf16[192,768]{1,0:T(8,128)(2,1)S(1)}, bf16[192,768]{1,0:T(8,128)(2,1)}, u32[]{:S(2)}) copy-start(bf16[192,768]{1,0:T(8,128)(2,1)} %copy-done.22) | copy-start | bytes 884740
  96.4 3.6 %copy-start.37 = (bf16[128,768]{1,0:T(8,128)(2,1)S(1)}, bf16[128,768]{1,0:T(8,128)(2,1)}, u32[]{:S(2)}) copy-start(bf16[128,768]{1,0:T(8,128)(2,1)} %copy-done.36) | copy-start | bytes 589828
  96.4 3.6 %copy-start.39 = (bf16[128,768]{1,0:T(8,128)(2,1)S(1)}, bf16[128,768]{1,0:T(8,128)(2,1)}, u32[]{:S(2)}) copy-start(bf16[128,768]{1,0:T(8,128)(2,1)} %copy-done.38) | copy-start | bytes 589828
  96.4 3.6 %copy-start.41 = (f32[192,256]{1,0:T(8,128)S(1)}, f32[192,256]{1,0:T(8,128)}, u32[]{:S(2)}) copy-start(f32[192,256]{1,0:T(8,128)} %copy-done.40) | copy-start | bytes 589828
  96.4 3.6 %copy-start.85 = (bf16[192,128]{1,0:T(8,128)(2,1)S(1)}, bf16[192,128]{1,0:T(8,128)(2,1)}, u32[]{:S(2)}) copy-start(bf16[192,128]{1,0:T(8,128)(2,1)} %copy-done.84) | copy-start | bytes 147460
  100.7 7.9 %copy-start.79 = (bf16[192,128]{1,0:T(8,128)(2,1)S(1)}, bf16[192,128]{1,0:T(8,128)(2,1)}, u32[]{:S(2)}) copy-start(bf16[192,128]{1,0:T(8,128)(2,1)} %copy-done.78) | copy-start | bytes 147460
  100.7 7.9 %copy-start.83 = (f32[8,768]{1,0:T(8,128)S(1)}, f32[8,768]{1,0:T(8,128)}, u32[]{:S(2)}) copy-start(f32[8,768]{1,0:T(8,128)} %copy-done.82) | copy-start | bytes 73732
  104.2 10.0 %collective-permute-start.8 = (bf16[2,256,128]{2,1,0:T(8,128)(2,1)S(1)}, bf16[2,256,128]{2,1,0:T(8,128)(2,1)S(1)}, u32[]{:S(2)}, u32[]{:S(2)}) collective-permute-start(bf16[2,256,128]{2,1,0:T(8,128)(2,1)S(1)} %get-tuple-element.200), channel_id=1, source_target_pairs={{0,2},{1,3},{2,0},{3,1},{4,6},{5,7},{6,4},{7,5},{8,10},{9,11},{10,... | collective-permute-start | bytes 393224 | tf_op jit(solution)/shard_map/ppermute | solution.py:494
  105.8 8.4 %collective-permute-start.7 = (bf16[2,256,128]{2,1,0:T(8,128)(2,1)S(1)}, bf16[2,256,128]{2,1,0:T(8,128)(2,1)S(1)}, u32[]{:S(2)}, u32[]{:S(2)}) collective-permute-start(bf16[2,256,128]{2,1,0:T(8,128)(2,1)S(1)} %get-tuple-element.199), channel_id=1, source_target_pairs={{0,1},{1,0},{2,3},{3,2},{4,5},{5,4},{6,7},{7,6},{8,9},{9,8},{10,11... | collective-permute-start | bytes 393224 | tf_op jit(solution)/shard_map/ppermute | solution.py:494
  111.2 8.4 %collective-permute-start.9 = (bf16[2,256,128]{2,1,0:T(8,128)(2,1)S(1)}, bf16[2,256,128]{2,1,0:T(8,128)(2,1)S(1)}, u32[]{:S(2)}, u32[]{:S(2)}) collective-permute-start(bf16[2,256,128]{2,1,0:T(8,128)(2,1)S(1)} %get-tuple-element.214), channel_id=1, source_target_pairs={{0,3},{1,2},{2,1},{3,0},{4,7},{5,6},{6,5},{7,4},{8,11},{9,10},{10,... | collective-permute-start | bytes 393224 | tf_op jit(solution)/shard_map/ppermute | solution.py:494
  111.3 1.2 collective-permute-start.6
  112.5 3.6 %collective-permute-start.10 = (f32[2,128]{1,0:T(2,128)S(1)}, f32[2,128]{1,0:T(2,128)S(1)}, u32[]{:S(2)}, u32[]{:S(2)}) collective-permute-start(f32[2,128]{1,0:T(2,128)S(1)} %add.14), channel_id=1, source_target_pairs={{0,8},{4,12},{8,0},{12,4},{16,24},{20,28},{24,16},{28,20},{1,9},{5... | collective-permute-start | bytes 3080 | tf_op jit(solution)/shard_map/ppermute | solution.py:532
  116.1 3.6 %collective-permute-start.11 = (f32[2,128]{1,0:T(2,128)S(1)}, f32[2,128]{1,0:T(2,128)S(1)}, u32[]{:S(2)}, u32[]{:S(2)}) collective-permute-start(f32[2,128]{1,0:T(2,128)S(1)} %add.15), channel_id=1, source_target_pairs={{0,16},{4,20},{8,24},{12,28},{16,0},{20,4},{24,8},{28,12},{1,17},{... | collective-permute-start | bytes 3080 | tf_op jit(solution)/shard_map/ppermute | solution.py:532
  119.7 6.1 %collective-permute-start.12 = (bf16[528,128]{1,0:T(8,128)(2,1)S(1)}, bf16[528,128]{1,0:T(8,128)(2,1)S(1)}, u32[]{:S(2)}, u32[]{:S(2)}) collective-permute-start(bf16[528,128]{1,0:T(8,128)(2,1)S(1)} %join_parts.1.refs_0_), channel_id=1, source_target_pairs={{0,1},{1,0},{2,3},{3,2},{4,5},{5,4},{6,7},{7,6},{8,9},{9,8},{10,11... | collective-permute-start | bytes 405512 | tf_op jit(solution)/shard_map/ppermute | solution.py:494
  121.3 11.9 %collective-permute-start.13 = (bf16[528,128]{1,0:T(8,128)(2,1)S(1)}, bf16[528,128]{1,0:T(8,128)(2,1)S(1)}, u32[]{:S(2)}, u32[]{:S(2)}) collective-permute-start(bf16[528,128]{1,0:T(8,128)(2,1)S(1)} %join_parts.1.refs_0_), channel_id=1, source_target_pairs={{0,2},{1,3},{2,0},{3,1},{4,6},{5,7},{6,4},{7,5},{8,10},{9,11},{10,... | collective-permute-start | bytes 405512 | tf_op jit(solution)/shard_map/ppermute | solution.py:494
  124.7 8.6 %collective-permute-start.14 = (bf16[528,128]{1,0:T(8,128)(2,1)S(1)}, bf16[528,128]{1,0:T(8,128)(2,1)S(1)}, u32[]{:S(2)}, u32[]{:S(2)}) collective-permute-start(bf16[528,128]{1,0:T(8,128)(2,1)S(1)} %join_parts.1.refs_0_), channel_id=1, source_target_pairs={{0,3},{1,2},{2,1},{3,0},{4,7},{5,6},{6,5},{7,4},{8,11},{9,10},{10,... | collective-permute-start | bytes 405512 | tf_op jit(solution)/shard_map/ppermute | solution.py:494
  (65 other events, 45.0 us)

commit v12 on v11

--- a/solution.py
+++ b/solution.py
@@ -56,14 +56,14 @@
     )(order, cache)
 
 
-def pick_kernel(which, *refs):
+def pick_kernel(meta, *refs):
     picked = refs[0][...]
     for i in range(1, len(refs) - 1):
-        picked = jnp.where(which[0] == i, refs[i][...], picked)
+        picked = jnp.where(meta[meta.shape[0] - 2] == i, refs[i][...], picked)
     refs[-1][...] = picked
 
 
-def pick(which, blocks):
+def pick(meta, blocks):
     return pl.pallas_call(
         pick_kernel,
         out_shape=jax.ShapeDtypeStruct(blocks[0].shape, BF),
@@ -71,10 +71,14 @@
         out_specs=VMEM,
         compiler_params=params(4),
         name="pick_owner",
-    )(which, *blocks)
+    )(meta, *blocks)
 
 
 KEPT = 8
+
+
+def column(row):
+    return jnp.broadcast_to(row, (8, HD)).T[:, 0:1]
 
 
 def prepare_kernel(turn, count, share, rows, width, meta, q_in, g_in, k_in, v_in, gain_ref, kg_ref, *rest):
@@ -117,7 +121,7 @@
         gains.append(copy)
     for copy in gains:
         copy.wait()
-    q_gain = jnp.broadcast_to(gain_buf[0].reshape(1, HD), (8, HD)).T[:, 0:1]
+    q_gain = column(gain_buf[0].reshape(1, HD))
     k_gain = gain_buf[1].reshape(1, HD)
     for s in range(count):
         qt_ref, gt_ref, row_ref, er_ref, ot_ref, dp_ref, kh_ref, ku_ref = outs[s * KEPT : (s + 1) * KEPT]
@@ -286,16 +290,16 @@
     kept, (gain_ref, kg_ref, acc_ref) = rest[:KEPT], rest[KEPT : KEPT + 3]
     part_ref, gacc_ref, *rest = rest[-13:]
     outs, (at_ref, dq_ref), bufs, sems = rest[:4], rest[4:6], rest[6:10], rest[10]
-    q_gain = gain_ref[...]
+    q_gain = column(gain_ref[...])
     d_kr, d_vr = attend(width, pr_ref, kept, q_gain, acc_ref, part_ref, at_ref, dq_ref, gacc_ref)
-    live_len = meta[meta.shape[0] - 2]
+    live_len = meta[meta.shape[0] - 4]
     settle(width, meta[s], live_len, kept, q_gain, kg_ref[...], at_ref, dq_ref, d_kr, d_vr, outs, bufs, sems)
 
 
 def first_kernel(width, pr_ref, *rest):
     kept, (gain_ref, acc_ref) = rest[:KEPT], rest[KEPT : KEPT + 2]
     part_ref, gacc_ref, at_ref, dq_ref, dkr_ref, dvr_ref = rest[-6:]
-    d_kr, d_vr = attend(width, pr_ref, kept, gain_ref[...], acc_ref, part_ref, at_ref, dq_ref, gacc_ref)
+    d_kr, d_vr = attend(width, pr_ref, kept, column(gain_ref[...]), acc_ref, part_ref, at_ref, dq_ref, gacc_ref)
     dkr_ref[...] = d_kr
     dvr_ref[...] = d_vr
 
@@ -303,9 +307,9 @@
 def second_kernel(s, width, meta, *rest):
     kept, (gain_ref, kg_ref, at_ref, dq_ref, dkr_ref, dvr_ref) = rest[:KEPT], rest[KEPT : KEPT + 6]
     outs, bufs, sems = rest[-9:-5], rest[-5:-1], rest[-1]
-    live_len = meta[meta.shape[0] - 2]
+    live_len = meta[meta.shape[0] - 4]
     settle(
-        width, meta[s], live_len, kept, gain_ref[...], kg_ref[...], at_ref, dq_ref,
+        width, meta[s], live_len, kept, column(gain_ref[...]), kg_ref[...], at_ref, dq_ref,
         dkr_ref[...], dvr_ref[...], outs, bufs, sems,
     )
 
@@ -422,15 +426,15 @@
 
 def place_kernel(meta, *refs):
     payloads, out_ref, gain_ref, stage = refs[:-3], refs[-3], refs[-2], refs[-1]
-    mine = meta[0] > 0
+    mine = meta[meta.shape[0] - 1] > 0
     depth, rows, _ = out_ref.shape
     for i, ref in enumerate(payloads):
-        at = pl.multiple_of(meta[1 + i] * HD, HD)
+        at = pl.multiple_of(meta[i] * HD, HD)
         for d in range(depth):
             block = ref[d * rows : (d + 1) * rows, :]
             out_ref[d, :, pl.ds(at, HD)] = jnp.where(mine, block, jnp.zeros_like(block))
         tail = ref[depth * rows :, :].astype(F32)
-        stage[meta[1 + i]] = tail[0:2] + tail[2:4] + tail[4:6]
+        stage[meta[i]] = tail[0:2] + tail[2:4] + tail[4:6]
     total = stage[0]
     for i in range(1, len(payloads)):
         total = total + stage[i]
@@ -478,13 +482,14 @@
     depth, p_rows, _ = cache.shape
     direct = n_group == kv_heads
 
-    gain_col = q_gain[:, None]
-    gain_row = k_gain[None, :]
+    q_row = q_gain[None, :]
+    k_row = k_gain[None, :]
     order = jnp.arange(kv_heads, dtype=jnp.int32)
     if direct:
         order = order ^ me
     turn = lax.axis_index("dp") % 2 if direct else jnp.int32(0)
-    meta = jnp.concatenate([order, jnp.stack([live_len, turn.astype(jnp.int32)])])
+    mine_flag = (me == owner).astype(jnp.int32)
+    meta = jnp.concatenate([order, jnp.stack([live_len, turn.astype(jnp.int32), owner ^ me, mine_flag])])
     q, g, k, v, *gains_in = [
         pltpu.with_memory_space_constraint(x, pltpu.HBM) for x in (q, g, k, v, q_gain, k_gain)
     ]
@@ -500,7 +505,7 @@
         kept = prepare(1, meta, q, g, k, v, *gains_in, kv_heads, kept)
         for s in range(1, n_group):
             got[s] = after(got[s], kept[0][2])
-        mine = pick(jnp.reshape(owner ^ me, (1,)).astype(jnp.int32), got)
+        mine = pick(meta, got)
         prompts = [mine] + [swap(mine, s) for s in range(1, n_group)]
     else:
         cache = lax.psum(jnp.where(me == owner, cache, jnp.zeros_like(cache)), "group")
@@ -511,17 +516,16 @@
     for s, prompt in enumerate(prompts):
         last = s == kv_heads - 1
         if last:
-            part, acc, *results = first_half(prompt, kept[s], gain_col, acc)
+            part, acc, *results = first_half(prompt, kept[s], q_row, acc)
         else:
             part, acc, buffers = whole_head(
-                s, meta, prompt, kept[s], gain_col, gain_row, acc, buffers, q.shape[1], k.shape[1]
+                s, meta, prompt, kept[s], q_row, k_row, acc, buffers, q.shape[1], k.shape[1]
             )
         parts.append(part)
         if direct and s > 0:
             backs.append(swap(part, s))
-    mine_flag = (me == owner).astype(jnp.int32)
     def settled(results, buffers):
-        return list(second_half(kv_heads - 1, meta, kept[-1], gain_col, gain_row, results, buffers))
+        return list(second_half(kv_heads - 1, meta, kept[-1], q_row, k_row, results, buffers))
 
     if direct:
         gains = acc + lax.ppermute(acc, "dp", [(i, i ^ 1) for i in range(n_dp)])
@@ -534,7 +538,7 @@
             step *= 2
         payload = join(parts[0], backs, gains)
         payloads = [payload] + [swap(payload, s) for s in range(1, n_group)]
-        placed, gains = place(jnp.concatenate([mine_flag[None], order]), payloads, depth, p_rows)
+        placed, gains = place(meta, payloads, depth, p_rows)
     else:
         total = lax.psum(jnp.concatenate(parts, axis=-1).astype(F32), "group").astype(BF)
         placed = jnp.where(mine_flag > 0, total, jnp.zeros((), BF))

time: 137 us -> 67.2 us (0.49); the launches traced: 135 us -> 67 us
  local copies, waits for them, and re-layouts: 71.4 us -> 0.76 us
  waiting for transfers between devices: 11.1 us -> 18 us
  Pallas kernels: 26.7 us -> 24 us
    unnamed x228 -> x4, local copies, waits for them, and re-layouts: 71.3 us -> 0.67 us
    ppermute x12, waiting for transfers between devices: 7.83 us -> 14.4 us  [swap(): return lax.ppermute(x, 'group', [(i, i ^ step) for i in range(n_group)])]
  transfers between devices with their start and end apart: 15 -> 15, of which waited for: 5 -> 8; matrix products, arithmetic and copies ran while one was open for 0% -> 0% of each run, Pallas kernels for 12% -> 22%
where the time goes in v12:
time: 67.2 us; the launch traced here: 67 us
  Pallas kernels  24 us (36%)
  starting transfers between devices  22.2 us (33%)
  waiting for transfers between devices  18 us (27%)
  between operations  2.06 us (3%)
  local copies, waits for them, and re-layouts  0.76 us (1%)
    ppermute x12, starting transfers between devices, swap(): return lax.ppermute(x, 'group', [(i, i ^ step) for i in range(n_group)])  19.2 us
    ppermute x12, waiting for transfers between devices, swap(): return lax.ppermute(x, 'group', [(i, i ^ step) for i in range(n_group)])  14.4 us
    pallas_call x3, Pallas kernels, whole_head(): pl.pallas_call(functools.partial(whole_kernel, s, 2 * HD), out_shape=[jax...  9.55 us
    pallas_call x2, Pallas kernels, prepare(): pl.pallas_call(functools.partial(prepare_kernel, turn, count, share, rows...  7.07 us
    ppermute x2, starting transfers between devices, local(): hop = lax.ppermute(gains, 'dp', [(i, i ^ step) for i in range(n_dp)])  3.01 us
    ppermute x2, waiting for transfers between devices, local(): hop = lax.ppermute(gains, 'dp', [(i, i ^ step) for i in range(n_dp)])  2.42 us
    pallas_call x1, Pallas kernels, first_half(): pl.pallas_call(functools.partial(first_kernel, 2 * HD), out_shape=[jax.Sh...  1.8 us
    pallas_call x1, Pallas kernels, second_half(): pl.pallas_call(functools.partial(second_kernel, s, 2 * HD), out_shape=out...  1.7 us
  transfers between devices with their start and end apart: 15, of which 8 were waited for; matrix products, arithmetic and copies ran while one was open for 0% of the time, Pallas kernels for 22%

profile of v12, /device:TPU:0, one launch (start us, length us, event | category | flops | bytes accessed | tf_op | source)
XLA Modules:
  0.0 67.0 jit_solution(12125919362150069273)
XLA Ops:
  2.0 1.7 %cut_prompt.1 = (bf16[2,256,128]{2,1,0:T(8,128)(2,1)S(1)}, bf16[2,256,128]{2,1,0:T(8,128)(2,1)S(1)}, bf16[2,256,128]{2,1,0:T(8,128)(2,1)S(1)}, bf16[2,256,128]{2,1,0:T(8,128)(2,1)S(1)}) custom-call(s32[4]{0:T(128)S(1)} %iota_xor_fusion.order, bf16[2,256,512]{2,1,0:T(8,128)(2,1)} %bitcast.41), custom_call_target="tpu_custom_call" | custom-call | tf_op jit(solution)/shard_map/cut_prompt/pallas_call | solution.py:48
  3.7 0.1 concatenate.3.meta
  3.7 5.6 %prepare_response.2 = (bf16[128,768]{1,0:T(8,128)(2,1)S(1)}, bf16[128,768]{1,0:T(8,128)(2,1)S(1)}, f32[8,768]{1,0:T(8,128)S(1)}, bf16[192,768]{1,0:T(8,128)(2,1)...) custom-call(s32[8]{0:T(128)S(1)} %concatenate.3.meta, ...), custom_call_target="tpu_custom_call" | custom-call | flops 452984832 | bytes 3932160 | tf_op jit(solution)/shard_map/prepare_response/pallas_call | solution.py:174
  9.4 5.1 %collective-permute-start.2 = (bf16[2,256,128]{2,1,0:T(8,128)(2,1)S(1)}, bf16[2,256,128]{2,1,0:T(8,128)(2,1)S(1)}, u32[]{:S(2)}, u32[]{:S(2)}) collective-permute-start(bf16[2,256,128]{2,1,0:T(8,128)(2,1)S(1)} %get-tuple-element.161), channel_id=1, source_target_pairs={{0,3},{1,2},{2,1},{3,0},{4,7},{5,6},{6,5},{7,4},{8,11},{9,10},{10,... | collective-permute-start | bytes 393224 | tf_op jit(solution)/shard_map/ppermute | solution.py:499
  14.5 0.0 collective-permute-start.1
  14.5 0.6 collective-permute-start
  15.1 1.4 %prepare_response.3 = (bf16[128,768]{1,0:T(8,128)(2,1)S(1)}, bf16[128,768]{1,0:T(8,128)(2,1)S(1)}, f32[8,768]{1,0:T(8,128)S(1)}, bf16[192,768]{1,0:T(8,128)(2,1)...) custom-call(s32[8]{0:T(128)S(1)} %concatenate.3.meta, ...), custom_call_target="tpu_custom_call" | custom-call | flops 452984832 | bytes 3932160 | tf_op jit(solution)/shard_map/prepare_response/pallas_call | solution.py:174
  16.6 1.0 %collective-permute-done.2.refs_3_ = bf16[2,256,128]{2,1,0:T(8,128)(2,1)S(1)} collective-permute-done((bf16[2,256,128]{2,1,0:T(8,128)(2,1)S(1)}, bf16[2,256,128]{2,1,0:T(8,128)(2,1)S(1)}, u32[]{:S(2)}, u32[]{:S(2)}) %collective-permute-start.2) | collective-permute-done | bytes 131104 | tf_op jit(solution)/shard_map/ppermute | solution.py:499
  17.6 4.0 %collective-permute-done.1.refs_2_ = bf16[2,256,128]{2,1,0:T(8,128)(2,1)S(1)} collective-permute-done((bf16[2,256,128]{2,1,0:T(8,128)(2,1)S(1)}, bf16[2,256,128]{2,1,0:T(8,128)(2,1)S(1)}, u32[]{:S(2)}, u32[]{:S(2)}) %collective-permute-start.1) | collective-permute-done | bytes 131104 | tf_op jit(solution)/shard_map/ppermute | solution.py:499
  21.6 1.6 %collective-permute-done.refs_1_ = bf16[2,256,128]{2,1,0:T(8,128)(2,1)S(1)} collective-permute-done((bf16[2,256,128]{2,1,0:T(8,128)(2,1)S(1)}, bf16[2,256,128]{2,1,0:T(8,128)(2,1)S(1)}, u32[]{:S(2)}, u32[]{:S(2)}) %collective-permute-start) | collective-permute-done | bytes 131104 | tf_op jit(solution)/shard_map/ppermute | solution.py:499
  23.2 0.6 pick_owner.1.pr_ref
  23.8 1.4 %collective-permute-start.5 = (bf16[2,256,128]{2,1,0:T(8,128)(2,1)S(1)}, bf16[2,256,128]{2,1,0:T(8,128)(2,1)S(1)}, u32[]{:S(2)}, u32[]{:S(2)}) collective-permute-start(bf16[2,256,128]{2,1,0:T(8,128)(2,1)S(1)} %pick_owner.1.pr_ref), channel_id=1, source_target_pairs={{0,1},{1,0},{2,3},{3,2},{4,5},{5,4},{6,7},{7,6},{8,9},{9,8},{10,11... | collective-permute-start | bytes 393224 | tf_op jit(solution)/shard_map/ppermute | solution.py:499
  25.2 1.6 %collective-permute-start.4 = (bf16[2,256,128]{2,1,0:T(8,128)(2,1)S(1)}, bf16[2,256,128]{2,1,0:T(8,128)(2,1)S(1)}, u32[]{:S(2)}, u32[]{:S(2)}) collective-permute-start(bf16[2,256,128]{2,1,0:T(8,128)(2,1)S(1)} %pick_owner.1.pr_ref), channel_id=1, source_target_pairs={{0,2},{1,3},{2,0},{3,1},{4,6},{5,7},{6,4},{7,5},{8,10},{9,11},{10,... | collective-permute-start | bytes 393224 | tf_op jit(solution)/shard_map/ppermute | solution.py:499
  26.9 1.4 %collective-permute-start.3 = (bf16[2,256,128]{2,1,0:T(8,128)(2,1)S(1)}, bf16[2,256,128]{2,1,0:T(8,128)(2,1)S(1)}, u32[]{:S(2)}, u32[]{:S(2)}) collective-permute-start(bf16[2,256,128]{2,1,0:T(8,128)(2,1)S(1)} %pick_owner.1.pr_ref), channel_id=1, source_target_pairs={{0,3},{1,2},{2,1},{3,0},{4,7},{5,6},{6,5},{7,4},{8,11},{9,10},{10,... | collective-permute-start | bytes 393224 | tf_op jit(solution)/shard_map/ppermute | solution.py:499
  28.2 0.0 copy-start
  28.2 0.0 copy-start.1
  28.2 0.6 copy-done
  28.9 0.0 copy-done.1
  28.9 3.2 %attend_head.3 = (bf16[2,256,128]{2,1,0:T(8,128)(2,1)S(1)}, f32[2,128]{1,0:T(2,128)S(1)}, bf16[192,2048]{1,0:T(8,128)(2,1)}, bf16[192,2048]{1,0:T(8,128)(2,1)}, ...) custom-call(s32[8]{0:T(128)S(1)} %concatenate.3.meta, bf16[2,256,128]{2,1,0:T(8,128)(2,1)S(1)} %pick_owner.1.pr_ref, ...), custom_call_target="tpu_custom_call" | custom-call | flops 276824064 | bytes 1048576 | tf_op jit(solution)/shard_map/attend_head/pallas_call | solution.py:338
  32.1 0.0 collective-permute-done.5.pr_ref
  32.1 3.2 %attend_head.4 = (bf16[2,256,128]{2,1,0:T(8,128)(2,1)S(1)}, f32[2,128]{1,0:T(2,128)S(1)}, bf16[192,2048]{1,0:T(8,128)(2,1)}, bf16[192,2048]{1,0:T(8,128)(2,1)}, ...) custom-call(s32[8]{0:T(128)S(1)} %concatenate.3.meta, ...), custom_call_target="tpu_custom_call", output_to_operand_aliasing={{2}: (13, {}), {3}: (14, {}), {4}: (15, {}), {5}: (16, {})} | custom-call | flops 276824064 | bytes 1048576 | tf_op jit(solution)/shard_map/attend_head/pallas_call | solution.py:338
  35.3 0.0 collective-permute-done.4.pr_ref
  35.3 3.2 %attend_head.5 = (bf16[2,256,128]{2,1,0:T(8,128)(2,1)S(1)}, f32[2,128]{1,0:T(2,128)S(1)}, bf16[192,2048]{1,0:T(8,128)(2,1)}, bf16[192,2048]{1,0:T(8,128)(2,1)}, ...) custom-call(s32[8]{0:T(128)S(1)} %concatenate.3.meta, ...), custom_call_target="tpu_custom_call", output_to_operand_aliasing={{2}: (13, {}), {3}: (14, {}), {4}: (15, {}), {5}: (16, {})} | custom-call | flops 276824064 | bytes 1048576 | tf_op jit(solution)/shard_map/attend_head/pallas_call | solution.py:338
  38.5 0.2 collective-permute-start.8
  38.7 2.8 %collective-permute-start.7 = (bf16[2,256,128]{2,1,0:T(8,128)(2,1)S(1)}, bf16[2,256,128]{2,1,0:T(8,128)(2,1)S(1)}, u32[]{:S(2)}, u32[]{:S(2)}) collective-permute-start(bf16[2,256,128]{2,1,0:T(8,128)(2,1)S(1)} %get-tuple-element.199), channel_id=1, source_target_pairs={{0,1},{1,0},{2,3},{3,2},{4,5},{5,4},{6,7},{7,6},{8,9},{9,8},{10,11... | collective-permute-start | bytes 393224 | tf_op jit(solution)/shard_map/ppermute | solution.py:499
  41.6 0.0 collective-permute-done.3.pr_ref
  41.6 1.8 %attend_last_head.1 = (bf16[2,256,128]{2,1,0:T(8,128)(2,1)S(1)}, f32[2,128]{1,0:T(2,128)S(1)}, bf16[128,768]{1,0:T(8,128)(2,1)S(1)}, f32[128,768]{1,0:T(8,128)S(...) custom-call(bf16[2,256,128]{2,1,0:T(8,128)(2,1)S(1)} %collective-permute-done.3.pr_ref, ...), custom_call_target="tpu_custom_call" | custom-call | flops 276824064 | bytes 1048576 | tf_op jit(solution)/shard_map/attend_last_head/pallas_call | solution.py:360
  43.4 1.4 %collective-permute-start.9 = (bf16[2,256,128]{2,1,0:T(8,128)(2,1)S(1)}, bf16[2,256,128]{2,1,0:T(8,128)(2,1)S(1)}, u32[]{:S(2)}, u32[]{:S(2)}) collective-permute-start(bf16[2,256,128]{2,1,0:T(8,128)(2,1)S(1)} %get-tuple-element.214), channel_id=1, source_target_pairs={{0,3},{1,2},{2,1},{3,0},{4,7},{5,6},{6,5},{7,4},{8,11},{9,10},{10,... | collective-permute-start | bytes 393224 | tf_op jit(solution)/shard_map/ppermute | solution.py:499
  44.8 0.0 collective-permute-start.6
  44.8 1.1 %collective-permute-done.6 = f32[2,128]{1,0:T(2,128)S(1)} collective-permute-done((f32[2,128]{1,0:T(2,128)S(1)}, f32[2,128]{1,0:T(2,128)S(1)}, u32[]{:S(2)}, u32[]{:S(2)}) %collective-permute-start.6) | collective-permute-done | bytes 1056 | tf_op jit(solution)/shard_map/ppermute | solution.py:531
  46.0 1.5 %collective-permute-start.10 = (f32[2,128]{1,0:T(2,128)S(1)}, f32[2,128]{1,0:T(2,128)S(1)}, u32[]{:S(2)}, u32[]{:S(2)}) collective-permute-start(f32[2,128]{1,0:T(2,128)S(1)} %add.14), channel_id=1, source_target_pairs={{0,8},{4,12},{8,0},{12,4},{16,24},{20,28},{24,16},{28,20},{1,9},{5... | collective-permute-start | bytes 3080 | tf_op jit(solution)/shard_map/ppermute | solution.py:536
  47.5 0.0 collective-permute-done.8.rest_1_
  47.5 0.0 collective-permute-done.7.rest_0_
  47.5 1.7 %settle_last_head.1 = (bf16[192,2048]{1,0:T(8,128)(2,1)}, bf16[192,2048]{1,0:T(8,128)(2,1)}, bf16[192,512]{1,0:T(8,128)(2,1)}, bf16[192,512]{1,0:T(8,128)(2,1)}) custom-call(s32[8]{0:T(128)S(1)} %concatenate.3.meta, bf16[128,768]{1,0:T(8,128)(2,1)S(1)} %get-tuple-element.144.rest_0_, ...), custom_call_target="tpu_custom_call", output_to_operand_aliasing={{0}: (15, {}), {1}: (16, {}), {2}: (17, {}), {3}: (18, {})} | custom-call | bytes 1048576 | tf_op jit(solution)/shard_map/settle_last_head/pallas_call | solution.py:381
  49.2 0.4 collective-permute-done.10
  49.5 1.5 %collective-permute-start.11 = (f32[2,128]{1,0:T(2,128)S(1)}, f32[2,128]{1,0:T(2,128)S(1)}, u32[]{:S(2)}, u32[]{:S(2)}) collective-permute-start(f32[2,128]{1,0:T(2,128)S(1)} %add.15), channel_id=1, source_target_pairs={{0,16},{4,20},{8,24},{12,28},{16,0},{20,4},{24,8},{28,12},{1,17},{... | collective-permute-start | bytes 3080 | tf_op jit(solution)/shard_map/ppermute | solution.py:536
  51.1 2.0 %collective-permute-done.11 = f32[2,128]{1,0:T(2,128)S(1)} collective-permute-done((f32[2,128]{1,0:T(2,128)S(1)}, f32[2,128]{1,0:T(2,128)S(1)}, u32[]{:S(2)}, u32[]{:S(2)}) %collective-permute-start.11) | collective-permute-done | bytes 1056 | tf_op jit(solution)/shard_map/ppermute | solution.py:536
  53.1 0.0 collective-permute-done.9.rest_2_
  53.1 0.1 join_parts.1.refs_0_
  53.2 0.1 collective-permute-start.12
  53.3 3.0 %collective-permute-start.13 = (bf16[528,128]{1,0:T(8,128)(2,1)S(1)}, bf16[528,128]{1,0:T(8,128)(2,1)S(1)}, u32[]{:S(2)}, u32[]{:S(2)}) collective-permute-start(bf16[528,128]{1,0:T(8,128)(2,1)S(1)} %join_parts.1.refs_0_), channel_id=1, source_target_pairs={{0,2},{1,3},{2,0},{3,1},{4,6},{5,7},{6,4},{7,5},{8,10},{9,11},{10,... | collective-permute-start | bytes 405512 | tf_op jit(solution)/shard_map/ppermute | solution.py:499
  56.3 1.4 %collective-permute-start.14 = (bf16[528,128]{1,0:T(8,128)(2,1)S(1)}, bf16[528,128]{1,0:T(8,128)(2,1)S(1)}, u32[]{:S(2)}, u32[]{:S(2)}) collective-permute-start(bf16[528,128]{1,0:T(8,128)(2,1)S(1)} %join_parts.1.refs_0_), channel_id=1, source_target_pairs={{0,3},{1,2},{2,1},{3,0},{4,7},{5,6},{6,5},{7,4},{8,11},{9,10},{10,... | collective-permute-start | bytes 405512 | tf_op jit(solution)/shard_map/ppermute | solution.py:499
  57.7 1.9 %collective-permute-done.12.refs_1_ = bf16[528,128]{1,0:T(8,128)(2,1)S(1)} collective-permute-done((bf16[528,128]{1,0:T(8,128)(2,1)S(1)}, bf16[528,128]{1,0:T(8,128)(2,1)S(1)}, u32[]{:S(2)}, u32[]{:S(2)}) %collective-permute-start.12) | collective-permute-done | bytes 135200 | tf_op jit(solution)/shard_map/ppermute | solution.py:499
  59.5 6.0 %collective-permute-done.13.refs_2_ = bf16[528,128]{1,0:T(8,128)(2,1)S(1)} collective-permute-done((bf16[528,128]{1,0:T(8,128)(2,1)S(1)}, bf16[528,128]{1,0:T(8,128)(2,1)S(1)}, u32[]{:S(2)}, u32[]{:S(2)}) %collective-permute-start.13) | collective-permute-done | bytes 135200 | tf_op jit(solution)/shard_map/ppermute | solution.py:499
  65.5 0.0 collective-permute-done.14.refs_3_
  65.5 1.5 %place_prompt_grad.1 = (bf16[2,256,512]{2,1,0:T(8,128)(2,1)}, f32[2,128]{1,0:T(2,128)}) custom-call(s32[8]{0:T(128)S(1)} %concatenate.3.meta, bf16[528,128]{1,0:T(8,128)(2,1)S(1)} %join_parts.1.refs_0_, bf16[528,128]{1,0:T(8,128)(2,1)S(1)} %collective-permute-done.12.refs_1_, bf16[528,128]{1,0:T(8,128)(2,1)S(1)} %collective-permute-done.13.refs_2_, ...), custom_call_target="tpu_custom_call" | custom-call | tf_op jit(solution)/shard_map/place_prompt_grad/pallas_call | solution.py:446
  (5 shorter events, 0.0 us)
Async XLA Ops:
  9.4 8.2 %collective-permute-start.2 = (bf16[2,256,128]{2,1,0:T(8,128)(2,1)S(1)}, bf16[2,256,128]{2,1,0:T(8,128)(2,1)S(1)}, u32[]{:S(2)}, u32[]{:S(2)}) collective-permute-start(bf16[2,256,128]{2,1,0:T(8,128)(2,1)S(1)} %get-tuple-element.161), channel_id=1, source_target_pairs={{0,3},{1,2},{2,1},{3,0},{4,7},{5,6},{6,5},{7,4},{8,11},{9,10},{10,... | collective-permute-start | bytes 393224 | tf_op jit(solution)/shard_map/ppermute | solution.py:499
  14.5 7.1 %collective-permute-start.1 = (bf16[2,256,128]{2,1,0:T(8,128)(2,1)S(1)}, bf16[2,256,128]{2,1,0:T(8,128)(2,1)S(1)}, u32[]{:S(2)}, u32[]{:S(2)}) collective-permute-start(bf16[2,256,128]{2,1,0:T(8,128)(2,1)S(1)} %get-tuple-element.158), channel_id=1, source_target_pairs={{0,2},{1,3},{2,0},{3,1},{4,6},{5,7},{6,4},{7,5},{8,10},{9,11},{10,... | collective-permute-start | bytes 393224 | tf_op jit(solution)/shard_map/ppermute | solution.py:499
  14.5 8.7 %collective-permute-start = (bf16[2,256,128]{2,1,0:T(8,128)(2,1)S(1)}, bf16[2,256,128]{2,1,0:T(8,128)(2,1)S(1)}, u32[]{:S(2)}, u32[]{:S(2)}) collective-permute-start(bf16[2,256,128]{2,1,0:T(8,128)(2,1)S(1)} %get-tuple-element.154), channel_id=1, source_target_pairs={{0,1},{1,0},{2,3},{3,2},{4,5},{5,4},{6,7},{7,6},{8,9},{9,8},{10,11... | collective-permute-start | bytes 393224 | tf_op jit(solution)/shard_map/ppermute | solution.py:499
  23.8 8.3 %collective-permute-start.5 = (bf16[2,256,128]{2,1,0:T(8,128)(2,1)S(1)}, bf16[2,256,128]{2,1,0:T(8,128)(2,1)S(1)}, u32[]{:S(2)}, u32[]{:S(2)}) collective-permute-start(bf16[2,256,128]{2,1,0:T(8,128)(2,1)S(1)} %pick_owner.1.pr_ref), channel_id=1, source_target_pairs={{0,1},{1,0},{2,3},{3,2},{4,5},{5,4},{6,7},{7,6},{8,9},{9,8},{10,11... | collective-permute-start | bytes 393224 | tf_op jit(solution)/shard_map/ppermute | solution.py:499
  25.2 10.1 %collective-permute-start.4 = (bf16[2,256,128]{2,1,0:T(8,128)(2,1)S(1)}, bf16[2,256,128]{2,1,0:T(8,128)(2,1)S(1)}, u32[]{:S(2)}, u32[]{:S(2)}) collective-permute-start(bf16[2,256,128]{2,1,0:T(8,128)(2,1)S(1)} %pick_owner.1.pr_ref), channel_id=1, source_target_pairs={{0,2},{1,3},{2,0},{3,1},{4,6},{5,7},{6,4},{7,5},{8,10},{9,11},{10,... | collective-permute-start | bytes 393224 | tf_op jit(solution)/shard_map/ppermute | solution.py:499
  26.9 14.7 %collective-permute-start.3 = (bf16[2,256,128]{2,1,0:T(8,128)(2,1)S(1)}, bf16[2,256,128]{2,1,0:T(8,128)(2,1)S(1)}, u32[]{:S(2)}, u32[]{:S(2)}) collective-permute-start(bf16[2,256,128]{2,1,0:T(8,128)(2,1)S(1)} %pick_owner.1.pr_ref), channel_id=1, source_target_pairs={{0,3},{1,2},{2,1},{3,0},{4,7},{5,6},{6,5},{7,4},{8,11},{9,10},{10,... | collective-permute-start | bytes 393224 | tf_op jit(solution)/shard_map/ppermute | solution.py:499
  28.2 0.7 copy-start
  28.2 0.7 copy-start.1
  38.5 9.0 %collective-permute-start.8 = (bf16[2,256,128]{2,1,0:T(8,128)(2,1)S(1)}, bf16[2,256,128]{2,1,0:T(8,128)(2,1)S(1)}, u32[]{:S(2)}, u32[]{:S(2)}) collective-permute-start(bf16[2,256,128]{2,1,0:T(8,128)(2,1)S(1)} %get-tuple-element.200), channel_id=1, source_target_pairs={{0,2},{1,3},{2,0},{3,1},{4,6},{5,7},{6,4},{7,5},{8,10},{9,11},{10,... | collective-permute-start | bytes 393224 | tf_op jit(solution)/shard_map/ppermute | solution.py:499
  38.7 8.7 %collective-permute-start.7 = (bf16[2,256,128]{2,1,0:T(8,128)(2,1)S(1)}, bf16[2,256,128]{2,1,0:T(8,128)(2,1)S(1)}, u32[]{:S(2)}, u32[]{:S(2)}) collective-permute-start(bf16[2,256,128]{2,1,0:T(8,128)(2,1)S(1)} %get-tuple-element.199), channel_id=1, source_target_pairs={{0,1},{1,0},{2,3},{3,2},{4,5},{5,4},{6,7},{7,6},{8,9},{9,8},{10,11... | collective-permute-start | bytes 393224 | tf_op jit(solution)/shard_map/ppermute | solution.py:499
  43.4 9.7 %collective-permute-start.9 = (bf16[2,256,128]{2,1,0:T(8,128)(2,1)S(1)}, bf16[2,256,128]{2,1,0:T(8,128)(2,1)S(1)}, u32[]{:S(2)}, u32[]{:S(2)}) collective-permute-start(bf16[2,256,128]{2,1,0:T(8,128)(2,1)S(1)} %get-tuple-element.214), channel_id=1, source_target_pairs={{0,3},{1,2},{2,1},{3,0},{4,7},{5,6},{6,5},{7,4},{8,11},{9,10},{10,... | collective-permute-start | bytes 393224 | tf_op jit(solution)/shard_map/ppermute | solution.py:499
  44.8 1.1 %collective-permute-start.6 = (f32[2,128]{1,0:T(2,128)S(1)}, f32[2,128]{1,0:T(2,128)S(1)}, u32[]{:S(2)}, u32[]{:S(2)}) collective-permute-start(f32[2,128]{1,0:T(2,128)S(1)} %get-tuple-element.198), channel_id=1, source_target_pairs={{0,4},{4,0},{8,12},{12,8},{16,20},{20,16},{24,28},{28,24},{1,5},{5... | collective-permute-start | bytes 3080 | tf_op jit(solution)/shard_map/ppermute | solution.py:531
  46.0 3.6 %collective-permute-start.10 = (f32[2,128]{1,0:T(2,128)S(1)}, f32[2,128]{1,0:T(2,128)S(1)}, u32[]{:S(2)}, u32[]{:S(2)}) collective-permute-start(f32[2,128]{1,0:T(2,128)S(1)} %add.14), channel_id=1, source_target_pairs={{0,8},{4,12},{8,0},{12,4},{16,24},{20,28},{24,16},{28,20},{1,9},{5... | collective-permute-start | bytes 3080 | tf_op jit(solution)/shard_map/ppermute | solution.py:536
  49.5 3.6 %collective-permute-start.11 = (f32[2,128]{1,0:T(2,128)S(1)}, f32[2,128]{1,0:T(2,128)S(1)}, u32[]{:S(2)}, u32[]{:S(2)}) collective-permute-start(f32[2,128]{1,0:T(2,128)S(1)} %add.15), channel_id=1, source_target_pairs={{0,16},{4,20},{8,24},{12,28},{16,0},{20,4},{24,8},{28,12},{1,17},{... | collective-permute-start | bytes 3080 | tf_op jit(solution)/shard_map/ppermute | solution.py:536
  53.2 6.3 %collective-permute-start.12 = (bf16[528,128]{1,0:T(8,128)(2,1)S(1)}, bf16[528,128]{1,0:T(8,128)(2,1)S(1)}, u32[]{:S(2)}, u32[]{:S(2)}) collective-permute-start(bf16[528,128]{1,0:T(8,128)(2,1)S(1)} %join_parts.1.refs_0_), channel_id=1, source_target_pairs={{0,1},{1,0},{2,3},{3,2},{4,5},{5,4},{6,7},{7,6},{8,9},{9,8},{10,11... | collective-permute-start | bytes 405512 | tf_op jit(solution)/shard_map/ppermute | solution.py:499
  53.3 12.2 %collective-permute-start.13 = (bf16[528,128]{1,0:T(8,128)(2,1)S(1)}, bf16[528,128]{1,0:T(8,128)(2,1)S(1)}, u32[]{:S(2)}, u32[]{:S(2)}) collective-permute-start(bf16[528,128]{1,0:T(8,128)(2,1)S(1)} %join_parts.1.refs_0_), channel_id=1, source_target_pairs={{0,2},{1,3},{2,0},{3,1},{4,6},{5,7},{6,4},{7,5},{8,10},{9,11},{10,... | collective-permute-start | bytes 405512 | tf_op jit(solution)/shard_map/ppermute | solution.py:499
  56.3 9.2 %collective-permute-start.14 = (bf16[528,128]{1,0:T(8,128)(2,1)S(1)}, bf16[528,128]{1,0:T(8,128)(2,1)S(1)}, u32[]{:S(2)}, u32[]{:S(2)}) collective-permute-start(bf16[528,128]{1,0:T(8,128)(2,1)S(1)} %join_parts.1.refs_0_), channel_id=1, source_target_pairs={{0,3},{1,2},{2,1},{3,0},{4,7},{5,6},{6,5},{7,4},{8,11},{9,10},{10,... | collective-permute-start | bytes 405512 | tf_op jit(solution)/shard_map/ppermute | solution.py:499

commit v13 on v12

--- a/solution.py
+++ b/solution.py
@@ -81,35 +81,36 @@
     return jnp.broadcast_to(row, (8, HD)).T[:, 0:1]
 
 
-def prepare_kernel(turn, count, share, rows, width, meta, q_in, g_in, k_in, v_in, gain_ref, kg_ref, *rest):
-    tail = count * KEPT + 6
-
-    @pl.when(meta[count + 1] == turn)
-    def _():
-        prepare_body(
-            count, share, rows, width, meta, q_in, g_in, k_in, v_in, gain_ref, kg_ref, *rest[-tail:]
-        )
-
-    if len(rest) > tail:
-
-        @pl.when(meta[count + 1] != turn)
+def prepare_kernel(turn, slots, share, rows, width, meta, *refs):
+    tail = len(slots) * KEPT + 6
+    before = len(refs) - 6 - tail
+    run = functools.partial(prepare_body, slots, share, rows, width, meta, *refs[:6], *refs[6 + before :])
+    if turn is None:
+        run()
+        return
+    mine = meta[meta.shape[0] - 3] == turn
+    pl.when(mine)(run)
+    if before > 0:
+
+        @pl.when(jnp.logical_not(mine))
         def _():
-            for old, new in zip(rest[:-tail], rest[-tail:-6]):
+            for old, new in zip(refs[6 : 6 + before], refs[6 + before : -6]):
                 new[...] = old[...]
 
 
-def prepare_body(count, share, rows, width, meta, q_in, g_in, k_in, v_in, gain_ref, kg_ref, *rest):
+def prepare_body(slots, share, rows, width, meta, q_in, g_in, k_in, v_in, gain_ref, kg_ref, *rest):
     outs, (q_buf, g_buf, k_buf, v_buf, gain_buf, sems) = rest[:-6], rest[-6:]
-    live_len = meta[count]
+    live_len = meta[meta.shape[0] - 4]
+    count = len(slots)
     scale = HD ** (-0.5)
     wide = share * HD
     copies = []
-    for s in range(count):
+    for s, slot in enumerate(slots):
         group = []
         for j, (src, buf, size) in enumerate(
             ((q_in, q_buf, wide), (k_in, k_buf, HD), (g_in, g_buf, wide), (v_in, v_buf, HD))
         ):
-            at = pl.multiple_of(meta[s] * size, size)
+            at = pl.multiple_of(meta[slot] * size, size)
             copy = pltpu.make_async_copy(src.at[:, pl.ds(at, size)], buf.at[s], sems.at[s, j])
             copy.start()
             group.append(copy)
@@ -157,7 +158,8 @@
             row_ref[1:2, cols] = jnp.sum(e_r, axis=0, keepdims=True)
 
 
-def prepare(turn, meta, q, g, k, v, q_gain, k_gain, count, before):
+def prepare(turn, slots, meta, q, g, k, v, q_gain, k_gain, before=()):
+    count = len(slots)
     rows, q_width = q.shape
     share = q_width // k.shape[1]
     total = share * rows
@@ -172,7 +174,7 @@
         jax.ShapeDtypeStruct((rows, 2 * HD), F32),
     ]
     outs = pl.pallas_call(
-        functools.partial(prepare_kernel, turn, count, share, rows, 2 * HD),
+        functools.partial(prepare_kernel, turn, slots, share, rows, 2 * HD),
         out_shape=each * count,
         in_specs=[SMEM] + [HBM] * 6 + [VMEM] * (KEPT * len(before)),
         out_specs=[VMEM] * (KEPT * count),
@@ -244,7 +246,7 @@
 
 
 def settle(width, head, live_len, kept, q_gain, k_gain, at_ref, dq_ref, d_kr, d_vr, outs, bufs, sems):
-    qt_ref, row_ref, ku_ref = kept[0], kept[2], kept[7]
+    qt_ref, row_ref, ku_ref = kept
     a_buf, q_buf, k_buf, v_buf = bufs
     rows, wide = a_buf.shape
     share = wide // HD
@@ -282,18 +284,7 @@
     for i in range(share):
         q_buf[:, i * HD : (i + 1) * HD] = d_q[i * rows : (i + 1) * rows, :]
     send(1, q_buf)
-    for copy in copies:
-        copy.wait()
-
-
-def whole_kernel(s, width, meta, pr_ref, *rest):
-    kept, (gain_ref, kg_ref, acc_ref) = rest[:KEPT], rest[KEPT : KEPT + 3]
-    part_ref, gacc_ref, *rest = rest[-13:]
-    outs, (at_ref, dq_ref), bufs, sems = rest[:4], rest[4:6], rest[6:10], rest[10]
-    q_gain = column(gain_ref[...])
-    d_kr, d_vr = attend(width, pr_ref, kept, q_gain, acc_ref, part_ref, at_ref, dq_ref, gacc_ref)
-    live_len = meta[meta.shape[0] - 4]
-    settle(width, meta[s], live_len, kept, q_gain, kg_ref[...], at_ref, dq_ref, d_kr, d_vr, outs, bufs, sems)
+    return copies
 
 
 def first_kernel(width, pr_ref, *rest):
@@ -304,14 +295,19 @@
     dvr_ref[...] = d_vr
 
 
-def second_kernel(s, width, meta, *rest):
-    kept, (gain_ref, kg_ref, at_ref, dq_ref, dkr_ref, dvr_ref) = rest[:KEPT], rest[KEPT : KEPT + 6]
+def settle_kernel(width, meta, gain_ref, kg_ref, *rest):
     outs, bufs, sems = rest[-9:-5], rest[-5:-1], rest[-1]
-    live_len = meta[meta.shape[0] - 4]
-    settle(
-        width, meta[s], live_len, kept, column(gain_ref[...]), kg_ref[...], at_ref, dq_ref,
-        dkr_ref[...], dvr_ref[...], outs, bufs, sems,
-    )
+    q_gain = column(gain_ref[...])
+    copies = []
+    for i in range(sems.shape[0]):
+        kept, results = rest[i * 7 : i * 7 + 3], rest[i * 7 + 3 : i * 7 + 7]
+        at_ref, dq_ref, dkr_ref, dvr_ref = results
+        copies += settle(
+            width, meta[i], meta[meta.shape[0] - 4], kept, q_gain, kg_ref[...], at_ref, dq_ref,
+            dkr_ref[...], dvr_ref[...], outs, [buf.at[i] for buf in bufs], sems.at[i],
+        )
+    for copy in copies:
+        copy.wait()
 
 
 def out_shapes(rows, q_width, k_width):
@@ -319,9 +315,9 @@
     return [jax.ShapeDtypeStruct((rows, w), BF) for w in widths]
 
 
-def out_scratch(rows, share):
+def out_scratch(count, rows, share):
     widths = (share * HD, share * HD, HD, HD)
-    return [pltpu.VMEM((rows, w), BF) for w in widths] + [pltpu.SemaphoreType.DMA((4,))]
+    return [pltpu.VMEM((count, rows, w), BF) for w in widths] + [pltpu.SemaphoreType.DMA((count, 4))]
 
 
 def cost(prompt_rows, rows, total):
@@ -330,28 +326,6 @@
         bytes_accessed=2**20,
         transcendentals=total * prompt_rows,
     )
-
-
-def whole_head(s, meta, prompt, kept, q_gain, k_gain, acc, buffers, q_width, k_width):
-    total = kept[0].shape[1]
-    rows = kept[3].shape[0]
-    outs = pl.pallas_call(
-        functools.partial(whole_kernel, s, 2 * HD),
-        out_shape=[
-            jax.ShapeDtypeStruct(prompt.shape, BF),
-            jax.ShapeDtypeStruct(acc.shape, F32),
-        ]
-        + out_shapes(rows, q_width, k_width),
-        in_specs=[SMEM] + [VMEM] * (4 + KEPT) + [HBM] * len(buffers),
-        out_specs=[VMEM] * 2 + [HBM] * 4,
-        scratch_shapes=[pltpu.VMEM((HD, total), BF), pltpu.VMEM((HD, total), F32)]
-        + out_scratch(rows, total // rows),
-        input_output_aliases={5 + KEPT + i: 2 + i for i in range(len(buffers))},
-        compiler_params=params(16),
-        cost_estimate=cost(prompt.shape[1], rows, total),
-        name="attend_head",
-    )(meta, prompt, *kept, q_gain, k_gain, acc, *buffers)
-    return outs[0], outs[1], outs[2:]
 
 
 def first_half(prompt, kept, q_gain, acc):
@@ -371,24 +345,24 @@
         out_specs=[VMEM] * 6,
         compiler_params=params(16),
         cost_estimate=cost(prompt.shape[1], rows, total),
-        name="attend_last_head",
+        name="attend_head",
     )(prompt, *kept, q_gain, acc)
 
 
-def second_half(s, meta, kept, q_gain, k_gain, results, buffers):
-    total = kept[0].shape[1]
-    rows = kept[3].shape[0]
+def settle_heads(meta, q_gain, k_gain, per_head, q_width, k_width):
+    count = len(per_head)
+    total = per_head[0][0].shape[1]
+    rows = per_head[0][5].shape[0]
+    flat = [x for group in per_head for x in group]
     return pl.pallas_call(
-        functools.partial(second_kernel, s, 2 * HD),
-        out_shape=out_shapes(rows, buffers[0].shape[1], buffers[2].shape[1]),
-        in_specs=[SMEM] + [VMEM] * (KEPT + 6) + [HBM] * 4,
+        functools.partial(settle_kernel, 2 * HD),
+        out_shape=out_shapes(rows, q_width, k_width),
+        in_specs=[SMEM] + [VMEM] * (2 + len(flat)),
         out_specs=[HBM] * 4,
-        scratch_shapes=out_scratch(rows, total // rows),
-        input_output_aliases={7 + KEPT + i: i for i in range(4)},
+        scratch_shapes=out_scratch(count, rows, total // rows),
         compiler_params=params(16),
-        cost_estimate=pl.CostEstimate(flops=0, bytes_accessed=2**20, transcendentals=0),
-        name="settle_last_head",
-    )(meta, *kept, q_gain, k_gain, *results, *buffers)
+        name="settle_heads",
+    )(meta, q_gain, k_gain, *flat)
 
 
 TAIL = 16
@@ -493,7 +467,10 @@
     q, g, k, v, *gains_in = [
         pltpu.with_memory_space_constraint(x, pltpu.HBM) for x in (q, g, k, v, q_gain, k_gain)
     ]
-    kept = prepare(0, meta, q, g, k, v, *gains_in, kv_heads, ())
+    half = kv_heads // 2 if direct else kv_heads
+    ahead, beside = tuple(range(half)), tuple(range(half, kv_heads))
+    acc = jnp.zeros((2, HD), F32)
+    kept = prepare(0 if direct else None, ahead, meta, q, g, k, v, *gains_in)
 
     def swap(x, step):
         return lax.ppermute(x, "group", [(i, i ^ step) for i in range(n_group)])
@@ -502,48 +479,53 @@
         blocks = list(cut(order, pltpu.with_memory_space_constraint(cache, pltpu.HBM), kv_heads))
         blocks[1:] = [after(x, kept[0][2]) for x in blocks[1:]]
         got = [blocks[0]] + [swap(blocks[s], s) for s in range(1, n_group)]
-        kept = prepare(1, meta, q, g, k, v, *gains_in, kv_heads, kept)
+        kept = prepare(1, ahead, meta, q, g, k, v, *gains_in, kept)
+        kept += prepare(None, beside, meta, q, g, k, v, *gains_in)
         for s in range(1, n_group):
-            got[s] = after(got[s], kept[0][2])
+            got[s] = after(got[s], kept[0][2], kept[-1][2])
         mine = pick(meta, got)
         prompts = [mine] + [swap(mine, s) for s in range(1, n_group)]
     else:
         cache = lax.psum(jnp.where(me == owner, cache, jnp.zeros_like(cache)), "group")
         prompts = cut(order, cache, kv_heads)
 
-    acc = jnp.zeros((2, HD), F32)
-    parts, backs, buffers = [], [], ()
+    parts, backs, per_head = [], [], []
     for s, prompt in enumerate(prompts):
-        last = s == kv_heads - 1
-        if last:
-            part, acc, *results = first_half(prompt, kept[s], q_row, acc)
-        else:
-            part, acc, buffers = whole_head(
-                s, meta, prompt, kept[s], q_row, k_row, acc, buffers, q.shape[1], k.shape[1]
-            )
+        part, acc, *results = first_half(prompt, kept[s], q_row, acc)
+        per_head.append([kept[s][0], kept[s][2], kept[s][7], *results])
         parts.append(part)
         if direct and s > 0:
             backs.append(swap(part, s))
-    def settled(results, buffers):
-        return list(second_half(kv_heads - 1, meta, kept[-1], q_row, k_row, results, buffers))
-
+
+    def hop(x, step):
+        return lax.ppermute(x, "dp", [(i, i ^ step) for i in range(n_dp)])
+
+    gains = acc + hop(acc, 1)
     if direct:
-        gains = acc + lax.ppermute(acc, "dp", [(i, i ^ 1) for i in range(n_dp)])
-        results[0] = after(results[0], gains, *backs[:-1])
-        buffers = settled(results, buffers)
-        step = 2
-        while step < n_dp:
-            hop = lax.ppermute(gains, "dp", [(i, i ^ step) for i in range(n_dp)])
-            gains = gains + (after(hop, buffers[2]) if step == 2 else hop)
+        gains = after(gains, *backs[:-1])
+    step = 2
+    while step < n_dp:
+        if 2 * step < n_dp:
+            near, far, both = hop(gains, step), hop(gains, 2 * step), hop(gains, 3 * step)
+            if direct:
+                near = after(near, *backs)
+            gains = (gains + near) + (far + both)
+            step *= 4
+        else:
+            gains = gains + hop(gains, step)
             step *= 2
+    if direct:
         payload = join(parts[0], backs, gains)
         payloads = [payload] + [swap(payload, s) for s in range(1, n_group)]
+        per_head[0][3] = after(per_head[0][3], payload)
+        buffers = settle_heads(meta, q_row, k_row, per_head, q.shape[1], k.shape[1])
+        payloads[1] = after(payloads[1], buffers[2])
         placed, gains = place(meta, payloads, depth, p_rows)
     else:
         total = lax.psum(jnp.concatenate(parts, axis=-1).astype(F32), "group").astype(BF)
         placed = jnp.where(mine_flag > 0, total, jnp.zeros((), BF))
-        gains = pair_sum(pair_sum(acc, "dp", n_dp), "group", n_group)
-        buffers = settled(results, buffers)
+        gains = pair_sum(gains, "group", n_group)
+        buffers = settle_heads(meta, q_row, k_row, per_head, q.shape[1], k.shape[1])
     attended, d_query, d_key, d_value = buffers
     return (
         attended[None, None],

time: 67.2 us -> 65.9 us (0.981)
  Pallas kernels: 24 us -> 21.8 us
    pallas_call x6 -> x4, Pallas kernels: 18.3 us -> 10.8 us  [the longest x3 8.2 us: prepare(): pl.pallas_call(functools.partial(prepare_kernel, turn, slots, share, rows...]
    pallas_call x1 -> x4, Pallas kernels: 1.8 us -> 7.2 us  [first_half(): pl.pallas_call(functools.partial(first_kernel, 2 * HD), out_shape=[jax.Sh...]
    ppermute x12, waiting for transfers between devices: 14.4 us -> 12.6 us  [swap(): return lax.ppermute(x, 'group', [(i, i ^ step) for i in range(n_group)])]
    ppermute x3 -> x4, waiting for transfers between devices: 3.55 us -> 5.12 us  [hop(): return lax.ppermute(x, 'dp', [(i, i ^ step) for i in range(n_dp)])]
    ppermute x3 -> x4, starting transfers between devices: 3.01 us -> 3.56 us  [hop(): return lax.ppermute(x, 'dp', [(i, i ^ step) for i in range(n_dp)])]
  transfers between devices with their start and end apart: 15 -> 16, of which waited for: 8 -> 7; matrix products, arithmetic and copies ran while one was open for 0% -> 0% of each run, Pallas kernels for 22% -> 22%
where the time goes in v13:
time: 65.9 us; the launch traced here: 65.7 us
  starting transfers between devices  22.7 us (34%)
  Pallas kernels  21.8 us (33%)
  waiting for transfers between devices  17.7 us (27%)
  between operations  2.07 us (3%)
  local copies, waits for them, and re-layouts  1.4 us (2%)
    ppermute x12, starting transfers between devices, swap(): return lax.ppermute(x, 'group', [(i, i ^ step) for i in range(n_group)])  19.2 us
    ppermute x12, waiting for transfers between devices, swap(): return lax.ppermute(x, 'group', [(i, i ^ step) for i in range(n_group)])  12.6 us
    pallas_call x3, Pallas kernels, prepare(): pl.pallas_call(functools.partial(prepare_kernel, turn, slots, share, rows...  8.2 us
    pallas_call x4, Pallas kernels, first_half(): pl.pallas_call(functools.partial(first_kernel, 2 * HD), out_shape=[jax.Sh...  7.2 us
    ppermute x4, waiting for transfers between devices, hop(): return lax.ppermute(x, 'dp', [(i, i ^ step) for i in range(n_dp)])  5.12 us
    ppermute x4, starting transfers between devices, hop(): return lax.ppermute(x, 'dp', [(i, i ^ step) for i in range(n_dp)])  3.56 us
    pallas_call x1, Pallas kernels, settle_heads(): pl.pallas_call(functools.partial(settle_kernel, 2 * HD), out_shape=out_sh...  2.6 us
    pallas_call x1, Pallas kernels, cut(): pl.pallas_call(cut_kernel, out_shape=[jax.ShapeDtypeStruct((depth, rows,...  1.69 us
  transfers between devices with their start and end apart: 16, of which 7 were waited for; matrix products, arithmetic and copies ran while one was open for 0% of the time, Pallas kernels for 22%

profile of v13, /device:TPU:0, one launch (start us, length us, event | category | flops | bytes accessed | tf_op | source)
XLA Modules:
  0.0 65.7 jit_solution(1839944250846848660)
XLA Ops:
  2.0 1.7 %cut_prompt.1 = (bf16[2,256,128]{2,1,0:T(8,128)(2,1)S(1)}, bf16[2,256,128]{2,1,0:T(8,128)(2,1)S(1)}, bf16[2,256,128]{2,1,0:T(8,128)(2,1)S(1)}, bf16[2,256,128]{2,1,0:T(8,128)(2,1)S(1)}) custom-call(s32[4]{0:T(128)S(1)} %iota_xor_fusion.order, bf16[2,256,512]{2,1,0:T(8,128)(2,1)} %bitcast.38), custom_call_target="tpu_custom_call" | custom-call | tf_op jit(solution)/shard_map/cut_prompt/pallas_call | solution.py:48
  3.7 0.1 concatenate.3.meta
  3.7 3.5 %prepare_response.3 = (bf16[128,768]{1,0:T(8,128)(2,1)S(1)}, bf16[128,768]{1,0:T(8,128)(2,1)S(1)}, f32[8,768]{1,0:T(8,128)S(1)}, bf16[192,768]{1,0:T(8,128)(2,1)...) custom-call(s32[8]{0:T(128)S(1)} %concatenate.3.meta, ...), custom_call_target="tpu_custom_call" | custom-call | flops 226492416 | bytes 3932160 | tf_op jit(solution)/shard_map/prepare_response/pallas_call | solution.py:176
  7.3 5.1 %collective-permute-start.2 = (bf16[2,256,128]{2,1,0:T(8,128)(2,1)S(1)}, bf16[2,256,128]{2,1,0:T(8,128)(2,1)S(1)}, u32[]{:S(2)}, u32[]{:S(2)}) collective-permute-start(bf16[2,256,128]{2,1,0:T(8,128)(2,1)S(1)} %get-tuple-element.126), channel_id=1, source_target_pairs={{0,3},{1,2},{2,1},{3,0},{4,7},{5,6},{6,5},{7,4},{8,11},{9,10},{10,... | collective-permute-start | bytes 393224 | tf_op jit(solution)/shard_map/ppermute | solution.py:476
  12.4 0.0 collective-permute-start.1
  12.4 0.6 collective-permute-start
  13.0 3.5 %prepare_response.5 = (bf16[128,768]{1,0:T(8,128)(2,1)S(1)}, bf16[128,768]{1,0:T(8,128)(2,1)S(1)}, f32[8,768]{1,0:T(8,128)S(1)}, bf16[192,768]{1,0:T(8,128)(2,1)...) custom-call(s32[8]{0:T(128)S(1)} %concatenate.3.meta, ...), custom_call_target="tpu_custom_call" | custom-call | flops 226492416 | bytes 3932160 | tf_op jit(solution)/shard_map/prepare_response/pallas_call | solution.py:176
  16.5 1.2 %prepare_response.4 = (bf16[128,768]{1,0:T(8,128)(2,1)S(1)}, bf16[128,768]{1,0:T(8,128)(2,1)S(1)}, f32[8,768]{1,0:T(8,128)S(1)}, bf16[192,768]{1,0:T(8,128)(2,1)...) custom-call(s32[8]{0:T(128)S(1)} %concatenate.3.meta, ...), custom_call_target="tpu_custom_call" | custom-call | flops 226492416 | bytes 3932160 | tf_op jit(solution)/shard_map/prepare_response/pallas_call | solution.py:176
  17.7 0.0 collective-permute-done.2.refs_3_
  17.7 2.9 %collective-permute-done.1.refs_2_ = bf16[2,256,128]{2,1,0:T(8,128)(2,1)S(1)} collective-permute-done((bf16[2,256,128]{2,1,0:T(8,128)(2,1)S(1)}, bf16[2,256,128]{2,1,0:T(8,128)(2,1)S(1)}, u32[]{:S(2)}, u32[]{:S(2)}) %collective-permute-start.1) | collective-permute-done | bytes 131104 | tf_op jit(solution)/shard_map/ppermute | solution.py:476
  20.6 0.0 collective-permute-done.refs_1_
  20.6 0.6 pick_owner.1.pr_ref
  21.2 0.1 collective-permute-start.3
  21.3 3.1 %collective-permute-start.5 = (bf16[2,256,128]{2,1,0:T(8,128)(2,1)S(1)}, bf16[2,256,128]{2,1,0:T(8,128)(2,1)S(1)}, u32[]{:S(2)}, u32[]{:S(2)}) collective-permute-start(bf16[2,256,128]{2,1,0:T(8,128)(2,1)S(1)} %pick_owner.1.pr_ref), channel_id=1, source_target_pairs={{0,2},{1,3},{2,0},{3,1},{4,6},{5,7},{6,4},{7,5},{8,10},{9,11},{10,... | collective-permute-start | bytes 393224 | tf_op jit(solution)/shard_map/ppermute | solution.py:476
  24.3 1.3 %collective-permute-start.7 = (bf16[2,256,128]{2,1,0:T(8,128)(2,1)S(1)}, bf16[2,256,128]{2,1,0:T(8,128)(2,1)S(1)}, u32[]{:S(2)}, u32[]{:S(2)}) collective-permute-start(bf16[2,256,128]{2,1,0:T(8,128)(2,1)S(1)} %pick_owner.1.pr_ref), channel_id=1, source_target_pairs={{0,3},{1,2},{2,1},{3,0},{4,7},{5,6},{6,5},{7,4},{8,11},{9,10},{10,... | collective-permute-start | bytes 393224 | tf_op jit(solution)/shard_map/ppermute | solution.py:476
  25.7 0.0 copy-start
  25.7 0.7 copy-done
  26.3 1.8 %attend_head.4 = (bf16[2,256,128]{2,1,0:T(8,128)(2,1)S(1)}, f32[2,128]{1,0:T(2,128)S(1)}, bf16[128,768]{1,0:T(8,128)(2,1)S(1)}, f32[128,768]{1,0:T(8,128)S(1)}, ...) custom-call(bf16[2,256,128]{2,1,0:T(8,128)(2,1)S(1)} %pick_owner.1.pr_ref, ...), custom_call_target="tpu_custom_call" | custom-call | flops 276824064 | bytes 1048576 | tf_op jit(solution)/shard_map/attend_head/pallas_call | solution.py:334
  28.1 0.0 collective-permute-done.3.pr_ref
  28.1 1.8 %attend_head.5 = (bf16[2,256,128]{2,1,0:T(8,128)(2,1)S(1)}, f32[2,128]{1,0:T(2,128)S(1)}, bf16[128,768]{1,0:T(8,128)(2,1)S(1)}, f32[128,768]{1,0:T(8,128)S(1)}, ...) custom-call(bf16[2,256,128]{2,1,0:T(8,128)(2,1)S(1)} %collective-permute-done.3.pr_ref, ...), custom_call_target="tpu_custom_call" | custom-call | flops 276824064 | bytes 1048576 | tf_op jit(solution)/shard_map/attend_head/pallas_call | solution.py:334
  29.9 5.1 %collective-permute-done.5.pr_ref = bf16[2,256,128]{2,1,0:T(8,128)(2,1)S(1)} collective-permute-done((bf16[2,256,128]{2,1,0:T(8,128)(2,1)S(1)}, bf16[2,256,128]{2,1,0:T(8,128)(2,1)S(1)}, u32[]{:S(2)}, u32[]{:S(2)}) %collective-permute-start.5) | collective-permute-done | bytes 131104 | tf_op jit(solution)/shard_map/ppermute | solution.py:476
  35.0 1.8 %attend_head.6 = (bf16[2,256,128]{2,1,0:T(8,128)(2,1)S(1)}, f32[2,128]{1,0:T(2,128)S(1)}, bf16[128,768]{1,0:T(8,128)(2,1)S(1)}, f32[128,768]{1,0:T(8,128)S(1)}, ...) custom-call(bf16[2,256,128]{2,1,0:T(8,128)(2,1)S(1)} %collective-permute-done.5.pr_ref, ...), custom_call_target="tpu_custom_call" | custom-call | flops 276824064 | bytes 1048576 | tf_op jit(solution)/shard_map/attend_head/pallas_call | solution.py:334
  36.8 0.1 collective-permute-start.6
  36.9 2.3 %collective-permute-start.4 = (bf16[2,256,128]{2,1,0:T(8,128)(2,1)S(1)}, bf16[2,256,128]{2,1,0:T(8,128)(2,1)S(1)}, u32[]{:S(2)}, u32[]{:S(2)}) collective-permute-start(bf16[2,256,128]{2,1,0:T(8,128)(2,1)S(1)} %get-tuple-element.144), channel_id=1, source_target_pairs={{0,1},{1,0},{2,3},{3,2},{4,5},{5,4},{6,7},{7,6},{8,9},{9,8},{10,11... | collective-permute-start | bytes 393224 | tf_op jit(solution)/shard_map/ppermute | solution.py:476
  39.2 0.0 collective-permute-done.7.pr_ref
  39.2 1.8 %attend_head.7 = (bf16[2,256,128]{2,1,0:T(8,128)(2,1)S(1)}, f32[2,128]{1,0:T(2,128)S(1)}, bf16[128,768]{1,0:T(8,128)(2,1)S(1)}, f32[128,768]{1,0:T(8,128)S(1)}, ...) custom-call(bf16[2,256,128]{2,1,0:T(8,128)(2,1)S(1)} %collective-permute-done.7.pr_ref, ...), custom_call_target="tpu_custom_call" | custom-call | flops 276824064 | bytes 1048576 | tf_op jit(solution)/shard_map/attend_head/pallas_call | solution.py:334
  41.0 2.1 %collective-permute-start.8 = (bf16[2,256,128]{2,1,0:T(8,128)(2,1)S(1)}, bf16[2,256,128]{2,1,0:T(8,128)(2,1)S(1)}, u32[]{:S(2)}, u32[]{:S(2)}) collective-permute-start(bf16[2,256,128]{2,1,0:T(8,128)(2,1)S(1)} %get-tuple-element.163), channel_id=1, source_target_pairs={{0,3},{1,2},{2,1},{3,0},{4,7},{5,6},{6,5},{7,4},{8,11},{9,10},{10,... | collective-permute-start | bytes 393224 | tf_op jit(solution)/shard_map/ppermute | solution.py:476
  43.2 0.0 collective-permute-start.9
  43.2 1.1 %collective-permute-done.9 = f32[2,128]{1,0:T(2,128)S(1)} collective-permute-done((f32[2,128]{1,0:T(2,128)S(1)}, f32[2,128]{1,0:T(2,128)S(1)}, u32[]{:S(2)}, u32[]{:S(2)}) %collective-permute-start.9) | collective-permute-done | bytes 1056 | tf_op jit(solution)/shard_map/ppermute | solution.py:501
  44.3 0.0 collective-permute-done.6.rest_1_
  44.3 0.0 collective-permute-done.4.rest_0_
  44.3 1.6 %collective-permute-start.10 = (f32[2,128]{1,0:T(2,128)S(1)}, f32[2,128]{1,0:T(2,128)S(1)}, u32[]{:S(2)}, u32[]{:S(2)}) collective-permute-start(f32[2,128]{1,0:T(2,128)S(1)} %add.17), channel_id=1, source_target_pairs={{0,8},{4,12},{8,0},{12,4},{16,24},{20,28},{24,16},{28,20},{1,9},{5... | collective-permute-start | bytes 3080 | tf_op jit(solution)/shard_map/ppermute | solution.py:501
  45.9 1.5 %collective-permute-start.11 = (f32[2,128]{1,0:T(2,128)S(1)}, f32[2,128]{1,0:T(2,128)S(1)}, u32[]{:S(2)}, u32[]{:S(2)}) collective-permute-start(f32[2,128]{1,0:T(2,128)S(1)} %add.17), channel_id=1, source_target_pairs={{0,16},{4,20},{8,24},{12,28},{16,0},{20,4},{24,8},{28,12},{1,17},{... | collective-permute-start | bytes 3080 | tf_op jit(solution)/shard_map/ppermute | solution.py:501
  47.4 0.5 collective-permute-start.12
  47.9 0.0 collective-permute-done.8.rest_2_
  47.9 0.1 collective-permute-done.10
  47.9 1.5 %collective-permute-done.11 = f32[2,128]{1,0:T(2,128)S(1)} collective-permute-done((f32[2,128]{1,0:T(2,128)S(1)}, f32[2,128]{1,0:T(2,128)S(1)}, u32[]{:S(2)}, u32[]{:S(2)}) %collective-permute-start.11) | collective-permute-done | bytes 1056 | tf_op jit(solution)/shard_map/ppermute | solution.py:501
  49.4 2.4 %collective-permute-done.12 = f32[2,128]{1,0:T(2,128)S(1)} collective-permute-done((f32[2,128]{1,0:T(2,128)S(1)}, f32[2,128]{1,0:T(2,128)S(1)}, u32[]{:S(2)}, u32[]{:S(2)}) %collective-permute-start.12) | collective-permute-done | bytes 1056 | tf_op jit(solution)/shard_map/ppermute | solution.py:501
  51.9 0.1 join_parts.1.refs_0_
  51.9 0.1 collective-permute-start.13
  52.0 2.3 %collective-permute-start.14 = (bf16[528,128]{1,0:T(8,128)(2,1)S(1)}, bf16[528,128]{1,0:T(8,128)(2,1)S(1)}, u32[]{:S(2)}, u32[]{:S(2)}) collective-permute-start(bf16[528,128]{1,0:T(8,128)(2,1)S(1)} %join_parts.1.refs_0_), channel_id=1, source_target_pairs={{0,2},{1,3},{2,0},{3,1},{4,6},{5,7},{6,4},{7,5},{8,10},{9,11},{10,... | collective-permute-start | bytes 405512 | tf_op jit(solution)/shard_map/ppermute | solution.py:476
  54.3 2.1 %collective-permute-start.15 = (bf16[528,128]{1,0:T(8,128)(2,1)S(1)}, bf16[528,128]{1,0:T(8,128)(2,1)S(1)}, u32[]{:S(2)}, u32[]{:S(2)}) collective-permute-start(bf16[528,128]{1,0:T(8,128)(2,1)S(1)} %join_parts.1.refs_0_), channel_id=1, source_target_pairs={{0,3},{1,2},{2,1},{3,0},{4,7},{5,6},{6,5},{7,4},{8,11},{9,10},{10,... | collective-permute-start | bytes 405512 | tf_op jit(solution)/shard_map/ppermute | solution.py:476
  56.4 0.0 copy-start.1
  56.4 0.7 copy-done.1
  57.0 2.6 %settle_heads.1 = (bf16[192,2048]{1,0:T(8,128)(2,1)}, bf16[192,2048]{1,0:T(8,128)(2,1)}, bf16[192,512]{1,0:T(8,128)(2,1)}, bf16[192,512]{1,0:T(8,128)(2,1)}) custom-call(s32[8]{0:T(128)S(1)} %concatenate.3.meta, f32[1,128]{1,0:T(1,128)S(1)} %bitcast.24, f32[1,128]{1,0:T(1,128)S(1)} %bitcast.25, bf16[128,768]{1,0:T(8,128)(2,1)S(1)} %get-tuple-element.114.rest_0_, ...), custom_call_target="tpu_custom_call" | custom-call | tf_op jit(solution)/shard_map/settle_heads/pallas_call | solution.py:357
  59.6 0.0 collective-permute-done.13.refs_1_
  59.7 4.6 %collective-permute-done.14.refs_2_ = bf16[528,128]{1,0:T(8,128)(2,1)S(1)} collective-permute-done((bf16[528,128]{1,0:T(8,128)(2,1)S(1)}, bf16[528,128]{1,0:T(8,128)(2,1)S(1)}, u32[]{:S(2)}, u32[]{:S(2)}) %collective-permute-start.14) | collective-permute-done | bytes 135200 | tf_op jit(solution)/shard_map/ppermute | solution.py:476
  64.2 0.0 collective-permute-done.15.refs_3_
  64.2 1.5 %place_prompt_grad.1 = (bf16[2,256,512]{2,1,0:T(8,128)(2,1)}, f32[2,128]{1,0:T(2,128)}) custom-call(s32[8]{0:T(128)S(1)} %concatenate.3.meta, bf16[528,128]{1,0:T(8,128)(2,1)S(1)} %join_parts.1.refs_0_, bf16[528,128]{1,0:T(8,128)(2,1)S(1)} %collective-permute-done.13.refs_1_, bf16[528,128]{1,0:T(8,128)(2,1)S(1)} %collective-permute-done.14.refs_2_, ...), custom_call_target="tpu_custom_call" | custom-call | tf_op jit(solution)/shard_map/place_prompt_grad/pallas_call | solution.py:420
  (4 shorter events, 0.0 us)
Async XLA Ops:
  7.3 10.5 %collective-permute-start.2 = (bf16[2,256,128]{2,1,0:T(8,128)(2,1)S(1)}, bf16[2,256,128]{2,1,0:T(8,128)(2,1)S(1)}, u32[]{:S(2)}, u32[]{:S(2)}) collective-permute-start(bf16[2,256,128]{2,1,0:T(8,128)(2,1)S(1)} %get-tuple-element.126), channel_id=1, source_target_pairs={{0,3},{1,2},{2,1},{3,0},{4,7},{5,6},{6,5},{7,4},{8,11},{9,10},{10,... | collective-permute-start | bytes 393224 | tf_op jit(solution)/shard_map/ppermute | solution.py:476
  12.4 8.2 %collective-permute-start.1 = (bf16[2,256,128]{2,1,0:T(8,128)(2,1)S(1)}, bf16[2,256,128]{2,1,0:T(8,128)(2,1)S(1)}, u32[]{:S(2)}, u32[]{:S(2)}) collective-permute-start(bf16[2,256,128]{2,1,0:T(8,128)(2,1)S(1)} %get-tuple-element.123), channel_id=1, source_target_pairs={{0,2},{1,3},{2,0},{3,1},{4,6},{5,7},{6,4},{7,5},{8,10},{9,11},{10,... | collective-permute-start | bytes 393224 | tf_op jit(solution)/shard_map/ppermute | solution.py:476
  12.4 8.2 %collective-permute-start = (bf16[2,256,128]{2,1,0:T(8,128)(2,1)S(1)}, bf16[2,256,128]{2,1,0:T(8,128)(2,1)S(1)}, u32[]{:S(2)}, u32[]{:S(2)}) collective-permute-start(bf16[2,256,128]{2,1,0:T(8,128)(2,1)S(1)} %get-tuple-element.119), channel_id=1, source_target_pairs={{0,1},{1,0},{2,3},{3,2},{4,5},{5,4},{6,7},{7,6},{8,9},{9,8},{10,11... | collective-permute-start | bytes 393224 | tf_op jit(solution)/shard_map/ppermute | solution.py:476
  21.2 6.9 %collective-permute-start.3 = (bf16[2,256,128]{2,1,0:T(8,128)(2,1)S(1)}, bf16[2,256,128]{2,1,0:T(8,128)(2,1)S(1)}, u32[]{:S(2)}, u32[]{:S(2)}) collective-permute-start(bf16[2,256,128]{2,1,0:T(8,128)(2,1)S(1)} %pick_owner.1.pr_ref), channel_id=1, source_target_pairs={{0,1},{1,0},{2,3},{3,2},{4,5},{5,4},{6,7},{7,6},{8,9},{9,8},{10,11... | collective-permute-start | bytes 393224 | tf_op jit(solution)/shard_map/ppermute | solution.py:476
  21.3 13.7 %collective-permute-start.5 = (bf16[2,256,128]{2,1,0:T(8,128)(2,1)S(1)}, bf16[2,256,128]{2,1,0:T(8,128)(2,1)S(1)}, u32[]{:S(2)}, u32[]{:S(2)}) collective-permute-start(bf16[2,256,128]{2,1,0:T(8,128)(2,1)S(1)} %pick_owner.1.pr_ref), channel_id=1, source_target_pairs={{0,2},{1,3},{2,0},{3,1},{4,6},{5,7},{6,4},{7,5},{8,10},{9,11},{10,... | collective-permute-start | bytes 393224 | tf_op jit(solution)/shard_map/ppermute | solution.py:476
  24.3 14.9 %collective-permute-start.7 = (bf16[2,256,128]{2,1,0:T(8,128)(2,1)S(1)}, bf16[2,256,128]{2,1,0:T(8,128)(2,1)S(1)}, u32[]{:S(2)}, u32[]{:S(2)}) collective-permute-start(bf16[2,256,128]{2,1,0:T(8,128)(2,1)S(1)} %pick_owner.1.pr_ref), channel_id=1, source_target_pairs={{0,3},{1,2},{2,1},{3,0},{4,7},{5,6},{6,5},{7,4},{8,11},{9,10},{10,... | collective-permute-start | bytes 393224 | tf_op jit(solution)/shard_map/ppermute | solution.py:476
  25.7 0.7 copy-start
  36.8 7.5 %collective-permute-start.6 = (bf16[2,256,128]{2,1,0:T(8,128)(2,1)S(1)}, bf16[2,256,128]{2,1,0:T(8,128)(2,1)S(1)}, u32[]{:S(2)}, u32[]{:S(2)}) collective-permute-start(bf16[2,256,128]{2,1,0:T(8,128)(2,1)S(1)} %get-tuple-element.154), channel_id=1, source_target_pairs={{0,2},{1,3},{2,0},{3,1},{4,6},{5,7},{6,4},{7,5},{8,10},{9,11},{10,... | collective-permute-start | bytes 393224 | tf_op jit(solution)/shard_map/ppermute | solution.py:476
  36.9 7.4 %collective-permute-start.4 = (bf16[2,256,128]{2,1,0:T(8,128)(2,1)S(1)}, bf16[2,256,128]{2,1,0:T(8,128)(2,1)S(1)}, u32[]{:S(2)}, u32[]{:S(2)}) collective-permute-start(bf16[2,256,128]{2,1,0:T(8,128)(2,1)S(1)} %get-tuple-element.144), channel_id=1, source_target_pairs={{0,1},{1,0},{2,3},{3,2},{4,5},{5,4},{6,7},{7,6},{8,9},{9,8},{10,11... | collective-permute-start | bytes 393224 | tf_op jit(solution)/shard_map/ppermute | solution.py:476
  41.0 6.9 %collective-permute-start.8 = (bf16[2,256,128]{2,1,0:T(8,128)(2,1)S(1)}, bf16[2,256,128]{2,1,0:T(8,128)(2,1)S(1)}, u32[]{:S(2)}, u32[]{:S(2)}) collective-permute-start(bf16[2,256,128]{2,1,0:T(8,128)(2,1)S(1)} %get-tuple-element.163), channel_id=1, source_target_pairs={{0,3},{1,2},{2,1},{3,0},{4,7},{5,6},{6,5},{7,4},{8,11},{9,10},{10,... | collective-permute-start | bytes 393224 | tf_op jit(solution)/shard_map/ppermute | solution.py:476
  43.2 1.1 %collective-permute-start.9 = (f32[2,128]{1,0:T(2,128)S(1)}, f32[2,128]{1,0:T(2,128)S(1)}, u32[]{:S(2)}, u32[]{:S(2)}) collective-permute-start(f32[2,128]{1,0:T(2,128)S(1)} %get-tuple-element.164), channel_id=1, source_target_pairs={{0,4},{4,0},{8,12},{12,8},{16,20},{20,16},{24,28},{28,24},{1,5},{5... | collective-permute-start | bytes 3080 | tf_op jit(solution)/shard_map/ppermute | solution.py:501
  44.3 3.6 %collective-permute-start.10 = (f32[2,128]{1,0:T(2,128)S(1)}, f32[2,128]{1,0:T(2,128)S(1)}, u32[]{:S(2)}, u32[]{:S(2)}) collective-permute-start(f32[2,128]{1,0:T(2,128)S(1)} %add.17), channel_id=1, source_target_pairs={{0,8},{4,12},{8,0},{12,4},{16,24},{20,28},{24,16},{28,20},{1,9},{5... | collective-permute-start | bytes 3080 | tf_op jit(solution)/shard_map/ppermute | solution.py:501
  45.9 3.6 %collective-permute-start.11 = (f32[2,128]{1,0:T(2,128)S(1)}, f32[2,128]{1,0:T(2,128)S(1)}, u32[]{:S(2)}, u32[]{:S(2)}) collective-permute-start(f32[2,128]{1,0:T(2,128)S(1)} %add.17), channel_id=1, source_target_pairs={{0,16},{4,20},{8,24},{12,28},{16,0},{20,4},{24,8},{28,12},{1,17},{... | collective-permute-start | bytes 3080 | tf_op jit(solution)/shard_map/ppermute | solution.py:501
  47.4 4.5 %collective-permute-start.12 = (f32[2,128]{1,0:T(2,128)S(1)}, f32[2,128]{1,0:T(2,128)S(1)}, u32[]{:S(2)}, u32[]{:S(2)}) collective-permute-start(f32[2,128]{1,0:T(2,128)S(1)} %add.17), channel_id=1, source_target_pairs={{0,24},{4,28},{8,16},{12,20},{16,8},{20,12},{24,0},{28,4},{1,25},{... | collective-permute-start | bytes 3080 | tf_op jit(solution)/shard_map/ppermute | solution.py:501
  51.9 7.7 %collective-permute-start.13 = (bf16[528,128]{1,0:T(8,128)(2,1)S(1)}, bf16[528,128]{1,0:T(8,128)(2,1)S(1)}, u32[]{:S(2)}, u32[]{:S(2)}) collective-permute-start(bf16[528,128]{1,0:T(8,128)(2,1)S(1)} %join_parts.1.refs_0_), channel_id=1, source_target_pairs={{0,1},{1,0},{2,3},{3,2},{4,5},{5,4},{6,7},{7,6},{8,9},{9,8},{10,11... | collective-permute-start | bytes 405512 | tf_op jit(solution)/shard_map/ppermute | solution.py:476
  52.0 12.2 %collective-permute-start.14 = (bf16[528,128]{1,0:T(8,128)(2,1)S(1)}, bf16[528,128]{1,0:T(8,128)(2,1)S(1)}, u32[]{:S(2)}, u32[]{:S(2)}) collective-permute-start(bf16[528,128]{1,0:T(8,128)(2,1)S(1)} %join_parts.1.refs_0_), channel_id=1, source_target_pairs={{0,2},{1,3},{2,0},{3,1},{4,6},{5,7},{6,4},{7,5},{8,10},{9,11},{10,... | collective-permute-start | bytes 405512 | tf_op jit(solution)/shard_map/ppermute | solution.py:476
  54.3 9.9 %collective-permute-start.15 = (bf16[528,128]{1,0:T(8,128)(2,1)S(1)}, bf16[528,128]{1,0:T(8,128)(2,1)S(1)}, u32[]{:S(2)}, u32[]{:S(2)}) collective-permute-start(bf16[528,128]{1,0:T(8,128)(2,1)S(1)} %join_parts.1.refs_0_), channel_id=1, source_target_pairs={{0,3},{1,2},{2,1},{3,0},{4,7},{5,6},{6,5},{7,4},{8,11},{9,10},{10,... | collective-permute-start | bytes 405512 | tf_op jit(solution)/shard_map/ppermute | solution.py:476
  56.4 0.7 copy-start.1

commit v14 on v13

--- a/solution.py
+++ b/solution.py
@@ -81,26 +81,9 @@
     return jnp.broadcast_to(row, (8, HD)).T[:, 0:1]
 
 
-def prepare_kernel(turn, slots, share, rows, width, meta, *refs):
-    tail = len(slots) * KEPT + 6
-    before = len(refs) - 6 - tail
-    run = functools.partial(prepare_body, slots, share, rows, width, meta, *refs[:6], *refs[6 + before :])
-    if turn is None:
-        run()
-        return
-    mine = meta[meta.shape[0] - 3] == turn
-    pl.when(mine)(run)
-    if before > 0:
-
-        @pl.when(jnp.logical_not(mine))
-        def _():
-            for old, new in zip(refs[6 : 6 + before], refs[6 + before : -6]):
-                new[...] = old[...]
-
-
-def prepare_body(slots, share, rows, width, meta, q_in, g_in, k_in, v_in, gain_ref, kg_ref, *rest):
+def prepare_kernel(slots, share, rows, width, meta, q_in, g_in, k_in, v_in, gain_ref, kg_ref, *rest):
     outs, (q_buf, g_buf, k_buf, v_buf, gain_buf, sems) = rest[:-6], rest[-6:]
-    live_len = meta[meta.shape[0] - 4]
+    live_len = meta[meta.shape[0] - 3]
     count = len(slots)
     scale = HD ** (-0.5)
     wide = share * HD
@@ -122,7 +105,8 @@
         gains.append(copy)
     for copy in gains:
         copy.wait()
-    q_gain = column(gain_buf[0].reshape(1, HD))
+    q_row = gain_buf[0].reshape(1, HD)
+    q_gain = column(q_row)
     k_gain = gain_buf[1].reshape(1, HD)
     for s in range(count):
         qt_ref, gt_ref, row_ref, er_ref, ot_ref, dp_ref, kh_ref, ku_ref = outs[s * KEPT : (s + 1) * KEPT]
@@ -131,6 +115,8 @@
         q_t = jnp.concatenate([q_buf[s, :, i * HD : (i + 1) * HD] for i in range(share)], axis=0).T
         g_t = jnp.concatenate([g_buf[s, :, i * HD : (i + 1) * HD] for i in range(share)], axis=0).T
         qt_ref[...] = q_t
+        row_ref[2:3, :HD] = q_row
+        row_ref[3:4, :HD] = k_gain
         raw_k = k_buf[s].astype(F32)
         k_inv = lax.rsqrt(jnp.mean(raw_k * raw_k, axis=-1, keepdims=True) + EPS)
         k_unit = raw_k * k_inv
@@ -158,7 +144,7 @@
             row_ref[1:2, cols] = jnp.sum(e_r, axis=0, keepdims=True)
 
 
-def prepare(turn, slots, meta, q, g, k, v, q_gain, k_gain, before=()):
+def prepare(slots, meta, q, g, k, v, q_gain, k_gain):
     count = len(slots)
     rows, q_width = q.shape
     share = q_width // k.shape[1]
@@ -174,9 +160,9 @@
         jax.ShapeDtypeStruct((rows, 2 * HD), F32),
     ]
     outs = pl.pallas_call(
-        functools.partial(prepare_kernel, turn, slots, share, rows, 2 * HD),
+        functools.partial(prepare_kernel, slots, share, rows, 2 * HD),
         out_shape=each * count,
-        in_specs=[SMEM] + [HBM] * 6 + [VMEM] * (KEPT * len(before)),
+        in_specs=[SMEM] + [HBM] * 6,
         out_specs=[VMEM] * (KEPT * count),
         scratch_shapes=[
             pltpu.VMEM((count, rows, share * HD), BF),
@@ -193,13 +179,14 @@
             transcendentals=count * total * rows,
         ),
         name="prepare_response",
-    )(meta, q, g, k, v, q_gain, k_gain, *[x for group in before for x in group])
+    )(meta, q, g, k, v, q_gain, k_gain)
     return [list(outs[s * KEPT : (s + 1) * KEPT]) for s in range(count)]
 
 
-def attend(width, pr_ref, kept, q_gain, acc_ref, part_ref, at_ref, dq_ref, gacc_ref):
+def attend(width, pr_ref, kept, acc_ref, part_ref, at_ref, dq_ref, gacc_ref):
     qt_ref, gt_ref, row_ref, er_ref, ot_ref, dp_ref, kh_ref, ku_ref = kept
     scale = HD ** (-0.5)
+    q_gain = column(row_ref[2:3, :HD])
     p_key = pr_ref[0]
     p_val = pr_ref[1]
     k_hat_t = kh_ref[...].T
@@ -245,8 +232,10 @@
     return d_kr, d_vr
 
 
-def settle(width, head, live_len, kept, q_gain, k_gain, at_ref, dq_ref, d_kr, d_vr, outs, bufs, sems):
+def settle(width, head, live_len, kept, at_ref, dq_ref, d_kr, d_vr, outs, bufs, sems):
     qt_ref, row_ref, ku_ref = kept
+    q_gain = column(row_ref[2:3, :HD])
+    k_gain = row_ref[3:4, :HD]
     a_buf, q_buf, k_buf, v_buf = bufs
     rows, wide = a_buf.shape
     share = wide // HD
@@ -288,22 +277,21 @@
 
 
 def first_kernel(width, pr_ref, *rest):
-    kept, (gain_ref, acc_ref) = rest[:KEPT], rest[KEPT : KEPT + 2]
+    kept, acc_ref = rest[:KEPT], rest[KEPT]
     part_ref, gacc_ref, at_ref, dq_ref, dkr_ref, dvr_ref = rest[-6:]
-    d_kr, d_vr = attend(width, pr_ref, kept, column(gain_ref[...]), acc_ref, part_ref, at_ref, dq_ref, gacc_ref)
+    d_kr, d_vr = attend(width, pr_ref, kept, acc_ref, part_ref, at_ref, dq_ref, gacc_ref)
     dkr_ref[...] = d_kr
     dvr_ref[...] = d_vr
 
 
-def settle_kernel(width, meta, gain_ref, kg_ref, *rest):
+def settle_kernel(width, meta, *rest):
     outs, bufs, sems = rest[-9:-5], rest[-5:-1], rest[-1]
-    q_gain = column(gain_ref[...])
     copies = []
     for i in range(sems.shape[0]):
         kept, results = rest[i * 7 : i * 7 + 3], rest[i * 7 + 3 : i * 7 + 7]
         at_ref, dq_ref, dkr_ref, dvr_ref = results
         copies += settle(
-            width, meta[i], meta[meta.shape[0] - 4], kept, q_gain, kg_ref[...], at_ref, dq_ref,
+            width, meta[i], meta[meta.shape[0] - 3], kept, at_ref, dq_ref,
             dkr_ref[...], dvr_ref[...], outs, [buf.at[i] for buf in bufs], sems.at[i],
         )
     for copy in copies:
@@ -328,7 +316,7 @@
     )
 
 
-def first_half(prompt, kept, q_gain, acc):
+def first_half(prompt, kept, acc):
     total = kept[0].shape[1]
     rows = kept[3].shape[0]
     return pl.pallas_call(
@@ -341,15 +329,15 @@
             jax.ShapeDtypeStruct((rows, HD), F32),
             jax.ShapeDtypeStruct((rows, HD), F32),
         ],
-        in_specs=[VMEM] * (3 + KEPT),
+        in_specs=[VMEM] * (2 + KEPT),
         out_specs=[VMEM] * 6,
         compiler_params=params(16),
         cost_estimate=cost(prompt.shape[1], rows, total),
         name="attend_head",
-    )(prompt, *kept, q_gain, acc)
-
-
-def settle_heads(meta, q_gain, k_gain, per_head, q_width, k_width):
+    )(prompt, *kept, acc)
+
+
+def settle_heads(meta, per_head, q_width, k_width):
     count = len(per_head)
     total = per_head[0][0].shape[1]
     rows = per_head[0][5].shape[0]
@@ -357,12 +345,12 @@
     return pl.pallas_call(
         functools.partial(settle_kernel, 2 * HD),
         out_shape=out_shapes(rows, q_width, k_width),
-        in_specs=[SMEM] + [VMEM] * (2 + len(flat)),
+        in_specs=[SMEM] + [VMEM] * len(flat),
         out_specs=[HBM] * 4,
         scratch_shapes=out_scratch(count, rows, total // rows),
         compiler_params=params(16),
         name="settle_heads",
-    )(meta, q_gain, k_gain, *flat)
+    )(meta, *flat)
 
 
 TAIL = 16
@@ -456,33 +444,25 @@
     depth, p_rows, _ = cache.shape
     direct = n_group == kv_heads
 
-    q_row = q_gain[None, :]
-    k_row = k_gain[None, :]
     order = jnp.arange(kv_heads, dtype=jnp.int32)
     if direct:
         order = order ^ me
-    turn = lax.axis_index("dp") % 2 if direct else jnp.int32(0)
     mine_flag = (me == owner).astype(jnp.int32)
-    meta = jnp.concatenate([order, jnp.stack([live_len, turn.astype(jnp.int32), owner ^ me, mine_flag])])
+    meta = jnp.concatenate([order, jnp.stack([live_len, owner ^ me, mine_flag])])
     q, g, k, v, *gains_in = [
         pltpu.with_memory_space_constraint(x, pltpu.HBM) for x in (q, g, k, v, q_gain, k_gain)
     ]
-    half = kv_heads // 2 if direct else kv_heads
-    ahead, beside = tuple(range(half)), tuple(range(half, kv_heads))
     acc = jnp.zeros((2, HD), F32)
-    kept = prepare(0 if direct else None, ahead, meta, q, g, k, v, *gains_in)
+    kept = prepare(tuple(range(kv_heads)), meta, q, g, k, v, *gains_in)
 
     def swap(x, step):
         return lax.ppermute(x, "group", [(i, i ^ step) for i in range(n_group)])
 
     if direct:
         blocks = list(cut(order, pltpu.with_memory_space_constraint(cache, pltpu.HBM), kv_heads))
-        blocks[1:] = [after(x, kept[0][2]) for x in blocks[1:]]
         got = [blocks[0]] + [swap(blocks[s], s) for s in range(1, n_group)]
-        kept = prepare(1, ahead, meta, q, g, k, v, *gains_in, kept)
-        kept += prepare(None, beside, meta, q, g, k, v, *gains_in)
         for s in range(1, n_group):
-            got[s] = after(got[s], kept[0][2], kept[-1][2])
+            got[s] = after(got[s], kept[0][2])
         mine = pick(meta, got)
         prompts = [mine] + [swap(mine, s) for s in range(1, n_group)]
     else:
@@ -491,7 +471,7 @@
 
     parts, backs, per_head = [], [], []
     for s, prompt in enumerate(prompts):
-        part, acc, *results = first_half(prompt, kept[s], q_row, acc)
+        part, acc, *results = first_half(prompt, kept[s], acc)
         per_head.append([kept[s][0], kept[s][2], kept[s][7], *results])
         parts.append(part)
         if direct and s > 0:
@@ -505,27 +485,20 @@
         gains = after(gains, *backs[:-1])
     step = 2
     while step < n_dp:
-        if 2 * step < n_dp:
-            near, far, both = hop(gains, step), hop(gains, 2 * step), hop(gains, 3 * step)
-            if direct:
-                near = after(near, *backs)
-            gains = (gains + near) + (far + both)
-            step *= 4
-        else:
-            gains = gains + hop(gains, step)
-            step *= 2
+        gains = gains + hop(gains, step)
+        step *= 2
     if direct:
         payload = join(parts[0], backs, gains)
         payloads = [payload] + [swap(payload, s) for s in range(1, n_group)]
         per_head[0][3] = after(per_head[0][3], payload)
-        buffers = settle_heads(meta, q_row, k_row, per_head, q.shape[1], k.shape[1])
+        buffers = settle_heads(meta, per_head, q.shape[1], k.shape[1])
         payloads[1] = after(payloads[1], buffers[2])
         placed, gains = place(meta, payloads, depth, p_rows)
     else:
         total = lax.psum(jnp.concatenate(parts, axis=-1).astype(F32), "group").astype(BF)
         placed = jnp.where(mine_flag > 0, total, jnp.zeros((), BF))
         gains = pair_sum(gains, "group", n_group)
-        buffers = settle_heads(meta, q_row, k_row, per_head, q.shape[1], k.shape[1])
+        buffers = settle_heads(meta, per_head, q.shape[1], k.shape[1])
     attended, d_query, d_key, d_value = buffers
     return (
         attended[None, None],

time: 65.9 us -> 65 us (0.986)
  waiting for transfers between devices: 17.7 us -> 21.8 us
  Pallas kernels: 21.8 us -> 19.3 us
  local copies, waits for them, and re-layouts: 1.4 us -> 0.01 us
  starting transfers between devices: 22.7 us -> 21.6 us
    ppermute x12, waiting for transfers between devices: 12.6 us -> 16.6 us  [swap(): return lax.ppermute(x, 'group', [(i, i ^ step) for i in range(n_group)])]
    pallas_call x3 -> x1, Pallas kernels: 8.2 us -> 5.64 us  [prepare(): pl.pallas_call(functools.partial(prepare_kernel, slots, share, rows, 2 *...]
    unnamed x4 -> x0, local copies, waits for them, and re-layouts: 1.31 us -> none
    ppermute x4 -> x3, starting transfers between devices: 3.56 us -> 3.02 us  [hop(): return lax.ppermute(x, 'dp', [(i, i ^ step) for i in range(n_dp)])]
    ppermute x4 -> x3, waiting for transfers between devices: 5.12 us -> 5.26 us  [hop(): return lax.ppermute(x, 'dp', [(i, i ^ step) for i in range(n_dp)])]
  transfers between devices with their start and end apart: 16 -> 15, of which waited for: 7 -> 10; matrix products, arithmetic and copies ran while one was open for 0% -> 0% of each run, Pallas kernels for 22% -> 24%
where the time goes in v14:
time: 65 us; the launch traced here: 64.9 us
  waiting for transfers between devices  21.8 us (34%)
  starting transfers between devices  21.6 us (33%)
  Pallas kernels  19.3 us (30%)
  between operations  2.02 us (3%)
    ppermute x12, starting transfers between devices, swap(): return lax.ppermute(x, 'group', [(i, i ^ step) for i in range(n_group)])  18.6 us
    ppermute x12, waiting for transfers between devices, swap(): return lax.ppermute(x, 'group', [(i, i ^ step) for i in range(n_group)])  16.6 us
    pallas_call x4, Pallas kernels, first_half(): pl.pallas_call(functools.partial(first_kernel, 2 * HD), out_shape=[jax.Sh...  7.17 us
    pallas_call x1, Pallas kernels, prepare(): pl.pallas_call(functools.partial(prepare_kernel, slots, share, rows, 2 *...  5.64 us
    ppermute x3, waiting for transfers between devices, hop(): return lax.ppermute(x, 'dp', [(i, i ^ step) for i in range(n_dp)])  5.26 us
    ppermute x3, starting transfers between devices, hop(): return lax.ppermute(x, 'dp', [(i, i ^ step) for i in range(n_dp)])  3.02 us
    pallas_call x1, Pallas kernels, settle_heads(): pl.pallas_call(functools.partial(settle_kernel, 2 * HD), out_shape=out_sh...  2.69 us
    pallas_call x1, Pallas kernels, cut(): pl.pallas_call(cut_kernel, out_shape=[jax.ShapeDtypeStruct((depth, rows,...  1.69 us
  transfers between devices with their start and end apart: 15, of which 10 were waited for; matrix products, arithmetic and copies ran while one was open for 0% of the time, Pallas kernels for 24%

profile of v14, /device:TPU:0, one launch (start us, length us, event | category | flops | bytes accessed | tf_op | source)
XLA Modules:
  0.0 64.9 jit_solution(10786371699160504196)
XLA Ops:
  0.6 1.7 %cut_prompt.1 = (bf16[2,256,128]{2,1,0:T(8,128)(2,1)S(1)}, bf16[2,256,128]{2,1,0:T(8,128)(2,1)S(1)}, bf16[2,256,128]{2,1,0:T(8,128)(2,1)S(1)}, bf16[2,256,128]{2,1,0:T(8,128)(2,1)S(1)}) custom-call(s32[4]{0:T(128)S(1)} %iota_xor_fusion.order, bf16[2,256,512]{2,1,0:T(8,128)(2,1)} %bitcast.19), custom_call_target="tpu_custom_call" | custom-call | tf_op jit(solution)/shard_map/cut_prompt/pallas_call | solution.py:48
  2.3 3.1 %collective-permute-start = (bf16[2,256,128]{2,1,0:T(8,128)(2,1)S(1)}, bf16[2,256,128]{2,1,0:T(8,128)(2,1)S(1)}, u32[]{:S(2)}, u32[]{:S(2)}) collective-permute-start(bf16[2,256,128]{2,1,0:T(8,128)(2,1)S(1)} %get-tuple-element.82), channel_id=1, source_target_pairs={{0,1},{1,0},{2,3},{3,2},{4,5},{5,4},{6,7},{7,6},{8,9},{9,8},{10,11... | collective-permute-start | bytes 393224 | tf_op jit(solution)/shard_map/ppermute | solution.py:459
  5.4 2.6 %collective-permute-start.1 = (bf16[2,256,128]{2,1,0:T(8,128)(2,1)S(1)}, bf16[2,256,128]{2,1,0:T(8,128)(2,1)S(1)}, u32[]{:S(2)}, u32[]{:S(2)}) collective-permute-start(bf16[2,256,128]{2,1,0:T(8,128)(2,1)S(1)} %get-tuple-element.84), channel_id=1, source_target_pairs={{0,2},{1,3},{2,0},{3,1},{4,6},{5,7},{6,4},{7,5},{8,10},{9,11},{10,... | collective-permute-start | bytes 393224 | tf_op jit(solution)/shard_map/ppermute | solution.py:459
  8.0 0.0 collective-permute-start.2
  9.3 0.1 pad_add_fusion.meta
  9.4 5.6 %prepare_response.1 = (bf16[128,768]{1,0:T(8,128)(2,1)S(1)}, bf16[128,768]{1,0:T(8,128)(2,1)S(1)}, f32[8,768]{1,0:T(8,128)S(1)}, bf16[192,768]{1,0:T(8,128)(2,1)...) custom-call(s32[7]{0:T(128)S(1)} %pad_add_fusion.meta, ...), custom_call_target="tpu_custom_call" | custom-call | flops 452984832 | bytes 3932160 | tf_op jit(solution)/shard_map/prepare_response/pallas_call | solution.py:162
  15.1 1.8 %collective-permute-done.2.refs_3_ = bf16[2,256,128]{2,1,0:T(8,128)(2,1)S(1)} collective-permute-done((bf16[2,256,128]{2,1,0:T(8,128)(2,1)S(1)}, bf16[2,256,128]{2,1,0:T(8,128)(2,1)S(1)}, u32[]{:S(2)}, u32[]{:S(2)}) %collective-permute-start.2) | collective-permute-done | bytes 131104 | tf_op jit(solution)/shard_map/ppermute | solution.py:459
  16.8 1.5 %collective-permute-done.1.refs_2_ = bf16[2,256,128]{2,1,0:T(8,128)(2,1)S(1)} collective-permute-done((bf16[2,256,128]{2,1,0:T(8,128)(2,1)S(1)}, bf16[2,256,128]{2,1,0:T(8,128)(2,1)S(1)}, u32[]{:S(2)}, u32[]{:S(2)}) %collective-permute-start.1) | collective-permute-done | bytes 131104 | tf_op jit(solution)/shard_map/ppermute | solution.py:459
  18.4 0.0 collective-permute-done.refs_1_
  18.4 0.6 pick_owner.1.pr_ref
  19.0 2.0 %collective-permute-start.3 = (bf16[2,256,128]{2,1,0:T(8,128)(2,1)S(1)}, bf16[2,256,128]{2,1,0:T(8,128)(2,1)S(1)}, u32[]{:S(2)}, u32[]{:S(2)}) collective-permute-start(bf16[2,256,128]{2,1,0:T(8,128)(2,1)S(1)} %pick_owner.1.pr_ref), channel_id=1, source_target_pairs={{0,1},{1,0},{2,3},{3,2},{4,5},{5,4},{6,7},{7,6},{8,9},{9,8},{10,11... | collective-permute-start | bytes 393224 | tf_op jit(solution)/shard_map/ppermute | solution.py:459
  21.0 1.1 %collective-permute-start.5 = (bf16[2,256,128]{2,1,0:T(8,128)(2,1)S(1)}, bf16[2,256,128]{2,1,0:T(8,128)(2,1)S(1)}, u32[]{:S(2)}, u32[]{:S(2)}) collective-permute-start(bf16[2,256,128]{2,1,0:T(8,128)(2,1)S(1)} %pick_owner.1.pr_ref), channel_id=1, source_target_pairs={{0,2},{1,3},{2,0},{3,1},{4,6},{5,7},{6,4},{7,5},{8,10},{9,11},{10,... | collective-permute-start | bytes 393224 | tf_op jit(solution)/shard_map/ppermute | solution.py:459
  22.1 1.4 %collective-permute-start.7 = (bf16[2,256,128]{2,1,0:T(8,128)(2,1)S(1)}, bf16[2,256,128]{2,1,0:T(8,128)(2,1)S(1)}, u32[]{:S(2)}, u32[]{:S(2)}) collective-permute-start(bf16[2,256,128]{2,1,0:T(8,128)(2,1)S(1)} %pick_owner.1.pr_ref), channel_id=1, source_target_pairs={{0,3},{1,2},{2,1},{3,0},{4,7},{5,6},{6,5},{7,4},{8,11},{9,10},{10,... | collective-permute-start | bytes 393224 | tf_op jit(solution)/shard_map/ppermute | solution.py:459
  23.5 1.8 %attend_head.4 = (bf16[2,256,128]{2,1,0:T(8,128)(2,1)S(1)}, f32[2,128]{1,0:T(2,128)S(1)}, bf16[128,768]{1,0:T(8,128)(2,1)S(1)}, f32[128,768]{1,0:T(8,128)S(1)}, ...) custom-call(bf16[2,256,128]{2,1,0:T(8,128)(2,1)S(1)} %pick_owner.1.pr_ref, ...), custom_call_target="tpu_custom_call" | custom-call | flops 276824064 | bytes 1048576 | tf_op jit(solution)/shard_map/attend_head/pallas_call | solution.py:322
  25.3 0.1 collective-permute-done.3.pr_ref
  25.4 1.8 %attend_head.5 = (bf16[2,256,128]{2,1,0:T(8,128)(2,1)S(1)}, f32[2,128]{1,0:T(2,128)S(1)}, bf16[128,768]{1,0:T(8,128)(2,1)S(1)}, f32[128,768]{1,0:T(8,128)S(1)}, ...) custom-call(bf16[2,256,128]{2,1,0:T(8,128)(2,1)S(1)} %collective-permute-done.3.pr_ref, ...), custom_call_target="tpu_custom_call" | custom-call | flops 276824064 | bytes 1048576 | tf_op jit(solution)/shard_map/attend_head/pallas_call | solution.py:322
  27.2 5.8 %collective-permute-done.5.pr_ref = bf16[2,256,128]{2,1,0:T(8,128)(2,1)S(1)} collective-permute-done((bf16[2,256,128]{2,1,0:T(8,128)(2,1)S(1)}, bf16[2,256,128]{2,1,0:T(8,128)(2,1)S(1)}, u32[]{:S(2)}, u32[]{:S(2)}) %collective-permute-start.5) | collective-permute-done | bytes 131104 | tf_op jit(solution)/shard_map/ppermute | solution.py:459
  32.9 1.8 %attend_head.6 = (bf16[2,256,128]{2,1,0:T(8,128)(2,1)S(1)}, f32[2,128]{1,0:T(2,128)S(1)}, bf16[128,768]{1,0:T(8,128)(2,1)S(1)}, f32[128,768]{1,0:T(8,128)S(1)}, ...) custom-call(bf16[2,256,128]{2,1,0:T(8,128)(2,1)S(1)} %collective-permute-done.5.pr_ref, ...), custom_call_target="tpu_custom_call" | custom-call | flops 276824064 | bytes 1048576 | tf_op jit(solution)/shard_map/attend_head/pallas_call | solution.py:322
  34.8 0.1 collective-permute-start.6
  34.8 3.6 %collective-permute-start.4 = (bf16[2,256,128]{2,1,0:T(8,128)(2,1)S(1)}, bf16[2,256,128]{2,1,0:T(8,128)(2,1)S(1)}, u32[]{:S(2)}, u32[]{:S(2)}) collective-permute-start(bf16[2,256,128]{2,1,0:T(8,128)(2,1)S(1)} %get-tuple-element.104), channel_id=1, source_target_pairs={{0,1},{1,0},{2,3},{3,2},{4,5},{5,4},{6,7},{7,6},{8,9},{9,8},{10,11... | collective-permute-start | bytes 393224 | tf_op jit(solution)/shard_map/ppermute | solution.py:459
  38.5 0.0 collective-permute-done.7.pr_ref
  38.5 1.8 %attend_head.7 = (bf16[2,256,128]{2,1,0:T(8,128)(2,1)S(1)}, f32[2,128]{1,0:T(2,128)S(1)}, bf16[128,768]{1,0:T(8,128)(2,1)S(1)}, f32[128,768]{1,0:T(8,128)S(1)}, ...) custom-call(bf16[2,256,128]{2,1,0:T(8,128)(2,1)S(1)} %collective-permute-done.7.pr_ref, ...), custom_call_target="tpu_custom_call" | custom-call | flops 276824064 | bytes 1048576 | tf_op jit(solution)/shard_map/attend_head/pallas_call | solution.py:322
  40.3 0.8 %collective-permute-start.8 = (bf16[2,256,128]{2,1,0:T(8,128)(2,1)S(1)}, bf16[2,256,128]{2,1,0:T(8,128)(2,1)S(1)}, u32[]{:S(2)}, u32[]{:S(2)}) collective-permute-start(bf16[2,256,128]{2,1,0:T(8,128)(2,1)S(1)} %get-tuple-element.124), channel_id=1, source_target_pairs={{0,3},{1,2},{2,1},{3,0},{4,7},{5,6},{6,5},{7,4},{8,11},{9,10},{10,... | collective-permute-start | bytes 393224 | tf_op jit(solution)/shard_map/ppermute | solution.py:459
  41.1 0.0 collective-permute-start.9
  41.1 1.1 %collective-permute-done.9 = f32[2,128]{1,0:T(2,128)S(1)} collective-permute-done((f32[2,128]{1,0:T(2,128)S(1)}, f32[2,128]{1,0:T(2,128)S(1)}, u32[]{:S(2)}, u32[]{:S(2)}) %collective-permute-start.9) | collective-permute-done | bytes 1056 | tf_op jit(solution)/shard_map/ppermute | solution.py:481
  42.2 2.5 %collective-permute-done.6.rest_1_ = bf16[2,256,128]{2,1,0:T(8,128)(2,1)S(1)} collective-permute-done((bf16[2,256,128]{2,1,0:T(8,128)(2,1)S(1)}, bf16[2,256,128]{2,1,0:T(8,128)(2,1)S(1)}, u32[]{:S(2)}, u32[]{:S(2)}) %collective-permute-start.6) | collective-permute-done | bytes 131104 | tf_op jit(solution)/shard_map/ppermute | solution.py:459
  44.7 0.0 collective-permute-done.4.rest_0_
  44.7 1.5 %collective-permute-start.10 = (f32[2,128]{1,0:T(2,128)S(1)}, f32[2,128]{1,0:T(2,128)S(1)}, u32[]{:S(2)}, u32[]{:S(2)}) collective-permute-start(f32[2,128]{1,0:T(2,128)S(1)} %add.9), channel_id=1, source_target_pairs={{0,8},{4,12},{8,0},{12,4},{16,24},{20,28},{24,16},{28,20},{1,9},{5... | collective-permute-start | bytes 3080 | tf_op jit(solution)/shard_map/ppermute | solution.py:481
  46.2 2.1 %collective-permute-done.10 = f32[2,128]{1,0:T(2,128)S(1)} collective-permute-done((f32[2,128]{1,0:T(2,128)S(1)}, f32[2,128]{1,0:T(2,128)S(1)}, u32[]{:S(2)}, u32[]{:S(2)}) %collective-permute-start.10) | collective-permute-done | bytes 1056 | tf_op jit(solution)/shard_map/ppermute | solution.py:481
  48.3 1.5 %collective-permute-start.11 = (f32[2,128]{1,0:T(2,128)S(1)}, f32[2,128]{1,0:T(2,128)S(1)}, u32[]{:S(2)}, u32[]{:S(2)}) collective-permute-start(f32[2,128]{1,0:T(2,128)S(1)} %add.10), channel_id=1, source_target_pairs={{0,16},{4,20},{8,24},{12,28},{16,0},{20,4},{24,8},{28,12},{1,17},{... | collective-permute-start | bytes 3080 | tf_op jit(solution)/shard_map/ppermute | solution.py:481
  49.8 2.0 %collective-permute-done.11 = f32[2,128]{1,0:T(2,128)S(1)} collective-permute-done((f32[2,128]{1,0:T(2,128)S(1)}, f32[2,128]{1,0:T(2,128)S(1)}, u32[]{:S(2)}, u32[]{:S(2)}) %collective-permute-start.11) | collective-permute-done | bytes 1056 | tf_op jit(solution)/shard_map/ppermute | solution.py:481
  51.9 0.0 collective-permute-done.8.rest_2_
  51.9 0.1 join_parts.1.refs_0_
  52.0 0.1 collective-permute-start.12
  52.0 3.3 %collective-permute-start.14 = (bf16[528,128]{1,0:T(8,128)(2,1)S(1)}, bf16[528,128]{1,0:T(8,128)(2,1)S(1)}, u32[]{:S(2)}, u32[]{:S(2)}) collective-permute-start(bf16[528,128]{1,0:T(8,128)(2,1)S(1)} %join_parts.1.refs_0_), channel_id=1, source_target_pairs={{0,3},{1,2},{2,1},{3,0},{4,7},{5,6},{6,5},{7,4},{8,11},{9,10},{10,... | collective-permute-start | bytes 405512 | tf_op jit(solution)/shard_map/ppermute | solution.py:459
  55.3 0.5 collective-permute-start.13
  55.8 2.7 %settle_heads.1 = (bf16[192,2048]{1,0:T(8,128)(2,1)}, bf16[192,2048]{1,0:T(8,128)(2,1)}, bf16[192,512]{1,0:T(8,128)(2,1)}, bf16[192,512]{1,0:T(8,128)(2,1)}) custom-call(s32[7]{0:T(128)S(1)} %pad_add_fusion.meta, bf16[128,768]{1,0:T(8,128)(2,1)S(1)} %get-tuple-element.78.rest_0_, f32[8,768]{1,0:T(8,128)S(1)} %get-tuple-element.79.rest_2_.rest_1_, ...), custom_call_target="tpu_custom_call" | custom-call | tf_op jit(solution)/shard_map/settle_heads/pallas_call | solution.py:345
  58.5 1.4 %collective-permute-done.12.refs_1_ = bf16[528,128]{1,0:T(8,128)(2,1)S(1)} collective-permute-done((bf16[528,128]{1,0:T(8,128)(2,1)S(1)}, bf16[528,128]{1,0:T(8,128)(2,1)S(1)}, u32[]{:S(2)}, u32[]{:S(2)}) %collective-permute-start.12) | collective-permute-done | bytes 135200 | tf_op jit(solution)/shard_map/ppermute | solution.py:459
  59.9 0.0 collective-permute-done.14.refs_3_
  59.9 3.5 %collective-permute-done.13.refs_2_ = bf16[528,128]{1,0:T(8,128)(2,1)S(1)} collective-permute-done((bf16[528,128]{1,0:T(8,128)(2,1)S(1)}, bf16[528,128]{1,0:T(8,128)(2,1)S(1)}, u32[]{:S(2)}, u32[]{:S(2)}) %collective-permute-start.13) | collective-permute-done | bytes 135200 | tf_op jit(solution)/shard_map/ppermute | solution.py:459
  63.4 1.5 %place_prompt_grad.1 = (bf16[2,256,512]{2,1,0:T(8,128)(2,1)}, f32[2,128]{1,0:T(2,128)}) custom-call(s32[7]{0:T(128)S(1)} %pad_add_fusion.meta, bf16[528,128]{1,0:T(8,128)(2,1)S(1)} %join_parts.1.refs_0_, bf16[528,128]{1,0:T(8,128)(2,1)S(1)} %collective-permute-done.12.refs_1_, bf16[528,128]{1,0:T(8,128)(2,1)S(1)} %collective-permute-done.13.refs_2_, ...), custom_call_target="tpu_custom_call" | custom-call | tf_op jit(solution)/shard_map/place_prompt_grad/pallas_call | solution.py:408
  (5 shorter events, 0.0 us)
Async XLA Ops:
  2.3 16.0 %collective-permute-start = (bf16[2,256,128]{2,1,0:T(8,128)(2,1)S(1)}, bf16[2,256,128]{2,1,0:T(8,128)(2,1)S(1)}, u32[]{:S(2)}, u32[]{:S(2)}) collective-permute-start(bf16[2,256,128]{2,1,0:T(8,128)(2,1)S(1)} %get-tuple-element.82), channel_id=1, source_target_pairs={{0,1},{1,0},{2,3},{3,2},{4,5},{5,4},{6,7},{7,6},{8,9},{9,8},{10,11... | collective-permute-start | bytes 393224 | tf_op jit(solution)/shard_map/ppermute | solution.py:459
  5.4 12.9 %collective-permute-start.1 = (bf16[2,256,128]{2,1,0:T(8,128)(2,1)S(1)}, bf16[2,256,128]{2,1,0:T(8,128)(2,1)S(1)}, u32[]{:S(2)}, u32[]{:S(2)}) collective-permute-start(bf16[2,256,128]{2,1,0:T(8,128)(2,1)S(1)} %get-tuple-element.84), channel_id=1, source_target_pairs={{0,2},{1,3},{2,0},{3,1},{4,6},{5,7},{6,4},{7,5},{8,10},{9,11},{10,... | collective-permute-start | bytes 393224 | tf_op jit(solution)/shard_map/ppermute | solution.py:459
  8.0 8.8 %collective-permute-start.2 = (bf16[2,256,128]{2,1,0:T(8,128)(2,1)S(1)}, bf16[2,256,128]{2,1,0:T(8,128)(2,1)S(1)}, u32[]{:S(2)}, u32[]{:S(2)}) collective-permute-start(bf16[2,256,128]{2,1,0:T(8,128)(2,1)S(1)} %get-tuple-element.86), channel_id=1, source_target_pairs={{0,3},{1,2},{2,1},{3,0},{4,7},{5,6},{6,5},{7,4},{8,11},{9,10},{10,... | collective-permute-start | bytes 393224 | tf_op jit(solution)/shard_map/ppermute | solution.py:459
  19.0 6.4 %collective-permute-start.3 = (bf16[2,256,128]{2,1,0:T(8,128)(2,1)S(1)}, bf16[2,256,128]{2,1,0:T(8,128)(2,1)S(1)}, u32[]{:S(2)}, u32[]{:S(2)}) collective-permute-start(bf16[2,256,128]{2,1,0:T(8,128)(2,1)S(1)} %pick_owner.1.pr_ref), channel_id=1, source_target_pairs={{0,1},{1,0},{2,3},{3,2},{4,5},{5,4},{6,7},{7,6},{8,9},{9,8},{10,11... | collective-permute-start | bytes 393224 | tf_op jit(solution)/shard_map/ppermute | solution.py:459
  21.0 11.9 %collective-permute-start.5 = (bf16[2,256,128]{2,1,0:T(8,128)(2,1)S(1)}, bf16[2,256,128]{2,1,0:T(8,128)(2,1)S(1)}, u32[]{:S(2)}, u32[]{:S(2)}) collective-permute-start(bf16[2,256,128]{2,1,0:T(8,128)(2,1)S(1)} %pick_owner.1.pr_ref), channel_id=1, source_target_pairs={{0,2},{1,3},{2,0},{3,1},{4,6},{5,7},{6,4},{7,5},{8,10},{9,11},{10,... | collective-permute-start | bytes 393224 | tf_op jit(solution)/shard_map/ppermute | solution.py:459
  22.1 16.4 %collective-permute-start.7 = (bf16[2,256,128]{2,1,0:T(8,128)(2,1)S(1)}, bf16[2,256,128]{2,1,0:T(8,128)(2,1)S(1)}, u32[]{:S(2)}, u32[]{:S(2)}) collective-permute-start(bf16[2,256,128]{2,1,0:T(8,128)(2,1)S(1)} %pick_owner.1.pr_ref), channel_id=1, source_target_pairs={{0,3},{1,2},{2,1},{3,0},{4,7},{5,6},{6,5},{7,4},{8,11},{9,10},{10,... | collective-permute-start | bytes 393224 | tf_op jit(solution)/shard_map/ppermute | solution.py:459
  34.8 10.0 %collective-permute-start.6 = (bf16[2,256,128]{2,1,0:T(8,128)(2,1)S(1)}, bf16[2,256,128]{2,1,0:T(8,128)(2,1)S(1)}, u32[]{:S(2)}, u32[]{:S(2)}) collective-permute-start(bf16[2,256,128]{2,1,0:T(8,128)(2,1)S(1)} %get-tuple-element.114), channel_id=1, source_target_pairs={{0,2},{1,3},{2,0},{3,1},{4,6},{5,7},{6,4},{7,5},{8,10},{9,11},{10,... | collective-permute-start | bytes 393224 | tf_op jit(solution)/shard_map/ppermute | solution.py:459
  34.8 9.9 %collective-permute-start.4 = (bf16[2,256,128]{2,1,0:T(8,128)(2,1)S(1)}, bf16[2,256,128]{2,1,0:T(8,128)(2,1)S(1)}, u32[]{:S(2)}, u32[]{:S(2)}) collective-permute-start(bf16[2,256,128]{2,1,0:T(8,128)(2,1)S(1)} %get-tuple-element.104), channel_id=1, source_target_pairs={{0,1},{1,0},{2,3},{3,2},{4,5},{5,4},{6,7},{7,6},{8,9},{9,8},{10,11... | collective-permute-start | bytes 393224 | tf_op jit(solution)/shard_map/ppermute | solution.py:459
  40.3 11.6 %collective-permute-start.8 = (bf16[2,256,128]{2,1,0:T(8,128)(2,1)S(1)}, bf16[2,256,128]{2,1,0:T(8,128)(2,1)S(1)}, u32[]{:S(2)}, u32[]{:S(2)}) collective-permute-start(bf16[2,256,128]{2,1,0:T(8,128)(2,1)S(1)} %get-tuple-element.124), channel_id=1, source_target_pairs={{0,3},{1,2},{2,1},{3,0},{4,7},{5,6},{6,5},{7,4},{8,11},{9,10},{10,... | collective-permute-start | bytes 393224 | tf_op jit(solution)/shard_map/ppermute | solution.py:459
  41.1 1.1 %collective-permute-start.9 = (f32[2,128]{1,0:T(2,128)S(1)}, f32[2,128]{1,0:T(2,128)S(1)}, u32[]{:S(2)}, u32[]{:S(2)}) collective-permute-start(f32[2,128]{1,0:T(2,128)S(1)} %get-tuple-element.125), channel_id=1, source_target_pairs={{0,4},{4,0},{8,12},{12,8},{16,20},{20,16},{24,28},{28,24},{1,5},{5... | collective-permute-start | bytes 3080 | tf_op jit(solution)/shard_map/ppermute | solution.py:481
  44.7 3.6 %collective-permute-start.10 = (f32[2,128]{1,0:T(2,128)S(1)}, f32[2,128]{1,0:T(2,128)S(1)}, u32[]{:S(2)}, u32[]{:S(2)}) collective-permute-start(f32[2,128]{1,0:T(2,128)S(1)} %add.9), channel_id=1, source_target_pairs={{0,8},{4,12},{8,0},{12,4},{16,24},{20,28},{24,16},{28,20},{1,9},{5... | collective-permute-start | bytes 3080 | tf_op jit(solution)/shard_map/ppermute | solution.py:481
  48.3 3.6 %collective-permute-start.11 = (f32[2,128]{1,0:T(2,128)S(1)}, f32[2,128]{1,0:T(2,128)S(1)}, u32[]{:S(2)}, u32[]{:S(2)}) collective-permute-start(f32[2,128]{1,0:T(2,128)S(1)} %add.10), channel_id=1, source_target_pairs={{0,16},{4,20},{8,24},{12,28},{16,0},{20,4},{24,8},{28,12},{1,17},{... | collective-permute-start | bytes 3080 | tf_op jit(solution)/shard_map/ppermute | solution.py:481
  52.0 8.0 %collective-permute-start.12 = (bf16[528,128]{1,0:T(8,128)(2,1)S(1)}, bf16[528,128]{1,0:T(8,128)(2,1)S(1)}, u32[]{:S(2)}, u32[]{:S(2)}) collective-permute-start(bf16[528,128]{1,0:T(8,128)(2,1)S(1)} %join_parts.1.refs_0_), channel_id=1, source_target_pairs={{0,1},{1,0},{2,3},{3,2},{4,5},{5,4},{6,7},{7,6},{8,9},{9,8},{10,11... | collective-permute-start | bytes 405512 | tf_op jit(solution)/shard_map/ppermute | solution.py:459
  52.0 7.9 %collective-permute-start.14 = (bf16[528,128]{1,0:T(8,128)(2,1)S(1)}, bf16[528,128]{1,0:T(8,128)(2,1)S(1)}, u32[]{:S(2)}, u32[]{:S(2)}) collective-permute-start(bf16[528,128]{1,0:T(8,128)(2,1)S(1)} %join_parts.1.refs_0_), channel_id=1, source_target_pairs={{0,3},{1,2},{2,1},{3,0},{4,7},{5,6},{6,5},{7,4},{8,11},{9,10},{10,... | collective-permute-start | bytes 405512 | tf_op jit(solution)/shard_map/ppermute | solution.py:459
  55.3 8.1 %collective-permute-start.13 = (bf16[528,128]{1,0:T(8,128)(2,1)S(1)}, bf16[528,128]{1,0:T(8,128)(2,1)S(1)}, u32[]{:S(2)}, u32[]{:S(2)}) collective-permute-start(bf16[528,128]{1,0:T(8,128)(2,1)S(1)} %join_parts.1.refs_0_), channel_id=1, source_target_pairs={{0,2},{1,3},{2,0},{3,1},{4,6},{5,7},{6,4},{7,5},{8,10},{9,11},{10,... | collective-permute-start | bytes 405512 | tf_op jit(solution)/shard_map/ppermute | solution.py:459

commit v15 on v14

--- a/solution.py
+++ b/solution.py
@@ -442,13 +442,15 @@
     me = lax.axis_index("group")
     kv_heads = k.shape[1] // HD
     depth, p_rows, _ = cache.shape
-    direct = n_group == kv_heads
+    direct = n_group == kv_heads and n_group <= 4
+    steps = [s ^ (s >> 1) for s in range(kv_heads)]
 
     order = jnp.arange(kv_heads, dtype=jnp.int32)
     if direct:
-        order = order ^ me
+        order = order ^ (order >> 1) ^ me
     mine_flag = (me == owner).astype(jnp.int32)
-    meta = jnp.concatenate([order, jnp.stack([live_len, owner ^ me, mine_flag])])
+    away = owner ^ me
+    meta = jnp.concatenate([order, jnp.stack([live_len, away ^ (away >> 1), mine_flag])])
     q, g, k, v, *gains_in = [
         pltpu.with_memory_space_constraint(x, pltpu.HBM) for x in (q, g, k, v, q_gain, k_gain)
     ]
@@ -460,11 +462,11 @@
 
     if direct:
         blocks = list(cut(order, pltpu.with_memory_space_constraint(cache, pltpu.HBM), kv_heads))
-        got = [blocks[0]] + [swap(blocks[s], s) for s in range(1, n_group)]
+        got = [blocks[0]] + [swap(blocks[s], steps[s]) for s in range(1, n_group)]
         for s in range(1, n_group):
             got[s] = after(got[s], kept[0][2])
         mine = pick(meta, got)
-        prompts = [mine] + [swap(mine, s) for s in range(1, n_group)]
+        prompts = [mine] + [swap(mine, steps[s]) for s in range(1, n_group)]
     else:
         cache = lax.psum(jnp.where(me == owner, cache, jnp.zeros_like(cache)), "group")
         prompts = cut(order, cache, kv_heads)
@@ -475,7 +477,7 @@
         per_head.append([kept[s][0], kept[s][2], kept[s][7], *results])
         parts.append(part)
         if direct and s > 0:
-            backs.append(swap(part, s))
+            backs.append(swap(part, steps[s]))
 
     def hop(x, step):
         return lax.ppermute(x, "dp", [(i, i ^ step) for i in range(n_dp)])
@@ -489,7 +491,7 @@
         step *= 2
     if direct:
         payload = join(parts[0], backs, gains)
-        payloads = [payload] + [swap(payload, s) for s in range(1, n_group)]
+        payloads = [payload] + [swap(payload, steps[s]) for s in range(1, n_group)]
         per_head[0][3] = after(per_head[0][3], payload)
         buffers = settle_heads(meta, per_head, q.shape[1], k.shape[1])
         payloads[1] = after(payloads[1], buffers[2])

time: 65 us -> 64.6 us (level)
  waiting for transfers between devices: 21.8 us -> 18.4 us
  starting transfers between devices: 21.6 us -> 24.5 us
    ppermute x12, waiting for transfers between devices: 16.6 us -> 13.2 us  [swap(): return lax.ppermute(x, 'group', [(i, i ^ step) for i in range(n_group)])]
    ppermute x12, starting transfers between devices: 18.6 us -> 21.4 us  [swap(): return lax.ppermute(x, 'group', [(i, i ^ step) for i in range(n_group)])]
where the time goes in v15:
time: 64.6 us; the launch traced here: 64.4 us
  starting transfers between devices  24.5 us (38%)
  Pallas kernels  19.3 us (30%)
  waiting for transfers between devices  18.4 us (28%)
  between operations  2.03 us (3%)
    ppermute x12, starting transfers between devices, swap(): return lax.ppermute(x, 'group', [(i, i ^ step) for i in range(n_group)])  21.4 us
    ppermute x12, waiting for transfers between devices, swap(): return lax.ppermute(x, 'group', [(i, i ^ step) for i in range(n_group)])  13.2 us
    pallas_call x4, Pallas kernels, first_half(): pl.pallas_call(functools.partial(first_kernel, 2 * HD), out_shape=[jax.Sh...  7.17 us
    pallas_call x1, Pallas kernels, prepare(): pl.pallas_call(functools.partial(prepare_kernel, slots, share, rows, 2 *...  5.64 us
    ppermute x3, waiting for transfers between devices, hop(): return lax.ppermute(x, 'dp', [(i, i ^ step) for i in range(n_dp)])  5.26 us
    ppermute x3, starting transfers between devices, hop(): return lax.ppermute(x, 'dp', [(i, i ^ step) for i in range(n_dp)])  3.08 us
    pallas_call x1, Pallas kernels, settle_heads(): pl.pallas_call(functools.partial(settle_kernel, 2 * HD), out_shape=out_sh...  2.69 us
    pallas_call x1, Pallas kernels, cut(): pl.pallas_call(cut_kernel, out_shape=[jax.ShapeDtypeStruct((depth, rows,...  1.69 us
  transfers between devices with their start and end apart: 15, of which 10 were waited for; matrix products, arithmetic and copies ran while one was open for 0% of the time, Pallas kernels for 24%

profile of v15, /device:TPU:0, one launch (start us, length us, event | category | flops | bytes accessed | tf_op | source)
XLA Modules:
  0.0 64.4 jit_solution(18108416992579138317)
XLA Ops:
  0.6 1.7 %cut_prompt.1 = (bf16[2,256,128]{2,1,0:T(8,128)(2,1)S(1)}, bf16[2,256,128]{2,1,0:T(8,128)(2,1)S(1)}, bf16[2,256,128]{2,1,0:T(8,128)(2,1)S(1)}, bf16[2,256,128]{2,1,0:T(8,128)(2,1)S(1)}) custom-call(s32[4]{0:T(128)S(1)} %fusion.order, bf16[2,256,512]{2,1,0:T(8,128)(2,1)} %bitcast.19), custom_call_target="tpu_custom_call" | custom-call | tf_op jit(solution)/shard_map/cut_prompt/pallas_call | solution.py:48
  2.3 3.1 %collective-permute-start = (bf16[2,256,128]{2,1,0:T(8,128)(2,1)S(1)}, bf16[2,256,128]{2,1,0:T(8,128)(2,1)S(1)}, u32[]{:S(2)}, u32[]{:S(2)}) collective-permute-start(bf16[2,256,128]{2,1,0:T(8,128)(2,1)S(1)} %get-tuple-element.82), channel_id=1, source_target_pairs={{0,1},{1,0},{2,3},{3,2},{4,5},{5,4},{6,7},{7,6},{8,9},{9,8},{10,11... | collective-permute-start | bytes 393224 | tf_op jit(solution)/shard_map/ppermute | solution.py:461
  5.4 2.5 %collective-permute-start.1 = (bf16[2,256,128]{2,1,0:T(8,128)(2,1)S(1)}, bf16[2,256,128]{2,1,0:T(8,128)(2,1)S(1)}, u32[]{:S(2)}, u32[]{:S(2)}) collective-permute-start(bf16[2,256,128]{2,1,0:T(8,128)(2,1)S(1)} %get-tuple-element.84), channel_id=1, source_target_pairs={{0,3},{1,2},{2,1},{3,0},{4,7},{5,6},{6,5},{7,4},{8,11},{9,10},{10,... | collective-permute-start | bytes 393224 | tf_op jit(solution)/shard_map/ppermute | solution.py:461
  7.9 0.1 collective-permute-start.2
  9.3 0.1 pad_add_fusion.meta
  9.4 5.6 %prepare_response.1 = (bf16[128,768]{1,0:T(8,128)(2,1)S(1)}, bf16[128,768]{1,0:T(8,128)(2,1)S(1)}, f32[8,768]{1,0:T(8,128)S(1)}, bf16[192,768]{1,0:T(8,128)(2,1)...) custom-call(s32[7]{0:T(128)S(1)} %pad_add_fusion.meta, ...), custom_call_target="tpu_custom_call" | custom-call | flops 452984832 | bytes 3932160 | tf_op jit(solution)/shard_map/prepare_response/pallas_call | solution.py:162
  15.1 4.6 %collective-permute-done.2.refs_3_ = bf16[2,256,128]{2,1,0:T(8,128)(2,1)S(1)} collective-permute-done((bf16[2,256,128]{2,1,0:T(8,128)(2,1)S(1)}, bf16[2,256,128]{2,1,0:T(8,128)(2,1)S(1)}, u32[]{:S(2)}, u32[]{:S(2)}) %collective-permute-start.2) | collective-permute-done | bytes 131104 | tf_op jit(solution)/shard_map/ppermute | solution.py:461
  19.7 0.0 collective-permute-done.1.refs_2_
  19.7 0.0 collective-permute-done.refs_1_
  19.7 0.6 pick_owner.1.pr_ref
  20.3 0.1 collective-permute-start.3
  20.4 2.7 %collective-permute-start.5 = (bf16[2,256,128]{2,1,0:T(8,128)(2,1)S(1)}, bf16[2,256,128]{2,1,0:T(8,128)(2,1)S(1)}, u32[]{:S(2)}, u32[]{:S(2)}) collective-permute-start(bf16[2,256,128]{2,1,0:T(8,128)(2,1)S(1)} %pick_owner.1.pr_ref), channel_id=1, source_target_pairs={{0,3},{1,2},{2,1},{3,0},{4,7},{5,6},{6,5},{7,4},{8,11},{9,10},{10,... | collective-permute-start | bytes 393224 | tf_op jit(solution)/shard_map/ppermute | solution.py:461
  23.1 0.8 %collective-permute-start.7 = (bf16[2,256,128]{2,1,0:T(8,128)(2,1)S(1)}, bf16[2,256,128]{2,1,0:T(8,128)(2,1)S(1)}, u32[]{:S(2)}, u32[]{:S(2)}) collective-permute-start(bf16[2,256,128]{2,1,0:T(8,128)(2,1)S(1)} %pick_owner.1.pr_ref), channel_id=1, source_target_pairs={{0,2},{1,3},{2,0},{3,1},{4,6},{5,7},{6,4},{7,5},{8,10},{9,11},{10,... | collective-permute-start | bytes 393224 | tf_op jit(solution)/shard_map/ppermute | solution.py:461
  23.8 1.8 %attend_head.4 = (bf16[2,256,128]{2,1,0:T(8,128)(2,1)S(1)}, f32[2,128]{1,0:T(2,128)S(1)}, bf16[128,768]{1,0:T(8,128)(2,1)S(1)}, f32[128,768]{1,0:T(8,128)S(1)}, ...) custom-call(bf16[2,256,128]{2,1,0:T(8,128)(2,1)S(1)} %pick_owner.1.pr_ref, ...), custom_call_target="tpu_custom_call" | custom-call | flops 276824064 | bytes 1048576 | tf_op jit(solution)/shard_map/attend_head/pallas_call | solution.py:322
  25.6 1.4 %collective-permute-done.3.pr_ref = bf16[2,256,128]{2,1,0:T(8,128)(2,1)S(1)} collective-permute-done((bf16[2,256,128]{2,1,0:T(8,128)(2,1)S(1)}, bf16[2,256,128]{2,1,0:T(8,128)(2,1)S(1)}, u32[]{:S(2)}, u32[]{:S(2)}) %collective-permute-start.3) | collective-permute-done | bytes 131104 | tf_op jit(solution)/shard_map/ppermute | solution.py:461
  27.0 1.8 %attend_head.5 = (bf16[2,256,128]{2,1,0:T(8,128)(2,1)S(1)}, f32[2,128]{1,0:T(2,128)S(1)}, bf16[128,768]{1,0:T(8,128)(2,1)S(1)}, f32[128,768]{1,0:T(8,128)S(1)}, ...) custom-call(bf16[2,256,128]{2,1,0:T(8,128)(2,1)S(1)} %collective-permute-done.3.pr_ref, ...), custom_call_target="tpu_custom_call" | custom-call | flops 276824064 | bytes 1048576 | tf_op jit(solution)/shard_map/attend_head/pallas_call | solution.py:322
  28.8 1.0 %collective-permute-done.5.pr_ref = bf16[2,256,128]{2,1,0:T(8,128)(2,1)S(1)} collective-permute-done((bf16[2,256,128]{2,1,0:T(8,128)(2,1)S(1)}, bf16[2,256,128]{2,1,0:T(8,128)(2,1)S(1)}, u32[]{:S(2)}, u32[]{:S(2)}) %collective-permute-start.5) | collective-permute-done | bytes 131104 | tf_op jit(solution)/shard_map/ppermute | solution.py:461
  29.8 1.8 %attend_head.6 = (bf16[2,256,128]{2,1,0:T(8,128)(2,1)S(1)}, f32[2,128]{1,0:T(2,128)S(1)}, bf16[128,768]{1,0:T(8,128)(2,1)S(1)}, f32[128,768]{1,0:T(8,128)S(1)}, ...) custom-call(bf16[2,256,128]{2,1,0:T(8,128)(2,1)S(1)} %collective-permute-done.5.pr_ref, ...), custom_call_target="tpu_custom_call" | custom-call | flops 276824064 | bytes 1048576 | tf_op jit(solution)/shard_map/attend_head/pallas_call | solution.py:322
  31.6 2.2 %collective-permute-start.6 = (bf16[2,256,128]{2,1,0:T(8,128)(2,1)S(1)}, bf16[2,256,128]{2,1,0:T(8,128)(2,1)S(1)}, u32[]{:S(2)}, u32[]{:S(2)}) collective-permute-start(bf16[2,256,128]{2,1,0:T(8,128)(2,1)S(1)} %get-tuple-element.114), channel_id=1, source_target_pairs={{0,3},{1,2},{2,1},{3,0},{4,7},{5,6},{6,5},{7,4},{8,11},{9,10},{10,... | collective-permute-start | bytes 393224 | tf_op jit(solution)/shard_map/ppermute | solution.py:461
  33.8 4.7 %collective-permute-start.4 = (bf16[2,256,128]{2,1,0:T(8,128)(2,1)S(1)}, bf16[2,256,128]{2,1,0:T(8,128)(2,1)S(1)}, u32[]{:S(2)}, u32[]{:S(2)}) collective-permute-start(bf16[2,256,128]{2,1,0:T(8,128)(2,1)S(1)} %get-tuple-element.104), channel_id=1, source_target_pairs={{0,1},{1,0},{2,3},{3,2},{4,5},{5,4},{6,7},{7,6},{8,9},{9,8},{10,11... | collective-permute-start | bytes 393224 | tf_op jit(solution)/shard_map/ppermute | solution.py:461
  38.5 0.1 collective-permute-done.7.pr_ref
  38.7 1.8 %attend_head.7 = (bf16[2,256,128]{2,1,0:T(8,128)(2,1)S(1)}, f32[2,128]{1,0:T(2,128)S(1)}, bf16[128,768]{1,0:T(8,128)(2,1)S(1)}, f32[128,768]{1,0:T(8,128)S(1)}, ...) custom-call(bf16[2,256,128]{2,1,0:T(8,128)(2,1)S(1)} %collective-permute-done.7.pr_ref, ...), custom_call_target="tpu_custom_call" | custom-call | flops 276824064 | bytes 1048576 | tf_op jit(solution)/shard_map/attend_head/pallas_call | solution.py:322
  40.5 0.1 collective-permute-start.8
  40.6 0.1 collective-permute-start.9
  40.7 1.1 %collective-permute-done.9 = f32[2,128]{1,0:T(2,128)S(1)} collective-permute-done((f32[2,128]{1,0:T(2,128)S(1)}, f32[2,128]{1,0:T(2,128)S(1)}, u32[]{:S(2)}, u32[]{:S(2)}) %collective-permute-start.9) | collective-permute-done | bytes 1056 | tf_op jit(solution)/shard_map/ppermute | solution.py:483
  41.8 0.0 collective-permute-done.6.rest_1_
  41.8 0.3 collective-permute-done.4.rest_0_
  42.1 1.5 %collective-permute-start.10 = (f32[2,128]{1,0:T(2,128)S(1)}, f32[2,128]{1,0:T(2,128)S(1)}, u32[]{:S(2)}, u32[]{:S(2)}) collective-permute-start(f32[2,128]{1,0:T(2,128)S(1)} %add.9), channel_id=1, source_target_pairs={{0,8},{4,12},{8,0},{12,4},{16,24},{20,28},{24,16},{28,20},{1,9},{5... | collective-permute-start | bytes 3080 | tf_op jit(solution)/shard_map/ppermute | solution.py:483
  43.6 2.1 %collective-permute-done.10 = f32[2,128]{1,0:T(2,128)S(1)} collective-permute-done((f32[2,128]{1,0:T(2,128)S(1)}, f32[2,128]{1,0:T(2,128)S(1)}, u32[]{:S(2)}, u32[]{:S(2)}) %collective-permute-start.10) | collective-permute-done | bytes 1056 | tf_op jit(solution)/shard_map/ppermute | solution.py:483
  45.7 1.5 %collective-permute-start.11 = (f32[2,128]{1,0:T(2,128)S(1)}, f32[2,128]{1,0:T(2,128)S(1)}, u32[]{:S(2)}, u32[]{:S(2)}) collective-permute-start(f32[2,128]{1,0:T(2,128)S(1)} %add.10), channel_id=1, source_target_pairs={{0,16},{4,20},{8,24},{12,28},{16,0},{20,4},{24,8},{28,12},{1,17},{... | collective-permute-start | bytes 3080 | tf_op jit(solution)/shard_map/ppermute | solution.py:483
  47.2 2.0 %collective-permute-done.11 = f32[2,128]{1,0:T(2,128)S(1)} collective-permute-done((f32[2,128]{1,0:T(2,128)S(1)}, f32[2,128]{1,0:T(2,128)S(1)}, u32[]{:S(2)}, u32[]{:S(2)}) %collective-permute-start.11) | collective-permute-done | bytes 1056 | tf_op jit(solution)/shard_map/ppermute | solution.py:483
  49.3 0.0 collective-permute-done.8.rest_2_
  49.3 0.1 join_parts.1.refs_0_
  49.4 2.7 %collective-permute-start.12 = (bf16[528,128]{1,0:T(8,128)(2,1)S(1)}, bf16[528,128]{1,0:T(8,128)(2,1)S(1)}, u32[]{:S(2)}, u32[]{:S(2)}) collective-permute-start(bf16[528,128]{1,0:T(8,128)(2,1)S(1)} %join_parts.1.refs_0_), channel_id=1, source_target_pairs={{0,1},{1,0},{2,3},{3,2},{4,5},{5,4},{6,7},{7,6},{8,9},{9,8},{10,11... | collective-permute-start | bytes 405512 | tf_op jit(solution)/shard_map/ppermute | solution.py:461
  52.1 0.1 collective-permute-start.14
  52.2 2.4 %collective-permute-start.13 = (bf16[528,128]{1,0:T(8,128)(2,1)S(1)}, bf16[528,128]{1,0:T(8,128)(2,1)S(1)}, u32[]{:S(2)}, u32[]{:S(2)}) collective-permute-start(bf16[528,128]{1,0:T(8,128)(2,1)S(1)} %join_parts.1.refs_0_), channel_id=1, source_target_pairs={{0,3},{1,2},{2,1},{3,0},{4,7},{5,6},{6,5},{7,4},{8,11},{9,10},{10,... | collective-permute-start | bytes 405512 | tf_op jit(solution)/shard_map/ppermute | solution.py:461
  54.5 2.7 %settle_heads.1 = (bf16[192,2048]{1,0:T(8,128)(2,1)}, bf16[192,2048]{1,0:T(8,128)(2,1)}, bf16[192,512]{1,0:T(8,128)(2,1)}, bf16[192,512]{1,0:T(8,128)(2,1)}) custom-call(s32[7]{0:T(128)S(1)} %pad_add_fusion.meta, bf16[128,768]{1,0:T(8,128)(2,1)S(1)} %get-tuple-element.78.rest_0_, f32[8,768]{1,0:T(8,128)S(1)} %get-tuple-element.79.rest_2_.rest_1_, ...), custom_call_target="tpu_custom_call" | custom-call | tf_op jit(solution)/shard_map/settle_heads/pallas_call | solution.py:345
  57.2 0.7 %collective-permute-done.12.refs_1_ = bf16[528,128]{1,0:T(8,128)(2,1)S(1)} collective-permute-done((bf16[528,128]{1,0:T(8,128)(2,1)S(1)}, bf16[528,128]{1,0:T(8,128)(2,1)S(1)}, u32[]{:S(2)}, u32[]{:S(2)}) %collective-permute-start.12) | collective-permute-done | bytes 135200 | tf_op jit(solution)/shard_map/ppermute | solution.py:461
  57.9 5.0 %collective-permute-done.14.refs_3_ = bf16[528,128]{1,0:T(8,128)(2,1)S(1)} collective-permute-done((bf16[528,128]{1,0:T(8,128)(2,1)S(1)}, bf16[528,128]{1,0:T(8,128)(2,1)S(1)}, u32[]{:S(2)}, u32[]{:S(2)}) %collective-permute-start.14) | collective-permute-done | bytes 135200 | tf_op jit(solution)/shard_map/ppermute | solution.py:461
  62.9 0.0 collective-permute-done.13.refs_2_
  62.9 1.5 %place_prompt_grad.1 = (bf16[2,256,512]{2,1,0:T(8,128)(2,1)}, f32[2,128]{1,0:T(2,128)}) custom-call(s32[7]{0:T(128)S(1)} %pad_add_fusion.meta, bf16[528,128]{1,0:T(8,128)(2,1)S(1)} %join_parts.1.refs_0_, bf16[528,128]{1,0:T(8,128)(2,1)S(1)} %collective-permute-done.12.refs_1_, bf16[528,128]{1,0:T(8,128)(2,1)S(1)} %collective-permute-done.13.refs_2_, ...), custom_call_target="tpu_custom_call" | custom-call | tf_op jit(solution)/shard_map/place_prompt_grad/pallas_call | solution.py:408
  (5 shorter events, 0.0 us)
Async XLA Ops:
  2.3 17.3 %collective-permute-start = (bf16[2,256,128]{2,1,0:T(8,128)(2,1)S(1)}, bf16[2,256,128]{2,1,0:T(8,128)(2,1)S(1)}, u32[]{:S(2)}, u32[]{:S(2)}) collective-permute-start(bf16[2,256,128]{2,1,0:T(8,128)(2,1)S(1)} %get-tuple-element.82), channel_id=1, source_target_pairs={{0,1},{1,0},{2,3},{3,2},{4,5},{5,4},{6,7},{7,6},{8,9},{9,8},{10,11... | collective-permute-start | bytes 393224 | tf_op jit(solution)/shard_map/ppermute | solution.py:461
  5.4 14.2 %collective-permute-start.1 = (bf16[2,256,128]{2,1,0:T(8,128)(2,1)S(1)}, bf16[2,256,128]{2,1,0:T(8,128)(2,1)S(1)}, u32[]{:S(2)}, u32[]{:S(2)}) collective-permute-start(bf16[2,256,128]{2,1,0:T(8,128)(2,1)S(1)} %get-tuple-element.84), channel_id=1, source_target_pairs={{0,3},{1,2},{2,1},{3,0},{4,7},{5,6},{6,5},{7,4},{8,11},{9,10},{10,... | collective-permute-start | bytes 393224 | tf_op jit(solution)/shard_map/ppermute | solution.py:461
  7.9 11.8 %collective-permute-start.2 = (bf16[2,256,128]{2,1,0:T(8,128)(2,1)S(1)}, bf16[2,256,128]{2,1,0:T(8,128)(2,1)S(1)}, u32[]{:S(2)}, u32[]{:S(2)}) collective-permute-start(bf16[2,256,128]{2,1,0:T(8,128)(2,1)S(1)} %get-tuple-element.86), channel_id=1, source_target_pairs={{0,2},{1,3},{2,0},{3,1},{4,6},{5,7},{6,4},{7,5},{8,10},{9,11},{10,... | collective-permute-start | bytes 393224 | tf_op jit(solution)/shard_map/ppermute | solution.py:461
  20.3 6.7 %collective-permute-start.3 = (bf16[2,256,128]{2,1,0:T(8,128)(2,1)S(1)}, bf16[2,256,128]{2,1,0:T(8,128)(2,1)S(1)}, u32[]{:S(2)}, u32[]{:S(2)}) collective-permute-start(bf16[2,256,128]{2,1,0:T(8,128)(2,1)S(1)} %pick_owner.1.pr_ref), channel_id=1, source_target_pairs={{0,1},{1,0},{2,3},{3,2},{4,5},{5,4},{6,7},{7,6},{8,9},{9,8},{10,11... | collective-permute-start | bytes 393224 | tf_op jit(solution)/shard_map/ppermute | solution.py:461
  20.4 9.5 %collective-permute-start.5 = (bf16[2,256,128]{2,1,0:T(8,128)(2,1)S(1)}, bf16[2,256,128]{2,1,0:T(8,128)(2,1)S(1)}, u32[]{:S(2)}, u32[]{:S(2)}) collective-permute-start(bf16[2,256,128]{2,1,0:T(8,128)(2,1)S(1)} %pick_owner.1.pr_ref), channel_id=1, source_target_pairs={{0,3},{1,2},{2,1},{3,0},{4,7},{5,6},{6,5},{7,4},{8,11},{9,10},{10,... | collective-permute-start | bytes 393224 | tf_op jit(solution)/shard_map/ppermute | solution.py:461
  23.1 15.6 %collective-permute-start.7 = (bf16[2,256,128]{2,1,0:T(8,128)(2,1)S(1)}, bf16[2,256,128]{2,1,0:T(8,128)(2,1)S(1)}, u32[]{:S(2)}, u32[]{:S(2)}) collective-permute-start(bf16[2,256,128]{2,1,0:T(8,128)(2,1)S(1)} %pick_owner.1.pr_ref), channel_id=1, source_target_pairs={{0,2},{1,3},{2,0},{3,1},{4,6},{5,7},{6,4},{7,5},{8,10},{9,11},{10,... | collective-permute-start | bytes 393224 | tf_op jit(solution)/shard_map/ppermute | solution.py:461
  31.6 10.2 %collective-permute-start.6 = (bf16[2,256,128]{2,1,0:T(8,128)(2,1)S(1)}, bf16[2,256,128]{2,1,0:T(8,128)(2,1)S(1)}, u32[]{:S(2)}, u32[]{:S(2)}) collective-permute-start(bf16[2,256,128]{2,1,0:T(8,128)(2,1)S(1)} %get-tuple-element.114), channel_id=1, source_target_pairs={{0,3},{1,2},{2,1},{3,0},{4,7},{5,6},{6,5},{7,4},{8,11},{9,10},{10,... | collective-permute-start | bytes 393224 | tf_op jit(solution)/shard_map/ppermute | solution.py:461
  33.8 8.3 %collective-permute-start.4 = (bf16[2,256,128]{2,1,0:T(8,128)(2,1)S(1)}, bf16[2,256,128]{2,1,0:T(8,128)(2,1)S(1)}, u32[]{:S(2)}, u32[]{:S(2)}) collective-permute-start(bf16[2,256,128]{2,1,0:T(8,128)(2,1)S(1)} %get-tuple-element.104), channel_id=1, source_target_pairs={{0,1},{1,0},{2,3},{3,2},{4,5},{5,4},{6,7},{7,6},{8,9},{9,8},{10,11... | collective-permute-start | bytes 393224 | tf_op jit(solution)/shard_map/ppermute | solution.py:461
  40.5 8.8 %collective-permute-start.8 = (bf16[2,256,128]{2,1,0:T(8,128)(2,1)S(1)}, bf16[2,256,128]{2,1,0:T(8,128)(2,1)S(1)}, u32[]{:S(2)}, u32[]{:S(2)}) collective-permute-start(bf16[2,256,128]{2,1,0:T(8,128)(2,1)S(1)} %get-tuple-element.124), channel_id=1, source_target_pairs={{0,2},{1,3},{2,0},{3,1},{4,6},{5,7},{6,4},{7,5},{8,10},{9,11},{10,... | collective-permute-start | bytes 393224 | tf_op jit(solution)/shard_map/ppermute | solution.py:461
  40.6 1.2 %collective-permute-start.9 = (f32[2,128]{1,0:T(2,128)S(1)}, f32[2,128]{1,0:T(2,128)S(1)}, u32[]{:S(2)}, u32[]{:S(2)}) collective-permute-start(f32[2,128]{1,0:T(2,128)S(1)} %get-tuple-element.125), channel_id=1, source_target_pairs={{0,4},{4,0},{8,12},{12,8},{16,20},{20,16},{24,28},{28,24},{1,5},{5... | collective-permute-start | bytes 3080 | tf_op jit(solution)/shard_map/ppermute | solution.py:483
  42.1 3.6 %collective-permute-start.10 = (f32[2,128]{1,0:T(2,128)S(1)}, f32[2,128]{1,0:T(2,128)S(1)}, u32[]{:S(2)}, u32[]{:S(2)}) collective-permute-start(f32[2,128]{1,0:T(2,128)S(1)} %add.9), channel_id=1, source_target_pairs={{0,8},{4,12},{8,0},{12,4},{16,24},{20,28},{24,16},{28,20},{1,9},{5... | collective-permute-start | bytes 3080 | tf_op jit(solution)/shard_map/ppermute | solution.py:483
  45.7 3.6 %collective-permute-start.11 = (f32[2,128]{1,0:T(2,128)S(1)}, f32[2,128]{1,0:T(2,128)S(1)}, u32[]{:S(2)}, u32[]{:S(2)}) collective-permute-start(f32[2,128]{1,0:T(2,128)S(1)} %add.10), channel_id=1, source_target_pairs={{0,16},{4,20},{8,24},{12,28},{16,0},{20,4},{24,8},{28,12},{1,17},{... | collective-permute-start | bytes 3080 | tf_op jit(solution)/shard_map/ppermute | solution.py:483
  49.4 8.5 %collective-permute-start.12 = (bf16[528,128]{1,0:T(8,128)(2,1)S(1)}, bf16[528,128]{1,0:T(8,128)(2,1)S(1)}, u32[]{:S(2)}, u32[]{:S(2)}) collective-permute-start(bf16[528,128]{1,0:T(8,128)(2,1)S(1)} %join_parts.1.refs_0_), channel_id=1, source_target_pairs={{0,1},{1,0},{2,3},{3,2},{4,5},{5,4},{6,7},{7,6},{8,9},{9,8},{10,11... | collective-permute-start | bytes 405512 | tf_op jit(solution)/shard_map/ppermute | solution.py:461
  52.1 10.8 %collective-permute-start.14 = (bf16[528,128]{1,0:T(8,128)(2,1)S(1)}, bf16[528,128]{1,0:T(8,128)(2,1)S(1)}, u32[]{:S(2)}, u32[]{:S(2)}) collective-permute-start(bf16[528,128]{1,0:T(8,128)(2,1)S(1)} %join_parts.1.refs_0_), channel_id=1, source_target_pairs={{0,2},{1,3},{2,0},{3,1},{4,6},{5,7},{6,4},{7,5},{8,10},{9,11},{10,... | collective-permute-start | bytes 405512 | tf_op jit(solution)/shard_map/ppermute | solution.py:461
  52.2 10.7 %collective-permute-start.13 = (bf16[528,128]{1,0:T(8,128)(2,1)S(1)}, bf16[528,128]{1,0:T(8,128)(2,1)S(1)}, u32[]{:S(2)}, u32[]{:S(2)}) collective-permute-start(bf16[528,128]{1,0:T(8,128)(2,1)S(1)} %join_parts.1.refs_0_), channel_id=1, source_target_pairs={{0,3},{1,2},{2,1},{3,0},{4,7},{5,6},{6,5},{7,4},{8,11},{9,10},{10,... | collective-permute-start | bytes 405512 | tf_op jit(solution)/shard_map/ppermute | solution.py:461

commit v16 on v15

--- a/solution.py
+++ b/solution.py
@@ -56,14 +56,14 @@
     )(order, cache)
 
 
-def pick_kernel(meta, *refs):
+def pick_kernel(which, *refs):
     picked = refs[0][...]
     for i in range(1, len(refs) - 1):
-        picked = jnp.where(meta[meta.shape[0] - 2] == i, refs[i][...], picked)
+        picked = jnp.where(which[0] == i, refs[i][...], picked)
     refs[-1][...] = picked
 
 
-def pick(meta, blocks):
+def pick(which, blocks):
     return pl.pallas_call(
         pick_kernel,
         out_shape=jax.ShapeDtypeStruct(blocks[0].shape, BF),
@@ -71,7 +71,7 @@
         out_specs=VMEM,
         compiler_params=params(4),
         name="pick_owner",
-    )(meta, *blocks)
+    )(which, *blocks)
 
 
 KEPT = 8
@@ -83,7 +83,7 @@
 
 def prepare_kernel(slots, share, rows, width, meta, q_in, g_in, k_in, v_in, gain_ref, kg_ref, *rest):
     outs, (q_buf, g_buf, k_buf, v_buf, gain_buf, sems) = rest[:-6], rest[-6:]
-    live_len = meta[meta.shape[0] - 3]
+    live_len = meta[meta.shape[0] - 1]
     count = len(slots)
     scale = HD ** (-0.5)
     wide = share * HD
@@ -291,7 +291,7 @@
         kept, results = rest[i * 7 : i * 7 + 3], rest[i * 7 + 3 : i * 7 + 7]
         at_ref, dq_ref, dkr_ref, dvr_ref = results
         copies += settle(
-            width, meta[i], meta[meta.shape[0] - 3], kept, at_ref, dq_ref,
+            width, meta[i], meta[meta.shape[0] - 1], kept, at_ref, dq_ref,
             dkr_ref[...], dvr_ref[...], outs, [buf.at[i] for buf in bufs], sems.at[i],
         )
     for copy in copies:
@@ -386,37 +386,62 @@
     )(own, *backs, gains)
 
 
-def place_kernel(meta, *refs):
-    payloads, out_ref, gain_ref, stage = refs[:-3], refs[-3], refs[-2], refs[-1]
-    mine = meta[meta.shape[0] - 1] > 0
-    depth, rows, _ = out_ref.shape
+def place_kernel(steps, flag, me, *refs):
+    payloads, (out_ref, gain_ref, stage, zeros, sems) = refs[:-5], refs[-5:]
+    depth, rows, width = out_ref.shape
+
+    @pl.when(flag[0] > 0)
+    def _():
+        copies = []
+        for i, ref in enumerate(payloads):
+            at = pl.ds(pl.multiple_of((me[0] ^ steps[i]) * HD, HD), HD)
+            for d in range(depth):
+                src = ref.at[d * rows : (d + 1) * rows, :]
+                copy = pltpu.make_async_copy(src, out_ref.at[d, :, at], sems.at[i * depth + d])
+                copy.start()
+                copies.append(copy)
+        for copy in copies:
+            copy.wait()
+
+    @pl.when(flag[0] == 0)
+    def _():
+        zeros[...] = jnp.zeros_like(zeros)
+        copies = []
+        for d in range(depth):
+            copy = pltpu.make_async_copy(zeros, out_ref.at[d], sems.at[d])
+            copy.start()
+            copies.append(copy)
+        for copy in copies:
+            copy.wait()
+
     for i, ref in enumerate(payloads):
-        at = pl.multiple_of(meta[i] * HD, HD)
-        for d in range(depth):
-            block = ref[d * rows : (d + 1) * rows, :]
-            out_ref[d, :, pl.ds(at, HD)] = jnp.where(mine, block, jnp.zeros_like(block))
         tail = ref[depth * rows :, :].astype(F32)
-        stage[meta[i]] = tail[0:2] + tail[2:4] + tail[4:6]
+        stage[me[0] ^ steps[i]] = tail[0:2] + tail[2:4] + tail[4:6]
     total = stage[0]
     for i in range(1, len(payloads)):
         total = total + stage[i]
     gain_ref[...] = total
 
 
-def place(meta, payloads, depth, rows):
+def place(steps, flag, me, payloads, depth, rows):
     count = len(payloads)
+    width = HD * count
     return pl.pallas_call(
-        place_kernel,
+        functools.partial(place_kernel, tuple(steps)),
         out_shape=[
-            jax.ShapeDtypeStruct((depth, rows, HD * count), BF),
+            jax.ShapeDtypeStruct((depth, rows, width), BF),
             jax.ShapeDtypeStruct((2, HD), F32),
         ],
-        in_specs=[SMEM] + [VMEM] * count,
-        out_specs=[VMEM, VMEM],
-        scratch_shapes=[pltpu.VMEM((count, 2, HD), F32)],
+        in_specs=[SMEM] * 2 + [VMEM] * count,
+        out_specs=[HBM, VMEM],
+        scratch_shapes=[
+            pltpu.VMEM((count, 2, HD), F32),
+            pltpu.VMEM((rows, width), BF),
+            pltpu.SemaphoreType.DMA((count * depth,)),
+        ],
         compiler_params=params(8),
         name="place_prompt_grad",
-    )(meta, *payloads)
+    )(flag, me, *payloads)
 
 
 def after(x, *others):
@@ -450,7 +475,11 @@
         order = order ^ (order >> 1) ^ me
     mine_flag = (me == owner).astype(jnp.int32)
     away = owner ^ me
-    meta = jnp.concatenate([order, jnp.stack([live_len, away ^ (away >> 1), mine_flag])])
+    meta = jnp.concatenate([order, live_len[None]])
+    which, flag, self_index = [
+        jnp.reshape(x, (1,)).astype(jnp.int32) for x in (away ^ (away >> 1), mine_flag, me)
+    ]
+    meta, which, flag, self_index = lax.optimization_barrier((meta, which, flag, self_index))
     q, g, k, v, *gains_in = [
         pltpu.with_memory_space_constraint(x, pltpu.HBM) for x in (q, g, k, v, q_gain, k_gain)
     ]
@@ -465,7 +494,7 @@
         got = [blocks[0]] + [swap(blocks[s], steps[s]) for s in range(1, n_group)]
         for s in range(1, n_group):
             got[s] = after(got[s], kept[0][2])
-        mine = pick(meta, got)
+        mine = pick(which, got)
         prompts = [mine] + [swap(mine, steps[s]) for s in range(1, n_group)]
     else:
         cache = lax.psum(jnp.where(me == owner, cache, jnp.zeros_like(cache)), "group")
@@ -495,7 +524,7 @@
         per_head[0][3] = after(per_head[0][3], payload)
         buffers = settle_heads(meta, per_head, q.shape[1], k.shape[1])
         payloads[1] = after(payloads[1], buffers[2])
-        placed, gains = place(meta, payloads, depth, p_rows)
+        placed, gains = place(steps, flag, self_index, payloads, depth, p_rows)
     else:
         total = lax.psum(jnp.concatenate(parts, axis=-1).astype(F32), "group").astype(BF)
         placed = jnp.where(mine_flag > 0, total, jnp.zeros((), BF))

time: 64.6 us -> 64 us (level)
  no operation moved by 1% of the time
where the time goes in v16:
time: 64 us; the launch traced here: 63.8 us
  starting transfers between devices  24.5 us (38%)
  Pallas kernels  18.8 us (29%)
  waiting for transfers between devices  18.4 us (29%)
  between operations  2.03 us (3%)
    ppermute x12, starting transfers between devices, swap(): return lax.ppermute(x, 'group', [(i, i ^ step) for i in range(n_group)])  21.4 us
    ppermute x12, waiting for transfers between devices, swap(): return lax.ppermute(x, 'group', [(i, i ^ step) for i in range(n_group)])  13.2 us
    pallas_call x4, Pallas kernels, first_half(): pl.pallas_call(functools.partial(first_kernel, 2 * HD), out_shape=[jax.Sh...  7.16 us
    pallas_call x1, Pallas kernels, prepare(): pl.pallas_call(functools.partial(prepare_kernel, slots, share, rows, 2 *...  5.64 us
    ppermute x3, waiting for transfers between devices, hop(): return lax.ppermute(x, 'dp', [(i, i ^ step) for i in range(n_dp)])  5.23 us
    ppermute x3, starting transfers between devices, hop(): return lax.ppermute(x, 'dp', [(i, i ^ step) for i in range(n_dp)])  3.11 us
    pallas_call x1, Pallas kernels, settle_heads(): pl.pallas_call(functools.partial(settle_kernel, 2 * HD), out_shape=out_sh...  2.69 us
    pallas_call x1, Pallas kernels, cut(): pl.pallas_call(cut_kernel, out_shape=[jax.ShapeDtypeStruct((depth, rows,...  1.69 us
  transfers between devices with their start and end apart: 15, of which 10 were waited for; matrix products, arithmetic and copies ran while one was open for 0% of the time, Pallas kernels for 24%

profile of v16, /device:TPU:0, one launch (start us, length us, event | category | flops | bytes accessed | tf_op | source)
XLA Modules:
  0.0 63.8 jit_solution(710136947576062518)
XLA Ops:
  0.6 1.7 %cut_prompt.1 = (bf16[2,256,128]{2,1,0:T(8,128)(2,1)S(1)}, bf16[2,256,128]{2,1,0:T(8,128)(2,1)S(1)}, bf16[2,256,128]{2,1,0:T(8,128)(2,1)S(1)}, bf16[2,256,128]{2,1,0:T(8,128)(2,1)S(1)}) custom-call(s32[4]{0:T(128)S(1)} %fusion.order, bf16[2,256,512]{2,1,0:T(8,128)(2,1)} %bitcast.20), custom_call_target="tpu_custom_call" | custom-call | tf_op jit(solution)/shard_map/cut_prompt/pallas_call | solution.py:48
  2.3 3.1 %collective-permute-start = (bf16[2,256,128]{2,1,0:T(8,128)(2,1)S(1)}, bf16[2,256,128]{2,1,0:T(8,128)(2,1)S(1)}, u32[]{:S(2)}, u32[]{:S(2)}) collective-permute-start(bf16[2,256,128]{2,1,0:T(8,128)(2,1)S(1)} %get-tuple-element.88), channel_id=1, source_target_pairs={{0,1},{1,0},{2,3},{3,2},{4,5},{5,4},{6,7},{7,6},{8,9},{9,8},{10,11... | collective-permute-start | bytes 393224 | tf_op jit(solution)/shard_map/ppermute | solution.py:490
  5.4 2.5 %collective-permute-start.1 = (bf16[2,256,128]{2,1,0:T(8,128)(2,1)S(1)}, bf16[2,256,128]{2,1,0:T(8,128)(2,1)S(1)}, u32[]{:S(2)}, u32[]{:S(2)}) collective-permute-start(bf16[2,256,128]{2,1,0:T(8,128)(2,1)S(1)} %get-tuple-element.90), channel_id=1, source_target_pairs={{0,3},{1,2},{2,1},{3,0},{4,7},{5,6},{6,5},{7,4},{8,11},{9,10},{10,... | collective-permute-start | bytes 393224 | tf_op jit(solution)/shard_map/ppermute | solution.py:490
  7.9 0.1 collective-permute-start.2
  9.3 0.1 pad_add_fusion.meta
  9.4 5.6 %prepare_response.1 = (bf16[128,768]{1,0:T(8,128)(2,1)S(1)}, bf16[128,768]{1,0:T(8,128)(2,1)S(1)}, f32[8,768]{1,0:T(8,128)S(1)}, bf16[192,768]{1,0:T(8,128)(2,1)...) custom-call(s32[5]{0:T(128)S(1)} %pad_add_fusion.meta, ...), custom_call_target="tpu_custom_call" | custom-call | flops 452984832 | bytes 3932160 | tf_op jit(solution)/shard_map/prepare_response/pallas_call | solution.py:162
  15.1 4.6 %collective-permute-done.2.refs_3_ = bf16[2,256,128]{2,1,0:T(8,128)(2,1)S(1)} collective-permute-done((bf16[2,256,128]{2,1,0:T(8,128)(2,1)S(1)}, bf16[2,256,128]{2,1,0:T(8,128)(2,1)S(1)}, u32[]{:S(2)}, u32[]{:S(2)}) %collective-permute-start.2) | collective-permute-done | bytes 131104 | tf_op jit(solution)/shard_map/ppermute | solution.py:490
  19.7 0.0 collective-permute-done.1.refs_2_
  19.7 0.0 collective-permute-done.refs_1_
  19.7 0.1 pick_owner.1.pr_ref
  19.7 0.1 collective-permute-start.3
  19.8 2.7 %collective-permute-start.5 = (bf16[2,256,128]{2,1,0:T(8,128)(2,1)S(1)}, bf16[2,256,128]{2,1,0:T(8,128)(2,1)S(1)}, u32[]{:S(2)}, u32[]{:S(2)}) collective-permute-start(bf16[2,256,128]{2,1,0:T(8,128)(2,1)S(1)} %pick_owner.1.pr_ref), channel_id=1, source_target_pairs={{0,3},{1,2},{2,1},{3,0},{4,7},{5,6},{6,5},{7,4},{8,11},{9,10},{10,... | collective-permute-start | bytes 393224 | tf_op jit(solution)/shard_map/ppermute | solution.py:490
  22.5 0.8 %collective-permute-start.7 = (bf16[2,256,128]{2,1,0:T(8,128)(2,1)S(1)}, bf16[2,256,128]{2,1,0:T(8,128)(2,1)S(1)}, u32[]{:S(2)}, u32[]{:S(2)}) collective-permute-start(bf16[2,256,128]{2,1,0:T(8,128)(2,1)S(1)} %pick_owner.1.pr_ref), channel_id=1, source_target_pairs={{0,2},{1,3},{2,0},{3,1},{4,6},{5,7},{6,4},{7,5},{8,10},{9,11},{10,... | collective-permute-start | bytes 393224 | tf_op jit(solution)/shard_map/ppermute | solution.py:490
  23.3 1.8 %attend_head.4 = (bf16[2,256,128]{2,1,0:T(8,128)(2,1)S(1)}, f32[2,128]{1,0:T(2,128)S(1)}, bf16[128,768]{1,0:T(8,128)(2,1)S(1)}, f32[128,768]{1,0:T(8,128)S(1)}, ...) custom-call(bf16[2,256,128]{2,1,0:T(8,128)(2,1)S(1)} %pick_owner.1.pr_ref, ...), custom_call_target="tpu_custom_call" | custom-call | flops 276824064 | bytes 1048576 | tf_op jit(solution)/shard_map/attend_head/pallas_call | solution.py:322
  25.1 1.4 %collective-permute-done.3.pr_ref = bf16[2,256,128]{2,1,0:T(8,128)(2,1)S(1)} collective-permute-done((bf16[2,256,128]{2,1,0:T(8,128)(2,1)S(1)}, bf16[2,256,128]{2,1,0:T(8,128)(2,1)S(1)}, u32[]{:S(2)}, u32[]{:S(2)}) %collective-permute-start.3) | collective-permute-done | bytes 131104 | tf_op jit(solution)/shard_map/ppermute | solution.py:490
  26.5 1.8 %attend_head.5 = (bf16[2,256,128]{2,1,0:T(8,128)(2,1)S(1)}, f32[2,128]{1,0:T(2,128)S(1)}, bf16[128,768]{1,0:T(8,128)(2,1)S(1)}, f32[128,768]{1,0:T(8,128)S(1)}, ...) custom-call(bf16[2,256,128]{2,1,0:T(8,128)(2,1)S(1)} %collective-permute-done.3.pr_ref, ...), custom_call_target="tpu_custom_call" | custom-call | flops 276824064 | bytes 1048576 | tf_op jit(solution)/shard_map/attend_head/pallas_call | solution.py:322
  28.3 1.0 %collective-permute-done.5.pr_ref = bf16[2,256,128]{2,1,0:T(8,128)(2,1)S(1)} collective-permute-done((bf16[2,256,128]{2,1,0:T(8,128)(2,1)S(1)}, bf16[2,256,128]{2,1,0:T(8,128)(2,1)S(1)}, u32[]{:S(2)}, u32[]{:S(2)}) %collective-permute-start.5) | collective-permute-done | bytes 131104 | tf_op jit(solution)/shard_map/ppermute | solution.py:490
  29.3 1.8 %attend_head.6 = (bf16[2,256,128]{2,1,0:T(8,128)(2,1)S(1)}, f32[2,128]{1,0:T(2,128)S(1)}, bf16[128,768]{1,0:T(8,128)(2,1)S(1)}, f32[128,768]{1,0:T(8,128)S(1)}, ...) custom-call(bf16[2,256,128]{2,1,0:T(8,128)(2,1)S(1)} %collective-permute-done.5.pr_ref, ...), custom_call_target="tpu_custom_call" | custom-call | flops 276824064 | bytes 1048576 | tf_op jit(solution)/shard_map/attend_head/pallas_call | solution.py:322
  31.1 2.2 %collective-permute-start.6 = (bf16[2,256,128]{2,1,0:T(8,128)(2,1)S(1)}, bf16[2,256,128]{2,1,0:T(8,128)(2,1)S(1)}, u32[]{:S(2)}, u32[]{:S(2)}) collective-permute-start(bf16[2,256,128]{2,1,0:T(8,128)(2,1)S(1)} %get-tuple-element.120), channel_id=1, source_target_pairs={{0,3},{1,2},{2,1},{3,0},{4,7},{5,6},{6,5},{7,4},{8,11},{9,10},{10,... | collective-permute-start | bytes 393224 | tf_op jit(solution)/shard_map/ppermute | solution.py:490
  33.3 4.7 %collective-permute-start.4 = (bf16[2,256,128]{2,1,0:T(8,128)(2,1)S(1)}, bf16[2,256,128]{2,1,0:T(8,128)(2,1)S(1)}, u32[]{:S(2)}, u32[]{:S(2)}) collective-permute-start(bf16[2,256,128]{2,1,0:T(8,128)(2,1)S(1)} %get-tuple-element.110), channel_id=1, source_target_pairs={{0,1},{1,0},{2,3},{3,2},{4,5},{5,4},{6,7},{7,6},{8,9},{9,8},{10,11... | collective-permute-start | bytes 393224 | tf_op jit(solution)/shard_map/ppermute | solution.py:490
  38.0 0.2 collective-permute-done.7.pr_ref
  38.1 1.8 %attend_head.7 = (bf16[2,256,128]{2,1,0:T(8,128)(2,1)S(1)}, f32[2,128]{1,0:T(2,128)S(1)}, bf16[128,768]{1,0:T(8,128)(2,1)S(1)}, f32[128,768]{1,0:T(8,128)S(1)}, ...) custom-call(bf16[2,256,128]{2,1,0:T(8,128)(2,1)S(1)} %collective-permute-done.7.pr_ref, ...), custom_call_target="tpu_custom_call" | custom-call | flops 276824064 | bytes 1048576 | tf_op jit(solution)/shard_map/attend_head/pallas_call | solution.py:322
  39.9 0.1 collective-permute-start.8
  40.0 0.1 collective-permute-start.9
  40.1 1.1 %collective-permute-done.9 = f32[2,128]{1,0:T(2,128)S(1)} collective-permute-done((f32[2,128]{1,0:T(2,128)S(1)}, f32[2,128]{1,0:T(2,128)S(1)}, u32[]{:S(2)}, u32[]{:S(2)}) %collective-permute-start.9) | collective-permute-done | bytes 1056 | tf_op jit(solution)/shard_map/ppermute | solution.py:512
  41.2 0.0 collective-permute-done.6.rest_1_
  41.2 0.3 collective-permute-done.4.rest_0_
  41.6 1.5 %collective-permute-start.10 = (f32[2,128]{1,0:T(2,128)S(1)}, f32[2,128]{1,0:T(2,128)S(1)}, u32[]{:S(2)}, u32[]{:S(2)}) collective-permute-start(f32[2,128]{1,0:T(2,128)S(1)} %add.9), channel_id=1, source_target_pairs={{0,8},{4,12},{8,0},{12,4},{16,24},{20,28},{24,16},{28,20},{1,9},{5... | collective-permute-start | bytes 3080 | tf_op jit(solution)/shard_map/ppermute | solution.py:512
  43.1 2.1 %collective-permute-done.10 = f32[2,128]{1,0:T(2,128)S(1)} collective-permute-done((f32[2,128]{1,0:T(2,128)S(1)}, f32[2,128]{1,0:T(2,128)S(1)}, u32[]{:S(2)}, u32[]{:S(2)}) %collective-permute-start.10) | collective-permute-done | bytes 1056 | tf_op jit(solution)/shard_map/ppermute | solution.py:512
  45.2 1.5 %collective-permute-start.11 = (f32[2,128]{1,0:T(2,128)S(1)}, f32[2,128]{1,0:T(2,128)S(1)}, u32[]{:S(2)}, u32[]{:S(2)}) collective-permute-start(f32[2,128]{1,0:T(2,128)S(1)} %add.10), channel_id=1, source_target_pairs={{0,16},{4,20},{8,24},{12,28},{16,0},{20,4},{24,8},{28,12},{1,17},{... | collective-permute-start | bytes 3080 | tf_op jit(solution)/shard_map/ppermute | solution.py:512
  46.7 2.0 %collective-permute-done.11 = f32[2,128]{1,0:T(2,128)S(1)} collective-permute-done((f32[2,128]{1,0:T(2,128)S(1)}, f32[2,128]{1,0:T(2,128)S(1)}, u32[]{:S(2)}, u32[]{:S(2)}) %collective-permute-start.11) | collective-permute-done | bytes 1056 | tf_op jit(solution)/shard_map/ppermute | solution.py:512
  48.7 0.0 collective-permute-done.8.rest_2_
  48.7 0.1 join_parts.1.refs_0_
  48.8 2.7 %collective-permute-start.12 = (bf16[528,128]{1,0:T(8,128)(2,1)S(1)}, bf16[528,128]{1,0:T(8,128)(2,1)S(1)}, u32[]{:S(2)}, u32[]{:S(2)}) collective-permute-start(bf16[528,128]{1,0:T(8,128)(2,1)S(1)} %join_parts.1.refs_0_), channel_id=1, source_target_pairs={{0,1},{1,0},{2,3},{3,2},{4,5},{5,4},{6,7},{7,6},{8,9},{9,8},{10,11... | collective-permute-start | bytes 405512 | tf_op jit(solution)/shard_map/ppermute | solution.py:490
  51.6 0.1 collective-permute-start.14
  51.6 2.4 %collective-permute-start.13 = (bf16[528,128]{1,0:T(8,128)(2,1)S(1)}, bf16[528,128]{1,0:T(8,128)(2,1)S(1)}, u32[]{:S(2)}, u32[]{:S(2)}) collective-permute-start(bf16[528,128]{1,0:T(8,128)(2,1)S(1)} %join_parts.1.refs_0_), channel_id=1, source_target_pairs={{0,3},{1,2},{2,1},{3,0},{4,7},{5,6},{6,5},{7,4},{8,11},{9,10},{10,... | collective-permute-start | bytes 405512 | tf_op jit(solution)/shard_map/ppermute | solution.py:490
  54.0 2.7 %settle_heads.1 = (bf16[192,2048]{1,0:T(8,128)(2,1)}, bf16[192,2048]{1,0:T(8,128)(2,1)}, bf16[192,512]{1,0:T(8,128)(2,1)}, bf16[192,512]{1,0:T(8,128)(2,1)}) custom-call(s32[5]{0:T(128)S(1)} %pad_add_fusion.meta, bf16[128,768]{1,0:T(8,128)(2,1)S(1)} %get-tuple-element.83.rest_0_, f32[8,768]{1,0:T(8,128)S(1)} %get-tuple-element.84.rest_2_.rest_1_, ...), custom_call_target="tpu_custom_call" | custom-call | tf_op jit(solution)/shard_map/settle_heads/pallas_call | solution.py:345
  56.7 0.7 %collective-permute-done.12.refs_1_ = bf16[528,128]{1,0:T(8,128)(2,1)S(1)} collective-permute-done((bf16[528,128]{1,0:T(8,128)(2,1)S(1)}, bf16[528,128]{1,0:T(8,128)(2,1)S(1)}, u32[]{:S(2)}, u32[]{:S(2)}) %collective-permute-start.12) | collective-permute-done | bytes 135200 | tf_op jit(solution)/shard_map/ppermute | solution.py:490
  57.3 5.0 %collective-permute-done.14.refs_3_ = bf16[528,128]{1,0:T(8,128)(2,1)S(1)} collective-permute-done((bf16[528,128]{1,0:T(8,128)(2,1)S(1)}, bf16[528,128]{1,0:T(8,128)(2,1)S(1)}, u32[]{:S(2)}, u32[]{:S(2)}) %collective-permute-start.14) | collective-permute-done | bytes 135200 | tf_op jit(solution)/shard_map/ppermute | solution.py:490
  62.4 0.0 collective-permute-done.13.refs_2_
  62.4 1.5 %place_prompt_grad.1 = (bf16[2,256,512]{2,1,0:T(8,128)(2,1)}, f32[2,128]{1,0:T(2,128)}) custom-call(s32[1]{0:T(128)} %bitcast.3.flag, s32[1]{0:T(128)} %bitcast.4.me, bf16[528,128]{1,0:T(8,128)(2,1)S(1)} %join_parts.1.refs_0_, bf16[528,128]{1,0:T(8,128)(2,1)S(1)} %collective-permute-done.12.refs_1_, bf16[528,128]{1,0:T(8,128)(2,1)S(1)} %collective-permute-done.13.refs_2_, ...), custom_call_target="tpu_custom_call" | custom-call | tf_op jit(solution)/shard_map/place_prompt_grad/pallas_call | solution.py:429
  (5 shorter events, 0.0 us)
Async XLA Ops:
  2.3 17.3 %collective-permute-start = (bf16[2,256,128]{2,1,0:T(8,128)(2,1)S(1)}, bf16[2,256,128]{2,1,0:T(8,128)(2,1)S(1)}, u32[]{:S(2)}, u32[]{:S(2)}) collective-permute-start(bf16[2,256,128]{2,1,0:T(8,128)(2,1)S(1)} %get-tuple-element.88), channel_id=1, source_target_pairs={{0,1},{1,0},{2,3},{3,2},{4,5},{5,4},{6,7},{7,6},{8,9},{9,8},{10,11... | collective-permute-start | bytes 393224 | tf_op jit(solution)/shard_map/ppermute | solution.py:490
  5.4 14.2 %collective-permute-start.1 = (bf16[2,256,128]{2,1,0:T(8,128)(2,1)S(1)}, bf16[2,256,128]{2,1,0:T(8,128)(2,1)S(1)}, u32[]{:S(2)}, u32[]{:S(2)}) collective-permute-start(bf16[2,256,128]{2,1,0:T(8,128)(2,1)S(1)} %get-tuple-element.90), channel_id=1, source_target_pairs={{0,3},{1,2},{2,1},{3,0},{4,7},{5,6},{6,5},{7,4},{8,11},{9,10},{10,... | collective-permute-start | bytes 393224 | tf_op jit(solution)/shard_map/ppermute | solution.py:490
  7.9 11.8 %collective-permute-start.2 = (bf16[2,256,128]{2,1,0:T(8,128)(2,1)S(1)}, bf16[2,256,128]{2,1,0:T(8,128)(2,1)S(1)}, u32[]{:S(2)}, u32[]{:S(2)}) collective-permute-start(bf16[2,256,128]{2,1,0:T(8,128)(2,1)S(1)} %get-tuple-element.92), channel_id=1, source_target_pairs={{0,2},{1,3},{2,0},{3,1},{4,6},{5,7},{6,4},{7,5},{8,10},{9,11},{10,... | collective-permute-start | bytes 393224 | tf_op jit(solution)/shard_map/ppermute | solution.py:490
  19.7 6.7 %collective-permute-start.3 = (bf16[2,256,128]{2,1,0:T(8,128)(2,1)S(1)}, bf16[2,256,128]{2,1,0:T(8,128)(2,1)S(1)}, u32[]{:S(2)}, u32[]{:S(2)}) collective-permute-start(bf16[2,256,128]{2,1,0:T(8,128)(2,1)S(1)} %pick_owner.1.pr_ref), channel_id=1, source_target_pairs={{0,1},{1,0},{2,3},{3,2},{4,5},{5,4},{6,7},{7,6},{8,9},{9,8},{10,11... | collective-permute-start | bytes 393224 | tf_op jit(solution)/shard_map/ppermute | solution.py:490
  19.8 9.5 %collective-permute-start.5 = (bf16[2,256,128]{2,1,0:T(8,128)(2,1)S(1)}, bf16[2,256,128]{2,1,0:T(8,128)(2,1)S(1)}, u32[]{:S(2)}, u32[]{:S(2)}) collective-permute-start(bf16[2,256,128]{2,1,0:T(8,128)(2,1)S(1)} %pick_owner.1.pr_ref), channel_id=1, source_target_pairs={{0,3},{1,2},{2,1},{3,0},{4,7},{5,6},{6,5},{7,4},{8,11},{9,10},{10,... | collective-permute-start | bytes 393224 | tf_op jit(solution)/shard_map/ppermute | solution.py:490
  22.5 15.6 %collective-permute-start.7 = (bf16[2,256,128]{2,1,0:T(8,128)(2,1)S(1)}, bf16[2,256,128]{2,1,0:T(8,128)(2,1)S(1)}, u32[]{:S(2)}, u32[]{:S(2)}) collective-permute-start(bf16[2,256,128]{2,1,0:T(8,128)(2,1)S(1)} %pick_owner.1.pr_ref), channel_id=1, source_target_pairs={{0,2},{1,3},{2,0},{3,1},{4,6},{5,7},{6,4},{7,5},{8,10},{9,11},{10,... | collective-permute-start | bytes 393224 | tf_op jit(solution)/shard_map/ppermute | solution.py:490
  31.1 10.2 %collective-permute-start.6 = (bf16[2,256,128]{2,1,0:T(8,128)(2,1)S(1)}, bf16[2,256,128]{2,1,0:T(8,128)(2,1)S(1)}, u32[]{:S(2)}, u32[]{:S(2)}) collective-permute-start(bf16[2,256,128]{2,1,0:T(8,128)(2,1)S(1)} %get-tuple-element.120), channel_id=1, source_target_pairs={{0,3},{1,2},{2,1},{3,0},{4,7},{5,6},{6,5},{7,4},{8,11},{9,10},{10,... | collective-permute-start | bytes 393224 | tf_op jit(solution)/shard_map/ppermute | solution.py:490
  33.3 8.3 %collective-permute-start.4 = (bf16[2,256,128]{2,1,0:T(8,128)(2,1)S(1)}, bf16[2,256,128]{2,1,0:T(8,128)(2,1)S(1)}, u32[]{:S(2)}, u32[]{:S(2)}) collective-permute-start(bf16[2,256,128]{2,1,0:T(8,128)(2,1)S(1)} %get-tuple-element.110), channel_id=1, source_target_pairs={{0,1},{1,0},{2,3},{3,2},{4,5},{5,4},{6,7},{7,6},{8,9},{9,8},{10,11... | collective-permute-start | bytes 393224 | tf_op jit(solution)/shard_map/ppermute | solution.py:490
  39.9 8.8 %collective-permute-start.8 = (bf16[2,256,128]{2,1,0:T(8,128)(2,1)S(1)}, bf16[2,256,128]{2,1,0:T(8,128)(2,1)S(1)}, u32[]{:S(2)}, u32[]{:S(2)}) collective-permute-start(bf16[2,256,128]{2,1,0:T(8,128)(2,1)S(1)} %get-tuple-element.130), channel_id=1, source_target_pairs={{0,2},{1,3},{2,0},{3,1},{4,6},{5,7},{6,4},{7,5},{8,10},{9,11},{10,... | collective-permute-start | bytes 393224 | tf_op jit(solution)/shard_map/ppermute | solution.py:490
  40.0 1.2 %collective-permute-start.9 = (f32[2,128]{1,0:T(2,128)S(1)}, f32[2,128]{1,0:T(2,128)S(1)}, u32[]{:S(2)}, u32[]{:S(2)}) collective-permute-start(f32[2,128]{1,0:T(2,128)S(1)} %get-tuple-element.131), channel_id=1, source_target_pairs={{0,4},{4,0},{8,12},{12,8},{16,20},{20,16},{24,28},{28,24},{1,5},{5... | collective-permute-start | bytes 3080 | tf_op jit(solution)/shard_map/ppermute | solution.py:512
  41.6 3.6 %collective-permute-start.10 = (f32[2,128]{1,0:T(2,128)S(1)}, f32[2,128]{1,0:T(2,128)S(1)}, u32[]{:S(2)}, u32[]{:S(2)}) collective-permute-start(f32[2,128]{1,0:T(2,128)S(1)} %add.9), channel_id=1, source_target_pairs={{0,8},{4,12},{8,0},{12,4},{16,24},{20,28},{24,16},{28,20},{1,9},{5... | collective-permute-start | bytes 3080 | tf_op jit(solution)/shard_map/ppermute | solution.py:512
  45.2 3.6 %collective-permute-start.11 = (f32[2,128]{1,0:T(2,128)S(1)}, f32[2,128]{1,0:T(2,128)S(1)}, u32[]{:S(2)}, u32[]{:S(2)}) collective-permute-start(f32[2,128]{1,0:T(2,128)S(1)} %add.10), channel_id=1, source_target_pairs={{0,16},{4,20},{8,24},{12,28},{16,0},{20,4},{24,8},{28,12},{1,17},{... | collective-permute-start | bytes 3080 | tf_op jit(solution)/shard_map/ppermute | solution.py:512
  48.8 8.5 %collective-permute-start.12 = (bf16[528,128]{1,0:T(8,128)(2,1)S(1)}, bf16[528,128]{1,0:T(8,128)(2,1)S(1)}, u32[]{:S(2)}, u32[]{:S(2)}) collective-permute-start(bf16[528,128]{1,0:T(8,128)(2,1)S(1)} %join_parts.1.refs_0_), channel_id=1, source_target_pairs={{0,1},{1,0},{2,3},{3,2},{4,5},{5,4},{6,7},{7,6},{8,9},{9,8},{10,11... | collective-permute-start | bytes 405512 | tf_op jit(solution)/shard_map/ppermute | solution.py:490
  51.6 10.8 %collective-permute-start.14 = (bf16[528,128]{1,0:T(8,128)(2,1)S(1)}, bf16[528,128]{1,0:T(8,128)(2,1)S(1)}, u32[]{:S(2)}, u32[]{:S(2)}) collective-permute-start(bf16[528,128]{1,0:T(8,128)(2,1)S(1)} %join_parts.1.refs_0_), channel_id=1, source_target_pairs={{0,2},{1,3},{2,0},{3,1},{4,6},{5,7},{6,4},{7,5},{8,10},{9,11},{10,... | collective-permute-start | bytes 405512 | tf_op jit(solution)/shard_map/ppermute | solution.py:490
  51.6 10.7 %collective-permute-start.13 = (bf16[528,128]{1,0:T(8,128)(2,1)S(1)}, bf16[528,128]{1,0:T(8,128)(2,1)S(1)}, u32[]{:S(2)}, u32[]{:S(2)}) collective-permute-start(bf16[528,128]{1,0:T(8,128)(2,1)S(1)} %join_parts.1.refs_0_), channel_id=1, source_target_pairs={{0,3},{1,2},{2,1},{3,0},{4,7},{5,6},{6,5},{7,4},{8,11},{9,10},{10,... | collective-permute-start | bytes 405512 | tf_op jit(solution)/shard_map/ppermute | solution.py:490

commit v17 on v16

--- a/solution.py
+++ b/solution.py
@@ -500,23 +500,27 @@
         cache = lax.psum(jnp.where(me == owner, cache, jnp.zeros_like(cache)), "group")
         prompts = cut(order, cache, kv_heads)
 
-    parts, backs, per_head = [], [], []
+    parts, per_head = [], []
     for s, prompt in enumerate(prompts):
         part, acc, *results = first_half(prompt, kept[s], acc)
         per_head.append([kept[s][0], kept[s][2], kept[s][7], *results])
         parts.append(part)
-        if direct and s > 0:
-            backs.append(swap(part, steps[s]))
+
+    if direct:
+        backs = [swap(after(x, acc), s) for x, s in zip(parts[1:], steps[1:])]
 
     def hop(x, step):
         return lax.ppermute(x, "dp", [(i, i ^ step) for i in range(n_dp)])
 
     gains = acc + hop(acc, 1)
-    if direct:
-        gains = after(gains, *backs[:-1])
     step = 2
     while step < n_dp:
-        gains = gains + hop(gains, step)
+        arrived = hop(gains, step)
+        if direct and step == 2:
+            arrived = after(arrived, *backs[:-1])
+        elif direct:
+            arrived = after(arrived, *backs)
+        gains = gains + arrived
         step *= 2
     if direct:
         payload = join(parts[0], backs, gains)

time: 64 us -> 64.4 us (level)
  waiting for transfers between devices: 18.4 us -> 22.8 us
  starting transfers between devices: 24.5 us -> 20.5 us
    ppermute x12, waiting for transfers between devices: 13.2 us -> 19.6 us  [swap(): return lax.ppermute(x, 'group', [(i, i ^ step) for i in range(n_group)])]
    ppermute x12, starting transfers between devices: 21.4 us -> 17.5 us  [swap(): return lax.ppermute(x, 'group', [(i, i ^ step) for i in range(n_group)])]
    ppermute x3, waiting for transfers between devices: 5.23 us -> 3.22 us  [hop(): return lax.ppermute(x, 'dp', [(i, i ^ step) for i in range(n_dp)])]
  transfers between devices with their start and end apart: 15 -> 15, of which waited for: 10 -> 10; matrix products, arithmetic and copies ran while one was open for 0% -> 0% of each run, Pallas kernels for 24% -> 21%
where the time goes in v17:
time: 64.4 us; the launch traced here: 64.2 us
  waiting for transfers between devices  22.8 us (35%)
  starting transfers between devices  20.5 us (32%)
  Pallas kernels  18.7 us (29%)
  between operations  2.01 us (3%)
    ppermute x12, waiting for transfers between devices, swap(): return lax.ppermute(x, 'group', [(i, i ^ step) for i in range(n_group)])  19.6 us
    ppermute x12, starting transfers between devices, swap(): return lax.ppermute(x, 'group', [(i, i ^ step) for i in range(n_group)])  17.5 us
    pallas_call x4, Pallas kernels, first_half(): pl.pallas_call(functools.partial(first_kernel, 2 * HD), out_shape=[jax.Sh...  7.17 us
    pallas_call x1, Pallas kernels, prepare(): pl.pallas_call(functools.partial(prepare_kernel, slots, share, rows, 2 *...  5.64 us
    ppermute x3, waiting for transfers between devices, hop(): return lax.ppermute(x, 'dp', [(i, i ^ step) for i in range(n_dp)])  3.22 us
    ppermute x3, starting transfers between devices, hop(): return lax.ppermute(x, 'dp', [(i, i ^ step) for i in range(n_dp)])  3.01 us
    pallas_call x1, Pallas kernels, settle_heads(): pl.pallas_call(functools.partial(settle_kernel, 2 * HD), out_shape=out_sh...  2.69 us
    pallas_call x1, Pallas kernels, cut(): pl.pallas_call(cut_kernel, out_shape=[jax.ShapeDtypeStruct((depth, rows,...  1.69 us
  transfers between devices with their start and end apart: 15, of which 10 were waited for; matrix products, arithmetic and copies ran while one was open for 0% of the time, Pallas kernels for 21%

profile of v17, /device:TPU:0, one launch (start us, length us, event | category | flops | bytes accessed | tf_op | source)
XLA Modules:
  0.0 64.2 jit_solution(11179651709057933046)
XLA Ops:
  0.6 1.7 %cut_prompt.1 = (bf16[2,256,128]{2,1,0:T(8,128)(2,1)S(1)}, bf16[2,256,128]{2,1,0:T(8,128)(2,1)S(1)}, bf16[2,256,128]{2,1,0:T(8,128)(2,1)S(1)}, bf16[2,256,128]{2,1,0:T(8,128)(2,1)S(1)}) custom-call(s32[4]{0:T(128)S(1)} %fusion.order, bf16[2,256,512]{2,1,0:T(8,128)(2,1)} %bitcast.20), custom_call_target="tpu_custom_call" | custom-call | tf_op jit(solution)/shard_map/cut_prompt/pallas_call | solution.py:48
  2.3 3.1 %collective-permute-start = (bf16[2,256,128]{2,1,0:T(8,128)(2,1)S(1)}, bf16[2,256,128]{2,1,0:T(8,128)(2,1)S(1)}, u32[]{:S(2)}, u32[]{:S(2)}) collective-permute-start(bf16[2,256,128]{2,1,0:T(8,128)(2,1)S(1)} %get-tuple-element.92), channel_id=1, source_target_pairs={{0,1},{1,0},{2,3},{3,2},{4,5},{5,4},{6,7},{7,6},{8,9},{9,8},{10,11... | collective-permute-start | bytes 393224 | tf_op jit(solution)/shard_map/ppermute | solution.py:490
  5.4 2.5 %collective-permute-start.1 = (bf16[2,256,128]{2,1,0:T(8,128)(2,1)S(1)}, bf16[2,256,128]{2,1,0:T(8,128)(2,1)S(1)}, u32[]{:S(2)}, u32[]{:S(2)}) collective-permute-start(bf16[2,256,128]{2,1,0:T(8,128)(2,1)S(1)} %get-tuple-element.94), channel_id=1, source_target_pairs={{0,3},{1,2},{2,1},{3,0},{4,7},{5,6},{6,5},{7,4},{8,11},{9,10},{10,... | collective-permute-start | bytes 393224 | tf_op jit(solution)/shard_map/ppermute | solution.py:490
  7.9 0.1 collective-permute-start.2
  9.3 0.1 pad_add_fusion.meta
  9.4 5.6 %prepare_response.1 = (bf16[128,768]{1,0:T(8,128)(2,1)S(1)}, bf16[128,768]{1,0:T(8,128)(2,1)S(1)}, f32[8,768]{1,0:T(8,128)S(1)}, bf16[192,768]{1,0:T(8,128)(2,1)...) custom-call(s32[5]{0:T(128)S(1)} %pad_add_fusion.meta, ...), custom_call_target="tpu_custom_call" | custom-call | flops 452984832 | bytes 3932160 | tf_op jit(solution)/shard_map/prepare_response/pallas_call | solution.py:162
  15.1 4.6 %collective-permute-done.2.refs_3_ = bf16[2,256,128]{2,1,0:T(8,128)(2,1)S(1)} collective-permute-done((bf16[2,256,128]{2,1,0:T(8,128)(2,1)S(1)}, bf16[2,256,128]{2,1,0:T(8,128)(2,1)S(1)}, u32[]{:S(2)}, u32[]{:S(2)}) %collective-permute-start.2) | collective-permute-done | bytes 131104 | tf_op jit(solution)/shard_map/ppermute | solution.py:490
  19.7 0.0 collective-permute-done.1.refs_2_
  19.7 0.0 collective-permute-done.refs_1_
  19.7 0.1 pick_owner.1.pr_ref
  19.7 0.1 collective-permute-start.3
  19.8 2.7 %collective-permute-start.5 = (bf16[2,256,128]{2,1,0:T(8,128)(2,1)S(1)}, bf16[2,256,128]{2,1,0:T(8,128)(2,1)S(1)}, u32[]{:S(2)}, u32[]{:S(2)}) collective-permute-start(bf16[2,256,128]{2,1,0:T(8,128)(2,1)S(1)} %pick_owner.1.pr_ref), channel_id=1, source_target_pairs={{0,3},{1,2},{2,1},{3,0},{4,7},{5,6},{6,5},{7,4},{8,11},{9,10},{10,... | collective-permute-start | bytes 393224 | tf_op jit(solution)/shard_map/ppermute | solution.py:490
  22.5 0.8 %collective-permute-start.4 = (bf16[2,256,128]{2,1,0:T(8,128)(2,1)S(1)}, bf16[2,256,128]{2,1,0:T(8,128)(2,1)S(1)}, u32[]{:S(2)}, u32[]{:S(2)}) collective-permute-start(bf16[2,256,128]{2,1,0:T(8,128)(2,1)S(1)} %pick_owner.1.pr_ref), channel_id=1, source_target_pairs={{0,2},{1,3},{2,0},{3,1},{4,6},{5,7},{6,4},{7,5},{8,10},{9,11},{10,... | collective-permute-start | bytes 393224 | tf_op jit(solution)/shard_map/ppermute | solution.py:490
  23.3 1.8 %attend_head.4 = (bf16[2,256,128]{2,1,0:T(8,128)(2,1)S(1)}, f32[2,128]{1,0:T(2,128)S(1)}, bf16[128,768]{1,0:T(8,128)(2,1)S(1)}, f32[128,768]{1,0:T(8,128)S(1)}, ...) custom-call(bf16[2,256,128]{2,1,0:T(8,128)(2,1)S(1)} %pick_owner.1.pr_ref, ...), custom_call_target="tpu_custom_call" | custom-call | flops 276824064 | bytes 1048576 | tf_op jit(solution)/shard_map/attend_head/pallas_call | solution.py:322
  25.1 1.4 %collective-permute-done.3.pr_ref = bf16[2,256,128]{2,1,0:T(8,128)(2,1)S(1)} collective-permute-done((bf16[2,256,128]{2,1,0:T(8,128)(2,1)S(1)}, bf16[2,256,128]{2,1,0:T(8,128)(2,1)S(1)}, u32[]{:S(2)}, u32[]{:S(2)}) %collective-permute-start.3) | collective-permute-done | bytes 131104 | tf_op jit(solution)/shard_map/ppermute | solution.py:490
  26.5 1.8 %attend_head.5 = (bf16[2,256,128]{2,1,0:T(8,128)(2,1)S(1)}, f32[2,128]{1,0:T(2,128)S(1)}, bf16[128,768]{1,0:T(8,128)(2,1)S(1)}, f32[128,768]{1,0:T(8,128)S(1)}, ...) custom-call(bf16[2,256,128]{2,1,0:T(8,128)(2,1)S(1)} %collective-permute-done.3.pr_ref, ...), custom_call_target="tpu_custom_call" | custom-call | flops 276824064 | bytes 1048576 | tf_op jit(solution)/shard_map/attend_head/pallas_call | solution.py:322
  28.3 1.0 %collective-permute-done.5.pr_ref = bf16[2,256,128]{2,1,0:T(8,128)(2,1)S(1)} collective-permute-done((bf16[2,256,128]{2,1,0:T(8,128)(2,1)S(1)}, bf16[2,256,128]{2,1,0:T(8,128)(2,1)S(1)}, u32[]{:S(2)}, u32[]{:S(2)}) %collective-permute-start.5) | collective-permute-done | bytes 131104 | tf_op jit(solution)/shard_map/ppermute | solution.py:490
  29.3 1.8 %attend_head.6 = (bf16[2,256,128]{2,1,0:T(8,128)(2,1)S(1)}, f32[2,128]{1,0:T(2,128)S(1)}, bf16[128,768]{1,0:T(8,128)(2,1)S(1)}, f32[128,768]{1,0:T(8,128)S(1)}, ...) custom-call(bf16[2,256,128]{2,1,0:T(8,128)(2,1)S(1)} %collective-permute-done.5.pr_ref, ...), custom_call_target="tpu_custom_call" | custom-call | flops 276824064 | bytes 1048576 | tf_op jit(solution)/shard_map/attend_head/pallas_call | solution.py:322
  31.1 2.9 %collective-permute-done.4.pr_ref = bf16[2,256,128]{2,1,0:T(8,128)(2,1)S(1)} collective-permute-done((bf16[2,256,128]{2,1,0:T(8,128)(2,1)S(1)}, bf16[2,256,128]{2,1,0:T(8,128)(2,1)S(1)}, u32[]{:S(2)}, u32[]{:S(2)}) %collective-permute-start.4) | collective-permute-done | bytes 131104 | tf_op jit(solution)/shard_map/ppermute | solution.py:490
  34.0 1.8 %attend_head.7 = (bf16[2,256,128]{2,1,0:T(8,128)(2,1)S(1)}, f32[2,128]{1,0:T(2,128)S(1)}, bf16[128,768]{1,0:T(8,128)(2,1)S(1)}, f32[128,768]{1,0:T(8,128)S(1)}, ...) custom-call(bf16[2,256,128]{2,1,0:T(8,128)(2,1)S(1)} %collective-permute-done.4.pr_ref, ...), custom_call_target="tpu_custom_call" | custom-call | flops 276824064 | bytes 1048576 | tf_op jit(solution)/shard_map/attend_head/pallas_call | solution.py:322
  35.8 1.0 %collective-permute-start.6 = (bf16[2,256,128]{2,1,0:T(8,128)(2,1)S(1)}, bf16[2,256,128]{2,1,0:T(8,128)(2,1)S(1)}, u32[]{:S(2)}, u32[]{:S(2)}) collective-permute-start(bf16[2,256,128]{2,1,0:T(8,128)(2,1)S(1)} %get-tuple-element.134), channel_id=1, source_target_pairs={{0,1},{1,0},{2,3},{3,2},{4,5},{5,4},{6,7},{7,6},{8,9},{9,8},{10,11... | collective-permute-start | bytes 393224 | tf_op jit(solution)/shard_map/ppermute | solution.py:490
  36.8 2.5 %collective-permute-start.7 = (bf16[2,256,128]{2,1,0:T(8,128)(2,1)S(1)}, bf16[2,256,128]{2,1,0:T(8,128)(2,1)S(1)}, u32[]{:S(2)}, u32[]{:S(2)}) collective-permute-start(bf16[2,256,128]{2,1,0:T(8,128)(2,1)S(1)} %get-tuple-element.136), channel_id=1, source_target_pairs={{0,3},{1,2},{2,1},{3,0},{4,7},{5,6},{6,5},{7,4},{8,11},{9,10},{10,... | collective-permute-start | bytes 393224 | tf_op jit(solution)/shard_map/ppermute | solution.py:490
  39.2 0.1 collective-permute-start.8
  39.4 0.0 collective-permute-start.9
  39.4 1.1 %collective-permute-done.9 = f32[2,128]{1,0:T(2,128)S(1)} collective-permute-done((f32[2,128]{1,0:T(2,128)S(1)}, f32[2,128]{1,0:T(2,128)S(1)}, u32[]{:S(2)}, u32[]{:S(2)}) %collective-permute-start.9) | collective-permute-done | bytes 1056 | tf_op jit(solution)/shard_map/ppermute | solution.py:513
  40.5 1.5 %collective-permute-start.10 = (f32[2,128]{1,0:T(2,128)S(1)}, f32[2,128]{1,0:T(2,128)S(1)}, u32[]{:S(2)}, u32[]{:S(2)}) collective-permute-start(f32[2,128]{1,0:T(2,128)S(1)} %add.9), channel_id=1, source_target_pairs={{0,8},{4,12},{8,0},{12,4},{16,24},{20,28},{24,16},{28,20},{1,9},{5... | collective-permute-start | bytes 3080 | tf_op jit(solution)/shard_map/ppermute | solution.py:513
  42.0 2.1 %collective-permute-done.10 = f32[2,128]{1,0:T(2,128)S(1)} collective-permute-done((f32[2,128]{1,0:T(2,128)S(1)}, f32[2,128]{1,0:T(2,128)S(1)}, u32[]{:S(2)}, u32[]{:S(2)}) %collective-permute-start.10) | collective-permute-done | bytes 1056 | tf_op jit(solution)/shard_map/ppermute | solution.py:513
  44.1 0.0 collective-permute-done.6.rest_0_
  44.1 0.7 %collective-permute-done.7.rest_1_ = bf16[2,256,128]{2,1,0:T(8,128)(2,1)S(1)} collective-permute-done((bf16[2,256,128]{2,1,0:T(8,128)(2,1)S(1)}, bf16[2,256,128]{2,1,0:T(8,128)(2,1)S(1)}, u32[]{:S(2)}, u32[]{:S(2)}) %collective-permute-start.7) | collective-permute-done | bytes 131104 | tf_op jit(solution)/shard_map/ppermute | solution.py:490
  44.8 1.5 %collective-permute-start.11 = (f32[2,128]{1,0:T(2,128)S(1)}, f32[2,128]{1,0:T(2,128)S(1)}, u32[]{:S(2)}, u32[]{:S(2)}) collective-permute-start(f32[2,128]{1,0:T(2,128)S(1)} %add.10), channel_id=1, source_target_pairs={{0,16},{4,20},{8,24},{12,28},{16,0},{20,4},{24,8},{28,12},{1,17},{... | collective-permute-start | bytes 3080 | tf_op jit(solution)/shard_map/ppermute | solution.py:513
  46.3 3.4 %collective-permute-done.8.rest_2_ = bf16[2,256,128]{2,1,0:T(8,128)(2,1)S(1)} collective-permute-done((bf16[2,256,128]{2,1,0:T(8,128)(2,1)S(1)}, bf16[2,256,128]{2,1,0:T(8,128)(2,1)S(1)}, u32[]{:S(2)}, u32[]{:S(2)}) %collective-permute-start.8) | collective-permute-done | bytes 131104 | tf_op jit(solution)/shard_map/ppermute | solution.py:490
  49.7 0.0 collective-permute-done.11
  49.7 0.1 join_parts.1.refs_0_
  49.8 2.2 %collective-permute-start.12 = (bf16[528,128]{1,0:T(8,128)(2,1)S(1)}, bf16[528,128]{1,0:T(8,128)(2,1)S(1)}, u32[]{:S(2)}, u32[]{:S(2)}) collective-permute-start(bf16[528,128]{1,0:T(8,128)(2,1)S(1)} %join_parts.1.refs_0_), channel_id=1, source_target_pairs={{0,1},{1,0},{2,3},{3,2},{4,5},{5,4},{6,7},{7,6},{8,9},{9,8},{10,11... | collective-permute-start | bytes 405512 | tf_op jit(solution)/shard_map/ppermute | solution.py:490
  52.0 1.1 %collective-permute-start.14 = (bf16[528,128]{1,0:T(8,128)(2,1)S(1)}, bf16[528,128]{1,0:T(8,128)(2,1)S(1)}, u32[]{:S(2)}, u32[]{:S(2)}) collective-permute-start(bf16[528,128]{1,0:T(8,128)(2,1)S(1)} %join_parts.1.refs_0_), channel_id=1, source_target_pairs={{0,2},{1,3},{2,0},{3,1},{4,6},{5,7},{6,4},{7,5},{8,10},{9,11},{10,... | collective-permute-start | bytes 405512 | tf_op jit(solution)/shard_map/ppermute | solution.py:490
  53.1 1.4 %collective-permute-start.13 = (bf16[528,128]{1,0:T(8,128)(2,1)S(1)}, bf16[528,128]{1,0:T(8,128)(2,1)S(1)}, u32[]{:S(2)}, u32[]{:S(2)}) collective-permute-start(bf16[528,128]{1,0:T(8,128)(2,1)S(1)} %join_parts.1.refs_0_), channel_id=1, source_target_pairs={{0,3},{1,2},{2,1},{3,0},{4,7},{5,6},{6,5},{7,4},{8,11},{9,10},{10,... | collective-permute-start | bytes 405512 | tf_op jit(solution)/shard_map/ppermute | solution.py:490
  54.5 2.7 %settle_heads.1 = (bf16[192,2048]{1,0:T(8,128)(2,1)}, bf16[192,2048]{1,0:T(8,128)(2,1)}, bf16[192,512]{1,0:T(8,128)(2,1)}, bf16[192,512]{1,0:T(8,128)(2,1)}) custom-call(s32[5]{0:T(128)S(1)} %pad_add_fusion.meta, bf16[128,768]{1,0:T(8,128)(2,1)S(1)} %get-tuple-element.87.rest_0_, f32[8,768]{1,0:T(8,128)S(1)} %get-tuple-element.88.rest_2_.rest_1_, ...), custom_call_target="tpu_custom_call" | custom-call | tf_op jit(solution)/shard_map/settle_heads/pallas_call | solution.py:345
  57.2 0.8 %collective-permute-done.12.refs_1_ = bf16[528,128]{1,0:T(8,128)(2,1)S(1)} collective-permute-done((bf16[528,128]{1,0:T(8,128)(2,1)S(1)}, bf16[528,128]{1,0:T(8,128)(2,1)S(1)}, u32[]{:S(2)}, u32[]{:S(2)}) %collective-permute-start.12) | collective-permute-done | bytes 135200 | tf_op jit(solution)/shard_map/ppermute | solution.py:490
  58.0 4.8 %collective-permute-done.14.refs_3_ = bf16[528,128]{1,0:T(8,128)(2,1)S(1)} collective-permute-done((bf16[528,128]{1,0:T(8,128)(2,1)S(1)}, bf16[528,128]{1,0:T(8,128)(2,1)S(1)}, u32[]{:S(2)}, u32[]{:S(2)}) %collective-permute-start.14) | collective-permute-done | bytes 135200 | tf_op jit(solution)/shard_map/ppermute | solution.py:490
  62.7 0.0 collective-permute-done.13.refs_2_
  62.7 1.4 %place_prompt_grad.1 = (bf16[2,256,512]{2,1,0:T(8,128)(2,1)}, f32[2,128]{1,0:T(2,128)}) custom-call(s32[1]{0:T(128)} %bitcast.3.flag, s32[1]{0:T(128)} %bitcast.4.me, bf16[528,128]{1,0:T(8,128)(2,1)S(1)} %join_parts.1.refs_0_, bf16[528,128]{1,0:T(8,128)(2,1)S(1)} %collective-permute-done.12.refs_1_, bf16[528,128]{1,0:T(8,128)(2,1)S(1)} %collective-permute-done.13.refs_2_, ...), custom_call_target="tpu_custom_call" | custom-call | tf_op jit(solution)/shard_map/place_prompt_grad/pallas_call | solution.py:429
  (5 shorter events, 0.0 us)
Async XLA Ops:
  2.3 17.3 %collective-permute-start = (bf16[2,256,128]{2,1,0:T(8,128)(2,1)S(1)}, bf16[2,256,128]{2,1,0:T(8,128)(2,1)S(1)}, u32[]{:S(2)}, u32[]{:S(2)}) collective-permute-start(bf16[2,256,128]{2,1,0:T(8,128)(2,1)S(1)} %get-tuple-element.92), channel_id=1, source_target_pairs={{0,1},{1,0},{2,3},{3,2},{4,5},{5,4},{6,7},{7,6},{8,9},{9,8},{10,11... | collective-permute-start | bytes 393224 | tf_op jit(solution)/shard_map/ppermute | solution.py:490
  5.4 14.2 %collective-permute-start.1 = (bf16[2,256,128]{2,1,0:T(8,128)(2,1)S(1)}, bf16[2,256,128]{2,1,0:T(8,128)(2,1)S(1)}, u32[]{:S(2)}, u32[]{:S(2)}) collective-permute-start(bf16[2,256,128]{2,1,0:T(8,128)(2,1)S(1)} %get-tuple-element.94), channel_id=1, source_target_pairs={{0,3},{1,2},{2,1},{3,0},{4,7},{5,6},{6,5},{7,4},{8,11},{9,10},{10,... | collective-permute-start | bytes 393224 | tf_op jit(solution)/shard_map/ppermute | solution.py:490
  7.9 11.8 %collective-permute-start.2 = (bf16[2,256,128]{2,1,0:T(8,128)(2,1)S(1)}, bf16[2,256,128]{2,1,0:T(8,128)(2,1)S(1)}, u32[]{:S(2)}, u32[]{:S(2)}) collective-permute-start(bf16[2,256,128]{2,1,0:T(8,128)(2,1)S(1)} %get-tuple-element.96), channel_id=1, source_target_pairs={{0,2},{1,3},{2,0},{3,1},{4,6},{5,7},{6,4},{7,5},{8,10},{9,11},{10,... | collective-permute-start | bytes 393224 | tf_op jit(solution)/shard_map/ppermute | solution.py:490
  19.7 6.7 %collective-permute-start.3 = (bf16[2,256,128]{2,1,0:T(8,128)(2,1)S(1)}, bf16[2,256,128]{2,1,0:T(8,128)(2,1)S(1)}, u32[]{:S(2)}, u32[]{:S(2)}) collective-permute-start(bf16[2,256,128]{2,1,0:T(8,128)(2,1)S(1)} %pick_owner.1.pr_ref), channel_id=1, source_target_pairs={{0,1},{1,0},{2,3},{3,2},{4,5},{5,4},{6,7},{7,6},{8,9},{9,8},{10,11... | collective-permute-start | bytes 393224 | tf_op jit(solution)/shard_map/ppermute | solution.py:490
  19.8 9.5 %collective-permute-start.5 = (bf16[2,256,128]{2,1,0:T(8,128)(2,1)S(1)}, bf16[2,256,128]{2,1,0:T(8,128)(2,1)S(1)}, u32[]{:S(2)}, u32[]{:S(2)}) collective-permute-start(bf16[2,256,128]{2,1,0:T(8,128)(2,1)S(1)} %pick_owner.1.pr_ref), channel_id=1, source_target_pairs={{0,3},{1,2},{2,1},{3,0},{4,7},{5,6},{6,5},{7,4},{8,11},{9,10},{10,... | collective-permute-start | bytes 393224 | tf_op jit(solution)/shard_map/ppermute | solution.py:490
  22.5 11.5 %collective-permute-start.4 = (bf16[2,256,128]{2,1,0:T(8,128)(2,1)S(1)}, bf16[2,256,128]{2,1,0:T(8,128)(2,1)S(1)}, u32[]{:S(2)}, u32[]{:S(2)}) collective-permute-start(bf16[2,256,128]{2,1,0:T(8,128)(2,1)S(1)} %pick_owner.1.pr_ref), channel_id=1, source_target_pairs={{0,2},{1,3},{2,0},{3,1},{4,6},{5,7},{6,4},{7,5},{8,10},{9,11},{10,... | collective-permute-start | bytes 393224 | tf_op jit(solution)/shard_map/ppermute | solution.py:490
  35.8 8.3 %collective-permute-start.6 = (bf16[2,256,128]{2,1,0:T(8,128)(2,1)S(1)}, bf16[2,256,128]{2,1,0:T(8,128)(2,1)S(1)}, u32[]{:S(2)}, u32[]{:S(2)}) collective-permute-start(bf16[2,256,128]{2,1,0:T(8,128)(2,1)S(1)} %get-tuple-element.134), channel_id=1, source_target_pairs={{0,1},{1,0},{2,3},{3,2},{4,5},{5,4},{6,7},{7,6},{8,9},{9,8},{10,11... | collective-permute-start | bytes 393224 | tf_op jit(solution)/shard_map/ppermute | solution.py:490
  36.8 8.0 %collective-permute-start.7 = (bf16[2,256,128]{2,1,0:T(8,128)(2,1)S(1)}, bf16[2,256,128]{2,1,0:T(8,128)(2,1)S(1)}, u32[]{:S(2)}, u32[]{:S(2)}) collective-permute-start(bf16[2,256,128]{2,1,0:T(8,128)(2,1)S(1)} %get-tuple-element.136), channel_id=1, source_target_pairs={{0,3},{1,2},{2,1},{3,0},{4,7},{5,6},{6,5},{7,4},{8,11},{9,10},{10,... | collective-permute-start | bytes 393224 | tf_op jit(solution)/shard_map/ppermute | solution.py:490
  39.2 10.4 %collective-permute-start.8 = (bf16[2,256,128]{2,1,0:T(8,128)(2,1)S(1)}, bf16[2,256,128]{2,1,0:T(8,128)(2,1)S(1)}, u32[]{:S(2)}, u32[]{:S(2)}) collective-permute-start(bf16[2,256,128]{2,1,0:T(8,128)(2,1)S(1)} %get-tuple-element.138), channel_id=1, source_target_pairs={{0,2},{1,3},{2,0},{3,1},{4,6},{5,7},{6,4},{7,5},{8,10},{9,11},{10,... | collective-permute-start | bytes 393224 | tf_op jit(solution)/shard_map/ppermute | solution.py:490
  39.4 1.1 %collective-permute-start.9 = (f32[2,128]{1,0:T(2,128)S(1)}, f32[2,128]{1,0:T(2,128)S(1)}, u32[]{:S(2)}, u32[]{:S(2)}) collective-permute-start(f32[2,128]{1,0:T(2,128)S(1)} %get-tuple-element.133), channel_id=1, source_target_pairs={{0,4},{4,0},{8,12},{12,8},{16,20},{20,16},{24,28},{28,24},{1,5},{5... | collective-permute-start | bytes 3080 | tf_op jit(solution)/shard_map/ppermute | solution.py:513
  40.5 3.6 %collective-permute-start.10 = (f32[2,128]{1,0:T(2,128)S(1)}, f32[2,128]{1,0:T(2,128)S(1)}, u32[]{:S(2)}, u32[]{:S(2)}) collective-permute-start(f32[2,128]{1,0:T(2,128)S(1)} %add.9), channel_id=1, source_target_pairs={{0,8},{4,12},{8,0},{12,4},{16,24},{20,28},{24,16},{28,20},{1,9},{5... | collective-permute-start | bytes 3080 | tf_op jit(solution)/shard_map/ppermute | solution.py:513
  44.8 4.9 %collective-permute-start.11 = (f32[2,128]{1,0:T(2,128)S(1)}, f32[2,128]{1,0:T(2,128)S(1)}, u32[]{:S(2)}, u32[]{:S(2)}) collective-permute-start(f32[2,128]{1,0:T(2,128)S(1)} %add.10), channel_id=1, source_target_pairs={{0,16},{4,20},{8,24},{12,28},{16,0},{20,4},{24,8},{28,12},{1,17},{... | collective-permute-start | bytes 3080 | tf_op jit(solution)/shard_map/ppermute | solution.py:513
  49.8 8.2 %collective-permute-start.12 = (bf16[528,128]{1,0:T(8,128)(2,1)S(1)}, bf16[528,128]{1,0:T(8,128)(2,1)S(1)}, u32[]{:S(2)}, u32[]{:S(2)}) collective-permute-start(bf16[528,128]{1,0:T(8,128)(2,1)S(1)} %join_parts.1.refs_0_), channel_id=1, source_target_pairs={{0,1},{1,0},{2,3},{3,2},{4,5},{5,4},{6,7},{7,6},{8,9},{9,8},{10,11... | collective-permute-start | bytes 405512 | tf_op jit(solution)/shard_map/ppermute | solution.py:490
  52.0 10.7 %collective-permute-start.14 = (bf16[528,128]{1,0:T(8,128)(2,1)S(1)}, bf16[528,128]{1,0:T(8,128)(2,1)S(1)}, u32[]{:S(2)}, u32[]{:S(2)}) collective-permute-start(bf16[528,128]{1,0:T(8,128)(2,1)S(1)} %join_parts.1.refs_0_), channel_id=1, source_target_pairs={{0,2},{1,3},{2,0},{3,1},{4,6},{5,7},{6,4},{7,5},{8,10},{9,11},{10,... | collective-permute-start | bytes 405512 | tf_op jit(solution)/shard_map/ppermute | solution.py:490
  53.1 9.6 %collective-permute-start.13 = (bf16[528,128]{1,0:T(8,128)(2,1)S(1)}, bf16[528,128]{1,0:T(8,128)(2,1)S(1)}, u32[]{:S(2)}, u32[]{:S(2)}) collective-permute-start(bf16[528,128]{1,0:T(8,128)(2,1)S(1)} %join_parts.1.refs_0_), channel_id=1, source_target_pairs={{0,3},{1,2},{2,1},{3,0},{4,7},{5,6},{6,5},{7,4},{8,11},{9,10},{10,... | collective-permute-start | bytes 405512 | tf_op jit(solution)/shard_map/ppermute | solution.py:490

commit v18 on v17

--- a/solution.py
+++ b/solution.py
@@ -507,12 +507,16 @@
         parts.append(part)
 
     if direct:
-        backs = [swap(after(x, acc), s) for x, s in zip(parts[1:], steps[1:])]
+        last_crossing = kv_heads - 2
+        sent = [x if s == last_crossing else after(x, acc) for s, x in enumerate(parts)]
+        backs = [swap(x, s) for x, s in zip(sent[1:], steps[1:])]
 
     def hop(x, step):
         return lax.ppermute(x, "dp", [(i, i ^ step) for i in range(n_dp)])
 
     gains = acc + hop(acc, 1)
+    if direct:
+        gains = after(gains, backs[last_crossing - 1])
     step = 2
     while step < n_dp:
         arrived = hop(gains, step)

time: 64.4 us -> 64.8 us (level)
  starting transfers between devices: 20.5 us -> 22 us
  waiting for transfers between devices: 22.8 us -> 21.7 us
    ppermute x12, waiting for transfers between devices: 19.6 us -> 17.2 us  [swap(): return lax.ppermute(x, 'group', [(i, i ^ step) for i in range(n_group)])]
    ppermute x12, starting transfers between devices: 17.5 us -> 19 us  [swap(): return lax.ppermute(x, 'group', [(i, i ^ step) for i in range(n_group)])]
    ppermute x3, waiting for transfers between devices: 3.22 us -> 4.56 us  [hop(): return lax.ppermute(x, 'dp', [(i, i ^ step) for i in range(n_dp)])]
  transfers between devices with their start and end apart: 15 -> 15, of which waited for: 10 -> 10; matrix products, arithmetic and copies ran while one was open for 0% -> 0% of each run, Pallas kernels for 21% -> 24%
where the time goes in v18:
time: 64.8 us; the launch traced here: 64.6 us
  starting transfers between devices  22 us (34%)
  waiting for transfers between devices  21.7 us (33%)
  Pallas kernels  18.7 us (29%)
  between operations  2.02 us (3%)
    ppermute x12, starting transfers between devices, swap(): return lax.ppermute(x, 'group', [(i, i ^ step) for i in range(n_group)])  19 us
    ppermute x12, waiting for transfers between devices, swap(): return lax.ppermute(x, 'group', [(i, i ^ step) for i in range(n_group)])  17.2 us
    pallas_call x4, Pallas kernels, first_half(): pl.pallas_call(functools.partial(first_kernel, 2 * HD), out_shape=[jax.Sh...  7.17 us
    pallas_call x1, Pallas kernels, prepare(): pl.pallas_call(functools.partial(prepare_kernel, slots, share, rows, 2 *...  5.64 us
    ppermute x3, waiting for transfers between devices, hop(): return lax.ppermute(x, 'dp', [(i, i ^ step) for i in range(n_dp)])  4.56 us
    ppermute x3, starting transfers between devices, hop(): return lax.ppermute(x, 'dp', [(i, i ^ step) for i in range(n_dp)])  3.01 us
    pallas_call x1, Pallas kernels, settle_heads(): pl.pallas_call(functools.partial(settle_kernel, 2 * HD), out_shape=out_sh...  2.69 us
    pallas_call x1, Pallas kernels, cut(): pl.pallas_call(cut_kernel, out_shape=[jax.ShapeDtypeStruct((depth, rows,...  1.69 us
  transfers between devices with their start and end apart: 15, of which 10 were waited for; matrix products, arithmetic and copies ran while one was open for 0% of the time, Pallas kernels for 24%

profile of v18, /device:TPU:0, one launch (start us, length us, event | category | flops | bytes accessed | tf_op | source)
XLA Modules:
  0.0 64.6 jit_solution(16381578062778859346)
XLA Ops:
  0.6 1.7 %cut_prompt.1 = (bf16[2,256,128]{2,1,0:T(8,128)(2,1)S(1)}, bf16[2,256,128]{2,1,0:T(8,128)(2,1)S(1)}, bf16[2,256,128]{2,1,0:T(8,128)(2,1)S(1)}, bf16[2,256,128]{2,1,0:T(8,128)(2,1)S(1)}) custom-call(s32[4]{0:T(128)S(1)} %fusion.order, bf16[2,256,512]{2,1,0:T(8,128)(2,1)} %bitcast.20), custom_call_target="tpu_custom_call" | custom-call | tf_op jit(solution)/shard_map/cut_prompt/pallas_call | solution.py:48
  2.3 3.1 %collective-permute-start = (bf16[2,256,128]{2,1,0:T(8,128)(2,1)S(1)}, bf16[2,256,128]{2,1,0:T(8,128)(2,1)S(1)}, u32[]{:S(2)}, u32[]{:S(2)}) collective-permute-start(bf16[2,256,128]{2,1,0:T(8,128)(2,1)S(1)} %get-tuple-element.92), channel_id=1, source_target_pairs={{0,1},{1,0},{2,3},{3,2},{4,5},{5,4},{6,7},{7,6},{8,9},{9,8},{10,11... | collective-permute-start | bytes 393224 | tf_op jit(solution)/shard_map/ppermute | solution.py:490
  5.4 2.5 %collective-permute-start.1 = (bf16[2,256,128]{2,1,0:T(8,128)(2,1)S(1)}, bf16[2,256,128]{2,1,0:T(8,128)(2,1)S(1)}, u32[]{:S(2)}, u32[]{:S(2)}) collective-permute-start(bf16[2,256,128]{2,1,0:T(8,128)(2,1)S(1)} %get-tuple-element.94), channel_id=1, source_target_pairs={{0,3},{1,2},{2,1},{3,0},{4,7},{5,6},{6,5},{7,4},{8,11},{9,10},{10,... | collective-permute-start | bytes 393224 | tf_op jit(solution)/shard_map/ppermute | solution.py:490
  7.9 0.1 collective-permute-start.2
  9.3 0.1 pad_add_fusion.meta
  9.4 5.6 %prepare_response.1 = (bf16[128,768]{1,0:T(8,128)(2,1)S(1)}, bf16[128,768]{1,0:T(8,128)(2,1)S(1)}, f32[8,768]{1,0:T(8,128)S(1)}, bf16[192,768]{1,0:T(8,128)(2,1)...) custom-call(s32[5]{0:T(128)S(1)} %pad_add_fusion.meta, ...), custom_call_target="tpu_custom_call" | custom-call | flops 452984832 | bytes 3932160 | tf_op jit(solution)/shard_map/prepare_response/pallas_call | solution.py:162
  15.1 4.6 %collective-permute-done.2.refs_3_ = bf16[2,256,128]{2,1,0:T(8,128)(2,1)S(1)} collective-permute-done((bf16[2,256,128]{2,1,0:T(8,128)(2,1)S(1)}, bf16[2,256,128]{2,1,0:T(8,128)(2,1)S(1)}, u32[]{:S(2)}, u32[]{:S(2)}) %collective-permute-start.2) | collective-permute-done | bytes 131104 | tf_op jit(solution)/shard_map/ppermute | solution.py:490
  19.7 0.0 collective-permute-done.1.refs_2_
  19.7 0.0 collective-permute-done.refs_1_
  19.7 0.1 pick_owner.1.pr_ref
  19.7 0.1 collective-permute-start.3
  19.8 2.7 %collective-permute-start.5 = (bf16[2,256,128]{2,1,0:T(8,128)(2,1)S(1)}, bf16[2,256,128]{2,1,0:T(8,128)(2,1)S(1)}, u32[]{:S(2)}, u32[]{:S(2)}) collective-permute-start(bf16[2,256,128]{2,1,0:T(8,128)(2,1)S(1)} %pick_owner.1.pr_ref), channel_id=1, source_target_pairs={{0,3},{1,2},{2,1},{3,0},{4,7},{5,6},{6,5},{7,4},{8,11},{9,10},{10,... | collective-permute-start | bytes 393224 | tf_op jit(solution)/shard_map/ppermute | solution.py:490
  22.5 0.8 %collective-permute-start.4 = (bf16[2,256,128]{2,1,0:T(8,128)(2,1)S(1)}, bf16[2,256,128]{2,1,0:T(8,128)(2,1)S(1)}, u32[]{:S(2)}, u32[]{:S(2)}) collective-permute-start(bf16[2,256,128]{2,1,0:T(8,128)(2,1)S(1)} %pick_owner.1.pr_ref), channel_id=1, source_target_pairs={{0,2},{1,3},{2,0},{3,1},{4,6},{5,7},{6,4},{7,5},{8,10},{9,11},{10,... | collective-permute-start | bytes 393224 | tf_op jit(solution)/shard_map/ppermute | solution.py:490
  23.3 1.8 %attend_head.4 = (bf16[2,256,128]{2,1,0:T(8,128)(2,1)S(1)}, f32[2,128]{1,0:T(2,128)S(1)}, bf16[128,768]{1,0:T(8,128)(2,1)S(1)}, f32[128,768]{1,0:T(8,128)S(1)}, ...) custom-call(bf16[2,256,128]{2,1,0:T(8,128)(2,1)S(1)} %pick_owner.1.pr_ref, ...), custom_call_target="tpu_custom_call" | custom-call | flops 276824064 | bytes 1048576 | tf_op jit(solution)/shard_map/attend_head/pallas_call | solution.py:322
  25.1 1.4 %collective-permute-done.3.pr_ref = bf16[2,256,128]{2,1,0:T(8,128)(2,1)S(1)} collective-permute-done((bf16[2,256,128]{2,1,0:T(8,128)(2,1)S(1)}, bf16[2,256,128]{2,1,0:T(8,128)(2,1)S(1)}, u32[]{:S(2)}, u32[]{:S(2)}) %collective-permute-start.3) | collective-permute-done | bytes 131104 | tf_op jit(solution)/shard_map/ppermute | solution.py:490
  26.5 1.8 %attend_head.5 = (bf16[2,256,128]{2,1,0:T(8,128)(2,1)S(1)}, f32[2,128]{1,0:T(2,128)S(1)}, bf16[128,768]{1,0:T(8,128)(2,1)S(1)}, f32[128,768]{1,0:T(8,128)S(1)}, ...) custom-call(bf16[2,256,128]{2,1,0:T(8,128)(2,1)S(1)} %collective-permute-done.3.pr_ref, ...), custom_call_target="tpu_custom_call" | custom-call | flops 276824064 | bytes 1048576 | tf_op jit(solution)/shard_map/attend_head/pallas_call | solution.py:322
  28.3 1.0 %collective-permute-done.5.pr_ref = bf16[2,256,128]{2,1,0:T(8,128)(2,1)S(1)} collective-permute-done((bf16[2,256,128]{2,1,0:T(8,128)(2,1)S(1)}, bf16[2,256,128]{2,1,0:T(8,128)(2,1)S(1)}, u32[]{:S(2)}, u32[]{:S(2)}) %collective-permute-start.5) | collective-permute-done | bytes 131104 | tf_op jit(solution)/shard_map/ppermute | solution.py:490
  29.3 1.8 %attend_head.6 = (bf16[2,256,128]{2,1,0:T(8,128)(2,1)S(1)}, f32[2,128]{1,0:T(2,128)S(1)}, bf16[128,768]{1,0:T(8,128)(2,1)S(1)}, f32[128,768]{1,0:T(8,128)S(1)}, ...) custom-call(bf16[2,256,128]{2,1,0:T(8,128)(2,1)S(1)} %collective-permute-done.5.pr_ref, ...), custom_call_target="tpu_custom_call" | custom-call | flops 276824064 | bytes 1048576 | tf_op jit(solution)/shard_map/attend_head/pallas_call | solution.py:322
  31.1 2.2 %collective-permute-start.7 = (bf16[2,256,128]{2,1,0:T(8,128)(2,1)S(1)}, bf16[2,256,128]{2,1,0:T(8,128)(2,1)S(1)}, u32[]{:S(2)}, u32[]{:S(2)}) collective-permute-start(bf16[2,256,128]{2,1,0:T(8,128)(2,1)S(1)} %get-tuple-element.135), channel_id=1, source_target_pairs={{0,3},{1,2},{2,1},{3,0},{4,7},{5,6},{6,5},{7,4},{8,11},{9,10},{10,... | collective-permute-start | bytes 393224 | tf_op jit(solution)/shard_map/ppermute | solution.py:490
  33.3 4.9 %collective-permute-done.4.pr_ref = bf16[2,256,128]{2,1,0:T(8,128)(2,1)S(1)} collective-permute-done((bf16[2,256,128]{2,1,0:T(8,128)(2,1)S(1)}, bf16[2,256,128]{2,1,0:T(8,128)(2,1)S(1)}, u32[]{:S(2)}, u32[]{:S(2)}) %collective-permute-start.4) | collective-permute-done | bytes 131104 | tf_op jit(solution)/shard_map/ppermute | solution.py:490
  38.1 1.8 %attend_head.7 = (bf16[2,256,128]{2,1,0:T(8,128)(2,1)S(1)}, f32[2,128]{1,0:T(2,128)S(1)}, bf16[128,768]{1,0:T(8,128)(2,1)S(1)}, f32[128,768]{1,0:T(8,128)S(1)}, ...) custom-call(bf16[2,256,128]{2,1,0:T(8,128)(2,1)S(1)} %collective-permute-done.4.pr_ref, ...), custom_call_target="tpu_custom_call" | custom-call | flops 276824064 | bytes 1048576 | tf_op jit(solution)/shard_map/attend_head/pallas_call | solution.py:322
  39.9 0.1 collective-permute-start.6
  40.0 3.0 %collective-permute-start.8 = (bf16[2,256,128]{2,1,0:T(8,128)(2,1)S(1)}, bf16[2,256,128]{2,1,0:T(8,128)(2,1)S(1)}, u32[]{:S(2)}, u32[]{:S(2)}) collective-permute-start(bf16[2,256,128]{2,1,0:T(8,128)(2,1)S(1)} %get-tuple-element.137), channel_id=1, source_target_pairs={{0,2},{1,3},{2,0},{3,1},{4,6},{5,7},{6,4},{7,5},{8,10},{9,11},{10,... | collective-permute-start | bytes 393224 | tf_op jit(solution)/shard_map/ppermute | solution.py:490
  43.0 0.0 collective-permute-start.9
  43.1 1.1 %collective-permute-done.9 = f32[2,128]{1,0:T(2,128)S(1)} collective-permute-done((f32[2,128]{1,0:T(2,128)S(1)}, f32[2,128]{1,0:T(2,128)S(1)}, u32[]{:S(2)}, u32[]{:S(2)}) %collective-permute-start.9) | collective-permute-done | bytes 1056 | tf_op jit(solution)/shard_map/ppermute | solution.py:515
  44.2 0.0 collective-permute-done.7.rest_1_
  44.2 1.5 %collective-permute-start.10 = (f32[2,128]{1,0:T(2,128)S(1)}, f32[2,128]{1,0:T(2,128)S(1)}, u32[]{:S(2)}, u32[]{:S(2)}) collective-permute-start(f32[2,128]{1,0:T(2,128)S(1)} %add.9), channel_id=1, source_target_pairs={{0,8},{4,12},{8,0},{12,4},{16,24},{20,28},{24,16},{28,20},{1,9},{5... | collective-permute-start | bytes 3080 | tf_op jit(solution)/shard_map/ppermute | solution.py:515
  45.7 0.7 %collective-permute-done.6.rest_0_ = bf16[2,256,128]{2,1,0:T(8,128)(2,1)S(1)} collective-permute-done((bf16[2,256,128]{2,1,0:T(8,128)(2,1)S(1)}, bf16[2,256,128]{2,1,0:T(8,128)(2,1)S(1)}, u32[]{:S(2)}, u32[]{:S(2)}) %collective-permute-start.6) | collective-permute-done | bytes 131104 | tf_op jit(solution)/shard_map/ppermute | solution.py:490
  46.4 1.4 %collective-permute-done.10 = f32[2,128]{1,0:T(2,128)S(1)} collective-permute-done((f32[2,128]{1,0:T(2,128)S(1)}, f32[2,128]{1,0:T(2,128)S(1)}, u32[]{:S(2)}, u32[]{:S(2)}) %collective-permute-start.10) | collective-permute-done | bytes 1056 | tf_op jit(solution)/shard_map/ppermute | solution.py:515
  47.8 1.5 %collective-permute-start.11 = (f32[2,128]{1,0:T(2,128)S(1)}, f32[2,128]{1,0:T(2,128)S(1)}, u32[]{:S(2)}, u32[]{:S(2)}) collective-permute-start(f32[2,128]{1,0:T(2,128)S(1)} %add.10), channel_id=1, source_target_pairs={{0,16},{4,20},{8,24},{12,28},{16,0},{20,4},{24,8},{28,12},{1,17},{... | collective-permute-start | bytes 3080 | tf_op jit(solution)/shard_map/ppermute | solution.py:515
  49.3 0.0 collective-permute-done.8.rest_2_
  49.3 2.0 %collective-permute-done.11 = f32[2,128]{1,0:T(2,128)S(1)} collective-permute-done((f32[2,128]{1,0:T(2,128)S(1)}, f32[2,128]{1,0:T(2,128)S(1)}, u32[]{:S(2)}, u32[]{:S(2)}) %collective-permute-start.11) | collective-permute-done | bytes 1056 | tf_op jit(solution)/shard_map/ppermute | solution.py:515
  51.3 0.1 join_parts.1.refs_0_
  51.4 0.1 collective-permute-start.12
  51.6 1.8 %collective-permute-start.14 = (bf16[528,128]{1,0:T(8,128)(2,1)S(1)}, bf16[528,128]{1,0:T(8,128)(2,1)S(1)}, u32[]{:S(2)}, u32[]{:S(2)}) collective-permute-start(bf16[528,128]{1,0:T(8,128)(2,1)S(1)} %join_parts.1.refs_0_), channel_id=1, source_target_pairs={{0,2},{1,3},{2,0},{3,1},{4,6},{5,7},{6,4},{7,5},{8,10},{9,11},{10,... | collective-permute-start | bytes 405512 | tf_op jit(solution)/shard_map/ppermute | solution.py:490
  53.4 2.5 %collective-permute-start.13 = (bf16[528,128]{1,0:T(8,128)(2,1)S(1)}, bf16[528,128]{1,0:T(8,128)(2,1)S(1)}, u32[]{:S(2)}, u32[]{:S(2)}) collective-permute-start(bf16[528,128]{1,0:T(8,128)(2,1)S(1)} %join_parts.1.refs_0_), channel_id=1, source_target_pairs={{0,3},{1,2},{2,1},{3,0},{4,7},{5,6},{6,5},{7,4},{8,11},{9,10},{10,... | collective-permute-start | bytes 405512 | tf_op jit(solution)/shard_map/ppermute | solution.py:490
  55.9 2.7 %settle_heads.1 = (bf16[192,2048]{1,0:T(8,128)(2,1)}, bf16[192,2048]{1,0:T(8,128)(2,1)}, bf16[192,512]{1,0:T(8,128)(2,1)}, bf16[192,512]{1,0:T(8,128)(2,1)}) custom-call(s32[5]{0:T(128)S(1)} %pad_add_fusion.meta, bf16[128,768]{1,0:T(8,128)(2,1)S(1)} %get-tuple-element.87.rest_0_, f32[8,768]{1,0:T(8,128)S(1)} %get-tuple-element.88.rest_2_.rest_1_, ...), custom_call_target="tpu_custom_call" | custom-call | tf_op jit(solution)/shard_map/settle_heads/pallas_call | solution.py:345
  58.6 0.1 collective-permute-done.12.refs_1_
  58.7 4.4 %collective-permute-done.14.refs_3_ = bf16[528,128]{1,0:T(8,128)(2,1)S(1)} collective-permute-done((bf16[528,128]{1,0:T(8,128)(2,1)S(1)}, bf16[528,128]{1,0:T(8,128)(2,1)S(1)}, u32[]{:S(2)}, u32[]{:S(2)}) %collective-permute-start.14) | collective-permute-done | bytes 135200 | tf_op jit(solution)/shard_map/ppermute | solution.py:490
  63.1 0.0 collective-permute-done.13.refs_2_
  63.1 1.4 %place_prompt_grad.1 = (bf16[2,256,512]{2,1,0:T(8,128)(2,1)}, f32[2,128]{1,0:T(2,128)}) custom-call(s32[1]{0:T(128)} %bitcast.3.flag, s32[1]{0:T(128)} %bitcast.4.me, bf16[528,128]{1,0:T(8,128)(2,1)S(1)} %join_parts.1.refs_0_, bf16[528,128]{1,0:T(8,128)(2,1)S(1)} %collective-permute-done.12.refs_1_, bf16[528,128]{1,0:T(8,128)(2,1)S(1)} %collective-permute-done.13.refs_2_, ...), custom_call_target="tpu_custom_call" | custom-call | tf_op jit(solution)/shard_map/place_prompt_grad/pallas_call | solution.py:429
  (5 shorter events, 0.0 us)
Async XLA Ops:
  2.3 17.3 %collective-permute-start = (bf16[2,256,128]{2,1,0:T(8,128)(2,1)S(1)}, bf16[2,256,128]{2,1,0:T(8,128)(2,1)S(1)}, u32[]{:S(2)}, u32[]{:S(2)}) collective-permute-start(bf16[2,256,128]{2,1,0:T(8,128)(2,1)S(1)} %get-tuple-element.92), channel_id=1, source_target_pairs={{0,1},{1,0},{2,3},{3,2},{4,5},{5,4},{6,7},{7,6},{8,9},{9,8},{10,11... | collective-permute-start | bytes 393224 | tf_op jit(solution)/shard_map/ppermute | solution.py:490
  5.4 14.2 %collective-permute-start.1 = (bf16[2,256,128]{2,1,0:T(8,128)(2,1)S(1)}, bf16[2,256,128]{2,1,0:T(8,128)(2,1)S(1)}, u32[]{:S(2)}, u32[]{:S(2)}) collective-permute-start(bf16[2,256,128]{2,1,0:T(8,128)(2,1)S(1)} %get-tuple-element.94), channel_id=1, source_target_pairs={{0,3},{1,2},{2,1},{3,0},{4,7},{5,6},{6,5},{7,4},{8,11},{9,10},{10,... | collective-permute-start | bytes 393224 | tf_op jit(solution)/shard_map/ppermute | solution.py:490
  7.9 11.8 %collective-permute-start.2 = (bf16[2,256,128]{2,1,0:T(8,128)(2,1)S(1)}, bf16[2,256,128]{2,1,0:T(8,128)(2,1)S(1)}, u32[]{:S(2)}, u32[]{:S(2)}) collective-permute-start(bf16[2,256,128]{2,1,0:T(8,128)(2,1)S(1)} %get-tuple-element.96), channel_id=1, source_target_pairs={{0,2},{1,3},{2,0},{3,1},{4,6},{5,7},{6,4},{7,5},{8,10},{9,11},{10,... | collective-permute-start | bytes 393224 | tf_op jit(solution)/shard_map/ppermute | solution.py:490
  19.7 6.7 %collective-permute-start.3 = (bf16[2,256,128]{2,1,0:T(8,128)(2,1)S(1)}, bf16[2,256,128]{2,1,0:T(8,128)(2,1)S(1)}, u32[]{:S(2)}, u32[]{:S(2)}) collective-permute-start(bf16[2,256,128]{2,1,0:T(8,128)(2,1)S(1)} %pick_owner.1.pr_ref), channel_id=1, source_target_pairs={{0,1},{1,0},{2,3},{3,2},{4,5},{5,4},{6,7},{7,6},{8,9},{9,8},{10,11... | collective-permute-start | bytes 393224 | tf_op jit(solution)/shard_map/ppermute | solution.py:490
  19.8 9.5 %collective-permute-start.5 = (bf16[2,256,128]{2,1,0:T(8,128)(2,1)S(1)}, bf16[2,256,128]{2,1,0:T(8,128)(2,1)S(1)}, u32[]{:S(2)}, u32[]{:S(2)}) collective-permute-start(bf16[2,256,128]{2,1,0:T(8,128)(2,1)S(1)} %pick_owner.1.pr_ref), channel_id=1, source_target_pairs={{0,3},{1,2},{2,1},{3,0},{4,7},{5,6},{6,5},{7,4},{8,11},{9,10},{10,... | collective-permute-start | bytes 393224 | tf_op jit(solution)/shard_map/ppermute | solution.py:490
  22.5 15.6 %collective-permute-start.4 = (bf16[2,256,128]{2,1,0:T(8,128)(2,1)S(1)}, bf16[2,256,128]{2,1,0:T(8,128)(2,1)S(1)}, u32[]{:S(2)}, u32[]{:S(2)}) collective-permute-start(bf16[2,256,128]{2,1,0:T(8,128)(2,1)S(1)} %pick_owner.1.pr_ref), channel_id=1, source_target_pairs={{0,2},{1,3},{2,0},{3,1},{4,6},{5,7},{6,4},{7,5},{8,10},{9,11},{10,... | collective-permute-start | bytes 393224 | tf_op jit(solution)/shard_map/ppermute | solution.py:490
  31.1 13.1 %collective-permute-start.7 = (bf16[2,256,128]{2,1,0:T(8,128)(2,1)S(1)}, bf16[2,256,128]{2,1,0:T(8,128)(2,1)S(1)}, u32[]{:S(2)}, u32[]{:S(2)}) collective-permute-start(bf16[2,256,128]{2,1,0:T(8,128)(2,1)S(1)} %get-tuple-element.135), channel_id=1, source_target_pairs={{0,3},{1,2},{2,1},{3,0},{4,7},{5,6},{6,5},{7,4},{8,11},{9,10},{10,... | collective-permute-start | bytes 393224 | tf_op jit(solution)/shard_map/ppermute | solution.py:490
  39.9 6.4 %collective-permute-start.6 = (bf16[2,256,128]{2,1,0:T(8,128)(2,1)S(1)}, bf16[2,256,128]{2,1,0:T(8,128)(2,1)S(1)}, u32[]{:S(2)}, u32[]{:S(2)}) collective-permute-start(bf16[2,256,128]{2,1,0:T(8,128)(2,1)S(1)} %get-tuple-element.134), channel_id=1, source_target_pairs={{0,1},{1,0},{2,3},{3,2},{4,5},{5,4},{6,7},{7,6},{8,9},{9,8},{10,11... | collective-permute-start | bytes 393224 | tf_op jit(solution)/shard_map/ppermute | solution.py:490
  40.0 9.3 %collective-permute-start.8 = (bf16[2,256,128]{2,1,0:T(8,128)(2,1)S(1)}, bf16[2,256,128]{2,1,0:T(8,128)(2,1)S(1)}, u32[]{:S(2)}, u32[]{:S(2)}) collective-permute-start(bf16[2,256,128]{2,1,0:T(8,128)(2,1)S(1)} %get-tuple-element.137), channel_id=1, source_target_pairs={{0,2},{1,3},{2,0},{3,1},{4,6},{5,7},{6,4},{7,5},{8,10},{9,11},{10,... | collective-permute-start | bytes 393224 | tf_op jit(solution)/shard_map/ppermute | solution.py:490
  43.0 1.1 %collective-permute-start.9 = (f32[2,128]{1,0:T(2,128)S(1)}, f32[2,128]{1,0:T(2,128)S(1)}, u32[]{:S(2)}, u32[]{:S(2)}) collective-permute-start(f32[2,128]{1,0:T(2,128)S(1)} %get-tuple-element.133), channel_id=1, source_target_pairs={{0,4},{4,0},{8,12},{12,8},{16,20},{20,16},{24,28},{28,24},{1,5},{5... | collective-permute-start | bytes 3080 | tf_op jit(solution)/shard_map/ppermute | solution.py:515
  44.2 3.6 %collective-permute-start.10 = (f32[2,128]{1,0:T(2,128)S(1)}, f32[2,128]{1,0:T(2,128)S(1)}, u32[]{:S(2)}, u32[]{:S(2)}) collective-permute-start(f32[2,128]{1,0:T(2,128)S(1)} %add.9), channel_id=1, source_target_pairs={{0,8},{4,12},{8,0},{12,4},{16,24},{20,28},{24,16},{28,20},{1,9},{5... | collective-permute-start | bytes 3080 | tf_op jit(solution)/shard_map/ppermute | solution.py:515
  47.8 3.6 %collective-permute-start.11 = (f32[2,128]{1,0:T(2,128)S(1)}, f32[2,128]{1,0:T(2,128)S(1)}, u32[]{:S(2)}, u32[]{:S(2)}) collective-permute-start(f32[2,128]{1,0:T(2,128)S(1)} %add.10), channel_id=1, source_target_pairs={{0,16},{4,20},{8,24},{12,28},{16,0},{20,4},{24,8},{28,12},{1,17},{... | collective-permute-start | bytes 3080 | tf_op jit(solution)/shard_map/ppermute | solution.py:515
  51.4 7.3 %collective-permute-start.12 = (bf16[528,128]{1,0:T(8,128)(2,1)S(1)}, bf16[528,128]{1,0:T(8,128)(2,1)S(1)}, u32[]{:S(2)}, u32[]{:S(2)}) collective-permute-start(bf16[528,128]{1,0:T(8,128)(2,1)S(1)} %join_parts.1.refs_0_), channel_id=1, source_target_pairs={{0,1},{1,0},{2,3},{3,2},{4,5},{5,4},{6,7},{7,6},{8,9},{9,8},{10,11... | collective-permute-start | bytes 405512 | tf_op jit(solution)/shard_map/ppermute | solution.py:490
  51.6 11.6 %collective-permute-start.14 = (bf16[528,128]{1,0:T(8,128)(2,1)S(1)}, bf16[528,128]{1,0:T(8,128)(2,1)S(1)}, u32[]{:S(2)}, u32[]{:S(2)}) collective-permute-start(bf16[528,128]{1,0:T(8,128)(2,1)S(1)} %join_parts.1.refs_0_), channel_id=1, source_target_pairs={{0,2},{1,3},{2,0},{3,1},{4,6},{5,7},{6,4},{7,5},{8,10},{9,11},{10,... | collective-permute-start | bytes 405512 | tf_op jit(solution)/shard_map/ppermute | solution.py:490
  53.4 9.7 %collective-permute-start.13 = (bf16[528,128]{1,0:T(8,128)(2,1)S(1)}, bf16[528,128]{1,0:T(8,128)(2,1)S(1)}, u32[]{:S(2)}, u32[]{:S(2)}) collective-permute-start(bf16[528,128]{1,0:T(8,128)(2,1)S(1)} %join_parts.1.refs_0_), channel_id=1, source_target_pairs={{0,3},{1,2},{2,1},{3,0},{4,7},{5,6},{6,5},{7,4},{8,11},{9,10},{10,... | collective-permute-start | bytes 405512 | tf_op jit(solution)/shard_map/ppermute | solution.py:490

commit v19 on v16

--- a/solution.py
+++ b/solution.py
@@ -31,11 +31,11 @@
     return pltpu.CompilerParams(vmem_limit_bytes=mib * 2**20)
 
 
-def cut_kernel(order, cache_ref, *rest):
+def cut_kernel(steps, me, cache_ref, *rest):
     outs, sems = rest[:-1], rest[-1]
     copies = []
     for i, out in enumerate(outs):
-        at = pl.multiple_of(order[i] * HD, HD)
+        at = pl.multiple_of((me[0] ^ steps[i]) * HD, HD)
         copy = pltpu.make_async_copy(cache_ref.at[:, :, pl.ds(at, HD)], out, sems.at[i])
         copy.start()
         copies.append(copy)
@@ -43,17 +43,17 @@
         copy.wait()
 
 
-def cut(order, cache, count):
+def cut(steps, me, cache, count):
     depth, rows, _ = cache.shape
     return pl.pallas_call(
-        cut_kernel,
+        functools.partial(cut_kernel, tuple(steps)),
         out_shape=[jax.ShapeDtypeStruct((depth, rows, HD), BF)] * count,
         in_specs=[SMEM, HBM],
         out_specs=[VMEM] * count,
         scratch_shapes=[pltpu.SemaphoreType.DMA((count,))],
         compiler_params=params(4),
         name="cut_prompt",
-    )(order, cache)
+    )(me, cache)
 
 
 def pick_kernel(which, *refs):
@@ -490,7 +490,7 @@
         return lax.ppermute(x, "group", [(i, i ^ step) for i in range(n_group)])
 
     if direct:
-        blocks = list(cut(order, pltpu.with_memory_space_constraint(cache, pltpu.HBM), kv_heads))
+        blocks = list(cut(steps, jnp.reshape(me, (1,)).astype(jnp.int32), pltpu.with_memory_space_constraint(cache, pltpu.HBM), kv_heads))
         got = [blocks[0]] + [swap(blocks[s], steps[s]) for s in range(1, n_group)]
         for s in range(1, n_group):
             got[s] = after(got[s], kept[0][2])
@@ -498,7 +498,7 @@
         prompts = [mine] + [swap(mine, steps[s]) for s in range(1, n_group)]
     else:
         cache = lax.psum(jnp.where(me == owner, cache, jnp.zeros_like(cache)), "group")
-        prompts = cut(order, cache, kv_heads)
+        prompts = cut(range(kv_heads), jnp.zeros((1,), jnp.int32), cache, kv_heads)
 
     parts, backs, per_head = [], [], []
     for s, prompt in enumerate(prompts):

time: 64 us -> 63.4 us (level)
  no operation moved by 1% of the time
where the time goes in v19:
time: 63.4 us; the launch traced here: 63.3 us
  starting transfers between devices  24.5 us (39%)
  waiting for transfers between devices  18.5 us (29%)
  Pallas kernels  18.2 us (29%)
  between operations  2.02 us (3%)
    ppermute x12, starting transfers between devices, swap(): return lax.ppermute(x, 'group', [(i, i ^ step) for i in range(n_group)])  21.4 us
    ppermute x12, waiting for transfers between devices, swap(): return lax.ppermute(x, 'group', [(i, i ^ step) for i in range(n_group)])  13.2 us
    pallas_call x4, Pallas kernels, first_half(): pl.pallas_call(functools.partial(first_kernel, 2 * HD), out_shape=[jax.Sh...  7.17 us
    pallas_call x1, Pallas kernels, prepare(): pl.pallas_call(functools.partial(prepare_kernel, slots, share, rows, 2 *...  5.64 us
    ppermute x3, waiting for transfers between devices, hop(): return lax.ppermute(x, 'dp', [(i, i ^ step) for i in range(n_dp)])  5.27 us
    ppermute x3, starting transfers between devices, hop(): return lax.ppermute(x, 'dp', [(i, i ^ step) for i in range(n_dp)])  3.07 us
    pallas_call x1, Pallas kernels, settle_heads(): pl.pallas_call(functools.partial(settle_kernel, 2 * HD), out_shape=out_sh...  2.69 us
    pallas_call x1, Pallas kernels, place(): pl.pallas_call(functools.partial(place_kernel, tuple(steps)), out_shape=[...  1.45 us
  transfers between devices with their start and end apart: 15, of which 10 were waited for; matrix products, arithmetic and copies ran while one was open for 0% of the time, Pallas kernels for 24%

profile of v19, /device:TPU:0, one launch (start us, length us, event | category | flops | bytes accessed | tf_op | source)
XLA Modules:
  0.0 63.3 jit_solution(5741599666500377883)
XLA Ops:
  0.6 1.1 %cut_prompt.1 = (bf16[2,256,128]{2,1,0:T(8,128)(2,1)S(1)}, bf16[2,256,128]{2,1,0:T(8,128)(2,1)S(1)}, bf16[2,256,128]{2,1,0:T(8,128)(2,1)S(1)}, bf16[2,256,128]{2,1,0:T(8,128)(2,1)S(1)}) custom-call(s32[1]{0:T(128)} %bitcast.4.me, bf16[2,256,512]{2,1,0:T(8,128)(2,1)} %bitcast.20), custom_call_target="tpu_custom_call" | custom-call | tf_op jit(solution)/shard_map/cut_prompt/pallas_call | solution.py:48
  1.8 3.1 %collective-permute-start = (bf16[2,256,128]{2,1,0:T(8,128)(2,1)S(1)}, bf16[2,256,128]{2,1,0:T(8,128)(2,1)S(1)}, u32[]{:S(2)}, u32[]{:S(2)}) collective-permute-start(bf16[2,256,128]{2,1,0:T(8,128)(2,1)S(1)} %get-tuple-element.88), channel_id=1, source_target_pairs={{0,1},{1,0},{2,3},{3,2},{4,5},{5,4},{6,7},{7,6},{8,9},{9,8},{10,11... | collective-permute-start | bytes 393224 | tf_op jit(solution)/shard_map/ppermute | solution.py:490
  4.9 2.5 %collective-permute-start.1 = (bf16[2,256,128]{2,1,0:T(8,128)(2,1)S(1)}, bf16[2,256,128]{2,1,0:T(8,128)(2,1)S(1)}, u32[]{:S(2)}, u32[]{:S(2)}) collective-permute-start(bf16[2,256,128]{2,1,0:T(8,128)(2,1)S(1)} %get-tuple-element.90), channel_id=1, source_target_pairs={{0,3},{1,2},{2,1},{3,0},{4,7},{5,6},{6,5},{7,4},{8,11},{9,10},{10,... | collective-permute-start | bytes 393224 | tf_op jit(solution)/shard_map/ppermute | solution.py:490
  7.4 0.1 collective-permute-start.2
  8.8 0.1 pad_add_fusion.meta
  8.9 5.6 %prepare_response.1 = (bf16[128,768]{1,0:T(8,128)(2,1)S(1)}, bf16[128,768]{1,0:T(8,128)(2,1)S(1)}, f32[8,768]{1,0:T(8,128)S(1)}, bf16[192,768]{1,0:T(8,128)(2,1)...) custom-call(s32[5]{0:T(128)S(1)} %pad_add_fusion.meta, ...), custom_call_target="tpu_custom_call" | custom-call | flops 452984832 | bytes 3932160 | tf_op jit(solution)/shard_map/prepare_response/pallas_call | solution.py:162
  14.5 4.6 %collective-permute-done.2.refs_3_ = bf16[2,256,128]{2,1,0:T(8,128)(2,1)S(1)} collective-permute-done((bf16[2,256,128]{2,1,0:T(8,128)(2,1)S(1)}, bf16[2,256,128]{2,1,0:T(8,128)(2,1)S(1)}, u32[]{:S(2)}, u32[]{:S(2)}) %collective-permute-start.2) | collective-permute-done | bytes 131104 | tf_op jit(solution)/shard_map/ppermute | solution.py:490
  19.1 0.0 collective-permute-done.1.refs_2_
  19.1 0.0 collective-permute-done.refs_1_
  19.1 0.1 pick_owner.1.pr_ref
  19.2 0.1 collective-permute-start.3
  19.3 2.7 %collective-permute-start.5 = (bf16[2,256,128]{2,1,0:T(8,128)(2,1)S(1)}, bf16[2,256,128]{2,1,0:T(8,128)(2,1)S(1)}, u32[]{:S(2)}, u32[]{:S(2)}) collective-permute-start(bf16[2,256,128]{2,1,0:T(8,128)(2,1)S(1)} %pick_owner.1.pr_ref), channel_id=1, source_target_pairs={{0,3},{1,2},{2,1},{3,0},{4,7},{5,6},{6,5},{7,4},{8,11},{9,10},{10,... | collective-permute-start | bytes 393224 | tf_op jit(solution)/shard_map/ppermute | solution.py:490
  22.0 0.8 %collective-permute-start.7 = (bf16[2,256,128]{2,1,0:T(8,128)(2,1)S(1)}, bf16[2,256,128]{2,1,0:T(8,128)(2,1)S(1)}, u32[]{:S(2)}, u32[]{:S(2)}) collective-permute-start(bf16[2,256,128]{2,1,0:T(8,128)(2,1)S(1)} %pick_owner.1.pr_ref), channel_id=1, source_target_pairs={{0,2},{1,3},{2,0},{3,1},{4,6},{5,7},{6,4},{7,5},{8,10},{9,11},{10,... | collective-permute-start | bytes 393224 | tf_op jit(solution)/shard_map/ppermute | solution.py:490
  22.7 1.8 %attend_head.4 = (bf16[2,256,128]{2,1,0:T(8,128)(2,1)S(1)}, f32[2,128]{1,0:T(2,128)S(1)}, bf16[128,768]{1,0:T(8,128)(2,1)S(1)}, f32[128,768]{1,0:T(8,128)S(1)}, ...) custom-call(bf16[2,256,128]{2,1,0:T(8,128)(2,1)S(1)} %pick_owner.1.pr_ref, ...), custom_call_target="tpu_custom_call" | custom-call | flops 276824064 | bytes 1048576 | tf_op jit(solution)/shard_map/attend_head/pallas_call | solution.py:322
  24.5 1.4 %collective-permute-done.3.pr_ref = bf16[2,256,128]{2,1,0:T(8,128)(2,1)S(1)} collective-permute-done((bf16[2,256,128]{2,1,0:T(8,128)(2,1)S(1)}, bf16[2,256,128]{2,1,0:T(8,128)(2,1)S(1)}, u32[]{:S(2)}, u32[]{:S(2)}) %collective-permute-start.3) | collective-permute-done | bytes 131104 | tf_op jit(solution)/shard_map/ppermute | solution.py:490
  25.9 1.8 %attend_head.5 = (bf16[2,256,128]{2,1,0:T(8,128)(2,1)S(1)}, f32[2,128]{1,0:T(2,128)S(1)}, bf16[128,768]{1,0:T(8,128)(2,1)S(1)}, f32[128,768]{1,0:T(8,128)S(1)}, ...) custom-call(bf16[2,256,128]{2,1,0:T(8,128)(2,1)S(1)} %collective-permute-done.3.pr_ref, ...), custom_call_target="tpu_custom_call" | custom-call | flops 276824064 | bytes 1048576 | tf_op jit(solution)/shard_map/attend_head/pallas_call | solution.py:322
  27.7 1.0 %collective-permute-done.5.pr_ref = bf16[2,256,128]{2,1,0:T(8,128)(2,1)S(1)} collective-permute-done((bf16[2,256,128]{2,1,0:T(8,128)(2,1)S(1)}, bf16[2,256,128]{2,1,0:T(8,128)(2,1)S(1)}, u32[]{:S(2)}, u32[]{:S(2)}) %collective-permute-start.5) | collective-permute-done | bytes 131104 | tf_op jit(solution)/shard_map/ppermute | solution.py:490
  28.7 1.8 %attend_head.6 = (bf16[2,256,128]{2,1,0:T(8,128)(2,1)S(1)}, f32[2,128]{1,0:T(2,128)S(1)}, bf16[128,768]{1,0:T(8,128)(2,1)S(1)}, f32[128,768]{1,0:T(8,128)S(1)}, ...) custom-call(bf16[2,256,128]{2,1,0:T(8,128)(2,1)S(1)} %collective-permute-done.5.pr_ref, ...), custom_call_target="tpu_custom_call" | custom-call | flops 276824064 | bytes 1048576 | tf_op jit(solution)/shard_map/attend_head/pallas_call | solution.py:322
  30.5 2.2 %collective-permute-start.6 = (bf16[2,256,128]{2,1,0:T(8,128)(2,1)S(1)}, bf16[2,256,128]{2,1,0:T(8,128)(2,1)S(1)}, u32[]{:S(2)}, u32[]{:S(2)}) collective-permute-start(bf16[2,256,128]{2,1,0:T(8,128)(2,1)S(1)} %get-tuple-element.120), channel_id=1, source_target_pairs={{0,3},{1,2},{2,1},{3,0},{4,7},{5,6},{6,5},{7,4},{8,11},{9,10},{10,... | collective-permute-start | bytes 393224 | tf_op jit(solution)/shard_map/ppermute | solution.py:490
  32.7 4.7 %collective-permute-start.4 = (bf16[2,256,128]{2,1,0:T(8,128)(2,1)S(1)}, bf16[2,256,128]{2,1,0:T(8,128)(2,1)S(1)}, u32[]{:S(2)}, u32[]{:S(2)}) collective-permute-start(bf16[2,256,128]{2,1,0:T(8,128)(2,1)S(1)} %get-tuple-element.110), channel_id=1, source_target_pairs={{0,1},{1,0},{2,3},{3,2},{4,5},{5,4},{6,7},{7,6},{8,9},{9,8},{10,11... | collective-permute-start | bytes 393224 | tf_op jit(solution)/shard_map/ppermute | solution.py:490
  37.5 0.1 collective-permute-done.7.pr_ref
  37.6 1.8 %attend_head.7 = (bf16[2,256,128]{2,1,0:T(8,128)(2,1)S(1)}, f32[2,128]{1,0:T(2,128)S(1)}, bf16[128,768]{1,0:T(8,128)(2,1)S(1)}, f32[128,768]{1,0:T(8,128)S(1)}, ...) custom-call(bf16[2,256,128]{2,1,0:T(8,128)(2,1)S(1)} %collective-permute-done.7.pr_ref, ...), custom_call_target="tpu_custom_call" | custom-call | flops 276824064 | bytes 1048576 | tf_op jit(solution)/shard_map/attend_head/pallas_call | solution.py:322
  39.4 0.1 collective-permute-start.8
  39.5 0.1 collective-permute-start.9
  39.5 1.1 %collective-permute-done.9 = f32[2,128]{1,0:T(2,128)S(1)} collective-permute-done((f32[2,128]{1,0:T(2,128)S(1)}, f32[2,128]{1,0:T(2,128)S(1)}, u32[]{:S(2)}, u32[]{:S(2)}) %collective-permute-start.9) | collective-permute-done | bytes 1056 | tf_op jit(solution)/shard_map/ppermute | solution.py:512
  40.7 0.0 collective-permute-done.6.rest_1_
  40.7 0.4 collective-permute-done.4.rest_0_
  41.0 1.5 %collective-permute-start.10 = (f32[2,128]{1,0:T(2,128)S(1)}, f32[2,128]{1,0:T(2,128)S(1)}, u32[]{:S(2)}, u32[]{:S(2)}) collective-permute-start(f32[2,128]{1,0:T(2,128)S(1)} %add.9), channel_id=1, source_target_pairs={{0,8},{4,12},{8,0},{12,4},{16,24},{20,28},{24,16},{28,20},{1,9},{5... | collective-permute-start | bytes 3080 | tf_op jit(solution)/shard_map/ppermute | solution.py:512
  42.5 2.1 %collective-permute-done.10 = f32[2,128]{1,0:T(2,128)S(1)} collective-permute-done((f32[2,128]{1,0:T(2,128)S(1)}, f32[2,128]{1,0:T(2,128)S(1)}, u32[]{:S(2)}, u32[]{:S(2)}) %collective-permute-start.10) | collective-permute-done | bytes 1056 | tf_op jit(solution)/shard_map/ppermute | solution.py:512
  44.6 1.5 %collective-permute-start.11 = (f32[2,128]{1,0:T(2,128)S(1)}, f32[2,128]{1,0:T(2,128)S(1)}, u32[]{:S(2)}, u32[]{:S(2)}) collective-permute-start(f32[2,128]{1,0:T(2,128)S(1)} %add.10), channel_id=1, source_target_pairs={{0,16},{4,20},{8,24},{12,28},{16,0},{20,4},{24,8},{28,12},{1,17},{... | collective-permute-start | bytes 3080 | tf_op jit(solution)/shard_map/ppermute | solution.py:512
  46.1 2.1 %collective-permute-done.11 = f32[2,128]{1,0:T(2,128)S(1)} collective-permute-done((f32[2,128]{1,0:T(2,128)S(1)}, f32[2,128]{1,0:T(2,128)S(1)}, u32[]{:S(2)}, u32[]{:S(2)}) %collective-permute-start.11) | collective-permute-done | bytes 1056 | tf_op jit(solution)/shard_map/ppermute | solution.py:512
  48.2 0.0 collective-permute-done.8.rest_2_
  48.2 0.1 join_parts.1.refs_0_
  48.3 2.7 %collective-permute-start.12 = (bf16[528,128]{1,0:T(8,128)(2,1)S(1)}, bf16[528,128]{1,0:T(8,128)(2,1)S(1)}, u32[]{:S(2)}, u32[]{:S(2)}) collective-permute-start(bf16[528,128]{1,0:T(8,128)(2,1)S(1)} %join_parts.1.refs_0_), channel_id=1, source_target_pairs={{0,1},{1,0},{2,3},{3,2},{4,5},{5,4},{6,7},{7,6},{8,9},{9,8},{10,11... | collective-permute-start | bytes 405512 | tf_op jit(solution)/shard_map/ppermute | solution.py:490
  51.0 0.1 collective-permute-start.14
  51.1 2.4 %collective-permute-start.13 = (bf16[528,128]{1,0:T(8,128)(2,1)S(1)}, bf16[528,128]{1,0:T(8,128)(2,1)S(1)}, u32[]{:S(2)}, u32[]{:S(2)}) collective-permute-start(bf16[528,128]{1,0:T(8,128)(2,1)S(1)} %join_parts.1.refs_0_), channel_id=1, source_target_pairs={{0,3},{1,2},{2,1},{3,0},{4,7},{5,6},{6,5},{7,4},{8,11},{9,10},{10,... | collective-permute-start | bytes 405512 | tf_op jit(solution)/shard_map/ppermute | solution.py:490
  53.4 2.7 %settle_heads.1 = (bf16[192,2048]{1,0:T(8,128)(2,1)}, bf16[192,2048]{1,0:T(8,128)(2,1)}, bf16[192,512]{1,0:T(8,128)(2,1)}, bf16[192,512]{1,0:T(8,128)(2,1)}) custom-call(s32[5]{0:T(128)S(1)} %pad_add_fusion.meta, bf16[128,768]{1,0:T(8,128)(2,1)S(1)} %get-tuple-element.83.rest_0_, f32[8,768]{1,0:T(8,128)S(1)} %get-tuple-element.84.rest_2_.rest_1_, ...), custom_call_target="tpu_custom_call" | custom-call | tf_op jit(solution)/shard_map/settle_heads/pallas_call | solution.py:345
  56.1 0.7 %collective-permute-done.12.refs_1_ = bf16[528,128]{1,0:T(8,128)(2,1)S(1)} collective-permute-done((bf16[528,128]{1,0:T(8,128)(2,1)S(1)}, bf16[528,128]{1,0:T(8,128)(2,1)S(1)}, u32[]{:S(2)}, u32[]{:S(2)}) %collective-permute-start.12) | collective-permute-done | bytes 135200 | tf_op jit(solution)/shard_map/ppermute | solution.py:490
  56.8 5.0 %collective-permute-done.14.refs_3_ = bf16[528,128]{1,0:T(8,128)(2,1)S(1)} collective-permute-done((bf16[528,128]{1,0:T(8,128)(2,1)S(1)}, bf16[528,128]{1,0:T(8,128)(2,1)S(1)}, u32[]{:S(2)}, u32[]{:S(2)}) %collective-permute-start.14) | collective-permute-done | bytes 135200 | tf_op jit(solution)/shard_map/ppermute | solution.py:490
  61.8 0.0 collective-permute-done.13.refs_2_
  61.8 1.5 %place_prompt_grad.1 = (bf16[2,256,512]{2,1,0:T(8,128)(2,1)}, f32[2,128]{1,0:T(2,128)}) custom-call(s32[1]{0:T(128)} %bitcast.3.flag, s32[1]{0:T(128)} %bitcast.4.me, bf16[528,128]{1,0:T(8,128)(2,1)S(1)} %join_parts.1.refs_0_, bf16[528,128]{1,0:T(8,128)(2,1)S(1)} %collective-permute-done.12.refs_1_, bf16[528,128]{1,0:T(8,128)(2,1)S(1)} %collective-permute-done.13.refs_2_, ...), custom_call_target="tpu_custom_call" | custom-call | tf_op jit(solution)/shard_map/place_prompt_grad/pallas_call | solution.py:429
  (5 shorter events, 0.0 us)
Async XLA Ops:
  1.8 17.3 %collective-permute-start = (bf16[2,256,128]{2,1,0:T(8,128)(2,1)S(1)}, bf16[2,256,128]{2,1,0:T(8,128)(2,1)S(1)}, u32[]{:S(2)}, u32[]{:S(2)}) collective-permute-start(bf16[2,256,128]{2,1,0:T(8,128)(2,1)S(1)} %get-tuple-element.88), channel_id=1, source_target_pairs={{0,1},{1,0},{2,3},{3,2},{4,5},{5,4},{6,7},{7,6},{8,9},{9,8},{10,11... | collective-permute-start | bytes 393224 | tf_op jit(solution)/shard_map/ppermute | solution.py:490
  4.9 14.2 %collective-permute-start.1 = (bf16[2,256,128]{2,1,0:T(8,128)(2,1)S(1)}, bf16[2,256,128]{2,1,0:T(8,128)(2,1)S(1)}, u32[]{:S(2)}, u32[]{:S(2)}) collective-permute-start(bf16[2,256,128]{2,1,0:T(8,128)(2,1)S(1)} %get-tuple-element.90), channel_id=1, source_target_pairs={{0,3},{1,2},{2,1},{3,0},{4,7},{5,6},{6,5},{7,4},{8,11},{9,10},{10,... | collective-permute-start | bytes 393224 | tf_op jit(solution)/shard_map/ppermute | solution.py:490
  7.4 11.8 %collective-permute-start.2 = (bf16[2,256,128]{2,1,0:T(8,128)(2,1)S(1)}, bf16[2,256,128]{2,1,0:T(8,128)(2,1)S(1)}, u32[]{:S(2)}, u32[]{:S(2)}) collective-permute-start(bf16[2,256,128]{2,1,0:T(8,128)(2,1)S(1)} %get-tuple-element.92), channel_id=1, source_target_pairs={{0,2},{1,3},{2,0},{3,1},{4,6},{5,7},{6,4},{7,5},{8,10},{9,11},{10,... | collective-permute-start | bytes 393224 | tf_op jit(solution)/shard_map/ppermute | solution.py:490
  19.2 6.7 %collective-permute-start.3 = (bf16[2,256,128]{2,1,0:T(8,128)(2,1)S(1)}, bf16[2,256,128]{2,1,0:T(8,128)(2,1)S(1)}, u32[]{:S(2)}, u32[]{:S(2)}) collective-permute-start(bf16[2,256,128]{2,1,0:T(8,128)(2,1)S(1)} %pick_owner.1.pr_ref), channel_id=1, source_target_pairs={{0,1},{1,0},{2,3},{3,2},{4,5},{5,4},{6,7},{7,6},{8,9},{9,8},{10,11... | collective-permute-start | bytes 393224 | tf_op jit(solution)/shard_map/ppermute | solution.py:490
  19.3 9.5 %collective-permute-start.5 = (bf16[2,256,128]{2,1,0:T(8,128)(2,1)S(1)}, bf16[2,256,128]{2,1,0:T(8,128)(2,1)S(1)}, u32[]{:S(2)}, u32[]{:S(2)}) collective-permute-start(bf16[2,256,128]{2,1,0:T(8,128)(2,1)S(1)} %pick_owner.1.pr_ref), channel_id=1, source_target_pairs={{0,3},{1,2},{2,1},{3,0},{4,7},{5,6},{6,5},{7,4},{8,11},{9,10},{10,... | collective-permute-start | bytes 393224 | tf_op jit(solution)/shard_map/ppermute | solution.py:490
  22.0 15.6 %collective-permute-start.7 = (bf16[2,256,128]{2,1,0:T(8,128)(2,1)S(1)}, bf16[2,256,128]{2,1,0:T(8,128)(2,1)S(1)}, u32[]{:S(2)}, u32[]{:S(2)}) collective-permute-start(bf16[2,256,128]{2,1,0:T(8,128)(2,1)S(1)} %pick_owner.1.pr_ref), channel_id=1, source_target_pairs={{0,2},{1,3},{2,0},{3,1},{4,6},{5,7},{6,4},{7,5},{8,10},{9,11},{10,... | collective-permute-start | bytes 393224 | tf_op jit(solution)/shard_map/ppermute | solution.py:490
  30.5 10.2 %collective-permute-start.6 = (bf16[2,256,128]{2,1,0:T(8,128)(2,1)S(1)}, bf16[2,256,128]{2,1,0:T(8,128)(2,1)S(1)}, u32[]{:S(2)}, u32[]{:S(2)}) collective-permute-start(bf16[2,256,128]{2,1,0:T(8,128)(2,1)S(1)} %get-tuple-element.120), channel_id=1, source_target_pairs={{0,3},{1,2},{2,1},{3,0},{4,7},{5,6},{6,5},{7,4},{8,11},{9,10},{10,... | collective-permute-start | bytes 393224 | tf_op jit(solution)/shard_map/ppermute | solution.py:490
  32.7 8.3 %collective-permute-start.4 = (bf16[2,256,128]{2,1,0:T(8,128)(2,1)S(1)}, bf16[2,256,128]{2,1,0:T(8,128)(2,1)S(1)}, u32[]{:S(2)}, u32[]{:S(2)}) collective-permute-start(bf16[2,256,128]{2,1,0:T(8,128)(2,1)S(1)} %get-tuple-element.110), channel_id=1, source_target_pairs={{0,1},{1,0},{2,3},{3,2},{4,5},{5,4},{6,7},{7,6},{8,9},{9,8},{10,11... | collective-permute-start | bytes 393224 | tf_op jit(solution)/shard_map/ppermute | solution.py:490
  39.4 8.8 %collective-permute-start.8 = (bf16[2,256,128]{2,1,0:T(8,128)(2,1)S(1)}, bf16[2,256,128]{2,1,0:T(8,128)(2,1)S(1)}, u32[]{:S(2)}, u32[]{:S(2)}) collective-permute-start(bf16[2,256,128]{2,1,0:T(8,128)(2,1)S(1)} %get-tuple-element.130), channel_id=1, source_target_pairs={{0,2},{1,3},{2,0},{3,1},{4,6},{5,7},{6,4},{7,5},{8,10},{9,11},{10,... | collective-permute-start | bytes 393224 | tf_op jit(solution)/shard_map/ppermute | solution.py:490
  39.5 1.2 %collective-permute-start.9 = (f32[2,128]{1,0:T(2,128)S(1)}, f32[2,128]{1,0:T(2,128)S(1)}, u32[]{:S(2)}, u32[]{:S(2)}) collective-permute-start(f32[2,128]{1,0:T(2,128)S(1)} %get-tuple-element.131), channel_id=1, source_target_pairs={{0,4},{4,0},{8,12},{12,8},{16,20},{20,16},{24,28},{28,24},{1,5},{5... | collective-permute-start | bytes 3080 | tf_op jit(solution)/shard_map/ppermute | solution.py:512
  41.0 3.6 %collective-permute-start.10 = (f32[2,128]{1,0:T(2,128)S(1)}, f32[2,128]{1,0:T(2,128)S(1)}, u32[]{:S(2)}, u32[]{:S(2)}) collective-permute-start(f32[2,128]{1,0:T(2,128)S(1)} %add.9), channel_id=1, source_target_pairs={{0,8},{4,12},{8,0},{12,4},{16,24},{20,28},{24,16},{28,20},{1,9},{5... | collective-permute-start | bytes 3080 | tf_op jit(solution)/shard_map/ppermute | solution.py:512
  44.6 3.6 %collective-permute-start.11 = (f32[2,128]{1,0:T(2,128)S(1)}, f32[2,128]{1,0:T(2,128)S(1)}, u32[]{:S(2)}, u32[]{:S(2)}) collective-permute-start(f32[2,128]{1,0:T(2,128)S(1)} %add.10), channel_id=1, source_target_pairs={{0,16},{4,20},{8,24},{12,28},{16,0},{20,4},{24,8},{28,12},{1,17},{... | collective-permute-start | bytes 3080 | tf_op jit(solution)/shard_map/ppermute | solution.py:512
  48.3 8.5 %collective-permute-start.12 = (bf16[528,128]{1,0:T(8,128)(2,1)S(1)}, bf16[528,128]{1,0:T(8,128)(2,1)S(1)}, u32[]{:S(2)}, u32[]{:S(2)}) collective-permute-start(bf16[528,128]{1,0:T(8,128)(2,1)S(1)} %join_parts.1.refs_0_), channel_id=1, source_target_pairs={{0,1},{1,0},{2,3},{3,2},{4,5},{5,4},{6,7},{7,6},{8,9},{9,8},{10,11... | collective-permute-start | bytes 405512 | tf_op jit(solution)/shard_map/ppermute | solution.py:490
  51.0 10.8 %collective-permute-start.14 = (bf16[528,128]{1,0:T(8,128)(2,1)S(1)}, bf16[528,128]{1,0:T(8,128)(2,1)S(1)}, u32[]{:S(2)}, u32[]{:S(2)}) collective-permute-start(bf16[528,128]{1,0:T(8,128)(2,1)S(1)} %join_parts.1.refs_0_), channel_id=1, source_target_pairs={{0,2},{1,3},{2,0},{3,1},{4,6},{5,7},{6,4},{7,5},{8,10},{9,11},{10,... | collective-permute-start | bytes 405512 | tf_op jit(solution)/shard_map/ppermute | solution.py:490
  51.1 10.7 %collective-permute-start.13 = (bf16[528,128]{1,0:T(8,128)(2,1)S(1)}, bf16[528,128]{1,0:T(8,128)(2,1)S(1)}, u32[]{:S(2)}, u32[]{:S(2)}) collective-permute-start(bf16[528,128]{1,0:T(8,128)(2,1)S(1)} %join_parts.1.refs_0_), channel_id=1, source_target_pairs={{0,3},{1,2},{2,1},{3,0},{4,7},{5,6},{6,5},{7,4},{8,11},{9,10},{10,... | collective-permute-start | bytes 405512 | tf_op jit(solution)/shard_map/ppermute | solution.py:490
